TPU v7x, 32 devices: a whole 2x2x4 slice. The times are simulated.
32 devices in a mesh: pipe: 2 (over y), expert: 16 (over z, x, core).
Axes of the slice: x: 2, y: 2, z: 4, core: 2. Of those that a mesh axis runs over, the one named last changes fastest.
Arguments:
- upstream: bfloat16 [2, 1024, 2048], P('pipe', 'expert'), may hold values from -6 to 6
- expert_ids: int32 [2, 1024, 8], P('pipe', 'expert'), may hold values from 0 to 15, all different within a row; in each aligned block of 64 rows (0 to 63, 64 to 127, ..., all dimensions but the last counted through in order) at most 64 rows name the same one
- gate_weights: bfloat16 [2, 1024, 8], P('pipe', 'expert'), may hold values from 0.099609375 to 2
- expert_weight: bfloat16 [2, 16, 768, 2048], P('pipe', 'expert'), may hold values from -0.125 to 0.125
Outputs:
- hidden_grad: bfloat16 [2, 1024, 8, 768], P('pipe', 'expert')
Inputs may be any that keep to these rules, and one draw needn't show every extreme that they name: `expert_ids`: each token names 8 different experts. Among the 64 tokens of one device (aligned blocks of the section's tokens) no expert is named by more than 64 tokens, and in some blocks one expert is named by exactly 64.
All inputs are finite; a program needn't handle non-finite values.
Results may differ from a plain program's by a relative error of at most 0.001.
Values may be sent and summed in bfloat16 or wider, within the bound.
No kernel may reach another device: no remote copies, remote signals or barrier semaphores. Data moves between devices by JAX's collectives and lax.ppermute only.
A program may use at most 64 MiB of HBM per device.

v0:
```python
import jax
import jax.numpy as jnp
from jax import lax
from jax.sharding import PartitionSpec as P


def shifted(block, axis, distance):
    devices = range(lax.axis_size(axis))
    route = [((i - distance) % len(devices), i) for i in devices]
    return lax.ppermute(block, axis, route)


def per_device(upstream, expert_ids, gate_weights, expert_weight):
    section_grad = shifted(upstream, "pipe", -1)[0]
    route_ids = expert_ids[0]
    route_gates = gate_weights[0]
    weight_mat = expert_weight[0, 0]
    token_count, top_count = route_ids.shape
    owner_count = lax.axis_size("expert")
    capacity = 2 * token_count * top_count // owner_count
    owners = jnp.arange(owner_count, dtype=jnp.int32)
    slot_index = jnp.arange(capacity, dtype=jnp.int32)
    matched = (route_ids[:, :, None] == owners[None, None, :]).astype(jnp.int32)
    hit_count = jnp.sum(matched, axis=1)
    slot_rank = jnp.cumsum(hit_count, axis=0) - hit_count
    route_rank = jnp.sum(matched * slot_rank[:, None, :], axis=2)
    position = route_ids * capacity + route_rank
    gate_owner = jnp.einsum(
        "tk,tke->te", route_gates.astype(jnp.float32), matched.astype(jnp.float32)
    )
    slot_pick = (hit_count[:, :, None] == 1) & (slot_rank[:, :, None] == slot_index[None, None, :])
    send_rows = jnp.einsum(
        "tem,td->emd",
        slot_pick.astype(jnp.bfloat16),
        section_grad,
        preferred_element_type=jnp.float32,
    ).astype(jnp.bfloat16)
    send_gates = jnp.einsum("tem,te->em", slot_pick.astype(jnp.float32), gate_owner).astype(
        jnp.bfloat16
    )
    got_rows, got_gates = (
        lax.all_to_all(send_rows, "expert", split_axis=0, concat_axis=0, tiled=True),
        lax.all_to_all(send_gates, "expert", split_axis=0, concat_axis=0, tiled=True),
    )
    blocks = got_rows.shape[0]
    slot_span = got_rows.shape[1]
    flat_rows = got_rows.reshape(blocks * slot_span, got_rows.shape[2])
    product = lax.dot_general(
        flat_rows, weight_mat, (((1,), (1,)), ((), ())), preferred_element_type=jnp.float32
    )
    product = product.reshape(blocks, slot_span, weight_mat.shape[0])
    returned = lax.all_to_all(
        (product * got_gates.astype(jnp.float32)[:, :, None]).astype(jnp.bfloat16),
        "expert",
        split_axis=0,
        concat_axis=0,
        tiled=True,
    )
    flat_back = returned.reshape(owner_count * capacity, returned.shape[2])
    hidden_grad = jnp.take(flat_back, position.reshape(token_count * top_count), axis=0)
    return hidden_grad.reshape(token_count, top_count, returned.shape[2])[None]


def solution(mesh):
    in_specs = (
        P("pipe", "expert", None),
        P("pipe", "expert", None),
        P("pipe", "expert", None),
        P("pipe", "expert", None, None),
    )
    out_specs = P("pipe", "expert", None, None)
    return jax.shard_map(
        per_device, mesh=mesh, in_specs=in_specs, out_specs=out_specs, check_vma=False
    )
```

profile of v0, /device:TPU:11, one launch (start us, length us, event | category | flops | bytes accessed | tf_op | source)
XLA Modules:
  0.0 169.5 jit_solution(12308118657791534713)
XLA Ops:
  0.0 0.0 copy-start
  0.0 1.2 collective-permute-start
  1.2 0.7 convert_reduce_fusion
  1.9 0.1 copy.24
  2.0 0.1 reduce_window_sum.11
  2.1 0.1 copy.26
  2.2 0.7 bitcast_convert_fusion
  2.9 0.7 fusion.14
  3.6 0.2 fusion.5
  3.9 0.6 copy.29
  4.5 6.8 %all-to-all-start.1 = ((bf16[16,1,64]{2,1,0:T(2,128)(2,1)}), bf16[16,1,64]{2,1,0:T(2,128)(2,1)S(1)}, u32[]{:S(2)}, u32[]{:S(2)}) async-start(bf16[16,1,64]{2,1,0:T(2,128)(2,1)} %copy.29), calls=%async_computation.1 | async-start | bytes 16384 | tf_op jit(solution)/shard_map/all_to_all | solution.py:43
  11.3 0.0 collective-permute-done
  11.3 3.2 %convolution_convert_fusion = bf16[16,64,2048]{2,1,0:T(8,128)(2,1)} fusion(bf16[1,64,2048]{2,1,0:T(8,128)(2,1)S(1)} %collective-permute-done, s32[64,16]{0,1:T(8,128)S(1)} %copy.26, pred[64,16]{0,1:T(8,128)(4,1)S(1)} %broadcast_compare_fusion), kind=kOutput, calls=%fused_computation.1 | convolution fusion | flops 270663680 | bytes 4461568 | tf_op jit(solution)/shard_map/tem,td->emd/dot_general | solution.py:32
  14.5 0.5 all-to-all-done.1
  15.0 7.0 %all-to-all-start = ((bf16[16,64,2048]{2,1,0:T(8,128)(2,1)}), bf16[16,64,2048]{2,1,0:T(8,128)(2,1)}, u32[]{:S(2)}, u32[]{:S(2)}) async-start(bf16[16,64,2048]{2,1,0:T(8,128)(2,1)} %convolution_convert_fusion), calls=%async_computation | async-start | bytes 8388608 | tf_op jit(solution)/shard_map/all_to_all | solution.py:42
  22.1 92.5 %all-to-all-done = bf16[16,64,2048]{2,1,0:T(8,128)(2,1)} async-done(((bf16[16,64,2048]{2,1,0:T(8,128)(2,1)}), bf16[16,64,2048]{2,1,0:T(8,128)(2,1)}, u32[]{:S(2)}, u32[]{:S(2)}) %all-to-all-start) | async-done | bytes 4194336 | tf_op jit(solution)/shard_map/all_to_all | solution.py:42
  114.5 0.0 copy-done
  114.5 6.8 %multiply_convert_fusion = bf16[16,64,768]{2,1,0:T(8,128)(2,1)} fusion(bf16[16,64,2048]{2,1,0:T(8,128)(2,1)} %all-to-all-done, bf16[1,1,768,2048]{3,2,1,0:T(8,128)(2,1)S(1)} %copy-done, f32[16,64]{1,0:T(8,128)S(1)} %bitcast.34), kind=kOutput, calls=%fused_computation.4 | convolution fusion | flops 3222798336 | bytes 8916992 | tf_op jit(solution)/shard_map/dot_general | solution.py:48
  121.3 0.0 copy-start.1
  121.3 5.0 %all-to-all-start.2 = ((bf16[16,64,768]{2,1,0:T(8,128)(2,1)}), bf16[16,64,768]{2,1,0:T(8,128)(2,1)}, u32[]{:S(2)}, u32[]{:S(2)}) async-start(bf16[16,64,768]{2,1,0:T(8,128)(2,1)} %multiply_convert_fusion), calls=%async_computation.2 | async-start | bytes 3145728 | tf_op jit(solution)/shard_map/all_to_all | solution.py:52
  126.4 0.0 copy-done.1
  126.4 0.1 copy.30
  126.5 0.1 mul.48
  126.6 0.1 copy.31
  126.7 0.1 reduce_sum.22
  126.8 0.1 copy.27
  126.9 35.7 %all-to-all-done.2 = bf16[16,64,768]{2,1,0:T(8,128)(2,1)} async-done(((bf16[16,64,768]{2,1,0:T(8,128)(2,1)}), bf16[16,64,768]{2,1,0:T(8,128)(2,1)}, u32[]{:S(2)}, u32[]{:S(2)}) %all-to-all-start.2) | async-done | bytes 1572896 | tf_op jit(solution)/shard_map/all_to_all | solution.py:52
  162.6 4.7 %gather_fusion = bf16[512,768]{1,0:T(8,128)(2,1)} fusion(bf16[1024,768]{1,0:T(8,128)(2,1)} %bitcast.11, s32[1024]{0:T(1024)S(1)} %pad_clamp_fusion), kind=kCustom, calls=%fused_computation | custom fusion | bytes 1574912 | tf_op jit(solution)/shard_map/jit(_take)/gather | solution.py:60
  167.4 2.2 %bitcast_select_fusion = bf16[1,64,8,768]{3,2,1,0:T(8,128)(2,1)} fusion(bf16[512,768]{1,0:T(8,128)(2,1)} %gather_fusion, pred[64,8]{1,0:T(8,128)(4,1)S(1)} %copy.27), kind=kLoop, calls=%fused_computation.5 | loop fusion | flops 393216 | bytes 1573376 | tf_op jit(solution)/shard_map/jit(_take)/select_n | solution.py:60
  (9 shorter events, 0.1 us)
Async XLA Ops:
  0.0 114.5 %copy-start = (bf16[1,1,768,2048]{3,2,1,0:T(8,128)(2,1)S(1)}, bf16[1,1,768,2048]{3,2,1,0:T(8,128)(2,1)}, u32[]{:S(2)}) copy-start(bf16[1,1,768,2048]{3,2,1,0:T(8,128)(2,1)} %param.7) | copy-start | bytes 9437188
  0.0 11.3 %collective-permute-start = (bf16[1,64,2048]{2,1,0:T(8,128)(2,1)}, bf16[1,64,2048]{2,1,0:T(8,128)(2,1)S(1)}, u32[]{:S(2)}, u32[]{:S(2)}) collective-permute-start(bf16[1,64,2048]{2,1,0:T(8,128)(2,1)} %param.4), channel_id=1, source_target_pairs={{16,0},{0,16},{17,1},{1,17},{18,2},{2,18},{19,3},{3,19},{20,4},{4,... | collective-permute-start | bytes 786440 | tf_op jit(solution)/shard_map/ppermute | solution.py:10
  4.5 10.6 %all-to-all-start.1 = ((bf16[16,1,64]{2,1,0:T(2,128)(2,1)}), bf16[16,1,64]{2,1,0:T(2,128)(2,1)S(1)}, u32[]{:S(2)}, u32[]{:S(2)}) async-start(bf16[16,1,64]{2,1,0:T(2,128)(2,1)} %copy.29), calls=%async_computation.1 | async-start | bytes 16384 | tf_op jit(solution)/shard_map/all_to_all | solution.py:43
  15.0 99.5 %all-to-all-start = ((bf16[16,64,2048]{2,1,0:T(8,128)(2,1)}), bf16[16,64,2048]{2,1,0:T(8,128)(2,1)}, u32[]{:S(2)}, u32[]{:S(2)}) async-start(bf16[16,64,2048]{2,1,0:T(8,128)(2,1)} %convolution_convert_fusion), calls=%async_computation | async-start | bytes 8388608 | tf_op jit(solution)/shard_map/all_to_all | solution.py:42
  121.3 5.0 %copy-start.1 = (s32[1,64,8]{1,2,0:T(8,128)S(1)}, s32[1,64,8]{1,2,0:T(8,128)}, u32[]{:S(2)}) copy-start(s32[1,64,8]{1,2,0:T(8,128)} %param.5) | copy-start | bytes 6148
  121.3 41.3 %all-to-all-start.2 = ((bf16[16,64,768]{2,1,0:T(8,128)(2,1)}), bf16[16,64,768]{2,1,0:T(8,128)(2,1)}, u32[]{:S(2)}, u32[]{:S(2)}) async-start(bf16[16,64,768]{2,1,0:T(8,128)(2,1)} %multiply_convert_fusion), calls=%async_computation.2 | async-start | bytes 3145728 | tf_op jit(solution)/shard_map/all_to_all | solution.py:52
where the time goes:
time: 170 us
  waiting for transfers between devices  129 us (76%)
  starting transfers between devices  20.1 us (12%)
  matrix products  10.3 us (6%)
  local copies, waits for them, and re-layouts  5.95 us (4%)
  other arithmetic  4.42 us (3%)
    all_to_all x1, waiting for transfers between devices, per_device(): lax.all_to_all(send_rows, 'expert', split_axis=0, concat_axis=0, tiled=True)  92.5 us
    all_to_all x1, waiting for transfers between devices, per_device(): lax.all_to_all((product * got_gates.astype(jnp.float32)[:, :, None]).asty...  35.7 us
    all_to_all x1, starting transfers between devices, per_device(): lax.all_to_all(send_rows, 'expert', split_axis=0, concat_axis=0, tiled=True)  7 us
    all_to_all x1, starting transfers between devices, per_device(): lax.all_to_all(send_gates, 'expert', split_axis=0, concat_axis=0, tiled=T...  6.83 us
    dot_general x1, matrix products, per_device(): lax.dot_general(flat_rows, weight_mat, (((1,), (1,)), ((), ())), preferre...  6.81 us
    all_to_all x1, starting transfers between devices, per_device(): lax.all_to_all((product * got_gates.astype(jnp.float32)[:, :, None]).asty...  5.02 us
    gather x1, local copies, waits for them, and re-layouts, per_device(): jnp.take(flat_back, position.reshape(token_count * top_count), axis=0)  4.71 us
  transfers between devices with their start and end apart: 4, of which 3 were waited for; matrix products, arithmetic and copies ran while one was open for 4% of the time, Pallas kernels for 0%

commit v1 on v0

v1 whole, which is shorter than its diff:
```python
import jax
import jax.numpy as jnp
from jax import lax
from jax.sharding import PartitionSpec as P


def shifted(block, axis, distance):
    devices = range(lax.axis_size(axis))
    route = [((i - distance) % len(devices), i) for i in devices]
    return lax.ppermute(block, axis, route)


def per_device(upstream, expert_ids, gate_weights, expert_weight):
    section_grad = shifted(upstream, "pipe", -1)[0]
    route_ids = expert_ids[0]
    route_gates = gate_weights[0]
    weight_mat = expert_weight[0, 0]
    tokens, top = route_ids.shape
    owners = lax.axis_size("expert")
    hidden = weight_mat.shape[0]

    matched = route_ids[:, :, None] == jnp.arange(owners, dtype=jnp.int32)
    dense_gates = jnp.sum(
        jnp.where(matched, route_gates[:, :, None].astype(jnp.float32), 0.0), axis=1
    ).T.astype(jnp.bfloat16)
    got_gates = lax.all_to_all(dense_gates, "expert", split_axis=0, concat_axis=0, tiled=True)

    got_rows = lax.all_gather(section_grad, "expert", axis=0, tiled=True)
    product = lax.dot_general(
        got_rows, weight_mat, (((1,), (1,)), ((), ())), preferred_element_type=jnp.float32
    )
    scaled = product.reshape(owners, tokens, hidden) * got_gates.astype(jnp.float32)[:, :, None]
    returned = lax.all_to_all(
        scaled.astype(jnp.bfloat16), "expert", split_axis=0, concat_axis=0, tiled=True
    )
    same = jnp.arange(tokens)[:, None] == jnp.arange(tokens)[None, :]
    pick = (matched[:, :, :, None] & same[:, None, None, :]).astype(jnp.bfloat16)
    out = lax.dot_general(
        pick.reshape(tokens * top, owners * tokens),
        returned.reshape(owners * tokens, hidden),
        (((1,), (0,)), ((), ())),
        preferred_element_type=jnp.float32,
    )
    return out.astype(jnp.bfloat16).reshape(1, tokens, top, hidden)


def solution(mesh):
    in_specs = (
        P("pipe", "expert", None),
        P("pipe", "expert", None),
        P("pipe", "expert", None),
        P("pipe", "expert", None, None),
    )
    out_specs = P("pipe", "expert", None, None)
    return jax.shard_map(
        per_device, mesh=mesh, in_specs=in_specs, out_specs=out_specs, check_vma=False
    )
```

time: 170 us -> 126 us (0.74)
  waiting for transfers between devices: 129 us -> 75.5 us
  between operations: 0.06 us -> 13.4 us
  starting transfers between devices: 20.1 us -> 6.87 us
  blocking collectives: 0 us -> 11 us
    all_to_all x3 -> x1, waiting for transfers between devices: 129 us -> 29.5 us  [per_device(): lax.all_to_all(scaled.astype(jnp.bfloat16), 'expert', split_axis=0, conca...]
    all_gather x0 -> x1, waiting for transfers between devices: none -> 39.8 us  [per_device(): got_rows = lax.all_gather(section_grad, 'expert', axis=0, tiled=True)]
    all_to_all x3 -> x1, starting transfers between devices: 18.8 us -> 5.63 us  [per_device(): lax.all_to_all(scaled.astype(jnp.bfloat16), 'expert', split_axis=0, conca...]
    all_to_all x0 -> x1, blocking collectives: none -> 11 us  [per_device(): lax.all_to_all(dense_gates, 'expert', split_axis=0, concat_axis=0, tiled=...]
    ppermute x1, waiting for transfers between devices: 0.01 us -> 6.14 us  [shifted(): return lax.ppermute(block, axis, route)]
    gather x1 -> x0, local copies, waits for them, and re-layouts: 4.71 us -> none  [per_device(): jnp.take(flat_back, position.reshape(token_count * top_count), axis=0)]
    and x1, local copies, waits for them, and re-layouts: 0.1 us -> 4.08 us  [per_device(): matched[:, :, :, None] & same[:, None, None, :]]
    and x1, other arithmetic: 0.01 us -> 2.46 us  [per_device(): matched[:, :, :, None] & same[:, None, None, :]]
  transfers between devices with their start and end apart: 4 -> 3, of which waited for: 3 -> 3; matrix products, arithmetic and copies ran while one was open for 4% -> 6% of each run, Pallas kernels for 0% -> 0%
where the time goes in v1:
time: 126 us
  waiting for transfers between devices  75.5 us (60%)
  between operations  13.4 us (11%)
  blocking collectives  11 us (9%)
  matrix products  10.3 us (8%)
  starting transfers between devices  6.87 us (5%)
  local copies, waits for them, and re-layouts  4.97 us (4%)
  other arithmetic  3.88 us (3%)
    all_gather x1, waiting for transfers between devices, per_device(): got_rows = lax.all_gather(section_grad, 'expert', axis=0, tiled=True)  39.8 us
    all_to_all x1, waiting for transfers between devices, per_device(): lax.all_to_all(scaled.astype(jnp.bfloat16), 'expert', split_axis=0, conca...  29.5 us
    all_to_all x1, blocking collectives, per_device(): lax.all_to_all(dense_gates, 'expert', split_axis=0, concat_axis=0, tiled=...  11 us
    dot_general x1, matrix products, per_device(): lax.dot_general(got_rows, weight_mat, (((1,), (1,)), ((), ())), preferred...  6.81 us
    ppermute x1, waiting for transfers between devices, shifted(): return lax.ppermute(block, axis, route)  6.14 us
    all_to_all x1, starting transfers between devices, per_device(): lax.all_to_all(scaled.astype(jnp.bfloat16), 'expert', split_axis=0, conca...  5.63 us
    and x1, local copies, waits for them, and re-layouts, per_device(): matched[:, :, :, None] & same[:, None, None, :]  4.08 us
    dot_general x1, matrix products, per_device(): lax.dot_general(pick.reshape(tokens * top, owners * tokens), returned.res...  3.45 us
  transfers between devices with their start and end apart: 3, of which 3 were waited for; matrix products, arithmetic and copies ran while one was open for 6% of the time, Pallas kernels for 0%

profile of v1, /device:TPU:11, one launch (start us, length us, event | category | flops | bytes accessed | tf_op | source)
XLA Modules:
  0.0 125.9 jit_solution(15355330533256934864)
XLA Ops:
  6.5 0.0 copy-start
  6.5 0.0 all-gather.3.cloned.1.call-start
  6.5 1.2 collective-permute-start
  7.8 6.1 %collective-permute-done = bf16[1,64,2048]{2,1,0:T(8,128)(2,1)S(1)} collective-permute-done((bf16[1,64,2048]{2,1,0:T(8,128)(2,1)}, bf16[1,64,2048]{2,1,0:T(8,128)(2,1)S(1)}, u32[]{:S(2)}, u32[]{:S(2)}) %collective-permute-start) | collective-permute-done | bytes 262176 | tf_op jit(solution)/shard_map/ppermute | solution.py:10
  13.9 0.0 copy-start.1
  13.9 0.7 copy-done.1
  14.6 0.0 all-gather.3.cloned.1.call-update
  14.7 0.7 bitcast_convert_fusion
  15.3 0.7 select_reduce_fusion
  16.1 11.0 %all_to_all.14 = bf16[16,1,64]{2,1,0:T(2,128)(2,1)S(1)} all-to-all(bf16[16,1,64]{2,1,0:T(2,128)(2,1)S(1)} %copy.13), channel_id=1, replica_groups=mesh['pipe'=2,'expert'=16] {'expert'}, dimensions={0} | all-to-all | bytes 4096 | tf_op jit(solution)/shard_map/all_to_all | solution.py:26
  27.1 39.8 %all-gather.3.cloned.1.call-done = bf16[1,1024,2048]{2,1,0:T(8,128)(2,1)} async-done(((bf16[1,64,2048]{2,1,0:T(8,128)(2,1)}), bf16[1,1024,2048]{2,1,0:T(8,128)(2,1)}) %all-gather.3.cloned.1.call-update) | async-done | bytes 4194320 | tf_op jit(solution)/shard_map/all_gather | solution.py:28
  66.9 0.0 copy-done
  66.9 6.8 %multiply_convert_fusion = bf16[16,64,768]{2,1,0:T(8,128)(2,1)} fusion(bf16[16,64,2048]{2,1,0:T(8,128)(2,1)} %bitcast.30, bf16[1,1,768,2048]{3,2,1,0:T(8,128)(2,1)S(1)} %copy-done, f32[16,64]{1,0:T(8,128)S(1)} %bitcast.29), kind=kOutput, calls=%fused_computation.2 | convolution fusion | flops 3222798336 | bytes 8916992 | tf_op jit(solution)/shard_map/dot_general | solution.py:29
  73.7 0.0 copy-start.2
  73.7 5.6 %all-to-all-start.1 = ((bf16[16,64,768]{2,1,0:T(8,128)(2,1)}), bf16[16,64,768]{2,1,0:T(8,128)(2,1)}, u32[]{:S(2)}, u32[]{:S(2)}) async-start(bf16[16,64,768]{2,1,0:T(8,128)(2,1)} %multiply_convert_fusion), calls=%async_computation.1 | async-start | bytes 3145728 | tf_op jit(solution)/shard_map/all_to_all | solution.py:33
  79.3 0.0 copy-done.2
  79.4 0.2 copy.12
  79.6 2.5 %broadcast_and_fusion = pred[64,8,16,64]{3,2,1,0:T(8,128)(4,1)} fusion(pred[64,64]{1,0:T(8,128)(4,1)S(1)} %iota_compare_fusion.1, pred[64,8,16]{2,1,0:T(8,128)(4,1)S(1)} %copy.12), kind=kLoop, calls=%fused_computation.3 | loop fusion | flops 524288 | bytes 536576 | tf_op jit(solution)/shard_map/and | solution.py:37
  82.0 4.1 %and.26 = pred[512,1024]{1,0:T(32,128)(4,1)} reshape(pred[64,8,16,64]{3,2,1,0:T(8,128)(4,1)} %broadcast_and_fusion) | data formatting | bytes 1048576 | tf_op jit(solution)/shard_map/and | solution.py:37
  86.1 29.5 %all-to-all-done.1 = bf16[16,64,768]{2,1,0:T(8,128)(2,1)} async-done(((bf16[16,64,768]{2,1,0:T(8,128)(2,1)}), bf16[16,64,768]{2,1,0:T(8,128)(2,1)}, u32[]{:S(2)}, u32[]{:S(2)}) %all-to-all-start.1) | async-done | bytes 1572896 | tf_op jit(solution)/shard_map/all_to_all | solution.py:33
  115.7 3.4 %fusion.4 = bf16[1,64,8,768]{3,2,1,0:T(8,128)(2,1)} fusion(pred[512,1024]{1,0:T(32,128)(4,1)} %and.26, bf16[1024,768]{1,0:T(8,128)(2,1)} %bitcast.8), kind=kOutput, calls=%fused_computation.5 | convolution fusion | flops 805699584 | bytes 2883584 | tf_op jit(solution)/shard_map/dot_general | solution.py:38
  (4 shorter events, 0.0 us)
Async XLA Ops:
  6.5 60.4 %copy-start = (bf16[1,1,768,2048]{3,2,1,0:T(8,128)(2,1)S(1)}, bf16[1,1,768,2048]{3,2,1,0:T(8,128)(2,1)}, u32[]{:S(2)}) copy-start(bf16[1,1,768,2048]{3,2,1,0:T(8,128)(2,1)} %param.7) | copy-start | bytes 9437188
  6.5 60.4 %all-gather.3.cloned.1.call-start = ((), (), s32[]{:S(2)}) async-start(), calls=%async_computation.2 | async-start | bytes 4456448 | tf_op jit(solution)/shard_map/all_gather | solution.py:28
  6.5 7.4 %collective-permute-start = (bf16[1,64,2048]{2,1,0:T(8,128)(2,1)}, bf16[1,64,2048]{2,1,0:T(8,128)(2,1)S(1)}, u32[]{:S(2)}, u32[]{:S(2)}) collective-permute-start(bf16[1,64,2048]{2,1,0:T(8,128)(2,1)} %param.4), channel_id=1, source_target_pairs={{16,0},{0,16},{17,1},{1,17},{18,2},{2,18},{19,3},{3,19},{20,4},{4,... | collective-permute-start | bytes 786440 | tf_op jit(solution)/shard_map/ppermute | solution.py:10
  13.9 0.7 copy-start.1
  73.7 5.6 %copy-start.2 = (s32[1,64,8]{1,2,0:T(8,128)S(1)}, s32[1,64,8]{1,2,0:T(8,128)}, u32[]{:S(2)}) copy-start(s32[1,64,8]{1,2,0:T(8,128)} %param.5) | copy-start | bytes 6148
  73.7 41.9 %all-to-all-start.1 = ((bf16[16,64,768]{2,1,0:T(8,128)(2,1)}), bf16[16,64,768]{2,1,0:T(8,128)(2,1)}, u32[]{:S(2)}, u32[]{:S(2)}) async-start(bf16[16,64,768]{2,1,0:T(8,128)(2,1)} %multiply_convert_fusion), calls=%async_computation.1 | async-start | bytes 3145728 | tf_op jit(solution)/shard_map/all_to_all | solution.py:33
Sparse Core Ops, SparseCore 0:
  14.8 52.0 all-gather.2

commit v2 on v0

v2 whole, which is shorter than its diff:
```python
import functools

import jax
import jax.numpy as jnp
from jax import lax
from jax.experimental import pallas as pl
from jax.experimental.pallas import tpu as pltpu
from jax.sharding import PartitionSpec as P

COLUMNS = 2
CORES = 2


def shifted(block, axis, distance):
    devices = range(lax.axis_size(axis))
    route = [((i - distance) % len(devices), i) for i in devices]
    return lax.ppermute(block, axis, route)


def ring_order(owners):
    height = owners // (COLUMNS * CORES)
    up = [z * COLUMNS for z in range(height)]
    down = [z * COLUMNS + 1 for z in reversed(range(height))]
    return up + down


def ring_route(owners, distance, flip):
    order = ring_order(owners)
    route = []
    for place, chip in enumerate(order):
        target = order[(place + distance) % len(order)]
        for core in range(CORES):
            route.append((chip * CORES + core, target * CORES + (core ^ flip)))
    return route


def send(block, owners, distance, flip):
    return lax.ppermute(block, "expert", ring_route(owners, distance, flip))


def expert_kernel(count, *refs):
    rows, (weight, gates), outs = refs[:count], refs[count : count + 2], refs[count + 2 :]
    stacked = jnp.concatenate([r[...] for r in rows], axis=0)
    scale = jnp.concatenate([gates[:, j : j + 1] for j in range(gates.shape[1])], axis=0)
    product = lax.dot_general(
        stacked, weight[...], (((1,), (1,)), ((), ())), preferred_element_type=jnp.float32
    )
    scaled = (product * scale).astype(jnp.bfloat16)
    tokens = gates.shape[0]
    for j, out in enumerate(outs):
        out[...] = scaled[j * tokens : (j + 1) * tokens]


def expert_rows(rows, weight, gates):
    tokens, blocks = gates.shape
    hidden, depth = weight.shape
    return pl.pallas_call(
        functools.partial(expert_kernel, len(rows)),
        out_shape=[jax.ShapeDtypeStruct((tokens, hidden), jnp.bfloat16)] * blocks,
        compiler_params=pltpu.CompilerParams(vmem_limit_bytes=40 << 20),
        cost_estimate=pl.CostEstimate(
            flops=2 * blocks * tokens * hidden * depth,
            bytes_accessed=2 * (blocks * tokens * (hidden + depth) + hidden * depth),
            transcendentals=0,
        ),
    )(*rows, weight, gates)


def pick_kernel(labels_ref, *refs):
    blocks, out = refs[:-1], refs[-1]
    tokens, hidden = blocks[0].shape
    top = out.shape[0] // tokens
    span = 16
    routes = span * top
    column = lax.broadcasted_iota(jnp.int32, (routes, len(blocks) * span), 1)
    token = lax.broadcasted_iota(jnp.int32, (routes, len(blocks) * span), 0) // top
    for g in range(tokens // span):
        stacked = jnp.concatenate([b[g * span : (g + 1) * span, :] for b in blocks], axis=0)
        wanted = labels_ref[g * routes : (g + 1) * routes, :] * span + token
        pick = jnp.where(column == wanted, 1.0, 0.0).astype(jnp.bfloat16)
        rows = jnp.dot(pick, stacked, preferred_element_type=jnp.float32)
        out[g * routes : (g + 1) * routes, :] = rows.astype(jnp.bfloat16)


def pick_routes(labels, blocks):
    tokens, hidden = blocks[0].shape
    return pl.pallas_call(
        pick_kernel,
        out_shape=jax.ShapeDtypeStruct((labels.shape[0], hidden), jnp.bfloat16),
        compiler_params=pltpu.CompilerParams(vmem_limit_bytes=40 << 20),
    )(labels, *blocks)


def dense_device(section_grad, route_ids, route_gates, weight_mat):
    tokens, top = route_ids.shape
    owners = lax.axis_size("expert")
    hidden = weight_mat.shape[0]
    order = ring_order(owners)
    size = len(order)
    place_of_chip = jnp.array([order.index(c) for c in range(size)], jnp.int32)
    chip_of_place = jnp.array(order, jnp.int32)
    me = lax.axis_index("expert")
    my_place, my_core = place_of_chip[me // CORES], me % CORES

    matched = route_ids[:, :, None] == jnp.arange(owners, dtype=jnp.int32)
    dense_gates = jnp.sum(
        jnp.where(matched, route_gates[:, :, None].astype(jnp.float32), 0.0), axis=1
    ).T.astype(jnp.bfloat16)
    got_gates = lax.all_to_all(dense_gates, "expert", split_axis=0, concat_axis=0, tiled=True)
    labels = jnp.arange(owners, dtype=jnp.int32)
    label_owner = (
        chip_of_place[(my_place + labels // CORES) % size] * CORES + (my_core ^ (labels % CORES))
    )
    gates = jnp.take(got_gates, label_owner, axis=0).T.astype(jnp.float32)
    route_labels = (place_of_chip[route_ids // CORES] - my_place) % size * CORES + (
        (route_ids % CORES) ^ my_core
    )

    half = tokens // 2
    own = {0: section_grad}
    back = ahead = section_grad
    for step in range(1, size // 2):
        back, ahead = send(back, owners, 1, 0), send(ahead, owners, -1, 0)
        own[size - step], own[step] = back, ahead
    top_half = send(back[:half], owners, 1, 0)
    low_half = send(ahead[half:], owners, -1, 0)

    results = {}

    def products(distances, pieces):
        names = [d * CORES + c for d in distances for c in range(CORES)]
        picked = jnp.concatenate([gates[:, n : n + 1] for n in names], axis=1)
        results.update(zip(names, expert_rows(pieces, weight_mat, picked)))

    for step in range(size // 2):
        distances = [0] if step == 0 else [size - step, step]
        pieces = []
        for d in distances:
            pieces += [own[d], send(own[d], owners, 0, 1)]
        products(distances, pieces)
    products(
        [size // 2], [top_half, low_half, send(top_half, owners, 0, 1), send(low_half, owners, 0, 1)]
    )

    received = [None] * owners
    for d in range(size):
        for c in range(CORES):
            block = results[d * CORES + c]
            if d or c:
                block = send(block, owners, d, c)
            received[(-d) % size * CORES + c] = block
    out = pick_routes(route_labels.reshape(tokens * top, 1), received)
    return out.reshape(1, tokens, top, hidden)


def slotted_device(section_grad, route_ids, route_gates, weight_mat, capacity):
    tokens, top = route_ids.shape
    owners = lax.axis_size("expert")
    ids = jnp.arange(owners, dtype=jnp.int32)
    slots = jnp.arange(capacity, dtype=jnp.int32)
    matched = (route_ids[:, :, None] == ids[None, None, :]).astype(jnp.int32)
    hits = jnp.sum(matched, axis=1)
    rank = jnp.cumsum(hits, axis=0) - hits
    position = route_ids * capacity + jnp.sum(matched * rank[:, None, :], axis=2)
    gate_owner = jnp.einsum(
        "tk,tke->te", route_gates.astype(jnp.float32), matched.astype(jnp.float32)
    )
    slot_pick = (hits[:, :, None] == 1) & (rank[:, :, None] == slots[None, None, :])
    send_rows = jnp.einsum(
        "tem,td->emd",
        slot_pick.astype(jnp.bfloat16),
        section_grad,
        preferred_element_type=jnp.float32,
    ).astype(jnp.bfloat16)
    send_gates = jnp.einsum("tem,te->em", slot_pick.astype(jnp.float32), gate_owner).astype(
        jnp.bfloat16
    )
    got_rows = lax.all_to_all(send_rows, "expert", split_axis=0, concat_axis=0, tiled=True)
    got_gates = lax.all_to_all(send_gates, "expert", split_axis=0, concat_axis=0, tiled=True)
    product = lax.dot_general(
        got_rows.reshape(owners * capacity, got_rows.shape[2]),
        weight_mat,
        (((1,), (1,)), ((), ())),
        preferred_element_type=jnp.float32,
    ).reshape(owners, capacity, weight_mat.shape[0])
    returned = lax.all_to_all(
        (product * got_gates.astype(jnp.float32)[:, :, None]).astype(jnp.bfloat16),
        "expert",
        split_axis=0,
        concat_axis=0,
        tiled=True,
    )
    flat = returned.reshape(owners * capacity, returned.shape[2])
    out = jnp.take(flat, position.reshape(tokens * top), axis=0)
    return out.reshape(1, tokens, top, returned.shape[2])


def per_device(upstream, expert_ids, gate_weights, expert_weight):
    section_grad = shifted(upstream, "pipe", -1)[0]
    route_ids = expert_ids[0]
    route_gates = gate_weights[0]
    weight_mat = expert_weight[0, 0]
    tokens, top = route_ids.shape
    owners = lax.axis_size("expert")
    capacity = 2 * tokens * top // owners
    if capacity >= tokens:
        return dense_device(section_grad, route_ids, route_gates, weight_mat)
    return slotted_device(section_grad, route_ids, route_gates, weight_mat, capacity)


def solution(mesh):
    in_specs = (
        P("pipe", "expert", None),
        P("pipe", "expert", None),
        P("pipe", "expert", None),
        P("pipe", "expert", None, None),
    )
    out_specs = P("pipe", "expert", None, None)
    return jax.shard_map(
        per_device, mesh=mesh, in_specs=in_specs, out_specs=out_specs, check_vma=False
    )
```

time: 170 us -> 107 us (0.63)
  the two profiles are of different devices: /device:TPU:11 before, /device:TPU:0 now
where the time goes in v2:
time: 107 us; the launch traced here: 106 us
  starting transfers between devices  44.1 us (41%)
  waiting for transfers between devices  28.6 us (27%)
  local copies, waits for them, and re-layouts  17.9 us (17%)
  Pallas kernels  11.1 us (10%)
  other arithmetic  3.94 us (4%)
    ppermute x32, starting transfers between devices, send(): return lax.ppermute(block, 'expert', ring_route(owners, distance, flip))  35.3 us
    ppermute x32, waiting for transfers between devices, send(): return lax.ppermute(block, 'expert', ring_route(owners, distance, flip))  28.6 us
    pallas_call x5, Pallas kernels, expert_rows(): pl.pallas_call(functools.partial(expert_kernel, len(rows)), out_shape=[ja...  9.75 us
    unnamed x38, local copies, waits for them, and re-layouts  8.4 us
    all_to_all x1, starting transfers between devices, dense_device(): lax.all_to_all(dense_gates, 'expert', split_axis=0, concat_axis=0, tiled=...  5.91 us
    ppermute x1, starting transfers between devices, shifted(): return lax.ppermute(block, axis, route)  2.97 us
    sub x2, local copies, waits for them, and re-layouts, dense_device(): place_of_chip[route_ids // CORES] - my_place  2.28 us
  transfers between devices with their start and end apart: 34, of which 8 were waited for; matrix products, arithmetic and copies ran while one was open for 13% of the time, Pallas kernels for 9%

profile of v2, /device:TPU:0, one launch (start us, length us, event | category | flops | bytes accessed | tf_op | source)
XLA Modules:
  0.0 105.9 jit_solution(13903265034690336758)
XLA Ops:
  0.0 3.0 %collective-permute-start = (bf16[1,64,2048]{2,1,0:T(8,128)(2,1)}, bf16[1,64,2048]{2,1,0:T(8,128)(2,1)S(1)}, u32[]{:S(2)}, u32[]{:S(2)}) collective-permute-start(bf16[1,64,2048]{2,1,0:T(8,128)(2,1)} %param.6), channel_id=1, source_target_pairs={{16,0},{0,16},{17,1},{1,17},{18,2},{2,18},{19,3},{3,19},{20,4},{4,... | collective-permute-start | bytes 786440 | tf_op jit(solution)/shard_map/ppermute | solution.py:17
  3.0 0.7 bitcast_convert_fusion
  3.7 0.7 select_reduce_fusion
  4.4 0.6 copy.72
  5.0 5.9 %all-to-all-start = ((bf16[16,1,64]{2,1,0:T(2,128)(2,1)}), bf16[16,1,64]{2,1,0:T(2,128)(2,1)S(1)}, u32[]{:S(2)}, u32[]{:S(2)}) async-start(bf16[16,1,64]{2,1,0:T(2,128)(2,1)} %copy.72), calls=%async_computation | async-start | bytes 16384 | tf_op jit(solution)/shard_map/all_to_all | solution.py:109
  10.9 1.3 %dynamic_slice.3 = s32[1]{0:T(128)} dynamic-slice(s32[8]{0:T(128)} %constant.112.clone, s32[]{:T(128)S(6)} %select_n.138), dynamic_slice_sizes={1} | dynamic-slice | bytes 12 | tf_op jit(solution)/shard_map/dynamic_slice | solution.py:103
  12.2 0.6 fusion.15
  12.9 1.3 %gather_fusion = s32[16]{0:T(128)S(1)} fusion(s32[8]{0:T(128)} %constant.113.clone, s32[1024]{0:T(1024)S(1)} %pad_clamp_fusion.1), kind=kCustom, calls=%fused_computation | custom fusion | bytes 192 | tf_op jit(solution)/shard_map/gather | solution.py:112
  14.2 1.9 %collective-permute-start.3 = (bf16[64,2048]{1,0:T(8,128)(2,1)S(1)}, bf16[64,2048]{1,0:T(8,128)(2,1)}, u32[]{:S(2)}, u32[]{:S(2)}) collective-permute-start(bf16[64,2048]{1,0:T(8,128)(2,1)S(1)} %bitcast.53), channel_id=1, source_target_pairs={{0,4},{1,5},{4,8},{5,9},{8,12},{9,13},{12,14},{13,15},{14,10},{15,... | collective-permute-start | bytes 786440 | tf_op jit(solution)/shard_map/ppermute | solution.py:38
  16.3 6.6 %collective-permute-done.3.refs_0_ = bf16[64,2048]{1,0:T(8,128)(2,1)} collective-permute-done((bf16[64,2048]{1,0:T(8,128)(2,1)S(1)}, bf16[64,2048]{1,0:T(8,128)(2,1)}, u32[]{:S(2)}, u32[]{:S(2)}) %collective-permute-start.3) | collective-permute-done | bytes 262176 | tf_op jit(solution)/shard_map/ppermute | solution.py:38
  23.0 1.7 %collective-permute-start.9 = (bf16[64,2048]{1,0:T(8,128)(2,1)}, bf16[64,2048]{1,0:T(8,128)(2,1)}, u32[]{:S(2)}, u32[]{:S(2)}) collective-permute-start(bf16[64,2048]{1,0:T(8,128)(2,1)} %collective-permute-done.3.refs_0_), channel_id=1, source_target_pairs={{0,4},{1,5},{4,8},{5,9},{8,12},{9,13},{12,14},{13,15},{14,10},{15,... | collective-permute-start | bytes 786440 | tf_op jit(solution)/shard_map/ppermute | solution.py:38
  24.6 0.4 collective-permute-start.11
  25.0 0.6 gather_fusion.1
  25.8 0.5 collective-permute-start.4
  26.4 4.7 %collective-permute-done.9.refs_0_ = bf16[64,2048]{1,0:T(8,128)(2,1)} collective-permute-done((bf16[64,2048]{1,0:T(8,128)(2,1)}, bf16[64,2048]{1,0:T(8,128)(2,1)}, u32[]{:S(2)}, u32[]{:S(2)}) %collective-permute-start.9) | collective-permute-done | bytes 262176 | tf_op jit(solution)/shard_map/ppermute | solution.py:38
  31.1 1.4 %collective-permute-start.15 = (bf16[64,2048]{1,0:T(8,128)(2,1)}, bf16[64,2048]{1,0:T(8,128)(2,1)S(1)}, u32[]{:S(2)}, u32[]{:S(2)}) collective-permute-start(bf16[64,2048]{1,0:T(8,128)(2,1)} %collective-permute-done.9.refs_0_), channel_id=1, source_target_pairs={{0,4},{1,5},{4,8},{5,9},{8,12},{9,13},{12,14},{13,15},{14,10},{15,... | collective-permute-start | bytes 786440 | tf_op jit(solution)/shard_map/ppermute | solution.py:38
  32.5 0.6 collective-permute-start.17
  33.1 0.8 fusion.17
  34.0 1.9 %copy-done = bf16[1,1,768,2048]{3,2,1,0:T(8,128)(2,1)S(1)} copy-done((bf16[1,1,768,2048]{3,2,1,0:T(8,128)(2,1)S(1)}, bf16[1,1,768,2048]{3,2,1,0:T(8,128)(2,1)}, u32[]{:S(2)}) %copy-start) | copy-done | bytes 3145752
  35.9 0.9 copy-done.3
  36.8 1.2 %shard_map.64 = (bf16[64,768]{1,0:T(8,128)(2,1)S(1)}, bf16[64,768]{1,0:T(8,128)(2,1)S(1)}) custom-call(bf16[64,2048]{1,0:T(8,128)(2,1)S(1)} %bitcast.56, bf16[64,2048]{1,0:T(8,128)(2,1)S(1)} %collective-permute-done.1.refs_1_, bf16[768,2048]{1,0:T(8,128)(2,1)S(1)} %bitcast.48, f32[64,2]{1,0:T(8,128)S(1)} %get-tuple-element.44.refs_3_), custom_call_target="tpu_custom_call" | custom-call | flops 402653184 | bytes 3866624 | tf_op jit(solution)/shard_map/pallas_call | solution.py:57
  38.0 0.2 collective-permute-done.15.refs_0_
  38.2 0.4 collective-permute-start.2
  38.6 0.6 collective-permute-done.17.refs_2_
  39.2 1.5 %collective-permute-start.21 = (bf16[32,2048]{1,0:T(8,128)(2,1)S(1)}, bf16[32,2048]{1,0:T(8,128)(2,1)}, u32[]{:S(2)}, u32[]{:S(2)}) collective-permute-start(bf16[32,2048]{1,0:T(8,128)(2,1)S(1)} %slice.69), channel_id=1, source_target_pairs={{0,4},{1,5},{4,8},{5,9},{8,12},{9,13},{12,14},{13,15},{14,10},{15,... | collective-permute-start | bytes 393224 | tf_op jit(solution)/shard_map/ppermute | solution.py:38
  40.6 0.9 slice.70
  41.6 0.6 collective-permute-start.22
  42.2 2.0 %shard_map.65 = (bf16[64,768]{1,0:T(8,128)(2,1)S(1)}, bf16[64,768]{1,0:T(8,128)(2,1)S(1)}, bf16[64,768]{1,0:T(8,128)(2,1)S(1)}, bf16[64,768]{1,0:T(8,128)(2,1)S(1)}) custom-call(bf16[64,2048]{1,0:T(8,128)(2,1)} %collective-permute-done.3.refs_0_, bf16[64,2048]{1,0:T(8,128)(2,1)S(1)} %collective-permute-done.4.refs_1_, ...), custom_call_target="tpu_custom_call" | custom-call | flops 805306368 | bytes 4587520 | tf_op jit(solution)/shard_map/pallas_call | solution.py:57
  44.2 0.6 copy-done.10
  44.9 0.6 copy-done.11
  45.5 0.6 copy-done.12
  46.1 0.9 collective-permute-start.7
  47.0 0.6 copy-done.6
  47.7 3.1 %collective-permute-done.7.refs_2_ = bf16[64,768]{1,0:T(8,128)(2,1)S(1)} collective-permute-done((bf16[64,768]{1,0:T(8,128)(2,1)S(1)}, bf16[64,768]{1,0:T(8,128)(2,1)S(1)}, u32[]{:S(2)}, u32[]{:S(2)}) %collective-permute-start.7) | collective-permute-done | bytes 98336 | tf_op jit(solution)/shard_map/ppermute | solution.py:38
  50.7 0.6 copy-done.8
  51.4 0.7 copy-done.4
  52.1 0.5 collective-permute-start.18
  52.6 0.5 collective-permute-start.24
  53.1 0.6 fusion.6
  53.8 0.7 copy.68
  54.5 1.6 %squeeze.19 = s32[512,1]{1,0:T(8,128)} reshape(s32[1,64,8]{2,1,0:T(8,128)} %copy.68) | data formatting | bytes 4096 | tf_op jit(solution)/shard_map/squeeze | solution.py:200
  56.1 0.7 copy.64
  56.7 1.6 %sub.36 = s32[512,1]{1,0:T(8,128)} reshape(s32[64,8]{1,0:T(8,128)} %copy.64) | data formatting | bytes 4096 | tf_op jit(solution)/shard_map/sub | solution.py:115
  58.3 0.9 pad_maximum_fusion.1.refs_5_
  59.2 0.6 collective-permute-start.8
  59.8 1.1 %collective-permute-start.31 = (bf16[64,768]{1,0:T(8,128)(2,1)}, bf16[64,768]{1,0:T(8,128)(2,1)S(1)}, u32[]{:S(2)}, u32[]{:S(2)}) collective-permute-start(bf16[64,768]{1,0:T(8,128)(2,1)} %copy-done.11), channel_id=1, source_target_pairs={{0,4},{1,5},{4,8},{5,9},{8,12},{9,13},{12,14},{13,15},{14,10},{15,... | collective-permute-start | bytes 294920 | tf_op jit(solution)/shard_map/ppermute | solution.py:38
  60.9 1.2 %collective-permute-start.32 = (bf16[64,768]{1,0:T(8,128)(2,1)}, bf16[64,768]{1,0:T(8,128)(2,1)S(1)}, u32[]{:S(2)}, u32[]{:S(2)}) collective-permute-start(bf16[64,768]{1,0:T(8,128)(2,1)} %copy-done.10), channel_id=1, source_target_pairs={{0,5},{1,4},{4,9},{5,8},{8,13},{9,12},{12,15},{13,14},{14,11},{15,... | collective-permute-start | bytes 294920 | tf_op jit(solution)/shard_map/ppermute | solution.py:38
  62.2 0.9 copy-done.5
  63.1 2.1 %shard_map.66 = (bf16[64,768]{1,0:T(8,128)(2,1)S(1)}, bf16[64,768]{1,0:T(8,128)(2,1)S(1)}, bf16[64,768]{1,0:T(8,128)(2,1)S(1)}, bf16[64,768]{1,0:T(8,128)(2,1)S(1)}) custom-call(bf16[64,2048]{1,0:T(8,128)(2,1)} %collective-permute-done.9.refs_0_, bf16[64,2048]{1,0:T(8,128)(2,1)S(1)} %copy-done.5, bf16[64,2048]{1,0:T(8,128)(2,1)} %collective-permute-done.11.refs_2_, ...), custom_call_target="tpu_custom_call" | custom-call | flops 805306368 | bytes 4587520 | tf_op jit(solution)/shard_map/pallas_call | solution.py:57
  65.3 2.3 %shard_map.68 = (bf16[64,768]{1,0:T(8,128)(2,1)S(1)}, bf16[64,768]{1,0:T(8,128)(2,1)S(1)}) custom-call(bf16[32,2048]{1,0:T(8,128)(2,1)} %collective-permute-done.21.refs_0_, bf16[32,2048]{1,0:T(8,128)(2,1)} %collective-permute-done.22.refs_1_, bf16[32,2048]{1,0:T(8,128)(2,1)} %collective-permute-done.23.refs_2_, ...), custom_call_target="tpu_custom_call" | custom-call | flops 402653184 | bytes 3866624 | tf_op jit(solution)/shard_map/pallas_call | solution.py:57
  67.6 0.9 collective-permute-start.13
  68.6 2.0 %collective-permute-start.14 = (bf16[64,768]{1,0:T(8,128)(2,1)S(1)}, bf16[64,768]{1,0:T(8,128)(2,1)S(1)}, u32[]{:S(2)}, u32[]{:S(2)}) collective-permute-start(bf16[64,768]{1,0:T(8,128)(2,1)S(1)} %get-tuple-element.26), channel_id=1, source_target_pairs={{0,7},{1,6},{4,3},{5,2},{8,1},{9,0},{12,5},{13,4},{14,9},{15,8},{1... | collective-permute-start | bytes 294920 | tf_op jit(solution)/shard_map/ppermute | solution.py:38
  70.6 0.6 collective-permute-start.29
  71.2 1.8 %collective-permute-start.30 = (bf16[64,768]{1,0:T(8,128)(2,1)S(1)}, bf16[64,768]{1,0:T(8,128)(2,1)S(1)}, u32[]{:S(2)}, u32[]{:S(2)}) collective-permute-start(bf16[64,768]{1,0:T(8,128)(2,1)S(1)} %get-tuple-element.34), channel_id=1, source_target_pairs={{0,9},{1,8},{4,13},{5,12},{8,15},{9,14},{12,11},{13,10},{14,7},{15... | collective-permute-start | bytes 294920 | tf_op jit(solution)/shard_map/ppermute | solution.py:38
  73.0 2.7 %collective-permute-start.25 = (bf16[64,768]{1,0:T(8,128)(2,1)S(1)}, bf16[64,768]{1,0:T(8,128)(2,1)S(1)}, u32[]{:S(2)}, u32[]{:S(2)}) collective-permute-start(bf16[64,768]{1,0:T(8,128)(2,1)S(1)} %get-tuple-element.29), channel_id=1, source_target_pairs={{0,14},{1,15},{4,10},{5,11},{8,6},{9,7},{12,2},{13,3},{14,0},{15,1... | collective-permute-start | bytes 294920 | tf_op jit(solution)/shard_map/ppermute | solution.py:38
  75.8 2.1 %shard_map.67 = (bf16[64,768]{1,0:T(8,128)(2,1)S(1)}, bf16[64,768]{1,0:T(8,128)(2,1)S(1)}, bf16[64,768]{1,0:T(8,128)(2,1)S(1)}, bf16[64,768]{1,0:T(8,128)(2,1)S(1)}) custom-call(bf16[64,2048]{1,0:T(8,128)(2,1)S(1)} %collective-permute-done.15.refs_0_, bf16[64,2048]{1,0:T(8,128)(2,1)} %collective-permute-done.16.refs_1_, ...), custom_call_target="tpu_custom_call" | custom-call | flops 805306368 | bytes 4587520 | tf_op jit(solution)/shard_map/pallas_call | solution.py:57
  77.9 0.5 collective-permute-done.13.refs_4_
  78.4 1.7 %collective-permute-start.26 = (bf16[64,768]{1,0:T(8,128)(2,1)S(1)}, bf16[64,768]{1,0:T(8,128)(2,1)S(1)}, u32[]{:S(2)}, u32[]{:S(2)}) collective-permute-start(bf16[64,768]{1,0:T(8,128)(2,1)S(1)} %get-tuple-element.30), channel_id=1, source_target_pairs={{0,15},{1,14},{4,11},{5,10},{8,7},{9,6},{12,3},{13,2},{14,1},{15,0... | collective-permute-start | bytes 294920 | tf_op jit(solution)/shard_map/ppermute | solution.py:38
  80.1 1.3 %collective-permute-start.20 = (bf16[64,768]{1,0:T(8,128)(2,1)S(1)}, bf16[64,768]{1,0:T(8,128)(2,1)S(1)}, u32[]{:S(2)}, u32[]{:S(2)}) collective-permute-start(bf16[64,768]{1,0:T(8,128)(2,1)S(1)} %get-tuple-element.28), channel_id=1, source_target_pairs={{0,11},{1,10},{4,7},{5,6},{8,3},{9,2},{12,1},{13,0},{14,5},{15,4},... | collective-permute-start | bytes 294920 | tf_op jit(solution)/shard_map/ppermute | solution.py:38
  81.5 10.0 %collective-permute-start.27 = (bf16[64,768]{1,0:T(8,128)(2,1)S(1)}, bf16[64,768]{1,0:T(8,128)(2,1)S(1)}, u32[]{:S(2)}, u32[]{:S(2)}) collective-permute-start(bf16[64,768]{1,0:T(8,128)(2,1)S(1)} %get-tuple-element.31), channel_id=1, source_target_pairs={{0,12},{1,13},{4,14},{5,15},{8,10},{9,11},{12,6},{13,7},{14,2},{15... | collective-permute-start | bytes 294920 | tf_op jit(solution)/shard_map/ppermute | solution.py:38
  91.5 0.2 fusion.2.labels_ref
  91.8 11.6 %collective-permute-done.27.refs_10_ = bf16[64,768]{1,0:T(8,128)(2,1)S(1)} collective-permute-done((bf16[64,768]{1,0:T(8,128)(2,1)S(1)}, bf16[64,768]{1,0:T(8,128)(2,1)S(1)}, u32[]{:S(2)}, u32[]{:S(2)}) %collective-permute-start.27) | collective-permute-done | bytes 98336 | tf_op jit(solution)/shard_map/ppermute | solution.py:38
  103.4 1.2 %collective-permute-done.28.refs_11_ = bf16[64,768]{1,0:T(8,128)(2,1)S(1)} collective-permute-done((bf16[64,768]{1,0:T(8,128)(2,1)S(1)}, bf16[64,768]{1,0:T(8,128)(2,1)S(1)}, u32[]{:S(2)}, u32[]{:S(2)}) %collective-permute-start.28) | collective-permute-done | bytes 98336 | tf_op jit(solution)/shard_map/ppermute | solution.py:38
  104.6 1.3 %shard_map.69 = bf16[512,768]{1,0:T(8,128)(2,1)} custom-call(s32[512,1]{1,0:T(8,128)S(1)} %fusion.2.labels_ref, bf16[64,768]{1,0:T(8,128)(2,1)S(1)} %get-tuple-element.21.refs_0_, bf16[64,768]{1,0:T(8,128)(2,1)S(1)} %copy-done.7, bf16[64,768]{1,0:T(8,128)(2,1)S(1)} %copy-done.9, bf16[64,768]{1,0:T(8,128)(2,1)S(1)} %collective-permute-done.8.refs_3_, ...), custom_call_target="tpu_custom_call" | custom-call | tf_op jit(solution)/shard_map/pallas_call | solution.py:87
  (72 shorter events, 0.7 us)
Async XLA Ops:
  0.0 14.2 %collective-permute-start = (bf16[1,64,2048]{2,1,0:T(8,128)(2,1)}, bf16[1,64,2048]{2,1,0:T(8,128)(2,1)S(1)}, u32[]{:S(2)}, u32[]{:S(2)}) collective-permute-start(bf16[1,64,2048]{2,1,0:T(8,128)(2,1)} %param.6), channel_id=1, source_target_pairs={{16,0},{0,16},{17,1},{1,17},{18,2},{2,18},{19,3},{3,19},{20,4},{4,... | collective-permute-start | bytes 786440 | tf_op jit(solution)/shard_map/ppermute | solution.py:17
  5.0 20.0 %all-to-all-start = ((bf16[16,1,64]{2,1,0:T(2,128)(2,1)}), bf16[16,1,64]{2,1,0:T(2,128)(2,1)S(1)}, u32[]{:S(2)}, u32[]{:S(2)}) async-start(bf16[16,1,64]{2,1,0:T(2,128)(2,1)} %copy.72), calls=%async_computation | async-start | bytes 16384 | tf_op jit(solution)/shard_map/all_to_all | solution.py:109
  14.2 19.8 %copy-start.2 = (bf16[1,64,2048]{2,1,0:T(8,128)(2,1)}, bf16[1,64,2048]{2,1,0:T(8,128)(2,1)S(1)}, u32[]{:S(2)}) copy-start(bf16[1,64,2048]{2,1,0:T(8,128)(2,1)S(1)} %collective-permute-done) | copy-start | bytes 786436
  14.2 8.8 %collective-permute-start.3 = (bf16[64,2048]{1,0:T(8,128)(2,1)S(1)}, bf16[64,2048]{1,0:T(8,128)(2,1)}, u32[]{:S(2)}, u32[]{:S(2)}) collective-permute-start(bf16[64,2048]{1,0:T(8,128)(2,1)S(1)} %bitcast.53), channel_id=1, source_target_pairs={{0,4},{1,5},{4,8},{5,9},{8,12},{9,13},{12,14},{13,15},{14,10},{15,... | collective-permute-start | bytes 786440 | tf_op jit(solution)/shard_map/ppermute | solution.py:38
  16.2 8.5 %collective-permute-start.5 = (bf16[64,2048]{1,0:T(8,128)(2,1)S(1)}, bf16[64,2048]{1,0:T(8,128)(2,1)}, u32[]{:S(2)}, u32[]{:S(2)}) collective-permute-start(bf16[64,2048]{1,0:T(8,128)(2,1)S(1)} %bitcast.54), channel_id=1, source_target_pairs={{0,2},{1,3},{4,0},{5,1},{8,4},{9,5},{12,8},{13,9},{14,12},{15,13},... | collective-permute-start | bytes 786440 | tf_op jit(solution)/shard_map/ppermute | solution.py:38
  23.0 8.1 %collective-permute-start.9 = (bf16[64,2048]{1,0:T(8,128)(2,1)}, bf16[64,2048]{1,0:T(8,128)(2,1)}, u32[]{:S(2)}, u32[]{:S(2)}) collective-permute-start(bf16[64,2048]{1,0:T(8,128)(2,1)} %collective-permute-done.3.refs_0_), channel_id=1, source_target_pairs={{0,4},{1,5},{4,8},{5,9},{8,12},{9,13},{12,14},{13,15},{14,10},{15,... | collective-permute-start | bytes 786440 | tf_op jit(solution)/shard_map/ppermute | solution.py:38
  24.6 7.8 %collective-permute-start.11 = (bf16[64,2048]{1,0:T(8,128)(2,1)}, bf16[64,2048]{1,0:T(8,128)(2,1)}, u32[]{:S(2)}, u32[]{:S(2)}) collective-permute-start(bf16[64,2048]{1,0:T(8,128)(2,1)} %collective-permute-done.5.refs_2_), channel_id=1, source_target_pairs={{0,2},{1,3},{4,0},{5,1},{8,4},{9,5},{12,8},{13,9},{14,12},{15,13},... | collective-permute-start | bytes 786440 | tf_op jit(solution)/shard_map/ppermute | solution.py:38
  25.7 8.2 %collective-permute-start.1 = (bf16[64,2048]{1,0:T(8,128)(2,1)S(1)}, bf16[64,2048]{1,0:T(8,128)(2,1)S(1)}, u32[]{:S(2)}, u32[]{:S(2)}) collective-permute-start(bf16[64,2048]{1,0:T(8,128)(2,1)S(1)} %bitcast.55), channel_id=1, source_target_pairs={{0,1},{1,0},{4,5},{5,4},{8,9},{9,8},{12,13},{13,12},{14,15},{15,14... | collective-permute-start | bytes 786440 | tf_op jit(solution)/shard_map/ppermute | solution.py:38
  25.8 15.8 %collective-permute-start.4 = (bf16[64,2048]{1,0:T(8,128)(2,1)}, bf16[64,2048]{1,0:T(8,128)(2,1)S(1)}, u32[]{:S(2)}, u32[]{:S(2)}) collective-permute-start(bf16[64,2048]{1,0:T(8,128)(2,1)} %collective-permute-done.3.refs_0_), channel_id=1, source_target_pairs={{0,1},{1,0},{4,5},{5,4},{8,9},{9,8},{12,13},{13,12},{14,15},{15,14... | collective-permute-start | bytes 786440 | tf_op jit(solution)/shard_map/ppermute | solution.py:38
  26.3 15.9 %collective-permute-start.6 = (bf16[64,2048]{1,0:T(8,128)(2,1)}, bf16[64,2048]{1,0:T(8,128)(2,1)S(1)}, u32[]{:S(2)}, u32[]{:S(2)}) collective-permute-start(bf16[64,2048]{1,0:T(8,128)(2,1)} %collective-permute-done.5.refs_2_), channel_id=1, source_target_pairs={{0,1},{1,0},{4,5},{5,4},{8,9},{9,8},{12,13},{13,12},{14,15},{15,14... | collective-permute-start | bytes 786440 | tf_op jit(solution)/shard_map/ppermute | solution.py:38
  31.1 7.1 %collective-permute-start.15 = (bf16[64,2048]{1,0:T(8,128)(2,1)}, bf16[64,2048]{1,0:T(8,128)(2,1)S(1)}, u32[]{:S(2)}, u32[]{:S(2)}) collective-permute-start(bf16[64,2048]{1,0:T(8,128)(2,1)} %collective-permute-done.9.refs_0_), channel_id=1, source_target_pairs={{0,4},{1,5},{4,8},{5,9},{8,12},{9,13},{12,14},{13,15},{14,10},{15,... | collective-permute-start | bytes 786440 | tf_op jit(solution)/shard_map/ppermute | solution.py:38
  32.5 6.7 %collective-permute-start.17 = (bf16[64,2048]{1,0:T(8,128)(2,1)}, bf16[64,2048]{1,0:T(8,128)(2,1)}, u32[]{:S(2)}, u32[]{:S(2)}) collective-permute-start(bf16[64,2048]{1,0:T(8,128)(2,1)} %collective-permute-done.11.refs_2_), channel_id=1, source_target_pairs={{0,2},{1,3},{4,0},{5,1},{8,4},{9,5},{12,8},{13,9},{14,12},{15,13},... | collective-permute-start | bytes 786440 | tf_op jit(solution)/shard_map/ppermute | solution.py:38
  33.9 17.5 %collective-permute-start.10 = (bf16[64,2048]{1,0:T(8,128)(2,1)}, bf16[64,2048]{1,0:T(8,128)(2,1)S(1)}, u32[]{:S(2)}, u32[]{:S(2)}) collective-permute-start(bf16[64,2048]{1,0:T(8,128)(2,1)} %collective-permute-done.9.refs_0_), channel_id=1, source_target_pairs={{0,1},{1,0},{4,5},{5,4},{8,9},{9,8},{12,13},{13,12},{14,15},{15,14... | collective-permute-start | bytes 786440 | tf_op jit(solution)/shard_map/ppermute | solution.py:38
  34.0 1.9 %copy-start = (bf16[1,1,768,2048]{3,2,1,0:T(8,128)(2,1)S(1)}, bf16[1,1,768,2048]{3,2,1,0:T(8,128)(2,1)}, u32[]{:S(2)}) copy-start(bf16[1,1,768,2048]{3,2,1,0:T(8,128)(2,1)} %param.9) | copy-start | bytes 9437188
  35.8 0.9 copy-start.3
  36.8 5.4 %copy-start.1 = (bf16[1,1,768,2048]{3,2,1,0:T(8,128)(2,1)S(1)}, bf16[1,1,768,2048]{3,2,1,0:T(8,128)(2,1)}, u32[]{:S(2)}) copy-start(bf16[1,1,768,2048]{3,2,1,0:T(8,128)(2,1)} %param.9) | copy-start | bytes 9437188
  38.0 15.1 %copy-start.17 = (s32[1,64,8]{1,2,0:T(8,128)S(1)}, s32[1,64,8]{1,2,0:T(8,128)}, u32[]{:S(2)}) copy-start(s32[1,64,8]{1,2,0:T(8,128)} %param.7) | copy-start | bytes 6148
  38.2 8.9 %collective-permute-start.2 = (bf16[64,768]{1,0:T(8,128)(2,1)S(1)}, bf16[64,768]{1,0:T(8,128)(2,1)S(1)}, u32[]{:S(2)}, u32[]{:S(2)}) collective-permute-start(bf16[64,768]{1,0:T(8,128)(2,1)S(1)} %get-tuple-element.22), channel_id=1, source_target_pairs={{0,1},{1,0},{4,5},{5,4},{8,9},{9,8},{12,13},{13,12},{14,15},{15,14... | collective-permute-start | bytes 294920 | tf_op jit(solution)/shard_map/ppermute | solution.py:38
  39.2 13.4 %collective-permute-start.21 = (bf16[32,2048]{1,0:T(8,128)(2,1)S(1)}, bf16[32,2048]{1,0:T(8,128)(2,1)}, u32[]{:S(2)}, u32[]{:S(2)}) collective-permute-start(bf16[32,2048]{1,0:T(8,128)(2,1)S(1)} %slice.69), channel_id=1, source_target_pairs={{0,4},{1,5},{4,8},{5,9},{8,12},{9,13},{12,14},{13,15},{14,10},{15,... | collective-permute-start | bytes 393224 | tf_op jit(solution)/shard_map/ppermute | solution.py:38
  41.6 11.0 %collective-permute-start.22 = (bf16[32,2048]{1,0:T(8,128)(2,1)S(1)}, bf16[32,2048]{1,0:T(8,128)(2,1)}, u32[]{:S(2)}, u32[]{:S(2)}) collective-permute-start(bf16[32,2048]{1,0:T(8,128)(2,1)S(1)} %slice.70), channel_id=1, source_target_pairs={{0,2},{1,3},{4,0},{5,1},{8,4},{9,5},{12,8},{13,9},{14,12},{15,13},... | collective-permute-start | bytes 393224 | tf_op jit(solution)/shard_map/ppermute | solution.py:38
  44.2 0.6 copy-start.10
  44.9 0.6 copy-start.11
  45.5 0.6 copy-start.12
  46.1 4.6 %collective-permute-start.7 = (bf16[64,768]{1,0:T(8,128)(2,1)S(1)}, bf16[64,768]{1,0:T(8,128)(2,1)S(1)}, u32[]{:S(2)}, u32[]{:S(2)}) collective-permute-start(bf16[64,768]{1,0:T(8,128)(2,1)S(1)} %get-tuple-element.23), channel_id=1, source_target_pairs={{0,2},{1,3},{4,0},{5,1},{8,4},{9,5},{12,8},{13,9},{14,12},{15,13},... | collective-permute-start | bytes 294920 | tf_op jit(solution)/shard_map/ppermute | solution.py:38
  47.0 0.6 copy-start.6
  47.6 11.5 %collective-permute-start.12 = (bf16[64,2048]{1,0:T(8,128)(2,1)}, bf16[64,2048]{1,0:T(8,128)(2,1)}, u32[]{:S(2)}, u32[]{:S(2)}) collective-permute-start(bf16[64,2048]{1,0:T(8,128)(2,1)} %collective-permute-done.11.refs_2_), channel_id=1, source_target_pairs={{0,1},{1,0},{4,5},{5,4},{8,9},{9,8},{12,13},{13,12},{14,15},{15,14... | collective-permute-start | bytes 786440 | tf_op jit(solution)/shard_map/ppermute | solution.py:38
  50.7 0.6 copy-start.8
  51.4 19.8 %collective-permute-start.16 = (bf16[64,2048]{1,0:T(8,128)(2,1)S(1)}, bf16[64,2048]{1,0:T(8,128)(2,1)}, u32[]{:S(2)}, u32[]{:S(2)}) collective-permute-start(bf16[64,2048]{1,0:T(8,128)(2,1)S(1)} %collective-permute-done.15.refs_0_), channel_id=1, source_target_pairs={{0,1},{1,0},{4,5},{5,4},{8,9},{9,8},{12,13},{13,12},{14,15},{15,14... | collective-permute-start | bytes 786440 | tf_op jit(solution)/shard_map/ppermute | solution.py:38
  51.4 0.7 copy-start.4
  52.1 20.9 %collective-permute-start.18 = (bf16[64,2048]{1,0:T(8,128)(2,1)}, bf16[64,2048]{1,0:T(8,128)(2,1)}, u32[]{:S(2)}, u32[]{:S(2)}) collective-permute-start(bf16[64,2048]{1,0:T(8,128)(2,1)} %collective-permute-done.17.refs_2_), channel_id=1, source_target_pairs={{0,1},{1,0},{4,5},{5,4},{8,9},{9,8},{12,13},{13,12},{14,15},{15,14... | collective-permute-start | bytes 786440 | tf_op jit(solution)/shard_map/ppermute | solution.py:38
  52.6 7.2 %collective-permute-start.23 = (bf16[32,2048]{1,0:T(8,128)(2,1)}, bf16[32,2048]{1,0:T(8,128)(2,1)}, u32[]{:S(2)}, u32[]{:S(2)}) collective-permute-start(bf16[32,2048]{1,0:T(8,128)(2,1)} %collective-permute-done.21.refs_0_), channel_id=1, source_target_pairs={{0,1},{1,0},{4,5},{5,4},{8,9},{9,8},{12,13},{13,12},{14,15},{15,14... | collective-permute-start | bytes 393224 | tf_op jit(solution)/shard_map/ppermute | solution.py:38
  52.6 8.3 %collective-permute-start.24 = (bf16[32,2048]{1,0:T(8,128)(2,1)}, bf16[32,2048]{1,0:T(8,128)(2,1)}, u32[]{:S(2)}, u32[]{:S(2)}) collective-permute-start(bf16[32,2048]{1,0:T(8,128)(2,1)} %collective-permute-done.22.refs_1_), channel_id=1, source_target_pairs={{0,1},{1,0},{4,5},{5,4},{8,9},{9,8},{12,13},{13,12},{14,15},{15,14... | collective-permute-start | bytes 393224 | tf_op jit(solution)/shard_map/ppermute | solution.py:38
  59.2 8.4 %collective-permute-start.8 = (bf16[64,768]{1,0:T(8,128)(2,1)}, bf16[64,768]{1,0:T(8,128)(2,1)S(1)}, u32[]{:S(2)}, u32[]{:S(2)}) collective-permute-start(bf16[64,768]{1,0:T(8,128)(2,1)} %copy-done.12), channel_id=1, source_target_pairs={{0,3},{1,2},{4,1},{5,0},{8,5},{9,4},{12,9},{13,8},{14,13},{15,12},... | collective-permute-start | bytes 294920 | tf_op jit(solution)/shard_map/ppermute | solution.py:38
  59.8 8.8 %collective-permute-start.31 = (bf16[64,768]{1,0:T(8,128)(2,1)}, bf16[64,768]{1,0:T(8,128)(2,1)S(1)}, u32[]{:S(2)}, u32[]{:S(2)}) collective-permute-start(bf16[64,768]{1,0:T(8,128)(2,1)} %copy-done.11), channel_id=1, source_target_pairs={{0,4},{1,5},{4,8},{5,9},{8,12},{9,13},{12,14},{13,15},{14,10},{15,... | collective-permute-start | bytes 294920 | tf_op jit(solution)/shard_map/ppermute | solution.py:38
  60.9 9.7 %collective-permute-start.32 = (bf16[64,768]{1,0:T(8,128)(2,1)}, bf16[64,768]{1,0:T(8,128)(2,1)S(1)}, u32[]{:S(2)}, u32[]{:S(2)}) collective-permute-start(bf16[64,768]{1,0:T(8,128)(2,1)} %copy-done.10), channel_id=1, source_target_pairs={{0,5},{1,4},{4,9},{5,8},{8,13},{9,12},{12,15},{13,14},{14,11},{15,... | collective-permute-start | bytes 294920 | tf_op jit(solution)/shard_map/ppermute | solution.py:38
  62.2 0.9 copy-start.5
  63.1 12.5 %copy-start.15 = (f32[64,2]{1,0:T(8,128)S(1)}, f32[64,2]{1,0:T(8,128)}, u32[]{:S(2)}) copy-start(f32[64,2]{1,0:T(8,128)} %get-tuple-element.38) | copy-start | bytes 1540
  63.1 12.5 %copy-start.16 = (f32[64,2]{1,0:T(8,128)S(1)}, f32[64,2]{1,0:T(8,128)}, u32[]{:S(2)}) copy-start(f32[64,2]{1,0:T(8,128)} %get-tuple-element.39) | copy-start | bytes 1540
  65.3 26.2 %copy-start.13 = (s32[512,1]{1,0:T(8,128)S(1)}, s32[512,1]{1,0:T(8,128)}, u32[]{:S(2)}) copy-start(s32[512,1]{1,0:T(8,128)} %squeeze.19) | copy-start | bytes 6148
  65.3 26.2 %copy-start.14 = (s32[512,1]{1,0:T(8,128)S(1)}, s32[512,1]{1,0:T(8,128)}, u32[]{:S(2)}) copy-start(s32[512,1]{1,0:T(8,128)} %sub.36) | copy-start | bytes 6148
  67.6 37.0 %copy-start.7 = (bf16[64,768]{1,0:T(8,128)(2,1)S(1)}, bf16[64,768]{1,0:T(8,128)(2,1)}, u32[]{:S(2)}) copy-start(bf16[64,768]{1,0:T(8,128)(2,1)} %copy-done.6) | copy-start | bytes 294916
  67.6 37.0 %copy-start.9 = (bf16[64,768]{1,0:T(8,128)(2,1)S(1)}, bf16[64,768]{1,0:T(8,128)(2,1)}, u32[]{:S(2)}) copy-start(bf16[64,768]{1,0:T(8,128)(2,1)} %copy-done.8) | copy-start | bytes 294916
  67.6 10.8 %collective-permute-start.13 = (bf16[64,768]{1,0:T(8,128)(2,1)S(1)}, bf16[64,768]{1,0:T(8,128)(2,1)S(1)}, u32[]{:S(2)}, u32[]{:S(2)}) collective-permute-start(bf16[64,768]{1,0:T(8,128)(2,1)S(1)} %get-tuple-element.25), channel_id=1, source_target_pairs={{0,6},{1,7},{4,2},{5,3},{8,0},{9,1},{12,4},{13,5},{14,8},{15,9},{1... | collective-permute-start | bytes 294920 | tf_op jit(solution)/shard_map/ppermute | solution.py:38
  68.6 11.6 %collective-permute-start.14 = (bf16[64,768]{1,0:T(8,128)(2,1)S(1)}, bf16[64,768]{1,0:T(8,128)(2,1)S(1)}, u32[]{:S(2)}, u32[]{:S(2)}) collective-permute-start(bf16[64,768]{1,0:T(8,128)(2,1)S(1)} %get-tuple-element.26), channel_id=1, source_target_pairs={{0,7},{1,6},{4,3},{5,2},{8,1},{9,0},{12,5},{13,4},{14,9},{15,8},{1... | collective-permute-start | bytes 294920 | tf_op jit(solution)/shard_map/ppermute | solution.py:38
  70.6 9.5 %collective-permute-start.29 = (bf16[64,768]{1,0:T(8,128)(2,1)S(1)}, bf16[64,768]{1,0:T(8,128)(2,1)S(1)}, u32[]{:S(2)}, u32[]{:S(2)}) collective-permute-start(bf16[64,768]{1,0:T(8,128)(2,1)S(1)} %get-tuple-element.33), channel_id=1, source_target_pairs={{0,8},{1,9},{4,12},{5,13},{8,14},{9,15},{12,10},{13,11},{14,6},{15... | collective-permute-start | bytes 294920 | tf_op jit(solution)/shard_map/ppermute | solution.py:38
  71.2 10.3 %collective-permute-start.30 = (bf16[64,768]{1,0:T(8,128)(2,1)S(1)}, bf16[64,768]{1,0:T(8,128)(2,1)S(1)}, u32[]{:S(2)}, u32[]{:S(2)}) collective-permute-start(bf16[64,768]{1,0:T(8,128)(2,1)S(1)} %get-tuple-element.34), channel_id=1, source_target_pairs={{0,9},{1,8},{4,13},{5,12},{8,15},{9,14},{12,11},{13,10},{14,7},{15... | collective-permute-start | bytes 294920 | tf_op jit(solution)/shard_map/ppermute | solution.py:38
  73.0 18.5 %collective-permute-start.25 = (bf16[64,768]{1,0:T(8,128)(2,1)S(1)}, bf16[64,768]{1,0:T(8,128)(2,1)S(1)}, u32[]{:S(2)}, u32[]{:S(2)}) collective-permute-start(bf16[64,768]{1,0:T(8,128)(2,1)S(1)} %get-tuple-element.29), channel_id=1, source_target_pairs={{0,14},{1,15},{4,10},{5,11},{8,6},{9,7},{12,2},{13,3},{14,0},{15,1... | collective-permute-start | bytes 294920 | tf_op jit(solution)/shard_map/ppermute | solution.py:38
  78.4 13.3 %collective-permute-start.26 = (bf16[64,768]{1,0:T(8,128)(2,1)S(1)}, bf16[64,768]{1,0:T(8,128)(2,1)S(1)}, u32[]{:S(2)}, u32[]{:S(2)}) collective-permute-start(bf16[64,768]{1,0:T(8,128)(2,1)S(1)} %get-tuple-element.30), channel_id=1, source_target_pairs={{0,15},{1,14},{4,11},{5,10},{8,7},{9,6},{12,3},{13,2},{14,1},{15,0... | collective-permute-start | bytes 294920 | tf_op jit(solution)/shard_map/ppermute | solution.py:38
  80.1 11.6 %collective-permute-start.19 = (bf16[64,768]{1,0:T(8,128)(2,1)S(1)}, bf16[64,768]{1,0:T(8,128)(2,1)S(1)}, u32[]{:S(2)}, u32[]{:S(2)}) collective-permute-start(bf16[64,768]{1,0:T(8,128)(2,1)S(1)} %get-tuple-element.27), channel_id=1, source_target_pairs={{0,10},{1,11},{4,6},{5,7},{8,2},{9,3},{12,0},{13,1},{14,4},{15,5},... | collective-permute-start | bytes 294920 | tf_op jit(solution)/shard_map/ppermute | solution.py:38
  80.1 11.6 %collective-permute-start.20 = (bf16[64,768]{1,0:T(8,128)(2,1)S(1)}, bf16[64,768]{1,0:T(8,128)(2,1)S(1)}, u32[]{:S(2)}, u32[]{:S(2)}) collective-permute-start(bf16[64,768]{1,0:T(8,128)(2,1)S(1)} %get-tuple-element.28), channel_id=1, source_target_pairs={{0,11},{1,10},{4,7},{5,6},{8,3},{9,2},{12,1},{13,0},{14,5},{15,4},... | collective-permute-start | bytes 294920 | tf_op jit(solution)/shard_map/ppermute | solution.py:38
  81.5 21.9 %collective-permute-start.27 = (bf16[64,768]{1,0:T(8,128)(2,1)S(1)}, bf16[64,768]{1,0:T(8,128)(2,1)S(1)}, u32[]{:S(2)}, u32[]{:S(2)}) collective-permute-start(bf16[64,768]{1,0:T(8,128)(2,1)S(1)} %get-tuple-element.31), channel_id=1, source_target_pairs={{0,12},{1,13},{4,14},{5,15},{8,10},{9,11},{12,6},{13,7},{14,2},{15... | collective-permute-start | bytes 294920 | tf_op jit(solution)/shard_map/ppermute | solution.py:38
  91.5 13.1 %collective-permute-start.28 = (bf16[64,768]{1,0:T(8,128)(2,1)S(1)}, bf16[64,768]{1,0:T(8,128)(2,1)S(1)}, u32[]{:S(2)}, u32[]{:S(2)}) collective-permute-start(bf16[64,768]{1,0:T(8,128)(2,1)S(1)} %get-tuple-element.32), channel_id=1, source_target_pairs={{0,13},{1,12},{4,15},{5,14},{8,11},{9,10},{12,7},{13,6},{14,3},{15... | collective-permute-start | bytes 294920 | tf_op jit(solution)/shard_map/ppermute | solution.py:38

commit v3 on v2

--- a/solution.py
+++ b/solution.py
@@ -15,6 +15,16 @@
     devices = range(lax.axis_size(axis))
     route = [((i - distance) % len(devices), i) for i in devices]
     return lax.ppermute(block, axis, route)
+
+
+def ring_chip(place, size):
+    height = size // COLUMNS
+    return jnp.where(place < height, place * COLUMNS, (size - 1 - place) * COLUMNS + 1)
+
+
+def ring_place(chip, size):
+    z, x = chip // COLUMNS, lax.rem(chip, COLUMNS)
+    return jnp.where(x == 0, z, size - 1 - z)
 
 
 def ring_order(owners):
@@ -38,83 +48,101 @@
     return lax.ppermute(block, "expert", ring_route(owners, distance, flip))
 
 
-def expert_kernel(count, *refs):
-    rows, (weight, gates), outs = refs[:count], refs[count : count + 2], refs[count + 2 :]
+def products_kernel(count, places, weight, other, gates, *refs):
+    rows, (out, stage, sem) = refs[:count], refs[-3:]
+    size = out.shape[0]
+    tokens = gates.shape[2]
+    me = lax.axis_index("expert")
+    place, core = ring_place(me // CORES, size), lax.rem(me, CORES)
     stacked = jnp.concatenate([r[...] for r in rows], axis=0)
-    scale = jnp.concatenate([gates[:, j : j + 1] for j in range(gates.shape[1])], axis=0)
-    product = lax.dot_general(
-        stacked, weight[...], (((1,), (1,)), ((), ())), preferred_element_type=jnp.float32
-    )
-    scaled = (product * scale).astype(jnp.bfloat16)
-    tokens = gates.shape[0]
-    for j, out in enumerate(outs):
-        out[...] = scaled[j * tokens : (j + 1) * tokens]
-
-
-def expert_rows(rows, weight, gates):
-    tokens, blocks = gates.shape
+    copies = []
+    for c, mat in enumerate((weight, other)):
+        product = lax.dot_general(
+            stacked, mat[...], (((1,), (1,)), ((), ())), preferred_element_type=jnp.float32
+        )
+        expert = core if c == 0 else 1 - core
+        for j, distance in enumerate(places):
+            chip = ring_chip(lax.rem(place + distance, size), size)
+            scale = gates[chip, expert]
+            stage[c, j] = (product[j * tokens : (j + 1) * tokens] * scale).astype(jnp.bfloat16)
+            copies.append(
+                pltpu.make_async_copy(stage.at[c, j], out.at[chip, expert], sem.at[c, j])
+            )
+            copies[-1].start()
+    for copy in copies:
+        copy.wait()
+
+
+def add_products(buffer, places, pieces, weight, other, gates):
+    size, experts, tokens, _ = gates.shape
     hidden, depth = weight.shape
+    n = len(places)
+    kept = [] if buffer is None else [buffer]
+    whole = pl.BlockSpec(memory_space=pltpu.VMEM)
     return pl.pallas_call(
-        functools.partial(expert_kernel, len(rows)),
-        out_shape=[jax.ShapeDtypeStruct((tokens, hidden), jnp.bfloat16)] * blocks,
+        functools.partial(products_kernel, len(pieces), places),
+        in_specs=[whole] * (3 + len(pieces)) + [pl.BlockSpec(memory_space=pl.ANY)] * len(kept),
+        out_specs=pl.BlockSpec(memory_space=pl.ANY),
+        out_shape=jax.ShapeDtypeStruct((size, experts, tokens, hidden), jnp.bfloat16),
+        input_output_aliases={3 + len(pieces): 0} if kept else {},
+        scratch_shapes=[
+            pltpu.VMEM((experts, n, tokens, hidden), jnp.bfloat16),
+            pltpu.SemaphoreType.DMA((experts, n)),
+        ],
         compiler_params=pltpu.CompilerParams(vmem_limit_bytes=40 << 20),
         cost_estimate=pl.CostEstimate(
-            flops=2 * blocks * tokens * hidden * depth,
-            bytes_accessed=2 * (blocks * tokens * (hidden + depth) + hidden * depth),
+            flops=2 * experts * n * tokens * hidden * depth,
+            bytes_accessed=2 * (n * tokens * (2 * hidden + depth) + 2 * hidden * depth),
             transcendentals=0,
         ),
-    )(*rows, weight, gates)
-
-
-def pick_kernel(labels_ref, *refs):
-    blocks, out = refs[:-1], refs[-1]
-    tokens, hidden = blocks[0].shape
+    )(weight, other, gates, *pieces, *kept)
+
+
+def pick_kernel(ids, blocks, out):
+    owners, tokens, hidden = blocks.shape
     top = out.shape[0] // tokens
     span = 16
     routes = span * top
-    column = lax.broadcasted_iota(jnp.int32, (routes, len(blocks) * span), 1)
-    token = lax.broadcasted_iota(jnp.int32, (routes, len(blocks) * span), 0) // top
+    column = lax.broadcasted_iota(jnp.int32, (routes, owners * span), 1)
+    token = lax.broadcasted_iota(jnp.int32, (routes, owners * span), 0) // top
     for g in range(tokens // span):
-        stacked = jnp.concatenate([b[g * span : (g + 1) * span, :] for b in blocks], axis=0)
-        wanted = labels_ref[g * routes : (g + 1) * routes, :] * span + token
+        stacked = jnp.concatenate([blocks[e, g * span : (g + 1) * span, :] for e in range(owners)], axis=0)
+        wanted = ids[g * routes : (g + 1) * routes, :] * span + token
         pick = jnp.where(column == wanted, 1.0, 0.0).astype(jnp.bfloat16)
         rows = jnp.dot(pick, stacked, preferred_element_type=jnp.float32)
         out[g * routes : (g + 1) * routes, :] = rows.astype(jnp.bfloat16)
 
 
-def pick_routes(labels, blocks):
-    tokens, hidden = blocks[0].shape
+def pick_routes(ids, blocks):
     return pl.pallas_call(
         pick_kernel,
-        out_shape=jax.ShapeDtypeStruct((labels.shape[0], hidden), jnp.bfloat16),
+        out_shape=jax.ShapeDtypeStruct((ids.shape[0], blocks.shape[2]), jnp.bfloat16),
         compiler_params=pltpu.CompilerParams(vmem_limit_bytes=40 << 20),
-    )(labels, *blocks)
+    )(ids, blocks)
 
 
 def dense_device(section_grad, route_ids, route_gates, weight_mat):
     tokens, top = route_ids.shape
     owners = lax.axis_size("expert")
     hidden = weight_mat.shape[0]
-    order = ring_order(owners)
-    size = len(order)
-    place_of_chip = jnp.array([order.index(c) for c in range(size)], jnp.int32)
-    chip_of_place = jnp.array(order, jnp.int32)
-    me = lax.axis_index("expert")
-    my_place, my_core = place_of_chip[me // CORES], me % CORES
-
+    size = owners // CORES
+    same_core = [list(range(core, owners, CORES)) for core in range(CORES)]
+
+    other_mat = send(weight_mat, owners, 0, 1)
     matched = route_ids[:, :, None] == jnp.arange(owners, dtype=jnp.int32)
     dense_gates = jnp.sum(
         jnp.where(matched, route_gates[:, :, None].astype(jnp.float32), 0.0), axis=1
     ).T.astype(jnp.bfloat16)
-    got_gates = lax.all_to_all(dense_gates, "expert", split_axis=0, concat_axis=0, tiled=True)
-    labels = jnp.arange(owners, dtype=jnp.int32)
-    label_owner = (
-        chip_of_place[(my_place + labels // CORES) % size] * CORES + (my_core ^ (labels % CORES))
-    )
-    gates = jnp.take(got_gates, label_owner, axis=0).T.astype(jnp.float32)
-    route_labels = (place_of_chip[route_ids // CORES] - my_place) % size * CORES + (
-        (route_ids % CORES) ^ my_core
-    )
+    dense_gates, section_grad = lax.optimization_barrier((dense_gates, section_grad))
+    got_gates = lax.all_to_all(
+        dense_gates.reshape(size, CORES * tokens),
+        "expert",
+        split_axis=0,
+        concat_axis=0,
+        tiled=True,
+        axis_index_groups=same_core,
+    )
+    gates = got_gates.astype(jnp.float32).reshape(size, CORES, tokens, 1)
 
     half = tokens // 2
     own = {0: section_grad}
@@ -125,31 +153,25 @@
     top_half = send(back[:half], owners, 1, 0)
     low_half = send(ahead[half:], owners, -1, 0)
 
-    results = {}
-
-    def products(distances, pieces):
-        names = [d * CORES + c for d in distances for c in range(CORES)]
-        picked = jnp.concatenate([gates[:, n : n + 1] for n in names], axis=1)
-        results.update(zip(names, expert_rows(pieces, weight_mat, picked)))
-
-    for step in range(size // 2):
-        distances = [0] if step == 0 else [size - step, step]
-        pieces = []
-        for d in distances:
-            pieces += [own[d], send(own[d], owners, 0, 1)]
-        products(distances, pieces)
-    products(
-        [size // 2], [top_half, low_half, send(top_half, owners, 0, 1), send(low_half, owners, 0, 1)]
-    )
-
-    received = [None] * owners
-    for d in range(size):
-        for c in range(CORES):
-            block = results[d * CORES + c]
-            if d or c:
-                block = send(block, owners, d, c)
-            received[(-d) % size * CORES + c] = block
-    out = pick_routes(route_labels.reshape(tokens * top, 1), received)
+    buffer = None
+    early = [0] + [d for s in range(1, size // 2 - 1) for d in (size - s, s)]
+    late = [size // 2 + 1, size // 2 - 1]
+    for places in (early, late):
+        pieces = [own[d] for d in places]
+        buffer = add_products(buffer, places, pieces, weight_mat, other_mat, gates)
+    buffer = add_products(buffer, [size // 2], [top_half, low_half], weight_mat, other_mat, gates)
+
+    returned = lax.all_to_all(
+        buffer.reshape(size, CORES * tokens, hidden),
+        "expert",
+        split_axis=0,
+        concat_axis=0,
+        tiled=True,
+        axis_index_groups=same_core,
+    )
+    out = pick_routes(
+        route_ids.reshape(tokens * top, 1), returned.reshape(owners, tokens, hidden)
+    )
     return out.reshape(1, tokens, top, hidden)
 
 

time: 107 us -> 103 us (0.963)
  starting transfers between devices: 44.1 us -> 14.9 us
  waiting for transfers between devices: 28.6 us -> 48.2 us
  blocking collectives: 0 us -> 11.9 us
  local copies, waits for them, and re-layouts: 17.9 us -> 11.4 us
  Pallas kernels: 11.1 us -> 14.8 us
  other arithmetic: 3.94 us -> 1.4 us
    all_to_all x1, waiting for transfers between devices: 0.01 us -> 32.7 us  [dense_device(): lax.all_to_all(buffer.reshape(size, CORES * tokens, hidden), 'expert', sp...]
    ppermute x32 -> x9, starting transfers between devices: 35.3 us -> 8.66 us  [send(): return lax.ppermute(block, 'expert', ring_route(owners, distance, flip))]
    ppermute x32 -> x9, waiting for transfers between devices: 28.6 us -> 9.79 us  [send(): return lax.ppermute(block, 'expert', ring_route(owners, distance, flip))]
    all_to_all x0 -> x1, blocking collectives: none -> 11.9 us  [dense_device(): lax.all_to_all(dense_gates.reshape(size, CORES * tokens), 'expert', split...]
    ppermute x1, waiting for transfers between devices: 0.01 us -> 5.8 us  [shifted(): return lax.ppermute(block, axis, route)]
    pallas_call x6 -> x4, Pallas kernels: 11.1 us -> 14.8 us  [the longest x3 13.5 us: add_products(): pl.pallas_call(functools.partial(products_kernel, len(pieces), places), i...]
    sub x2 -> x0, local copies, waits for them, and re-layouts: 2.28 us -> none  [dense_device(): place_of_chip[route_ids // CORES] - my_place]
    all_to_all x1, starting transfers between devices: 5.91 us -> 3.71 us  [dense_device(): lax.all_to_all(buffer.reshape(size, CORES * tokens, hidden), 'expert', sp...]
  transfers between devices with their start and end apart: 34 -> 11, of which waited for: 8 -> 5; matrix products, arithmetic and copies ran while one was open for 13% -> 4% of each run, Pallas kernels for 9% -> 10%
where the time goes in v3:
time: 103 us
  waiting for transfers between devices  48.2 us (47%)
  starting transfers between devices  14.9 us (14%)
  Pallas kernels  14.8 us (14%)
  blocking collectives  11.9 us (12%)
  local copies, waits for them, and re-layouts  11.4 us (11%)
  other arithmetic  1.4 us (1%)
    all_to_all x1, waiting for transfers between devices, dense_device(): lax.all_to_all(buffer.reshape(size, CORES * tokens, hidden), 'expert', sp...  32.7 us
    pallas_call x3, Pallas kernels, add_products(): pl.pallas_call(functools.partial(products_kernel, len(pieces), places), i...  13.5 us
    all_to_all x1, blocking collectives, dense_device(): lax.all_to_all(dense_gates.reshape(size, CORES * tokens), 'expert', split...  11.9 us
    ppermute x9, waiting for transfers between devices, send(): return lax.ppermute(block, 'expert', ring_route(owners, distance, flip))  9.79 us
    unnamed x21, local copies, waits for them, and re-layouts  9.17 us
    ppermute x9, starting transfers between devices, send(): return lax.ppermute(block, 'expert', ring_route(owners, distance, flip))  8.66 us
    ppermute x1, waiting for transfers between devices, shifted(): return lax.ppermute(block, axis, route)  5.8 us
    all_to_all x1, starting transfers between devices, dense_device(): lax.all_to_all(buffer.reshape(size, CORES * tokens, hidden), 'expert', sp...  3.71 us
  transfers between devices with their start and end apart: 11, of which 5 were waited for; matrix products, arithmetic and copies ran while one was open for 4% of the time, Pallas kernels for 10%

profile of v3, /device:TPU:0, one launch (start us, length us, event | category | flops | bytes accessed | tf_op | source)
XLA Modules:
  0.0 102.7 jit_solution(17106093065531049290)
XLA Ops:
  0.0 0.5 collective-permute-start
  0.5 2.5 %collective-permute-start.1 = (bf16[1,64,2048]{2,1,0:T(8,128)(2,1)}, bf16[1,64,2048]{2,1,0:T(8,128)(2,1)S(1)}, u32[]{:S(2)}, u32[]{:S(2)}) collective-permute-start(bf16[1,64,2048]{2,1,0:T(8,128)(2,1)} %param.4), channel_id=1, source_target_pairs={{16,0},{0,16},{17,1},{1,17},{18,2},{2,18},{19,3},{3,19},{20,4},{4,... | collective-permute-start | bytes 786440 | tf_op jit(solution)/shard_map/ppermute | solution.py:17
  3.0 0.7 bitcast_convert_fusion
  3.7 0.7 select_reduce_fusion
  4.4 5.8 %collective-permute-done.1 = bf16[1,64,2048]{2,1,0:T(8,128)(2,1)S(1)} collective-permute-done((bf16[1,64,2048]{2,1,0:T(8,128)(2,1)}, bf16[1,64,2048]{2,1,0:T(8,128)(2,1)S(1)}, u32[]{:S(2)}, u32[]{:S(2)}) %collective-permute-start.1) | collective-permute-done | bytes 262176 | tf_op jit(solution)/shard_map/ppermute | solution.py:17
  10.2 1.8 %collective-permute-start.2 = (bf16[64,2048]{1,0:T(8,128)(2,1)S(1)}, bf16[64,2048]{1,0:T(8,128)(2,1)S(1)}, u32[]{:S(2)}, u32[]{:S(2)}) collective-permute-start(bf16[64,2048]{1,0:T(8,128)(2,1)S(1)} %bitcast.18), channel_id=1, source_target_pairs={{0,4},{1,5},{4,8},{5,9},{8,12},{9,13},{12,14},{13,15},{14,10},{15,... | collective-permute-start | bytes 786440 | tf_op jit(solution)/shard_map/ppermute | solution.py:48
  12.0 0.2 collective-permute-start.6
  12.2 0.0 copy-start.3
  12.2 0.7 copy-done.3
  12.9 5.4 %collective-permute-done.2.refs_1_ = bf16[64,2048]{1,0:T(8,128)(2,1)S(1)} collective-permute-done((bf16[64,2048]{1,0:T(8,128)(2,1)S(1)}, bf16[64,2048]{1,0:T(8,128)(2,1)S(1)}, u32[]{:S(2)}, u32[]{:S(2)}) %collective-permute-start.2) | collective-permute-done | bytes 262176 | tf_op jit(solution)/shard_map/ppermute | solution.py:48
  18.3 1.6 %collective-permute-start.3 = (bf16[64,2048]{1,0:T(8,128)(2,1)S(1)}, bf16[64,2048]{1,0:T(8,128)(2,1)}, u32[]{:S(2)}, u32[]{:S(2)}) collective-permute-start(bf16[64,2048]{1,0:T(8,128)(2,1)S(1)} %collective-permute-done.2.refs_1_), channel_id=1, source_target_pairs={{0,4},{1,5},{4,8},{5,9},{8,12},{9,13},{12,14},{13,15},{14,10},{15,... | collective-permute-start | bytes 786440 | tf_op jit(solution)/shard_map/ppermute | solution.py:48
  19.9 0.0 copy-start.5
  19.9 0.7 copy-done.5
  20.6 0.0 collective-permute-done.6.refs_2_
  20.6 0.4 collective-permute-start.7
  21.1 0.0 copy-start.7
  21.1 0.7 copy-done.7
  21.8 3.9 %collective-permute-done.3.refs_3_ = bf16[64,2048]{1,0:T(8,128)(2,1)} collective-permute-done((bf16[64,2048]{1,0:T(8,128)(2,1)S(1)}, bf16[64,2048]{1,0:T(8,128)(2,1)}, u32[]{:S(2)}, u32[]{:S(2)}) %collective-permute-start.3) | collective-permute-done | bytes 262176 | tf_op jit(solution)/shard_map/ppermute | solution.py:48
  25.7 1.4 %collective-permute-start.4 = (bf16[64,2048]{1,0:T(8,128)(2,1)}, bf16[64,2048]{1,0:T(8,128)(2,1)S(1)}, u32[]{:S(2)}, u32[]{:S(2)}) collective-permute-start(bf16[64,2048]{1,0:T(8,128)(2,1)} %collective-permute-done.3.refs_3_), channel_id=1, source_target_pairs={{0,4},{1,5},{4,8},{5,9},{8,12},{9,13},{12,14},{13,15},{14,10},{15,... | collective-permute-start | bytes 786440 | tf_op jit(solution)/shard_map/ppermute | solution.py:48
  27.0 0.4 collective-permute-done.7.refs_4_
  27.5 0.7 collective-permute-start.8
  28.2 0.1 all_to_all.12
  28.2 11.9 %all_to_all.15 = bf16[8,1,128]{2,1,0:T(2,128)(2,1)S(1)} all-to-all(bf16[8,1,128]{2,1,0:T(2,128)(2,1)S(1)} %all_to_all.12), channel_id=1, replica_groups={{0,2,4,6,8,10,12,14},{1,3,5,7,9,11,13,15},{16,18,20,22,24,26,28,30},{17..., dimensions={0} | all-to-all | bytes 4096 | tf_op jit(solution)/shard_map/all_to_all | solution.py:137
  40.1 1.1 %reshape.41.gates = f32[8,2,64,1]{3,2,1,0:T(8,128)} reshape(f32[8,128]{1,0:T(8,128)S(1)} %convert_reduce_fusion) | data formatting | bytes 8192 | tf_op jit(solution)/shard_map/convert_element_type | solution.py:145
  41.3 0.0 collective-permute-done.4.refs_0_
  41.3 0.6 collective-permute-start.5
  41.9 0.0 collective-permute-done.8.refs_1_
  41.9 0.9 slice.9
  42.8 1.6 %collective-permute-start.9 = (bf16[32,2048]{1,0:T(8,128)(2,1)S(1)}, bf16[32,2048]{1,0:T(8,128)(2,1)S(1)}, u32[]{:S(2)}, u32[]{:S(2)}) collective-permute-start(bf16[32,2048]{1,0:T(8,128)(2,1)S(1)} %slice.9), channel_id=1, source_target_pairs={{0,2},{1,3},{4,0},{5,1},{8,4},{9,5},{12,8},{13,9},{14,12},{15,13},... | collective-permute-start | bytes 393224 | tf_op jit(solution)/shard_map/ppermute | solution.py:48
  44.3 0.0 collective-permute-done.other
  44.4 0.0 copy-start
  44.4 1.9 %copy-done = bf16[1,1,768,2048]{3,2,1,0:T(8,128)(2,1)S(1)} copy-done((bf16[1,1,768,2048]{3,2,1,0:T(8,128)(2,1)S(1)}, bf16[1,1,768,2048]{3,2,1,0:T(8,128)(2,1)}, u32[]{:S(2)}) %copy-start) | copy-done | bytes 3145752
  46.2 0.0 copy-start.2
  46.2 1.0 %copy-done.2 = f32[8,2,64,1]{3,2,1,0:T(8,128)S(1)} copy-done((f32[8,2,64,1]{3,2,1,0:T(8,128)S(1)}, f32[8,2,64,1]{3,2,1,0:T(8,128)}, u32[]{:S(2)}) %copy-start.2) | copy-done | bytes 4120
  47.3 0.0 copy-start.4
  47.3 0.9 copy-done.4
  48.2 0.0 copy-start.6
  48.2 0.9 copy-done.6
  49.2 0.0 copy-start.8
  49.2 0.9 copy-done.8
  50.1 6.2 %shard_map.46.refs_2_ = bf16[8,2,64,768]{3,2,1,0:T(8,128)(2,1)S(1)} custom-call(bf16[768,2048]{1,0:T(8,128)(2,1)S(1)} %bitcast.13, bf16[768,2048]{1,0:T(8,128)(2,1)S(1)} %collective-permute-done.other, f32[8,2,64,1]{3,2,1,0:T(8,128)S(1)} %copy-done.2, bf16[64,2048]{1,0:T(8,128)(2,1)S(1)} %bitcast.20, bf16[64,2048]{1,0:T(8,128)(2,1)S(1)} %copy-done.6, ...), custom_call_target="tpu_custom_call" | custom-call | flops 2013265920 | bytes 8585216 | tf_op jit(solution)/shard_map/pallas_call | solution.py:82
  56.4 4.4 %shard_map.47.refs_2_ = bf16[8,2,64,768]{3,2,1,0:T(8,128)(2,1)S(1)} custom-call(bf16[768,2048]{1,0:T(8,128)(2,1)S(1)} %bitcast.14, bf16[768,2048]{1,0:T(8,128)(2,1)S(1)} %collective-permute-done.other, f32[8,2,64,1]{3,2,1,0:T(8,128)S(1)} %copy-done.2, bf16[64,2048]{1,0:T(8,128)(2,1)S(1)} %collective-permute-done.4.refs_0_, ...), custom_call_target="tpu_custom_call", output_to_operand_aliasing={{}: (5, {})} | custom-call | flops 805306368 | bytes 7208960 | tf_op jit(solution)/shard_map/pallas_call | solution.py:82
  60.7 0.0 collective-permute-done.5.refs_0_
  60.8 0.0 collective-permute-done.9.refs_1_
  60.8 2.9 %shard_map.48 = bf16[8,2,64,768]{3,2,1,0:T(8,128)(2,1)S(1)} custom-call(bf16[768,2048]{1,0:T(8,128)(2,1)S(1)} %bitcast.15, bf16[768,2048]{1,0:T(8,128)(2,1)S(1)} %collective-permute-done.other, f32[8,2,64,1]{3,2,1,0:T(8,128)S(1)} %copy-done.2, bf16[32,2048]{1,0:T(8,128)(2,1)S(1)} %collective-permute-done.5.refs_0_, ...), custom_call_target="tpu_custom_call", output_to_operand_aliasing={{}: (5, {})} | custom-call | flops 402653184 | bytes 6750208 | tf_op jit(solution)/shard_map/pallas_call | solution.py:82
  63.6 0.0 copy-start.1
  63.6 1.2 %copy-done.1 = bf16[8,2,64,768]{3,2,1,0:T(8,128)(2,1)} copy-done((bf16[8,2,64,768]{3,2,1,0:T(8,128)(2,1)}, bf16[8,2,64,768]{3,2,1,0:T(8,128)(2,1)S(1)}, u32[]{:S(2)}) %copy-start.1) | copy-done | bytes 1572888
  64.8 0.0 copy-start.9
  64.8 3.7 %all-to-all-start.1 = ((bf16[8,128,768]{2,1,0:T(8,128)(2,1)}), bf16[8,128,768]{2,1,0:T(8,128)(2,1)S(1)}, u32[]{:S(2)}, u32[]{:S(2)}) async-start(bf16[8,128,768]{2,1,0:T(8,128)(2,1)} %bitcast.16), calls=%async_computation.1 | async-start | bytes 3145728 | tf_op jit(solution)/shard_map/all_to_all | solution.py:164
  68.5 0.0 copy-done.9
  68.5 0.1 copy.32
  68.6 0.1 reshape_squeeze.4.ids
  68.8 32.7 %all-to-all-done.1 = bf16[8,128,768]{2,1,0:T(8,128)(2,1)S(1)} async-done(((bf16[8,128,768]{2,1,0:T(8,128)(2,1)}), bf16[8,128,768]{2,1,0:T(8,128)(2,1)S(1)}, u32[]{:S(2)}, u32[]{:S(2)}) %all-to-all-start.1) | async-done | bytes 1572896 | tf_op jit(solution)/shard_map/all_to_all | solution.py:164
  101.4 1.3 %shard_map.49 = bf16[512,768]{1,0:T(8,128)(2,1)} custom-call(s32[512,1]{1,0:T(8,128)S(1)} %reshape_squeeze.4.ids, bf16[16,64,768]{2,1,0:T(8,128)(2,1)S(1)} %bitcast.17), custom_call_target="tpu_custom_call" | custom-call | tf_op jit(solution)/shard_map/pallas_call | solution.py:117
  (2 shorter events, 0.0 us)
Async XLA Ops:
  0.0 44.3 %collective-permute-start = (bf16[768,2048]{1,0:T(8,128)(2,1)}, bf16[768,2048]{1,0:T(8,128)(2,1)S(1)}, u32[]{:S(2)}, u32[]{:S(2)}) collective-permute-start(bf16[768,2048]{1,0:T(8,128)(2,1)} %bitcast.12), channel_id=1, source_target_pairs={{0,1},{1,0},{4,5},{5,4},{8,9},{9,8},{12,13},{13,12},{14,15},{15,14... | collective-permute-start | bytes 9437192 | tf_op jit(solution)/shard_map/ppermute | solution.py:48
  0.5 9.7 %collective-permute-start.1 = (bf16[1,64,2048]{2,1,0:T(8,128)(2,1)}, bf16[1,64,2048]{2,1,0:T(8,128)(2,1)S(1)}, u32[]{:S(2)}, u32[]{:S(2)}) collective-permute-start(bf16[1,64,2048]{2,1,0:T(8,128)(2,1)} %param.4), channel_id=1, source_target_pairs={{16,0},{0,16},{17,1},{1,17},{18,2},{2,18},{19,3},{3,19},{20,4},{4,... | collective-permute-start | bytes 786440 | tf_op jit(solution)/shard_map/ppermute | solution.py:17
  10.2 8.1 %collective-permute-start.2 = (bf16[64,2048]{1,0:T(8,128)(2,1)S(1)}, bf16[64,2048]{1,0:T(8,128)(2,1)S(1)}, u32[]{:S(2)}, u32[]{:S(2)}) collective-permute-start(bf16[64,2048]{1,0:T(8,128)(2,1)S(1)} %bitcast.18), channel_id=1, source_target_pairs={{0,4},{1,5},{4,8},{5,9},{8,12},{9,13},{12,14},{13,15},{14,10},{15,... | collective-permute-start | bytes 786440 | tf_op jit(solution)/shard_map/ppermute | solution.py:48
  12.0 8.7 %collective-permute-start.6 = (bf16[64,2048]{1,0:T(8,128)(2,1)S(1)}, bf16[64,2048]{1,0:T(8,128)(2,1)S(1)}, u32[]{:S(2)}, u32[]{:S(2)}) collective-permute-start(bf16[64,2048]{1,0:T(8,128)(2,1)S(1)} %bitcast.19), channel_id=1, source_target_pairs={{0,2},{1,3},{4,0},{5,1},{8,4},{9,5},{12,8},{13,9},{14,12},{15,13},... | collective-permute-start | bytes 786440 | tf_op jit(solution)/shard_map/ppermute | solution.py:48
  12.2 0.7 copy-start.3
  18.3 7.4 %collective-permute-start.3 = (bf16[64,2048]{1,0:T(8,128)(2,1)S(1)}, bf16[64,2048]{1,0:T(8,128)(2,1)}, u32[]{:S(2)}, u32[]{:S(2)}) collective-permute-start(bf16[64,2048]{1,0:T(8,128)(2,1)S(1)} %collective-permute-done.2.refs_1_), channel_id=1, source_target_pairs={{0,4},{1,5},{4,8},{5,9},{8,12},{9,13},{12,14},{13,15},{14,10},{15,... | collective-permute-start | bytes 786440 | tf_op jit(solution)/shard_map/ppermute | solution.py:48
  19.9 0.7 copy-start.5
  20.6 6.9 %collective-permute-start.7 = (bf16[64,2048]{1,0:T(8,128)(2,1)S(1)}, bf16[64,2048]{1,0:T(8,128)(2,1)}, u32[]{:S(2)}, u32[]{:S(2)}) collective-permute-start(bf16[64,2048]{1,0:T(8,128)(2,1)S(1)} %collective-permute-done.6.refs_2_), channel_id=1, source_target_pairs={{0,2},{1,3},{4,0},{5,1},{8,4},{9,5},{12,8},{13,9},{14,12},{15,13},... | collective-permute-start | bytes 786440 | tf_op jit(solution)/shard_map/ppermute | solution.py:48
  21.1 0.7 copy-start.7
  25.7 15.6 %collective-permute-start.4 = (bf16[64,2048]{1,0:T(8,128)(2,1)}, bf16[64,2048]{1,0:T(8,128)(2,1)S(1)}, u32[]{:S(2)}, u32[]{:S(2)}) collective-permute-start(bf16[64,2048]{1,0:T(8,128)(2,1)} %collective-permute-done.3.refs_3_), channel_id=1, source_target_pairs={{0,4},{1,5},{4,8},{5,9},{8,12},{9,13},{12,14},{13,15},{14,10},{15,... | collective-permute-start | bytes 786440 | tf_op jit(solution)/shard_map/ppermute | solution.py:48
  27.5 14.4 %collective-permute-start.8 = (bf16[64,2048]{1,0:T(8,128)(2,1)}, bf16[64,2048]{1,0:T(8,128)(2,1)}, u32[]{:S(2)}, u32[]{:S(2)}) collective-permute-start(bf16[64,2048]{1,0:T(8,128)(2,1)} %collective-permute-done.7.refs_4_), channel_id=1, source_target_pairs={{0,2},{1,3},{4,0},{5,1},{8,4},{9,5},{12,8},{13,9},{14,12},{15,13},... | collective-permute-start | bytes 786440 | tf_op jit(solution)/shard_map/ppermute | solution.py:48
  41.3 19.5 %collective-permute-start.5 = (bf16[32,2048]{1,0:T(8,128)(2,1)S(1)}, bf16[32,2048]{1,0:T(8,128)(2,1)S(1)}, u32[]{:S(2)}, u32[]{:S(2)}) collective-permute-start(bf16[32,2048]{1,0:T(8,128)(2,1)S(1)} %slice.8), channel_id=1, source_target_pairs={{0,4},{1,5},{4,8},{5,9},{8,12},{9,13},{12,14},{13,15},{14,10},{15,... | collective-permute-start | bytes 393224 | tf_op jit(solution)/shard_map/ppermute | solution.py:48
  42.8 18.0 %collective-permute-start.9 = (bf16[32,2048]{1,0:T(8,128)(2,1)S(1)}, bf16[32,2048]{1,0:T(8,128)(2,1)S(1)}, u32[]{:S(2)}, u32[]{:S(2)}) collective-permute-start(bf16[32,2048]{1,0:T(8,128)(2,1)S(1)} %slice.9), channel_id=1, source_target_pairs={{0,2},{1,3},{4,0},{5,1},{8,4},{9,5},{12,8},{13,9},{14,12},{15,13},... | collective-permute-start | bytes 393224 | tf_op jit(solution)/shard_map/ppermute | solution.py:48
  44.4 1.9 %copy-start = (bf16[1,1,768,2048]{3,2,1,0:T(8,128)(2,1)S(1)}, bf16[1,1,768,2048]{3,2,1,0:T(8,128)(2,1)}, u32[]{:S(2)}) copy-start(bf16[1,1,768,2048]{3,2,1,0:T(8,128)(2,1)} %param.7) | copy-start | bytes 9437188
  46.2 1.0 %copy-start.2 = (f32[8,2,64,1]{3,2,1,0:T(8,128)S(1)}, f32[8,2,64,1]{3,2,1,0:T(8,128)}, u32[]{:S(2)}) copy-start(f32[8,2,64,1]{3,2,1,0:T(8,128)} %reshape.41.gates) | copy-start | bytes 12292
  47.3 0.9 copy-start.4
  48.2 0.9 copy-start.6
  49.2 0.9 copy-start.8
  63.6 1.2 %copy-start.1 = (bf16[8,2,64,768]{3,2,1,0:T(8,128)(2,1)}, bf16[8,2,64,768]{3,2,1,0:T(8,128)(2,1)S(1)}, u32[]{:S(2)}) copy-start(bf16[8,2,64,768]{3,2,1,0:T(8,128)(2,1)S(1)} %shard_map.48) | copy-start | bytes 4718596
  64.8 3.7 %copy-start.9 = (s32[1,64,8]{1,2,0:T(8,128)S(1)}, s32[1,64,8]{1,2,0:T(8,128)}, u32[]{:S(2)}) copy-start(s32[1,64,8]{1,2,0:T(8,128)} %param.5) | copy-start | bytes 6148
  64.8 36.6 %all-to-all-start.1 = ((bf16[8,128,768]{2,1,0:T(8,128)(2,1)}), bf16[8,128,768]{2,1,0:T(8,128)(2,1)S(1)}, u32[]{:S(2)}, u32[]{:S(2)}) async-start(bf16[8,128,768]{2,1,0:T(8,128)(2,1)} %bitcast.16), calls=%async_computation.1 | async-start | bytes 3145728 | tf_op jit(solution)/shard_map/all_to_all | solution.py:164

commit v4 on v3

--- a/solution.py
+++ b/solution.py
@@ -81,15 +81,15 @@
     whole = pl.BlockSpec(memory_space=pltpu.VMEM)
     return pl.pallas_call(
         functools.partial(products_kernel, len(pieces), places),
-        in_specs=[whole] * (3 + len(pieces)) + [pl.BlockSpec(memory_space=pl.ANY)] * len(kept),
-        out_specs=pl.BlockSpec(memory_space=pl.ANY),
+        in_specs=[whole] * (3 + len(pieces)) + [pl.BlockSpec(memory_space=pltpu.HBM)] * len(kept),
+        out_specs=pl.BlockSpec(memory_space=pltpu.HBM),
         out_shape=jax.ShapeDtypeStruct((size, experts, tokens, hidden), jnp.bfloat16),
         input_output_aliases={3 + len(pieces): 0} if kept else {},
         scratch_shapes=[
             pltpu.VMEM((experts, n, tokens, hidden), jnp.bfloat16),
             pltpu.SemaphoreType.DMA((experts, n)),
         ],
-        compiler_params=pltpu.CompilerParams(vmem_limit_bytes=40 << 20),
+        compiler_params=pltpu.CompilerParams(vmem_limit_bytes=16 << 20),
         cost_estimate=pl.CostEstimate(
             flops=2 * experts * n * tokens * hidden * depth,
             bytes_accessed=2 * (n * tokens * (2 * hidden + depth) + 2 * hidden * depth),
@@ -117,7 +117,7 @@
     return pl.pallas_call(
         pick_kernel,
         out_shape=jax.ShapeDtypeStruct((ids.shape[0], blocks.shape[2]), jnp.bfloat16),
-        compiler_params=pltpu.CompilerParams(vmem_limit_bytes=40 << 20),
+        compiler_params=pltpu.CompilerParams(vmem_limit_bytes=16 << 20),
     )(ids, blocks)
 
 
@@ -133,7 +133,6 @@
     dense_gates = jnp.sum(
         jnp.where(matched, route_gates[:, :, None].astype(jnp.float32), 0.0), axis=1
     ).T.astype(jnp.bfloat16)
-    dense_gates, section_grad = lax.optimization_barrier((dense_gates, section_grad))
     got_gates = lax.all_to_all(
         dense_gates.reshape(size, CORES * tokens),
         "expert",
@@ -142,23 +141,30 @@
         tiled=True,
         axis_index_groups=same_core,
     )
+    section_grad, got_gates = lax.optimization_barrier((section_grad, got_gates))
     gates = got_gates.astype(jnp.float32).reshape(size, CORES, tokens, 1)
 
     half = tokens // 2
-    own = {0: section_grad}
+    buffer = None
     back = ahead = section_grad
+    waiting = {0: section_grad}
     for step in range(1, size // 2):
-        back, ahead = send(back, owners, 1, 0), send(ahead, owners, -1, 0)
-        own[size - step], own[step] = back, ahead
+        next_back, next_ahead = send(back, owners, 1, 0), send(ahead, owners, -1, 0)
+        if step > 1:
+            buffer = add_products(
+                buffer, list(waiting), list(waiting.values()), weight_mat, other_mat, gates
+            )
+            waiting = {}
+            next_back, next_ahead, buffer = lax.optimization_barrier(
+                (next_back, next_ahead, buffer)
+            )
+        back, ahead = next_back, next_ahead
+        waiting.update({size - step: back, step: ahead})
     top_half = send(back[:half], owners, 1, 0)
     low_half = send(ahead[half:], owners, -1, 0)
-
-    buffer = None
-    early = [0] + [d for s in range(1, size // 2 - 1) for d in (size - s, s)]
-    late = [size // 2 + 1, size // 2 - 1]
-    for places in (early, late):
-        pieces = [own[d] for d in places]
-        buffer = add_products(buffer, places, pieces, weight_mat, other_mat, gates)
+    buffer = add_products(
+        buffer, list(waiting), list(waiting.values()), weight_mat, other_mat, gates
+    )
     buffer = add_products(buffer, [size // 2], [top_half, low_half], weight_mat, other_mat, gates)
 
     returned = lax.all_to_all(

time: 103 us -> 90.1 us (0.87)
  waiting for transfers between devices: 48.2 us -> 38.6 us
  local copies, waits for them, and re-layouts: 11.4 us -> 5.53 us
  Pallas kernels: 14.8 us -> 17 us
    ppermute x1, waiting for transfers between devices: 5.8 us -> 0.01 us  [shifted(): return lax.ppermute(block, axis, route)]
    unnamed x21 -> x10, local copies, waits for them, and re-layouts: 9.17 us -> 4.18 us
    ppermute x9, waiting for transfers between devices: 9.79 us -> 6.58 us  [send(): return lax.ppermute(block, 'expert', ring_route(owners, distance, flip))]
    pallas_call x3 -> x4, Pallas kernels: 13.5 us -> 15.7 us  [add_products(): pl.pallas_call(functools.partial(products_kernel, len(pieces), places), i...]
    convert_element_type x1 -> x0, local copies, waits for them, and re-layouts: 1.13 us -> none  [dense_device(): gates = got_gates.astype(jnp.float32).reshape(size, CORES, tokens, 1)]
    reshape x0 -> x1, local copies, waits for them, and re-layouts: none -> 1.13 us  [dense_device(): gates = got_gates.astype(jnp.float32).reshape(size, CORES, tokens, 1)]
  transfers between devices with their start and end apart: 11 -> 11, of which waited for: 5 -> 5; matrix products, arithmetic and copies ran while one was open for 4% -> 3% of each run, Pallas kernels for 10% -> 14%
where the time goes in v4:
time: 90.1 us; the launch traced here: 89.7 us
  waiting for transfers between devices  38.6 us (43%)
  Pallas kernels  17 us (19%)
  starting transfers between devices  15 us (17%)
  blocking collectives  12.1 us (13%)
  local copies, waits for them, and re-layouts  5.53 us (6%)
  other arithmetic  1.39 us (2%)
    all_to_all x1, waiting for transfers between devices, dense_device(): lax.all_to_all(buffer.reshape(size, CORES * tokens, hidden), 'expert', sp...  32 us
    pallas_call x4, Pallas kernels, add_products(): pl.pallas_call(functools.partial(products_kernel, len(pieces), places), i...  15.7 us
    all_to_all x1, blocking collectives, dense_device(): lax.all_to_all(dense_gates.reshape(size, CORES * tokens), 'expert', split...  12.1 us
    ppermute x9, starting transfers between devices, send(): return lax.ppermute(block, 'expert', ring_route(owners, distance, flip))  8.71 us
    ppermute x9, waiting for transfers between devices, send(): return lax.ppermute(block, 'expert', ring_route(owners, distance, flip))  6.58 us
    unnamed x10, local copies, waits for them, and re-layouts  4.18 us
    all_to_all x1, starting transfers between devices, dense_device(): lax.all_to_all(buffer.reshape(size, CORES * tokens, hidden), 'expert', sp...  3.78 us
    ppermute x1, starting transfers between devices, shifted(): return lax.ppermute(block, axis, route)  2.52 us
  transfers between devices with their start and end apart: 11, of which 5 were waited for; matrix products, arithmetic and copies ran while one was open for 3% of the time, Pallas kernels for 14%

profile of v4, /device:TPU:0, one launch (start us, length us, event | category | flops | bytes accessed | tf_op | source)
XLA Modules:
  0.0 89.7 jit_solution(8575069573912549399)
XLA Ops:
  0.0 0.5 collective-permute-start
  0.5 2.5 %collective-permute-start.1 = (bf16[1,64,2048]{2,1,0:T(8,128)(2,1)}, bf16[1,64,2048]{2,1,0:T(8,128)(2,1)S(1)}, u32[]{:S(2)}, u32[]{:S(2)}) collective-permute-start(bf16[1,64,2048]{2,1,0:T(8,128)(2,1)} %param.4), channel_id=1, source_target_pairs={{16,0},{0,16},{17,1},{1,17},{18,2},{2,18},{19,3},{3,19},{20,4},{4,... | collective-permute-start | bytes 786440 | tf_op jit(solution)/shard_map/ppermute | solution.py:17
  3.0 0.7 bitcast_convert_fusion
  3.7 0.7 select_reduce_fusion
  4.4 0.1 all_to_all.15
  4.4 12.1 %all_to_all.18 = bf16[8,1,128]{2,1,0:T(2,128)(2,1)S(1)} all-to-all(bf16[8,1,128]{2,1,0:T(2,128)(2,1)S(1)} %all_to_all.15), channel_id=1, replica_groups={{0,2,4,6,8,10,12,14},{1,3,5,7,9,11,13,15},{16,18,20,22,24,26,28,30},{17..., dimensions={0} | all-to-all | bytes 4096 | tf_op jit(solution)/shard_map/all_to_all | solution.py:136
  16.5 0.0 collective-permute-done.1
  16.5 0.5 collective-permute-start.2
  17.1 1.5 %collective-permute-start.4 = (bf16[64,2048]{1,0:T(8,128)(2,1)S(1)}, bf16[64,2048]{1,0:T(8,128)(2,1)}, u32[]{:S(2)}, u32[]{:S(2)}) collective-permute-start(bf16[64,2048]{1,0:T(8,128)(2,1)S(1)} %bitcast.23), channel_id=1, source_target_pairs={{0,2},{1,3},{4,0},{5,1},{8,4},{9,5},{12,8},{13,9},{14,12},{15,13},... | collective-permute-start | bytes 786440 | tf_op jit(solution)/shard_map/ppermute | solution.py:48
  18.5 5.1 %collective-permute-done.2.refs_1_ = bf16[64,2048]{1,0:T(8,128)(2,1)} collective-permute-done((bf16[64,2048]{1,0:T(8,128)(2,1)S(1)}, bf16[64,2048]{1,0:T(8,128)(2,1)}, u32[]{:S(2)}, u32[]{:S(2)}) %collective-permute-start.2) | collective-permute-done | bytes 262176 | tf_op jit(solution)/shard_map/ppermute | solution.py:48
  23.6 0.5 collective-permute-start.3
  24.2 0.0 collective-permute-done.4.refs_2_
  24.2 1.5 %collective-permute-start.5 = (bf16[64,2048]{1,0:T(8,128)(2,1)}, bf16[64,2048]{1,0:T(8,128)(2,1)}, u32[]{:S(2)}, u32[]{:S(2)}) collective-permute-start(bf16[64,2048]{1,0:T(8,128)(2,1)} %collective-permute-done.4.refs_2_), channel_id=1, source_target_pairs={{0,2},{1,3},{4,0},{5,1},{8,4},{9,5},{12,8},{13,9},{14,12},{15,13},... | collective-permute-start | bytes 786440 | tf_op jit(solution)/shard_map/ppermute | solution.py:48
  25.7 1.1 %reshape.36.gates = f32[8,2,64,1]{3,2,1,0:T(8,128)} reshape(bf16[8,128]{1,0:T(8,128)(2,1)S(1)} %bitcast.27) | data formatting | bytes 6144 | tf_op jit(solution)/shard_map/reshape | solution.py:145
  26.8 0.0 collective-permute-done.other
  26.8 0.0 copy-start
  26.8 1.9 %copy-done = bf16[1,1,768,2048]{3,2,1,0:T(8,128)(2,1)S(1)} copy-done((bf16[1,1,768,2048]{3,2,1,0:T(8,128)(2,1)S(1)}, bf16[1,1,768,2048]{3,2,1,0:T(8,128)(2,1)}, u32[]{:S(2)}) %copy-start) | copy-done | bytes 3145752
  28.7 0.0 copy-start.2
  28.7 1.0 %copy-done.2 = f32[8,2,64,1]{3,2,1,0:T(8,128)S(1)} copy-done((f32[8,2,64,1]{3,2,1,0:T(8,128)S(1)}, f32[8,2,64,1]{3,2,1,0:T(8,128)}, u32[]{:S(2)}) %copy-start.2) | copy-done | bytes 4120
  29.7 4.9 %shard_map.46.refs_2_ = bf16[8,2,64,768]{3,2,1,0:T(8,128)(2,1)S(1)} custom-call(bf16[768,2048]{1,0:T(8,128)(2,1)S(1)} %bitcast.16, bf16[768,2048]{1,0:T(8,128)(2,1)S(1)} %collective-permute-done.other, f32[8,2,64,1]{3,2,1,0:T(8,128)S(1)} %copy-done.2, bf16[64,2048]{1,0:T(8,128)(2,1)S(1)} %bitcast.24, bf16[64,2048]{1,0:T(8,128)(2,1)} %collective-permute-done.2.refs_1_, ...), custom_call_target="tpu_custom_call" | custom-call | flops 1207959552 | bytes 7667712 | tf_op jit(solution)/shard_map/pallas_call | solution.py:82
  34.7 0.0 collective-permute-done.3.refs_0_
  34.7 0.0 collective-permute-done.5.refs_1_
  34.7 0.6 collective-permute-start.6
  35.3 1.5 %collective-permute-start.7 = (bf16[64,2048]{1,0:T(8,128)(2,1)}, bf16[64,2048]{1,0:T(8,128)(2,1)S(1)}, u32[]{:S(2)}, u32[]{:S(2)}) collective-permute-start(bf16[64,2048]{1,0:T(8,128)(2,1)} %collective-permute-done.5.refs_1_), channel_id=1, source_target_pairs={{0,2},{1,3},{4,0},{5,1},{8,4},{9,5},{12,8},{13,9},{14,12},{15,13},... | collective-permute-start | bytes 786440 | tf_op jit(solution)/shard_map/ppermute | solution.py:48
  36.8 4.5 %shard_map.47.refs_2_ = bf16[8,2,64,768]{3,2,1,0:T(8,128)(2,1)S(1)} custom-call(bf16[768,2048]{1,0:T(8,128)(2,1)S(1)} %bitcast.17, bf16[768,2048]{1,0:T(8,128)(2,1)S(1)} %collective-permute-done.other, f32[8,2,64,1]{3,2,1,0:T(8,128)S(1)} %copy-done.2, bf16[64,2048]{1,0:T(8,128)(2,1)} %collective-permute-done.3.refs_0_, ...), custom_call_target="tpu_custom_call", output_to_operand_aliasing={{}: (5, {})} | custom-call | flops 805306368 | bytes 7208960 | tf_op jit(solution)/shard_map/pallas_call | solution.py:82
  41.2 0.7 collective-permute-done.6.refs_0_
  41.9 0.8 collective-permute-done.7.refs_1_
  42.7 0.6 collective-permute-start.8
  43.3 1.5 %collective-permute-start.9 = (bf16[32,2048]{1,0:T(8,128)(2,1)S(1)}, bf16[32,2048]{1,0:T(8,128)(2,1)S(1)}, u32[]{:S(2)}, u32[]{:S(2)}) collective-permute-start(bf16[32,2048]{1,0:T(8,128)(2,1)S(1)} %slice.7), channel_id=1, source_target_pairs={{0,2},{1,3},{4,0},{5,1},{8,4},{9,5},{12,8},{13,9},{14,12},{15,13},... | collective-permute-start | bytes 393224 | tf_op jit(solution)/shard_map/ppermute | solution.py:48
  44.8 3.4 %shard_map.48.refs_2_ = bf16[8,2,64,768]{3,2,1,0:T(8,128)(2,1)S(1)} custom-call(bf16[768,2048]{1,0:T(8,128)(2,1)S(1)} %bitcast.18, bf16[768,2048]{1,0:T(8,128)(2,1)S(1)} %collective-permute-done.other, f32[8,2,64,1]{3,2,1,0:T(8,128)S(1)} %copy-done.2, bf16[64,2048]{1,0:T(8,128)(2,1)S(1)} %collective-permute-done.6.refs_0_, ...), custom_call_target="tpu_custom_call", output_to_operand_aliasing={{}: (5, {})} | custom-call | flops 805306368 | bytes 7208960 | tf_op jit(solution)/shard_map/pallas_call | solution.py:82
  48.3 0.0 collective-permute-done.8.refs_0_
  48.3 0.1 collective-permute-done.9.refs_1_
  48.3 2.9 %shard_map.49 = bf16[8,2,64,768]{3,2,1,0:T(8,128)(2,1)S(1)} custom-call(bf16[768,2048]{1,0:T(8,128)(2,1)S(1)} %bitcast.19, bf16[768,2048]{1,0:T(8,128)(2,1)S(1)} %collective-permute-done.other, f32[8,2,64,1]{3,2,1,0:T(8,128)S(1)} %copy-done.2, bf16[32,2048]{1,0:T(8,128)(2,1)S(1)} %collective-permute-done.8.refs_0_, ...), custom_call_target="tpu_custom_call", output_to_operand_aliasing={{}: (5, {})} | custom-call | flops 402653184 | bytes 6750208 | tf_op jit(solution)/shard_map/pallas_call | solution.py:82
  51.2 0.0 copy-start.1
  51.2 1.2 %copy-done.1 = bf16[8,2,64,768]{3,2,1,0:T(8,128)(2,1)} copy-done((bf16[8,2,64,768]{3,2,1,0:T(8,128)(2,1)}, bf16[8,2,64,768]{3,2,1,0:T(8,128)(2,1)S(1)}, u32[]{:S(2)}) %copy-start.1) | copy-done | bytes 1572888
  52.4 0.0 copy-start.3
  52.4 3.8 %all-to-all-start.1 = ((bf16[8,128,768]{2,1,0:T(8,128)(2,1)}), bf16[8,128,768]{2,1,0:T(8,128)(2,1)S(1)}, u32[]{:S(2)}, u32[]{:S(2)}) async-start(bf16[8,128,768]{2,1,0:T(8,128)(2,1)} %bitcast.20), calls=%async_computation.1 | async-start | bytes 3145728 | tf_op jit(solution)/shard_map/all_to_all | solution.py:170
  56.1 0.0 copy-done.3
  56.2 0.1 copy.36
  56.2 0.1 reshape_squeeze.4.ids
  56.4 32.0 %all-to-all-done.1 = bf16[8,128,768]{2,1,0:T(8,128)(2,1)S(1)} async-done(((bf16[8,128,768]{2,1,0:T(8,128)(2,1)}), bf16[8,128,768]{2,1,0:T(8,128)(2,1)S(1)}, u32[]{:S(2)}, u32[]{:S(2)}) %all-to-all-start.1) | async-done | bytes 1572896 | tf_op jit(solution)/shard_map/all_to_all | solution.py:170
  88.4 1.3 %shard_map.50 = bf16[512,768]{1,0:T(8,128)(2,1)} custom-call(s32[512,1]{1,0:T(8,128)S(1)} %reshape_squeeze.4.ids, bf16[16,64,768]{2,1,0:T(8,128)(2,1)S(1)} %bitcast.21), custom_call_target="tpu_custom_call" | custom-call | tf_op jit(solution)/shard_map/pallas_call | solution.py:117
  (3 shorter events, 0.0 us)
Async XLA Ops:
  0.0 26.8 %collective-permute-start = (bf16[768,2048]{1,0:T(8,128)(2,1)}, bf16[768,2048]{1,0:T(8,128)(2,1)S(1)}, u32[]{:S(2)}, u32[]{:S(2)}) collective-permute-start(bf16[768,2048]{1,0:T(8,128)(2,1)} %bitcast.15), channel_id=1, source_target_pairs={{0,1},{1,0},{4,5},{5,4},{8,9},{9,8},{12,13},{13,12},{14,15},{15,14... | collective-permute-start | bytes 9437192 | tf_op jit(solution)/shard_map/ppermute | solution.py:48
  0.5 16.1 %collective-permute-start.1 = (bf16[1,64,2048]{2,1,0:T(8,128)(2,1)}, bf16[1,64,2048]{2,1,0:T(8,128)(2,1)S(1)}, u32[]{:S(2)}, u32[]{:S(2)}) collective-permute-start(bf16[1,64,2048]{2,1,0:T(8,128)(2,1)} %param.4), channel_id=1, source_target_pairs={{16,0},{0,16},{17,1},{1,17},{18,2},{2,18},{19,3},{3,19},{20,4},{4,... | collective-permute-start | bytes 786440 | tf_op jit(solution)/shard_map/ppermute | solution.py:17
  16.5 7.1 %collective-permute-start.2 = (bf16[64,2048]{1,0:T(8,128)(2,1)S(1)}, bf16[64,2048]{1,0:T(8,128)(2,1)}, u32[]{:S(2)}, u32[]{:S(2)}) collective-permute-start(bf16[64,2048]{1,0:T(8,128)(2,1)S(1)} %bitcast.22), channel_id=1, source_target_pairs={{0,4},{1,5},{4,8},{5,9},{8,12},{9,13},{12,14},{13,15},{14,10},{15,... | collective-permute-start | bytes 786440 | tf_op jit(solution)/shard_map/ppermute | solution.py:48
  17.1 7.1 %collective-permute-start.4 = (bf16[64,2048]{1,0:T(8,128)(2,1)S(1)}, bf16[64,2048]{1,0:T(8,128)(2,1)}, u32[]{:S(2)}, u32[]{:S(2)}) collective-permute-start(bf16[64,2048]{1,0:T(8,128)(2,1)S(1)} %bitcast.23), channel_id=1, source_target_pairs={{0,2},{1,3},{4,0},{5,1},{8,4},{9,5},{12,8},{13,9},{14,12},{15,13},... | collective-permute-start | bytes 786440 | tf_op jit(solution)/shard_map/ppermute | solution.py:48
  23.6 11.1 %collective-permute-start.3 = (bf16[64,2048]{1,0:T(8,128)(2,1)}, bf16[64,2048]{1,0:T(8,128)(2,1)}, u32[]{:S(2)}, u32[]{:S(2)}) collective-permute-start(bf16[64,2048]{1,0:T(8,128)(2,1)} %collective-permute-done.2.refs_1_), channel_id=1, source_target_pairs={{0,4},{1,5},{4,8},{5,9},{8,12},{9,13},{12,14},{13,15},{14,10},{15,... | collective-permute-start | bytes 786440 | tf_op jit(solution)/shard_map/ppermute | solution.py:48
  24.2 10.5 %collective-permute-start.5 = (bf16[64,2048]{1,0:T(8,128)(2,1)}, bf16[64,2048]{1,0:T(8,128)(2,1)}, u32[]{:S(2)}, u32[]{:S(2)}) collective-permute-start(bf16[64,2048]{1,0:T(8,128)(2,1)} %collective-permute-done.4.refs_2_), channel_id=1, source_target_pairs={{0,2},{1,3},{4,0},{5,1},{8,4},{9,5},{12,8},{13,9},{14,12},{15,13},... | collective-permute-start | bytes 786440 | tf_op jit(solution)/shard_map/ppermute | solution.py:48
  26.8 1.9 %copy-start = (bf16[1,1,768,2048]{3,2,1,0:T(8,128)(2,1)S(1)}, bf16[1,1,768,2048]{3,2,1,0:T(8,128)(2,1)}, u32[]{:S(2)}) copy-start(bf16[1,1,768,2048]{3,2,1,0:T(8,128)(2,1)} %param.7) | copy-start | bytes 9437188
  28.7 1.0 %copy-start.2 = (f32[8,2,64,1]{3,2,1,0:T(8,128)S(1)}, f32[8,2,64,1]{3,2,1,0:T(8,128)}, u32[]{:S(2)}) copy-start(f32[8,2,64,1]{3,2,1,0:T(8,128)} %reshape.36.gates) | copy-start | bytes 12292
  34.7 7.2 %collective-permute-start.6 = (bf16[64,2048]{1,0:T(8,128)(2,1)}, bf16[64,2048]{1,0:T(8,128)(2,1)S(1)}, u32[]{:S(2)}, u32[]{:S(2)}) collective-permute-start(bf16[64,2048]{1,0:T(8,128)(2,1)} %collective-permute-done.3.refs_0_), channel_id=1, source_target_pairs={{0,4},{1,5},{4,8},{5,9},{8,12},{9,13},{12,14},{13,15},{14,10},{15,... | collective-permute-start | bytes 786440 | tf_op jit(solution)/shard_map/ppermute | solution.py:48
  35.3 7.4 %collective-permute-start.7 = (bf16[64,2048]{1,0:T(8,128)(2,1)}, bf16[64,2048]{1,0:T(8,128)(2,1)S(1)}, u32[]{:S(2)}, u32[]{:S(2)}) collective-permute-start(bf16[64,2048]{1,0:T(8,128)(2,1)} %collective-permute-done.5.refs_1_), channel_id=1, source_target_pairs={{0,2},{1,3},{4,0},{5,1},{8,4},{9,5},{12,8},{13,9},{14,12},{15,13},... | collective-permute-start | bytes 786440 | tf_op jit(solution)/shard_map/ppermute | solution.py:48
  42.7 5.6 %collective-permute-start.8 = (bf16[32,2048]{1,0:T(8,128)(2,1)S(1)}, bf16[32,2048]{1,0:T(8,128)(2,1)S(1)}, u32[]{:S(2)}, u32[]{:S(2)}) collective-permute-start(bf16[32,2048]{1,0:T(8,128)(2,1)S(1)} %slice.6), channel_id=1, source_target_pairs={{0,4},{1,5},{4,8},{5,9},{8,12},{9,13},{12,14},{13,15},{14,10},{15,... | collective-permute-start | bytes 393224 | tf_op jit(solution)/shard_map/ppermute | solution.py:48
  43.3 5.0 %collective-permute-start.9 = (bf16[32,2048]{1,0:T(8,128)(2,1)S(1)}, bf16[32,2048]{1,0:T(8,128)(2,1)S(1)}, u32[]{:S(2)}, u32[]{:S(2)}) collective-permute-start(bf16[32,2048]{1,0:T(8,128)(2,1)S(1)} %slice.7), channel_id=1, source_target_pairs={{0,2},{1,3},{4,0},{5,1},{8,4},{9,5},{12,8},{13,9},{14,12},{15,13},... | collective-permute-start | bytes 393224 | tf_op jit(solution)/shard_map/ppermute | solution.py:48
  51.2 1.2 %copy-start.1 = (bf16[8,2,64,768]{3,2,1,0:T(8,128)(2,1)}, bf16[8,2,64,768]{3,2,1,0:T(8,128)(2,1)S(1)}, u32[]{:S(2)}) copy-start(bf16[8,2,64,768]{3,2,1,0:T(8,128)(2,1)S(1)} %shard_map.49) | copy-start | bytes 4718596
  52.4 3.8 %copy-start.3 = (s32[1,64,8]{1,2,0:T(8,128)S(1)}, s32[1,64,8]{1,2,0:T(8,128)}, u32[]{:S(2)}) copy-start(s32[1,64,8]{1,2,0:T(8,128)} %param.5) | copy-start | bytes 6148
  52.4 36.0 %all-to-all-start.1 = ((bf16[8,128,768]{2,1,0:T(8,128)(2,1)}), bf16[8,128,768]{2,1,0:T(8,128)(2,1)S(1)}, u32[]{:S(2)}, u32[]{:S(2)}) async-start(bf16[8,128,768]{2,1,0:T(8,128)(2,1)} %bitcast.20), calls=%async_computation.1 | async-start | bytes 3145728 | tf_op jit(solution)/shard_map/all_to_all | solution.py:170

commit v5 on v4

--- a/solution.py
+++ b/solution.py
@@ -48,54 +48,94 @@
     return lax.ppermute(block, "expert", ring_route(owners, distance, flip))
 
 
-def products_kernel(count, places, weight, other, gates, *refs):
-    rows, (out, stage, sem) = refs[:count], refs[-3:]
+def scaled_products(rows, weight, gates, expert, distances, size):
+    tokens = rows.shape[0] // len(distances)
+    product = lax.dot_general(
+        rows, weight[...], (((1,), (1,)), ((), ())), preferred_element_type=jnp.float32
+    )
+    parts = []
+    for j, distance in enumerate(distances):
+        start = (-distance) % size * tokens
+        block = gates[start : start + tokens, :].astype(jnp.float32)
+        column = lax.broadcasted_iota(jnp.int32, block.shape, 1)
+        scale = jnp.sum(jnp.where(column == expert, block, 0.0), axis=1, keepdims=True)
+        parts.append((product[j * tokens : (j + 1) * tokens] * scale).astype(jnp.bfloat16))
+    return parts
+
+
+def products_kernel(count, size, distances, weight, other, gates, *refs):
+    rows, out = refs[:count], refs[count]
+    me = lax.axis_index("expert")
+    core = lax.rem(me, CORES)
+    stacked = jnp.concatenate([r[...] for r in rows], axis=0)
+    for mat, to in ((weight, core), (other, 1 - core)):
+        expert = me - core + to
+        for j, part in enumerate(scaled_products(stacked, mat, gates, expert, distances, size)):
+            out[j, to] = part
+
+
+def products(distances, pieces, size, weight, other, gates):
+    hidden, depth = weight.shape
+    tokens = pieces[0].shape[0]
+    n = len(distances)
+    return pl.pallas_call(
+        functools.partial(products_kernel, len(pieces), size, distances),
+        out_shape=jax.ShapeDtypeStruct((n, CORES, tokens, hidden), jnp.bfloat16),
+        compiler_params=pltpu.CompilerParams(vmem_limit_bytes=16 << 20),
+        cost_estimate=pl.CostEstimate(
+            flops=2 * CORES * n * tokens * hidden * depth,
+            bytes_accessed=2 * (n * tokens * (2 * hidden + depth) + 2 * hidden * depth),
+            transcendentals=0,
+        ),
+    )(weight, other, gates, *pieces)
+
+
+def layout_kernel(groups, far, weight, other, gates, top, low, *refs):
+    blocks, (out, stage, sem, far_sem) = refs[: len(groups)], refs[len(groups) :]
     size = out.shape[0]
-    tokens = gates.shape[2]
     me = lax.axis_index("expert")
-    place, core = ring_place(me // CORES, size), lax.rem(me, CORES)
-    stacked = jnp.concatenate([r[...] for r in rows], axis=0)
+    core = lax.rem(me, CORES)
+    place = ring_place(me // CORES, size)
+
+    def slot(distance):
+        return out.at[ring_chip(lax.rem(place + distance, size), size)]
+
     copies = []
-    for c, mat in enumerate((weight, other)):
-        product = lax.dot_general(
-            stacked, mat[...], (((1,), (1,)), ((), ())), preferred_element_type=jnp.float32
-        )
-        expert = core if c == 0 else 1 - core
-        for j, distance in enumerate(places):
-            chip = ring_chip(lax.rem(place + distance, size), size)
-            scale = gates[chip, expert]
-            stage[c, j] = (product[j * tokens : (j + 1) * tokens] * scale).astype(jnp.bfloat16)
-            copies.append(
-                pltpu.make_async_copy(stage.at[c, j], out.at[chip, expert], sem.at[c, j])
-            )
+    for block, distances in zip(blocks, groups):
+        for j, distance in enumerate(distances):
+            copies.append(pltpu.make_async_copy(block.at[j], slot(distance), sem.at[len(copies)]))
             copies[-1].start()
+    stacked = jnp.concatenate([top[...], low[...]], axis=0)
+    for mat, to in ((weight, core), (other, 1 - core)):
+        expert = me - core + to
+        stage[to] = scaled_products(stacked, mat, gates, expert, [far], size)[0]
+    copies.append(pltpu.make_async_copy(stage, slot(far), far_sem))
+    copies[-1].start()
     for copy in copies:
         copy.wait()
 
 
-def add_products(buffer, places, pieces, weight, other, gates):
-    size, experts, tokens, _ = gates.shape
+def laid_out(groups, blocks, far, top, low, size, weight, other, gates):
     hidden, depth = weight.shape
-    n = len(places)
-    kept = [] if buffer is None else [buffer]
+    tokens = blocks[0].shape[2]
     whole = pl.BlockSpec(memory_space=pltpu.VMEM)
     return pl.pallas_call(
-        functools.partial(products_kernel, len(pieces), places),
-        in_specs=[whole] * (3 + len(pieces)) + [pl.BlockSpec(memory_space=pltpu.HBM)] * len(kept),
+        functools.partial(layout_kernel, groups, far),
+        in_specs=[whole] * (5 + len(blocks)),
         out_specs=pl.BlockSpec(memory_space=pltpu.HBM),
-        out_shape=jax.ShapeDtypeStruct((size, experts, tokens, hidden), jnp.bfloat16),
-        input_output_aliases={3 + len(pieces): 0} if kept else {},
+        out_shape=pltpu.HBM((size, CORES, tokens, hidden), jnp.bfloat16),
         scratch_shapes=[
-            pltpu.VMEM((experts, n, tokens, hidden), jnp.bfloat16),
-            pltpu.SemaphoreType.DMA((experts, n)),
+            pltpu.VMEM((CORES, tokens, hidden), jnp.bfloat16),
+            pltpu.SemaphoreType.DMA((size - 1,)),
+            pltpu.SemaphoreType.DMA,
         ],
         compiler_params=pltpu.CompilerParams(vmem_limit_bytes=16 << 20),
         cost_estimate=pl.CostEstimate(
-            flops=2 * experts * n * tokens * hidden * depth,
-            bytes_accessed=2 * (n * tokens * (2 * hidden + depth) + 2 * hidden * depth),
+            flops=2 * CORES * tokens * hidden * depth,
+            bytes_accessed=2 * (size * tokens * 4 * hidden + 2 * hidden * depth),
             transcendentals=0,
         ),
-    )(weight, other, gates, *pieces, *kept)
+    )(weight, other, gates, top, low, *blocks)
 
 
 def pick_kernel(ids, blocks, out):
@@ -130,42 +170,42 @@
 
     other_mat = send(weight_mat, owners, 0, 1)
     matched = route_ids[:, :, None] == jnp.arange(owners, dtype=jnp.int32)
-    dense_gates = jnp.sum(
+    gates = jnp.sum(
         jnp.where(matched, route_gates[:, :, None].astype(jnp.float32), 0.0), axis=1
-    ).T.astype(jnp.bfloat16)
-    got_gates = lax.all_to_all(
-        dense_gates.reshape(size, CORES * tokens),
-        "expert",
-        split_axis=0,
-        concat_axis=0,
-        tiled=True,
-        axis_index_groups=same_core,
-    )
-    section_grad, got_gates = lax.optimization_barrier((section_grad, got_gates))
-    gates = got_gates.astype(jnp.float32).reshape(size, CORES, tokens, 1)
+    ).astype(jnp.bfloat16)
+    own_gates, reach = gates, 1
+    while reach < size:
+        gates = jnp.concatenate([gates, send(gates, owners, reach, 0)], axis=0)
+        reach *= 2
 
     half = tokens // 2
-    buffer = None
     back = ahead = section_grad
     waiting = {0: section_grad}
+    groups, blocks = [], []
     for step in range(1, size // 2):
         next_back, next_ahead = send(back, owners, 1, 0), send(ahead, owners, -1, 0)
-        if step > 1:
-            buffer = add_products(
-                buffer, list(waiting), list(waiting.values()), weight_mat, other_mat, gates
+        groups.append(list(waiting))
+        blocks.append(
+            products(
+                list(waiting),
+                list(waiting.values()),
+                size,
+                weight_mat,
+                other_mat,
+                own_gates if step == 1 else gates,
             )
-            waiting = {}
-            next_back, next_ahead, buffer = lax.optimization_barrier(
-                (next_back, next_ahead, buffer)
-            )
-        back, ahead = next_back, next_ahead
-        waiting.update({size - step: back, step: ahead})
+        )
+        back, ahead, blocks[-1] = lax.optimization_barrier((next_back, next_ahead, blocks[-1]))
+        waiting = {size - step: back, step: ahead}
     top_half = send(back[:half], owners, 1, 0)
     low_half = send(ahead[half:], owners, -1, 0)
-    buffer = add_products(
-        buffer, list(waiting), list(waiting.values()), weight_mat, other_mat, gates
-    )
-    buffer = add_products(buffer, [size // 2], [top_half, low_half], weight_mat, other_mat, gates)
+    groups.append(list(waiting))
+    blocks.append(
+        products(list(waiting), list(waiting.values()), size, weight_mat, other_mat, gates)
+    )
+    buffer = laid_out(
+        groups, blocks, size // 2, top_half, low_half, size, weight_mat, other_mat, gates
+    )
 
     returned = lax.all_to_all(
         buffer.reshape(size, CORES * tokens, hidden),

time: 90.1 us -> 95.7 us (1.062)
  waiting for transfers between devices: 38.6 us -> 52.9 us
  blocking collectives: 12.1 us -> 0 us
  starting transfers between devices: 15 us -> 23.8 us
  local copies, waits for them, and re-layouts: 5.53 us -> 2.23 us
  Pallas kernels: 17 us -> 14.8 us
    all_to_all x1 -> x0, blocking collectives: 12.1 us -> none  [dense_device(): lax.all_to_all(dense_gates.reshape(size, CORES * tokens), 'expert', split...]
    ppermute x9 -> x12, waiting for transfers between devices: 6.58 us -> 15.1 us  [send(): return lax.ppermute(block, 'expert', ring_route(owners, distance, flip))]
    ppermute x9 -> x12, starting transfers between devices: 8.71 us -> 16.6 us  [send(): return lax.ppermute(block, 'expert', ring_route(owners, distance, flip))]
    ppermute x1, waiting for transfers between devices: 0.01 us -> 6.61 us  [shifted(): return lax.ppermute(block, axis, route)]
    unnamed x10 -> x5, local copies, waits for them, and re-layouts: 4.18 us -> 1.98 us
    pallas_call x4 -> x5, Pallas kernels: 15.7 us -> 13.5 us  [the longest x4 10.4 us: products(): pl.pallas_call(functools.partial(products_kernel, len(pieces), size, dist...]
    reshape x1 -> x0, local copies, waits for them, and re-layouts: 1.13 us -> none  [dense_device(): gates = got_gates.astype(jnp.float32).reshape(size, CORES, tokens, 1)]
    all_to_all x1, starting transfers between devices: 3.78 us -> 4.74 us  [dense_device(): lax.all_to_all(buffer.reshape(size, CORES * tokens, hidden), 'expert', sp...]
  transfers between devices with their start and end apart: 11 -> 14, of which waited for: 5 -> 8; matrix products, arithmetic and copies ran while one was open for 3% -> 2% of each run, Pallas kernels for 14% -> 11%
where the time goes in v5:
time: 95.7 us; the launch traced here: 95.4 us
  waiting for transfers between devices  52.9 us (55%)
  starting transfers between devices  23.8 us (25%)
  Pallas kernels  14.8 us (15%)
  local copies, waits for them, and re-layouts  2.23 us (2%)
  other arithmetic  1.44 us (2%)
    all_to_all x1, waiting for transfers between devices, dense_device(): lax.all_to_all(buffer.reshape(size, CORES * tokens, hidden), 'expert', sp...  31.2 us
    ppermute x12, starting transfers between devices, send(): return lax.ppermute(block, 'expert', ring_route(owners, distance, flip))  16.6 us
    ppermute x12, waiting for transfers between devices, send(): return lax.ppermute(block, 'expert', ring_route(owners, distance, flip))  15.1 us
    pallas_call x4, Pallas kernels, products(): pl.pallas_call(functools.partial(products_kernel, len(pieces), size, dist...  10.4 us
    ppermute x1, waiting for transfers between devices, shifted(): return lax.ppermute(block, axis, route)  6.61 us
    all_to_all x1, starting transfers between devices, dense_device(): lax.all_to_all(buffer.reshape(size, CORES * tokens, hidden), 'expert', sp...  4.74 us
    pallas_call x1, Pallas kernels, laid_out(): pl.pallas_call(functools.partial(layout_kernel, groups, far), in_specs=[w...  3.09 us
    ppermute x1, starting transfers between devices, shifted(): return lax.ppermute(block, axis, route)  2.52 us
  transfers between devices with their start and end apart: 14, of which 8 were waited for; matrix products, arithmetic and copies ran while one was open for 2% of the time, Pallas kernels for 11%

profile of v5, /device:TPU:0, one launch (start us, length us, event | category | flops | bytes accessed | tf_op | source)
XLA Modules:
  0.0 95.4 jit_solution(6597269148034732294)
XLA Ops:
  0.0 0.5 collective-permute-start
  0.5 2.5 %collective-permute-start.4 = (bf16[1,64,2048]{2,1,0:T(8,128)(2,1)}, bf16[1,64,2048]{2,1,0:T(8,128)(2,1)}, u32[]{:S(2)}, u32[]{:S(2)}) collective-permute-start(bf16[1,64,2048]{2,1,0:T(8,128)(2,1)} %param.4), channel_id=1, source_target_pairs={{16,0},{0,16},{17,1},{1,17},{18,2},{2,18},{19,3},{3,19},{20,4},{4,... | collective-permute-start | bytes 786440 | tf_op jit(solution)/shard_map/ppermute | solution.py:17
  3.0 0.7 bitcast_convert_fusion
  3.7 6.6 %collective-permute-done.4 = bf16[1,64,2048]{2,1,0:T(8,128)(2,1)} collective-permute-done((bf16[1,64,2048]{2,1,0:T(8,128)(2,1)}, bf16[1,64,2048]{2,1,0:T(8,128)(2,1)}, u32[]{:S(2)}, u32[]{:S(2)}) %collective-permute-start.4) | collective-permute-done | bytes 262176 | tf_op jit(solution)/shard_map/ppermute | solution.py:17
  10.3 1.8 %collective-permute-start.5 = (bf16[64,2048]{1,0:T(8,128)(2,1)}, bf16[64,2048]{1,0:T(8,128)(2,1)S(1)}, u32[]{:S(2)}, u32[]{:S(2)}) collective-permute-start(bf16[64,2048]{1,0:T(8,128)(2,1)} %bitcast.3.refs_0_), channel_id=1, source_target_pairs={{0,4},{1,5},{4,8},{5,9},{8,12},{9,13},{12,14},{13,15},{14,10},{15,... | collective-permute-start | bytes 786440 | tf_op jit(solution)/shard_map/ppermute | solution.py:48
  12.1 0.2 collective-permute-start.6
  12.3 0.7 select_reduce_fusion
  13.0 0.1 copy.37.gates
  13.1 1.8 %collective-permute-start.1 = (bf16[64,16]{1,0:T(8,128)(2,1)S(1)}, bf16[64,16]{1,0:T(8,128)(2,1)S(1)}, u32[]{:S(2)}, u32[]{:S(2)}) collective-permute-start(bf16[64,16]{1,0:T(8,128)(2,1)S(1)} %copy.37.gates), channel_id=1, source_target_pairs={{0,4},{1,5},{4,8},{5,9},{8,12},{9,13},{12,14},{13,15},{14,10},{15,... | collective-permute-start | bytes 6152 | tf_op jit(solution)/shard_map/ppermute | solution.py:48
  14.9 4.0 %collective-permute-done.1 = bf16[64,16]{1,0:T(8,128)(2,1)S(1)} collective-permute-done((bf16[64,16]{1,0:T(8,128)(2,1)S(1)}, bf16[64,16]{1,0:T(8,128)(2,1)S(1)}, u32[]{:S(2)}, u32[]{:S(2)}) %collective-permute-start.1) | collective-permute-done | bytes 2080 | tf_op jit(solution)/shard_map/ppermute | solution.py:48
  19.0 2.7 %collective-permute-start.2 = (bf16[128,16]{1,0:T(8,128)(2,1)S(1)}, bf16[128,16]{1,0:T(8,128)(2,1)S(1)}, u32[]{:S(2)}, u32[]{:S(2)}) collective-permute-start(bf16[128,16]{1,0:T(8,128)(2,1)S(1)} %pad_maximum_fusion.2), channel_id=1, source_target_pairs={{0,8},{1,9},{4,12},{5,13},{8,14},{9,15},{12,10},{13,11},{14,6},{15... | collective-permute-start | bytes 12296 | tf_op jit(solution)/shard_map/ppermute | solution.py:48
  21.6 0.0 collective-permute-done.other
  21.6 0.0 copy-start
  21.6 1.9 %copy-done = bf16[1,1,768,2048]{3,2,1,0:T(8,128)(2,1)S(1)} copy-done((bf16[1,1,768,2048]{3,2,1,0:T(8,128)(2,1)S(1)}, bf16[1,1,768,2048]{3,2,1,0:T(8,128)(2,1)}, u32[]{:S(2)}) %copy-start) | copy-done | bytes 3145752
  23.5 3.0 %shard_map.46.refs_0_ = bf16[1,2,64,768]{3,2,1,0:T(8,128)(2,1)S(1)} custom-call(bf16[768,2048]{1,0:T(8,128)(2,1)S(1)} %bitcast.10, bf16[768,2048]{1,0:T(8,128)(2,1)S(1)} %collective-permute-done.other, bf16[64,16]{1,0:T(8,128)(2,1)S(1)} %copy.37.gates, bf16[64,2048]{1,0:T(8,128)(2,1)} %bitcast.3.refs_0_), custom_call_target="tpu_custom_call" | custom-call | flops 402653184 | bytes 6750208 | tf_op jit(solution)/shard_map/pallas_call | solution.py:81
  26.5 0.0 collective-permute-done.5.refs_0_
  26.5 0.0 collective-permute-done.6.refs_1_
  26.5 1.6 %collective-permute-start.7 = (bf16[64,2048]{1,0:T(8,128)(2,1)S(1)}, bf16[64,2048]{1,0:T(8,128)(2,1)S(1)}, u32[]{:S(2)}, u32[]{:S(2)}) collective-permute-start(bf16[64,2048]{1,0:T(8,128)(2,1)S(1)} %collective-permute-done.5.refs_0_), channel_id=1, source_target_pairs={{0,4},{1,5},{4,8},{5,9},{8,12},{9,13},{12,14},{13,15},{14,10},{15,... | collective-permute-start | bytes 786440 | tf_op jit(solution)/shard_map/ppermute | solution.py:48
  28.1 0.5 collective-permute-start.8
  28.6 0.0 collective-permute-done.2
  28.6 2.3 %collective-permute-start.3 = (bf16[256,16]{1,0:T(8,128)(2,1)S(1)}, bf16[256,16]{1,0:T(8,128)(2,1)S(1)}, u32[]{:S(2)}, u32[]{:S(2)}) collective-permute-start(bf16[256,16]{1,0:T(8,128)(2,1)S(1)} %pad_maximum_fusion.1), channel_id=1, source_target_pairs={{0,14},{1,15},{4,10},{5,11},{8,6},{9,7},{12,2},{13,3},{14,0},{15,1... | collective-permute-start | bytes 24584 | tf_op jit(solution)/shard_map/ppermute | solution.py:48
  31.0 4.8 %collective-permute-done.3 = bf16[256,16]{1,0:T(8,128)(2,1)S(1)} collective-permute-done((bf16[256,16]{1,0:T(8,128)(2,1)S(1)}, bf16[256,16]{1,0:T(8,128)(2,1)S(1)}, u32[]{:S(2)}, u32[]{:S(2)}) %collective-permute-start.3) | collective-permute-done | bytes 8224 | tf_op jit(solution)/shard_map/ppermute | solution.py:48
  35.8 3.1 %shard_map.47.refs_1_ = bf16[2,2,64,768]{3,2,1,0:T(8,128)(2,1)S(1)} custom-call(bf16[768,2048]{1,0:T(8,128)(2,1)S(1)} %bitcast.11, bf16[768,2048]{1,0:T(8,128)(2,1)S(1)} %collective-permute-done.other, bf16[512,16]{1,0:T(8,128)(2,1)S(1)} %pad_maximum_fusion.gates, bf16[64,2048]{1,0:T(8,128)(2,1)S(1)} %collective-permute-done.5.refs_0_, ...), custom_call_target="tpu_custom_call" | custom-call | flops 805306368 | bytes 7208960 | tf_op jit(solution)/shard_map/pallas_call | solution.py:81
  38.9 0.0 collective-permute-done.7.refs_0_
  38.9 0.0 collective-permute-done.8.refs_1_
  38.9 3.0 %collective-permute-start.10 = (bf16[64,2048]{1,0:T(8,128)(2,1)S(1)}, bf16[64,2048]{1,0:T(8,128)(2,1)S(1)}, u32[]{:S(2)}, u32[]{:S(2)}) collective-permute-start(bf16[64,2048]{1,0:T(8,128)(2,1)S(1)} %collective-permute-done.8.refs_1_), channel_id=1, source_target_pairs={{0,2},{1,3},{4,0},{5,1},{8,4},{9,5},{12,8},{13,9},{14,12},{15,13},... | collective-permute-start | bytes 786440 | tf_op jit(solution)/shard_map/ppermute | solution.py:48
  42.0 0.0 collective-permute-start.9
  42.0 2.2 %shard_map.48.refs_2_ = bf16[2,2,64,768]{3,2,1,0:T(8,128)(2,1)S(1)} custom-call(bf16[768,2048]{1,0:T(8,128)(2,1)S(1)} %bitcast.12, bf16[768,2048]{1,0:T(8,128)(2,1)S(1)} %collective-permute-done.other, bf16[512,16]{1,0:T(8,128)(2,1)S(1)} %pad_maximum_fusion.gates, bf16[64,2048]{1,0:T(8,128)(2,1)S(1)} %collective-permute-done.7.refs_0_, ...), custom_call_target="tpu_custom_call" | custom-call | flops 805306368 | bytes 7208960 | tf_op jit(solution)/shard_map/pallas_call | solution.py:81
  44.2 1.7 %collective-permute-done.10.refs_1_ = bf16[64,2048]{1,0:T(8,128)(2,1)S(1)} collective-permute-done((bf16[64,2048]{1,0:T(8,128)(2,1)S(1)}, bf16[64,2048]{1,0:T(8,128)(2,1)S(1)}, u32[]{:S(2)}, u32[]{:S(2)}) %collective-permute-start.10) | collective-permute-done | bytes 262176 | tf_op jit(solution)/shard_map/ppermute | solution.py:48
  45.9 3.8 %collective-permute-done.9.refs_0_ = bf16[64,2048]{1,0:T(8,128)(2,1)S(1)} collective-permute-done((bf16[64,2048]{1,0:T(8,128)(2,1)S(1)}, bf16[64,2048]{1,0:T(8,128)(2,1)S(1)}, u32[]{:S(2)}, u32[]{:S(2)}) %collective-permute-start.9) | collective-permute-done | bytes 262176 | tf_op jit(solution)/shard_map/ppermute | solution.py:48
  49.7 0.1 collective-permute-start.11
  49.8 2.1 %collective-permute-start.12 = (bf16[32,2048]{1,0:T(8,128)(2,1)S(1)}, bf16[32,2048]{1,0:T(8,128)(2,1)S(1)}, u32[]{:S(2)}, u32[]{:S(2)}) collective-permute-start(bf16[32,2048]{1,0:T(8,128)(2,1)S(1)} %slice.7), channel_id=1, source_target_pairs={{0,2},{1,3},{4,0},{5,1},{8,4},{9,5},{12,8},{13,9},{14,12},{15,13},... | collective-permute-start | bytes 393224 | tf_op jit(solution)/shard_map/ppermute | solution.py:48
  51.9 2.2 %shard_map.49.refs_3_ = bf16[2,2,64,768]{3,2,1,0:T(8,128)(2,1)S(1)} custom-call(bf16[768,2048]{1,0:T(8,128)(2,1)S(1)} %bitcast.13, bf16[768,2048]{1,0:T(8,128)(2,1)S(1)} %collective-permute-done.other, bf16[512,16]{1,0:T(8,128)(2,1)S(1)} %pad_maximum_fusion.gates, bf16[64,2048]{1,0:T(8,128)(2,1)S(1)} %collective-permute-done.9.refs_0_, ...), custom_call_target="tpu_custom_call" | custom-call | flops 805306368 | bytes 7208960 | tf_op jit(solution)/shard_map/pallas_call | solution.py:81
  54.1 0.7 collective-permute-done.11.top
  54.7 0.1 collective-permute-done.12.low
  54.8 3.1 %shard_map.50 = bf16[8,2,64,768]{3,2,1,0:T(8,128)(2,1)} custom-call(bf16[768,2048]{1,0:T(8,128)(2,1)S(1)} %bitcast.14, bf16[768,2048]{1,0:T(8,128)(2,1)S(1)} %collective-permute-done.other, bf16[512,16]{1,0:T(8,128)(2,1)S(1)} %pad_maximum_fusion.gates, bf16[32,2048]{1,0:T(8,128)(2,1)S(1)} %collective-permute-done.11.top, ...), custom_call_target="tpu_custom_call" | custom-call | flops 402653184 | bytes 9437184 | tf_op jit(solution)/shard_map/pallas_call | solution.py:122
  57.9 0.0 copy-start.1
  57.9 4.7 %all-to-all-start = ((bf16[8,128,768]{2,1,0:T(8,128)(2,1)}), bf16[8,128,768]{2,1,0:T(8,128)(2,1)S(1)}, u32[]{:S(2)}, u32[]{:S(2)}) async-start(bf16[8,128,768]{2,1,0:T(8,128)(2,1)} %bitcast.16), calls=%async_computation | async-start | bytes 3145728 | tf_op jit(solution)/shard_map/all_to_all | solution.py:210
  62.7 0.0 copy-done.1
  62.7 0.1 copy.36
  62.8 0.1 reshape_squeeze.4.ids
  62.9 31.2 %all-to-all-done = bf16[8,128,768]{2,1,0:T(8,128)(2,1)S(1)} async-done(((bf16[8,128,768]{2,1,0:T(8,128)(2,1)}), bf16[8,128,768]{2,1,0:T(8,128)(2,1)S(1)}, u32[]{:S(2)}, u32[]{:S(2)}) %all-to-all-start) | async-done | bytes 1572896 | tf_op jit(solution)/shard_map/all_to_all | solution.py:210
  94.1 1.3 %shard_map.51 = bf16[512,768]{1,0:T(8,128)(2,1)} custom-call(s32[512,1]{1,0:T(8,128)S(1)} %reshape_squeeze.4.ids, bf16[16,64,768]{2,1,0:T(8,128)(2,1)S(1)} %bitcast.15), custom_call_target="tpu_custom_call" | custom-call | tf_op jit(solution)/shard_map/pallas_call | solution.py:157
  (5 shorter events, 0.1 us)
Async XLA Ops:
  0.0 21.6 %collective-permute-start = (bf16[768,2048]{1,0:T(8,128)(2,1)}, bf16[768,2048]{1,0:T(8,128)(2,1)S(1)}, u32[]{:S(2)}, u32[]{:S(2)}) collective-permute-start(bf16[768,2048]{1,0:T(8,128)(2,1)} %bitcast.9), channel_id=1, source_target_pairs={{0,1},{1,0},{4,5},{5,4},{8,9},{9,8},{12,13},{13,12},{14,15},{15,14... | collective-permute-start | bytes 9437192 | tf_op jit(solution)/shard_map/ppermute | solution.py:48
  0.5 9.8 %collective-permute-start.4 = (bf16[1,64,2048]{2,1,0:T(8,128)(2,1)}, bf16[1,64,2048]{2,1,0:T(8,128)(2,1)}, u32[]{:S(2)}, u32[]{:S(2)}) collective-permute-start(bf16[1,64,2048]{2,1,0:T(8,128)(2,1)} %param.4), channel_id=1, source_target_pairs={{16,0},{0,16},{17,1},{1,17},{18,2},{2,18},{19,3},{3,19},{20,4},{4,... | collective-permute-start | bytes 786440 | tf_op jit(solution)/shard_map/ppermute | solution.py:17
  10.3 16.2 %collective-permute-start.5 = (bf16[64,2048]{1,0:T(8,128)(2,1)}, bf16[64,2048]{1,0:T(8,128)(2,1)S(1)}, u32[]{:S(2)}, u32[]{:S(2)}) collective-permute-start(bf16[64,2048]{1,0:T(8,128)(2,1)} %bitcast.3.refs_0_), channel_id=1, source_target_pairs={{0,4},{1,5},{4,8},{5,9},{8,12},{9,13},{12,14},{13,15},{14,10},{15,... | collective-permute-start | bytes 786440 | tf_op jit(solution)/shard_map/ppermute | solution.py:48
  12.1 14.4 %collective-permute-start.6 = (bf16[64,2048]{1,0:T(8,128)(2,1)}, bf16[64,2048]{1,0:T(8,128)(2,1)}, u32[]{:S(2)}, u32[]{:S(2)}) collective-permute-start(bf16[64,2048]{1,0:T(8,128)(2,1)} %bitcast.3.refs_0_), channel_id=1, source_target_pairs={{0,2},{1,3},{4,0},{5,1},{8,4},{9,5},{12,8},{13,9},{14,12},{15,13},... | collective-permute-start | bytes 786440 | tf_op jit(solution)/shard_map/ppermute | solution.py:48
  13.1 5.9 %collective-permute-start.1 = (bf16[64,16]{1,0:T(8,128)(2,1)S(1)}, bf16[64,16]{1,0:T(8,128)(2,1)S(1)}, u32[]{:S(2)}, u32[]{:S(2)}) collective-permute-start(bf16[64,16]{1,0:T(8,128)(2,1)S(1)} %copy.37.gates), channel_id=1, source_target_pairs={{0,4},{1,5},{4,8},{5,9},{8,12},{9,13},{12,14},{13,15},{14,10},{15,... | collective-permute-start | bytes 6152 | tf_op jit(solution)/shard_map/ppermute | solution.py:48
  19.0 9.6 %collective-permute-start.2 = (bf16[128,16]{1,0:T(8,128)(2,1)S(1)}, bf16[128,16]{1,0:T(8,128)(2,1)S(1)}, u32[]{:S(2)}, u32[]{:S(2)}) collective-permute-start(bf16[128,16]{1,0:T(8,128)(2,1)S(1)} %pad_maximum_fusion.2), channel_id=1, source_target_pairs={{0,8},{1,9},{4,12},{5,13},{8,14},{9,15},{12,10},{13,11},{14,6},{15... | collective-permute-start | bytes 12296 | tf_op jit(solution)/shard_map/ppermute | solution.py:48
  21.6 1.9 %copy-start = (bf16[1,1,768,2048]{3,2,1,0:T(8,128)(2,1)S(1)}, bf16[1,1,768,2048]{3,2,1,0:T(8,128)(2,1)}, u32[]{:S(2)}) copy-start(bf16[1,1,768,2048]{3,2,1,0:T(8,128)(2,1)} %param.7) | copy-start | bytes 9437188
  26.5 12.4 %collective-permute-start.7 = (bf16[64,2048]{1,0:T(8,128)(2,1)S(1)}, bf16[64,2048]{1,0:T(8,128)(2,1)S(1)}, u32[]{:S(2)}, u32[]{:S(2)}) collective-permute-start(bf16[64,2048]{1,0:T(8,128)(2,1)S(1)} %collective-permute-done.5.refs_0_), channel_id=1, source_target_pairs={{0,4},{1,5},{4,8},{5,9},{8,12},{9,13},{12,14},{13,15},{14,10},{15,... | collective-permute-start | bytes 786440 | tf_op jit(solution)/shard_map/ppermute | solution.py:48
  28.1 10.8 %collective-permute-start.8 = (bf16[64,2048]{1,0:T(8,128)(2,1)}, bf16[64,2048]{1,0:T(8,128)(2,1)S(1)}, u32[]{:S(2)}, u32[]{:S(2)}) collective-permute-start(bf16[64,2048]{1,0:T(8,128)(2,1)} %collective-permute-done.6.refs_1_), channel_id=1, source_target_pairs={{0,2},{1,3},{4,0},{5,1},{8,4},{9,5},{12,8},{13,9},{14,12},{15,13},... | collective-permute-start | bytes 786440 | tf_op jit(solution)/shard_map/ppermute | solution.py:48
  28.6 7.1 %collective-permute-start.3 = (bf16[256,16]{1,0:T(8,128)(2,1)S(1)}, bf16[256,16]{1,0:T(8,128)(2,1)S(1)}, u32[]{:S(2)}, u32[]{:S(2)}) collective-permute-start(bf16[256,16]{1,0:T(8,128)(2,1)S(1)} %pad_maximum_fusion.1), channel_id=1, source_target_pairs={{0,14},{1,15},{4,10},{5,11},{8,6},{9,7},{12,2},{13,3},{14,0},{15,1... | collective-permute-start | bytes 24584 | tf_op jit(solution)/shard_map/ppermute | solution.py:48
  38.9 6.9 %collective-permute-start.10 = (bf16[64,2048]{1,0:T(8,128)(2,1)S(1)}, bf16[64,2048]{1,0:T(8,128)(2,1)S(1)}, u32[]{:S(2)}, u32[]{:S(2)}) collective-permute-start(bf16[64,2048]{1,0:T(8,128)(2,1)S(1)} %collective-permute-done.8.refs_1_), channel_id=1, source_target_pairs={{0,2},{1,3},{4,0},{5,1},{8,4},{9,5},{12,8},{13,9},{14,12},{15,13},... | collective-permute-start | bytes 786440 | tf_op jit(solution)/shard_map/ppermute | solution.py:48
  42.0 7.7 %collective-permute-start.9 = (bf16[64,2048]{1,0:T(8,128)(2,1)S(1)}, bf16[64,2048]{1,0:T(8,128)(2,1)S(1)}, u32[]{:S(2)}, u32[]{:S(2)}) collective-permute-start(bf16[64,2048]{1,0:T(8,128)(2,1)S(1)} %collective-permute-done.7.refs_0_), channel_id=1, source_target_pairs={{0,4},{1,5},{4,8},{5,9},{8,12},{9,13},{12,14},{13,15},{14,10},{15,... | collective-permute-start | bytes 786440 | tf_op jit(solution)/shard_map/ppermute | solution.py:48
  49.7 5.0 %collective-permute-start.11 = (bf16[32,2048]{1,0:T(8,128)(2,1)S(1)}, bf16[32,2048]{1,0:T(8,128)(2,1)S(1)}, u32[]{:S(2)}, u32[]{:S(2)}) collective-permute-start(bf16[32,2048]{1,0:T(8,128)(2,1)S(1)} %slice.6), channel_id=1, source_target_pairs={{0,4},{1,5},{4,8},{5,9},{8,12},{9,13},{12,14},{13,15},{14,10},{15,... | collective-permute-start | bytes 393224 | tf_op jit(solution)/shard_map/ppermute | solution.py:48
  49.8 5.0 %collective-permute-start.12 = (bf16[32,2048]{1,0:T(8,128)(2,1)S(1)}, bf16[32,2048]{1,0:T(8,128)(2,1)S(1)}, u32[]{:S(2)}, u32[]{:S(2)}) collective-permute-start(bf16[32,2048]{1,0:T(8,128)(2,1)S(1)} %slice.7), channel_id=1, source_target_pairs={{0,2},{1,3},{4,0},{5,1},{8,4},{9,5},{12,8},{13,9},{14,12},{15,13},... | collective-permute-start | bytes 393224 | tf_op jit(solution)/shard_map/ppermute | solution.py:48
  57.9 4.8 %copy-start.1 = (s32[1,64,8]{1,2,0:T(8,128)S(1)}, s32[1,64,8]{1,2,0:T(8,128)}, u32[]{:S(2)}) copy-start(s32[1,64,8]{1,2,0:T(8,128)} %param.5) | copy-start | bytes 6148
  57.9 36.2 %all-to-all-start = ((bf16[8,128,768]{2,1,0:T(8,128)(2,1)}), bf16[8,128,768]{2,1,0:T(8,128)(2,1)S(1)}, u32[]{:S(2)}, u32[]{:S(2)}) async-start(bf16[8,128,768]{2,1,0:T(8,128)(2,1)} %bitcast.16), calls=%async_computation | async-start | bytes 3145728 | tf_op jit(solution)/shard_map/all_to_all | solution.py:210

commit v6 on v2

v6 whole, which is shorter than its diff:
```python
import functools

import jax
import jax.numpy as jnp
from jax import lax
from jax.experimental import pallas as pl
from jax.experimental.pallas import tpu as pltpu
from jax.sharding import PartitionSpec as P

COLUMNS = 2
CORES = 2
LANES = 128


def shifted(block, axis, distance):
    devices = range(lax.axis_size(axis))
    route = [((i - distance) % len(devices), i) for i in devices]
    return lax.ppermute(block, axis, route)


def ring_place(chip, size):
    z, x = lax.div(chip, COLUMNS), lax.rem(chip, COLUMNS)
    return jnp.where(x == 0, z, size - 1 - z)


def ring_order(owners):
    height = owners // (COLUMNS * CORES)
    up = [z * COLUMNS for z in range(height)]
    down = [z * COLUMNS + 1 for z in reversed(range(height))]
    return up + down


def ring_route(owners, distance, flip):
    order = ring_order(owners)
    route = []
    for place, chip in enumerate(order):
        target = order[(place + distance) % len(order)]
        for core in range(CORES):
            route.append((chip * CORES + core, target * CORES + (core ^ flip)))
    return route


def send(block, owners, distance, flip):
    return lax.ppermute(block, "expert", ring_route(owners, distance, flip))


def widen_kernel(ids, gates, rows, out):
    depth = rows.shape[1]
    out[:, :depth] = rows[...]
    expert = lax.broadcasted_iota(jnp.int32, (rows.shape[0], LANES), 1)
    total = jnp.zeros(expert.shape, jnp.float32)
    for k in range(ids.shape[1]):
        gate = gates[:, k : k + 1].astype(jnp.float32)
        total += jnp.where(expert == ids[:, k : k + 1], gate, 0.0)
    out[:, depth:] = total.astype(jnp.bfloat16)


def widened(ids, gates, rows):
    return pl.pallas_call(
        widen_kernel,
        out_shape=jax.ShapeDtypeStruct((rows.shape[0], rows.shape[1] + LANES), jnp.bfloat16),
        compiler_params=pltpu.CompilerParams(vmem_limit_bytes=16 << 20),
    )(ids, gates, rows)


def products_kernel(count, weight, other, *refs):
    rows, outs = refs[:count], refs[count:]
    hidden, depth = weight.shape
    tokens = outs[0].shape[1]
    me = lax.axis_index("expert")
    core = lax.rem(me, CORES)
    stacked = jnp.concatenate([r[...] for r in rows], axis=0)
    gates = stacked[:, depth:].astype(jnp.float32)
    column = lax.broadcasted_iota(jnp.int32, gates.shape, 1)
    for mat, to in ((weight, core), (other, 1 - core)):
        scale = jnp.sum(jnp.where(column == me - core + to, gates, 0.0), axis=1, keepdims=True)
        product = lax.dot_general(
            stacked[:, :depth],
            mat[...],
            (((1,), (1,)), ((), ())),
            preferred_element_type=jnp.float32,
        )
        scaled = (product * scale).astype(jnp.bfloat16)
        for j, out in enumerate(outs):
            out[to] = scaled[j * tokens : (j + 1) * tokens]


def products(pieces, tokens, weight, other):
    hidden, depth = weight.shape
    total = sum(p.shape[0] for p in pieces)
    return pl.pallas_call(
        functools.partial(products_kernel, len(pieces)),
        out_shape=[jax.ShapeDtypeStruct((CORES, tokens, hidden), jnp.bfloat16)] * (total // tokens),
        compiler_params=pltpu.CompilerParams(vmem_limit_bytes=16 << 20),
        cost_estimate=pl.CostEstimate(
            flops=2 * CORES * total * hidden * depth,
            bytes_accessed=2 * (total * (2 * hidden + depth) + 2 * hidden * depth),
            transcendentals=0,
        ),
    )(weight, other, *pieces)


def pick_kernel(labels, *refs):
    blocks, out = refs[:-1], refs[-1]
    experts, tokens, _ = blocks[0].shape
    top = out.shape[0] // tokens
    span = 16
    routes = span * top
    owners = len(blocks) * experts
    column = lax.broadcasted_iota(jnp.int32, (routes, owners * span), 1)
    token = lax.broadcasted_iota(jnp.int32, (routes, owners * span), 0) // top
    for g in range(tokens // span):
        stacked = jnp.concatenate(
            [b[c, g * span : (g + 1) * span, :] for b in blocks for c in range(experts)], axis=0
        )
        wanted = labels[g * routes : (g + 1) * routes, :] * span + token
        pick = jnp.where(column == wanted, 1.0, 0.0).astype(jnp.bfloat16)
        rows = jnp.dot(pick, stacked, preferred_element_type=jnp.float32)
        out[g * routes : (g + 1) * routes, :] = rows.astype(jnp.bfloat16)


def pick_routes(labels, blocks):
    return pl.pallas_call(
        pick_kernel,
        out_shape=jax.ShapeDtypeStruct((labels.shape[0], blocks[0].shape[2]), jnp.bfloat16),
        compiler_params=pltpu.CompilerParams(vmem_limit_bytes=16 << 20),
    )(labels, *blocks)


def dense_device(section_grad, route_ids, route_gates, weight_mat):
    tokens, top = route_ids.shape
    owners = lax.axis_size("expert")
    hidden = weight_mat.shape[0]
    size = owners // CORES
    place = ring_place(lax.axis_index("expert") // CORES, size)
    labels = lax.rem(ring_place(route_ids // CORES, size) - place + size, size) * CORES + lax.rem(
        route_ids, CORES
    )

    other_mat = send(weight_mat, owners, 0, 1)
    rows = widened(route_ids, route_gates, section_grad)

    half, far = tokens // 2, size // 2
    back = ahead = rows
    waiting = {0: rows}
    received = [None] * size
    for step in range(1, far + 1):
        if step < far:
            next_back, next_ahead = send(back, owners, 1, 0), send(ahead, owners, -1, 0)
        else:
            next_back, next_ahead = (
                send(back[:half], owners, 1, 0),
                send(ahead[half:], owners, -1, 0),
            )
        results = products(list(waiting.values()), tokens, weight_mat, other_mat)
        back, ahead, results = lax.optimization_barrier((next_back, next_ahead, results))
        for distance, result in zip(waiting, results):
            received[(-distance) % size] = send(result, owners, distance, 0) if distance else result
        waiting = {size - step: back, step: ahead}
    (result,) = products([back, ahead], tokens, weight_mat, other_mat)
    received[far] = send(result, owners, far, 0)
    out = pick_routes(labels.reshape(tokens * top, 1), received)
    return out.reshape(1, tokens, top, hidden)


def slotted_device(section_grad, route_ids, route_gates, weight_mat, capacity):
    tokens, top = route_ids.shape
    owners = lax.axis_size("expert")
    ids = jnp.arange(owners, dtype=jnp.int32)
    slots = jnp.arange(capacity, dtype=jnp.int32)
    matched = (route_ids[:, :, None] == ids[None, None, :]).astype(jnp.int32)
    hits = jnp.sum(matched, axis=1)
    rank = jnp.cumsum(hits, axis=0) - hits
    position = route_ids * capacity + jnp.sum(matched * rank[:, None, :], axis=2)
    gate_owner = jnp.einsum(
        "tk,tke->te", route_gates.astype(jnp.float32), matched.astype(jnp.float32)
    )
    slot_pick = (hits[:, :, None] == 1) & (rank[:, :, None] == slots[None, None, :])
    send_rows = jnp.einsum(
        "tem,td->emd",
        slot_pick.astype(jnp.bfloat16),
        section_grad,
        preferred_element_type=jnp.float32,
    ).astype(jnp.bfloat16)
    send_gates = jnp.einsum("tem,te->em", slot_pick.astype(jnp.float32), gate_owner).astype(
        jnp.bfloat16
    )
    got_rows = lax.all_to_all(send_rows, "expert", split_axis=0, concat_axis=0, tiled=True)
    got_gates = lax.all_to_all(send_gates, "expert", split_axis=0, concat_axis=0, tiled=True)
    product = lax.dot_general(
        got_rows.reshape(owners * capacity, got_rows.shape[2]),
        weight_mat,
        (((1,), (1,)), ((), ())),
        preferred_element_type=jnp.float32,
    ).reshape(owners, capacity, weight_mat.shape[0])
    returned = lax.all_to_all(
        (product * got_gates.astype(jnp.float32)[:, :, None]).astype(jnp.bfloat16),
        "expert",
        split_axis=0,
        concat_axis=0,
        tiled=True,
    )
    flat = returned.reshape(owners * capacity, returned.shape[2])
    out = jnp.take(flat, position.reshape(tokens * top), axis=0)
    return out.reshape(1, tokens, top, returned.shape[2])


def per_device(upstream, expert_ids, gate_weights, expert_weight):
    section_grad = shifted(upstream, "pipe", -1)[0]
    route_ids = expert_ids[0]
    route_gates = gate_weights[0]
    weight_mat = expert_weight[0, 0]
    tokens, top = route_ids.shape
    owners = lax.axis_size("expert")
    capacity = 2 * tokens * top // owners
    if capacity >= tokens:
        return dense_device(section_grad, route_ids, route_gates, weight_mat)
    return slotted_device(section_grad, route_ids, route_gates, weight_mat, capacity)


def solution(mesh):
    in_specs = (
        P("pipe", "expert", None),
        P("pipe", "expert", None),
        P("pipe", "expert", None),
        P("pipe", "expert", None, None),
    )
    out_specs = P("pipe", "expert", None, None)
    return jax.shard_map(
        per_device, mesh=mesh, in_specs=in_specs, out_specs=out_specs, check_vma=False
    )
```

time: 107 us -> 82.1 us (0.77)
  the two profiles are of different devices: /device:TPU:0 before, /device:TPU:2 now
where the time goes in v6:
time: 82.1 us; the launch traced here: 81.7 us
  waiting for transfers between devices  26.4 us (32%)
  starting transfers between devices  22.2 us (27%)
  local copies, waits for them, and re-layouts  16.9 us (21%)
  Pallas kernels  15.7 us (19%)
    ppermute x16, starting transfers between devices, send(): return lax.ppermute(block, 'expert', ring_route(owners, distance, flip))  20.7 us
    ppermute x16, waiting for transfers between devices, send(): return lax.ppermute(block, 'expert', ring_route(owners, distance, flip))  20.5 us
    unnamed x30, local copies, waits for them, and re-layouts  14.7 us
    pallas_call x5, Pallas kernels, products(): pl.pallas_call(functools.partial(products_kernel, len(pieces)), out_shape...  12.2 us
    ppermute x1, waiting for transfers between devices, shifted(): return lax.ppermute(block, axis, route)  5.97 us
    pallas_call x1, Pallas kernels, pick_routes(): pl.pallas_call(pick_kernel, out_shape=jax.ShapeDtypeStruct((labels.shape[...  2.32 us
  transfers between devices with their start and end apart: 17, of which 7 were waited for; matrix products, arithmetic and copies ran while one was open for 5% of the time, Pallas kernels for 16%

profile of v6, /device:TPU:2, one launch (start us, length us, event | category | flops | bytes accessed | tf_op | source)
XLA Modules:
  0.0 81.7 jit_solution(15328202947221372813)
XLA Ops:
  0.0 0.0 collective-permute-start.3
  0.0 1.5 %collective-permute-start = (bf16[1,64,2048]{2,1,0:T(8,128)(2,1)}, bf16[1,64,2048]{2,1,0:T(8,128)(2,1)}, u32[]{:S(2)}, u32[]{:S(2)}) collective-permute-start(bf16[1,64,2048]{2,1,0:T(8,128)(2,1)} %param.4), channel_id=1, source_target_pairs={{16,0},{0,16},{17,1},{1,17},{18,2},{2,18},{19,3},{3,19},{20,4},{4,... | collective-permute-start | bytes 786440 | tf_op jit(solution)/shard_map/ppermute | solution.py:18
  1.5 0.8 copy.8
  2.3 0.8 copy.14
  3.1 6.0 %collective-permute-done = bf16[1,64,2048]{2,1,0:T(8,128)(2,1)} collective-permute-done((bf16[1,64,2048]{2,1,0:T(8,128)(2,1)}, bf16[1,64,2048]{2,1,0:T(8,128)(2,1)}, u32[]{:S(2)}, u32[]{:S(2)}) %collective-permute-start) | collective-permute-done | bytes 262176 | tf_op jit(solution)/shard_map/ppermute | solution.py:18
  9.0 1.1 %shard_map.46.refs_0_ = bf16[64,2176]{1,0:T(8,128)(2,1)S(1)} custom-call(s32[64,8]{1,0:T(8,128)S(1)} %bitcast.11, bf16[64,8]{1,0:T(8,128)(2,1)S(1)} %bitcast.12, bf16[64,2048]{1,0:T(8,128)(2,1)} %bitcast.2.rows), custom_call_target="tpu_custom_call" | custom-call | tf_op jit(solution)/shard_map/pallas_call | solution.py:59
  10.2 0.4 collective-permute-start.1
  10.6 1.7 %collective-permute-start.2 = (bf16[64,2176]{1,0:T(8,128)(2,1)S(1)}, bf16[64,2176]{1,0:T(8,128)(2,1)S(1)}, u32[]{:S(2)}, u32[]{:S(2)}) collective-permute-start(bf16[64,2176]{1,0:T(8,128)(2,1)S(1)} %shard_map.46.refs_0_), channel_id=1, source_target_pairs={{0,2},{1,3},{4,0},{5,1},{8,4},{9,5},{12,8},{13,9},{14,12},{15,13},... | collective-permute-start | bytes 835592 | tf_op jit(solution)/shard_map/ppermute | solution.py:44
  12.3 0.0 collective-permute-done.3.other
  12.3 0.0 copy-start.2
  12.3 1.6 %copy-done.2 = bf16[768,2048]{1,0:T(8,128)(2,1)} copy-done((bf16[768,2048]{1,0:T(8,128)(2,1)}, bf16[768,2048]{1,0:T(8,128)(2,1)S(1)}, u32[]{:S(2)}) %copy-start.2) | copy-done | bytes 3145752
  13.9 0.0 copy-start
  13.9 1.9 %copy-done = bf16[1,1,768,2048]{3,2,1,0:T(8,128)(2,1)S(1)} copy-done((bf16[1,1,768,2048]{3,2,1,0:T(8,128)(2,1)S(1)}, bf16[1,1,768,2048]{3,2,1,0:T(8,128)(2,1)}, u32[]{:S(2)}) %copy-start) | copy-done | bytes 3145752
  15.8 1.9 %copy-done.3 = bf16[768,2048]{1,0:T(8,128)(2,1)S(1)} copy-done((bf16[768,2048]{1,0:T(8,128)(2,1)S(1)}, bf16[768,2048]{1,0:T(8,128)(2,1)}, u32[]{:S(2)}) %copy-start.3) | copy-done | bytes 3145752
  17.7 2.0 %shard_map.47.refs_0_ = bf16[2,64,768]{2,1,0:T(8,128)(2,1)S(1)} custom-call(bf16[768,2048]{1,0:T(8,128)(2,1)S(1)} %bitcast.6, bf16[768,2048]{1,0:T(8,128)(2,1)S(1)} %copy-done.3, bf16[64,2176]{1,0:T(8,128)(2,1)S(1)} %shard_map.46.refs_0_), custom_call_target="tpu_custom_call" | custom-call | flops 402653184 | bytes 6750208 | tf_op jit(solution)/shard_map/pallas_call | solution.py:91
  19.7 0.0 collective-permute-done.1.refs_0_
  19.7 0.0 collective-permute-done.2.refs_1_
  19.7 0.6 collective-permute-start.4
  20.4 1.4 %collective-permute-start.5 = (bf16[64,2176]{1,0:T(8,128)(2,1)S(1)}, bf16[64,2176]{1,0:T(8,128)(2,1)S(1)}, u32[]{:S(2)}, u32[]{:S(2)}) collective-permute-start(bf16[64,2176]{1,0:T(8,128)(2,1)S(1)} %collective-permute-done.2.refs_1_), channel_id=1, source_target_pairs={{0,2},{1,3},{4,0},{5,1},{8,4},{9,5},{12,8},{13,9},{14,12},{15,13},... | collective-permute-start | bytes 835592 | tf_op jit(solution)/shard_map/ppermute | solution.py:44
  21.8 0.0 copy-done.1
  21.8 1.9 %copy-done.4 = bf16[768,2048]{1,0:T(8,128)(2,1)S(1)} copy-done((bf16[768,2048]{1,0:T(8,128)(2,1)S(1)}, bf16[768,2048]{1,0:T(8,128)(2,1)}, u32[]{:S(2)}) %copy-start.4) | copy-done | bytes 3145752
  23.7 2.9 %shard_map.48 = (bf16[2,64,768]{2,1,0:T(8,128)(2,1)}, bf16[2,64,768]{2,1,0:T(8,128)(2,1)}) custom-call(bf16[768,2048]{1,0:T(8,128)(2,1)S(1)} %bitcast.7, bf16[768,2048]{1,0:T(8,128)(2,1)S(1)} %copy-done.4, bf16[64,2176]{1,0:T(8,128)(2,1)S(1)} %collective-permute-done.1.refs_0_, bf16[64,2176]{1,0:T(8,128)(2,1)S(1)} %collective-permute-done.2.refs_1_), custom_call_target="tpu_custom_call" | custom-call | flops 805306368 | bytes 7208960 | tf_op jit(solution)/shard_map/pallas_call | solution.py:91
  26.6 0.9 %collective-permute-done.4.refs_0_ = bf16[64,2176]{1,0:T(8,128)(2,1)S(1)} collective-permute-done((bf16[64,2176]{1,0:T(8,128)(2,1)S(1)}, bf16[64,2176]{1,0:T(8,128)(2,1)S(1)}, u32[]{:S(2)}, u32[]{:S(2)}) %collective-permute-start.4) | collective-permute-done | bytes 278560 | tf_op jit(solution)/shard_map/ppermute | solution.py:44
  27.5 0.2 collective-permute-done.5.refs_1_
  27.7 1.6 %collective-permute-start.7 = (bf16[64,2176]{1,0:T(8,128)(2,1)S(1)}, bf16[64,2176]{1,0:T(8,128)(2,1)S(1)}, u32[]{:S(2)}, u32[]{:S(2)}) collective-permute-start(bf16[64,2176]{1,0:T(8,128)(2,1)S(1)} %collective-permute-done.4.refs_0_), channel_id=1, source_target_pairs={{0,4},{1,5},{4,8},{5,9},{8,12},{9,13},{12,14},{13,15},{14,10},{15,... | collective-permute-start | bytes 835592 | tf_op jit(solution)/shard_map/ppermute | solution.py:44
  29.3 0.4 collective-permute-start.8
  29.8 1.6 %collective-permute-start.16 = (bf16[2,64,768]{2,1,0:T(8,128)(2,1)}, bf16[2,64,768]{2,1,0:T(8,128)(2,1)}, u32[]{:S(2)}, u32[]{:S(2)}) collective-permute-start(bf16[2,64,768]{2,1,0:T(8,128)(2,1)} %get-tuple-element.46), channel_id=1, source_target_pairs={{0,4},{1,5},{4,8},{5,9},{8,12},{9,13},{12,14},{13,15},{14,10},{15,... | collective-permute-start | bytes 589832 | tf_op jit(solution)/shard_map/ppermute | solution.py:44
  31.4 0.4 collective-permute-start.6
  31.8 2.2 %shard_map.49 = (bf16[2,64,768]{2,1,0:T(8,128)(2,1)S(1)}, bf16[2,64,768]{2,1,0:T(8,128)(2,1)S(1)}) custom-call(bf16[768,2048]{1,0:T(8,128)(2,1)S(1)} %bitcast.8, bf16[768,2048]{1,0:T(8,128)(2,1)S(1)} %copy-done.4, bf16[64,2176]{1,0:T(8,128)(2,1)S(1)} %collective-permute-done.4.refs_0_, bf16[64,2176]{1,0:T(8,128)(2,1)S(1)} %collective-permute-done.5.refs_1_), custom_call_target="tpu_custom_call" | custom-call | flops 805306368 | bytes 7208960 | tf_op jit(solution)/shard_map/pallas_call | solution.py:91
  34.0 0.0 copy-start.10
  34.0 0.7 copy-done.10
  34.7 0.7 copy-done.12
  35.3 1.1 %collective-permute-done.7.refs_0_ = bf16[64,2176]{1,0:T(8,128)(2,1)S(1)} collective-permute-done((bf16[64,2176]{1,0:T(8,128)(2,1)S(1)}, bf16[64,2176]{1,0:T(8,128)(2,1)S(1)}, u32[]{:S(2)}, u32[]{:S(2)}) %collective-permute-start.7) | collective-permute-done | bytes 278560 | tf_op jit(solution)/shard_map/ppermute | solution.py:44
  36.4 1.2 %collective-permute-done.8.refs_1_ = bf16[64,2176]{1,0:T(8,128)(2,1)S(1)} collective-permute-done((bf16[64,2176]{1,0:T(8,128)(2,1)S(1)}, bf16[64,2176]{1,0:T(8,128)(2,1)S(1)}, u32[]{:S(2)}, u32[]{:S(2)}) %collective-permute-start.8) | collective-permute-done | bytes 278560 | tf_op jit(solution)/shard_map/ppermute | solution.py:44
  37.6 0.7 slice.6
  38.3 0.7 copy-done.6
  39.0 1.6 %collective-permute-start.10 = (bf16[32,2176]{1,0:T(8,128)(2,1)}, bf16[32,2176]{1,0:T(8,128)(2,1)S(1)}, u32[]{:S(2)}, u32[]{:S(2)}) collective-permute-start(bf16[32,2176]{1,0:T(8,128)(2,1)} %slice.6), channel_id=1, source_target_pairs={{0,4},{1,5},{4,8},{5,9},{8,12},{9,13},{12,14},{13,15},{14,10},{15,... | collective-permute-start | bytes 417800 | tf_op jit(solution)/shard_map/ppermute | solution.py:44
  40.6 0.0 copy-done.8
  40.6 0.7 slice.7
  41.3 0.4 collective-permute-start.11
  41.7 0.8 %squeeze.19 = s32[512,1]{1,0:T(8,128)} reshape(s32[1,64,8]{2,1,0:T(8,128)S(1)} %copy.8) | data formatting | bytes 4096 | tf_op jit(solution)/shard_map/squeeze | solution.py:210
  42.6 2.6 %collective-permute-start.15 = (bf16[2,64,768]{2,1,0:T(8,128)(2,1)}, bf16[2,64,768]{2,1,0:T(8,128)(2,1)S(1)}, u32[]{:S(2)}, u32[]{:S(2)}) collective-permute-start(bf16[2,64,768]{2,1,0:T(8,128)(2,1)} %copy-done.12), channel_id=1, source_target_pairs={{0,8},{1,9},{4,12},{5,13},{8,14},{9,15},{12,10},{13,11},{14,6},{15... | collective-permute-start | bytes 589832 | tf_op jit(solution)/shard_map/ppermute | solution.py:44
  45.2 1.9 %copy-done.5 = bf16[768,2048]{1,0:T(8,128)(2,1)S(1)} copy-done((bf16[768,2048]{1,0:T(8,128)(2,1)S(1)}, bf16[768,2048]{1,0:T(8,128)(2,1)}, u32[]{:S(2)}) %copy-start.5) | copy-done | bytes 3145752
  47.1 1.0 %copy-done.7 = bf16[64,2176]{1,0:T(8,128)(2,1)S(1)} copy-done((bf16[64,2176]{1,0:T(8,128)(2,1)S(1)}, bf16[64,2176]{1,0:T(8,128)(2,1)}, u32[]{:S(2)}) %copy-start.7) | copy-done | bytes 278552
  48.1 1.0 %copy-done.9 = bf16[64,2176]{1,0:T(8,128)(2,1)S(1)} copy-done((bf16[64,2176]{1,0:T(8,128)(2,1)S(1)}, bf16[64,2176]{1,0:T(8,128)(2,1)}, u32[]{:S(2)}) %copy-start.9) | copy-done | bytes 278552
  49.0 2.2 %shard_map.50 = (bf16[2,64,768]{2,1,0:T(8,128)(2,1)S(1)}, bf16[2,64,768]{2,1,0:T(8,128)(2,1)S(1)}) custom-call(bf16[768,2048]{1,0:T(8,128)(2,1)S(1)} %bitcast.9, bf16[768,2048]{1,0:T(8,128)(2,1)S(1)} %copy-done.5, bf16[64,2176]{1,0:T(8,128)(2,1)S(1)} %copy-done.7, bf16[64,2176]{1,0:T(8,128)(2,1)S(1)} %copy-done.9), custom_call_target="tpu_custom_call" | custom-call | flops 805306368 | bytes 7208960 | tf_op jit(solution)/shard_map/pallas_call | solution.py:91
  51.2 0.0 collective-permute-done.10.refs_0_
  51.2 0.0 copy-done.11
  51.2 0.3 collective-permute-start.9
  51.5 0.0 collective-permute-done.11.refs_1_
  51.5 3.0 %shard_map.51 = bf16[2,64,768]{2,1,0:T(8,128)(2,1)S(1)} custom-call(bf16[768,2048]{1,0:T(8,128)(2,1)S(1)} %bitcast.10, bf16[768,2048]{1,0:T(8,128)(2,1)S(1)} %copy-done.5, bf16[32,2176]{1,0:T(8,128)(2,1)S(1)} %collective-permute-done.10.refs_0_, bf16[32,2176]{1,0:T(8,128)(2,1)} %collective-permute-done.11.refs_1_), custom_call_target="tpu_custom_call" | custom-call | flops 402653184 | bytes 6750208 | tf_op jit(solution)/shard_map/pallas_call | solution.py:91
  54.5 3.6 %collective-permute-start.13 = (bf16[2,64,768]{2,1,0:T(8,128)(2,1)S(1)}, bf16[2,64,768]{2,1,0:T(8,128)(2,1)S(1)}, u32[]{:S(2)}, u32[]{:S(2)}) collective-permute-start(bf16[2,64,768]{2,1,0:T(8,128)(2,1)S(1)} %shard_map.51), channel_id=1, source_target_pairs={{0,14},{1,15},{4,10},{5,11},{8,6},{9,7},{12,2},{13,3},{14,0},{15,1... | collective-permute-start | bytes 589832 | tf_op jit(solution)/shard_map/ppermute | solution.py:44
  58.2 0.0 collective-permute-done.16.refs_7_
  58.2 1.3 %collective-permute-start.12 = (bf16[2,64,768]{2,1,0:T(8,128)(2,1)S(1)}, bf16[2,64,768]{2,1,0:T(8,128)(2,1)S(1)}, u32[]{:S(2)}, u32[]{:S(2)}) collective-permute-start(bf16[2,64,768]{2,1,0:T(8,128)(2,1)S(1)} %get-tuple-element.41), channel_id=1, source_target_pairs={{0,10},{1,11},{4,6},{5,7},{8,2},{9,3},{12,0},{13,1},{14,4},{15,5},... | collective-permute-start | bytes 589832 | tf_op jit(solution)/shard_map/ppermute | solution.py:44
  59.4 0.0 collective-permute-done.6.refs_1_
  59.4 2.6 %collective-permute-start.14 = (bf16[2,64,768]{2,1,0:T(8,128)(2,1)S(1)}, bf16[2,64,768]{2,1,0:T(8,128)(2,1)S(1)}, u32[]{:S(2)}, u32[]{:S(2)}) collective-permute-start(bf16[2,64,768]{2,1,0:T(8,128)(2,1)S(1)} %get-tuple-element.44), channel_id=1, source_target_pairs={{0,12},{1,13},{4,14},{5,15},{8,10},{9,11},{12,6},{13,7},{14,2},{15... | collective-permute-start | bytes 589832 | tf_op jit(solution)/shard_map/ppermute | solution.py:44
  62.0 0.0 copy-done.13
  62.0 0.3 fusion.5.labels
  62.3 0.0 collective-permute-done.15.refs_6_
  62.3 0.0 collective-permute-done.9.refs_2_
  62.4 2.8 %collective-permute-done.13.refs_4_ = bf16[2,64,768]{2,1,0:T(8,128)(2,1)S(1)} collective-permute-done((bf16[2,64,768]{2,1,0:T(8,128)(2,1)S(1)}, bf16[2,64,768]{2,1,0:T(8,128)(2,1)S(1)}, u32[]{:S(2)}, u32[]{:S(2)}) %collective-permute-start.13) | collective-permute-done | bytes 196640 | tf_op jit(solution)/shard_map/ppermute | solution.py:44
  65.2 14.2 %collective-permute-done.12.refs_3_ = bf16[2,64,768]{2,1,0:T(8,128)(2,1)S(1)} collective-permute-done((bf16[2,64,768]{2,1,0:T(8,128)(2,1)S(1)}, bf16[2,64,768]{2,1,0:T(8,128)(2,1)S(1)}, u32[]{:S(2)}, u32[]{:S(2)}) %collective-permute-start.12) | collective-permute-done | bytes 196640 | tf_op jit(solution)/shard_map/ppermute | solution.py:44
  79.4 0.0 collective-permute-done.14.refs_5_
  79.4 2.3 %shard_map.52 = bf16[512,768]{1,0:T(8,128)(2,1)} custom-call(s32[512,1]{1,0:T(8,128)S(1)} %fusion.5.labels, bf16[2,64,768]{2,1,0:T(8,128)(2,1)S(1)} %shard_map.47.refs_0_, bf16[2,64,768]{2,1,0:T(8,128)(2,1)} %collective-permute-done.6.refs_1_, bf16[2,64,768]{2,1,0:T(8,128)(2,1)S(1)} %collective-permute-done.9.refs_2_, ...), custom_call_target="tpu_custom_call" | custom-call | tf_op jit(solution)/shard_map/pallas_call | solution.py:123
  (11 shorter events, 0.0 us)
Async XLA Ops:
  0.0 12.3 %collective-permute-start.3 = (bf16[768,2048]{1,0:T(8,128)(2,1)}, bf16[768,2048]{1,0:T(8,128)(2,1)S(1)}, u32[]{:S(2)}, u32[]{:S(2)}) collective-permute-start(bf16[768,2048]{1,0:T(8,128)(2,1)} %bitcast.5), channel_id=1, source_target_pairs={{0,1},{1,0},{4,5},{5,4},{8,9},{9,8},{12,13},{13,12},{14,15},{15,14... | collective-permute-start | bytes 9437192 | tf_op jit(solution)/shard_map/ppermute | solution.py:44
  0.0 9.0 %collective-permute-start = (bf16[1,64,2048]{2,1,0:T(8,128)(2,1)}, bf16[1,64,2048]{2,1,0:T(8,128)(2,1)}, u32[]{:S(2)}, u32[]{:S(2)}) collective-permute-start(bf16[1,64,2048]{2,1,0:T(8,128)(2,1)} %param.4), channel_id=1, source_target_pairs={{16,0},{0,16},{17,1},{1,17},{18,2},{2,18},{19,3},{3,19},{20,4},{4,... | collective-permute-start | bytes 786440 | tf_op jit(solution)/shard_map/ppermute | solution.py:18
  10.2 9.5 %collective-permute-start.1 = (bf16[64,2176]{1,0:T(8,128)(2,1)S(1)}, bf16[64,2176]{1,0:T(8,128)(2,1)S(1)}, u32[]{:S(2)}, u32[]{:S(2)}) collective-permute-start(bf16[64,2176]{1,0:T(8,128)(2,1)S(1)} %shard_map.46.refs_0_), channel_id=1, source_target_pairs={{0,4},{1,5},{4,8},{5,9},{8,12},{9,13},{12,14},{13,15},{14,10},{15,... | collective-permute-start | bytes 835592 | tf_op jit(solution)/shard_map/ppermute | solution.py:44
  10.6 9.2 %collective-permute-start.2 = (bf16[64,2176]{1,0:T(8,128)(2,1)S(1)}, bf16[64,2176]{1,0:T(8,128)(2,1)S(1)}, u32[]{:S(2)}, u32[]{:S(2)}) collective-permute-start(bf16[64,2176]{1,0:T(8,128)(2,1)S(1)} %shard_map.46.refs_0_), channel_id=1, source_target_pairs={{0,2},{1,3},{4,0},{5,1},{8,4},{9,5},{12,8},{13,9},{14,12},{15,13},... | collective-permute-start | bytes 835592 | tf_op jit(solution)/shard_map/ppermute | solution.py:44
  12.3 1.6 %copy-start.2 = (bf16[768,2048]{1,0:T(8,128)(2,1)}, bf16[768,2048]{1,0:T(8,128)(2,1)S(1)}, u32[]{:S(2)}) copy-start(bf16[768,2048]{1,0:T(8,128)(2,1)S(1)} %collective-permute-done.3.other) | copy-start | bytes 9437188
  13.9 1.9 %copy-start = (bf16[1,1,768,2048]{3,2,1,0:T(8,128)(2,1)S(1)}, bf16[1,1,768,2048]{3,2,1,0:T(8,128)(2,1)}, u32[]{:S(2)}) copy-start(bf16[1,1,768,2048]{3,2,1,0:T(8,128)(2,1)} %param.7) | copy-start | bytes 9437188
  15.8 1.9 %copy-start.3 = (bf16[768,2048]{1,0:T(8,128)(2,1)S(1)}, bf16[768,2048]{1,0:T(8,128)(2,1)}, u32[]{:S(2)}) copy-start(bf16[768,2048]{1,0:T(8,128)(2,1)} %copy-done.2) | copy-start | bytes 9437188
  17.7 4.1 %copy-start.1 = (bf16[1,1,768,2048]{3,2,1,0:T(8,128)(2,1)S(1)}, bf16[1,1,768,2048]{3,2,1,0:T(8,128)(2,1)}, u32[]{:S(2)}) copy-start(bf16[1,1,768,2048]{3,2,1,0:T(8,128)(2,1)} %param.7) | copy-start | bytes 9437188
  19.7 7.8 %collective-permute-start.4 = (bf16[64,2176]{1,0:T(8,128)(2,1)S(1)}, bf16[64,2176]{1,0:T(8,128)(2,1)S(1)}, u32[]{:S(2)}, u32[]{:S(2)}) collective-permute-start(bf16[64,2176]{1,0:T(8,128)(2,1)S(1)} %collective-permute-done.1.refs_0_), channel_id=1, source_target_pairs={{0,4},{1,5},{4,8},{5,9},{8,12},{9,13},{12,14},{13,15},{14,10},{15,... | collective-permute-start | bytes 835592 | tf_op jit(solution)/shard_map/ppermute | solution.py:44
  20.4 7.4 %collective-permute-start.5 = (bf16[64,2176]{1,0:T(8,128)(2,1)S(1)}, bf16[64,2176]{1,0:T(8,128)(2,1)S(1)}, u32[]{:S(2)}, u32[]{:S(2)}) collective-permute-start(bf16[64,2176]{1,0:T(8,128)(2,1)S(1)} %collective-permute-done.2.refs_1_), channel_id=1, source_target_pairs={{0,2},{1,3},{4,0},{5,1},{8,4},{9,5},{12,8},{13,9},{14,12},{15,13},... | collective-permute-start | bytes 835592 | tf_op jit(solution)/shard_map/ppermute | solution.py:44
  21.8 1.9 %copy-start.4 = (bf16[768,2048]{1,0:T(8,128)(2,1)S(1)}, bf16[768,2048]{1,0:T(8,128)(2,1)}, u32[]{:S(2)}) copy-start(bf16[768,2048]{1,0:T(8,128)(2,1)} %copy-done.2) | copy-start | bytes 9437188
  27.7 8.7 %collective-permute-start.7 = (bf16[64,2176]{1,0:T(8,128)(2,1)S(1)}, bf16[64,2176]{1,0:T(8,128)(2,1)S(1)}, u32[]{:S(2)}, u32[]{:S(2)}) collective-permute-start(bf16[64,2176]{1,0:T(8,128)(2,1)S(1)} %collective-permute-done.4.refs_0_), channel_id=1, source_target_pairs={{0,4},{1,5},{4,8},{5,9},{8,12},{9,13},{12,14},{13,15},{14,10},{15,... | collective-permute-start | bytes 835592 | tf_op jit(solution)/shard_map/ppermute | solution.py:44
  29.3 8.3 %collective-permute-start.8 = (bf16[64,2176]{1,0:T(8,128)(2,1)S(1)}, bf16[64,2176]{1,0:T(8,128)(2,1)S(1)}, u32[]{:S(2)}, u32[]{:S(2)}) collective-permute-start(bf16[64,2176]{1,0:T(8,128)(2,1)S(1)} %collective-permute-done.5.refs_1_), channel_id=1, source_target_pairs={{0,2},{1,3},{4,0},{5,1},{8,4},{9,5},{12,8},{13,9},{14,12},{15,13},... | collective-permute-start | bytes 835592 | tf_op jit(solution)/shard_map/ppermute | solution.py:44
  29.8 28.4 %collective-permute-start.16 = (bf16[2,64,768]{2,1,0:T(8,128)(2,1)}, bf16[2,64,768]{2,1,0:T(8,128)(2,1)}, u32[]{:S(2)}, u32[]{:S(2)}) collective-permute-start(bf16[2,64,768]{2,1,0:T(8,128)(2,1)} %get-tuple-element.46), channel_id=1, source_target_pairs={{0,4},{1,5},{4,8},{5,9},{8,12},{9,13},{12,14},{13,15},{14,10},{15,... | collective-permute-start | bytes 589832 | tf_op jit(solution)/shard_map/ppermute | solution.py:44
  31.4 28.1 %collective-permute-start.6 = (bf16[2,64,768]{2,1,0:T(8,128)(2,1)}, bf16[2,64,768]{2,1,0:T(8,128)(2,1)}, u32[]{:S(2)}, u32[]{:S(2)}) collective-permute-start(bf16[2,64,768]{2,1,0:T(8,128)(2,1)} %get-tuple-element.31), channel_id=1, source_target_pairs={{0,2},{1,3},{4,0},{5,1},{8,4},{9,5},{12,8},{13,9},{14,12},{15,13},... | collective-permute-start | bytes 589832 | tf_op jit(solution)/shard_map/ppermute | solution.py:44
  34.0 0.7 copy-start.10
  34.6 0.7 copy-start.12
  37.6 3.0 %copy-start.8 = (bf16[64,2176]{1,0:T(8,128)(2,1)}, bf16[64,2176]{1,0:T(8,128)(2,1)S(1)}, u32[]{:S(2)}) copy-start(bf16[64,2176]{1,0:T(8,128)(2,1)S(1)} %collective-permute-done.8.refs_1_) | copy-start | bytes 835588
  38.3 0.7 copy-start.6
  39.0 12.2 %collective-permute-start.10 = (bf16[32,2176]{1,0:T(8,128)(2,1)}, bf16[32,2176]{1,0:T(8,128)(2,1)S(1)}, u32[]{:S(2)}, u32[]{:S(2)}) collective-permute-start(bf16[32,2176]{1,0:T(8,128)(2,1)} %slice.6), channel_id=1, source_target_pairs={{0,4},{1,5},{4,8},{5,9},{8,12},{9,13},{12,14},{13,15},{14,10},{15,... | collective-permute-start | bytes 417800 | tf_op jit(solution)/shard_map/ppermute | solution.py:44
  41.3 10.3 %collective-permute-start.11 = (bf16[32,2176]{1,0:T(8,128)(2,1)}, bf16[32,2176]{1,0:T(8,128)(2,1)}, u32[]{:S(2)}, u32[]{:S(2)}) collective-permute-start(bf16[32,2176]{1,0:T(8,128)(2,1)} %slice.7), channel_id=1, source_target_pairs={{0,2},{1,3},{4,0},{5,1},{8,4},{9,5},{12,8},{13,9},{14,12},{15,13},... | collective-permute-start | bytes 417800 | tf_op jit(solution)/shard_map/ppermute | solution.py:44
  42.6 19.8 %collective-permute-start.15 = (bf16[2,64,768]{2,1,0:T(8,128)(2,1)}, bf16[2,64,768]{2,1,0:T(8,128)(2,1)S(1)}, u32[]{:S(2)}, u32[]{:S(2)}) collective-permute-start(bf16[2,64,768]{2,1,0:T(8,128)(2,1)} %copy-done.12), channel_id=1, source_target_pairs={{0,8},{1,9},{4,12},{5,13},{8,14},{9,15},{12,10},{13,11},{14,6},{15... | collective-permute-start | bytes 589832 | tf_op jit(solution)/shard_map/ppermute | solution.py:44
  45.2 1.9 %copy-start.5 = (bf16[768,2048]{1,0:T(8,128)(2,1)S(1)}, bf16[768,2048]{1,0:T(8,128)(2,1)}, u32[]{:S(2)}) copy-start(bf16[768,2048]{1,0:T(8,128)(2,1)} %copy-done.2) | copy-start | bytes 9437188
  47.1 1.0 %copy-start.7 = (bf16[64,2176]{1,0:T(8,128)(2,1)S(1)}, bf16[64,2176]{1,0:T(8,128)(2,1)}, u32[]{:S(2)}) copy-start(bf16[64,2176]{1,0:T(8,128)(2,1)} %copy-done.6) | copy-start | bytes 835588
  48.1 1.0 %copy-start.9 = (bf16[64,2176]{1,0:T(8,128)(2,1)S(1)}, bf16[64,2176]{1,0:T(8,128)(2,1)}, u32[]{:S(2)}) copy-start(bf16[64,2176]{1,0:T(8,128)(2,1)} %copy-done.8) | copy-start | bytes 835588
  49.0 2.2 %copy-start.11 = (bf16[2,64,768]{2,1,0:T(8,128)(2,1)S(1)}, bf16[2,64,768]{2,1,0:T(8,128)(2,1)}, u32[]{:S(2)}) copy-start(bf16[2,64,768]{2,1,0:T(8,128)(2,1)} %copy-done.10) | copy-start | bytes 589828
  51.2 11.1 %collective-permute-start.9 = (bf16[2,64,768]{2,1,0:T(8,128)(2,1)S(1)}, bf16[2,64,768]{2,1,0:T(8,128)(2,1)S(1)}, u32[]{:S(2)}, u32[]{:S(2)}) collective-permute-start(bf16[2,64,768]{2,1,0:T(8,128)(2,1)S(1)} %copy-done.11), channel_id=1, source_target_pairs={{0,6},{1,7},{4,2},{5,3},{8,0},{9,1},{12,4},{13,5},{14,8},{15,9},{1... | collective-permute-start | bytes 589832 | tf_op jit(solution)/shard_map/ppermute | solution.py:44
  51.5 10.4 %copy-start.13 = (s32[512,1]{1,0:T(8,128)S(1)}, s32[512,1]{1,0:T(8,128)}, u32[]{:S(2)}) copy-start(s32[512,1]{1,0:T(8,128)} %squeeze.19) | copy-start | bytes 6148
  54.5 10.6 %collective-permute-start.13 = (bf16[2,64,768]{2,1,0:T(8,128)(2,1)S(1)}, bf16[2,64,768]{2,1,0:T(8,128)(2,1)S(1)}, u32[]{:S(2)}, u32[]{:S(2)}) collective-permute-start(bf16[2,64,768]{2,1,0:T(8,128)(2,1)S(1)} %shard_map.51), channel_id=1, source_target_pairs={{0,14},{1,15},{4,10},{5,11},{8,6},{9,7},{12,2},{13,3},{14,0},{15,1... | collective-permute-start | bytes 589832 | tf_op jit(solution)/shard_map/ppermute | solution.py:44
  58.2 21.2 %collective-permute-start.12 = (bf16[2,64,768]{2,1,0:T(8,128)(2,1)S(1)}, bf16[2,64,768]{2,1,0:T(8,128)(2,1)S(1)}, u32[]{:S(2)}, u32[]{:S(2)}) collective-permute-start(bf16[2,64,768]{2,1,0:T(8,128)(2,1)S(1)} %get-tuple-element.41), channel_id=1, source_target_pairs={{0,10},{1,11},{4,6},{5,7},{8,2},{9,3},{12,0},{13,1},{14,4},{15,5},... | collective-permute-start | bytes 589832 | tf_op jit(solution)/shard_map/ppermute | solution.py:44
  59.4 19.9 %collective-permute-start.14 = (bf16[2,64,768]{2,1,0:T(8,128)(2,1)S(1)}, bf16[2,64,768]{2,1,0:T(8,128)(2,1)S(1)}, u32[]{:S(2)}, u32[]{:S(2)}) collective-permute-start(bf16[2,64,768]{2,1,0:T(8,128)(2,1)S(1)} %get-tuple-element.44), channel_id=1, source_target_pairs={{0,12},{1,13},{4,14},{5,15},{8,10},{9,11},{12,6},{13,7},{14,2},{15... | collective-permute-start | bytes 589832 | tf_op jit(solution)/shard_map/ppermute | solution.py:44

commit v7 on v6

--- a/solution.py
+++ b/solution.py
@@ -44,23 +44,37 @@
     return lax.ppermute(block, "expert", ring_route(owners, distance, flip))
 
 
-def widen_kernel(ids, gates, rows, out):
+def gates_kernel(ids, gates, out):
+    top, tokens = ids.shape
+    expert = lax.broadcasted_iota(jnp.int32, (LANES, tokens), 0)
+    total = jnp.zeros((LANES, tokens), jnp.float32)
+    for k in range(top):
+        gate = gates[k : k + 1, :].astype(jnp.float32)
+        total += jnp.where(expert == ids[k : k + 1, :], gate, 0.0)
+    out[...] = total.T.astype(jnp.bfloat16)
+
+
+def gate_columns(ids, gates):
+    return pl.pallas_call(
+        gates_kernel,
+        out_shape=jax.ShapeDtypeStruct((ids.shape[1], LANES), jnp.bfloat16),
+        compiler_params=pltpu.CompilerParams(vmem_limit_bytes=16 << 20),
+    )(ids, gates)
+
+
+def widen_kernel(rows, columns, out):
     depth = rows.shape[1]
     out[:, :depth] = rows[...]
-    expert = lax.broadcasted_iota(jnp.int32, (rows.shape[0], LANES), 1)
-    total = jnp.zeros(expert.shape, jnp.float32)
-    for k in range(ids.shape[1]):
-        gate = gates[:, k : k + 1].astype(jnp.float32)
-        total += jnp.where(expert == ids[:, k : k + 1], gate, 0.0)
-    out[:, depth:] = total.astype(jnp.bfloat16)
-
-
-def widened(ids, gates, rows):
+    out[:, depth:] = columns[...]
+
+
+def widened(rows, columns):
+    width = rows.shape[1] + columns.shape[1]
     return pl.pallas_call(
         widen_kernel,
-        out_shape=jax.ShapeDtypeStruct((rows.shape[0], rows.shape[1] + LANES), jnp.bfloat16),
-        compiler_params=pltpu.CompilerParams(vmem_limit_bytes=16 << 20),
-    )(ids, gates, rows)
+        out_shape=jax.ShapeDtypeStruct((rows.shape[0], width), jnp.bfloat16),
+        compiler_params=pltpu.CompilerParams(vmem_limit_bytes=16 << 20),
+    )(rows, columns)
 
 
 def products_kernel(count, weight, other, *refs):
@@ -100,45 +114,47 @@
     )(weight, other, *pieces)
 
 
-def pick_kernel(labels, *refs):
+def pick_kernel(ids, *refs):
     blocks, out = refs[:-1], refs[-1]
     experts, tokens, _ = blocks[0].shape
-    top = out.shape[0] // tokens
+    size = len(blocks)
+    top = ids.shape[0]
     span = 16
-    routes = span * top
-    owners = len(blocks) * experts
-    column = lax.broadcasted_iota(jnp.int32, (routes, owners * span), 1)
-    token = lax.broadcasted_iota(jnp.int32, (routes, owners * span), 0) // top
+    place = ring_place(lax.div(lax.axis_index("expert"), CORES), size)
+    chip = lax.div(ids[...], CORES)
+    label = lax.rem(ring_place(chip, size) - place + size, size) * CORES + lax.rem(ids[...], CORES)
+    column = lax.broadcasted_iota(jnp.int32, (top, size * experts * span), 1)
     for g in range(tokens // span):
         stacked = jnp.concatenate(
             [b[c, g * span : (g + 1) * span, :] for b in blocks for c in range(experts)], axis=0
         )
-        wanted = labels[g * routes : (g + 1) * routes, :] * span + token
-        pick = jnp.where(column == wanted, 1.0, 0.0).astype(jnp.bfloat16)
+        picks = [
+            jnp.where(column == label[:, g * span + t : g * span + t + 1] * span + t, 1.0, 0.0)
+            for t in range(span)
+        ]
+        pick = jnp.concatenate(picks, axis=0).astype(jnp.bfloat16)
         rows = jnp.dot(pick, stacked, preferred_element_type=jnp.float32)
-        out[g * routes : (g + 1) * routes, :] = rows.astype(jnp.bfloat16)
-
-
-def pick_routes(labels, blocks):
+        out[g * span * top : (g + 1) * span * top, :] = rows.astype(jnp.bfloat16)
+
+
+def pick_routes(ids, blocks):
+    top, tokens = ids.shape
     return pl.pallas_call(
         pick_kernel,
-        out_shape=jax.ShapeDtypeStruct((labels.shape[0], blocks[0].shape[2]), jnp.bfloat16),
-        compiler_params=pltpu.CompilerParams(vmem_limit_bytes=16 << 20),
-    )(labels, *blocks)
+        out_shape=jax.ShapeDtypeStruct((top * tokens, blocks[0].shape[2]), jnp.bfloat16),
+        compiler_params=pltpu.CompilerParams(vmem_limit_bytes=16 << 20),
+    )(ids, *blocks)
 
 
 def dense_device(section_grad, route_ids, route_gates, weight_mat):
     tokens, top = route_ids.shape
     owners = lax.axis_size("expert")
-    hidden = weight_mat.shape[0]
     size = owners // CORES
-    place = ring_place(lax.axis_index("expert") // CORES, size)
-    labels = lax.rem(ring_place(route_ids // CORES, size) - place + size, size) * CORES + lax.rem(
-        route_ids, CORES
-    )
-
     other_mat = send(weight_mat, owners, 0, 1)
-    rows = widened(route_ids, route_gates, section_grad)
+    section_grad, columns = lax.optimization_barrier(
+        (section_grad, gate_columns(route_ids.T, route_gates.T))
+    )
+    rows = widened(section_grad, columns)
 
     half, far = tokens // 2, size // 2
     back = ahead = rows
@@ -153,14 +169,14 @@
                 send(ahead[half:], owners, -1, 0),
             )
         results = products(list(waiting.values()), tokens, weight_mat, other_mat)
-        back, ahead, results = lax.optimization_barrier((next_back, next_ahead, results))
         for distance, result in zip(waiting, results):
             received[(-distance) % size] = send(result, owners, distance, 0) if distance else result
+        back, ahead, _ = lax.optimization_barrier((next_back, next_ahead, results))
         waiting = {size - step: back, step: ahead}
     (result,) = products([back, ahead], tokens, weight_mat, other_mat)
     received[far] = send(result, owners, far, 0)
-    out = pick_routes(labels.reshape(tokens * top, 1), received)
-    return out.reshape(1, tokens, top, hidden)
+    out = pick_routes(route_ids.T, received)
+    return out.reshape(1, tokens, top, weight_mat.shape[0])
 
 
 def slotted_device(section_grad, route_ids, route_gates, weight_mat, capacity):

time: 82.1 us -> 72.3 us (0.88)
  the two profiles are of different devices: /device:TPU:2 before, /device:TPU:10 now
where the time goes in v7:
time: 72.3 us; the launch traced here: 72.1 us
  waiting for transfers between devices  35.4 us (49%)
  starting transfers between devices  21.3 us (29%)
  Pallas kernels  12 us (17%)
  local copies, waits for them, and re-layouts  3.28 us (5%)
    ppermute x16, waiting for transfers between devices, send(): return lax.ppermute(block, 'expert', ring_route(owners, distance, flip))  29.5 us
    ppermute x16, starting transfers between devices, send(): return lax.ppermute(block, 'expert', ring_route(owners, distance, flip))  19.8 us
    pallas_call x5, Pallas kernels, products(): pl.pallas_call(functools.partial(products_kernel, len(pieces)), out_shape...  10.6 us
    ppermute x1, waiting for transfers between devices, shifted(): return lax.ppermute(block, axis, route)  5.93 us
    unnamed x8, local copies, waits for them, and re-layouts  3.26 us
    ppermute x1, starting transfers between devices, shifted(): return lax.ppermute(block, axis, route)  1.52 us
  transfers between devices with their start and end apart: 17, of which 12 were waited for; matrix products, arithmetic and copies ran while one was open for 0% of the time, Pallas kernels for 15%

profile of v7, /device:TPU:10, one launch (start us, length us, event | category | flops | bytes accessed | tf_op | source)
XLA Modules:
  0.0 72.1 jit_solution(12396734222252738717)
XLA Ops:
  0.0 0.0 collective-permute-start
  0.0 1.5 %collective-permute-start.1 = (bf16[1,64,2048]{2,1,0:T(8,128)(2,1)}, bf16[1,64,2048]{2,1,0:T(8,128)(2,1)S(1)}, u32[]{:S(2)}, u32[]{:S(2)}) collective-permute-start(bf16[1,64,2048]{2,1,0:T(8,128)(2,1)} %param.4), channel_id=1, source_target_pairs={{16,0},{0,16},{17,1},{1,17},{18,2},{2,18},{19,3},{3,19},{20,4},{4,... | collective-permute-start | bytes 786440 | tf_op jit(solution)/shard_map/ppermute | solution.py:18
  1.5 0.0 copy-start.2
  1.5 0.7 copy-done.2
  2.2 0.0 copy-start.3
  2.2 0.7 copy-done.3
  2.9 0.1 shard_map.46.columns
  3.0 5.9 %collective-permute-done.1 = bf16[1,64,2048]{2,1,0:T(8,128)(2,1)S(1)} collective-permute-done((bf16[1,64,2048]{2,1,0:T(8,128)(2,1)}, bf16[1,64,2048]{2,1,0:T(8,128)(2,1)S(1)}, u32[]{:S(2)}, u32[]{:S(2)}) %collective-permute-start.1) | collective-permute-done | bytes 262176 | tf_op jit(solution)/shard_map/ppermute | solution.py:18
  9.0 0.5 collective-permute-start.2
  9.5 1.6 %collective-permute-start.3 = (bf16[64,2176]{1,0:T(8,128)(2,1)S(1)}, bf16[64,2176]{1,0:T(8,128)(2,1)S(1)}, u32[]{:S(2)}, u32[]{:S(2)}) collective-permute-start(bf16[64,2176]{1,0:T(8,128)(2,1)S(1)} %shard_map.47.refs_0_), channel_id=1, source_target_pairs={{0,2},{1,3},{4,0},{5,1},{8,4},{9,5},{12,8},{13,9},{14,12},{15,13},... | collective-permute-start | bytes 835592 | tf_op jit(solution)/shard_map/ppermute | solution.py:44
  11.0 0.0 collective-permute-done.other
  11.0 0.0 copy-start
  11.0 1.9 %copy-done = bf16[1,1,768,2048]{3,2,1,0:T(8,128)(2,1)S(1)} copy-done((bf16[1,1,768,2048]{3,2,1,0:T(8,128)(2,1)S(1)}, bf16[1,1,768,2048]{3,2,1,0:T(8,128)(2,1)}, u32[]{:S(2)}) %copy-start) | copy-done | bytes 3145752
  12.9 0.0 copy-start.1
  12.9 2.0 %shard_map.48.refs_0_ = bf16[2,64,768]{2,1,0:T(8,128)(2,1)S(1)} custom-call(bf16[768,2048]{1,0:T(8,128)(2,1)S(1)} %bitcast.10, bf16[768,2048]{1,0:T(8,128)(2,1)S(1)} %collective-permute-done.other, bf16[64,2176]{1,0:T(8,128)(2,1)S(1)} %shard_map.47.refs_0_), custom_call_target="tpu_custom_call" | custom-call | flops 402653184 | bytes 6750208 | tf_op jit(solution)/shard_map/pallas_call | solution.py:105
  14.9 2.4 %collective-permute-done.2.refs_0_ = bf16[64,2176]{1,0:T(8,128)(2,1)S(1)} collective-permute-done((bf16[64,2176]{1,0:T(8,128)(2,1)S(1)}, bf16[64,2176]{1,0:T(8,128)(2,1)S(1)}, u32[]{:S(2)}, u32[]{:S(2)}) %collective-permute-start.2) | collective-permute-done | bytes 278560 | tf_op jit(solution)/shard_map/ppermute | solution.py:44
  17.3 0.2 collective-permute-done.3.refs_1_
  17.5 0.5 collective-permute-start.5
  18.0 1.5 %collective-permute-start.6 = (bf16[64,2176]{1,0:T(8,128)(2,1)S(1)}, bf16[64,2176]{1,0:T(8,128)(2,1)S(1)}, u32[]{:S(2)}, u32[]{:S(2)}) collective-permute-start(bf16[64,2176]{1,0:T(8,128)(2,1)S(1)} %collective-permute-done.3.refs_1_), channel_id=1, source_target_pairs={{0,2},{1,3},{4,0},{5,1},{8,4},{9,5},{12,8},{13,9},{14,12},{15,13},... | collective-permute-start | bytes 835592 | tf_op jit(solution)/shard_map/ppermute | solution.py:44
  19.5 0.0 copy-done.1
  19.5 2.2 %shard_map.49 = (bf16[2,64,768]{2,1,0:T(8,128)(2,1)S(1)}, bf16[2,64,768]{2,1,0:T(8,128)(2,1)S(1)}) custom-call(bf16[768,2048]{1,0:T(8,128)(2,1)S(1)} %bitcast.11, bf16[768,2048]{1,0:T(8,128)(2,1)S(1)} %collective-permute-done.other, bf16[64,2176]{1,0:T(8,128)(2,1)S(1)} %collective-permute-done.2.refs_0_, bf16[64,2176]{1,0:T(8,128)(2,1)S(1)} %collective-permute-done.3.refs_1_), custom_call_target="tpu_custom_call" | custom-call | flops 805306368 | bytes 7208960 | tf_op jit(solution)/shard_map/pallas_call | solution.py:105
  21.7 3.0 %collective-permute-done.5.refs_0_ = bf16[64,2176]{1,0:T(8,128)(2,1)S(1)} collective-permute-done((bf16[64,2176]{1,0:T(8,128)(2,1)S(1)}, bf16[64,2176]{1,0:T(8,128)(2,1)S(1)}, u32[]{:S(2)}, u32[]{:S(2)}) %collective-permute-start.5) | collective-permute-done | bytes 278560 | tf_op jit(solution)/shard_map/ppermute | solution.py:44
  24.7 0.3 collective-permute-done.6.refs_1_
  25.0 1.4 %collective-permute-start.8 = (bf16[64,2176]{1,0:T(8,128)(2,1)S(1)}, bf16[64,2176]{1,0:T(8,128)(2,1)S(1)}, u32[]{:S(2)}, u32[]{:S(2)}) collective-permute-start(bf16[64,2176]{1,0:T(8,128)(2,1)S(1)} %collective-permute-done.5.refs_0_), channel_id=1, source_target_pairs={{0,4},{1,5},{4,8},{5,9},{8,12},{9,13},{12,14},{13,15},{14,10},{15,... | collective-permute-start | bytes 835592 | tf_op jit(solution)/shard_map/ppermute | solution.py:44
  26.4 0.7 collective-permute-start.9
  27.0 1.4 %collective-permute-start.16 = (bf16[2,64,768]{2,1,0:T(8,128)(2,1)S(1)}, bf16[2,64,768]{2,1,0:T(8,128)(2,1)S(1)}, u32[]{:S(2)}, u32[]{:S(2)}) collective-permute-start(bf16[2,64,768]{2,1,0:T(8,128)(2,1)S(1)} %get-tuple-element.26), channel_id=1, source_target_pairs={{0,4},{1,5},{4,8},{5,9},{8,12},{9,13},{12,14},{13,15},{14,10},{15,... | collective-permute-start | bytes 589832 | tf_op jit(solution)/shard_map/ppermute | solution.py:44
  28.4 0.7 collective-permute-start.4
  29.1 2.2 %shard_map.50 = (bf16[2,64,768]{2,1,0:T(8,128)(2,1)S(1)}, bf16[2,64,768]{2,1,0:T(8,128)(2,1)S(1)}) custom-call(bf16[768,2048]{1,0:T(8,128)(2,1)S(1)} %bitcast.12, bf16[768,2048]{1,0:T(8,128)(2,1)S(1)} %collective-permute-done.other, bf16[64,2176]{1,0:T(8,128)(2,1)S(1)} %collective-permute-done.5.refs_0_, bf16[64,2176]{1,0:T(8,128)(2,1)S(1)} %collective-permute-done.6.refs_1_), custom_call_target="tpu_custom_call" | custom-call | flops 805306368 | bytes 7208960 | tf_op jit(solution)/shard_map/pallas_call | solution.py:105
  31.3 3.3 %collective-permute-done.8.refs_0_ = bf16[64,2176]{1,0:T(8,128)(2,1)S(1)} collective-permute-done((bf16[64,2176]{1,0:T(8,128)(2,1)S(1)}, bf16[64,2176]{1,0:T(8,128)(2,1)S(1)}, u32[]{:S(2)}, u32[]{:S(2)}) %collective-permute-start.8) | collective-permute-done | bytes 278560 | tf_op jit(solution)/shard_map/ppermute | solution.py:44
  34.6 0.4 collective-permute-done.9.refs_1_
  35.0 1.6 %collective-permute-start.11 = (bf16[32,2176]{1,0:T(8,128)(2,1)S(1)}, bf16[32,2176]{1,0:T(8,128)(2,1)S(1)}, u32[]{:S(2)}, u32[]{:S(2)}) collective-permute-start(bf16[32,2176]{1,0:T(8,128)(2,1)S(1)} %slice.6), channel_id=1, source_target_pairs={{0,4},{1,5},{4,8},{5,9},{8,12},{9,13},{12,14},{13,15},{14,10},{15,... | collective-permute-start | bytes 417800 | tf_op jit(solution)/shard_map/ppermute | solution.py:44
  36.6 0.5 collective-permute-start.12
  37.1 2.7 %collective-permute-start.15 = (bf16[2,64,768]{2,1,0:T(8,128)(2,1)S(1)}, bf16[2,64,768]{2,1,0:T(8,128)(2,1)S(1)}, u32[]{:S(2)}, u32[]{:S(2)}) collective-permute-start(bf16[2,64,768]{2,1,0:T(8,128)(2,1)S(1)} %get-tuple-element.30), channel_id=1, source_target_pairs={{0,8},{1,9},{4,12},{5,13},{8,14},{9,15},{12,10},{13,11},{14,6},{15... | collective-permute-start | bytes 589832 | tf_op jit(solution)/shard_map/ppermute | solution.py:44
  39.9 2.2 %shard_map.51 = (bf16[2,64,768]{2,1,0:T(8,128)(2,1)S(1)}, bf16[2,64,768]{2,1,0:T(8,128)(2,1)S(1)}) custom-call(bf16[768,2048]{1,0:T(8,128)(2,1)S(1)} %bitcast.13, bf16[768,2048]{1,0:T(8,128)(2,1)S(1)} %collective-permute-done.other, bf16[64,2176]{1,0:T(8,128)(2,1)S(1)} %collective-permute-done.8.refs_0_, bf16[64,2176]{1,0:T(8,128)(2,1)S(1)} %collective-permute-done.9.refs_1_), custom_call_target="tpu_custom_call" | custom-call | flops 805306368 | bytes 7208960 | tf_op jit(solution)/shard_map/pallas_call | solution.py:105
  42.1 0.5 collective-permute-done.11.refs_0_
  42.5 0.9 %collective-permute-start.7 = (bf16[2,64,768]{2,1,0:T(8,128)(2,1)S(1)}, bf16[2,64,768]{2,1,0:T(8,128)(2,1)S(1)}, u32[]{:S(2)}, u32[]{:S(2)}) collective-permute-start(bf16[2,64,768]{2,1,0:T(8,128)(2,1)S(1)} %get-tuple-element.29), channel_id=1, source_target_pairs={{0,6},{1,7},{4,2},{5,3},{8,0},{9,1},{12,4},{13,5},{14,8},{15,9},{1... | collective-permute-start | bytes 589832 | tf_op jit(solution)/shard_map/ppermute | solution.py:44
  43.4 0.2 collective-permute-done.12.refs_1_
  43.7 3.6 %collective-permute-start.10 = (bf16[2,64,768]{2,1,0:T(8,128)(2,1)S(1)}, bf16[2,64,768]{2,1,0:T(8,128)(2,1)S(1)}, u32[]{:S(2)}, u32[]{:S(2)}) collective-permute-start(bf16[2,64,768]{2,1,0:T(8,128)(2,1)S(1)} %get-tuple-element.33), channel_id=1, source_target_pairs={{0,10},{1,11},{4,6},{5,7},{8,2},{9,3},{12,0},{13,1},{14,4},{15,5},... | collective-permute-start | bytes 589832 | tf_op jit(solution)/shard_map/ppermute | solution.py:44
  47.3 2.0 %shard_map.52 = bf16[2,64,768]{2,1,0:T(8,128)(2,1)S(1)} custom-call(bf16[768,2048]{1,0:T(8,128)(2,1)S(1)} %bitcast.14, bf16[768,2048]{1,0:T(8,128)(2,1)S(1)} %collective-permute-done.other, bf16[32,2176]{1,0:T(8,128)(2,1)S(1)} %collective-permute-done.11.refs_0_, bf16[32,2176]{1,0:T(8,128)(2,1)S(1)} %collective-permute-done.12.refs_1_), custom_call_target="tpu_custom_call" | custom-call | flops 402653184 | bytes 6750208 | tf_op jit(solution)/shard_map/pallas_call | solution.py:105
  49.3 0.0 collective-permute-done.16.refs_7_
  49.3 1.8 %collective-permute-start.14 = (bf16[2,64,768]{2,1,0:T(8,128)(2,1)S(1)}, bf16[2,64,768]{2,1,0:T(8,128)(2,1)S(1)}, u32[]{:S(2)}, u32[]{:S(2)}) collective-permute-start(bf16[2,64,768]{2,1,0:T(8,128)(2,1)S(1)} %get-tuple-element.34), channel_id=1, source_target_pairs={{0,12},{1,13},{4,14},{5,15},{8,10},{9,11},{12,6},{13,7},{14,2},{15... | collective-permute-start | bytes 589832 | tf_op jit(solution)/shard_map/ppermute | solution.py:44
  51.1 0.0 collective-permute-done.4.refs_1_
  51.1 0.5 collective-permute-start.13
  51.6 0.0 collective-permute-done.15.refs_6_
  51.6 10.9 %collective-permute-done.7.refs_2_ = bf16[2,64,768]{2,1,0:T(8,128)(2,1)S(1)} collective-permute-done((bf16[2,64,768]{2,1,0:T(8,128)(2,1)S(1)}, bf16[2,64,768]{2,1,0:T(8,128)(2,1)S(1)}, u32[]{:S(2)}, u32[]{:S(2)}) %collective-permute-start.7) | collective-permute-done | bytes 196640 | tf_op jit(solution)/shard_map/ppermute | solution.py:44
  62.4 4.0 %collective-permute-done.10.refs_3_ = bf16[2,64,768]{2,1,0:T(8,128)(2,1)S(1)} collective-permute-done((bf16[2,64,768]{2,1,0:T(8,128)(2,1)S(1)}, bf16[2,64,768]{2,1,0:T(8,128)(2,1)S(1)}, u32[]{:S(2)}, u32[]{:S(2)}) %collective-permute-start.10) | collective-permute-done | bytes 196640 | tf_op jit(solution)/shard_map/ppermute | solution.py:44
  66.5 0.0 collective-permute-done.14.refs_5_
  66.5 4.3 %collective-permute-done.13.refs_4_ = bf16[2,64,768]{2,1,0:T(8,128)(2,1)S(1)} collective-permute-done((bf16[2,64,768]{2,1,0:T(8,128)(2,1)S(1)}, bf16[2,64,768]{2,1,0:T(8,128)(2,1)S(1)}, u32[]{:S(2)}, u32[]{:S(2)}) %collective-permute-start.13) | collective-permute-done | bytes 196640 | tf_op jit(solution)/shard_map/ppermute | solution.py:44
  70.8 1.3 %shard_map.53 = bf16[512,768]{1,0:T(8,128)(2,1)} custom-call(s32[8,64]{1,0:T(8,128)S(1)} %bitcast.17, bf16[2,64,768]{2,1,0:T(8,128)(2,1)S(1)} %shard_map.48.refs_0_, bf16[2,64,768]{2,1,0:T(8,128)(2,1)S(1)} %collective-permute-done.4.refs_1_, bf16[2,64,768]{2,1,0:T(8,128)(2,1)S(1)} %collective-permute-done.7.refs_2_, ...), custom_call_target="tpu_custom_call" | custom-call | tf_op jit(solution)/shard_map/pallas_call | solution.py:142
  (3 shorter events, 0.0 us)
Async XLA Ops:
  0.0 11.0 %collective-permute-start = (bf16[768,2048]{1,0:T(8,128)(2,1)}, bf16[768,2048]{1,0:T(8,128)(2,1)S(1)}, u32[]{:S(2)}, u32[]{:S(2)}) collective-permute-start(bf16[768,2048]{1,0:T(8,128)(2,1)} %bitcast.9), channel_id=1, source_target_pairs={{0,1},{1,0},{4,5},{5,4},{8,9},{9,8},{12,13},{13,12},{14,15},{15,14... | collective-permute-start | bytes 9437192 | tf_op jit(solution)/shard_map/ppermute | solution.py:44
  0.0 8.9 %collective-permute-start.1 = (bf16[1,64,2048]{2,1,0:T(8,128)(2,1)}, bf16[1,64,2048]{2,1,0:T(8,128)(2,1)S(1)}, u32[]{:S(2)}, u32[]{:S(2)}) collective-permute-start(bf16[1,64,2048]{2,1,0:T(8,128)(2,1)} %param.4), channel_id=1, source_target_pairs={{16,0},{0,16},{17,1},{1,17},{18,2},{2,18},{19,3},{3,19},{20,4},{4,... | collective-permute-start | bytes 786440 | tf_op jit(solution)/shard_map/ppermute | solution.py:18
  1.5 0.7 copy-start.2
  2.2 0.7 copy-start.3
  9.0 8.3 %collective-permute-start.2 = (bf16[64,2176]{1,0:T(8,128)(2,1)S(1)}, bf16[64,2176]{1,0:T(8,128)(2,1)S(1)}, u32[]{:S(2)}, u32[]{:S(2)}) collective-permute-start(bf16[64,2176]{1,0:T(8,128)(2,1)S(1)} %shard_map.47.refs_0_), channel_id=1, source_target_pairs={{0,4},{1,5},{4,8},{5,9},{8,12},{9,13},{12,14},{13,15},{14,10},{15,... | collective-permute-start | bytes 835592 | tf_op jit(solution)/shard_map/ppermute | solution.py:44
  9.5 8.0 %collective-permute-start.3 = (bf16[64,2176]{1,0:T(8,128)(2,1)S(1)}, bf16[64,2176]{1,0:T(8,128)(2,1)S(1)}, u32[]{:S(2)}, u32[]{:S(2)}) collective-permute-start(bf16[64,2176]{1,0:T(8,128)(2,1)S(1)} %shard_map.47.refs_0_), channel_id=1, source_target_pairs={{0,2},{1,3},{4,0},{5,1},{8,4},{9,5},{12,8},{13,9},{14,12},{15,13},... | collective-permute-start | bytes 835592 | tf_op jit(solution)/shard_map/ppermute | solution.py:44
  11.0 1.9 %copy-start = (bf16[1,1,768,2048]{3,2,1,0:T(8,128)(2,1)S(1)}, bf16[1,1,768,2048]{3,2,1,0:T(8,128)(2,1)}, u32[]{:S(2)}) copy-start(bf16[1,1,768,2048]{3,2,1,0:T(8,128)(2,1)} %param.7) | copy-start | bytes 9437188
  12.9 6.6 %copy-start.1 = (bf16[1,1,768,2048]{3,2,1,0:T(8,128)(2,1)S(1)}, bf16[1,1,768,2048]{3,2,1,0:T(8,128)(2,1)}, u32[]{:S(2)}) copy-start(bf16[1,1,768,2048]{3,2,1,0:T(8,128)(2,1)} %param.7) | copy-start | bytes 9437188
  17.5 7.2 %collective-permute-start.5 = (bf16[64,2176]{1,0:T(8,128)(2,1)S(1)}, bf16[64,2176]{1,0:T(8,128)(2,1)S(1)}, u32[]{:S(2)}, u32[]{:S(2)}) collective-permute-start(bf16[64,2176]{1,0:T(8,128)(2,1)S(1)} %collective-permute-done.2.refs_0_), channel_id=1, source_target_pairs={{0,4},{1,5},{4,8},{5,9},{8,12},{9,13},{12,14},{13,15},{14,10},{15,... | collective-permute-start | bytes 835592 | tf_op jit(solution)/shard_map/ppermute | solution.py:44
  18.0 7.0 %collective-permute-start.6 = (bf16[64,2176]{1,0:T(8,128)(2,1)S(1)}, bf16[64,2176]{1,0:T(8,128)(2,1)S(1)}, u32[]{:S(2)}, u32[]{:S(2)}) collective-permute-start(bf16[64,2176]{1,0:T(8,128)(2,1)S(1)} %collective-permute-done.3.refs_1_), channel_id=1, source_target_pairs={{0,2},{1,3},{4,0},{5,1},{8,4},{9,5},{12,8},{13,9},{14,12},{15,13},... | collective-permute-start | bytes 835592 | tf_op jit(solution)/shard_map/ppermute | solution.py:44
  25.0 9.6 %collective-permute-start.8 = (bf16[64,2176]{1,0:T(8,128)(2,1)S(1)}, bf16[64,2176]{1,0:T(8,128)(2,1)S(1)}, u32[]{:S(2)}, u32[]{:S(2)}) collective-permute-start(bf16[64,2176]{1,0:T(8,128)(2,1)S(1)} %collective-permute-done.5.refs_0_), channel_id=1, source_target_pairs={{0,4},{1,5},{4,8},{5,9},{8,12},{9,13},{12,14},{13,15},{14,10},{15,... | collective-permute-start | bytes 835592 | tf_op jit(solution)/shard_map/ppermute | solution.py:44
  26.4 8.6 %collective-permute-start.9 = (bf16[64,2176]{1,0:T(8,128)(2,1)S(1)}, bf16[64,2176]{1,0:T(8,128)(2,1)S(1)}, u32[]{:S(2)}, u32[]{:S(2)}) collective-permute-start(bf16[64,2176]{1,0:T(8,128)(2,1)S(1)} %collective-permute-done.6.refs_1_), channel_id=1, source_target_pairs={{0,2},{1,3},{4,0},{5,1},{8,4},{9,5},{12,8},{13,9},{14,12},{15,13},... | collective-permute-start | bytes 835592 | tf_op jit(solution)/shard_map/ppermute | solution.py:44
  27.0 22.2 %collective-permute-start.16 = (bf16[2,64,768]{2,1,0:T(8,128)(2,1)S(1)}, bf16[2,64,768]{2,1,0:T(8,128)(2,1)S(1)}, u32[]{:S(2)}, u32[]{:S(2)}) collective-permute-start(bf16[2,64,768]{2,1,0:T(8,128)(2,1)S(1)} %get-tuple-element.26), channel_id=1, source_target_pairs={{0,4},{1,5},{4,8},{5,9},{8,12},{9,13},{12,14},{13,15},{14,10},{15,... | collective-permute-start | bytes 589832 | tf_op jit(solution)/shard_map/ppermute | solution.py:44
  28.4 22.7 %collective-permute-start.4 = (bf16[2,64,768]{2,1,0:T(8,128)(2,1)S(1)}, bf16[2,64,768]{2,1,0:T(8,128)(2,1)S(1)}, u32[]{:S(2)}, u32[]{:S(2)}) collective-permute-start(bf16[2,64,768]{2,1,0:T(8,128)(2,1)S(1)} %get-tuple-element.25), channel_id=1, source_target_pairs={{0,2},{1,3},{4,0},{5,1},{8,4},{9,5},{12,8},{13,9},{14,12},{15,13},... | collective-permute-start | bytes 589832 | tf_op jit(solution)/shard_map/ppermute | solution.py:44
  35.0 7.5 %collective-permute-start.11 = (bf16[32,2176]{1,0:T(8,128)(2,1)S(1)}, bf16[32,2176]{1,0:T(8,128)(2,1)S(1)}, u32[]{:S(2)}, u32[]{:S(2)}) collective-permute-start(bf16[32,2176]{1,0:T(8,128)(2,1)S(1)} %slice.6), channel_id=1, source_target_pairs={{0,4},{1,5},{4,8},{5,9},{8,12},{9,13},{12,14},{13,15},{14,10},{15,... | collective-permute-start | bytes 417800 | tf_op jit(solution)/shard_map/ppermute | solution.py:44
  36.6 7.0 %collective-permute-start.12 = (bf16[32,2176]{1,0:T(8,128)(2,1)S(1)}, bf16[32,2176]{1,0:T(8,128)(2,1)S(1)}, u32[]{:S(2)}, u32[]{:S(2)}) collective-permute-start(bf16[32,2176]{1,0:T(8,128)(2,1)S(1)} %slice.7), channel_id=1, source_target_pairs={{0,2},{1,3},{4,0},{5,1},{8,4},{9,5},{12,8},{13,9},{14,12},{15,13},... | collective-permute-start | bytes 417800 | tf_op jit(solution)/shard_map/ppermute | solution.py:44
  37.1 14.4 %collective-permute-start.15 = (bf16[2,64,768]{2,1,0:T(8,128)(2,1)S(1)}, bf16[2,64,768]{2,1,0:T(8,128)(2,1)S(1)}, u32[]{:S(2)}, u32[]{:S(2)}) collective-permute-start(bf16[2,64,768]{2,1,0:T(8,128)(2,1)S(1)} %get-tuple-element.30), channel_id=1, source_target_pairs={{0,8},{1,9},{4,12},{5,13},{8,14},{9,15},{12,10},{13,11},{14,6},{15... | collective-permute-start | bytes 589832 | tf_op jit(solution)/shard_map/ppermute | solution.py:44
  42.5 19.9 %collective-permute-start.7 = (bf16[2,64,768]{2,1,0:T(8,128)(2,1)S(1)}, bf16[2,64,768]{2,1,0:T(8,128)(2,1)S(1)}, u32[]{:S(2)}, u32[]{:S(2)}) collective-permute-start(bf16[2,64,768]{2,1,0:T(8,128)(2,1)S(1)} %get-tuple-element.29), channel_id=1, source_target_pairs={{0,6},{1,7},{4,2},{5,3},{8,0},{9,1},{12,4},{13,5},{14,8},{15,9},{1... | collective-permute-start | bytes 589832 | tf_op jit(solution)/shard_map/ppermute | solution.py:44
  43.7 22.8 %collective-permute-start.10 = (bf16[2,64,768]{2,1,0:T(8,128)(2,1)S(1)}, bf16[2,64,768]{2,1,0:T(8,128)(2,1)S(1)}, u32[]{:S(2)}, u32[]{:S(2)}) collective-permute-start(bf16[2,64,768]{2,1,0:T(8,128)(2,1)S(1)} %get-tuple-element.33), channel_id=1, source_target_pairs={{0,10},{1,11},{4,6},{5,7},{8,2},{9,3},{12,0},{13,1},{14,4},{15,5},... | collective-permute-start | bytes 589832 | tf_op jit(solution)/shard_map/ppermute | solution.py:44
  49.3 17.2 %collective-permute-start.14 = (bf16[2,64,768]{2,1,0:T(8,128)(2,1)S(1)}, bf16[2,64,768]{2,1,0:T(8,128)(2,1)S(1)}, u32[]{:S(2)}, u32[]{:S(2)}) collective-permute-start(bf16[2,64,768]{2,1,0:T(8,128)(2,1)S(1)} %get-tuple-element.34), channel_id=1, source_target_pairs={{0,12},{1,13},{4,14},{5,15},{8,10},{9,11},{12,6},{13,7},{14,2},{15... | collective-permute-start | bytes 589832 | tf_op jit(solution)/shard_map/ppermute | solution.py:44
  51.1 19.7 %collective-permute-start.13 = (bf16[2,64,768]{2,1,0:T(8,128)(2,1)S(1)}, bf16[2,64,768]{2,1,0:T(8,128)(2,1)S(1)}, u32[]{:S(2)}, u32[]{:S(2)}) collective-permute-start(bf16[2,64,768]{2,1,0:T(8,128)(2,1)S(1)} %shard_map.52), channel_id=1, source_target_pairs={{0,14},{1,15},{4,10},{5,11},{8,6},{9,7},{12,2},{13,3},{14,0},{15,1... | collective-permute-start | bytes 589832 | tf_op jit(solution)/shard_map/ppermute | solution.py:44

commit v8 on v7

--- a/solution.py
+++ b/solution.py
@@ -7,8 +7,8 @@
 from jax.experimental.pallas import tpu as pltpu
 from jax.sharding import PartitionSpec as P
 
-COLUMNS = 2
 CORES = 2
+X, Z_NEAR, Z_FAR = 1, 2, 4
 LANES = 128
 
 
@@ -18,30 +18,9 @@
     return lax.ppermute(block, axis, route)
 
 
-def ring_place(chip, size):
-    z, x = lax.div(chip, COLUMNS), lax.rem(chip, COLUMNS)
-    return jnp.where(x == 0, z, size - 1 - z)
-
-
-def ring_order(owners):
-    height = owners // (COLUMNS * CORES)
-    up = [z * COLUMNS for z in range(height)]
-    down = [z * COLUMNS + 1 for z in reversed(range(height))]
-    return up + down
-
-
-def ring_route(owners, distance, flip):
-    order = ring_order(owners)
-    route = []
-    for place, chip in enumerate(order):
-        target = order[(place + distance) % len(order)]
-        for core in range(CORES):
-            route.append((chip * CORES + core, target * CORES + (core ^ flip)))
-    return route
-
-
-def send(block, owners, distance, flip):
-    return lax.ppermute(block, "expert", ring_route(owners, distance, flip))
+def send(block, owners, flip, core=0):
+    route = [(i, ((i // CORES) ^ flip) * CORES + ((i % CORES) ^ core)) for i in range(owners)]
+    return lax.ppermute(block, "expert", route)
 
 
 def gates_kernel(ids, gates, out):
@@ -117,13 +96,11 @@
 def pick_kernel(ids, *refs):
     blocks, out = refs[:-1], refs[-1]
     experts, tokens, _ = blocks[0].shape
-    size = len(blocks)
     top = ids.shape[0]
     span = 16
-    place = ring_place(lax.div(lax.axis_index("expert"), CORES), size)
-    chip = lax.div(ids[...], CORES)
-    label = lax.rem(ring_place(chip, size) - place + size, size) * CORES + lax.rem(ids[...], CORES)
-    column = lax.broadcasted_iota(jnp.int32, (top, size * experts * span), 1)
+    chip = lax.div(lax.axis_index("expert"), CORES)
+    label = (lax.div(ids[...], CORES) ^ chip) * CORES + lax.rem(ids[...], CORES)
+    column = lax.broadcasted_iota(jnp.int32, (top, len(blocks) * experts * span), 1)
     for g in range(tokens // span):
         stacked = jnp.concatenate(
             [b[c, g * span : (g + 1) * span, :] for b in blocks for c in range(experts)], axis=0
@@ -149,33 +126,51 @@
 def dense_device(section_grad, route_ids, route_gates, weight_mat):
     tokens, top = route_ids.shape
     owners = lax.axis_size("expert")
-    size = owners // CORES
     other_mat = send(weight_mat, owners, 0, 1)
     section_grad, columns = lax.optimization_barrier(
         (section_grad, gate_columns(route_ids.T, route_gates.T))
     )
     rows = widened(section_grad, columns)
 
-    half, far = tokens // 2, size // 2
-    back = ahead = rows
-    waiting = {0: rows}
-    received = [None] * size
-    for step in range(1, far + 1):
-        if step < far:
-            next_back, next_ahead = send(back, owners, 1, 0), send(ahead, owners, -1, 0)
-        else:
-            next_back, next_ahead = (
-                send(back[:half], owners, 1, 0),
-                send(ahead[half:], owners, -1, 0),
-            )
-        results = products(list(waiting.values()), tokens, weight_mat, other_mat)
-        for distance, result in zip(waiting, results):
-            received[(-distance) % size] = send(result, owners, distance, 0) if distance else result
-        back, ahead, _ = lax.optimization_barrier((next_back, next_ahead, results))
-        waiting = {size - step: back, step: ahead}
-    (result,) = products([back, ahead], tokens, weight_mat, other_mat)
-    received[far] = send(result, owners, far, 0)
-    out = pick_routes(route_ids.T, received)
+    def work(*pieces):
+        return products(list(pieces), tokens, weight_mat, other_mat)
+
+    tie = lax.optimization_barrier
+    far = send(rows, owners, Z_FAR)
+    near = send(rows, owners, Z_NEAR)
+    side = send(rows, owners, X)
+    near, side, (out_own,) = tie((near, side, work(rows)))
+    near_side = send(near, owners, X)
+    far, (out_side, out_near) = tie((far, work(side, near)))
+    cross = send(far, owners, Z_NEAR)
+    far_side = send(far, owners, X)
+    (out_far,) = work(far)
+    back_far = send(out_far, owners, Z_FAR)
+    cross, _ = tie((cross, out_far))
+    cross_side = send(cross, owners, X)
+    (out_cross,) = work(cross)
+    back_cross = send(out_cross, owners, Z_NEAR ^ Z_FAR)
+    far_side, near_side, back_far, out_side, out_near, _ = tie(
+        (far_side, near_side, back_far, out_side, out_near, out_cross)
+    )
+    out_far_side, out_near_side = work(far_side, near_side)
+    back_far_side = send(out_far_side, owners, X ^ Z_FAR)
+    back_near_side = send(out_near_side, owners, X ^ Z_NEAR)
+    back_side = send(out_side, owners, X)
+    back_near = send(out_near, owners, Z_NEAR)
+    cross_side, _ = tie((cross_side, out_far_side))
+    (out_cross_side,) = work(cross_side)
+    received = {
+        0: out_own,
+        X: back_side,
+        Z_NEAR: back_near,
+        X ^ Z_NEAR: back_near_side,
+        Z_FAR: back_far,
+        X ^ Z_FAR: back_far_side,
+        Z_NEAR ^ Z_FAR: back_cross,
+        X ^ Z_NEAR ^ Z_FAR: send(out_cross_side, owners, X ^ Z_NEAR ^ Z_FAR),
+    }
+    out = pick_routes(route_ids.T, [received[flip] for flip in sorted(received)])
     return out.reshape(1, tokens, top, weight_mat.shape[0])
 
 
@@ -229,7 +224,7 @@
     tokens, top = route_ids.shape
     owners = lax.axis_size("expert")
     capacity = 2 * tokens * top // owners
-    if capacity >= tokens:
+    if capacity >= tokens and owners == CORES * 2 * Z_FAR:
         return dense_device(section_grad, route_ids, route_gates, weight_mat)
     return slotted_device(section_grad, route_ids, route_gates, weight_mat, capacity)
 

time: 72.3 us -> 70.9 us (0.981)
  the two profiles are of different devices: /device:TPU:10 before, /device:TPU:0 now
where the time goes in v8:
time: 70.9 us; the launch traced here: 69.8 us
  waiting for transfers between devices  26.9 us (38%)
  starting transfers between devices  25.7 us (36%)
  Pallas kernels  13.8 us (19%)
  local copies, waits for them, and re-layouts  3.26 us (5%)
    ppermute x15, starting transfers between devices, send(): return lax.ppermute(block, 'expert', route)  23.2 us
    ppermute x15, waiting for transfers between devices, send(): return lax.ppermute(block, 'expert', route)  21.2 us
    pallas_call x6, Pallas kernels, products(): pl.pallas_call(functools.partial(products_kernel, len(pieces)), out_shape...  12.4 us
    ppermute x1, waiting for transfers between devices, shifted(): return lax.ppermute(block, axis, route)  5.71 us
    unnamed x8, local copies, waits for them, and re-layouts  3.26 us
    ppermute x1, starting transfers between devices, shifted(): return lax.ppermute(block, axis, route)  2.52 us
  transfers between devices with their start and end apart: 16, of which 9 were waited for; matrix products, arithmetic and copies ran while one was open for 0% of the time, Pallas kernels for 18%

profile of v8, /device:TPU:0, one launch (start us, length us, event | category | flops | bytes accessed | tf_op | source)
XLA Modules:
  0.0 69.8 jit_solution(9801327910878116306)
XLA Ops:
  0.0 0.5 collective-permute-start.3
  0.5 2.5 %collective-permute-start = (bf16[1,64,2048]{2,1,0:T(8,128)(2,1)}, bf16[1,64,2048]{2,1,0:T(8,128)(2,1)S(1)}, u32[]{:S(2)}, u32[]{:S(2)}) collective-permute-start(bf16[1,64,2048]{2,1,0:T(8,128)(2,1)} %param.4), channel_id=1, source_target_pairs={{16,0},{0,16},{17,1},{1,17},{18,2},{2,18},{19,3},{3,19},{20,4},{4,... | collective-permute-start | bytes 786440 | tf_op jit(solution)/shard_map/ppermute | solution.py:18
  3.0 0.0 copy-start.2
  3.0 0.7 copy-done.2
  3.7 0.0 copy-start.3
  3.7 0.7 copy-done.3
  4.3 0.1 shard_map.46.columns
  4.4 5.7 %collective-permute-done = bf16[1,64,2048]{2,1,0:T(8,128)(2,1)S(1)} collective-permute-done((bf16[1,64,2048]{2,1,0:T(8,128)(2,1)}, bf16[1,64,2048]{2,1,0:T(8,128)(2,1)S(1)}, u32[]{:S(2)}, u32[]{:S(2)}) %collective-permute-start) | collective-permute-done | bytes 262176 | tf_op jit(solution)/shard_map/ppermute | solution.py:18
  10.2 1.9 %collective-permute-start.1 = (bf16[64,2176]{1,0:T(8,128)(2,1)S(1)}, bf16[64,2176]{1,0:T(8,128)(2,1)S(1)}, u32[]{:S(2)}, u32[]{:S(2)}) collective-permute-start(bf16[64,2176]{1,0:T(8,128)(2,1)S(1)} %shard_map.47.refs_0_), channel_id=1, source_target_pairs={{0,4},{1,5},{2,6},{3,7},{4,0},{5,1},{6,2},{7,3},{8,12},{9,13},{10,... | collective-permute-start | bytes 835592 | tf_op jit(solution)/shard_map/ppermute | solution.py:23
  12.0 1.5 %collective-permute-start.2 = (bf16[64,2176]{1,0:T(8,128)(2,1)S(1)}, bf16[64,2176]{1,0:T(8,128)(2,1)S(1)}, u32[]{:S(2)}, u32[]{:S(2)}) collective-permute-start(bf16[64,2176]{1,0:T(8,128)(2,1)S(1)} %shard_map.47.refs_0_), channel_id=1, source_target_pairs={{0,2},{1,3},{2,0},{3,1},{4,6},{5,7},{6,4},{7,5},{8,10},{9,11},{10,... | collective-permute-start | bytes 835592 | tf_op jit(solution)/shard_map/ppermute | solution.py:23
  13.5 2.6 %collective-permute-start.4 = (bf16[64,2176]{1,0:T(8,128)(2,1)S(1)}, bf16[64,2176]{1,0:T(8,128)(2,1)S(1)}, u32[]{:S(2)}, u32[]{:S(2)}) collective-permute-start(bf16[64,2176]{1,0:T(8,128)(2,1)S(1)} %shard_map.47.refs_0_), channel_id=1, source_target_pairs={{0,8},{1,9},{2,10},{3,11},{4,12},{5,13},{6,14},{7,15},{8,0},{9,1},... | collective-permute-start | bytes 835592 | tf_op jit(solution)/shard_map/ppermute | solution.py:23
  16.1 0.0 collective-permute-done.3.other
  16.1 0.0 copy-start
  16.1 1.9 %copy-done = bf16[1,1,768,2048]{3,2,1,0:T(8,128)(2,1)S(1)} copy-done((bf16[1,1,768,2048]{3,2,1,0:T(8,128)(2,1)S(1)}, bf16[1,1,768,2048]{3,2,1,0:T(8,128)(2,1)}, u32[]{:S(2)}) %copy-start) | copy-done | bytes 3145752
  18.0 0.0 copy-start.1
  18.0 2.0 %shard_map.48.refs_0_ = bf16[2,64,768]{2,1,0:T(8,128)(2,1)S(1)} custom-call(bf16[768,2048]{1,0:T(8,128)(2,1)S(1)} %bitcast.10, bf16[768,2048]{1,0:T(8,128)(2,1)S(1)} %collective-permute-done.3.other, bf16[64,2176]{1,0:T(8,128)(2,1)S(1)} %shard_map.47.refs_0_), custom_call_target="tpu_custom_call" | custom-call | flops 402653184 | bytes 6750208 | tf_op jit(solution)/shard_map/pallas_call | solution.py:84
  20.0 3.3 %collective-permute-done.1.refs_1_ = bf16[64,2176]{1,0:T(8,128)(2,1)S(1)} collective-permute-done((bf16[64,2176]{1,0:T(8,128)(2,1)S(1)}, bf16[64,2176]{1,0:T(8,128)(2,1)S(1)}, u32[]{:S(2)}, u32[]{:S(2)}) %collective-permute-start.1) | collective-permute-done | bytes 278560 | tf_op jit(solution)/shard_map/ppermute | solution.py:23
  23.4 0.0 collective-permute-done.2.refs_0_
  23.4 0.0 copy-done.1
  23.4 2.2 %shard_map.49 = (bf16[2,64,768]{2,1,0:T(8,128)(2,1)S(1)}, bf16[2,64,768]{2,1,0:T(8,128)(2,1)S(1)}) custom-call(bf16[768,2048]{1,0:T(8,128)(2,1)S(1)} %bitcast.11, bf16[768,2048]{1,0:T(8,128)(2,1)S(1)} %collective-permute-done.3.other, bf16[64,2176]{1,0:T(8,128)(2,1)S(1)} %collective-permute-done.2.refs_0_, bf16[64,2176]{1,0:T(8,128)(2,1)S(1)} %collective-permute-done.1.refs_1_), custom_call_target="tpu_custom_call" | custom-call | flops 805306368 | bytes 7208960 | tf_op jit(solution)/shard_map/pallas_call | solution.py:84
  25.6 2.7 %collective-permute-done.4.refs_0_ = bf16[64,2176]{1,0:T(8,128)(2,1)S(1)} collective-permute-done((bf16[64,2176]{1,0:T(8,128)(2,1)S(1)}, bf16[64,2176]{1,0:T(8,128)(2,1)S(1)}, u32[]{:S(2)}, u32[]{:S(2)}) %collective-permute-start.4) | collective-permute-done | bytes 278560 | tf_op jit(solution)/shard_map/ppermute | solution.py:23
  28.3 0.0 collective-permute-start.8
  28.3 0.6 collective-permute-start.5
  28.9 1.4 %collective-permute-start.6 = (bf16[64,2176]{1,0:T(8,128)(2,1)S(1)}, bf16[64,2176]{1,0:T(8,128)(2,1)S(1)}, u32[]{:S(2)}, u32[]{:S(2)}) collective-permute-start(bf16[64,2176]{1,0:T(8,128)(2,1)S(1)} %collective-permute-done.1.refs_1_), channel_id=1, source_target_pairs={{0,2},{1,3},{2,0},{3,1},{4,6},{5,7},{6,4},{7,5},{8,10},{9,11},{10,... | collective-permute-start | bytes 835592 | tf_op jit(solution)/shard_map/ppermute | solution.py:23
  30.3 2.0 %shard_map.50 = bf16[2,64,768]{2,1,0:T(8,128)(2,1)S(1)} custom-call(bf16[768,2048]{1,0:T(8,128)(2,1)S(1)} %bitcast.12, bf16[768,2048]{1,0:T(8,128)(2,1)S(1)} %collective-permute-done.3.other, bf16[64,2176]{1,0:T(8,128)(2,1)S(1)} %collective-permute-done.4.refs_0_), custom_call_target="tpu_custom_call" | custom-call | flops 402653184 | bytes 6750208 | tf_op jit(solution)/shard_map/pallas_call | solution.py:84
  32.3 3.0 %collective-permute-start.7 = (bf16[2,64,768]{2,1,0:T(8,128)(2,1)S(1)}, bf16[2,64,768]{2,1,0:T(8,128)(2,1)S(1)}, u32[]{:S(2)}, u32[]{:S(2)}) collective-permute-start(bf16[2,64,768]{2,1,0:T(8,128)(2,1)S(1)} %shard_map.50), channel_id=1, source_target_pairs={{0,8},{1,9},{2,10},{3,11},{4,12},{5,13},{6,14},{7,15},{8,0},{9,1},... | collective-permute-start | bytes 589832 | tf_op jit(solution)/shard_map/ppermute | solution.py:23
  35.3 0.7 collective-permute-done.8.refs_0_
  36.0 1.4 %collective-permute-start.14 = (bf16[64,2176]{1,0:T(8,128)(2,1)S(1)}, bf16[64,2176]{1,0:T(8,128)(2,1)S(1)}, u32[]{:S(2)}, u32[]{:S(2)}) collective-permute-start(bf16[64,2176]{1,0:T(8,128)(2,1)S(1)} %collective-permute-done.8.refs_0_), channel_id=1, source_target_pairs={{0,2},{1,3},{2,0},{3,1},{4,6},{5,7},{6,4},{7,5},{8,10},{9,11},{10,... | collective-permute-start | bytes 835592 | tf_op jit(solution)/shard_map/ppermute | solution.py:23
  37.4 2.0 %shard_map.51 = bf16[2,64,768]{2,1,0:T(8,128)(2,1)S(1)} custom-call(bf16[768,2048]{1,0:T(8,128)(2,1)S(1)} %bitcast.13, bf16[768,2048]{1,0:T(8,128)(2,1)S(1)} %collective-permute-done.3.other, bf16[64,2176]{1,0:T(8,128)(2,1)S(1)} %collective-permute-done.8.refs_0_), custom_call_target="tpu_custom_call" | custom-call | flops 402653184 | bytes 6750208 | tf_op jit(solution)/shard_map/pallas_call | solution.py:84
  39.4 2.6 %collective-permute-done.7.refs_4_ = bf16[2,64,768]{2,1,0:T(8,128)(2,1)S(1)} collective-permute-done((bf16[2,64,768]{2,1,0:T(8,128)(2,1)S(1)}, bf16[2,64,768]{2,1,0:T(8,128)(2,1)S(1)}, u32[]{:S(2)}, u32[]{:S(2)}) %collective-permute-start.7) | collective-permute-done | bytes 196640 | tf_op jit(solution)/shard_map/ppermute | solution.py:23
  42.0 0.0 collective-permute-done.5.refs_0_
  42.0 1.9 %collective-permute-done.6.refs_1_ = bf16[64,2176]{1,0:T(8,128)(2,1)S(1)} collective-permute-done((bf16[64,2176]{1,0:T(8,128)(2,1)S(1)}, bf16[64,2176]{1,0:T(8,128)(2,1)S(1)}, u32[]{:S(2)}, u32[]{:S(2)}) %collective-permute-start.6) | collective-permute-done | bytes 278560 | tf_op jit(solution)/shard_map/ppermute | solution.py:23
  43.8 0.6 collective-permute-start.9
  44.5 2.3 %collective-permute-start.13 = (bf16[2,64,768]{2,1,0:T(8,128)(2,1)S(1)}, bf16[2,64,768]{2,1,0:T(8,128)(2,1)S(1)}, u32[]{:S(2)}, u32[]{:S(2)}) collective-permute-start(bf16[2,64,768]{2,1,0:T(8,128)(2,1)S(1)} %shard_map.51), channel_id=1, source_target_pairs={{0,12},{1,13},{2,14},{3,15},{4,8},{5,9},{6,10},{7,11},{8,4},{9,5},... | collective-permute-start | bytes 589832 | tf_op jit(solution)/shard_map/ppermute | solution.py:23
  46.8 1.1 %collective-permute-start.10 = (bf16[2,64,768]{2,1,0:T(8,128)(2,1)S(1)}, bf16[2,64,768]{2,1,0:T(8,128)(2,1)S(1)}, u32[]{:S(2)}, u32[]{:S(2)}) collective-permute-start(bf16[2,64,768]{2,1,0:T(8,128)(2,1)S(1)} %get-tuple-element.36), channel_id=1, source_target_pairs={{0,4},{1,5},{2,6},{3,7},{4,0},{5,1},{6,2},{7,3},{8,12},{9,13},{10,... | collective-permute-start | bytes 589832 | tf_op jit(solution)/shard_map/ppermute | solution.py:23
  47.9 2.2 %shard_map.52 = (bf16[2,64,768]{2,1,0:T(8,128)(2,1)S(1)}, bf16[2,64,768]{2,1,0:T(8,128)(2,1)S(1)}) custom-call(bf16[768,2048]{1,0:T(8,128)(2,1)S(1)} %bitcast.14, bf16[768,2048]{1,0:T(8,128)(2,1)S(1)} %collective-permute-done.3.other, bf16[64,2176]{1,0:T(8,128)(2,1)S(1)} %collective-permute-done.5.refs_0_, bf16[64,2176]{1,0:T(8,128)(2,1)S(1)} %collective-permute-done.6.refs_1_), custom_call_target="tpu_custom_call" | custom-call | flops 805306368 | bytes 7208960 | tf_op jit(solution)/shard_map/pallas_call | solution.py:84
  50.1 1.9 %collective-permute-start.11 = (bf16[2,64,768]{2,1,0:T(8,128)(2,1)S(1)}, bf16[2,64,768]{2,1,0:T(8,128)(2,1)S(1)}, u32[]{:S(2)}, u32[]{:S(2)}) collective-permute-start(bf16[2,64,768]{2,1,0:T(8,128)(2,1)S(1)} %get-tuple-element.39), channel_id=1, source_target_pairs={{0,6},{1,7},{2,4},{3,5},{4,2},{5,3},{6,0},{7,1},{8,14},{9,15},{10,... | collective-permute-start | bytes 589832 | tf_op jit(solution)/shard_map/ppermute | solution.py:23
  52.0 0.0 collective-permute-done.14.refs_0_
  52.0 1.2 %collective-permute-start.12 = (bf16[2,64,768]{2,1,0:T(8,128)(2,1)S(1)}, bf16[2,64,768]{2,1,0:T(8,128)(2,1)S(1)}, u32[]{:S(2)}, u32[]{:S(2)}) collective-permute-start(bf16[2,64,768]{2,1,0:T(8,128)(2,1)S(1)} %get-tuple-element.41), channel_id=1, source_target_pairs={{0,10},{1,11},{2,8},{3,9},{4,14},{5,15},{6,12},{7,13},{8,2},{9,3},... | collective-permute-start | bytes 589832 | tf_op jit(solution)/shard_map/ppermute | solution.py:23
  53.2 2.0 %shard_map.53 = bf16[2,64,768]{2,1,0:T(8,128)(2,1)S(1)} custom-call(bf16[768,2048]{1,0:T(8,128)(2,1)S(1)} %bitcast.15, bf16[768,2048]{1,0:T(8,128)(2,1)S(1)} %collective-permute-done.3.other, bf16[64,2176]{1,0:T(8,128)(2,1)S(1)} %collective-permute-done.14.refs_0_), custom_call_target="tpu_custom_call" | custom-call | flops 402653184 | bytes 6750208 | tf_op jit(solution)/shard_map/pallas_call | solution.py:84
  55.2 0.0 collective-permute-done.9.refs_1_
  55.2 3.2 %collective-permute-start.15 = (bf16[2,64,768]{2,1,0:T(8,128)(2,1)S(1)}, bf16[2,64,768]{2,1,0:T(8,128)(2,1)S(1)}, u32[]{:S(2)}, u32[]{:S(2)}) collective-permute-start(bf16[2,64,768]{2,1,0:T(8,128)(2,1)S(1)} %shard_map.53), channel_id=1, source_target_pairs={{0,14},{1,15},{2,12},{3,13},{4,10},{5,11},{6,8},{7,9},{8,6},{9,7},... | collective-permute-start | bytes 589832 | tf_op jit(solution)/shard_map/ppermute | solution.py:23
  58.4 1.5 %collective-permute-done.10.refs_2_ = bf16[2,64,768]{2,1,0:T(8,128)(2,1)S(1)} collective-permute-done((bf16[2,64,768]{2,1,0:T(8,128)(2,1)S(1)}, bf16[2,64,768]{2,1,0:T(8,128)(2,1)S(1)}, u32[]{:S(2)}, u32[]{:S(2)}) %collective-permute-start.10) | collective-permute-done | bytes 196640 | tf_op jit(solution)/shard_map/ppermute | solution.py:23
  59.9 3.7 %collective-permute-done.11.refs_3_ = bf16[2,64,768]{2,1,0:T(8,128)(2,1)S(1)} collective-permute-done((bf16[2,64,768]{2,1,0:T(8,128)(2,1)S(1)}, bf16[2,64,768]{2,1,0:T(8,128)(2,1)S(1)}, u32[]{:S(2)}, u32[]{:S(2)}) %collective-permute-start.11) | collective-permute-done | bytes 196640 | tf_op jit(solution)/shard_map/ppermute | solution.py:23
  63.6 4.8 %collective-permute-done.12.refs_5_ = bf16[2,64,768]{2,1,0:T(8,128)(2,1)S(1)} collective-permute-done((bf16[2,64,768]{2,1,0:T(8,128)(2,1)S(1)}, bf16[2,64,768]{2,1,0:T(8,128)(2,1)S(1)}, u32[]{:S(2)}, u32[]{:S(2)}) %collective-permute-start.12) | collective-permute-done | bytes 196640 | tf_op jit(solution)/shard_map/ppermute | solution.py:23
  68.5 0.0 collective-permute-done.13.refs_6_
  68.5 0.0 collective-permute-done.15.refs_7_
  68.5 1.3 %shard_map.54 = bf16[512,768]{1,0:T(8,128)(2,1)} custom-call(s32[8,64]{1,0:T(8,128)S(1)} %bitcast.18, bf16[2,64,768]{2,1,0:T(8,128)(2,1)S(1)} %shard_map.48.refs_0_, bf16[2,64,768]{2,1,0:T(8,128)(2,1)S(1)} %collective-permute-done.9.refs_1_, bf16[2,64,768]{2,1,0:T(8,128)(2,1)S(1)} %collective-permute-done.10.refs_2_, ...), custom_call_target="tpu_custom_call" | custom-call | tf_op jit(solution)/shard_map/pallas_call | solution.py:119
  (1 shorter events, 0.0 us)
Async XLA Ops:
  0.0 16.1 %collective-permute-start.3 = (bf16[768,2048]{1,0:T(8,128)(2,1)}, bf16[768,2048]{1,0:T(8,128)(2,1)S(1)}, u32[]{:S(2)}, u32[]{:S(2)}) collective-permute-start(bf16[768,2048]{1,0:T(8,128)(2,1)} %bitcast.9), channel_id=1, source_target_pairs={{0,1},{1,0},{2,3},{3,2},{4,5},{5,4},{6,7},{7,6},{8,9},{9,8},{10,11... | collective-permute-start | bytes 9437192 | tf_op jit(solution)/shard_map/ppermute | solution.py:23
  0.5 9.7 %collective-permute-start = (bf16[1,64,2048]{2,1,0:T(8,128)(2,1)}, bf16[1,64,2048]{2,1,0:T(8,128)(2,1)S(1)}, u32[]{:S(2)}, u32[]{:S(2)}) collective-permute-start(bf16[1,64,2048]{2,1,0:T(8,128)(2,1)} %param.4), channel_id=1, source_target_pairs={{16,0},{0,16},{17,1},{1,17},{18,2},{2,18},{19,3},{3,19},{20,4},{4,... | collective-permute-start | bytes 786440 | tf_op jit(solution)/shard_map/ppermute | solution.py:18
  3.0 0.7 copy-start.2
  3.7 0.7 copy-start.3
  10.2 13.2 %collective-permute-start.1 = (bf16[64,2176]{1,0:T(8,128)(2,1)S(1)}, bf16[64,2176]{1,0:T(8,128)(2,1)S(1)}, u32[]{:S(2)}, u32[]{:S(2)}) collective-permute-start(bf16[64,2176]{1,0:T(8,128)(2,1)S(1)} %shard_map.47.refs_0_), channel_id=1, source_target_pairs={{0,4},{1,5},{2,6},{3,7},{4,0},{5,1},{6,2},{7,3},{8,12},{9,13},{10,... | collective-permute-start | bytes 835592 | tf_op jit(solution)/shard_map/ppermute | solution.py:23
  12.0 11.3 %collective-permute-start.2 = (bf16[64,2176]{1,0:T(8,128)(2,1)S(1)}, bf16[64,2176]{1,0:T(8,128)(2,1)S(1)}, u32[]{:S(2)}, u32[]{:S(2)}) collective-permute-start(bf16[64,2176]{1,0:T(8,128)(2,1)S(1)} %shard_map.47.refs_0_), channel_id=1, source_target_pairs={{0,2},{1,3},{2,0},{3,1},{4,6},{5,7},{6,4},{7,5},{8,10},{9,11},{10,... | collective-permute-start | bytes 835592 | tf_op jit(solution)/shard_map/ppermute | solution.py:23
  13.5 14.7 %collective-permute-start.4 = (bf16[64,2176]{1,0:T(8,128)(2,1)S(1)}, bf16[64,2176]{1,0:T(8,128)(2,1)S(1)}, u32[]{:S(2)}, u32[]{:S(2)}) collective-permute-start(bf16[64,2176]{1,0:T(8,128)(2,1)S(1)} %shard_map.47.refs_0_), channel_id=1, source_target_pairs={{0,8},{1,9},{2,10},{3,11},{4,12},{5,13},{6,14},{7,15},{8,0},{9,1},... | collective-permute-start | bytes 835592 | tf_op jit(solution)/shard_map/ppermute | solution.py:23
  16.1 1.9 %copy-start = (bf16[1,1,768,2048]{3,2,1,0:T(8,128)(2,1)S(1)}, bf16[1,1,768,2048]{3,2,1,0:T(8,128)(2,1)}, u32[]{:S(2)}) copy-start(bf16[1,1,768,2048]{3,2,1,0:T(8,128)(2,1)} %param.7) | copy-start | bytes 9437188
  18.0 5.4 %copy-start.1 = (bf16[1,1,768,2048]{3,2,1,0:T(8,128)(2,1)S(1)}, bf16[1,1,768,2048]{3,2,1,0:T(8,128)(2,1)}, u32[]{:S(2)}) copy-start(bf16[1,1,768,2048]{3,2,1,0:T(8,128)(2,1)} %param.7) | copy-start | bytes 9437188
  28.3 7.7 %collective-permute-start.8 = (bf16[64,2176]{1,0:T(8,128)(2,1)S(1)}, bf16[64,2176]{1,0:T(8,128)(2,1)S(1)}, u32[]{:S(2)}, u32[]{:S(2)}) collective-permute-start(bf16[64,2176]{1,0:T(8,128)(2,1)S(1)} %collective-permute-done.4.refs_0_), channel_id=1, source_target_pairs={{0,4},{1,5},{2,6},{3,7},{4,0},{5,1},{6,2},{7,3},{8,12},{9,13},{10,... | collective-permute-start | bytes 835592 | tf_op jit(solution)/shard_map/ppermute | solution.py:23
  28.3 13.7 %collective-permute-start.5 = (bf16[64,2176]{1,0:T(8,128)(2,1)S(1)}, bf16[64,2176]{1,0:T(8,128)(2,1)S(1)}, u32[]{:S(2)}, u32[]{:S(2)}) collective-permute-start(bf16[64,2176]{1,0:T(8,128)(2,1)S(1)} %collective-permute-done.4.refs_0_), channel_id=1, source_target_pairs={{0,2},{1,3},{2,0},{3,1},{4,6},{5,7},{6,4},{7,5},{8,10},{9,11},{10,... | collective-permute-start | bytes 835592 | tf_op jit(solution)/shard_map/ppermute | solution.py:23
  28.9 14.9 %collective-permute-start.6 = (bf16[64,2176]{1,0:T(8,128)(2,1)S(1)}, bf16[64,2176]{1,0:T(8,128)(2,1)S(1)}, u32[]{:S(2)}, u32[]{:S(2)}) collective-permute-start(bf16[64,2176]{1,0:T(8,128)(2,1)S(1)} %collective-permute-done.1.refs_1_), channel_id=1, source_target_pairs={{0,2},{1,3},{2,0},{3,1},{4,6},{5,7},{6,4},{7,5},{8,10},{9,11},{10,... | collective-permute-start | bytes 835592 | tf_op jit(solution)/shard_map/ppermute | solution.py:23
  32.3 9.7 %collective-permute-start.7 = (bf16[2,64,768]{2,1,0:T(8,128)(2,1)S(1)}, bf16[2,64,768]{2,1,0:T(8,128)(2,1)S(1)}, u32[]{:S(2)}, u32[]{:S(2)}) collective-permute-start(bf16[2,64,768]{2,1,0:T(8,128)(2,1)S(1)} %shard_map.50), channel_id=1, source_target_pairs={{0,8},{1,9},{2,10},{3,11},{4,12},{5,13},{6,14},{7,15},{8,0},{9,1},... | collective-permute-start | bytes 589832 | tf_op jit(solution)/shard_map/ppermute | solution.py:23
  36.0 15.9 %collective-permute-start.14 = (bf16[64,2176]{1,0:T(8,128)(2,1)S(1)}, bf16[64,2176]{1,0:T(8,128)(2,1)S(1)}, u32[]{:S(2)}, u32[]{:S(2)}) collective-permute-start(bf16[64,2176]{1,0:T(8,128)(2,1)S(1)} %collective-permute-done.8.refs_0_), channel_id=1, source_target_pairs={{0,2},{1,3},{2,0},{3,1},{4,6},{5,7},{6,4},{7,5},{8,10},{9,11},{10,... | collective-permute-start | bytes 835592 | tf_op jit(solution)/shard_map/ppermute | solution.py:23
  43.8 11.4 %collective-permute-start.9 = (bf16[2,64,768]{2,1,0:T(8,128)(2,1)S(1)}, bf16[2,64,768]{2,1,0:T(8,128)(2,1)S(1)}, u32[]{:S(2)}, u32[]{:S(2)}) collective-permute-start(bf16[2,64,768]{2,1,0:T(8,128)(2,1)S(1)} %get-tuple-element.35), channel_id=1, source_target_pairs={{0,2},{1,3},{2,0},{3,1},{4,6},{5,7},{6,4},{7,5},{8,10},{9,11},{10,... | collective-permute-start | bytes 589832 | tf_op jit(solution)/shard_map/ppermute | solution.py:23
  44.5 24.0 %collective-permute-start.13 = (bf16[2,64,768]{2,1,0:T(8,128)(2,1)S(1)}, bf16[2,64,768]{2,1,0:T(8,128)(2,1)S(1)}, u32[]{:S(2)}, u32[]{:S(2)}) collective-permute-start(bf16[2,64,768]{2,1,0:T(8,128)(2,1)S(1)} %shard_map.51), channel_id=1, source_target_pairs={{0,12},{1,13},{2,14},{3,15},{4,8},{5,9},{6,10},{7,11},{8,4},{9,5},... | collective-permute-start | bytes 589832 | tf_op jit(solution)/shard_map/ppermute | solution.py:23
  46.8 13.2 %collective-permute-start.10 = (bf16[2,64,768]{2,1,0:T(8,128)(2,1)S(1)}, bf16[2,64,768]{2,1,0:T(8,128)(2,1)S(1)}, u32[]{:S(2)}, u32[]{:S(2)}) collective-permute-start(bf16[2,64,768]{2,1,0:T(8,128)(2,1)S(1)} %get-tuple-element.36), channel_id=1, source_target_pairs={{0,4},{1,5},{2,6},{3,7},{4,0},{5,1},{6,2},{7,3},{8,12},{9,13},{10,... | collective-permute-start | bytes 589832 | tf_op jit(solution)/shard_map/ppermute | solution.py:23
  50.1 13.6 %collective-permute-start.11 = (bf16[2,64,768]{2,1,0:T(8,128)(2,1)S(1)}, bf16[2,64,768]{2,1,0:T(8,128)(2,1)S(1)}, u32[]{:S(2)}, u32[]{:S(2)}) collective-permute-start(bf16[2,64,768]{2,1,0:T(8,128)(2,1)S(1)} %get-tuple-element.39), channel_id=1, source_target_pairs={{0,6},{1,7},{2,4},{3,5},{4,2},{5,3},{6,0},{7,1},{8,14},{9,15},{10,... | collective-permute-start | bytes 589832 | tf_op jit(solution)/shard_map/ppermute | solution.py:23
  52.0 16.5 %collective-permute-start.12 = (bf16[2,64,768]{2,1,0:T(8,128)(2,1)S(1)}, bf16[2,64,768]{2,1,0:T(8,128)(2,1)S(1)}, u32[]{:S(2)}, u32[]{:S(2)}) collective-permute-start(bf16[2,64,768]{2,1,0:T(8,128)(2,1)S(1)} %get-tuple-element.41), channel_id=1, source_target_pairs={{0,10},{1,11},{2,8},{3,9},{4,14},{5,15},{6,12},{7,13},{8,2},{9,3},... | collective-permute-start | bytes 589832 | tf_op jit(solution)/shard_map/ppermute | solution.py:23
  55.2 13.2 %collective-permute-start.15 = (bf16[2,64,768]{2,1,0:T(8,128)(2,1)S(1)}, bf16[2,64,768]{2,1,0:T(8,128)(2,1)S(1)}, u32[]{:S(2)}, u32[]{:S(2)}) collective-permute-start(bf16[2,64,768]{2,1,0:T(8,128)(2,1)S(1)} %shard_map.53), channel_id=1, source_target_pairs={{0,14},{1,15},{2,12},{3,13},{4,10},{5,11},{6,8},{7,9},{8,6},{9,7},... | collective-permute-start | bytes 589832 | tf_op jit(solution)/shard_map/ppermute | solution.py:23

commit v9 on v8

--- a/solution.py
+++ b/solution.py
@@ -139,27 +139,29 @@
     far = send(rows, owners, Z_FAR)
     near = send(rows, owners, Z_NEAR)
     side = send(rows, owners, X)
-    near, side, (out_own,) = tie((near, side, work(rows)))
-    near_side = send(near, owners, X)
-    far, (out_side, out_near) = tie((far, work(side, near)))
+    (out_own,) = work(rows)
+    far, _ = tie((far, out_own))
     cross = send(far, owners, Z_NEAR)
-    far_side = send(far, owners, X)
     (out_far,) = work(far)
     back_far = send(out_far, owners, Z_FAR)
-    cross, _ = tie((cross, out_far))
+    near, side, _ = tie((near, side, out_far))
+    far_side = send(tie((far, near))[0], owners, X)
+    out_side, out_near = work(side, near)
+    cross, near, _ = tie((cross, near, out_side))
     cross_side = send(cross, owners, X)
+    near_side = send(near, owners, X)
     (out_cross,) = work(cross)
     back_cross = send(out_cross, owners, Z_NEAR ^ Z_FAR)
-    far_side, near_side, back_far, out_side, out_near, _ = tie(
-        (far_side, near_side, back_far, out_side, out_near, out_cross)
-    )
-    out_far_side, out_near_side = work(far_side, near_side)
+    far_side, back_far, out_side, out_near, _ = tie(
+        (far_side, back_far, out_side, out_near, out_cross)
+    )
+    (out_far_side,) = work(far_side)
     back_far_side = send(out_far_side, owners, X ^ Z_FAR)
+    cross_side, near_side, _ = tie((cross_side, near_side, out_far_side))
+    (out_cross_side, out_near_side) = work(cross_side, near_side)
     back_near_side = send(out_near_side, owners, X ^ Z_NEAR)
     back_side = send(out_side, owners, X)
     back_near = send(out_near, owners, Z_NEAR)
-    cross_side, _ = tie((cross_side, out_far_side))
-    (out_cross_side,) = work(cross_side)
     received = {
         0: out_own,
         X: back_side,

time: 70.9 us -> 71.3 us (level); the launches traced: 69.8 us -> 71.1 us
  starting transfers between devices: 25.7 us -> 28.9 us
  waiting for transfers between devices: 26.9 us -> 25.1 us
    ppermute x15, starting transfers between devices: 23.2 us -> 26.4 us  [send(): return lax.ppermute(block, 'expert', route)]
    ppermute x15, waiting for transfers between devices: 21.2 us -> 19.4 us  [send(): return lax.ppermute(block, 'expert', route)]
  transfers between devices with their start and end apart: 16 -> 16, of which waited for: 9 -> 7; matrix products, arithmetic and copies ran while one was open for 0% -> 0% of each run, Pallas kernels for 18% -> 18%
where the time goes in v9:
time: 71.3 us; the launch traced here: 71.1 us
  starting transfers between devices  28.9 us (41%)
  waiting for transfers between devices  25.1 us (35%)
  Pallas kernels  13.8 us (19%)
  local copies, waits for them, and re-layouts  3.26 us (5%)
    ppermute x15, starting transfers between devices, send(): return lax.ppermute(block, 'expert', route)  26.4 us
    ppermute x15, waiting for transfers between devices, send(): return lax.ppermute(block, 'expert', route)  19.4 us
    pallas_call x6, Pallas kernels, products(): pl.pallas_call(functools.partial(products_kernel, len(pieces)), out_shape...  12.4 us
    ppermute x1, waiting for transfers between devices, shifted(): return lax.ppermute(block, axis, route)  5.71 us
    unnamed x8, local copies, waits for them, and re-layouts  3.26 us
    ppermute x1, starting transfers between devices, shifted(): return lax.ppermute(block, axis, route)  2.52 us
  transfers between devices with their start and end apart: 16, of which 7 were waited for; matrix products, arithmetic and copies ran while one was open for 0% of the time, Pallas kernels for 18%

profile of v9, /device:TPU:0, one launch (start us, length us, event | category | flops | bytes accessed | tf_op | source)
XLA Modules:
  0.0 71.1 jit_solution(5504202069731381217)
XLA Ops:
  0.0 0.5 collective-permute-start
  0.5 2.5 %collective-permute-start.1 = (bf16[1,64,2048]{2,1,0:T(8,128)(2,1)}, bf16[1,64,2048]{2,1,0:T(8,128)(2,1)S(1)}, u32[]{:S(2)}, u32[]{:S(2)}) collective-permute-start(bf16[1,64,2048]{2,1,0:T(8,128)(2,1)} %param.4), channel_id=1, source_target_pairs={{16,0},{0,16},{17,1},{1,17},{18,2},{2,18},{19,3},{3,19},{20,4},{4,... | collective-permute-start | bytes 786440 | tf_op jit(solution)/shard_map/ppermute | solution.py:18
  3.0 0.0 copy-start.2
  3.0 0.7 copy-done.2
  3.7 0.0 copy-start.3
  3.7 0.7 copy-done.3
  4.3 0.1 shard_map.46.columns
  4.4 5.7 %collective-permute-done.1 = bf16[1,64,2048]{2,1,0:T(8,128)(2,1)S(1)} collective-permute-done((bf16[1,64,2048]{2,1,0:T(8,128)(2,1)}, bf16[1,64,2048]{2,1,0:T(8,128)(2,1)S(1)}, u32[]{:S(2)}, u32[]{:S(2)}) %collective-permute-start.1) | collective-permute-done | bytes 262176 | tf_op jit(solution)/shard_map/ppermute | solution.py:18
  10.2 2.9 %collective-permute-start.2 = (bf16[64,2176]{1,0:T(8,128)(2,1)S(1)}, bf16[64,2176]{1,0:T(8,128)(2,1)S(1)}, u32[]{:S(2)}, u32[]{:S(2)}) collective-permute-start(bf16[64,2176]{1,0:T(8,128)(2,1)S(1)} %shard_map.47.refs_0_), channel_id=1, source_target_pairs={{0,8},{1,9},{2,10},{3,11},{4,12},{5,13},{6,14},{7,15},{8,0},{9,1},... | collective-permute-start | bytes 835592 | tf_op jit(solution)/shard_map/ppermute | solution.py:23
  13.1 1.6 %collective-permute-start.3 = (bf16[64,2176]{1,0:T(8,128)(2,1)S(1)}, bf16[64,2176]{1,0:T(8,128)(2,1)S(1)}, u32[]{:S(2)}, u32[]{:S(2)}) collective-permute-start(bf16[64,2176]{1,0:T(8,128)(2,1)S(1)} %shard_map.47.refs_0_), channel_id=1, source_target_pairs={{0,4},{1,5},{2,6},{3,7},{4,0},{5,1},{6,2},{7,3},{8,12},{9,13},{10,... | collective-permute-start | bytes 835592 | tf_op jit(solution)/shard_map/ppermute | solution.py:23
  14.6 1.5 %collective-permute-start.4 = (bf16[64,2176]{1,0:T(8,128)(2,1)S(1)}, bf16[64,2176]{1,0:T(8,128)(2,1)S(1)}, u32[]{:S(2)}, u32[]{:S(2)}) collective-permute-start(bf16[64,2176]{1,0:T(8,128)(2,1)S(1)} %shard_map.47.refs_0_), channel_id=1, source_target_pairs={{0,2},{1,3},{2,0},{3,1},{4,6},{5,7},{6,4},{7,5},{8,10},{9,11},{10,... | collective-permute-start | bytes 835592 | tf_op jit(solution)/shard_map/ppermute | solution.py:23
  16.1 0.0 collective-permute-done.other
  16.1 0.0 copy-start
  16.1 1.9 %copy-done = bf16[1,1,768,2048]{3,2,1,0:T(8,128)(2,1)S(1)} copy-done((bf16[1,1,768,2048]{3,2,1,0:T(8,128)(2,1)S(1)}, bf16[1,1,768,2048]{3,2,1,0:T(8,128)(2,1)}, u32[]{:S(2)}) %copy-start) | copy-done | bytes 3145752
  18.0 0.0 copy-start.1
  18.0 2.0 %shard_map.48.refs_0_ = bf16[2,64,768]{2,1,0:T(8,128)(2,1)S(1)} custom-call(bf16[768,2048]{1,0:T(8,128)(2,1)S(1)} %bitcast.10, bf16[768,2048]{1,0:T(8,128)(2,1)S(1)} %collective-permute-done.other, bf16[64,2176]{1,0:T(8,128)(2,1)S(1)} %shard_map.47.refs_0_), custom_call_target="tpu_custom_call" | custom-call | flops 402653184 | bytes 6750208 | tf_op jit(solution)/shard_map/pallas_call | solution.py:84
  20.0 5.7 %collective-permute-done.2.refs_0_ = bf16[64,2176]{1,0:T(8,128)(2,1)S(1)} collective-permute-done((bf16[64,2176]{1,0:T(8,128)(2,1)S(1)}, bf16[64,2176]{1,0:T(8,128)(2,1)S(1)}, u32[]{:S(2)}, u32[]{:S(2)}) %collective-permute-start.2) | collective-permute-done | bytes 278560 | tf_op jit(solution)/shard_map/ppermute | solution.py:23
  25.7 0.6 collective-permute-start.7
  26.3 0.0 copy-done.1
  26.3 2.0 %shard_map.49 = bf16[2,64,768]{2,1,0:T(8,128)(2,1)S(1)} custom-call(bf16[768,2048]{1,0:T(8,128)(2,1)S(1)} %bitcast.11, bf16[768,2048]{1,0:T(8,128)(2,1)S(1)} %collective-permute-done.other, bf16[64,2176]{1,0:T(8,128)(2,1)S(1)} %collective-permute-done.2.refs_0_), custom_call_target="tpu_custom_call" | custom-call | flops 402653184 | bytes 6750208 | tf_op jit(solution)/shard_map/pallas_call | solution.py:84
  28.3 0.0 collective-permute-done.3.refs_1_
  28.3 0.0 collective-permute-done.4.refs_0_
  28.3 1.6 %collective-permute-start.5 = (bf16[64,2176]{1,0:T(8,128)(2,1)S(1)}, bf16[64,2176]{1,0:T(8,128)(2,1)S(1)}, u32[]{:S(2)}, u32[]{:S(2)}) collective-permute-start(bf16[64,2176]{1,0:T(8,128)(2,1)S(1)} %collective-permute-done.2.refs_0_), channel_id=1, source_target_pairs={{0,2},{1,3},{2,0},{3,1},{4,6},{5,7},{6,4},{7,5},{8,10},{9,11},{10,... | collective-permute-start | bytes 835592 | tf_op jit(solution)/shard_map/ppermute | solution.py:23
  29.9 3.4 %collective-permute-start.6 = (bf16[2,64,768]{2,1,0:T(8,128)(2,1)S(1)}, bf16[2,64,768]{2,1,0:T(8,128)(2,1)S(1)}, u32[]{:S(2)}, u32[]{:S(2)}) collective-permute-start(bf16[2,64,768]{2,1,0:T(8,128)(2,1)S(1)} %shard_map.49), channel_id=1, source_target_pairs={{0,8},{1,9},{2,10},{3,11},{4,12},{5,13},{6,14},{7,15},{8,0},{9,1},... | collective-permute-start | bytes 589832 | tf_op jit(solution)/shard_map/ppermute | solution.py:23
  33.3 2.2 %shard_map.50 = (bf16[2,64,768]{2,1,0:T(8,128)(2,1)S(1)}, bf16[2,64,768]{2,1,0:T(8,128)(2,1)S(1)}) custom-call(bf16[768,2048]{1,0:T(8,128)(2,1)S(1)} %bitcast.12, bf16[768,2048]{1,0:T(8,128)(2,1)S(1)} %collective-permute-done.other, bf16[64,2176]{1,0:T(8,128)(2,1)S(1)} %collective-permute-done.4.refs_0_, bf16[64,2176]{1,0:T(8,128)(2,1)S(1)} %collective-permute-done.3.refs_1_), custom_call_target="tpu_custom_call" | custom-call | flops 805306368 | bytes 7208960 | tf_op jit(solution)/shard_map/pallas_call | solution.py:84
  35.4 0.0 collective-permute-done.7.refs_0_
  35.5 2.4 %collective-permute-start.10 = (bf16[64,2176]{1,0:T(8,128)(2,1)S(1)}, bf16[64,2176]{1,0:T(8,128)(2,1)S(1)}, u32[]{:S(2)}, u32[]{:S(2)}) collective-permute-start(bf16[64,2176]{1,0:T(8,128)(2,1)S(1)} %collective-permute-done.7.refs_0_), channel_id=1, source_target_pairs={{0,2},{1,3},{2,0},{3,1},{4,6},{5,7},{6,4},{7,5},{8,10},{9,11},{10,... | collective-permute-start | bytes 835592 | tf_op jit(solution)/shard_map/ppermute | solution.py:23
  37.9 0.0 collective-permute-start.11
  37.9 2.0 %shard_map.51 = bf16[2,64,768]{2,1,0:T(8,128)(2,1)S(1)} custom-call(bf16[768,2048]{1,0:T(8,128)(2,1)S(1)} %bitcast.13, bf16[768,2048]{1,0:T(8,128)(2,1)S(1)} %collective-permute-done.other, bf16[64,2176]{1,0:T(8,128)(2,1)S(1)} %collective-permute-done.7.refs_0_), custom_call_target="tpu_custom_call" | custom-call | flops 402653184 | bytes 6750208 | tf_op jit(solution)/shard_map/pallas_call | solution.py:84
  39.9 2.1 %collective-permute-done.6.refs_4_ = bf16[2,64,768]{2,1,0:T(8,128)(2,1)S(1)} collective-permute-done((bf16[2,64,768]{2,1,0:T(8,128)(2,1)S(1)}, bf16[2,64,768]{2,1,0:T(8,128)(2,1)S(1)}, u32[]{:S(2)}, u32[]{:S(2)}) %collective-permute-start.6) | collective-permute-done | bytes 196640 | tf_op jit(solution)/shard_map/ppermute | solution.py:23
  42.0 0.0 collective-permute-done.5.refs_0_
  42.0 2.0 %shard_map.52 = bf16[2,64,768]{2,1,0:T(8,128)(2,1)S(1)} custom-call(bf16[768,2048]{1,0:T(8,128)(2,1)S(1)} %bitcast.14, bf16[768,2048]{1,0:T(8,128)(2,1)S(1)} %collective-permute-done.other, bf16[64,2176]{1,0:T(8,128)(2,1)S(1)} %collective-permute-done.5.refs_0_), custom_call_target="tpu_custom_call" | custom-call | flops 402653184 | bytes 6750208 | tf_op jit(solution)/shard_map/pallas_call | solution.py:84
  44.0 0.6 collective-permute-start.13
  44.6 2.0 %collective-permute-start.14 = (bf16[2,64,768]{2,1,0:T(8,128)(2,1)S(1)}, bf16[2,64,768]{2,1,0:T(8,128)(2,1)S(1)}, u32[]{:S(2)}, u32[]{:S(2)}) collective-permute-start(bf16[2,64,768]{2,1,0:T(8,128)(2,1)S(1)} %shard_map.51), channel_id=1, source_target_pairs={{0,12},{1,13},{2,14},{3,15},{4,8},{5,9},{6,10},{7,11},{8,4},{9,5},... | collective-permute-start | bytes 589832 | tf_op jit(solution)/shard_map/ppermute | solution.py:23
  46.6 0.9 %collective-permute-start.8 = (bf16[2,64,768]{2,1,0:T(8,128)(2,1)S(1)}, bf16[2,64,768]{2,1,0:T(8,128)(2,1)S(1)}, u32[]{:S(2)}, u32[]{:S(2)}) collective-permute-start(bf16[2,64,768]{2,1,0:T(8,128)(2,1)S(1)} %get-tuple-element.32), channel_id=1, source_target_pairs={{0,2},{1,3},{2,0},{3,1},{4,6},{5,7},{6,4},{7,5},{8,10},{9,11},{10,... | collective-permute-start | bytes 589832 | tf_op jit(solution)/shard_map/ppermute | solution.py:23
  47.5 0.0 collective-permute-done.10.refs_0_
  47.5 1.5 %collective-permute-start.9 = (bf16[2,64,768]{2,1,0:T(8,128)(2,1)S(1)}, bf16[2,64,768]{2,1,0:T(8,128)(2,1)S(1)}, u32[]{:S(2)}, u32[]{:S(2)}) collective-permute-start(bf16[2,64,768]{2,1,0:T(8,128)(2,1)S(1)} %get-tuple-element.33), channel_id=1, source_target_pairs={{0,4},{1,5},{2,6},{3,7},{4,0},{5,1},{6,2},{7,3},{8,12},{9,13},{10,... | collective-permute-start | bytes 589832 | tf_op jit(solution)/shard_map/ppermute | solution.py:23
  49.0 2.8 %collective-permute-done.11.refs_1_ = bf16[64,2176]{1,0:T(8,128)(2,1)S(1)} collective-permute-done((bf16[64,2176]{1,0:T(8,128)(2,1)S(1)}, bf16[64,2176]{1,0:T(8,128)(2,1)S(1)}, u32[]{:S(2)}, u32[]{:S(2)}) %collective-permute-start.11) | collective-permute-done | bytes 278560 | tf_op jit(solution)/shard_map/ppermute | solution.py:23
  51.9 2.2 %shard_map.53 = (bf16[2,64,768]{2,1,0:T(8,128)(2,1)S(1)}, bf16[2,64,768]{2,1,0:T(8,128)(2,1)S(1)}) custom-call(bf16[768,2048]{1,0:T(8,128)(2,1)S(1)} %bitcast.15, bf16[768,2048]{1,0:T(8,128)(2,1)S(1)} %collective-permute-done.other, bf16[64,2176]{1,0:T(8,128)(2,1)S(1)} %collective-permute-done.10.refs_0_, bf16[64,2176]{1,0:T(8,128)(2,1)S(1)} %collective-permute-done.11.refs_1_), custom_call_target="tpu_custom_call" | custom-call | flops 805306368 | bytes 7208960 | tf_op jit(solution)/shard_map/pallas_call | solution.py:84
  54.0 4.4 %collective-permute-start.12 = (bf16[2,64,768]{2,1,0:T(8,128)(2,1)S(1)}, bf16[2,64,768]{2,1,0:T(8,128)(2,1)S(1)}, u32[]{:S(2)}, u32[]{:S(2)}) collective-permute-start(bf16[2,64,768]{2,1,0:T(8,128)(2,1)S(1)} %get-tuple-element.38), channel_id=1, source_target_pairs={{0,6},{1,7},{2,4},{3,5},{4,2},{5,3},{6,0},{7,1},{8,14},{9,15},{10,... | collective-permute-start | bytes 589832 | tf_op jit(solution)/shard_map/ppermute | solution.py:23
  58.4 0.8 %collective-permute-done.13.refs_5_ = bf16[2,64,768]{2,1,0:T(8,128)(2,1)S(1)} collective-permute-done((bf16[2,64,768]{2,1,0:T(8,128)(2,1)S(1)}, bf16[2,64,768]{2,1,0:T(8,128)(2,1)S(1)}, u32[]{:S(2)}, u32[]{:S(2)}) %collective-permute-start.13) | collective-permute-done | bytes 196640 | tf_op jit(solution)/shard_map/ppermute | solution.py:23
  59.2 2.6 %collective-permute-start.15 = (bf16[2,64,768]{2,1,0:T(8,128)(2,1)S(1)}, bf16[2,64,768]{2,1,0:T(8,128)(2,1)S(1)}, u32[]{:S(2)}, u32[]{:S(2)}) collective-permute-start(bf16[2,64,768]{2,1,0:T(8,128)(2,1)S(1)} %get-tuple-element.40), channel_id=1, source_target_pairs={{0,14},{1,15},{2,12},{3,13},{4,10},{5,11},{6,8},{7,9},{8,6},{9,7},... | collective-permute-start | bytes 589832 | tf_op jit(solution)/shard_map/ppermute | solution.py:23
  61.8 0.0 collective-permute-done.8.refs_1_
  61.8 0.0 collective-permute-done.9.refs_2_
  61.8 0.0 collective-permute-done.14.refs_6_
  61.8 4.8 %collective-permute-done.12.refs_3_ = bf16[2,64,768]{2,1,0:T(8,128)(2,1)S(1)} collective-permute-done((bf16[2,64,768]{2,1,0:T(8,128)(2,1)S(1)}, bf16[2,64,768]{2,1,0:T(8,128)(2,1)S(1)}, u32[]{:S(2)}, u32[]{:S(2)}) %collective-permute-start.12) | collective-permute-done | bytes 196640 | tf_op jit(solution)/shard_map/ppermute | solution.py:23
  66.6 3.2 %collective-permute-done.15.refs_7_ = bf16[2,64,768]{2,1,0:T(8,128)(2,1)S(1)} collective-permute-done((bf16[2,64,768]{2,1,0:T(8,128)(2,1)S(1)}, bf16[2,64,768]{2,1,0:T(8,128)(2,1)S(1)}, u32[]{:S(2)}, u32[]{:S(2)}) %collective-permute-start.15) | collective-permute-done | bytes 196640 | tf_op jit(solution)/shard_map/ppermute | solution.py:23
  69.8 1.3 %shard_map.54 = bf16[512,768]{1,0:T(8,128)(2,1)} custom-call(s32[8,64]{1,0:T(8,128)S(1)} %bitcast.18, bf16[2,64,768]{2,1,0:T(8,128)(2,1)S(1)} %shard_map.48.refs_0_, bf16[2,64,768]{2,1,0:T(8,128)(2,1)S(1)} %collective-permute-done.8.refs_1_, bf16[2,64,768]{2,1,0:T(8,128)(2,1)S(1)} %collective-permute-done.9.refs_2_, ...), custom_call_target="tpu_custom_call" | custom-call | tf_op jit(solution)/shard_map/pallas_call | solution.py:119
  (1 shorter events, 0.0 us)
Async XLA Ops:
  0.0 16.1 %collective-permute-start = (bf16[768,2048]{1,0:T(8,128)(2,1)}, bf16[768,2048]{1,0:T(8,128)(2,1)S(1)}, u32[]{:S(2)}, u32[]{:S(2)}) collective-permute-start(bf16[768,2048]{1,0:T(8,128)(2,1)} %bitcast.9), channel_id=1, source_target_pairs={{0,1},{1,0},{2,3},{3,2},{4,5},{5,4},{6,7},{7,6},{8,9},{9,8},{10,11... | collective-permute-start | bytes 9437192 | tf_op jit(solution)/shard_map/ppermute | solution.py:23
  0.5 9.7 %collective-permute-start.1 = (bf16[1,64,2048]{2,1,0:T(8,128)(2,1)}, bf16[1,64,2048]{2,1,0:T(8,128)(2,1)S(1)}, u32[]{:S(2)}, u32[]{:S(2)}) collective-permute-start(bf16[1,64,2048]{2,1,0:T(8,128)(2,1)} %param.4), channel_id=1, source_target_pairs={{16,0},{0,16},{17,1},{1,17},{18,2},{2,18},{19,3},{3,19},{20,4},{4,... | collective-permute-start | bytes 786440 | tf_op jit(solution)/shard_map/ppermute | solution.py:18
  3.0 0.7 copy-start.2
  3.7 0.7 copy-start.3
  10.2 15.5 %collective-permute-start.2 = (bf16[64,2176]{1,0:T(8,128)(2,1)S(1)}, bf16[64,2176]{1,0:T(8,128)(2,1)S(1)}, u32[]{:S(2)}, u32[]{:S(2)}) collective-permute-start(bf16[64,2176]{1,0:T(8,128)(2,1)S(1)} %shard_map.47.refs_0_), channel_id=1, source_target_pairs={{0,8},{1,9},{2,10},{3,11},{4,12},{5,13},{6,14},{7,15},{8,0},{9,1},... | collective-permute-start | bytes 835592 | tf_op jit(solution)/shard_map/ppermute | solution.py:23
  13.1 15.3 %collective-permute-start.3 = (bf16[64,2176]{1,0:T(8,128)(2,1)S(1)}, bf16[64,2176]{1,0:T(8,128)(2,1)S(1)}, u32[]{:S(2)}, u32[]{:S(2)}) collective-permute-start(bf16[64,2176]{1,0:T(8,128)(2,1)S(1)} %shard_map.47.refs_0_), channel_id=1, source_target_pairs={{0,4},{1,5},{2,6},{3,7},{4,0},{5,1},{6,2},{7,3},{8,12},{9,13},{10,... | collective-permute-start | bytes 835592 | tf_op jit(solution)/shard_map/ppermute | solution.py:23
  14.6 13.7 %collective-permute-start.4 = (bf16[64,2176]{1,0:T(8,128)(2,1)S(1)}, bf16[64,2176]{1,0:T(8,128)(2,1)S(1)}, u32[]{:S(2)}, u32[]{:S(2)}) collective-permute-start(bf16[64,2176]{1,0:T(8,128)(2,1)S(1)} %shard_map.47.refs_0_), channel_id=1, source_target_pairs={{0,2},{1,3},{2,0},{3,1},{4,6},{5,7},{6,4},{7,5},{8,10},{9,11},{10,... | collective-permute-start | bytes 835592 | tf_op jit(solution)/shard_map/ppermute | solution.py:23
  16.1 1.9 %copy-start = (bf16[1,1,768,2048]{3,2,1,0:T(8,128)(2,1)S(1)}, bf16[1,1,768,2048]{3,2,1,0:T(8,128)(2,1)}, u32[]{:S(2)}) copy-start(bf16[1,1,768,2048]{3,2,1,0:T(8,128)(2,1)} %param.7) | copy-start | bytes 9437188
  18.0 8.3 %copy-start.1 = (bf16[1,1,768,2048]{3,2,1,0:T(8,128)(2,1)S(1)}, bf16[1,1,768,2048]{3,2,1,0:T(8,128)(2,1)}, u32[]{:S(2)}) copy-start(bf16[1,1,768,2048]{3,2,1,0:T(8,128)(2,1)} %param.7) | copy-start | bytes 9437188
  25.7 9.7 %collective-permute-start.7 = (bf16[64,2176]{1,0:T(8,128)(2,1)S(1)}, bf16[64,2176]{1,0:T(8,128)(2,1)S(1)}, u32[]{:S(2)}, u32[]{:S(2)}) collective-permute-start(bf16[64,2176]{1,0:T(8,128)(2,1)S(1)} %collective-permute-done.2.refs_0_), channel_id=1, source_target_pairs={{0,4},{1,5},{2,6},{3,7},{4,0},{5,1},{6,2},{7,3},{8,12},{9,13},{10,... | collective-permute-start | bytes 835592 | tf_op jit(solution)/shard_map/ppermute | solution.py:23
  28.3 13.7 %collective-permute-start.5 = (bf16[64,2176]{1,0:T(8,128)(2,1)S(1)}, bf16[64,2176]{1,0:T(8,128)(2,1)S(1)}, u32[]{:S(2)}, u32[]{:S(2)}) collective-permute-start(bf16[64,2176]{1,0:T(8,128)(2,1)S(1)} %collective-permute-done.2.refs_0_), channel_id=1, source_target_pairs={{0,2},{1,3},{2,0},{3,1},{4,6},{5,7},{6,4},{7,5},{8,10},{9,11},{10,... | collective-permute-start | bytes 835592 | tf_op jit(solution)/shard_map/ppermute | solution.py:23
  29.9 12.1 %collective-permute-start.6 = (bf16[2,64,768]{2,1,0:T(8,128)(2,1)S(1)}, bf16[2,64,768]{2,1,0:T(8,128)(2,1)S(1)}, u32[]{:S(2)}, u32[]{:S(2)}) collective-permute-start(bf16[2,64,768]{2,1,0:T(8,128)(2,1)S(1)} %shard_map.49), channel_id=1, source_target_pairs={{0,8},{1,9},{2,10},{3,11},{4,12},{5,13},{6,14},{7,15},{8,0},{9,1},... | collective-permute-start | bytes 589832 | tf_op jit(solution)/shard_map/ppermute | solution.py:23
  35.5 12.0 %collective-permute-start.10 = (bf16[64,2176]{1,0:T(8,128)(2,1)S(1)}, bf16[64,2176]{1,0:T(8,128)(2,1)S(1)}, u32[]{:S(2)}, u32[]{:S(2)}) collective-permute-start(bf16[64,2176]{1,0:T(8,128)(2,1)S(1)} %collective-permute-done.7.refs_0_), channel_id=1, source_target_pairs={{0,2},{1,3},{2,0},{3,1},{4,6},{5,7},{6,4},{7,5},{8,10},{9,11},{10,... | collective-permute-start | bytes 835592 | tf_op jit(solution)/shard_map/ppermute | solution.py:23
  37.9 14.0 %collective-permute-start.11 = (bf16[64,2176]{1,0:T(8,128)(2,1)S(1)}, bf16[64,2176]{1,0:T(8,128)(2,1)S(1)}, u32[]{:S(2)}, u32[]{:S(2)}) collective-permute-start(bf16[64,2176]{1,0:T(8,128)(2,1)S(1)} %collective-permute-done.3.refs_1_), channel_id=1, source_target_pairs={{0,2},{1,3},{2,0},{3,1},{4,6},{5,7},{6,4},{7,5},{8,10},{9,11},{10,... | collective-permute-start | bytes 835592 | tf_op jit(solution)/shard_map/ppermute | solution.py:23
  44.0 15.2 %collective-permute-start.13 = (bf16[2,64,768]{2,1,0:T(8,128)(2,1)S(1)}, bf16[2,64,768]{2,1,0:T(8,128)(2,1)S(1)}, u32[]{:S(2)}, u32[]{:S(2)}) collective-permute-start(bf16[2,64,768]{2,1,0:T(8,128)(2,1)S(1)} %shard_map.52), channel_id=1, source_target_pairs={{0,10},{1,11},{2,8},{3,9},{4,14},{5,15},{6,12},{7,13},{8,2},{9,3},... | collective-permute-start | bytes 589832 | tf_op jit(solution)/shard_map/ppermute | solution.py:23
  44.6 17.2 %collective-permute-start.14 = (bf16[2,64,768]{2,1,0:T(8,128)(2,1)S(1)}, bf16[2,64,768]{2,1,0:T(8,128)(2,1)S(1)}, u32[]{:S(2)}, u32[]{:S(2)}) collective-permute-start(bf16[2,64,768]{2,1,0:T(8,128)(2,1)S(1)} %shard_map.51), channel_id=1, source_target_pairs={{0,12},{1,13},{2,14},{3,15},{4,8},{5,9},{6,10},{7,11},{8,4},{9,5},... | collective-permute-start | bytes 589832 | tf_op jit(solution)/shard_map/ppermute | solution.py:23
  46.6 15.2 %collective-permute-start.8 = (bf16[2,64,768]{2,1,0:T(8,128)(2,1)S(1)}, bf16[2,64,768]{2,1,0:T(8,128)(2,1)S(1)}, u32[]{:S(2)}, u32[]{:S(2)}) collective-permute-start(bf16[2,64,768]{2,1,0:T(8,128)(2,1)S(1)} %get-tuple-element.32), channel_id=1, source_target_pairs={{0,2},{1,3},{2,0},{3,1},{4,6},{5,7},{6,4},{7,5},{8,10},{9,11},{10,... | collective-permute-start | bytes 589832 | tf_op jit(solution)/shard_map/ppermute | solution.py:23
  47.5 14.3 %collective-permute-start.9 = (bf16[2,64,768]{2,1,0:T(8,128)(2,1)S(1)}, bf16[2,64,768]{2,1,0:T(8,128)(2,1)S(1)}, u32[]{:S(2)}, u32[]{:S(2)}) collective-permute-start(bf16[2,64,768]{2,1,0:T(8,128)(2,1)S(1)} %get-tuple-element.33), channel_id=1, source_target_pairs={{0,4},{1,5},{2,6},{3,7},{4,0},{5,1},{6,2},{7,3},{8,12},{9,13},{10,... | collective-permute-start | bytes 589832 | tf_op jit(solution)/shard_map/ppermute | solution.py:23
  54.0 12.6 %collective-permute-start.12 = (bf16[2,64,768]{2,1,0:T(8,128)(2,1)S(1)}, bf16[2,64,768]{2,1,0:T(8,128)(2,1)S(1)}, u32[]{:S(2)}, u32[]{:S(2)}) collective-permute-start(bf16[2,64,768]{2,1,0:T(8,128)(2,1)S(1)} %get-tuple-element.38), channel_id=1, source_target_pairs={{0,6},{1,7},{2,4},{3,5},{4,2},{5,3},{6,0},{7,1},{8,14},{9,15},{10,... | collective-permute-start | bytes 589832 | tf_op jit(solution)/shard_map/ppermute | solution.py:23
  59.2 10.6 %collective-permute-start.15 = (bf16[2,64,768]{2,1,0:T(8,128)(2,1)S(1)}, bf16[2,64,768]{2,1,0:T(8,128)(2,1)S(1)}, u32[]{:S(2)}, u32[]{:S(2)}) collective-permute-start(bf16[2,64,768]{2,1,0:T(8,128)(2,1)S(1)} %get-tuple-element.40), channel_id=1, source_target_pairs={{0,14},{1,15},{2,12},{3,13},{4,10},{5,11},{6,8},{7,9},{8,6},{9,7},... | collective-permute-start | bytes 589832 | tf_op jit(solution)/shard_map/ppermute | solution.py:23

commit v10 on v9

--- a/solution.py
+++ b/solution.py
@@ -86,7 +86,7 @@
         out_shape=[jax.ShapeDtypeStruct((CORES, tokens, hidden), jnp.bfloat16)] * (total // tokens),
         compiler_params=pltpu.CompilerParams(vmem_limit_bytes=16 << 20),
         cost_estimate=pl.CostEstimate(
-            flops=2 * CORES * total * hidden * depth,
+            flops=20 * CORES * total * hidden * depth,
             bytes_accessed=2 * (total * (2 * hidden + depth) + 2 * hidden * depth),
             transcendentals=0,
         ),
@@ -157,7 +157,7 @@
     )
     (out_far_side,) = work(far_side)
     back_far_side = send(out_far_side, owners, X ^ Z_FAR)
-    cross_side, near_side, _ = tie((cross_side, near_side, out_far_side))
+    cross_side, near_side, back_cross, _ = tie((cross_side, near_side, back_cross, out_far_side))
     (out_cross_side, out_near_side) = work(cross_side, near_side)
     back_near_side = send(out_near_side, owners, X ^ Z_NEAR)
     back_side = send(out_side, owners, X)

time: 71.3 us -> 72.4 us (1.015)
  starting transfers between devices: 28.9 us -> 31.8 us
  waiting for transfers between devices: 25.1 us -> 23.2 us
    ppermute x15, starting transfers between devices: 26.4 us -> 29.2 us  [send(): return lax.ppermute(block, 'expert', route)]
    ppermute x15, waiting for transfers between devices: 19.4 us -> 17.5 us  [send(): return lax.ppermute(block, 'expert', route)]
  transfers between devices with their start and end apart: 16 -> 16, of which waited for: 7 -> 6; matrix products, arithmetic and copies ran while one was open for 0% -> 0% of each run, Pallas kernels for 18% -> 17%
where the time goes in v10:
time: 72.4 us; the launch traced here: 72.2 us
  starting transfers between devices  31.8 us (44%)
  waiting for transfers between devices  23.2 us (32%)
  Pallas kernels  13.9 us (19%)
  local copies, waits for them, and re-layouts  3.26 us (5%)
    ppermute x15, starting transfers between devices, send(): return lax.ppermute(block, 'expert', route)  29.2 us
    ppermute x15, waiting for transfers between devices, send(): return lax.ppermute(block, 'expert', route)  17.5 us
    pallas_call x6, Pallas kernels, products(): pl.pallas_call(functools.partial(products_kernel, len(pieces)), out_shape...  12.4 us
    ppermute x1, waiting for transfers between devices, shifted(): return lax.ppermute(block, axis, route)  5.71 us
    unnamed x8, local copies, waits for them, and re-layouts  3.26 us
    ppermute x1, starting transfers between devices, shifted(): return lax.ppermute(block, axis, route)  2.52 us
  transfers between devices with their start and end apart: 16, of which 6 were waited for; matrix products, arithmetic and copies ran while one was open for 0% of the time, Pallas kernels for 17%

profile of v10, /device:TPU:0, one launch (start us, length us, event | category | flops | bytes accessed | tf_op | source)
XLA Modules:
  0.0 72.2 jit_solution(17624792885746693361)
XLA Ops:
  0.0 0.5 collective-permute-start
  0.5 2.5 %collective-permute-start.1 = (bf16[1,64,2048]{2,1,0:T(8,128)(2,1)}, bf16[1,64,2048]{2,1,0:T(8,128)(2,1)S(1)}, u32[]{:S(2)}, u32[]{:S(2)}) collective-permute-start(bf16[1,64,2048]{2,1,0:T(8,128)(2,1)} %param.4), channel_id=1, source_target_pairs={{16,0},{0,16},{17,1},{1,17},{18,2},{2,18},{19,3},{3,19},{20,4},{4,... | collective-permute-start | bytes 786440 | tf_op jit(solution)/shard_map/ppermute | solution.py:18
  3.0 0.0 copy-start
  3.0 0.7 copy-done
  3.7 0.0 copy-start.2
  3.7 0.7 copy-done.2
  4.3 0.1 shard_map.46.columns
  4.4 5.7 %collective-permute-done.1 = bf16[1,64,2048]{2,1,0:T(8,128)(2,1)S(1)} collective-permute-done((bf16[1,64,2048]{2,1,0:T(8,128)(2,1)}, bf16[1,64,2048]{2,1,0:T(8,128)(2,1)S(1)}, u32[]{:S(2)}, u32[]{:S(2)}) %collective-permute-start.1) | collective-permute-done | bytes 262176 | tf_op jit(solution)/shard_map/ppermute | solution.py:18
  10.2 2.9 %collective-permute-start.2 = (bf16[64,2176]{1,0:T(8,128)(2,1)S(1)}, bf16[64,2176]{1,0:T(8,128)(2,1)S(1)}, u32[]{:S(2)}, u32[]{:S(2)}) collective-permute-start(bf16[64,2176]{1,0:T(8,128)(2,1)S(1)} %shard_map.47.refs_0_), channel_id=1, source_target_pairs={{0,8},{1,9},{2,10},{3,11},{4,12},{5,13},{6,14},{7,15},{8,0},{9,1},... | collective-permute-start | bytes 835592 | tf_op jit(solution)/shard_map/ppermute | solution.py:23
  13.1 1.6 %collective-permute-start.3 = (bf16[64,2176]{1,0:T(8,128)(2,1)S(1)}, bf16[64,2176]{1,0:T(8,128)(2,1)S(1)}, u32[]{:S(2)}, u32[]{:S(2)}) collective-permute-start(bf16[64,2176]{1,0:T(8,128)(2,1)S(1)} %shard_map.47.refs_0_), channel_id=1, source_target_pairs={{0,4},{1,5},{2,6},{3,7},{4,0},{5,1},{6,2},{7,3},{8,12},{9,13},{10,... | collective-permute-start | bytes 835592 | tf_op jit(solution)/shard_map/ppermute | solution.py:23
  14.6 1.5 %collective-permute-start.4 = (bf16[64,2176]{1,0:T(8,128)(2,1)S(1)}, bf16[64,2176]{1,0:T(8,128)(2,1)S(1)}, u32[]{:S(2)}, u32[]{:S(2)}) collective-permute-start(bf16[64,2176]{1,0:T(8,128)(2,1)S(1)} %shard_map.47.refs_0_), channel_id=1, source_target_pairs={{0,2},{1,3},{2,0},{3,1},{4,6},{5,7},{6,4},{7,5},{8,10},{9,11},{10,... | collective-permute-start | bytes 835592 | tf_op jit(solution)/shard_map/ppermute | solution.py:23
  16.1 0.0 collective-permute-done.other
  16.1 0.0 copy-start.3
  16.1 1.9 %copy-done.3 = bf16[1,1,768,2048]{3,2,1,0:T(8,128)(2,1)S(1)} copy-done((bf16[1,1,768,2048]{3,2,1,0:T(8,128)(2,1)S(1)}, bf16[1,1,768,2048]{3,2,1,0:T(8,128)(2,1)}, u32[]{:S(2)}) %copy-start.3) | copy-done | bytes 3145752
  18.0 2.0 %shard_map.48.refs_0_ = bf16[2,64,768]{2,1,0:T(8,128)(2,1)S(1)} custom-call(bf16[768,2048]{1,0:T(8,128)(2,1)S(1)} %bitcast.14, bf16[768,2048]{1,0:T(8,128)(2,1)S(1)} %collective-permute-done.other, bf16[64,2176]{1,0:T(8,128)(2,1)S(1)} %shard_map.47.refs_0_), custom_call_target="tpu_custom_call" | custom-call | flops 4026531840 | bytes 6750208 | tf_op jit(solution)/shard_map/pallas_call | solution.py:84
  20.0 5.7 %collective-permute-done.2.refs_0_ = bf16[64,2176]{1,0:T(8,128)(2,1)S(1)} collective-permute-done((bf16[64,2176]{1,0:T(8,128)(2,1)S(1)}, bf16[64,2176]{1,0:T(8,128)(2,1)S(1)}, u32[]{:S(2)}, u32[]{:S(2)}) %collective-permute-start.2) | collective-permute-done | bytes 278560 | tf_op jit(solution)/shard_map/ppermute | solution.py:23
  25.7 0.6 collective-permute-start.7
  26.3 2.0 %shard_map.49 = bf16[2,64,768]{2,1,0:T(8,128)(2,1)S(1)} custom-call(bf16[768,2048]{1,0:T(8,128)(2,1)S(1)} %bitcast.15, bf16[768,2048]{1,0:T(8,128)(2,1)S(1)} %collective-permute-done.other, bf16[64,2176]{1,0:T(8,128)(2,1)S(1)} %collective-permute-done.2.refs_0_), custom_call_target="tpu_custom_call" | custom-call | flops 4026531840 | bytes 6750208 | tf_op jit(solution)/shard_map/pallas_call | solution.py:84
  28.3 3.4 %collective-permute-start.6 = (bf16[2,64,768]{2,1,0:T(8,128)(2,1)S(1)}, bf16[2,64,768]{2,1,0:T(8,128)(2,1)S(1)}, u32[]{:S(2)}, u32[]{:S(2)}) collective-permute-start(bf16[2,64,768]{2,1,0:T(8,128)(2,1)S(1)} %shard_map.49), channel_id=1, source_target_pairs={{0,8},{1,9},{2,10},{3,11},{4,12},{5,13},{6,14},{7,15},{8,0},{9,1},... | collective-permute-start | bytes 589832 | tf_op jit(solution)/shard_map/ppermute | solution.py:23
  31.8 0.0 collective-permute-done.3.refs_1_
  31.8 0.0 collective-permute-done.4.refs_0_
  31.8 1.5 %collective-permute-start.5 = (bf16[64,2176]{1,0:T(8,128)(2,1)S(1)}, bf16[64,2176]{1,0:T(8,128)(2,1)S(1)}, u32[]{:S(2)}, u32[]{:S(2)}) collective-permute-start(bf16[64,2176]{1,0:T(8,128)(2,1)S(1)} %collective-permute-done.2.refs_0_), channel_id=1, source_target_pairs={{0,2},{1,3},{2,0},{3,1},{4,6},{5,7},{6,4},{7,5},{8,10},{9,11},{10,... | collective-permute-start | bytes 835592 | tf_op jit(solution)/shard_map/ppermute | solution.py:23
  33.3 2.2 %shard_map.50 = (bf16[2,64,768]{2,1,0:T(8,128)(2,1)S(1)}, bf16[2,64,768]{2,1,0:T(8,128)(2,1)S(1)}) custom-call(bf16[768,2048]{1,0:T(8,128)(2,1)S(1)} %bitcast.16, bf16[768,2048]{1,0:T(8,128)(2,1)S(1)} %collective-permute-done.other, bf16[64,2176]{1,0:T(8,128)(2,1)S(1)} %collective-permute-done.4.refs_0_, bf16[64,2176]{1,0:T(8,128)(2,1)S(1)} %collective-permute-done.3.refs_1_), custom_call_target="tpu_custom_call" | custom-call | flops 8053063680 | bytes 7208960 | tf_op jit(solution)/shard_map/pallas_call | solution.py:84
  35.4 1.5 %collective-permute-done.7.refs_0_ = bf16[64,2176]{1,0:T(8,128)(2,1)S(1)} collective-permute-done((bf16[64,2176]{1,0:T(8,128)(2,1)S(1)}, bf16[64,2176]{1,0:T(8,128)(2,1)S(1)}, u32[]{:S(2)}, u32[]{:S(2)}) %collective-permute-start.7) | collective-permute-done | bytes 278560 | tf_op jit(solution)/shard_map/ppermute | solution.py:23
  36.9 1.4 %collective-permute-start.10 = (bf16[64,2176]{1,0:T(8,128)(2,1)S(1)}, bf16[64,2176]{1,0:T(8,128)(2,1)S(1)}, u32[]{:S(2)}, u32[]{:S(2)}) collective-permute-start(bf16[64,2176]{1,0:T(8,128)(2,1)S(1)} %collective-permute-done.7.refs_0_), channel_id=1, source_target_pairs={{0,2},{1,3},{2,0},{3,1},{4,6},{5,7},{6,4},{7,5},{8,10},{9,11},{10,... | collective-permute-start | bytes 835592 | tf_op jit(solution)/shard_map/ppermute | solution.py:23
  38.4 2.0 %shard_map.51 = bf16[2,64,768]{2,1,0:T(8,128)(2,1)S(1)} custom-call(bf16[768,2048]{1,0:T(8,128)(2,1)S(1)} %bitcast.17, bf16[768,2048]{1,0:T(8,128)(2,1)S(1)} %collective-permute-done.other, bf16[64,2176]{1,0:T(8,128)(2,1)S(1)} %collective-permute-done.7.refs_0_), custom_call_target="tpu_custom_call" | custom-call | flops 4026531840 | bytes 6750208 | tf_op jit(solution)/shard_map/pallas_call | solution.py:84
  40.4 2.9 %collective-permute-start.12 = (bf16[2,64,768]{2,1,0:T(8,128)(2,1)S(1)}, bf16[2,64,768]{2,1,0:T(8,128)(2,1)S(1)}, u32[]{:S(2)}, u32[]{:S(2)}) collective-permute-start(bf16[2,64,768]{2,1,0:T(8,128)(2,1)S(1)} %shard_map.51), channel_id=1, source_target_pairs={{0,12},{1,13},{2,14},{3,15},{4,8},{5,9},{6,10},{7,11},{8,4},{9,5},... | collective-permute-start | bytes 589832 | tf_op jit(solution)/shard_map/ppermute | solution.py:23
  43.3 0.0 collective-permute-done.6.refs_4_
  43.3 0.0 collective-permute-done.5.refs_0_
  43.3 0.5 collective-permute-start.11
  43.8 2.0 %shard_map.52 = bf16[2,64,768]{2,1,0:T(8,128)(2,1)S(1)} custom-call(bf16[768,2048]{1,0:T(8,128)(2,1)S(1)} %bitcast.18, bf16[768,2048]{1,0:T(8,128)(2,1)S(1)} %collective-permute-done.other, bf16[64,2176]{1,0:T(8,128)(2,1)S(1)} %collective-permute-done.5.refs_0_), custom_call_target="tpu_custom_call" | custom-call | flops 4026531840 | bytes 6750208 | tf_op jit(solution)/shard_map/pallas_call | solution.py:84
  45.9 0.0 copy-start.1
  45.9 0.1 collective-permute-start.14
  45.9 1.5 %collective-permute-start.8 = (bf16[2,64,768]{2,1,0:T(8,128)(2,1)S(1)}, bf16[2,64,768]{2,1,0:T(8,128)(2,1)S(1)}, u32[]{:S(2)}, u32[]{:S(2)}) collective-permute-start(bf16[2,64,768]{2,1,0:T(8,128)(2,1)S(1)} %get-tuple-element.33), channel_id=1, source_target_pairs={{0,2},{1,3},{2,0},{3,1},{4,6},{5,7},{6,4},{7,5},{8,10},{9,11},{10,... | collective-permute-start | bytes 589832 | tf_op jit(solution)/shard_map/ppermute | solution.py:23
  47.5 1.7 %collective-permute-done.12.refs_6_ = bf16[2,64,768]{2,1,0:T(8,128)(2,1)S(1)} collective-permute-done((bf16[2,64,768]{2,1,0:T(8,128)(2,1)S(1)}, bf16[2,64,768]{2,1,0:T(8,128)(2,1)S(1)}, u32[]{:S(2)}, u32[]{:S(2)}) %collective-permute-start.12) | collective-permute-done | bytes 196640 | tf_op jit(solution)/shard_map/ppermute | solution.py:23
  49.2 6.6 %collective-permute-start.9 = (bf16[2,64,768]{2,1,0:T(8,128)(2,1)S(1)}, bf16[2,64,768]{2,1,0:T(8,128)(2,1)S(1)}, u32[]{:S(2)}, u32[]{:S(2)}) collective-permute-start(bf16[2,64,768]{2,1,0:T(8,128)(2,1)S(1)} %get-tuple-element.34), channel_id=1, source_target_pairs={{0,4},{1,5},{2,6},{3,7},{4,0},{5,1},{6,2},{7,3},{8,12},{9,13},{10,... | collective-permute-start | bytes 589832 | tf_op jit(solution)/shard_map/ppermute | solution.py:23
  55.8 0.0 collective-permute-done.10.refs_0_
  55.8 0.0 collective-permute-done.11.refs_1_
  55.8 2.2 %shard_map.53 = (bf16[2,64,768]{2,1,0:T(8,128)(2,1)S(1)}, bf16[2,64,768]{2,1,0:T(8,128)(2,1)S(1)}) custom-call(bf16[768,2048]{1,0:T(8,128)(2,1)S(1)} %bitcast.19, bf16[768,2048]{1,0:T(8,128)(2,1)S(1)} %collective-permute-done.other, bf16[64,2176]{1,0:T(8,128)(2,1)S(1)} %collective-permute-done.10.refs_0_, bf16[64,2176]{1,0:T(8,128)(2,1)S(1)} %collective-permute-done.11.refs_1_), custom_call_target="tpu_custom_call" | custom-call | flops 8053063680 | bytes 7208960 | tf_op jit(solution)/shard_map/pallas_call | solution.py:84
  58.0 2.7 %collective-permute-start.13 = (bf16[2,64,768]{2,1,0:T(8,128)(2,1)S(1)}, bf16[2,64,768]{2,1,0:T(8,128)(2,1)S(1)}, u32[]{:S(2)}, u32[]{:S(2)}) collective-permute-start(bf16[2,64,768]{2,1,0:T(8,128)(2,1)S(1)} %get-tuple-element.39), channel_id=1, source_target_pairs={{0,6},{1,7},{2,4},{3,5},{4,2},{5,3},{6,0},{7,1},{8,14},{9,15},{10,... | collective-permute-start | bytes 589832 | tf_op jit(solution)/shard_map/ppermute | solution.py:23
  60.7 1.5 %collective-permute-start.15 = (bf16[2,64,768]{2,1,0:T(8,128)(2,1)S(1)}, bf16[2,64,768]{2,1,0:T(8,128)(2,1)S(1)}, u32[]{:S(2)}, u32[]{:S(2)}) collective-permute-start(bf16[2,64,768]{2,1,0:T(8,128)(2,1)S(1)} %get-tuple-element.42), channel_id=1, source_target_pairs={{0,14},{1,15},{2,12},{3,13},{4,10},{5,11},{6,8},{7,9},{8,6},{9,7},... | collective-permute-start | bytes 589832 | tf_op jit(solution)/shard_map/ppermute | solution.py:23
  62.2 0.0 collective-permute-done.14.refs_5_
  62.2 0.0 collective-permute-done.8.refs_1_
  62.2 0.0 collective-permute-done.9.refs_2_
  62.2 6.2 %collective-permute-done.13.refs_3_ = bf16[2,64,768]{2,1,0:T(8,128)(2,1)S(1)} collective-permute-done((bf16[2,64,768]{2,1,0:T(8,128)(2,1)S(1)}, bf16[2,64,768]{2,1,0:T(8,128)(2,1)S(1)}, u32[]{:S(2)}, u32[]{:S(2)}) %collective-permute-start.13) | collective-permute-done | bytes 196640 | tf_op jit(solution)/shard_map/ppermute | solution.py:23
  68.4 2.5 %collective-permute-done.15.refs_7_ = bf16[2,64,768]{2,1,0:T(8,128)(2,1)S(1)} collective-permute-done((bf16[2,64,768]{2,1,0:T(8,128)(2,1)S(1)}, bf16[2,64,768]{2,1,0:T(8,128)(2,1)S(1)}, u32[]{:S(2)}, u32[]{:S(2)}) %collective-permute-start.15) | collective-permute-done | bytes 196640 | tf_op jit(solution)/shard_map/ppermute | solution.py:23
  70.9 0.0 copy-done.1
  70.9 1.3 %shard_map.54 = bf16[512,768]{1,0:T(8,128)(2,1)} custom-call(s32[8,64]{1,0:T(8,128)S(1)} %bitcast.11, bf16[2,64,768]{2,1,0:T(8,128)(2,1)S(1)} %shard_map.48.refs_0_, bf16[2,64,768]{2,1,0:T(8,128)(2,1)S(1)} %collective-permute-done.8.refs_1_, bf16[2,64,768]{2,1,0:T(8,128)(2,1)S(1)} %collective-permute-done.9.refs_2_, ...), custom_call_target="tpu_custom_call" | custom-call | tf_op jit(solution)/shard_map/pallas_call | solution.py:119
  (1 shorter events, 0.0 us)
Async XLA Ops:
  0.0 16.1 %collective-permute-start = (bf16[768,2048]{1,0:T(8,128)(2,1)}, bf16[768,2048]{1,0:T(8,128)(2,1)S(1)}, u32[]{:S(2)}, u32[]{:S(2)}) collective-permute-start(bf16[768,2048]{1,0:T(8,128)(2,1)} %bitcast.13), channel_id=1, source_target_pairs={{0,1},{1,0},{2,3},{3,2},{4,5},{5,4},{6,7},{7,6},{8,9},{9,8},{10,11... | collective-permute-start | bytes 9437192 | tf_op jit(solution)/shard_map/ppermute | solution.py:23
  0.5 9.7 %collective-permute-start.1 = (bf16[1,64,2048]{2,1,0:T(8,128)(2,1)}, bf16[1,64,2048]{2,1,0:T(8,128)(2,1)S(1)}, u32[]{:S(2)}, u32[]{:S(2)}) collective-permute-start(bf16[1,64,2048]{2,1,0:T(8,128)(2,1)} %param.4), channel_id=1, source_target_pairs={{16,0},{0,16},{17,1},{1,17},{18,2},{2,18},{19,3},{3,19},{20,4},{4,... | collective-permute-start | bytes 786440 | tf_op jit(solution)/shard_map/ppermute | solution.py:18
  3.0 0.7 copy-start
  3.7 0.7 copy-start.2
  10.2 15.5 %collective-permute-start.2 = (bf16[64,2176]{1,0:T(8,128)(2,1)S(1)}, bf16[64,2176]{1,0:T(8,128)(2,1)S(1)}, u32[]{:S(2)}, u32[]{:S(2)}) collective-permute-start(bf16[64,2176]{1,0:T(8,128)(2,1)S(1)} %shard_map.47.refs_0_), channel_id=1, source_target_pairs={{0,8},{1,9},{2,10},{3,11},{4,12},{5,13},{6,14},{7,15},{8,0},{9,1},... | collective-permute-start | bytes 835592 | tf_op jit(solution)/shard_map/ppermute | solution.py:23
  13.1 18.7 %collective-permute-start.3 = (bf16[64,2176]{1,0:T(8,128)(2,1)S(1)}, bf16[64,2176]{1,0:T(8,128)(2,1)S(1)}, u32[]{:S(2)}, u32[]{:S(2)}) collective-permute-start(bf16[64,2176]{1,0:T(8,128)(2,1)S(1)} %shard_map.47.refs_0_), channel_id=1, source_target_pairs={{0,4},{1,5},{2,6},{3,7},{4,0},{5,1},{6,2},{7,3},{8,12},{9,13},{10,... | collective-permute-start | bytes 835592 | tf_op jit(solution)/shard_map/ppermute | solution.py:23
  14.6 17.1 %collective-permute-start.4 = (bf16[64,2176]{1,0:T(8,128)(2,1)S(1)}, bf16[64,2176]{1,0:T(8,128)(2,1)S(1)}, u32[]{:S(2)}, u32[]{:S(2)}) collective-permute-start(bf16[64,2176]{1,0:T(8,128)(2,1)S(1)} %shard_map.47.refs_0_), channel_id=1, source_target_pairs={{0,2},{1,3},{2,0},{3,1},{4,6},{5,7},{6,4},{7,5},{8,10},{9,11},{10,... | collective-permute-start | bytes 835592 | tf_op jit(solution)/shard_map/ppermute | solution.py:23
  16.1 1.9 %copy-start.3 = (bf16[1,1,768,2048]{3,2,1,0:T(8,128)(2,1)S(1)}, bf16[1,1,768,2048]{3,2,1,0:T(8,128)(2,1)}, u32[]{:S(2)}) copy-start(bf16[1,1,768,2048]{3,2,1,0:T(8,128)(2,1)} %param.7) | copy-start | bytes 9437188
  25.7 11.2 %collective-permute-start.7 = (bf16[64,2176]{1,0:T(8,128)(2,1)S(1)}, bf16[64,2176]{1,0:T(8,128)(2,1)S(1)}, u32[]{:S(2)}, u32[]{:S(2)}) collective-permute-start(bf16[64,2176]{1,0:T(8,128)(2,1)S(1)} %collective-permute-done.2.refs_0_), channel_id=1, source_target_pairs={{0,4},{1,5},{2,6},{3,7},{4,0},{5,1},{6,2},{7,3},{8,12},{9,13},{10,... | collective-permute-start | bytes 835592 | tf_op jit(solution)/shard_map/ppermute | solution.py:23
  28.3 15.0 %collective-permute-start.6 = (bf16[2,64,768]{2,1,0:T(8,128)(2,1)S(1)}, bf16[2,64,768]{2,1,0:T(8,128)(2,1)S(1)}, u32[]{:S(2)}, u32[]{:S(2)}) collective-permute-start(bf16[2,64,768]{2,1,0:T(8,128)(2,1)S(1)} %shard_map.49), channel_id=1, source_target_pairs={{0,8},{1,9},{2,10},{3,11},{4,12},{5,13},{6,14},{7,15},{8,0},{9,1},... | collective-permute-start | bytes 589832 | tf_op jit(solution)/shard_map/ppermute | solution.py:23
  31.8 11.5 %collective-permute-start.5 = (bf16[64,2176]{1,0:T(8,128)(2,1)S(1)}, bf16[64,2176]{1,0:T(8,128)(2,1)S(1)}, u32[]{:S(2)}, u32[]{:S(2)}) collective-permute-start(bf16[64,2176]{1,0:T(8,128)(2,1)S(1)} %collective-permute-done.2.refs_0_), channel_id=1, source_target_pairs={{0,2},{1,3},{2,0},{3,1},{4,6},{5,7},{6,4},{7,5},{8,10},{9,11},{10,... | collective-permute-start | bytes 835592 | tf_op jit(solution)/shard_map/ppermute | solution.py:23
  36.9 18.8 %collective-permute-start.10 = (bf16[64,2176]{1,0:T(8,128)(2,1)S(1)}, bf16[64,2176]{1,0:T(8,128)(2,1)S(1)}, u32[]{:S(2)}, u32[]{:S(2)}) collective-permute-start(bf16[64,2176]{1,0:T(8,128)(2,1)S(1)} %collective-permute-done.7.refs_0_), channel_id=1, source_target_pairs={{0,2},{1,3},{2,0},{3,1},{4,6},{5,7},{6,4},{7,5},{8,10},{9,11},{10,... | collective-permute-start | bytes 835592 | tf_op jit(solution)/shard_map/ppermute | solution.py:23
  40.4 8.8 %collective-permute-start.12 = (bf16[2,64,768]{2,1,0:T(8,128)(2,1)S(1)}, bf16[2,64,768]{2,1,0:T(8,128)(2,1)S(1)}, u32[]{:S(2)}, u32[]{:S(2)}) collective-permute-start(bf16[2,64,768]{2,1,0:T(8,128)(2,1)S(1)} %shard_map.51), channel_id=1, source_target_pairs={{0,12},{1,13},{2,14},{3,15},{4,8},{5,9},{6,10},{7,11},{8,4},{9,5},... | collective-permute-start | bytes 589832 | tf_op jit(solution)/shard_map/ppermute | solution.py:23
  43.3 12.5 %collective-permute-start.11 = (bf16[64,2176]{1,0:T(8,128)(2,1)S(1)}, bf16[64,2176]{1,0:T(8,128)(2,1)S(1)}, u32[]{:S(2)}, u32[]{:S(2)}) collective-permute-start(bf16[64,2176]{1,0:T(8,128)(2,1)S(1)} %collective-permute-done.3.refs_1_), channel_id=1, source_target_pairs={{0,2},{1,3},{2,0},{3,1},{4,6},{5,7},{6,4},{7,5},{8,10},{9,11},{10,... | collective-permute-start | bytes 835592 | tf_op jit(solution)/shard_map/ppermute | solution.py:23
  45.9 25.0 %copy-start.1 = (s32[1,64,8]{1,2,0:T(8,128)S(1)}, s32[1,64,8]{1,2,0:T(8,128)}, u32[]{:S(2)}) copy-start(s32[1,64,8]{1,2,0:T(8,128)} %param.5) | copy-start | bytes 6148
  45.9 16.3 %collective-permute-start.14 = (bf16[2,64,768]{2,1,0:T(8,128)(2,1)S(1)}, bf16[2,64,768]{2,1,0:T(8,128)(2,1)S(1)}, u32[]{:S(2)}, u32[]{:S(2)}) collective-permute-start(bf16[2,64,768]{2,1,0:T(8,128)(2,1)S(1)} %shard_map.52), channel_id=1, source_target_pairs={{0,10},{1,11},{2,8},{3,9},{4,14},{5,15},{6,12},{7,13},{8,2},{9,3},... | collective-permute-start | bytes 589832 | tf_op jit(solution)/shard_map/ppermute | solution.py:23
  45.9 16.2 %collective-permute-start.8 = (bf16[2,64,768]{2,1,0:T(8,128)(2,1)S(1)}, bf16[2,64,768]{2,1,0:T(8,128)(2,1)S(1)}, u32[]{:S(2)}, u32[]{:S(2)}) collective-permute-start(bf16[2,64,768]{2,1,0:T(8,128)(2,1)S(1)} %get-tuple-element.33), channel_id=1, source_target_pairs={{0,2},{1,3},{2,0},{3,1},{4,6},{5,7},{6,4},{7,5},{8,10},{9,11},{10,... | collective-permute-start | bytes 589832 | tf_op jit(solution)/shard_map/ppermute | solution.py:23
  49.2 13.0 %collective-permute-start.9 = (bf16[2,64,768]{2,1,0:T(8,128)(2,1)S(1)}, bf16[2,64,768]{2,1,0:T(8,128)(2,1)S(1)}, u32[]{:S(2)}, u32[]{:S(2)}) collective-permute-start(bf16[2,64,768]{2,1,0:T(8,128)(2,1)S(1)} %get-tuple-element.34), channel_id=1, source_target_pairs={{0,4},{1,5},{2,6},{3,7},{4,0},{5,1},{6,2},{7,3},{8,12},{9,13},{10,... | collective-permute-start | bytes 589832 | tf_op jit(solution)/shard_map/ppermute | solution.py:23
  58.0 10.4 %collective-permute-start.13 = (bf16[2,64,768]{2,1,0:T(8,128)(2,1)S(1)}, bf16[2,64,768]{2,1,0:T(8,128)(2,1)S(1)}, u32[]{:S(2)}, u32[]{:S(2)}) collective-permute-start(bf16[2,64,768]{2,1,0:T(8,128)(2,1)S(1)} %get-tuple-element.39), channel_id=1, source_target_pairs={{0,6},{1,7},{2,4},{3,5},{4,2},{5,3},{6,0},{7,1},{8,14},{9,15},{10,... | collective-permute-start | bytes 589832 | tf_op jit(solution)/shard_map/ppermute | solution.py:23
  60.7 10.2 %collective-permute-start.15 = (bf16[2,64,768]{2,1,0:T(8,128)(2,1)S(1)}, bf16[2,64,768]{2,1,0:T(8,128)(2,1)S(1)}, u32[]{:S(2)}, u32[]{:S(2)}) collective-permute-start(bf16[2,64,768]{2,1,0:T(8,128)(2,1)S(1)} %get-tuple-element.42), channel_id=1, source_target_pairs={{0,14},{1,15},{2,12},{3,13},{4,10},{5,11},{6,8},{7,9},{8,6},{9,7},... | collective-permute-start | bytes 589832 | tf_op jit(solution)/shard_map/ppermute | solution.py:23

commit v11 on v10

--- a/solution.py
+++ b/solution.py
@@ -23,7 +23,17 @@
     return lax.ppermute(block, "expert", route)
 
 
-def gates_kernel(ids, gates, out):
+def send_across(block, owners, flip):
+    sections = lax.axis_size("pipe")
+    route = []
+    for s in range(sections):
+        for i in range(owners):
+            target = ((i // CORES) ^ flip) * CORES + i % CORES
+            route.append((s * owners + i, (s - 1) % sections * owners + target))
+    return lax.ppermute(block, ("pipe", "expert"), route)
+
+
+def gates_kernel(ids, gates, weight, out):
     top, tokens = ids.shape
     expert = lax.broadcasted_iota(jnp.int32, (LANES, tokens), 0)
     total = jnp.zeros((LANES, tokens), jnp.float32)
@@ -33,12 +43,12 @@
     out[...] = total.T.astype(jnp.bfloat16)
 
 
-def gate_columns(ids, gates):
+def gate_columns(ids, gates, weight):
     return pl.pallas_call(
         gates_kernel,
         out_shape=jax.ShapeDtypeStruct((ids.shape[1], LANES), jnp.bfloat16),
         compiler_params=pltpu.CompilerParams(vmem_limit_bytes=16 << 20),
-    )(ids, gates)
+    )(ids, gates, weight)
 
 
 def widen_kernel(rows, columns, out):
@@ -56,41 +66,46 @@
     )(rows, columns)
 
 
-def products_kernel(count, weight, other, *refs):
-    rows, outs = refs[:count], refs[count:]
+def products_kernel(paired, weight, other, *refs):
     hidden, depth = weight.shape
+    rows, gates, at = [], [], 0
+    for pair in paired:
+        rows.append(refs[at][:, :depth])
+        gates.append(refs[at + 1][...] if pair else refs[at][:, depth:])
+        at += 1 + pair
+    outs = refs[at:]
     tokens = outs[0].shape[1]
     me = lax.axis_index("expert")
     core = lax.rem(me, CORES)
-    stacked = jnp.concatenate([r[...] for r in rows], axis=0)
-    gates = stacked[:, depth:].astype(jnp.float32)
+    stacked = jnp.concatenate(rows, axis=0)
+    gates = jnp.concatenate(gates, axis=0).astype(jnp.float32)
     column = lax.broadcasted_iota(jnp.int32, gates.shape, 1)
     for mat, to in ((weight, core), (other, 1 - core)):
         scale = jnp.sum(jnp.where(column == me - core + to, gates, 0.0), axis=1, keepdims=True)
         product = lax.dot_general(
-            stacked[:, :depth],
-            mat[...],
-            (((1,), (1,)), ((), ())),
-            preferred_element_type=jnp.float32,
+            stacked, mat[...], (((1,), (1,)), ((), ())), preferred_element_type=jnp.float32
         )
         scaled = (product * scale).astype(jnp.bfloat16)
         for j, out in enumerate(outs):
             out[to] = scaled[j * tokens : (j + 1) * tokens]
 
 
-def products(pieces, tokens, weight, other):
+def products(pieces, weight, other):
     hidden, depth = weight.shape
-    total = sum(p.shape[0] for p in pieces)
-    return pl.pallas_call(
-        functools.partial(products_kernel, len(pieces)),
-        out_shape=[jax.ShapeDtypeStruct((CORES, tokens, hidden), jnp.bfloat16)] * (total // tokens),
+    paired = [isinstance(p, tuple) for p in pieces]
+    operands = [x for p in pieces for x in (p if isinstance(p, tuple) else (p,))]
+    tokens = operands[0].shape[0]
+    total = len(pieces) * tokens
+    return pl.pallas_call(
+        functools.partial(products_kernel, paired),
+        out_shape=[jax.ShapeDtypeStruct((CORES, tokens, hidden), jnp.bfloat16)] * len(pieces),
         compiler_params=pltpu.CompilerParams(vmem_limit_bytes=16 << 20),
         cost_estimate=pl.CostEstimate(
             flops=20 * CORES * total * hidden * depth,
             bytes_accessed=2 * (total * (2 * hidden + depth) + 2 * hidden * depth),
             transcendentals=0,
         ),
-    )(weight, other, *pieces)
+    )(weight, other, *operands)
 
 
 def pick_kernel(ids, *refs):
@@ -123,45 +138,52 @@
     )(ids, *blocks)
 
 
-def dense_device(section_grad, route_ids, route_gates, weight_mat):
+def dense_device(upstream, route_ids, route_gates, weight_mat):
     tokens, top = route_ids.shape
     owners = lax.axis_size("expert")
+    tie = lax.optimization_barrier
+
+    def work(*pieces):
+        return products(list(pieces), weight_mat, other_mat)
+
+    rows = send_across(upstream, owners, 0)
+    far = send_across(upstream, owners, Z_FAR)
+    near_side = send_across(upstream, owners, X ^ Z_NEAR)
     other_mat = send(weight_mat, owners, 0, 1)
-    section_grad, columns = lax.optimization_barrier(
-        (section_grad, gate_columns(route_ids.T, route_gates.T))
-    )
-    rows = widened(section_grad, columns)
-
-    def work(*pieces):
-        return products(list(pieces), tokens, weight_mat, other_mat)
-
-    tie = lax.optimization_barrier
-    far = send(rows, owners, Z_FAR)
+    columns = gate_columns(route_ids.T, route_gates.T, weight_mat)
+    far_columns = send(columns, owners, Z_FAR)
+    near_side_columns = send(columns, owners, X ^ Z_NEAR)
+    rows, columns, other_mat = tie((rows, columns, other_mat))
+    rows = widened(rows, columns)
     near = send(rows, owners, Z_NEAR)
     side = send(rows, owners, X)
-    (out_own,) = work(rows)
-    far, _ = tie((far, out_own))
+    far, far_columns, rows = tie((far, far_columns, rows))
+    far = widened(far, far_columns)
     cross = send(far, owners, Z_NEAR)
     (out_far,) = work(far)
     back_far = send(out_far, owners, Z_FAR)
-    near, side, _ = tie((near, side, out_far))
-    far_side = send(tie((far, near))[0], owners, X)
-    out_side, out_near = work(side, near)
-    cross, near, _ = tie((cross, near, out_side))
+    near, side, near_side, near_side_columns, _ = tie(
+        (near, side, near_side, near_side_columns, out_far)
+    )
+    far_side = send(tie((far, out_far))[0], owners, X)
+    out_side, out_near, out_near_side = work(side, near, (near_side, near_side_columns))
+    cross, _ = tie((cross, out_side))
     cross_side = send(cross, owners, X)
-    near_side = send(near, owners, X)
     (out_cross,) = work(cross)
     back_cross = send(out_cross, owners, Z_NEAR ^ Z_FAR)
-    far_side, back_far, out_side, out_near, _ = tie(
-        (far_side, back_far, out_side, out_near, out_cross)
-    )
+    far_side, back_far, out_side, out_near, out_near_side, _ = tie(
+        (far_side, back_far, out_side, out_near, out_near_side, out_cross)
+    )
+    back_side = send(out_side, owners, X)
+    back_near = send(out_near, owners, Z_NEAR)
     (out_far_side,) = work(far_side)
     back_far_side = send(out_far_side, owners, X ^ Z_FAR)
-    cross_side, near_side, back_cross, _ = tie((cross_side, near_side, back_cross, out_far_side))
-    (out_cross_side, out_near_side) = work(cross_side, near_side)
+    cross_side, back_side, _ = tie((cross_side, back_side, out_far_side))
+    (out_cross_side,) = work(cross_side)
+    back_cross_side = send(out_cross_side, owners, X ^ Z_NEAR ^ Z_FAR)
     back_near_side = send(out_near_side, owners, X ^ Z_NEAR)
-    back_side = send(out_side, owners, X)
-    back_near = send(out_near, owners, Z_NEAR)
+    rows, _ = tie((rows, out_cross_side))
+    (out_own,) = work(rows)
     received = {
         0: out_own,
         X: back_side,
@@ -170,7 +192,7 @@
         Z_FAR: back_far,
         X ^ Z_FAR: back_far_side,
         Z_NEAR ^ Z_FAR: back_cross,
-        X ^ Z_NEAR ^ Z_FAR: send(out_cross_side, owners, X ^ Z_NEAR ^ Z_FAR),
+        X ^ Z_NEAR ^ Z_FAR: back_cross_side,
     }
     out = pick_routes(route_ids.T, [received[flip] for flip in sorted(received)])
     return out.reshape(1, tokens, top, weight_mat.shape[0])
@@ -219,7 +241,6 @@
 
 
 def per_device(upstream, expert_ids, gate_weights, expert_weight):
-    section_grad = shifted(upstream, "pipe", -1)[0]
     route_ids = expert_ids[0]
     route_gates = gate_weights[0]
     weight_mat = expert_weight[0, 0]
@@ -227,7 +248,8 @@
     owners = lax.axis_size("expert")
     capacity = 2 * tokens * top // owners
     if capacity >= tokens and owners == CORES * 2 * Z_FAR:
-        return dense_device(section_grad, route_ids, route_gates, weight_mat)
+        return dense_device(upstream[0], route_ids, route_gates, weight_mat)
+    section_grad = shifted(upstream, "pipe", -1)[0]
     return slotted_device(section_grad, route_ids, route_gates, weight_mat, capacity)
 
 

time: 72.4 us -> 71.6 us (0.989)
  waiting for transfers between devices: 23.2 us -> 20.8 us
  starting transfers between devices: 31.8 us -> 33.5 us
    ppermute x1 -> x3, starting transfers between devices: 2.52 us -> 12.7 us  [send_across(): return lax.ppermute(block, ('pipe', 'expert'), route)]
    ppermute x15, starting transfers between devices: 29.2 us -> 20.7 us  [send(): return lax.ppermute(block, 'expert', route)]
    ppermute x1 -> x3, waiting for transfers between devices: 5.71 us -> 0.26 us  [send_across(): return lax.ppermute(block, ('pipe', 'expert'), route)]
    ppermute x15, waiting for transfers between devices: 17.5 us -> 20.6 us  [send(): return lax.ppermute(block, 'expert', route)]
  transfers between devices with their start and end apart: 16 -> 18, of which waited for: 6 -> 6; matrix products, arithmetic and copies ran while one was open for 0% -> 0% of each run, Pallas kernels for 17% -> 17%
where the time goes in v11:
time: 71.6 us; the launch traced here: 71.4 us
  starting transfers between devices  33.5 us (47%)
  waiting for transfers between devices  20.8 us (29%)
  Pallas kernels  13.8 us (19%)
  local copies, waits for them, and re-layouts  3.26 us (5%)
    ppermute x15, starting transfers between devices, send(): return lax.ppermute(block, 'expert', route)  20.7 us
    ppermute x15, waiting for transfers between devices, send(): return lax.ppermute(block, 'expert', route)  20.6 us
    ppermute x3, starting transfers between devices, send_across(): return lax.ppermute(block, ('pipe', 'expert'), route)  12.7 us
    pallas_call x6, Pallas kernels, products(): pl.pallas_call(functools.partial(products_kernel, paired), out_shape=[jax...  12.3 us
    unnamed x8, local copies, waits for them, and re-layouts  3.26 us
  transfers between devices with their start and end apart: 18, of which 6 were waited for; matrix products, arithmetic and copies ran while one was open for 0% of the time, Pallas kernels for 17%

profile of v11, /device:TPU:0, one launch (start us, length us, event | category | flops | bytes accessed | tf_op | source)
XLA Modules:
  0.0 71.4 jit_solution(8593092875226484425)
XLA Ops:
  0.0 0.5 collective-permute-start.1
  0.5 2.5 %collective-permute-start = (bf16[64,2048]{1,0:T(8,128)(2,1)}, bf16[64,2048]{1,0:T(8,128)(2,1)S(1)}, u32[]{:S(2)}, u32[]{:S(2)}) collective-permute-start(bf16[64,2048]{1,0:T(8,128)(2,1)} %bitcast.20), channel_id=1, source_target_pairs={{0,16},{1,17},{2,18},{3,19},{4,20},{5,21},{6,22},{7,23},{8,24},{9,... | collective-permute-start | bytes 786440 | tf_op jit(solution)/shard_map/ppermute | solution.py:33
  3.0 2.5 %collective-permute-start.2 = (bf16[64,2048]{1,0:T(8,128)(2,1)}, bf16[64,2048]{1,0:T(8,128)(2,1)S(1)}, u32[]{:S(2)}, u32[]{:S(2)}) collective-permute-start(bf16[64,2048]{1,0:T(8,128)(2,1)} %bitcast.21), channel_id=1, source_target_pairs={{0,24},{1,25},{2,26},{3,27},{4,28},{5,29},{6,30},{7,31},{8,16},{9,... | collective-permute-start | bytes 786440 | tf_op jit(solution)/shard_map/ppermute | solution.py:33
  5.5 0.0 copy-start
  5.5 1.9 %copy-done = bf16[1,1,768,2048]{3,2,1,0:T(8,128)(2,1)S(1)} copy-done((bf16[1,1,768,2048]{3,2,1,0:T(8,128)(2,1)S(1)}, bf16[1,1,768,2048]{3,2,1,0:T(8,128)(2,1)}, u32[]{:S(2)}) %copy-start) | copy-done | bytes 3145752
  7.4 0.0 copy-start.2
  7.4 0.7 copy-done.2
  8.1 0.0 copy-start.3
  8.1 0.7 copy-done.3
  8.8 0.0 copy-start.1
  8.8 0.1 shard_map.46.columns
  8.9 0.1 collective-permute-start.3
  9.0 2.8 %collective-permute-start.8 = (bf16[64,128]{1,0:T(8,128)(2,1)S(1)}, bf16[64,128]{1,0:T(8,128)(2,1)S(1)}, u32[]{:S(2)}, u32[]{:S(2)}) collective-permute-start(bf16[64,128]{1,0:T(8,128)(2,1)S(1)} %shard_map.46.columns), channel_id=1, source_target_pairs={{0,6},{1,7},{2,4},{3,5},{4,2},{5,3},{6,0},{7,1},{8,14},{9,15},{10,... | collective-permute-start | bytes 49160 | tf_op jit(solution)/shard_map/ppermute | solution.py:23
  11.8 0.0 collective-permute-done.rows
  11.8 7.7 %collective-permute-start.7 = (bf16[64,2048]{1,0:T(8,128)(2,1)}, bf16[64,2048]{1,0:T(8,128)(2,1)S(1)}, u32[]{:S(2)}, u32[]{:S(2)}) collective-permute-start(bf16[64,2048]{1,0:T(8,128)(2,1)} %bitcast.22), channel_id=1, source_target_pairs={{0,22},{1,23},{2,20},{3,21},{4,18},{5,19},{6,16},{7,17},{8,30},{9,... | collective-permute-start | bytes 786440 | tf_op jit(solution)/shard_map/ppermute | solution.py:33
  19.5 0.0 collective-permute-done.1.other
  19.5 0.1 collective-permute-start.5
  19.6 0.0 collective-permute-done.3.columns
  19.6 0.8 %collective-permute-start.6 = (bf16[64,2176]{1,0:T(8,128)(2,1)S(1)}, bf16[64,2176]{1,0:T(8,128)(2,1)S(1)}, u32[]{:S(2)}, u32[]{:S(2)}) collective-permute-start(bf16[64,2176]{1,0:T(8,128)(2,1)S(1)} %shard_map.47.refs_0_), channel_id=1, source_target_pairs={{0,2},{1,3},{2,0},{3,1},{4,6},{5,7},{6,4},{7,5},{8,10},{9,11},{10,... | collective-permute-start | bytes 835592 | tf_op jit(solution)/shard_map/ppermute | solution.py:23
  20.4 0.0 collective-permute-done.2.rows
  20.4 1.8 %collective-permute-start.4 = (bf16[64,2176]{1,0:T(8,128)(2,1)S(1)}, bf16[64,2176]{1,0:T(8,128)(2,1)S(1)}, u32[]{:S(2)}, u32[]{:S(2)}) collective-permute-start(bf16[64,2176]{1,0:T(8,128)(2,1)S(1)} %shard_map.48.refs_0_), channel_id=1, source_target_pairs={{0,4},{1,5},{2,6},{3,7},{4,0},{5,1},{6,2},{7,3},{8,12},{9,13},{10,... | collective-permute-start | bytes 835592 | tf_op jit(solution)/shard_map/ppermute | solution.py:23
  22.2 0.0 copy-done.1
  22.2 2.0 %shard_map.49 = bf16[2,64,768]{2,1,0:T(8,128)(2,1)S(1)} custom-call(bf16[768,2048]{1,0:T(8,128)(2,1)S(1)} %bitcast.11, bf16[768,2048]{1,0:T(8,128)(2,1)S(1)} %collective-permute-done.1.other, bf16[64,2176]{1,0:T(8,128)(2,1)S(1)} %shard_map.48.refs_0_), custom_call_target="tpu_custom_call" | custom-call | flops 4026531840 | bytes 6750208 | tf_op jit(solution)/shard_map/pallas_call | solution.py:99
  24.2 0.0 collective-permute-done.8.refs_3_
  24.2 2.4 %collective-permute-start.11 = (bf16[2,64,768]{2,1,0:T(8,128)(2,1)S(1)}, bf16[2,64,768]{2,1,0:T(8,128)(2,1)S(1)}, u32[]{:S(2)}, u32[]{:S(2)}) collective-permute-start(bf16[2,64,768]{2,1,0:T(8,128)(2,1)S(1)} %shard_map.49), channel_id=1, source_target_pairs={{0,8},{1,9},{2,10},{3,11},{4,12},{5,13},{6,14},{7,15},{8,0},{9,1},... | collective-permute-start | bytes 589832 | tf_op jit(solution)/shard_map/ppermute | solution.py:23
  26.6 0.3 collective-permute-done.7.refs_2_
  26.9 0.5 collective-permute-start.10
  27.4 7.8 %collective-permute-done.5.refs_1_ = bf16[64,2176]{1,0:T(8,128)(2,1)S(1)} collective-permute-done((bf16[64,2176]{1,0:T(8,128)(2,1)S(1)}, bf16[64,2176]{1,0:T(8,128)(2,1)S(1)}, u32[]{:S(2)}, u32[]{:S(2)}) %collective-permute-start.5) | collective-permute-done | bytes 278560 | tf_op jit(solution)/shard_map/ppermute | solution.py:23
  35.2 0.0 collective-permute-done.6.refs_0_
  35.2 2.2 %shard_map.50 = (bf16[2,64,768]{2,1,0:T(8,128)(2,1)S(1)}, bf16[2,64,768]{2,1,0:T(8,128)(2,1)S(1)}, bf16[2,64,768]{2,1,0:T(8,128)(2,1)S(1)}) custom-call(bf16[768,2048]{1,0:T(8,128)(2,1)S(1)} %bitcast.12, bf16[768,2048]{1,0:T(8,128)(2,1)S(1)} %collective-permute-done.1.other, bf16[64,2176]{1,0:T(8,128)(2,1)S(1)} %collective-permute-done.6.refs_0_, ...), custom_call_target="tpu_custom_call" | custom-call | flops 12079595520 | bytes 7667712 | tf_op jit(solution)/shard_map/pallas_call | solution.py:99
  37.4 3.3 %collective-permute-done.4.refs_0_ = bf16[64,2176]{1,0:T(8,128)(2,1)S(1)} collective-permute-done((bf16[64,2176]{1,0:T(8,128)(2,1)S(1)}, bf16[64,2176]{1,0:T(8,128)(2,1)S(1)}, u32[]{:S(2)}, u32[]{:S(2)}) %collective-permute-start.4) | collective-permute-done | bytes 278560 | tf_op jit(solution)/shard_map/ppermute | solution.py:23
  40.6 1.5 %collective-permute-start.9 = (bf16[64,2176]{1,0:T(8,128)(2,1)S(1)}, bf16[64,2176]{1,0:T(8,128)(2,1)S(1)}, u32[]{:S(2)}, u32[]{:S(2)}) collective-permute-start(bf16[64,2176]{1,0:T(8,128)(2,1)S(1)} %collective-permute-done.4.refs_0_), channel_id=1, source_target_pairs={{0,2},{1,3},{2,0},{3,1},{4,6},{5,7},{6,4},{7,5},{8,10},{9,11},{10,... | collective-permute-start | bytes 835592 | tf_op jit(solution)/shard_map/ppermute | solution.py:23
  42.1 2.0 %shard_map.51 = bf16[2,64,768]{2,1,0:T(8,128)(2,1)S(1)} custom-call(bf16[768,2048]{1,0:T(8,128)(2,1)S(1)} %bitcast.13, bf16[768,2048]{1,0:T(8,128)(2,1)S(1)} %collective-permute-done.1.other, bf16[64,2176]{1,0:T(8,128)(2,1)S(1)} %collective-permute-done.4.refs_0_), custom_call_target="tpu_custom_call" | custom-call | flops 4026531840 | bytes 6750208 | tf_op jit(solution)/shard_map/pallas_call | solution.py:99
  44.1 3.6 %collective-permute-start.16 = (bf16[2,64,768]{2,1,0:T(8,128)(2,1)S(1)}, bf16[2,64,768]{2,1,0:T(8,128)(2,1)S(1)}, u32[]{:S(2)}, u32[]{:S(2)}) collective-permute-start(bf16[2,64,768]{2,1,0:T(8,128)(2,1)S(1)} %shard_map.51), channel_id=1, source_target_pairs={{0,12},{1,13},{2,14},{3,15},{4,8},{5,9},{6,10},{7,11},{8,4},{9,5},... | collective-permute-start | bytes 589832 | tf_op jit(solution)/shard_map/ppermute | solution.py:23
  47.7 0.0 collective-permute-done.11.refs_4_
  47.7 0.0 collective-permute-done.10.refs_0_
  47.7 0.7 collective-permute-start.12
  48.4 2.0 %shard_map.52 = bf16[2,64,768]{2,1,0:T(8,128)(2,1)S(1)} custom-call(bf16[768,2048]{1,0:T(8,128)(2,1)S(1)} %bitcast.14, bf16[768,2048]{1,0:T(8,128)(2,1)S(1)} %collective-permute-done.1.other, bf16[64,2176]{1,0:T(8,128)(2,1)S(1)} %collective-permute-done.10.refs_0_), custom_call_target="tpu_custom_call" | custom-call | flops 4026531840 | bytes 6750208 | tf_op jit(solution)/shard_map/pallas_call | solution.py:99
  50.4 0.1 collective-permute-start.15
  50.5 1.7 %collective-permute-start.13 = (bf16[2,64,768]{2,1,0:T(8,128)(2,1)S(1)}, bf16[2,64,768]{2,1,0:T(8,128)(2,1)S(1)}, u32[]{:S(2)}, u32[]{:S(2)}) collective-permute-start(bf16[2,64,768]{2,1,0:T(8,128)(2,1)S(1)} %get-tuple-element.48), channel_id=1, source_target_pairs={{0,4},{1,5},{2,6},{3,7},{4,0},{5,1},{6,2},{7,3},{8,12},{9,13},{10,... | collective-permute-start | bytes 589832 | tf_op jit(solution)/shard_map/ppermute | solution.py:23
  52.2 1.9 %collective-permute-done.12.refs_1_ = bf16[2,64,768]{2,1,0:T(8,128)(2,1)S(1)} collective-permute-done((bf16[2,64,768]{2,1,0:T(8,128)(2,1)S(1)}, bf16[2,64,768]{2,1,0:T(8,128)(2,1)S(1)}, u32[]{:S(2)}, u32[]{:S(2)}) %collective-permute-start.12) | collective-permute-done | bytes 196640 | tf_op jit(solution)/shard_map/ppermute | solution.py:23
  54.0 0.0 collective-permute-start.14
  54.0 0.0 collective-permute-done.9.refs_0_
  54.0 2.0 %shard_map.53 = bf16[2,64,768]{2,1,0:T(8,128)(2,1)S(1)} custom-call(bf16[768,2048]{1,0:T(8,128)(2,1)S(1)} %bitcast.15, bf16[768,2048]{1,0:T(8,128)(2,1)S(1)} %collective-permute-done.1.other, bf16[64,2176]{1,0:T(8,128)(2,1)S(1)} %collective-permute-done.9.refs_0_), custom_call_target="tpu_custom_call" | custom-call | flops 4026531840 | bytes 6750208 | tf_op jit(solution)/shard_map/pallas_call | solution.py:99
  56.0 4.3 %collective-permute-start.17 = (bf16[2,64,768]{2,1,0:T(8,128)(2,1)S(1)}, bf16[2,64,768]{2,1,0:T(8,128)(2,1)S(1)}, u32[]{:S(2)}, u32[]{:S(2)}) collective-permute-start(bf16[2,64,768]{2,1,0:T(8,128)(2,1)S(1)} %shard_map.53), channel_id=1, source_target_pairs={{0,14},{1,15},{2,12},{3,13},{4,10},{5,11},{6,8},{7,9},{8,6},{9,7},... | collective-permute-start | bytes 589832 | tf_op jit(solution)/shard_map/ppermute | solution.py:23
  60.4 2.0 %shard_map.54.refs_0_ = bf16[2,64,768]{2,1,0:T(8,128)(2,1)S(1)} custom-call(bf16[768,2048]{1,0:T(8,128)(2,1)S(1)} %bitcast.16, bf16[768,2048]{1,0:T(8,128)(2,1)S(1)} %collective-permute-done.1.other, bf16[64,2176]{1,0:T(8,128)(2,1)S(1)} %shard_map.47.refs_0_), custom_call_target="tpu_custom_call" | custom-call | flops 4026531840 | bytes 6750208 | tf_op jit(solution)/shard_map/pallas_call | solution.py:99
  62.4 2.2 %collective-permute-done.15.refs_5_ = bf16[2,64,768]{2,1,0:T(8,128)(2,1)S(1)} collective-permute-done((bf16[2,64,768]{2,1,0:T(8,128)(2,1)S(1)}, bf16[2,64,768]{2,1,0:T(8,128)(2,1)S(1)}, u32[]{:S(2)}, u32[]{:S(2)}) %collective-permute-start.15) | collective-permute-done | bytes 196640 | tf_op jit(solution)/shard_map/ppermute | solution.py:23
  64.6 0.0 collective-permute-done.13.refs_2_
  64.6 5.4 %collective-permute-done.14.refs_3_ = bf16[2,64,768]{2,1,0:T(8,128)(2,1)S(1)} collective-permute-done((bf16[2,64,768]{2,1,0:T(8,128)(2,1)S(1)}, bf16[2,64,768]{2,1,0:T(8,128)(2,1)S(1)}, u32[]{:S(2)}, u32[]{:S(2)}) %collective-permute-start.14) | collective-permute-done | bytes 196640 | tf_op jit(solution)/shard_map/ppermute | solution.py:23
  70.0 0.0 collective-permute-done.16.refs_6_
  70.0 0.0 collective-permute-done.17.refs_7_
  70.0 1.3 %shard_map.55 = bf16[512,768]{1,0:T(8,128)(2,1)} custom-call(s32[8,64]{1,0:T(8,128)S(1)} %bitcast.18, bf16[2,64,768]{2,1,0:T(8,128)(2,1)S(1)} %shard_map.54.refs_0_, bf16[2,64,768]{2,1,0:T(8,128)(2,1)S(1)} %collective-permute-done.12.refs_1_, bf16[2,64,768]{2,1,0:T(8,128)(2,1)S(1)} %collective-permute-done.13.refs_2_, ...), custom_call_target="tpu_custom_call" | custom-call | tf_op jit(solution)/shard_map/pallas_call | solution.py:134
  (2 shorter events, 0.0 us)
Async XLA Ops:
  0.0 19.5 %collective-permute-start.1 = (bf16[768,2048]{1,0:T(8,128)(2,1)}, bf16[768,2048]{1,0:T(8,128)(2,1)S(1)}, u32[]{:S(2)}, u32[]{:S(2)}) collective-permute-start(bf16[768,2048]{1,0:T(8,128)(2,1)} %bitcast.9), channel_id=1, source_target_pairs={{0,1},{1,0},{2,3},{3,2},{4,5},{5,4},{6,7},{7,6},{8,9},{9,8},{10,11... | collective-permute-start | bytes 9437192 | tf_op jit(solution)/shard_map/ppermute | solution.py:23
  0.5 11.3 %collective-permute-start = (bf16[64,2048]{1,0:T(8,128)(2,1)}, bf16[64,2048]{1,0:T(8,128)(2,1)S(1)}, u32[]{:S(2)}, u32[]{:S(2)}) collective-permute-start(bf16[64,2048]{1,0:T(8,128)(2,1)} %bitcast.20), channel_id=1, source_target_pairs={{0,16},{1,17},{2,18},{3,19},{4,20},{5,21},{6,22},{7,23},{8,24},{9,... | collective-permute-start | bytes 786440 | tf_op jit(solution)/shard_map/ppermute | solution.py:33
  3.0 17.4 %collective-permute-start.2 = (bf16[64,2048]{1,0:T(8,128)(2,1)}, bf16[64,2048]{1,0:T(8,128)(2,1)S(1)}, u32[]{:S(2)}, u32[]{:S(2)}) collective-permute-start(bf16[64,2048]{1,0:T(8,128)(2,1)} %bitcast.21), channel_id=1, source_target_pairs={{0,24},{1,25},{2,26},{3,27},{4,28},{5,29},{6,30},{7,31},{8,16},{9,... | collective-permute-start | bytes 786440 | tf_op jit(solution)/shard_map/ppermute | solution.py:33
  5.5 1.9 %copy-start = (bf16[1,1,768,2048]{3,2,1,0:T(8,128)(2,1)S(1)}, bf16[1,1,768,2048]{3,2,1,0:T(8,128)(2,1)}, u32[]{:S(2)}) copy-start(bf16[1,1,768,2048]{3,2,1,0:T(8,128)(2,1)} %param.7) | copy-start | bytes 9437188
  7.4 0.7 copy-start.2
  8.1 0.7 copy-start.3
  8.8 13.5 %copy-start.1 = (bf16[1,1,768,2048]{3,2,1,0:T(8,128)(2,1)S(1)}, bf16[1,1,768,2048]{3,2,1,0:T(8,128)(2,1)}, u32[]{:S(2)}) copy-start(bf16[1,1,768,2048]{3,2,1,0:T(8,128)(2,1)} %param.7) | copy-start | bytes 9437188
  8.9 10.7 %collective-permute-start.3 = (bf16[64,128]{1,0:T(8,128)(2,1)S(1)}, bf16[64,128]{1,0:T(8,128)(2,1)S(1)}, u32[]{:S(2)}, u32[]{:S(2)}) collective-permute-start(bf16[64,128]{1,0:T(8,128)(2,1)S(1)} %shard_map.46.columns), channel_id=1, source_target_pairs={{0,8},{1,9},{2,10},{3,11},{4,12},{5,13},{6,14},{7,15},{8,0},{9,1},... | collective-permute-start | bytes 49160 | tf_op jit(solution)/shard_map/ppermute | solution.py:23
  9.0 15.3 %collective-permute-start.8 = (bf16[64,128]{1,0:T(8,128)(2,1)S(1)}, bf16[64,128]{1,0:T(8,128)(2,1)S(1)}, u32[]{:S(2)}, u32[]{:S(2)}) collective-permute-start(bf16[64,128]{1,0:T(8,128)(2,1)S(1)} %shard_map.46.columns), channel_id=1, source_target_pairs={{0,6},{1,7},{2,4},{3,5},{4,2},{5,3},{6,0},{7,1},{8,14},{9,15},{10,... | collective-permute-start | bytes 49160 | tf_op jit(solution)/shard_map/ppermute | solution.py:23
  11.8 15.1 %collective-permute-start.7 = (bf16[64,2048]{1,0:T(8,128)(2,1)}, bf16[64,2048]{1,0:T(8,128)(2,1)S(1)}, u32[]{:S(2)}, u32[]{:S(2)}) collective-permute-start(bf16[64,2048]{1,0:T(8,128)(2,1)} %bitcast.22), channel_id=1, source_target_pairs={{0,22},{1,23},{2,20},{3,21},{4,18},{5,19},{6,16},{7,17},{8,30},{9,... | collective-permute-start | bytes 786440 | tf_op jit(solution)/shard_map/ppermute | solution.py:33
  19.5 15.7 %collective-permute-start.5 = (bf16[64,2176]{1,0:T(8,128)(2,1)S(1)}, bf16[64,2176]{1,0:T(8,128)(2,1)S(1)}, u32[]{:S(2)}, u32[]{:S(2)}) collective-permute-start(bf16[64,2176]{1,0:T(8,128)(2,1)S(1)} %shard_map.47.refs_0_), channel_id=1, source_target_pairs={{0,4},{1,5},{2,6},{3,7},{4,0},{5,1},{6,2},{7,3},{8,12},{9,13},{10,... | collective-permute-start | bytes 835592 | tf_op jit(solution)/shard_map/ppermute | solution.py:23
  19.6 15.6 %collective-permute-start.6 = (bf16[64,2176]{1,0:T(8,128)(2,1)S(1)}, bf16[64,2176]{1,0:T(8,128)(2,1)S(1)}, u32[]{:S(2)}, u32[]{:S(2)}) collective-permute-start(bf16[64,2176]{1,0:T(8,128)(2,1)S(1)} %shard_map.47.refs_0_), channel_id=1, source_target_pairs={{0,2},{1,3},{2,0},{3,1},{4,6},{5,7},{6,4},{7,5},{8,10},{9,11},{10,... | collective-permute-start | bytes 835592 | tf_op jit(solution)/shard_map/ppermute | solution.py:23
  20.4 20.2 %collective-permute-start.4 = (bf16[64,2176]{1,0:T(8,128)(2,1)S(1)}, bf16[64,2176]{1,0:T(8,128)(2,1)S(1)}, u32[]{:S(2)}, u32[]{:S(2)}) collective-permute-start(bf16[64,2176]{1,0:T(8,128)(2,1)S(1)} %shard_map.48.refs_0_), channel_id=1, source_target_pairs={{0,4},{1,5},{2,6},{3,7},{4,0},{5,1},{6,2},{7,3},{8,12},{9,13},{10,... | collective-permute-start | bytes 835592 | tf_op jit(solution)/shard_map/ppermute | solution.py:23
  24.2 23.5 %collective-permute-start.11 = (bf16[2,64,768]{2,1,0:T(8,128)(2,1)S(1)}, bf16[2,64,768]{2,1,0:T(8,128)(2,1)S(1)}, u32[]{:S(2)}, u32[]{:S(2)}) collective-permute-start(bf16[2,64,768]{2,1,0:T(8,128)(2,1)S(1)} %shard_map.49), channel_id=1, source_target_pairs={{0,8},{1,9},{2,10},{3,11},{4,12},{5,13},{6,14},{7,15},{8,0},{9,1},... | collective-permute-start | bytes 589832 | tf_op jit(solution)/shard_map/ppermute | solution.py:23
  26.9 20.8 %collective-permute-start.10 = (bf16[64,2176]{1,0:T(8,128)(2,1)S(1)}, bf16[64,2176]{1,0:T(8,128)(2,1)S(1)}, u32[]{:S(2)}, u32[]{:S(2)}) collective-permute-start(bf16[64,2176]{1,0:T(8,128)(2,1)S(1)} %shard_map.48.refs_0_), channel_id=1, source_target_pairs={{0,2},{1,3},{2,0},{3,1},{4,6},{5,7},{6,4},{7,5},{8,10},{9,11},{10,... | collective-permute-start | bytes 835592 | tf_op jit(solution)/shard_map/ppermute | solution.py:23
  40.6 13.4 %collective-permute-start.9 = (bf16[64,2176]{1,0:T(8,128)(2,1)S(1)}, bf16[64,2176]{1,0:T(8,128)(2,1)S(1)}, u32[]{:S(2)}, u32[]{:S(2)}) collective-permute-start(bf16[64,2176]{1,0:T(8,128)(2,1)S(1)} %collective-permute-done.4.refs_0_), channel_id=1, source_target_pairs={{0,2},{1,3},{2,0},{3,1},{4,6},{5,7},{6,4},{7,5},{8,10},{9,11},{10,... | collective-permute-start | bytes 835592 | tf_op jit(solution)/shard_map/ppermute | solution.py:23
  44.1 25.9 %collective-permute-start.16 = (bf16[2,64,768]{2,1,0:T(8,128)(2,1)S(1)}, bf16[2,64,768]{2,1,0:T(8,128)(2,1)S(1)}, u32[]{:S(2)}, u32[]{:S(2)}) collective-permute-start(bf16[2,64,768]{2,1,0:T(8,128)(2,1)S(1)} %shard_map.51), channel_id=1, source_target_pairs={{0,12},{1,13},{2,14},{3,15},{4,8},{5,9},{6,10},{7,11},{8,4},{9,5},... | collective-permute-start | bytes 589832 | tf_op jit(solution)/shard_map/ppermute | solution.py:23
  47.7 6.3 %collective-permute-start.12 = (bf16[2,64,768]{2,1,0:T(8,128)(2,1)S(1)}, bf16[2,64,768]{2,1,0:T(8,128)(2,1)S(1)}, u32[]{:S(2)}, u32[]{:S(2)}) collective-permute-start(bf16[2,64,768]{2,1,0:T(8,128)(2,1)S(1)} %get-tuple-element.43), channel_id=1, source_target_pairs={{0,2},{1,3},{2,0},{3,1},{4,6},{5,7},{6,4},{7,5},{8,10},{9,11},{10,... | collective-permute-start | bytes 589832 | tf_op jit(solution)/shard_map/ppermute | solution.py:23
  50.4 14.2 %collective-permute-start.15 = (bf16[2,64,768]{2,1,0:T(8,128)(2,1)S(1)}, bf16[2,64,768]{2,1,0:T(8,128)(2,1)S(1)}, u32[]{:S(2)}, u32[]{:S(2)}) collective-permute-start(bf16[2,64,768]{2,1,0:T(8,128)(2,1)S(1)} %shard_map.52), channel_id=1, source_target_pairs={{0,10},{1,11},{2,8},{3,9},{4,14},{5,15},{6,12},{7,13},{8,2},{9,3},... | collective-permute-start | bytes 589832 | tf_op jit(solution)/shard_map/ppermute | solution.py:23
  50.5 14.1 %collective-permute-start.13 = (bf16[2,64,768]{2,1,0:T(8,128)(2,1)S(1)}, bf16[2,64,768]{2,1,0:T(8,128)(2,1)S(1)}, u32[]{:S(2)}, u32[]{:S(2)}) collective-permute-start(bf16[2,64,768]{2,1,0:T(8,128)(2,1)S(1)} %get-tuple-element.48), channel_id=1, source_target_pairs={{0,4},{1,5},{2,6},{3,7},{4,0},{5,1},{6,2},{7,3},{8,12},{9,13},{10,... | collective-permute-start | bytes 589832 | tf_op jit(solution)/shard_map/ppermute | solution.py:23
  54.0 16.0 %collective-permute-start.14 = (bf16[2,64,768]{2,1,0:T(8,128)(2,1)S(1)}, bf16[2,64,768]{2,1,0:T(8,128)(2,1)S(1)}, u32[]{:S(2)}, u32[]{:S(2)}) collective-permute-start(bf16[2,64,768]{2,1,0:T(8,128)(2,1)S(1)} %get-tuple-element.49), channel_id=1, source_target_pairs={{0,6},{1,7},{2,4},{3,5},{4,2},{5,3},{6,0},{7,1},{8,14},{9,15},{10,... | collective-permute-start | bytes 589832 | tf_op jit(solution)/shard_map/ppermute | solution.py:23
  56.0 14.0 %collective-permute-start.17 = (bf16[2,64,768]{2,1,0:T(8,128)(2,1)S(1)}, bf16[2,64,768]{2,1,0:T(8,128)(2,1)S(1)}, u32[]{:S(2)}, u32[]{:S(2)}) collective-permute-start(bf16[2,64,768]{2,1,0:T(8,128)(2,1)S(1)} %shard_map.53), channel_id=1, source_target_pairs={{0,14},{1,15},{2,12},{3,13},{4,10},{5,11},{6,8},{7,9},{8,6},{9,7},... | collective-permute-start | bytes 589832 | tf_op jit(solution)/shard_map/ppermute | solution.py:23

commit v12 on v11

--- a/solution.py
+++ b/solution.py
@@ -148,11 +148,9 @@
 
     rows = send_across(upstream, owners, 0)
     far = send_across(upstream, owners, Z_FAR)
-    near_side = send_across(upstream, owners, X ^ Z_NEAR)
     other_mat = send(weight_mat, owners, 0, 1)
     columns = gate_columns(route_ids.T, route_gates.T, weight_mat)
     far_columns = send(columns, owners, Z_FAR)
-    near_side_columns = send(columns, owners, X ^ Z_NEAR)
     rows, columns, other_mat = tie((rows, columns, other_mat))
     rows = widened(rows, columns)
     near = send(rows, owners, Z_NEAR)
@@ -162,27 +160,28 @@
     cross = send(far, owners, Z_NEAR)
     (out_far,) = work(far)
     back_far = send(out_far, owners, Z_FAR)
-    near, side, near_side, near_side_columns, _ = tie(
-        (near, side, near_side, near_side_columns, out_far)
-    )
     far_side = send(tie((far, out_far))[0], owners, X)
-    out_side, out_near, out_near_side = work(side, near, (near_side, near_side_columns))
-    cross, _ = tie((cross, out_side))
+    near, side, _ = tie((near, side, out_far))
+    out_side, out_near = work(side, near)
+    cross, near, _ = tie((cross, near, out_side))
     cross_side = send(cross, owners, X)
+    near_side = send(near, owners, X)
     (out_cross,) = work(cross)
     back_cross = send(out_cross, owners, Z_NEAR ^ Z_FAR)
-    far_side, back_far, out_side, out_near, out_near_side, _ = tie(
-        (far_side, back_far, out_side, out_near, out_near_side, out_cross)
+    far_side, back_far, out_side, out_near, _ = tie(
+        (far_side, back_far, out_side, out_near, out_cross)
     )
     back_side = send(out_side, owners, X)
     back_near = send(out_near, owners, Z_NEAR)
     (out_far_side,) = work(far_side)
     back_far_side = send(out_far_side, owners, X ^ Z_FAR)
-    cross_side, back_side, _ = tie((cross_side, back_side, out_far_side))
+    cross_side, _ = tie((cross_side, out_far_side))
     (out_cross_side,) = work(cross_side)
+    near_side, back_side, _ = tie((near_side, back_side, out_cross_side))
+    (out_near_side,) = work(near_side)
     back_cross_side = send(out_cross_side, owners, X ^ Z_NEAR ^ Z_FAR)
     back_near_side = send(out_near_side, owners, X ^ Z_NEAR)
-    rows, _ = tie((rows, out_cross_side))
+    rows, _ = tie((rows, out_near_side))
     (out_own,) = work(rows)
     received = {
         0: out_own,

time: 71.6 us -> 71.1 us (level)
  Pallas kernels: 13.8 us -> 15.8 us
  waiting for transfers between devices: 20.8 us -> 19.2 us
  starting transfers between devices: 33.5 us -> 32.6 us
    ppermute x3 -> x2, starting transfers between devices: 12.7 us -> 5.05 us  [send_across(): return lax.ppermute(block, ('pipe', 'expert'), route)]
    ppermute x15, starting transfers between devices: 20.7 us -> 27.5 us  [send(): return lax.ppermute(block, 'expert', route)]
    ppermute x15, waiting for transfers between devices: 20.6 us -> 16.5 us  [send(): return lax.ppermute(block, 'expert', route)]
    ppermute x3 -> x2, waiting for transfers between devices: 0.26 us -> 2.73 us  [send_across(): return lax.ppermute(block, ('pipe', 'expert'), route)]
    pallas_call x6 -> x7, Pallas kernels: 12.3 us -> 14.3 us  [products(): pl.pallas_call(functools.partial(products_kernel, paired), out_shape=[jax...]
  transfers between devices with their start and end apart: 18 -> 17, of which waited for: 6 -> 7; matrix products, arithmetic and copies ran while one was open for 0% -> 0% of each run, Pallas kernels for 17% -> 20%
where the time goes in v12:
time: 71.1 us; the launch traced here: 70.9 us
  starting transfers between devices  32.6 us (46%)
  waiting for transfers between devices  19.2 us (27%)
  Pallas kernels  15.8 us (22%)
  local copies, waits for them, and re-layouts  3.26 us (5%)
    ppermute x15, starting transfers between devices, send(): return lax.ppermute(block, 'expert', route)  27.5 us
    ppermute x15, waiting for transfers between devices, send(): return lax.ppermute(block, 'expert', route)  16.5 us
    pallas_call x7, Pallas kernels, products(): pl.pallas_call(functools.partial(products_kernel, paired), out_shape=[jax...  14.3 us
    ppermute x2, starting transfers between devices, send_across(): return lax.ppermute(block, ('pipe', 'expert'), route)  5.05 us
    unnamed x8, local copies, waits for them, and re-layouts  3.26 us
    ppermute x2, waiting for transfers between devices, send_across(): return lax.ppermute(block, ('pipe', 'expert'), route)  2.73 us
  transfers between devices with their start and end apart: 17, of which 7 were waited for; matrix products, arithmetic and copies ran while one was open for 0% of the time, Pallas kernels for 20%

profile of v12, /device:TPU:0, one launch (start us, length us, event | category | flops | bytes accessed | tf_op | source)
XLA Modules:
  0.0 70.9 jit_solution(1568208695883327970)
XLA Ops:
  0.0 0.5 collective-permute-start.1
  0.5 2.5 %collective-permute-start = (bf16[64,2048]{1,0:T(8,128)(2,1)}, bf16[64,2048]{1,0:T(8,128)(2,1)S(1)}, u32[]{:S(2)}, u32[]{:S(2)}) collective-permute-start(bf16[64,2048]{1,0:T(8,128)(2,1)} %bitcast.21), channel_id=1, source_target_pairs={{0,16},{1,17},{2,18},{3,19},{4,20},{5,21},{6,22},{7,23},{8,24},{9,... | collective-permute-start | bytes 786440 | tf_op jit(solution)/shard_map/ppermute | solution.py:33
  3.0 2.5 %collective-permute-start.2 = (bf16[64,2048]{1,0:T(8,128)(2,1)}, bf16[64,2048]{1,0:T(8,128)(2,1)S(1)}, u32[]{:S(2)}, u32[]{:S(2)}) collective-permute-start(bf16[64,2048]{1,0:T(8,128)(2,1)} %bitcast.22), channel_id=1, source_target_pairs={{0,24},{1,25},{2,26},{3,27},{4,28},{5,29},{6,30},{7,31},{8,16},{9,... | collective-permute-start | bytes 786440 | tf_op jit(solution)/shard_map/ppermute | solution.py:33
  5.5 0.0 copy-start
  5.5 1.9 %copy-done = bf16[1,1,768,2048]{3,2,1,0:T(8,128)(2,1)S(1)} copy-done((bf16[1,1,768,2048]{3,2,1,0:T(8,128)(2,1)S(1)}, bf16[1,1,768,2048]{3,2,1,0:T(8,128)(2,1)}, u32[]{:S(2)}) %copy-start) | copy-done | bytes 3145752
  7.4 0.0 copy-start.2
  7.4 0.7 copy-done.2
  8.1 0.0 copy-start.3
  8.1 0.7 copy-done.3
  8.8 0.0 copy-start.1
  8.8 0.1 shard_map.46.columns
  8.9 0.1 collective-permute-start.3
  9.0 2.3 %collective-permute-done.rows = bf16[64,2048]{1,0:T(8,128)(2,1)S(1)} collective-permute-done((bf16[64,2048]{1,0:T(8,128)(2,1)}, bf16[64,2048]{1,0:T(8,128)(2,1)S(1)}, u32[]{:S(2)}, u32[]{:S(2)}) %collective-permute-start) | collective-permute-done | bytes 262176 | tf_op jit(solution)/shard_map/ppermute | solution.py:33
  11.3 0.0 collective-permute-done.1.other
  11.3 6.4 %collective-permute-start.5 = (bf16[64,2176]{1,0:T(8,128)(2,1)S(1)}, bf16[64,2176]{1,0:T(8,128)(2,1)S(1)}, u32[]{:S(2)}, u32[]{:S(2)}) collective-permute-start(bf16[64,2176]{1,0:T(8,128)(2,1)S(1)} %shard_map.47.refs_0_), channel_id=1, source_target_pairs={{0,4},{1,5},{2,6},{3,7},{4,0},{5,1},{6,2},{7,3},{8,12},{9,13},{10,... | collective-permute-start | bytes 835592 | tf_op jit(solution)/shard_map/ppermute | solution.py:23
  17.7 1.5 %collective-permute-start.6 = (bf16[64,2176]{1,0:T(8,128)(2,1)S(1)}, bf16[64,2176]{1,0:T(8,128)(2,1)S(1)}, u32[]{:S(2)}, u32[]{:S(2)}) collective-permute-start(bf16[64,2176]{1,0:T(8,128)(2,1)S(1)} %shard_map.47.refs_0_), channel_id=1, source_target_pairs={{0,2},{1,3},{2,0},{3,1},{4,6},{5,7},{6,4},{7,5},{8,10},{9,11},{10,... | collective-permute-start | bytes 835592 | tf_op jit(solution)/shard_map/ppermute | solution.py:23
  19.2 0.0 collective-permute-done.3.columns
  19.2 0.4 collective-permute-done.2.rows
  19.6 0.1 collective-permute-start.4
  19.7 0.0 copy-done.1
  19.7 2.0 %shard_map.49 = bf16[2,64,768]{2,1,0:T(8,128)(2,1)S(1)} custom-call(bf16[768,2048]{1,0:T(8,128)(2,1)S(1)} %bitcast.11, bf16[768,2048]{1,0:T(8,128)(2,1)S(1)} %collective-permute-done.1.other, bf16[64,2176]{1,0:T(8,128)(2,1)S(1)} %shard_map.48.refs_0_), custom_call_target="tpu_custom_call" | custom-call | flops 4026531840 | bytes 6750208 | tf_op jit(solution)/shard_map/pallas_call | solution.py:99
  21.7 4.0 %collective-permute-start.9 = (bf16[2,64,768]{2,1,0:T(8,128)(2,1)S(1)}, bf16[2,64,768]{2,1,0:T(8,128)(2,1)S(1)}, u32[]{:S(2)}, u32[]{:S(2)}) collective-permute-start(bf16[2,64,768]{2,1,0:T(8,128)(2,1)S(1)} %shard_map.49), channel_id=1, source_target_pairs={{0,8},{1,9},{2,10},{3,11},{4,12},{5,13},{6,14},{7,15},{8,0},{9,1},... | collective-permute-start | bytes 589832 | tf_op jit(solution)/shard_map/ppermute | solution.py:23
  25.8 1.5 %collective-permute-start.8 = (bf16[64,2176]{1,0:T(8,128)(2,1)S(1)}, bf16[64,2176]{1,0:T(8,128)(2,1)S(1)}, u32[]{:S(2)}, u32[]{:S(2)}) collective-permute-start(bf16[64,2176]{1,0:T(8,128)(2,1)S(1)} %shard_map.48.refs_0_), channel_id=1, source_target_pairs={{0,2},{1,3},{2,0},{3,1},{4,6},{5,7},{6,4},{7,5},{8,10},{9,11},{10,... | collective-permute-start | bytes 835592 | tf_op jit(solution)/shard_map/ppermute | solution.py:23
  27.3 0.0 collective-permute-done.5.refs_1_
  27.3 0.0 collective-permute-done.6.refs_0_
  27.3 2.2 %shard_map.50 = (bf16[2,64,768]{2,1,0:T(8,128)(2,1)S(1)}, bf16[2,64,768]{2,1,0:T(8,128)(2,1)S(1)}) custom-call(bf16[768,2048]{1,0:T(8,128)(2,1)S(1)} %bitcast.12, bf16[768,2048]{1,0:T(8,128)(2,1)S(1)} %collective-permute-done.1.other, bf16[64,2176]{1,0:T(8,128)(2,1)S(1)} %collective-permute-done.6.refs_0_, bf16[64,2176]{1,0:T(8,128)(2,1)S(1)} %collective-permute-done.5.refs_1_), custom_call_target="tpu_custom_call" | custom-call | flops 8053063680 | bytes 7208960 | tf_op jit(solution)/shard_map/pallas_call | solution.py:99
  29.5 5.5 %collective-permute-done.4.refs_0_ = bf16[64,2176]{1,0:T(8,128)(2,1)S(1)} collective-permute-done((bf16[64,2176]{1,0:T(8,128)(2,1)S(1)}, bf16[64,2176]{1,0:T(8,128)(2,1)S(1)}, u32[]{:S(2)}, u32[]{:S(2)}) %collective-permute-start.4) | collective-permute-done | bytes 278560 | tf_op jit(solution)/shard_map/ppermute | solution.py:23
  35.0 1.5 %collective-permute-start.7 = (bf16[64,2176]{1,0:T(8,128)(2,1)S(1)}, bf16[64,2176]{1,0:T(8,128)(2,1)S(1)}, u32[]{:S(2)}, u32[]{:S(2)}) collective-permute-start(bf16[64,2176]{1,0:T(8,128)(2,1)S(1)} %collective-permute-done.5.refs_1_), channel_id=1, source_target_pairs={{0,2},{1,3},{2,0},{3,1},{4,6},{5,7},{6,4},{7,5},{8,10},{9,11},{10,... | collective-permute-start | bytes 835592 | tf_op jit(solution)/shard_map/ppermute | solution.py:23
  36.5 0.5 collective-permute-start.11
  37.0 2.0 %shard_map.51 = bf16[2,64,768]{2,1,0:T(8,128)(2,1)S(1)} custom-call(bf16[768,2048]{1,0:T(8,128)(2,1)S(1)} %bitcast.13, bf16[768,2048]{1,0:T(8,128)(2,1)S(1)} %collective-permute-done.1.other, bf16[64,2176]{1,0:T(8,128)(2,1)S(1)} %collective-permute-done.4.refs_0_), custom_call_target="tpu_custom_call" | custom-call | flops 4026531840 | bytes 6750208 | tf_op jit(solution)/shard_map/pallas_call | solution.py:99
  39.0 3.5 %collective-permute-start.15 = (bf16[2,64,768]{2,1,0:T(8,128)(2,1)S(1)}, bf16[2,64,768]{2,1,0:T(8,128)(2,1)S(1)}, u32[]{:S(2)}, u32[]{:S(2)}) collective-permute-start(bf16[2,64,768]{2,1,0:T(8,128)(2,1)S(1)} %shard_map.51), channel_id=1, source_target_pairs={{0,12},{1,13},{2,14},{3,15},{4,8},{5,9},{6,10},{7,11},{8,4},{9,5},... | collective-permute-start | bytes 589832 | tf_op jit(solution)/shard_map/ppermute | solution.py:23
  42.5 0.0 collective-permute-done.9.refs_4_
  42.5 0.0 collective-permute-done.8.refs_0_
  42.5 1.5 %collective-permute-start.10 = (bf16[2,64,768]{2,1,0:T(8,128)(2,1)S(1)}, bf16[2,64,768]{2,1,0:T(8,128)(2,1)S(1)}, u32[]{:S(2)}, u32[]{:S(2)}) collective-permute-start(bf16[2,64,768]{2,1,0:T(8,128)(2,1)S(1)} %get-tuple-element.39), channel_id=1, source_target_pairs={{0,2},{1,3},{2,0},{3,1},{4,6},{5,7},{6,4},{7,5},{8,10},{9,11},{10,... | collective-permute-start | bytes 589832 | tf_op jit(solution)/shard_map/ppermute | solution.py:23
  44.0 0.0 collective-permute-start.12
  44.0 2.0 %shard_map.52 = bf16[2,64,768]{2,1,0:T(8,128)(2,1)S(1)} custom-call(bf16[768,2048]{1,0:T(8,128)(2,1)S(1)} %bitcast.14, bf16[768,2048]{1,0:T(8,128)(2,1)S(1)} %collective-permute-done.1.other, bf16[64,2176]{1,0:T(8,128)(2,1)S(1)} %collective-permute-done.8.refs_0_), custom_call_target="tpu_custom_call" | custom-call | flops 4026531840 | bytes 6750208 | tf_op jit(solution)/shard_map/pallas_call | solution.py:99
  46.1 4.4 %collective-permute-done.11.refs_0_ = bf16[64,2176]{1,0:T(8,128)(2,1)S(1)} collective-permute-done((bf16[64,2176]{1,0:T(8,128)(2,1)S(1)}, bf16[64,2176]{1,0:T(8,128)(2,1)S(1)}, u32[]{:S(2)}, u32[]{:S(2)}) %collective-permute-start.11) | collective-permute-done | bytes 278560 | tf_op jit(solution)/shard_map/ppermute | solution.py:23
  50.5 2.4 %collective-permute-start.14 = (bf16[2,64,768]{2,1,0:T(8,128)(2,1)S(1)}, bf16[2,64,768]{2,1,0:T(8,128)(2,1)S(1)}, u32[]{:S(2)}, u32[]{:S(2)}) collective-permute-start(bf16[2,64,768]{2,1,0:T(8,128)(2,1)S(1)} %shard_map.52), channel_id=1, source_target_pairs={{0,10},{1,11},{2,8},{3,9},{4,14},{5,15},{6,12},{7,13},{8,2},{9,3},... | collective-permute-start | bytes 589832 | tf_op jit(solution)/shard_map/ppermute | solution.py:23
  52.9 2.0 %shard_map.53 = bf16[2,64,768]{2,1,0:T(8,128)(2,1)S(1)} custom-call(bf16[768,2048]{1,0:T(8,128)(2,1)S(1)} %bitcast.15, bf16[768,2048]{1,0:T(8,128)(2,1)S(1)} %collective-permute-done.1.other, bf16[64,2176]{1,0:T(8,128)(2,1)S(1)} %collective-permute-done.11.refs_0_), custom_call_target="tpu_custom_call" | custom-call | flops 4026531840 | bytes 6750208 | tf_op jit(solution)/shard_map/pallas_call | solution.py:99
  54.9 0.1 collective-permute-done.10.refs_1_
  55.0 3.2 %collective-permute-start.16 = (bf16[2,64,768]{2,1,0:T(8,128)(2,1)S(1)}, bf16[2,64,768]{2,1,0:T(8,128)(2,1)S(1)}, u32[]{:S(2)}, u32[]{:S(2)}) collective-permute-start(bf16[2,64,768]{2,1,0:T(8,128)(2,1)S(1)} %shard_map.53), channel_id=1, source_target_pairs={{0,14},{1,15},{2,12},{3,13},{4,10},{5,11},{6,8},{7,9},{8,6},{9,7},... | collective-permute-start | bytes 589832 | tf_op jit(solution)/shard_map/ppermute | solution.py:23
  58.2 0.0 collective-permute-done.7.refs_0_
  58.2 2.0 %shard_map.54 = bf16[2,64,768]{2,1,0:T(8,128)(2,1)S(1)} custom-call(bf16[768,2048]{1,0:T(8,128)(2,1)S(1)} %bitcast.16, bf16[768,2048]{1,0:T(8,128)(2,1)S(1)} %collective-permute-done.1.other, bf16[64,2176]{1,0:T(8,128)(2,1)S(1)} %collective-permute-done.7.refs_0_), custom_call_target="tpu_custom_call" | custom-call | flops 4026531840 | bytes 6750208 | tf_op jit(solution)/shard_map/pallas_call | solution.py:99
  60.2 0.9 %collective-permute-start.13 = (bf16[2,64,768]{2,1,0:T(8,128)(2,1)S(1)}, bf16[2,64,768]{2,1,0:T(8,128)(2,1)S(1)}, u32[]{:S(2)}, u32[]{:S(2)}) collective-permute-start(bf16[2,64,768]{2,1,0:T(8,128)(2,1)S(1)} %shard_map.54), channel_id=1, source_target_pairs={{0,6},{1,7},{2,4},{3,5},{4,2},{5,3},{6,0},{7,1},{8,14},{9,15},{10,... | collective-permute-start | bytes 589832 | tf_op jit(solution)/shard_map/ppermute | solution.py:23
  61.1 2.0 %shard_map.55.refs_0_ = bf16[2,64,768]{2,1,0:T(8,128)(2,1)S(1)} custom-call(bf16[768,2048]{1,0:T(8,128)(2,1)S(1)} %bitcast.17, bf16[768,2048]{1,0:T(8,128)(2,1)S(1)} %collective-permute-done.1.other, bf16[64,2176]{1,0:T(8,128)(2,1)S(1)} %shard_map.47.refs_0_), custom_call_target="tpu_custom_call" | custom-call | flops 4026531840 | bytes 6750208 | tf_op jit(solution)/shard_map/pallas_call | solution.py:99
  63.1 0.0 collective-permute-done.12.refs_2_
  63.1 3.6 %collective-permute-done.14.refs_5_ = bf16[2,64,768]{2,1,0:T(8,128)(2,1)S(1)} collective-permute-done((bf16[2,64,768]{2,1,0:T(8,128)(2,1)S(1)}, bf16[2,64,768]{2,1,0:T(8,128)(2,1)S(1)}, u32[]{:S(2)}, u32[]{:S(2)}) %collective-permute-start.14) | collective-permute-done | bytes 196640 | tf_op jit(solution)/shard_map/ppermute | solution.py:23
  66.7 0.0 collective-permute-done.15.refs_6_
  66.7 2.8 %collective-permute-done.13.refs_3_ = bf16[2,64,768]{2,1,0:T(8,128)(2,1)S(1)} collective-permute-done((bf16[2,64,768]{2,1,0:T(8,128)(2,1)S(1)}, bf16[2,64,768]{2,1,0:T(8,128)(2,1)S(1)}, u32[]{:S(2)}, u32[]{:S(2)}) %collective-permute-start.13) | collective-permute-done | bytes 196640 | tf_op jit(solution)/shard_map/ppermute | solution.py:23
  69.5 0.0 collective-permute-done.16.refs_7_
  69.5 1.3 %shard_map.56 = bf16[512,768]{1,0:T(8,128)(2,1)} custom-call(s32[8,64]{1,0:T(8,128)S(1)} %bitcast.19, bf16[2,64,768]{2,1,0:T(8,128)(2,1)S(1)} %shard_map.55.refs_0_, bf16[2,64,768]{2,1,0:T(8,128)(2,1)S(1)} %collective-permute-done.10.refs_1_, bf16[2,64,768]{2,1,0:T(8,128)(2,1)S(1)} %collective-permute-done.12.refs_2_, ...), custom_call_target="tpu_custom_call" | custom-call | tf_op jit(solution)/shard_map/pallas_call | solution.py:134
  (2 shorter events, 0.0 us)
Async XLA Ops:
  0.0 11.3 %collective-permute-start.1 = (bf16[768,2048]{1,0:T(8,128)(2,1)}, bf16[768,2048]{1,0:T(8,128)(2,1)S(1)}, u32[]{:S(2)}, u32[]{:S(2)}) collective-permute-start(bf16[768,2048]{1,0:T(8,128)(2,1)} %bitcast.9), channel_id=1, source_target_pairs={{0,1},{1,0},{2,3},{3,2},{4,5},{5,4},{6,7},{7,6},{8,9},{9,8},{10,11... | collective-permute-start | bytes 9437192 | tf_op jit(solution)/shard_map/ppermute | solution.py:23
  0.5 10.8 %collective-permute-start = (bf16[64,2048]{1,0:T(8,128)(2,1)}, bf16[64,2048]{1,0:T(8,128)(2,1)S(1)}, u32[]{:S(2)}, u32[]{:S(2)}) collective-permute-start(bf16[64,2048]{1,0:T(8,128)(2,1)} %bitcast.21), channel_id=1, source_target_pairs={{0,16},{1,17},{2,18},{3,19},{4,20},{5,21},{6,22},{7,23},{8,24},{9,... | collective-permute-start | bytes 786440 | tf_op jit(solution)/shard_map/ppermute | solution.py:33
  3.0 16.6 %collective-permute-start.2 = (bf16[64,2048]{1,0:T(8,128)(2,1)}, bf16[64,2048]{1,0:T(8,128)(2,1)S(1)}, u32[]{:S(2)}, u32[]{:S(2)}) collective-permute-start(bf16[64,2048]{1,0:T(8,128)(2,1)} %bitcast.22), channel_id=1, source_target_pairs={{0,24},{1,25},{2,26},{3,27},{4,28},{5,29},{6,30},{7,31},{8,16},{9,... | collective-permute-start | bytes 786440 | tf_op jit(solution)/shard_map/ppermute | solution.py:33
  5.5 1.9 %copy-start = (bf16[1,1,768,2048]{3,2,1,0:T(8,128)(2,1)S(1)}, bf16[1,1,768,2048]{3,2,1,0:T(8,128)(2,1)}, u32[]{:S(2)}) copy-start(bf16[1,1,768,2048]{3,2,1,0:T(8,128)(2,1)} %param.7) | copy-start | bytes 9437188
  7.4 0.7 copy-start.2
  8.1 0.7 copy-start.3
  8.8 10.9 %copy-start.1 = (bf16[1,1,768,2048]{3,2,1,0:T(8,128)(2,1)S(1)}, bf16[1,1,768,2048]{3,2,1,0:T(8,128)(2,1)}, u32[]{:S(2)}) copy-start(bf16[1,1,768,2048]{3,2,1,0:T(8,128)(2,1)} %param.7) | copy-start | bytes 9437188
  8.9 10.3 %collective-permute-start.3 = (bf16[64,128]{1,0:T(8,128)(2,1)S(1)}, bf16[64,128]{1,0:T(8,128)(2,1)S(1)}, u32[]{:S(2)}, u32[]{:S(2)}) collective-permute-start(bf16[64,128]{1,0:T(8,128)(2,1)S(1)} %shard_map.46.columns), channel_id=1, source_target_pairs={{0,8},{1,9},{2,10},{3,11},{4,12},{5,13},{6,14},{7,15},{8,0},{9,1},... | collective-permute-start | bytes 49160 | tf_op jit(solution)/shard_map/ppermute | solution.py:23
  11.3 16.0 %collective-permute-start.5 = (bf16[64,2176]{1,0:T(8,128)(2,1)S(1)}, bf16[64,2176]{1,0:T(8,128)(2,1)S(1)}, u32[]{:S(2)}, u32[]{:S(2)}) collective-permute-start(bf16[64,2176]{1,0:T(8,128)(2,1)S(1)} %shard_map.47.refs_0_), channel_id=1, source_target_pairs={{0,4},{1,5},{2,6},{3,7},{4,0},{5,1},{6,2},{7,3},{8,12},{9,13},{10,... | collective-permute-start | bytes 835592 | tf_op jit(solution)/shard_map/ppermute | solution.py:23
  17.7 9.6 %collective-permute-start.6 = (bf16[64,2176]{1,0:T(8,128)(2,1)S(1)}, bf16[64,2176]{1,0:T(8,128)(2,1)S(1)}, u32[]{:S(2)}, u32[]{:S(2)}) collective-permute-start(bf16[64,2176]{1,0:T(8,128)(2,1)S(1)} %shard_map.47.refs_0_), channel_id=1, source_target_pairs={{0,2},{1,3},{2,0},{3,1},{4,6},{5,7},{6,4},{7,5},{8,10},{9,11},{10,... | collective-permute-start | bytes 835592 | tf_op jit(solution)/shard_map/ppermute | solution.py:23
  19.6 15.3 %collective-permute-start.4 = (bf16[64,2176]{1,0:T(8,128)(2,1)S(1)}, bf16[64,2176]{1,0:T(8,128)(2,1)S(1)}, u32[]{:S(2)}, u32[]{:S(2)}) collective-permute-start(bf16[64,2176]{1,0:T(8,128)(2,1)S(1)} %shard_map.48.refs_0_), channel_id=1, source_target_pairs={{0,4},{1,5},{2,6},{3,7},{4,0},{5,1},{6,2},{7,3},{8,12},{9,13},{10,... | collective-permute-start | bytes 835592 | tf_op jit(solution)/shard_map/ppermute | solution.py:23
  21.7 20.8 %collective-permute-start.9 = (bf16[2,64,768]{2,1,0:T(8,128)(2,1)S(1)}, bf16[2,64,768]{2,1,0:T(8,128)(2,1)S(1)}, u32[]{:S(2)}, u32[]{:S(2)}) collective-permute-start(bf16[2,64,768]{2,1,0:T(8,128)(2,1)S(1)} %shard_map.49), channel_id=1, source_target_pairs={{0,8},{1,9},{2,10},{3,11},{4,12},{5,13},{6,14},{7,15},{8,0},{9,1},... | collective-permute-start | bytes 589832 | tf_op jit(solution)/shard_map/ppermute | solution.py:23
  25.8 16.8 %collective-permute-start.8 = (bf16[64,2176]{1,0:T(8,128)(2,1)S(1)}, bf16[64,2176]{1,0:T(8,128)(2,1)S(1)}, u32[]{:S(2)}, u32[]{:S(2)}) collective-permute-start(bf16[64,2176]{1,0:T(8,128)(2,1)S(1)} %shard_map.48.refs_0_), channel_id=1, source_target_pairs={{0,2},{1,3},{2,0},{3,1},{4,6},{5,7},{6,4},{7,5},{8,10},{9,11},{10,... | collective-permute-start | bytes 835592 | tf_op jit(solution)/shard_map/ppermute | solution.py:23
  35.0 23.2 %collective-permute-start.7 = (bf16[64,2176]{1,0:T(8,128)(2,1)S(1)}, bf16[64,2176]{1,0:T(8,128)(2,1)S(1)}, u32[]{:S(2)}, u32[]{:S(2)}) collective-permute-start(bf16[64,2176]{1,0:T(8,128)(2,1)S(1)} %collective-permute-done.5.refs_1_), channel_id=1, source_target_pairs={{0,2},{1,3},{2,0},{3,1},{4,6},{5,7},{6,4},{7,5},{8,10},{9,11},{10,... | collective-permute-start | bytes 835592 | tf_op jit(solution)/shard_map/ppermute | solution.py:23
  36.5 14.0 %collective-permute-start.11 = (bf16[64,2176]{1,0:T(8,128)(2,1)S(1)}, bf16[64,2176]{1,0:T(8,128)(2,1)S(1)}, u32[]{:S(2)}, u32[]{:S(2)}) collective-permute-start(bf16[64,2176]{1,0:T(8,128)(2,1)S(1)} %collective-permute-done.4.refs_0_), channel_id=1, source_target_pairs={{0,2},{1,3},{2,0},{3,1},{4,6},{5,7},{6,4},{7,5},{8,10},{9,11},{10,... | collective-permute-start | bytes 835592 | tf_op jit(solution)/shard_map/ppermute | solution.py:23
  39.0 27.7 %collective-permute-start.15 = (bf16[2,64,768]{2,1,0:T(8,128)(2,1)S(1)}, bf16[2,64,768]{2,1,0:T(8,128)(2,1)S(1)}, u32[]{:S(2)}, u32[]{:S(2)}) collective-permute-start(bf16[2,64,768]{2,1,0:T(8,128)(2,1)S(1)} %shard_map.51), channel_id=1, source_target_pairs={{0,12},{1,13},{2,14},{3,15},{4,8},{5,9},{6,10},{7,11},{8,4},{9,5},... | collective-permute-start | bytes 589832 | tf_op jit(solution)/shard_map/ppermute | solution.py:23
  42.5 12.5 %collective-permute-start.10 = (bf16[2,64,768]{2,1,0:T(8,128)(2,1)S(1)}, bf16[2,64,768]{2,1,0:T(8,128)(2,1)S(1)}, u32[]{:S(2)}, u32[]{:S(2)}) collective-permute-start(bf16[2,64,768]{2,1,0:T(8,128)(2,1)S(1)} %get-tuple-element.39), channel_id=1, source_target_pairs={{0,2},{1,3},{2,0},{3,1},{4,6},{5,7},{6,4},{7,5},{8,10},{9,11},{10,... | collective-permute-start | bytes 589832 | tf_op jit(solution)/shard_map/ppermute | solution.py:23
  44.0 19.1 %collective-permute-start.12 = (bf16[2,64,768]{2,1,0:T(8,128)(2,1)S(1)}, bf16[2,64,768]{2,1,0:T(8,128)(2,1)S(1)}, u32[]{:S(2)}, u32[]{:S(2)}) collective-permute-start(bf16[2,64,768]{2,1,0:T(8,128)(2,1)S(1)} %get-tuple-element.45), channel_id=1, source_target_pairs={{0,4},{1,5},{2,6},{3,7},{4,0},{5,1},{6,2},{7,3},{8,12},{9,13},{10,... | collective-permute-start | bytes 589832 | tf_op jit(solution)/shard_map/ppermute | solution.py:23
  50.5 16.2 %collective-permute-start.14 = (bf16[2,64,768]{2,1,0:T(8,128)(2,1)S(1)}, bf16[2,64,768]{2,1,0:T(8,128)(2,1)S(1)}, u32[]{:S(2)}, u32[]{:S(2)}) collective-permute-start(bf16[2,64,768]{2,1,0:T(8,128)(2,1)S(1)} %shard_map.52), channel_id=1, source_target_pairs={{0,10},{1,11},{2,8},{3,9},{4,14},{5,15},{6,12},{7,13},{8,2},{9,3},... | collective-permute-start | bytes 589832 | tf_op jit(solution)/shard_map/ppermute | solution.py:23
  55.0 14.5 %collective-permute-start.16 = (bf16[2,64,768]{2,1,0:T(8,128)(2,1)S(1)}, bf16[2,64,768]{2,1,0:T(8,128)(2,1)S(1)}, u32[]{:S(2)}, u32[]{:S(2)}) collective-permute-start(bf16[2,64,768]{2,1,0:T(8,128)(2,1)S(1)} %shard_map.53), channel_id=1, source_target_pairs={{0,14},{1,15},{2,12},{3,13},{4,10},{5,11},{6,8},{7,9},{8,6},{9,7},... | collective-permute-start | bytes 589832 | tf_op jit(solution)/shard_map/ppermute | solution.py:23
  60.2 9.3 %collective-permute-start.13 = (bf16[2,64,768]{2,1,0:T(8,128)(2,1)S(1)}, bf16[2,64,768]{2,1,0:T(8,128)(2,1)S(1)}, u32[]{:S(2)}, u32[]{:S(2)}) collective-permute-start(bf16[2,64,768]{2,1,0:T(8,128)(2,1)S(1)} %shard_map.54), channel_id=1, source_target_pairs={{0,6},{1,7},{2,4},{3,5},{4,2},{5,3},{6,0},{7,1},{8,14},{9,15},{10,... | collective-permute-start | bytes 589832 | tf_op jit(solution)/shard_map/ppermute | solution.py:23

commit v13 on v12

--- a/solution.py
+++ b/solution.py
@@ -146,40 +146,38 @@
     def work(*pieces):
         return products(list(pieces), weight_mat, other_mat)
 
+    far = send_across(upstream, owners, Z_FAR)
     rows = send_across(upstream, owners, 0)
-    far = send_across(upstream, owners, Z_FAR)
     other_mat = send(weight_mat, owners, 0, 1)
     columns = gate_columns(route_ids.T, route_gates.T, weight_mat)
     far_columns = send(columns, owners, Z_FAR)
-    rows, columns, other_mat = tie((rows, columns, other_mat))
+    far, far_columns, other_mat = tie((far, far_columns, other_mat))
+    far = widened(far, far_columns)
+    cross = send(far, owners, Z_NEAR)
+    far_side = send(far, owners, X)
+    (out_far,) = work(far)
+    back_far = send(out_far, owners, Z_FAR)
+    rows, columns, _ = tie((rows, columns, out_far))
     rows = widened(rows, columns)
     near = send(rows, owners, Z_NEAR)
     side = send(rows, owners, X)
-    far, far_columns, rows = tie((far, far_columns, rows))
-    far = widened(far, far_columns)
-    cross = send(far, owners, Z_NEAR)
-    (out_far,) = work(far)
-    back_far = send(out_far, owners, Z_FAR)
-    far_side = send(tie((far, out_far))[0], owners, X)
-    near, side, _ = tie((near, side, out_far))
-    out_side, out_near = work(side, near)
-    cross, near, _ = tie((cross, near, out_side))
+    cross, rows = tie((cross, rows))
     cross_side = send(cross, owners, X)
-    near_side = send(near, owners, X)
     (out_cross,) = work(cross)
     back_cross = send(out_cross, owners, Z_NEAR ^ Z_FAR)
-    far_side, back_far, out_side, out_near, _ = tie(
-        (far_side, back_far, out_side, out_near, out_cross)
-    )
+    far_side, back_far, _ = tie((far_side, back_far, out_cross))
+    (out_far_side,) = work(far_side)
+    back_far_side = send(out_far_side, owners, X ^ Z_FAR)
+    near, cross_side, _ = tie((near, cross_side, out_far_side))
+    near_side = send(near, owners, X)
+    (out_cross_side,) = work(cross_side)
+    back_cross_side = send(out_cross_side, owners, X ^ Z_NEAR ^ Z_FAR)
+    side, near, _ = tie((side, near, out_cross_side))
+    out_side, out_near = work(side, near)
     back_side = send(out_side, owners, X)
     back_near = send(out_near, owners, Z_NEAR)
-    (out_far_side,) = work(far_side)
-    back_far_side = send(out_far_side, owners, X ^ Z_FAR)
-    cross_side, _ = tie((cross_side, out_far_side))
-    (out_cross_side,) = work(cross_side)
-    near_side, back_side, _ = tie((near_side, back_side, out_cross_side))
+    near_side, _ = tie((near_side, out_near))
     (out_near_side,) = work(near_side)
-    back_cross_side = send(out_cross_side, owners, X ^ Z_NEAR ^ Z_FAR)
     back_near_side = send(out_near_side, owners, X ^ Z_NEAR)
     rows, _ = tie((rows, out_near_side))
     (out_own,) = work(rows)

time: 71.1 us -> 67.2 us (0.945)
  starting transfers between devices: 32.6 us -> 29 us
    ppermute x15, starting transfers between devices: 27.5 us -> 24.2 us  [send(): return lax.ppermute(block, 'expert', route)]
    ppermute x2, waiting for transfers between devices: 2.73 us -> 0.01 us  [send_across(): return lax.ppermute(block, ('pipe', 'expert'), route)]
    ppermute x15, waiting for transfers between devices: 16.5 us -> 18.9 us  [send(): return lax.ppermute(block, 'expert', route)]
  transfers between devices with their start and end apart: 17 -> 17, of which waited for: 7 -> 6; matrix products, arithmetic and copies ran while one was open for 0% -> 0% of each run, Pallas kernels for 20% -> 22%
where the time goes in v13:
time: 67.2 us; the launch traced here: 67 us
  starting transfers between devices  29 us (43%)
  waiting for transfers between devices  18.9 us (28%)
  Pallas kernels  15.8 us (24%)
  local copies, waits for them, and re-layouts  3.26 us (5%)
    ppermute x15, starting transfers between devices, send(): return lax.ppermute(block, 'expert', route)  24.2 us
    ppermute x15, waiting for transfers between devices, send(): return lax.ppermute(block, 'expert', route)  18.9 us
    pallas_call x7, Pallas kernels, products(): pl.pallas_call(functools.partial(products_kernel, paired), out_shape=[jax...  14.3 us
    ppermute x2, starting transfers between devices, send_across(): return lax.ppermute(block, ('pipe', 'expert'), route)  4.79 us
    unnamed x8, local copies, waits for them, and re-layouts  3.26 us
  transfers between devices with their start and end apart: 17, of which 6 were waited for; matrix products, arithmetic and copies ran while one was open for 0% of the time, Pallas kernels for 22%

profile of v13, /device:TPU:0, one launch (start us, length us, event | category | flops | bytes accessed | tf_op | source)
XLA Modules:
  0.0 67.0 jit_solution(4830721368910139199)
XLA Ops:
  0.0 0.5 collective-permute-start.2
  0.5 4.5 %collective-permute-start = (bf16[64,2048]{1,0:T(8,128)(2,1)}, bf16[64,2048]{1,0:T(8,128)(2,1)S(1)}, u32[]{:S(2)}, u32[]{:S(2)}) collective-permute-start(bf16[64,2048]{1,0:T(8,128)(2,1)} %bitcast.21), channel_id=1, source_target_pairs={{0,24},{1,25},{2,26},{3,27},{4,28},{5,29},{6,30},{7,31},{8,16},{9,... | collective-permute-start | bytes 786440 | tf_op jit(solution)/shard_map/ppermute | solution.py:33
  5.0 0.0 copy-start
  5.0 1.9 %copy-done = bf16[1,1,768,2048]{3,2,1,0:T(8,128)(2,1)S(1)} copy-done((bf16[1,1,768,2048]{3,2,1,0:T(8,128)(2,1)S(1)}, bf16[1,1,768,2048]{3,2,1,0:T(8,128)(2,1)}, u32[]{:S(2)}) %copy-start) | copy-done | bytes 3145752
  6.9 0.0 copy-start.2
  6.9 0.7 %copy-done.2 = s32[1,64,8]{1,2,0:T(8,128)S(1)} copy-done((s32[1,64,8]{1,2,0:T(8,128)S(1)}, s32[1,64,8]{1,2,0:T(8,128)}, u32[]{:S(2)}) %copy-start.2) | copy-done | bytes 2072
  7.6 0.0 copy-start.3
  7.6 0.7 %copy-done.3 = bf16[1,64,8]{1,2,0:T(8,128)(2,1)S(1)} copy-done((bf16[1,64,8]{1,2,0:T(8,128)(2,1)S(1)}, bf16[1,64,8]{1,2,0:T(8,128)(2,1)}, u32[]{:S(2)}) %copy-start.3) | copy-done | bytes 1048
  8.3 0.0 copy-start.1
  8.3 0.1 shard_map.46.columns
  8.4 0.4 collective-permute-start.1
  8.7 0.2 collective-permute-start.4
  9.0 9.6 %collective-permute-done.1.columns = bf16[64,128]{1,0:T(8,128)(2,1)S(1)} collective-permute-done((bf16[64,128]{1,0:T(8,128)(2,1)S(1)}, bf16[64,128]{1,0:T(8,128)(2,1)S(1)}, u32[]{:S(2)}, u32[]{:S(2)}) %collective-permute-start.1) | collective-permute-done | bytes 16416 | tf_op jit(solution)/shard_map/ppermute | solution.py:23
  18.6 0.0 collective-permute-done.rows
  18.6 0.0 collective-permute-done.2.other
  18.6 0.8 %collective-permute-start.3 = (bf16[64,2176]{1,0:T(8,128)(2,1)S(1)}, bf16[64,2176]{1,0:T(8,128)(2,1)S(1)}, u32[]{:S(2)}, u32[]{:S(2)}) collective-permute-start(bf16[64,2176]{1,0:T(8,128)(2,1)S(1)} %shard_map.47.refs_0_), channel_id=1, source_target_pairs={{0,4},{1,5},{2,6},{3,7},{4,0},{5,1},{6,2},{7,3},{8,12},{9,13},{10,... | collective-permute-start | bytes 835592 | tf_op jit(solution)/shard_map/ppermute | solution.py:23
  19.3 1.5 %collective-permute-start.7 = (bf16[64,2176]{1,0:T(8,128)(2,1)S(1)}, bf16[64,2176]{1,0:T(8,128)(2,1)S(1)}, u32[]{:S(2)}, u32[]{:S(2)}) collective-permute-start(bf16[64,2176]{1,0:T(8,128)(2,1)S(1)} %shard_map.47.refs_0_), channel_id=1, source_target_pairs={{0,2},{1,3},{2,0},{3,1},{4,6},{5,7},{6,4},{7,5},{8,10},{9,11},{10,... | collective-permute-start | bytes 835592 | tf_op jit(solution)/shard_map/ppermute | solution.py:23
  20.8 0.0 copy-done.1
  20.8 2.0 %shard_map.48 = bf16[2,64,768]{2,1,0:T(8,128)(2,1)S(1)} custom-call(bf16[768,2048]{1,0:T(8,128)(2,1)S(1)} %bitcast.11, bf16[768,2048]{1,0:T(8,128)(2,1)S(1)} %collective-permute-done.2.other, bf16[64,2176]{1,0:T(8,128)(2,1)S(1)} %shard_map.47.refs_0_), custom_call_target="tpu_custom_call" | custom-call | flops 4026531840 | bytes 6750208 | tf_op jit(solution)/shard_map/pallas_call | solution.py:99
  22.9 3.5 %collective-permute-start.8 = (bf16[2,64,768]{2,1,0:T(8,128)(2,1)S(1)}, bf16[2,64,768]{2,1,0:T(8,128)(2,1)S(1)}, u32[]{:S(2)}, u32[]{:S(2)}) collective-permute-start(bf16[2,64,768]{2,1,0:T(8,128)(2,1)S(1)} %shard_map.48), channel_id=1, source_target_pairs={{0,8},{1,9},{2,10},{3,11},{4,12},{5,13},{6,14},{7,15},{8,0},{9,1},... | collective-permute-start | bytes 589832 | tf_op jit(solution)/shard_map/ppermute | solution.py:23
  26.3 0.0 collective-permute-done.4.rows
  26.4 0.1 collective-permute-start.5
  26.5 0.5 collective-permute-start.10
  27.0 2.2 %collective-permute-done.3.refs_0_ = bf16[64,2176]{1,0:T(8,128)(2,1)S(1)} collective-permute-done((bf16[64,2176]{1,0:T(8,128)(2,1)S(1)}, bf16[64,2176]{1,0:T(8,128)(2,1)S(1)}, u32[]{:S(2)}, u32[]{:S(2)}) %collective-permute-start.3) | collective-permute-done | bytes 278560 | tf_op jit(solution)/shard_map/ppermute | solution.py:23
  29.2 3.7 %collective-permute-start.6 = (bf16[64,2176]{1,0:T(8,128)(2,1)S(1)}, bf16[64,2176]{1,0:T(8,128)(2,1)S(1)}, u32[]{:S(2)}, u32[]{:S(2)}) collective-permute-start(bf16[64,2176]{1,0:T(8,128)(2,1)S(1)} %collective-permute-done.3.refs_0_), channel_id=1, source_target_pairs={{0,2},{1,3},{2,0},{3,1},{4,6},{5,7},{6,4},{7,5},{8,10},{9,11},{10,... | collective-permute-start | bytes 835592 | tf_op jit(solution)/shard_map/ppermute | solution.py:23
  32.9 2.0 %shard_map.50 = bf16[2,64,768]{2,1,0:T(8,128)(2,1)S(1)} custom-call(bf16[768,2048]{1,0:T(8,128)(2,1)S(1)} %bitcast.12, bf16[768,2048]{1,0:T(8,128)(2,1)S(1)} %collective-permute-done.2.other, bf16[64,2176]{1,0:T(8,128)(2,1)S(1)} %collective-permute-done.3.refs_0_), custom_call_target="tpu_custom_call" | custom-call | flops 4026531840 | bytes 6750208 | tf_op jit(solution)/shard_map/pallas_call | solution.py:99
  34.9 0.3 collective-permute-done.8.refs_4_
  35.2 3.1 %collective-permute-start.15 = (bf16[2,64,768]{2,1,0:T(8,128)(2,1)S(1)}, bf16[2,64,768]{2,1,0:T(8,128)(2,1)S(1)}, u32[]{:S(2)}, u32[]{:S(2)}) collective-permute-start(bf16[2,64,768]{2,1,0:T(8,128)(2,1)S(1)} %shard_map.50), channel_id=1, source_target_pairs={{0,12},{1,13},{2,14},{3,15},{4,8},{5,9},{6,10},{7,11},{8,4},{9,5},... | collective-permute-start | bytes 589832 | tf_op jit(solution)/shard_map/ppermute | solution.py:23
  38.3 0.0 collective-permute-done.7.refs_0_
  38.3 2.0 %shard_map.51 = bf16[2,64,768]{2,1,0:T(8,128)(2,1)S(1)} custom-call(bf16[768,2048]{1,0:T(8,128)(2,1)S(1)} %bitcast.13, bf16[768,2048]{1,0:T(8,128)(2,1)S(1)} %collective-permute-done.2.other, bf16[64,2176]{1,0:T(8,128)(2,1)S(1)} %collective-permute-done.7.refs_0_), custom_call_target="tpu_custom_call" | custom-call | flops 4026531840 | bytes 6750208 | tf_op jit(solution)/shard_map/pallas_call | solution.py:99
  40.3 0.1 collective-permute-start.14
  40.4 0.0 collective-permute-done.5.refs_1_
  40.4 0.0 collective-permute-done.6.refs_0_
  40.4 0.7 %collective-permute-start.9 = (bf16[64,2176]{1,0:T(8,128)(2,1)S(1)}, bf16[64,2176]{1,0:T(8,128)(2,1)S(1)}, u32[]{:S(2)}, u32[]{:S(2)}) collective-permute-start(bf16[64,2176]{1,0:T(8,128)(2,1)S(1)} %collective-permute-done.5.refs_1_), channel_id=1, source_target_pairs={{0,2},{1,3},{2,0},{3,1},{4,6},{5,7},{6,4},{7,5},{8,10},{9,11},{10,... | collective-permute-start | bytes 835592 | tf_op jit(solution)/shard_map/ppermute | solution.py:23
  41.1 2.0 %shard_map.52 = bf16[2,64,768]{2,1,0:T(8,128)(2,1)S(1)} custom-call(bf16[768,2048]{1,0:T(8,128)(2,1)S(1)} %bitcast.14, bf16[768,2048]{1,0:T(8,128)(2,1)S(1)} %collective-permute-done.2.other, bf16[64,2176]{1,0:T(8,128)(2,1)S(1)} %collective-permute-done.6.refs_0_), custom_call_target="tpu_custom_call" | custom-call | flops 4026531840 | bytes 6750208 | tf_op jit(solution)/shard_map/pallas_call | solution.py:99
  43.1 3.8 %collective-permute-start.16 = (bf16[2,64,768]{2,1,0:T(8,128)(2,1)S(1)}, bf16[2,64,768]{2,1,0:T(8,128)(2,1)S(1)}, u32[]{:S(2)}, u32[]{:S(2)}) collective-permute-start(bf16[2,64,768]{2,1,0:T(8,128)(2,1)S(1)} %shard_map.52), channel_id=1, source_target_pairs={{0,14},{1,15},{2,12},{3,13},{4,10},{5,11},{6,8},{7,9},{8,6},{9,7},... | collective-permute-start | bytes 589832 | tf_op jit(solution)/shard_map/ppermute | solution.py:23
  47.0 0.0 collective-permute-done.10.refs_0_
  47.0 2.2 %shard_map.53 = (bf16[2,64,768]{2,1,0:T(8,128)(2,1)S(1)}, bf16[2,64,768]{2,1,0:T(8,128)(2,1)S(1)}) custom-call(bf16[768,2048]{1,0:T(8,128)(2,1)S(1)} %bitcast.15, bf16[768,2048]{1,0:T(8,128)(2,1)S(1)} %collective-permute-done.2.other, bf16[64,2176]{1,0:T(8,128)(2,1)S(1)} %collective-permute-done.10.refs_0_, bf16[64,2176]{1,0:T(8,128)(2,1)S(1)} %collective-permute-done.5.refs_1_), custom_call_target="tpu_custom_call" | custom-call | flops 8053063680 | bytes 7208960 | tf_op jit(solution)/shard_map/pallas_call | solution.py:99
  49.2 2.1 %collective-permute-start.11 = (bf16[2,64,768]{2,1,0:T(8,128)(2,1)S(1)}, bf16[2,64,768]{2,1,0:T(8,128)(2,1)S(1)}, u32[]{:S(2)}, u32[]{:S(2)}) collective-permute-start(bf16[2,64,768]{2,1,0:T(8,128)(2,1)S(1)} %get-tuple-element.37), channel_id=1, source_target_pairs={{0,2},{1,3},{2,0},{3,1},{4,6},{5,7},{6,4},{7,5},{8,10},{9,11},{10,... | collective-permute-start | bytes 589832 | tf_op jit(solution)/shard_map/ppermute | solution.py:23
  51.2 0.0 collective-permute-done.9.refs_0_
  51.3 3.5 %collective-permute-start.12 = (bf16[2,64,768]{2,1,0:T(8,128)(2,1)S(1)}, bf16[2,64,768]{2,1,0:T(8,128)(2,1)S(1)}, u32[]{:S(2)}, u32[]{:S(2)}) collective-permute-start(bf16[2,64,768]{2,1,0:T(8,128)(2,1)S(1)} %get-tuple-element.34), channel_id=1, source_target_pairs={{0,4},{1,5},{2,6},{3,7},{4,0},{5,1},{6,2},{7,3},{8,12},{9,13},{10,... | collective-permute-start | bytes 589832 | tf_op jit(solution)/shard_map/ppermute | solution.py:23
  54.7 2.0 %shard_map.54 = bf16[2,64,768]{2,1,0:T(8,128)(2,1)S(1)} custom-call(bf16[768,2048]{1,0:T(8,128)(2,1)S(1)} %bitcast.16, bf16[768,2048]{1,0:T(8,128)(2,1)S(1)} %collective-permute-done.2.other, bf16[64,2176]{1,0:T(8,128)(2,1)S(1)} %collective-permute-done.9.refs_0_), custom_call_target="tpu_custom_call" | custom-call | flops 4026531840 | bytes 6750208 | tf_op jit(solution)/shard_map/pallas_call | solution.py:99
  56.8 0.8 %collective-permute-done.14.refs_5_ = bf16[2,64,768]{2,1,0:T(8,128)(2,1)S(1)} collective-permute-done((bf16[2,64,768]{2,1,0:T(8,128)(2,1)S(1)}, bf16[2,64,768]{2,1,0:T(8,128)(2,1)S(1)}, u32[]{:S(2)}, u32[]{:S(2)}) %collective-permute-start.14) | collective-permute-done | bytes 196640 | tf_op jit(solution)/shard_map/ppermute | solution.py:23
  57.5 0.0 collective-permute-start.13
  57.5 2.0 %shard_map.55.refs_0_ = bf16[2,64,768]{2,1,0:T(8,128)(2,1)S(1)} custom-call(bf16[768,2048]{1,0:T(8,128)(2,1)S(1)} %bitcast.17, bf16[768,2048]{1,0:T(8,128)(2,1)S(1)} %collective-permute-done.2.other, bf16[64,2176]{1,0:T(8,128)(2,1)S(1)} %shard_map.49.refs_0_), custom_call_target="tpu_custom_call" | custom-call | flops 4026531840 | bytes 6750208 | tf_op jit(solution)/shard_map/pallas_call | solution.py:99
  59.6 0.0 collective-permute-done.15.refs_6_
  59.6 2.0 %collective-permute-done.11.refs_1_ = bf16[2,64,768]{2,1,0:T(8,128)(2,1)S(1)} collective-permute-done((bf16[2,64,768]{2,1,0:T(8,128)(2,1)S(1)}, bf16[2,64,768]{2,1,0:T(8,128)(2,1)S(1)}, u32[]{:S(2)}, u32[]{:S(2)}) %collective-permute-start.11) | collective-permute-done | bytes 196640 | tf_op jit(solution)/shard_map/ppermute | solution.py:23
  61.6 0.0 collective-permute-done.12.refs_2_
  61.6 0.0 collective-permute-done.16.refs_7_
  61.6 4.1 %collective-permute-done.13.refs_3_ = bf16[2,64,768]{2,1,0:T(8,128)(2,1)S(1)} collective-permute-done((bf16[2,64,768]{2,1,0:T(8,128)(2,1)S(1)}, bf16[2,64,768]{2,1,0:T(8,128)(2,1)S(1)}, u32[]{:S(2)}, u32[]{:S(2)}) %collective-permute-start.13) | collective-permute-done | bytes 196640 | tf_op jit(solution)/shard_map/ppermute | solution.py:23
  65.7 1.3 %shard_map.56 = bf16[512,768]{1,0:T(8,128)(2,1)} custom-call(s32[8,64]{1,0:T(8,128)S(1)} %bitcast.19, bf16[2,64,768]{2,1,0:T(8,128)(2,1)S(1)} %shard_map.55.refs_0_, bf16[2,64,768]{2,1,0:T(8,128)(2,1)S(1)} %collective-permute-done.11.refs_1_, bf16[2,64,768]{2,1,0:T(8,128)(2,1)S(1)} %collective-permute-done.12.refs_2_, ...), custom_call_target="tpu_custom_call" | custom-call | tf_op jit(solution)/shard_map/pallas_call | solution.py:134
  (2 shorter events, 0.0 us)
Async XLA Ops:
  0.0 18.6 %collective-permute-start.2 = (bf16[768,2048]{1,0:T(8,128)(2,1)}, bf16[768,2048]{1,0:T(8,128)(2,1)S(1)}, u32[]{:S(2)}, u32[]{:S(2)}) collective-permute-start(bf16[768,2048]{1,0:T(8,128)(2,1)} %bitcast.9), channel_id=1, source_target_pairs={{0,1},{1,0},{2,3},{3,2},{4,5},{5,4},{6,7},{7,6},{8,9},{9,8},{10,11... | collective-permute-start | bytes 9437192 | tf_op jit(solution)/shard_map/ppermute | solution.py:23
  0.5 18.1 %collective-permute-start = (bf16[64,2048]{1,0:T(8,128)(2,1)}, bf16[64,2048]{1,0:T(8,128)(2,1)S(1)}, u32[]{:S(2)}, u32[]{:S(2)}) collective-permute-start(bf16[64,2048]{1,0:T(8,128)(2,1)} %bitcast.21), channel_id=1, source_target_pairs={{0,24},{1,25},{2,26},{3,27},{4,28},{5,29},{6,30},{7,31},{8,16},{9,... | collective-permute-start | bytes 786440 | tf_op jit(solution)/shard_map/ppermute | solution.py:33
  5.0 1.9 %copy-start = (bf16[1,1,768,2048]{3,2,1,0:T(8,128)(2,1)S(1)}, bf16[1,1,768,2048]{3,2,1,0:T(8,128)(2,1)}, u32[]{:S(2)}) copy-start(bf16[1,1,768,2048]{3,2,1,0:T(8,128)(2,1)} %param.7) | copy-start | bytes 9437188
  6.9 0.7 %copy-start.2 = (s32[1,64,8]{1,2,0:T(8,128)S(1)}, s32[1,64,8]{1,2,0:T(8,128)}, u32[]{:S(2)}) copy-start(s32[1,64,8]{1,2,0:T(8,128)} %param.5) | copy-start | bytes 6148
  7.6 0.7 %copy-start.3 = (bf16[1,64,8]{1,2,0:T(8,128)(2,1)S(1)}, bf16[1,64,8]{1,2,0:T(8,128)(2,1)}, u32[]{:S(2)}) copy-start(bf16[1,64,8]{1,2,0:T(8,128)(2,1)} %param.6) | copy-start | bytes 3076
  8.3 12.6 %copy-start.1 = (bf16[1,1,768,2048]{3,2,1,0:T(8,128)(2,1)S(1)}, bf16[1,1,768,2048]{3,2,1,0:T(8,128)(2,1)}, u32[]{:S(2)}) copy-start(bf16[1,1,768,2048]{3,2,1,0:T(8,128)(2,1)} %param.7) | copy-start | bytes 9437188
  8.4 10.2 %collective-permute-start.1 = (bf16[64,128]{1,0:T(8,128)(2,1)S(1)}, bf16[64,128]{1,0:T(8,128)(2,1)S(1)}, u32[]{:S(2)}, u32[]{:S(2)}) collective-permute-start(bf16[64,128]{1,0:T(8,128)(2,1)S(1)} %shard_map.46.columns), channel_id=1, source_target_pairs={{0,8},{1,9},{2,10},{3,11},{4,12},{5,13},{6,14},{7,15},{8,0},{9,1},... | collective-permute-start | bytes 49160 | tf_op jit(solution)/shard_map/ppermute | solution.py:23
  8.7 17.6 %collective-permute-start.4 = (bf16[64,2048]{1,0:T(8,128)(2,1)}, bf16[64,2048]{1,0:T(8,128)(2,1)S(1)}, u32[]{:S(2)}, u32[]{:S(2)}) collective-permute-start(bf16[64,2048]{1,0:T(8,128)(2,1)} %bitcast.22), channel_id=1, source_target_pairs={{0,16},{1,17},{2,18},{3,19},{4,20},{5,21},{6,22},{7,23},{8,24},{9,... | collective-permute-start | bytes 786440 | tf_op jit(solution)/shard_map/ppermute | solution.py:33
  18.6 10.6 %collective-permute-start.3 = (bf16[64,2176]{1,0:T(8,128)(2,1)S(1)}, bf16[64,2176]{1,0:T(8,128)(2,1)S(1)}, u32[]{:S(2)}, u32[]{:S(2)}) collective-permute-start(bf16[64,2176]{1,0:T(8,128)(2,1)S(1)} %shard_map.47.refs_0_), channel_id=1, source_target_pairs={{0,4},{1,5},{2,6},{3,7},{4,0},{5,1},{6,2},{7,3},{8,12},{9,13},{10,... | collective-permute-start | bytes 835592 | tf_op jit(solution)/shard_map/ppermute | solution.py:23
  19.3 19.0 %collective-permute-start.7 = (bf16[64,2176]{1,0:T(8,128)(2,1)S(1)}, bf16[64,2176]{1,0:T(8,128)(2,1)S(1)}, u32[]{:S(2)}, u32[]{:S(2)}) collective-permute-start(bf16[64,2176]{1,0:T(8,128)(2,1)S(1)} %shard_map.47.refs_0_), channel_id=1, source_target_pairs={{0,2},{1,3},{2,0},{3,1},{4,6},{5,7},{6,4},{7,5},{8,10},{9,11},{10,... | collective-permute-start | bytes 835592 | tf_op jit(solution)/shard_map/ppermute | solution.py:23
  22.9 12.4 %collective-permute-start.8 = (bf16[2,64,768]{2,1,0:T(8,128)(2,1)S(1)}, bf16[2,64,768]{2,1,0:T(8,128)(2,1)S(1)}, u32[]{:S(2)}, u32[]{:S(2)}) collective-permute-start(bf16[2,64,768]{2,1,0:T(8,128)(2,1)S(1)} %shard_map.48), channel_id=1, source_target_pairs={{0,8},{1,9},{2,10},{3,11},{4,12},{5,13},{6,14},{7,15},{8,0},{9,1},... | collective-permute-start | bytes 589832 | tf_op jit(solution)/shard_map/ppermute | solution.py:23
  26.4 14.1 %collective-permute-start.5 = (bf16[64,2176]{1,0:T(8,128)(2,1)S(1)}, bf16[64,2176]{1,0:T(8,128)(2,1)S(1)}, u32[]{:S(2)}, u32[]{:S(2)}) collective-permute-start(bf16[64,2176]{1,0:T(8,128)(2,1)S(1)} %shard_map.49.refs_0_), channel_id=1, source_target_pairs={{0,4},{1,5},{2,6},{3,7},{4,0},{5,1},{6,2},{7,3},{8,12},{9,13},{10,... | collective-permute-start | bytes 835592 | tf_op jit(solution)/shard_map/ppermute | solution.py:23
  26.5 20.5 %collective-permute-start.10 = (bf16[64,2176]{1,0:T(8,128)(2,1)S(1)}, bf16[64,2176]{1,0:T(8,128)(2,1)S(1)}, u32[]{:S(2)}, u32[]{:S(2)}) collective-permute-start(bf16[64,2176]{1,0:T(8,128)(2,1)S(1)} %shard_map.49.refs_0_), channel_id=1, source_target_pairs={{0,2},{1,3},{2,0},{3,1},{4,6},{5,7},{6,4},{7,5},{8,10},{9,11},{10,... | collective-permute-start | bytes 835592 | tf_op jit(solution)/shard_map/ppermute | solution.py:23
  29.2 11.2 %collective-permute-start.6 = (bf16[64,2176]{1,0:T(8,128)(2,1)S(1)}, bf16[64,2176]{1,0:T(8,128)(2,1)S(1)}, u32[]{:S(2)}, u32[]{:S(2)}) collective-permute-start(bf16[64,2176]{1,0:T(8,128)(2,1)S(1)} %collective-permute-done.3.refs_0_), channel_id=1, source_target_pairs={{0,2},{1,3},{2,0},{3,1},{4,6},{5,7},{6,4},{7,5},{8,10},{9,11},{10,... | collective-permute-start | bytes 835592 | tf_op jit(solution)/shard_map/ppermute | solution.py:23
  35.2 24.3 %collective-permute-start.15 = (bf16[2,64,768]{2,1,0:T(8,128)(2,1)S(1)}, bf16[2,64,768]{2,1,0:T(8,128)(2,1)S(1)}, u32[]{:S(2)}, u32[]{:S(2)}) collective-permute-start(bf16[2,64,768]{2,1,0:T(8,128)(2,1)S(1)} %shard_map.50), channel_id=1, source_target_pairs={{0,12},{1,13},{2,14},{3,15},{4,8},{5,9},{6,10},{7,11},{8,4},{9,5},... | collective-permute-start | bytes 589832 | tf_op jit(solution)/shard_map/ppermute | solution.py:23
  40.3 17.2 %collective-permute-start.14 = (bf16[2,64,768]{2,1,0:T(8,128)(2,1)S(1)}, bf16[2,64,768]{2,1,0:T(8,128)(2,1)S(1)}, u32[]{:S(2)}, u32[]{:S(2)}) collective-permute-start(bf16[2,64,768]{2,1,0:T(8,128)(2,1)S(1)} %shard_map.51), channel_id=1, source_target_pairs={{0,10},{1,11},{2,8},{3,9},{4,14},{5,15},{6,12},{7,13},{8,2},{9,3},... | collective-permute-start | bytes 589832 | tf_op jit(solution)/shard_map/ppermute | solution.py:23
  40.4 10.8 %collective-permute-start.9 = (bf16[64,2176]{1,0:T(8,128)(2,1)S(1)}, bf16[64,2176]{1,0:T(8,128)(2,1)S(1)}, u32[]{:S(2)}, u32[]{:S(2)}) collective-permute-start(bf16[64,2176]{1,0:T(8,128)(2,1)S(1)} %collective-permute-done.5.refs_1_), channel_id=1, source_target_pairs={{0,2},{1,3},{2,0},{3,1},{4,6},{5,7},{6,4},{7,5},{8,10},{9,11},{10,... | collective-permute-start | bytes 835592 | tf_op jit(solution)/shard_map/ppermute | solution.py:23
  43.1 18.4 %collective-permute-start.16 = (bf16[2,64,768]{2,1,0:T(8,128)(2,1)S(1)}, bf16[2,64,768]{2,1,0:T(8,128)(2,1)S(1)}, u32[]{:S(2)}, u32[]{:S(2)}) collective-permute-start(bf16[2,64,768]{2,1,0:T(8,128)(2,1)S(1)} %shard_map.52), channel_id=1, source_target_pairs={{0,14},{1,15},{2,12},{3,13},{4,10},{5,11},{6,8},{7,9},{8,6},{9,7},... | collective-permute-start | bytes 589832 | tf_op jit(solution)/shard_map/ppermute | solution.py:23
  49.2 12.4 %collective-permute-start.11 = (bf16[2,64,768]{2,1,0:T(8,128)(2,1)S(1)}, bf16[2,64,768]{2,1,0:T(8,128)(2,1)S(1)}, u32[]{:S(2)}, u32[]{:S(2)}) collective-permute-start(bf16[2,64,768]{2,1,0:T(8,128)(2,1)S(1)} %get-tuple-element.37), channel_id=1, source_target_pairs={{0,2},{1,3},{2,0},{3,1},{4,6},{5,7},{6,4},{7,5},{8,10},{9,11},{10,... | collective-permute-start | bytes 589832 | tf_op jit(solution)/shard_map/ppermute | solution.py:23
  51.3 10.3 %collective-permute-start.12 = (bf16[2,64,768]{2,1,0:T(8,128)(2,1)S(1)}, bf16[2,64,768]{2,1,0:T(8,128)(2,1)S(1)}, u32[]{:S(2)}, u32[]{:S(2)}) collective-permute-start(bf16[2,64,768]{2,1,0:T(8,128)(2,1)S(1)} %get-tuple-element.34), channel_id=1, source_target_pairs={{0,4},{1,5},{2,6},{3,7},{4,0},{5,1},{6,2},{7,3},{8,12},{9,13},{10,... | collective-permute-start | bytes 589832 | tf_op jit(solution)/shard_map/ppermute | solution.py:23
  57.5 8.1 %collective-permute-start.13 = (bf16[2,64,768]{2,1,0:T(8,128)(2,1)S(1)}, bf16[2,64,768]{2,1,0:T(8,128)(2,1)S(1)}, u32[]{:S(2)}, u32[]{:S(2)}) collective-permute-start(bf16[2,64,768]{2,1,0:T(8,128)(2,1)S(1)} %shard_map.54), channel_id=1, source_target_pairs={{0,6},{1,7},{2,4},{3,5},{4,2},{5,3},{6,0},{7,1},{8,14},{9,15},{10,... | collective-permute-start | bytes 589832 | tf_op jit(solution)/shard_map/ppermute | solution.py:23

commit v14 on v13

--- a/solution.py
+++ b/solution.py
@@ -108,34 +108,40 @@
     )(weight, other, *operands)
 
 
-def pick_kernel(ids, *refs):
-    blocks, out = refs[:-1], refs[-1]
+def pick_kernel(flips, ids, *refs):
+    blocks, kept, out = refs[: len(flips)], refs[len(flips) : -1], refs[-1]
     experts, tokens, _ = blocks[0].shape
     top = ids.shape[0]
     span = 16
     chip = lax.div(lax.axis_index("expert"), CORES)
-    label = (lax.div(ids[...], CORES) ^ chip) * CORES + lax.rem(ids[...], CORES)
+    flip = lax.div(ids[...], CORES) ^ chip
+    place = jnp.full(flip.shape, -1, jnp.int32)
+    for j, known in enumerate(flips):
+        place = jnp.where(flip == known, j * CORES + lax.rem(ids[...], CORES), place)
     column = lax.broadcasted_iota(jnp.int32, (top, len(blocks) * experts * span), 1)
     for g in range(tokens // span):
         stacked = jnp.concatenate(
             [b[c, g * span : (g + 1) * span, :] for b in blocks for c in range(experts)], axis=0
         )
         picks = [
-            jnp.where(column == label[:, g * span + t : g * span + t + 1] * span + t, 1.0, 0.0)
+            jnp.where(column == place[:, g * span + t : g * span + t + 1] * span + t, 1.0, 0.0)
             for t in range(span)
         ]
         pick = jnp.concatenate(picks, axis=0).astype(jnp.bfloat16)
-        rows = jnp.dot(pick, stacked, preferred_element_type=jnp.float32)
-        out[g * span * top : (g + 1) * span * top, :] = rows.astype(jnp.bfloat16)
-
-
-def pick_routes(ids, blocks):
+        rows = jnp.dot(pick, stacked, preferred_element_type=jnp.float32).astype(jnp.bfloat16)
+        part = slice(g * span * top, (g + 1) * span * top)
+        out[part, :] = rows + kept[0][part, :] if kept else rows
+
+
+def pick_routes(ids, received, *kept):
     top, tokens = ids.shape
-    return pl.pallas_call(
-        pick_kernel,
+    flips = sorted(received)
+    blocks = [received[flip] for flip in flips]
+    return pl.pallas_call(
+        functools.partial(pick_kernel, flips),
         out_shape=jax.ShapeDtypeStruct((top * tokens, blocks[0].shape[2]), jnp.bfloat16),
         compiler_params=pltpu.CompilerParams(vmem_limit_bytes=16 << 20),
-    )(ids, *blocks)
+    )(ids, *blocks, *kept)
 
 
 def dense_device(upstream, route_ids, route_gates, weight_mat):
@@ -160,38 +166,34 @@
     rows, columns, _ = tie((rows, columns, out_far))
     rows = widened(rows, columns)
     near = send(rows, owners, Z_NEAR)
-    side = send(rows, owners, X)
     cross, rows = tie((cross, rows))
     cross_side = send(cross, owners, X)
-    (out_cross,) = work(cross)
+    far_side, _ = tie((far_side, cross))
+    out_cross, out_far_side = work(cross, far_side)
     back_cross = send(out_cross, owners, Z_NEAR ^ Z_FAR)
-    far_side, back_far, _ = tie((far_side, back_far, out_cross))
-    (out_far_side,) = work(far_side)
     back_far_side = send(out_far_side, owners, X ^ Z_FAR)
-    near, cross_side, _ = tie((near, cross_side, out_far_side))
+    near, _ = tie((near, out_cross))
     near_side = send(near, owners, X)
+    side = send(tie((rows, near))[0], owners, X)
+    cross_side, back_far, _ = tie((cross_side, back_far, near))
     (out_cross_side,) = work(cross_side)
     back_cross_side = send(out_cross_side, owners, X ^ Z_NEAR ^ Z_FAR)
-    side, near, _ = tie((side, near, out_cross_side))
-    out_side, out_near = work(side, near)
+    rows, _ = tie((rows, out_cross_side))
+    (out_own,) = work(rows)
+    side, near, near_side, _ = tie((side, near, near_side, out_own))
+    out_side, out_near, out_near_side = work(side, near, near_side)
     back_side = send(out_side, owners, X)
     back_near = send(out_near, owners, Z_NEAR)
-    near_side, _ = tie((near_side, out_near))
-    (out_near_side,) = work(near_side)
     back_near_side = send(out_near_side, owners, X ^ Z_NEAR)
-    rows, _ = tie((rows, out_near_side))
-    (out_own,) = work(rows)
-    received = {
+    far_parts = {
         0: out_own,
-        X: back_side,
-        Z_NEAR: back_near,
-        X ^ Z_NEAR: back_near_side,
         Z_FAR: back_far,
         X ^ Z_FAR: back_far_side,
         Z_NEAR ^ Z_FAR: back_cross,
         X ^ Z_NEAR ^ Z_FAR: back_cross_side,
     }
-    out = pick_routes(route_ids.T, [received[flip] for flip in sorted(received)])
+    near_parts = {X: back_side, Z_NEAR: back_near, X ^ Z_NEAR: back_near_side}
+    out = pick_routes(route_ids.T, near_parts, pick_routes(route_ids.T, far_parts))
     return out.reshape(1, tokens, top, weight_mat.shape[0])
 
 

time: 67.2 us -> 79.7 us (1.19)
  the two profiles are of different devices: /device:TPU:0 before, /device:TPU:12 now
where the time goes in v14:
time: 79.7 us; the launch traced here: 79.5 us
  waiting for transfers between devices  34.3 us (43%)
  starting transfers between devices  29.5 us (37%)
  Pallas kernels  12.3 us (15%)
  local copies, waits for them, and re-layouts  3.26 us (4%)
    ppermute x15, waiting for transfers between devices, send(): return lax.ppermute(block, 'expert', route)  34.3 us
    ppermute x15, starting transfers between devices, send(): return lax.ppermute(block, 'expert', route)  25.5 us
    pallas_call x5, Pallas kernels, products(): pl.pallas_call(functools.partial(products_kernel, paired), out_shape=[jax...  10.4 us
    ppermute x2, starting transfers between devices, send_across(): return lax.ppermute(block, ('pipe', 'expert'), route)  4.05 us
    unnamed x8, local copies, waits for them, and re-layouts  3.26 us
    pallas_call x2, Pallas kernels, pick_routes(): pl.pallas_call(functools.partial(pick_kernel, flips), out_shape=jax.Shape...  1.75 us
  transfers between devices with their start and end apart: 17, of which 6 were waited for; matrix products, arithmetic and copies ran while one was open for 0% of the time, Pallas kernels for 14%

profile of v14, /device:TPU:12, one launch (start us, length us, event | category | flops | bytes accessed | tf_op | source)
XLA Modules:
  0.0 79.5 jit_solution(7612593905004997620)
XLA Ops:
  0.0 0.0 collective-permute-start.2
  0.0 2.5 %collective-permute-start = (bf16[64,2048]{1,0:T(8,128)(2,1)}, bf16[64,2048]{1,0:T(8,128)(2,1)S(1)}, u32[]{:S(2)}, u32[]{:S(2)}) collective-permute-start(bf16[64,2048]{1,0:T(8,128)(2,1)} %bitcast.20), channel_id=1, source_target_pairs={{0,24},{1,25},{2,26},{3,27},{4,28},{5,29},{6,30},{7,31},{8,16},{9,... | collective-permute-start | bytes 786440 | tf_op jit(solution)/shard_map/ppermute | solution.py:33
  2.5 0.0 copy-start
  2.5 1.9 %copy-done = bf16[1,1,768,2048]{3,2,1,0:T(8,128)(2,1)S(1)} copy-done((bf16[1,1,768,2048]{3,2,1,0:T(8,128)(2,1)S(1)}, bf16[1,1,768,2048]{3,2,1,0:T(8,128)(2,1)}, u32[]{:S(2)}) %copy-start) | copy-done | bytes 3145752
  4.4 0.0 copy-start.2
  4.4 0.7 copy-done.2
  5.1 0.0 copy-start.3
  5.1 0.7 copy-done.3
  5.8 0.0 copy-start.1
  5.8 0.1 shard_map.46.columns
  5.9 0.4 collective-permute-start.1
  6.3 1.5 %collective-permute-start.4 = (bf16[64,2048]{1,0:T(8,128)(2,1)}, bf16[64,2048]{1,0:T(8,128)(2,1)S(1)}, u32[]{:S(2)}, u32[]{:S(2)}) collective-permute-start(bf16[64,2048]{1,0:T(8,128)(2,1)} %bitcast.21), channel_id=1, source_target_pairs={{0,16},{1,17},{2,18},{3,19},{4,20},{5,21},{6,22},{7,23},{8,24},{9,... | collective-permute-start | bytes 786440 | tf_op jit(solution)/shard_map/ppermute | solution.py:33
  7.8 7.4 %collective-permute-done.1.columns = bf16[64,128]{1,0:T(8,128)(2,1)S(1)} collective-permute-done((bf16[64,128]{1,0:T(8,128)(2,1)S(1)}, bf16[64,128]{1,0:T(8,128)(2,1)S(1)}, u32[]{:S(2)}, u32[]{:S(2)}) %collective-permute-start.1) | collective-permute-done | bytes 16416 | tf_op jit(solution)/shard_map/ppermute | solution.py:23
  15.2 0.0 collective-permute-done.rows
  15.2 0.0 collective-permute-done.2.other
  15.2 2.2 %collective-permute-start.3 = (bf16[64,2176]{1,0:T(8,128)(2,1)S(1)}, bf16[64,2176]{1,0:T(8,128)(2,1)S(1)}, u32[]{:S(2)}, u32[]{:S(2)}) collective-permute-start(bf16[64,2176]{1,0:T(8,128)(2,1)S(1)} %shard_map.47.refs_0_), channel_id=1, source_target_pairs={{0,4},{1,5},{2,6},{3,7},{4,0},{5,1},{6,2},{7,3},{8,12},{9,13},{10,... | collective-permute-start | bytes 835592 | tf_op jit(solution)/shard_map/ppermute | solution.py:23
  17.4 1.5 %collective-permute-start.6 = (bf16[64,2176]{1,0:T(8,128)(2,1)S(1)}, bf16[64,2176]{1,0:T(8,128)(2,1)S(1)}, u32[]{:S(2)}, u32[]{:S(2)}) collective-permute-start(bf16[64,2176]{1,0:T(8,128)(2,1)S(1)} %shard_map.47.refs_0_), channel_id=1, source_target_pairs={{0,2},{1,3},{2,0},{3,1},{4,6},{5,7},{6,4},{7,5},{8,10},{9,11},{10,... | collective-permute-start | bytes 835592 | tf_op jit(solution)/shard_map/ppermute | solution.py:23
  18.9 0.0 copy-done.1
  18.9 2.0 %shard_map.48 = bf16[2,64,768]{2,1,0:T(8,128)(2,1)S(1)} custom-call(bf16[768,2048]{1,0:T(8,128)(2,1)S(1)} %bitcast.11, bf16[768,2048]{1,0:T(8,128)(2,1)S(1)} %collective-permute-done.2.other, bf16[64,2176]{1,0:T(8,128)(2,1)S(1)} %shard_map.47.refs_0_), custom_call_target="tpu_custom_call" | custom-call | flops 4026531840 | bytes 6750208 | tf_op jit(solution)/shard_map/pallas_call | solution.py:99
  21.0 2.1 %collective-permute-start.10 = (bf16[2,64,768]{2,1,0:T(8,128)(2,1)S(1)}, bf16[2,64,768]{2,1,0:T(8,128)(2,1)S(1)}, u32[]{:S(2)}, u32[]{:S(2)}) collective-permute-start(bf16[2,64,768]{2,1,0:T(8,128)(2,1)S(1)} %shard_map.48), channel_id=1, source_target_pairs={{0,8},{1,9},{2,10},{3,11},{4,12},{5,13},{6,14},{7,15},{8,0},{9,1},... | collective-permute-start | bytes 589832 | tf_op jit(solution)/shard_map/ppermute | solution.py:23
  23.0 0.0 collective-permute-done.4.rows
  23.1 2.0 %collective-permute-start.5 = (bf16[64,2176]{1,0:T(8,128)(2,1)S(1)}, bf16[64,2176]{1,0:T(8,128)(2,1)S(1)}, u32[]{:S(2)}, u32[]{:S(2)}) collective-permute-start(bf16[64,2176]{1,0:T(8,128)(2,1)S(1)} %shard_map.49.refs_0_), channel_id=1, source_target_pairs={{0,4},{1,5},{2,6},{3,7},{4,0},{5,1},{6,2},{7,3},{8,12},{9,13},{10,... | collective-permute-start | bytes 835592 | tf_op jit(solution)/shard_map/ppermute | solution.py:23
  25.1 0.0 collective-permute-done.3.refs_0_
  25.1 4.0 %collective-permute-start.9 = (bf16[64,2176]{1,0:T(8,128)(2,1)S(1)}, bf16[64,2176]{1,0:T(8,128)(2,1)S(1)}, u32[]{:S(2)}, u32[]{:S(2)}) collective-permute-start(bf16[64,2176]{1,0:T(8,128)(2,1)S(1)} %collective-permute-done.3.refs_0_), channel_id=1, source_target_pairs={{0,2},{1,3},{2,0},{3,1},{4,6},{5,7},{6,4},{7,5},{8,10},{9,11},{10,... | collective-permute-start | bytes 835592 | tf_op jit(solution)/shard_map/ppermute | solution.py:23
  29.0 0.0 collective-permute-done.6.refs_1_
  29.0 2.2 %shard_map.50 = (bf16[2,64,768]{2,1,0:T(8,128)(2,1)S(1)}, bf16[2,64,768]{2,1,0:T(8,128)(2,1)S(1)}) custom-call(bf16[768,2048]{1,0:T(8,128)(2,1)S(1)} %bitcast.12, bf16[768,2048]{1,0:T(8,128)(2,1)S(1)} %collective-permute-done.2.other, bf16[64,2176]{1,0:T(8,128)(2,1)S(1)} %collective-permute-done.3.refs_0_, bf16[64,2176]{1,0:T(8,128)(2,1)S(1)} %collective-permute-done.6.refs_1_), custom_call_target="tpu_custom_call" | custom-call | flops 8053063680 | bytes 7208960 | tf_op jit(solution)/shard_map/pallas_call | solution.py:99
  31.2 1.1 %collective-permute-start.15 = (bf16[2,64,768]{2,1,0:T(8,128)(2,1)S(1)}, bf16[2,64,768]{2,1,0:T(8,128)(2,1)S(1)}, u32[]{:S(2)}, u32[]{:S(2)}) collective-permute-start(bf16[2,64,768]{2,1,0:T(8,128)(2,1)S(1)} %get-tuple-element.34), channel_id=1, source_target_pairs={{0,12},{1,13},{2,14},{3,15},{4,8},{5,9},{6,10},{7,11},{8,4},{9,5},... | collective-permute-start | bytes 589832 | tf_op jit(solution)/shard_map/ppermute | solution.py:23
  32.3 4.3 %collective-permute-done.5.refs_1_ = bf16[64,2176]{1,0:T(8,128)(2,1)S(1)} collective-permute-done((bf16[64,2176]{1,0:T(8,128)(2,1)S(1)}, bf16[64,2176]{1,0:T(8,128)(2,1)S(1)}, u32[]{:S(2)}, u32[]{:S(2)}) %collective-permute-start.5) | collective-permute-done | bytes 278560 | tf_op jit(solution)/shard_map/ppermute | solution.py:23
  36.6 6.6 %collective-permute-start.14 = (bf16[2,64,768]{2,1,0:T(8,128)(2,1)S(1)}, bf16[2,64,768]{2,1,0:T(8,128)(2,1)S(1)}, u32[]{:S(2)}, u32[]{:S(2)}) collective-permute-start(bf16[2,64,768]{2,1,0:T(8,128)(2,1)S(1)} %get-tuple-element.46), channel_id=1, source_target_pairs={{0,10},{1,11},{2,8},{3,9},{4,14},{5,15},{6,12},{7,13},{8,2},{9,3},... | collective-permute-start | bytes 589832 | tf_op jit(solution)/shard_map/ppermute | solution.py:23
  43.2 0.0 collective-permute-start.8
  43.2 0.0 collective-permute-done.10.refs_1_
  43.2 2.0 %collective-permute-start.7 = (bf16[64,2176]{1,0:T(8,128)(2,1)S(1)}, bf16[64,2176]{1,0:T(8,128)(2,1)S(1)}, u32[]{:S(2)}, u32[]{:S(2)}) collective-permute-start(bf16[64,2176]{1,0:T(8,128)(2,1)S(1)} %shard_map.49.refs_0_), channel_id=1, source_target_pairs={{0,2},{1,3},{2,0},{3,1},{4,6},{5,7},{6,4},{7,5},{8,10},{9,11},{10,... | collective-permute-start | bytes 835592 | tf_op jit(solution)/shard_map/ppermute | solution.py:23
  45.3 0.0 collective-permute-done.9.refs_0_
  45.3 2.0 %shard_map.51 = bf16[2,64,768]{2,1,0:T(8,128)(2,1)S(1)} custom-call(bf16[768,2048]{1,0:T(8,128)(2,1)S(1)} %bitcast.13, bf16[768,2048]{1,0:T(8,128)(2,1)S(1)} %collective-permute-done.2.other, bf16[64,2176]{1,0:T(8,128)(2,1)S(1)} %collective-permute-done.9.refs_0_), custom_call_target="tpu_custom_call" | custom-call | flops 4026531840 | bytes 6750208 | tf_op jit(solution)/shard_map/pallas_call | solution.py:99
  47.3 0.1 collective-permute-start.16
  47.4 2.0 %shard_map.52.refs_0_ = bf16[2,64,768]{2,1,0:T(8,128)(2,1)S(1)} custom-call(bf16[768,2048]{1,0:T(8,128)(2,1)S(1)} %bitcast.14, bf16[768,2048]{1,0:T(8,128)(2,1)S(1)} %collective-permute-done.2.other, bf16[64,2176]{1,0:T(8,128)(2,1)S(1)} %shard_map.49.refs_0_), custom_call_target="tpu_custom_call" | custom-call | flops 4026531840 | bytes 6750208 | tf_op jit(solution)/shard_map/pallas_call | solution.py:99
  49.4 14.3 %collective-permute-done.7.refs_0_ = bf16[64,2176]{1,0:T(8,128)(2,1)S(1)} collective-permute-done((bf16[64,2176]{1,0:T(8,128)(2,1)S(1)}, bf16[64,2176]{1,0:T(8,128)(2,1)S(1)}, u32[]{:S(2)}, u32[]{:S(2)}) %collective-permute-start.7) | collective-permute-done | bytes 278560 | tf_op jit(solution)/shard_map/ppermute | solution.py:23
  63.6 0.0 collective-permute-done.8.refs_2_
  63.7 2.2 %shard_map.53 = (bf16[2,64,768]{2,1,0:T(8,128)(2,1)S(1)}, bf16[2,64,768]{2,1,0:T(8,128)(2,1)S(1)}, bf16[2,64,768]{2,1,0:T(8,128)(2,1)S(1)}) custom-call(bf16[768,2048]{1,0:T(8,128)(2,1)S(1)} %bitcast.15, bf16[768,2048]{1,0:T(8,128)(2,1)S(1)} %collective-permute-done.2.other, bf16[64,2176]{1,0:T(8,128)(2,1)S(1)} %collective-permute-done.7.refs_0_, ...), custom_call_target="tpu_custom_call" | custom-call | flops 12079595520 | bytes 7667712 | tf_op jit(solution)/shard_map/pallas_call | solution.py:99
  65.9 0.1 collective-permute-start.11
  65.9 0.1 collective-permute-start.12
  66.0 0.0 collective-permute-done.14.refs_2_
  66.0 3.4 %collective-permute-start.13 = (bf16[2,64,768]{2,1,0:T(8,128)(2,1)S(1)}, bf16[2,64,768]{2,1,0:T(8,128)(2,1)S(1)}, u32[]{:S(2)}, u32[]{:S(2)}) collective-permute-start(bf16[2,64,768]{2,1,0:T(8,128)(2,1)S(1)} %get-tuple-element.44), channel_id=1, source_target_pairs={{0,6},{1,7},{2,4},{3,5},{4,2},{5,3},{6,0},{7,1},{8,14},{9,15},{10,... | collective-permute-start | bytes 589832 | tf_op jit(solution)/shard_map/ppermute | solution.py:23
  69.4 0.0 collective-permute-done.15.refs_3_
  69.4 0.0 collective-permute-done.16.refs_4_
  69.4 0.4 shard_map.54.refs_3_
  69.9 3.0 %collective-permute-done.11.refs_0_ = bf16[2,64,768]{2,1,0:T(8,128)(2,1)S(1)} collective-permute-done((bf16[2,64,768]{2,1,0:T(8,128)(2,1)S(1)}, bf16[2,64,768]{2,1,0:T(8,128)(2,1)S(1)}, u32[]{:S(2)}, u32[]{:S(2)}) %collective-permute-start.11) | collective-permute-done | bytes 196640 | tf_op jit(solution)/shard_map/ppermute | solution.py:23
  72.8 0.9 %collective-permute-done.12.refs_1_ = bf16[2,64,768]{2,1,0:T(8,128)(2,1)S(1)} collective-permute-done((bf16[2,64,768]{2,1,0:T(8,128)(2,1)S(1)}, bf16[2,64,768]{2,1,0:T(8,128)(2,1)S(1)}, u32[]{:S(2)}, u32[]{:S(2)}) %collective-permute-start.12) | collective-permute-done | bytes 196640 | tf_op jit(solution)/shard_map/ppermute | solution.py:23
  73.8 4.4 %collective-permute-done.13.refs_2_ = bf16[2,64,768]{2,1,0:T(8,128)(2,1)S(1)} collective-permute-done((bf16[2,64,768]{2,1,0:T(8,128)(2,1)S(1)}, bf16[2,64,768]{2,1,0:T(8,128)(2,1)S(1)}, u32[]{:S(2)}, u32[]{:S(2)}) %collective-permute-start.13) | collective-permute-done | bytes 196640 | tf_op jit(solution)/shard_map/ppermute | solution.py:23
  78.1 1.3 %shard_map.55 = bf16[512,768]{1,0:T(8,128)(2,1)} custom-call(s32[8,64]{1,0:T(8,128)S(1)} %bitcast.18, bf16[2,64,768]{2,1,0:T(8,128)(2,1)S(1)} %collective-permute-done.11.refs_0_, bf16[2,64,768]{2,1,0:T(8,128)(2,1)S(1)} %collective-permute-done.12.refs_1_, bf16[2,64,768]{2,1,0:T(8,128)(2,1)S(1)} %collective-permute-done.13.refs_2_, ...), custom_call_target="tpu_custom_call" | custom-call | tf_op jit(solution)/shard_map/pallas_call | solution.py:140
  (2 shorter events, 0.0 us)
Async XLA Ops:
  0.0 15.2 %collective-permute-start.2 = (bf16[768,2048]{1,0:T(8,128)(2,1)}, bf16[768,2048]{1,0:T(8,128)(2,1)S(1)}, u32[]{:S(2)}, u32[]{:S(2)}) collective-permute-start(bf16[768,2048]{1,0:T(8,128)(2,1)} %bitcast.9), channel_id=1, source_target_pairs={{0,1},{1,0},{2,3},{3,2},{4,5},{5,4},{6,7},{7,6},{8,9},{9,8},{10,11... | collective-permute-start | bytes 9437192 | tf_op jit(solution)/shard_map/ppermute | solution.py:23
  0.0 15.2 %collective-permute-start = (bf16[64,2048]{1,0:T(8,128)(2,1)}, bf16[64,2048]{1,0:T(8,128)(2,1)S(1)}, u32[]{:S(2)}, u32[]{:S(2)}) collective-permute-start(bf16[64,2048]{1,0:T(8,128)(2,1)} %bitcast.20), channel_id=1, source_target_pairs={{0,24},{1,25},{2,26},{3,27},{4,28},{5,29},{6,30},{7,31},{8,16},{9,... | collective-permute-start | bytes 786440 | tf_op jit(solution)/shard_map/ppermute | solution.py:33
  2.5 1.9 %copy-start = (bf16[1,1,768,2048]{3,2,1,0:T(8,128)(2,1)S(1)}, bf16[1,1,768,2048]{3,2,1,0:T(8,128)(2,1)}, u32[]{:S(2)}) copy-start(bf16[1,1,768,2048]{3,2,1,0:T(8,128)(2,1)} %param.7) | copy-start | bytes 9437188
  4.4 0.7 copy-start.2
  5.1 0.7 copy-start.3
  5.8 13.1 %copy-start.1 = (bf16[1,1,768,2048]{3,2,1,0:T(8,128)(2,1)S(1)}, bf16[1,1,768,2048]{3,2,1,0:T(8,128)(2,1)}, u32[]{:S(2)}) copy-start(bf16[1,1,768,2048]{3,2,1,0:T(8,128)(2,1)} %param.7) | copy-start | bytes 9437188
  5.9 9.3 %collective-permute-start.1 = (bf16[64,128]{1,0:T(8,128)(2,1)S(1)}, bf16[64,128]{1,0:T(8,128)(2,1)S(1)}, u32[]{:S(2)}, u32[]{:S(2)}) collective-permute-start(bf16[64,128]{1,0:T(8,128)(2,1)S(1)} %shard_map.46.columns), channel_id=1, source_target_pairs={{0,8},{1,9},{2,10},{3,11},{4,12},{5,13},{6,14},{7,15},{8,0},{9,1},... | collective-permute-start | bytes 49160 | tf_op jit(solution)/shard_map/ppermute | solution.py:23
  6.3 16.7 %collective-permute-start.4 = (bf16[64,2048]{1,0:T(8,128)(2,1)}, bf16[64,2048]{1,0:T(8,128)(2,1)S(1)}, u32[]{:S(2)}, u32[]{:S(2)}) collective-permute-start(bf16[64,2048]{1,0:T(8,128)(2,1)} %bitcast.21), channel_id=1, source_target_pairs={{0,16},{1,17},{2,18},{3,19},{4,20},{5,21},{6,22},{7,23},{8,24},{9,... | collective-permute-start | bytes 786440 | tf_op jit(solution)/shard_map/ppermute | solution.py:33
  15.2 9.8 %collective-permute-start.3 = (bf16[64,2176]{1,0:T(8,128)(2,1)S(1)}, bf16[64,2176]{1,0:T(8,128)(2,1)S(1)}, u32[]{:S(2)}, u32[]{:S(2)}) collective-permute-start(bf16[64,2176]{1,0:T(8,128)(2,1)S(1)} %shard_map.47.refs_0_), channel_id=1, source_target_pairs={{0,4},{1,5},{2,6},{3,7},{4,0},{5,1},{6,2},{7,3},{8,12},{9,13},{10,... | collective-permute-start | bytes 835592 | tf_op jit(solution)/shard_map/ppermute | solution.py:23
  17.4 11.6 %collective-permute-start.6 = (bf16[64,2176]{1,0:T(8,128)(2,1)S(1)}, bf16[64,2176]{1,0:T(8,128)(2,1)S(1)}, u32[]{:S(2)}, u32[]{:S(2)}) collective-permute-start(bf16[64,2176]{1,0:T(8,128)(2,1)S(1)} %shard_map.47.refs_0_), channel_id=1, source_target_pairs={{0,2},{1,3},{2,0},{3,1},{4,6},{5,7},{6,4},{7,5},{8,10},{9,11},{10,... | collective-permute-start | bytes 835592 | tf_op jit(solution)/shard_map/ppermute | solution.py:23
  21.0 22.3 %collective-permute-start.10 = (bf16[2,64,768]{2,1,0:T(8,128)(2,1)S(1)}, bf16[2,64,768]{2,1,0:T(8,128)(2,1)S(1)}, u32[]{:S(2)}, u32[]{:S(2)}) collective-permute-start(bf16[2,64,768]{2,1,0:T(8,128)(2,1)S(1)} %shard_map.48), channel_id=1, source_target_pairs={{0,8},{1,9},{2,10},{3,11},{4,12},{5,13},{6,14},{7,15},{8,0},{9,1},... | collective-permute-start | bytes 589832 | tf_op jit(solution)/shard_map/ppermute | solution.py:23
  23.1 13.5 %collective-permute-start.5 = (bf16[64,2176]{1,0:T(8,128)(2,1)S(1)}, bf16[64,2176]{1,0:T(8,128)(2,1)S(1)}, u32[]{:S(2)}, u32[]{:S(2)}) collective-permute-start(bf16[64,2176]{1,0:T(8,128)(2,1)S(1)} %shard_map.49.refs_0_), channel_id=1, source_target_pairs={{0,4},{1,5},{2,6},{3,7},{4,0},{5,1},{6,2},{7,3},{8,12},{9,13},{10,... | collective-permute-start | bytes 835592 | tf_op jit(solution)/shard_map/ppermute | solution.py:23
  25.1 20.2 %collective-permute-start.9 = (bf16[64,2176]{1,0:T(8,128)(2,1)S(1)}, bf16[64,2176]{1,0:T(8,128)(2,1)S(1)}, u32[]{:S(2)}, u32[]{:S(2)}) collective-permute-start(bf16[64,2176]{1,0:T(8,128)(2,1)S(1)} %collective-permute-done.3.refs_0_), channel_id=1, source_target_pairs={{0,2},{1,3},{2,0},{3,1},{4,6},{5,7},{6,4},{7,5},{8,10},{9,11},{10,... | collective-permute-start | bytes 835592 | tf_op jit(solution)/shard_map/ppermute | solution.py:23
  31.2 38.2 %collective-permute-start.15 = (bf16[2,64,768]{2,1,0:T(8,128)(2,1)S(1)}, bf16[2,64,768]{2,1,0:T(8,128)(2,1)S(1)}, u32[]{:S(2)}, u32[]{:S(2)}) collective-permute-start(bf16[2,64,768]{2,1,0:T(8,128)(2,1)S(1)} %get-tuple-element.34), channel_id=1, source_target_pairs={{0,12},{1,13},{2,14},{3,15},{4,8},{5,9},{6,10},{7,11},{8,4},{9,5},... | collective-permute-start | bytes 589832 | tf_op jit(solution)/shard_map/ppermute | solution.py:23
  36.6 29.4 %collective-permute-start.14 = (bf16[2,64,768]{2,1,0:T(8,128)(2,1)S(1)}, bf16[2,64,768]{2,1,0:T(8,128)(2,1)S(1)}, u32[]{:S(2)}, u32[]{:S(2)}) collective-permute-start(bf16[2,64,768]{2,1,0:T(8,128)(2,1)S(1)} %get-tuple-element.46), channel_id=1, source_target_pairs={{0,10},{1,11},{2,8},{3,9},{4,14},{5,15},{6,12},{7,13},{8,2},{9,3},... | collective-permute-start | bytes 589832 | tf_op jit(solution)/shard_map/ppermute | solution.py:23
  43.2 20.4 %collective-permute-start.8 = (bf16[64,2176]{1,0:T(8,128)(2,1)S(1)}, bf16[64,2176]{1,0:T(8,128)(2,1)S(1)}, u32[]{:S(2)}, u32[]{:S(2)}) collective-permute-start(bf16[64,2176]{1,0:T(8,128)(2,1)S(1)} %collective-permute-done.5.refs_1_), channel_id=1, source_target_pairs={{0,2},{1,3},{2,0},{3,1},{4,6},{5,7},{6,4},{7,5},{8,10},{9,11},{10,... | collective-permute-start | bytes 835592 | tf_op jit(solution)/shard_map/ppermute | solution.py:23
  43.2 20.4 %collective-permute-start.7 = (bf16[64,2176]{1,0:T(8,128)(2,1)S(1)}, bf16[64,2176]{1,0:T(8,128)(2,1)S(1)}, u32[]{:S(2)}, u32[]{:S(2)}) collective-permute-start(bf16[64,2176]{1,0:T(8,128)(2,1)S(1)} %shard_map.49.refs_0_), channel_id=1, source_target_pairs={{0,2},{1,3},{2,0},{3,1},{4,6},{5,7},{6,4},{7,5},{8,10},{9,11},{10,... | collective-permute-start | bytes 835592 | tf_op jit(solution)/shard_map/ppermute | solution.py:23
  47.3 22.1 %collective-permute-start.16 = (bf16[2,64,768]{2,1,0:T(8,128)(2,1)S(1)}, bf16[2,64,768]{2,1,0:T(8,128)(2,1)S(1)}, u32[]{:S(2)}, u32[]{:S(2)}) collective-permute-start(bf16[2,64,768]{2,1,0:T(8,128)(2,1)S(1)} %shard_map.51), channel_id=1, source_target_pairs={{0,14},{1,15},{2,12},{3,13},{4,10},{5,11},{6,8},{7,9},{8,6},{9,7},... | collective-permute-start | bytes 589832 | tf_op jit(solution)/shard_map/ppermute | solution.py:23
  65.9 7.0 %collective-permute-start.11 = (bf16[2,64,768]{2,1,0:T(8,128)(2,1)S(1)}, bf16[2,64,768]{2,1,0:T(8,128)(2,1)S(1)}, u32[]{:S(2)}, u32[]{:S(2)}) collective-permute-start(bf16[2,64,768]{2,1,0:T(8,128)(2,1)S(1)} %get-tuple-element.42), channel_id=1, source_target_pairs={{0,2},{1,3},{2,0},{3,1},{4,6},{5,7},{6,4},{7,5},{8,10},{9,11},{10,... | collective-permute-start | bytes 589832 | tf_op jit(solution)/shard_map/ppermute | solution.py:23
  65.9 7.8 %collective-permute-start.12 = (bf16[2,64,768]{2,1,0:T(8,128)(2,1)S(1)}, bf16[2,64,768]{2,1,0:T(8,128)(2,1)S(1)}, u32[]{:S(2)}, u32[]{:S(2)}) collective-permute-start(bf16[2,64,768]{2,1,0:T(8,128)(2,1)S(1)} %get-tuple-element.43), channel_id=1, source_target_pairs={{0,4},{1,5},{2,6},{3,7},{4,0},{5,1},{6,2},{7,3},{8,12},{9,13},{10,... | collective-permute-start | bytes 589832 | tf_op jit(solution)/shard_map/ppermute | solution.py:23
  66.0 12.1 %collective-permute-start.13 = (bf16[2,64,768]{2,1,0:T(8,128)(2,1)S(1)}, bf16[2,64,768]{2,1,0:T(8,128)(2,1)S(1)}, u32[]{:S(2)}, u32[]{:S(2)}) collective-permute-start(bf16[2,64,768]{2,1,0:T(8,128)(2,1)S(1)} %get-tuple-element.44), channel_id=1, source_target_pairs={{0,6},{1,7},{2,4},{3,5},{4,2},{5,3},{6,0},{7,1},{8,14},{9,15},{10,... | collective-permute-start | bytes 589832 | tf_op jit(solution)/shard_map/ppermute | solution.py:23

commit v15 on v14

--- a/solution.py
+++ b/solution.py
@@ -66,46 +66,45 @@
     )(rows, columns)
 
 
-def products_kernel(paired, weight, other, *refs):
+def products_kernel(count, stack, weight, other, *refs):
     hidden, depth = weight.shape
-    rows, gates, at = [], [], 0
-    for pair in paired:
-        rows.append(refs[at][:, :depth])
-        gates.append(refs[at + 1][...] if pair else refs[at][:, depth:])
-        at += 1 + pair
-    outs = refs[at:]
+    pieces, outs = refs[:count], refs[count + stack :]
     tokens = outs[0].shape[1]
     me = lax.axis_index("expert")
     core = lax.rem(me, CORES)
-    stacked = jnp.concatenate(rows, axis=0)
-    gates = jnp.concatenate(gates, axis=0).astype(jnp.float32)
+    stacked = jnp.concatenate([p[...] for p in pieces], axis=0)
+    if stack:
+        refs[count][...] = stacked
+    gates = stacked[:, depth:].astype(jnp.float32)
     column = lax.broadcasted_iota(jnp.int32, gates.shape, 1)
     for mat, to in ((weight, core), (other, 1 - core)):
         scale = jnp.sum(jnp.where(column == me - core + to, gates, 0.0), axis=1, keepdims=True)
         product = lax.dot_general(
-            stacked, mat[...], (((1,), (1,)), ((), ())), preferred_element_type=jnp.float32
+            stacked[:, :depth],
+            mat[...],
+            (((1,), (1,)), ((), ())),
+            preferred_element_type=jnp.float32,
         )
         scaled = (product * scale).astype(jnp.bfloat16)
         for j, out in enumerate(outs):
             out[to] = scaled[j * tokens : (j + 1) * tokens]
 
 
-def products(pieces, weight, other):
+def products(pieces, tokens, weight, other, stack=False):
     hidden, depth = weight.shape
-    paired = [isinstance(p, tuple) for p in pieces]
-    operands = [x for p in pieces for x in (p if isinstance(p, tuple) else (p,))]
-    tokens = operands[0].shape[0]
-    total = len(pieces) * tokens
-    return pl.pallas_call(
-        functools.partial(products_kernel, paired),
-        out_shape=[jax.ShapeDtypeStruct((CORES, tokens, hidden), jnp.bfloat16)] * len(pieces),
+    total = sum(p.shape[0] for p in pieces)
+    one = jax.ShapeDtypeStruct((CORES, tokens, hidden), jnp.bfloat16)
+    both = jax.ShapeDtypeStruct((total, pieces[0].shape[1]), jnp.bfloat16)
+    return pl.pallas_call(
+        functools.partial(products_kernel, len(pieces), int(stack)),
+        out_shape=[both] * int(stack) + [one] * (total // tokens),
         compiler_params=pltpu.CompilerParams(vmem_limit_bytes=16 << 20),
         cost_estimate=pl.CostEstimate(
             flops=20 * CORES * total * hidden * depth,
             bytes_accessed=2 * (total * (2 * hidden + depth) + 2 * hidden * depth),
             transcendentals=0,
         ),
-    )(weight, other, *operands)
+    )(weight, other, *pieces)
 
 
 def pick_kernel(flips, ids, *refs):
@@ -149,40 +148,38 @@
     owners = lax.axis_size("expert")
     tie = lax.optimization_barrier
 
-    def work(*pieces):
-        return products(list(pieces), weight_mat, other_mat)
-
+    def work(*pieces, stack=False):
+        return products(list(pieces), tokens, weight_mat, other_mat, stack)
+
+    rows = send_across(upstream, owners, 0)
     far = send_across(upstream, owners, Z_FAR)
-    rows = send_across(upstream, owners, 0)
     other_mat = send(weight_mat, owners, 0, 1)
     columns = gate_columns(route_ids.T, route_gates.T, weight_mat)
     far_columns = send(columns, owners, Z_FAR)
-    far, far_columns, other_mat = tie((far, far_columns, other_mat))
+    rows, columns = tie((rows, columns))
+    rows = widened(rows, columns)
+    side = send(rows, owners, X)
+    far, far_columns, rows, other_mat = tie((far, far_columns, rows, other_mat))
     far = widened(far, far_columns)
     cross = send(far, owners, Z_NEAR)
     far_side = send(far, owners, X)
     (out_far,) = work(far)
     back_far = send(out_far, owners, Z_FAR)
-    rows, columns, _ = tie((rows, columns, out_far))
-    rows = widened(rows, columns)
-    near = send(rows, owners, Z_NEAR)
-    cross, rows = tie((cross, rows))
+    side, rows, _ = tie((side, rows, out_far))
+    pair, out_own, out_side = work(rows, side, stack=True)
+    pair = send(pair, owners, Z_NEAR)
+    cross, out_side, _ = tie((cross, out_side, out_own))
+    back_side = send(out_side, owners, X)
     cross_side = send(cross, owners, X)
     far_side, _ = tie((far_side, cross))
     out_cross, out_far_side = work(cross, far_side)
     back_cross = send(out_cross, owners, Z_NEAR ^ Z_FAR)
     back_far_side = send(out_far_side, owners, X ^ Z_FAR)
-    near, _ = tie((near, out_cross))
-    near_side = send(near, owners, X)
-    side = send(tie((rows, near))[0], owners, X)
-    cross_side, back_far, _ = tie((cross_side, back_far, near))
+    cross_side, back_far, back_side, _ = tie((cross_side, back_far, back_side, out_cross))
     (out_cross_side,) = work(cross_side)
     back_cross_side = send(out_cross_side, owners, X ^ Z_NEAR ^ Z_FAR)
-    rows, _ = tie((rows, out_cross_side))
-    (out_own,) = work(rows)
-    side, near, near_side, _ = tie((side, near, near_side, out_own))
-    out_side, out_near, out_near_side = work(side, near, near_side)
-    back_side = send(out_side, owners, X)
+    pair, _ = tie((pair, out_cross_side))
+    out_near, out_near_side = work(pair)
     back_near = send(out_near, owners, Z_NEAR)
     back_near_side = send(out_near_side, owners, X ^ Z_NEAR)
     far_parts = {

time: 79.7 us -> 69.6 us (0.87)
  the two profiles are of different devices: /device:TPU:12 before, /device:TPU:0 now
where the time goes in v15:
time: 69.6 us; the launch traced here: 69.4 us
  waiting for transfers between devices  27.5 us (40%)
  starting transfers between devices  26.1 us (38%)
  Pallas kernels  12.5 us (18%)
  local copies, waits for them, and re-layouts  3.26 us (5%)
    ppermute x14, waiting for transfers between devices, send(): return lax.ppermute(block, 'expert', route)  24.5 us
    ppermute x14, starting transfers between devices, send(): return lax.ppermute(block, 'expert', route)  21.1 us
    pallas_call x5, Pallas kernels, products(): pl.pallas_call(functools.partial(products_kernel, len(pieces), int(stack)...  10.6 us
    ppermute x2, starting transfers between devices, send_across(): return lax.ppermute(block, ('pipe', 'expert'), route)  5.05 us
    unnamed x8, local copies, waits for them, and re-layouts  3.26 us
    ppermute x2, waiting for transfers between devices, send_across(): return lax.ppermute(block, ('pipe', 'expert'), route)  3.04 us
    pallas_call x2, Pallas kernels, pick_routes(): pl.pallas_call(functools.partial(pick_kernel, flips), out_shape=jax.Shape...  1.74 us
  transfers between devices with their start and end apart: 16, of which 7 were waited for; matrix products, arithmetic and copies ran while one was open for 0% of the time, Pallas kernels for 16%

profile of v15, /device:TPU:0, one launch (start us, length us, event | category | flops | bytes accessed | tf_op | source)
XLA Modules:
  0.0 69.4 jit_solution(17894611578141341005)
XLA Ops:
  0.0 0.5 collective-permute-start.3
  0.5 2.5 %collective-permute-start.2 = (bf16[64,2048]{1,0:T(8,128)(2,1)}, bf16[64,2048]{1,0:T(8,128)(2,1)S(1)}, u32[]{:S(2)}, u32[]{:S(2)}) collective-permute-start(bf16[64,2048]{1,0:T(8,128)(2,1)} %bitcast.20), channel_id=1, source_target_pairs={{0,16},{1,17},{2,18},{3,19},{4,20},{5,21},{6,22},{7,23},{8,24},{9,... | collective-permute-start | bytes 786440 | tf_op jit(solution)/shard_map/ppermute | solution.py:33
  3.0 2.5 %collective-permute-start = (bf16[64,2048]{1,0:T(8,128)(2,1)}, bf16[64,2048]{1,0:T(8,128)(2,1)S(1)}, u32[]{:S(2)}, u32[]{:S(2)}) collective-permute-start(bf16[64,2048]{1,0:T(8,128)(2,1)} %bitcast.21), channel_id=1, source_target_pairs={{0,24},{1,25},{2,26},{3,27},{4,28},{5,29},{6,30},{7,31},{8,16},{9,... | collective-permute-start | bytes 786440 | tf_op jit(solution)/shard_map/ppermute | solution.py:33
  5.5 0.0 copy-start
  5.5 1.9 %copy-done = bf16[1,1,768,2048]{3,2,1,0:T(8,128)(2,1)S(1)} copy-done((bf16[1,1,768,2048]{3,2,1,0:T(8,128)(2,1)S(1)}, bf16[1,1,768,2048]{3,2,1,0:T(8,128)(2,1)}, u32[]{:S(2)}) %copy-start) | copy-done | bytes 3145752
  7.4 0.0 copy-start.2
  7.4 0.7 copy-done.2
  8.1 0.0 copy-start.3
  8.1 0.7 copy-done.3
  8.8 0.0 copy-start.1
  8.8 0.1 shard_map.46.columns
  8.9 0.1 collective-permute-start.1
  9.0 2.3 %collective-permute-done.2.rows = bf16[64,2048]{1,0:T(8,128)(2,1)S(1)} collective-permute-done((bf16[64,2048]{1,0:T(8,128)(2,1)}, bf16[64,2048]{1,0:T(8,128)(2,1)S(1)}, u32[]{:S(2)}, u32[]{:S(2)}) %collective-permute-start.2) | collective-permute-done | bytes 262176 | tf_op jit(solution)/shard_map/ppermute | solution.py:33
  11.3 1.8 %collective-permute-start.5 = (bf16[64,2176]{1,0:T(8,128)(2,1)S(1)}, bf16[64,2176]{1,0:T(8,128)(2,1)S(1)}, u32[]{:S(2)}, u32[]{:S(2)}) collective-permute-start(bf16[64,2176]{1,0:T(8,128)(2,1)S(1)} %shard_map.47.refs_0_), channel_id=1, source_target_pairs={{0,2},{1,3},{2,0},{3,1},{4,6},{5,7},{6,4},{7,5},{8,10},{9,11},{10,... | collective-permute-start | bytes 835592 | tf_op jit(solution)/shard_map/ppermute | solution.py:23
  13.1 5.7 %collective-permute-done.1.columns = bf16[64,128]{1,0:T(8,128)(2,1)S(1)} collective-permute-done((bf16[64,128]{1,0:T(8,128)(2,1)S(1)}, bf16[64,128]{1,0:T(8,128)(2,1)S(1)}, u32[]{:S(2)}, u32[]{:S(2)}) %collective-permute-start.1) | collective-permute-done | bytes 16416 | tf_op jit(solution)/shard_map/ppermute | solution.py:23
  18.8 0.7 %collective-permute-done.rows = bf16[64,2048]{1,0:T(8,128)(2,1)S(1)} collective-permute-done((bf16[64,2048]{1,0:T(8,128)(2,1)}, bf16[64,2048]{1,0:T(8,128)(2,1)S(1)}, u32[]{:S(2)}, u32[]{:S(2)}) %collective-permute-start) | collective-permute-done | bytes 262176 | tf_op jit(solution)/shard_map/ppermute | solution.py:33
  19.6 0.0 collective-permute-done.3.other
  19.6 0.1 collective-permute-start.4
  19.7 1.6 %collective-permute-start.9 = (bf16[64,2176]{1,0:T(8,128)(2,1)S(1)}, bf16[64,2176]{1,0:T(8,128)(2,1)S(1)}, u32[]{:S(2)}, u32[]{:S(2)}) collective-permute-start(bf16[64,2176]{1,0:T(8,128)(2,1)S(1)} %shard_map.48.refs_0_), channel_id=1, source_target_pairs={{0,2},{1,3},{2,0},{3,1},{4,6},{5,7},{6,4},{7,5},{8,10},{9,11},{10,... | collective-permute-start | bytes 835592 | tf_op jit(solution)/shard_map/ppermute | solution.py:23
  21.2 0.0 copy-done.1
  21.2 2.0 %shard_map.49 = bf16[2,64,768]{2,1,0:T(8,128)(2,1)S(1)} custom-call(bf16[768,2048]{1,0:T(8,128)(2,1)S(1)} %bitcast.11, bf16[768,2048]{1,0:T(8,128)(2,1)S(1)} %collective-permute-done.3.other, bf16[64,2176]{1,0:T(8,128)(2,1)S(1)} %shard_map.48.refs_0_), custom_call_target="tpu_custom_call" | custom-call | flops 4026531840 | bytes 6750208 | tf_op jit(solution)/shard_map/pallas_call | solution.py:98
  23.2 3.9 %collective-permute-start.7 = (bf16[2,64,768]{2,1,0:T(8,128)(2,1)S(1)}, bf16[2,64,768]{2,1,0:T(8,128)(2,1)S(1)}, u32[]{:S(2)}, u32[]{:S(2)}) collective-permute-start(bf16[2,64,768]{2,1,0:T(8,128)(2,1)S(1)} %shard_map.49), channel_id=1, source_target_pairs={{0,8},{1,9},{2,10},{3,11},{4,12},{5,13},{6,14},{7,15},{8,0},{9,1},... | collective-permute-start | bytes 589832 | tf_op jit(solution)/shard_map/ppermute | solution.py:23
  27.2 0.0 collective-permute-done.5.refs_1_
  27.2 2.2 %shard_map.50 = (bf16[128,2176]{1,0:T(8,128)(2,1)S(1)}, bf16[2,64,768]{2,1,0:T(8,128)(2,1)S(1)}, bf16[2,64,768]{2,1,0:T(8,128)(2,1)S(1)}) custom-call(bf16[768,2048]{1,0:T(8,128)(2,1)S(1)} %bitcast.12, bf16[768,2048]{1,0:T(8,128)(2,1)S(1)} %collective-permute-done.3.other, bf16[64,2176]{1,0:T(8,128)(2,1)S(1)} %shard_map.47.refs_0_, ...), custom_call_target="tpu_custom_call" | custom-call | flops 8053063680 | bytes 7208960 | tf_op jit(solution)/shard_map/pallas_call | solution.py:98
  29.4 0.1 collective-permute-start.10
  29.5 0.0 collective-permute-done.4.refs_0_
  29.5 3.2 %collective-permute-start.6 = (bf16[64,2176]{1,0:T(8,128)(2,1)S(1)}, bf16[64,2176]{1,0:T(8,128)(2,1)S(1)}, u32[]{:S(2)}, u32[]{:S(2)}) collective-permute-start(bf16[64,2176]{1,0:T(8,128)(2,1)S(1)} %collective-permute-done.4.refs_0_), channel_id=1, source_target_pairs={{0,2},{1,3},{2,0},{3,1},{4,6},{5,7},{6,4},{7,5},{8,10},{9,11},{10,... | collective-permute-start | bytes 835592 | tf_op jit(solution)/shard_map/ppermute | solution.py:23
  32.7 0.0 collective-permute-start.8
  32.7 0.0 collective-permute-done.9.refs_1_
  32.7 2.2 %shard_map.51 = (bf16[2,64,768]{2,1,0:T(8,128)(2,1)S(1)}, bf16[2,64,768]{2,1,0:T(8,128)(2,1)S(1)}) custom-call(bf16[768,2048]{1,0:T(8,128)(2,1)S(1)} %bitcast.13, bf16[768,2048]{1,0:T(8,128)(2,1)S(1)} %collective-permute-done.3.other, bf16[64,2176]{1,0:T(8,128)(2,1)S(1)} %collective-permute-done.4.refs_0_, bf16[64,2176]{1,0:T(8,128)(2,1)S(1)} %collective-permute-done.9.refs_1_), custom_call_target="tpu_custom_call" | custom-call | flops 8053063680 | bytes 7208960 | tf_op jit(solution)/shard_map/pallas_call | solution.py:98
  34.9 2.5 %collective-permute-start.13 = (bf16[2,64,768]{2,1,0:T(8,128)(2,1)S(1)}, bf16[2,64,768]{2,1,0:T(8,128)(2,1)S(1)}, u32[]{:S(2)}, u32[]{:S(2)}) collective-permute-start(bf16[2,64,768]{2,1,0:T(8,128)(2,1)S(1)} %get-tuple-element.48), channel_id=1, source_target_pairs={{0,10},{1,11},{2,8},{3,9},{4,14},{5,15},{6,12},{7,13},{8,2},{9,3},... | collective-permute-start | bytes 589832 | tf_op jit(solution)/shard_map/ppermute | solution.py:23
  37.4 0.0 collective-permute-done.7.refs_1_
  37.4 1.1 %collective-permute-start.14 = (bf16[2,64,768]{2,1,0:T(8,128)(2,1)S(1)}, bf16[2,64,768]{2,1,0:T(8,128)(2,1)S(1)}, u32[]{:S(2)}, u32[]{:S(2)}) collective-permute-start(bf16[2,64,768]{2,1,0:T(8,128)(2,1)S(1)} %get-tuple-element.40), channel_id=1, source_target_pairs={{0,12},{1,13},{2,14},{3,15},{4,8},{5,9},{6,10},{7,11},{8,4},{9,5},... | collective-permute-start | bytes 589832 | tf_op jit(solution)/shard_map/ppermute | solution.py:23
  38.5 7.2 %collective-permute-done.8.refs_0_ = bf16[2,64,768]{2,1,0:T(8,128)(2,1)S(1)} collective-permute-done((bf16[2,64,768]{2,1,0:T(8,128)(2,1)S(1)}, bf16[2,64,768]{2,1,0:T(8,128)(2,1)S(1)}, u32[]{:S(2)}, u32[]{:S(2)}) %collective-permute-start.8) | collective-permute-done | bytes 196640 | tf_op jit(solution)/shard_map/ppermute | solution.py:23
  45.6 0.0 collective-permute-done.6.refs_0_
  45.6 2.0 %shard_map.52 = bf16[2,64,768]{2,1,0:T(8,128)(2,1)S(1)} custom-call(bf16[768,2048]{1,0:T(8,128)(2,1)S(1)} %bitcast.14, bf16[768,2048]{1,0:T(8,128)(2,1)S(1)} %collective-permute-done.3.other, bf16[64,2176]{1,0:T(8,128)(2,1)S(1)} %collective-permute-done.6.refs_0_), custom_call_target="tpu_custom_call" | custom-call | flops 4026531840 | bytes 6750208 | tf_op jit(solution)/shard_map/pallas_call | solution.py:98
  47.7 4.2 %collective-permute-start.15 = (bf16[2,64,768]{2,1,0:T(8,128)(2,1)S(1)}, bf16[2,64,768]{2,1,0:T(8,128)(2,1)S(1)}, u32[]{:S(2)}, u32[]{:S(2)}) collective-permute-start(bf16[2,64,768]{2,1,0:T(8,128)(2,1)S(1)} %shard_map.52), channel_id=1, source_target_pairs={{0,14},{1,15},{2,12},{3,13},{4,10},{5,11},{6,8},{7,9},{8,6},{9,7},... | collective-permute-start | bytes 589832 | tf_op jit(solution)/shard_map/ppermute | solution.py:23
  51.9 0.0 collective-permute-done.10.refs_0_
  51.9 2.2 %shard_map.53 = (bf16[2,64,768]{2,1,0:T(8,128)(2,1)S(1)}, bf16[2,64,768]{2,1,0:T(8,128)(2,1)S(1)}) custom-call(bf16[768,2048]{1,0:T(8,128)(2,1)S(1)} %bitcast.15, bf16[768,2048]{1,0:T(8,128)(2,1)S(1)} %collective-permute-done.3.other, bf16[128,2176]{1,0:T(8,128)(2,1)S(1)} %collective-permute-done.10.refs_0_), custom_call_target="tpu_custom_call" | custom-call | flops 8053063680 | bytes 7208960 | tf_op jit(solution)/shard_map/pallas_call | solution.py:98
  54.0 0.1 collective-permute-start.11
  54.1 2.0 %collective-permute-start.12 = (bf16[2,64,768]{2,1,0:T(8,128)(2,1)S(1)}, bf16[2,64,768]{2,1,0:T(8,128)(2,1)S(1)}, u32[]{:S(2)}, u32[]{:S(2)}) collective-permute-start(bf16[2,64,768]{2,1,0:T(8,128)(2,1)S(1)} %get-tuple-element.46), channel_id=1, source_target_pairs={{0,6},{1,7},{2,4},{3,5},{4,2},{5,3},{6,0},{7,1},{8,14},{9,15},{10,... | collective-permute-start | bytes 589832 | tf_op jit(solution)/shard_map/ppermute | solution.py:23
  56.1 0.0 collective-permute-done.13.refs_2_
  56.1 0.0 collective-permute-done.14.refs_3_
  56.1 3.7 %collective-permute-done.15.refs_4_ = bf16[2,64,768]{2,1,0:T(8,128)(2,1)S(1)} collective-permute-done((bf16[2,64,768]{2,1,0:T(8,128)(2,1)S(1)}, bf16[2,64,768]{2,1,0:T(8,128)(2,1)S(1)}, u32[]{:S(2)}, u32[]{:S(2)}) %collective-permute-start.15) | collective-permute-done | bytes 196640 | tf_op jit(solution)/shard_map/ppermute | solution.py:23
  59.8 0.4 shard_map.54.refs_3_
  60.2 2.8 %collective-permute-done.11.refs_1_ = bf16[2,64,768]{2,1,0:T(8,128)(2,1)S(1)} collective-permute-done((bf16[2,64,768]{2,1,0:T(8,128)(2,1)S(1)}, bf16[2,64,768]{2,1,0:T(8,128)(2,1)S(1)}, u32[]{:S(2)}, u32[]{:S(2)}) %collective-permute-start.11) | collective-permute-done | bytes 196640 | tf_op jit(solution)/shard_map/ppermute | solution.py:23
  63.1 5.0 %collective-permute-done.12.refs_2_ = bf16[2,64,768]{2,1,0:T(8,128)(2,1)S(1)} collective-permute-done((bf16[2,64,768]{2,1,0:T(8,128)(2,1)S(1)}, bf16[2,64,768]{2,1,0:T(8,128)(2,1)S(1)}, u32[]{:S(2)}, u32[]{:S(2)}) %collective-permute-start.12) | collective-permute-done | bytes 196640 | tf_op jit(solution)/shard_map/ppermute | solution.py:23
  68.1 1.3 %shard_map.55 = bf16[512,768]{1,0:T(8,128)(2,1)} custom-call(s32[8,64]{1,0:T(8,128)S(1)} %bitcast.18, bf16[2,64,768]{2,1,0:T(8,128)(2,1)S(1)} %collective-permute-done.8.refs_0_, bf16[2,64,768]{2,1,0:T(8,128)(2,1)S(1)} %collective-permute-done.11.refs_1_, bf16[2,64,768]{2,1,0:T(8,128)(2,1)S(1)} %collective-permute-done.12.refs_2_, ...), custom_call_target="tpu_custom_call" | custom-call | tf_op jit(solution)/shard_map/pallas_call | solution.py:139
  (2 shorter events, 0.0 us)
Async XLA Ops:
  0.0 19.6 %collective-permute-start.3 = (bf16[768,2048]{1,0:T(8,128)(2,1)}, bf16[768,2048]{1,0:T(8,128)(2,1)S(1)}, u32[]{:S(2)}, u32[]{:S(2)}) collective-permute-start(bf16[768,2048]{1,0:T(8,128)(2,1)} %bitcast.9), channel_id=1, source_target_pairs={{0,1},{1,0},{2,3},{3,2},{4,5},{5,4},{6,7},{7,6},{8,9},{9,8},{10,11... | collective-permute-start | bytes 9437192 | tf_op jit(solution)/shard_map/ppermute | solution.py:23
  0.5 10.8 %collective-permute-start.2 = (bf16[64,2048]{1,0:T(8,128)(2,1)}, bf16[64,2048]{1,0:T(8,128)(2,1)S(1)}, u32[]{:S(2)}, u32[]{:S(2)}) collective-permute-start(bf16[64,2048]{1,0:T(8,128)(2,1)} %bitcast.20), channel_id=1, source_target_pairs={{0,16},{1,17},{2,18},{3,19},{4,20},{5,21},{6,22},{7,23},{8,24},{9,... | collective-permute-start | bytes 786440 | tf_op jit(solution)/shard_map/ppermute | solution.py:33
  3.0 16.6 %collective-permute-start = (bf16[64,2048]{1,0:T(8,128)(2,1)}, bf16[64,2048]{1,0:T(8,128)(2,1)S(1)}, u32[]{:S(2)}, u32[]{:S(2)}) collective-permute-start(bf16[64,2048]{1,0:T(8,128)(2,1)} %bitcast.21), channel_id=1, source_target_pairs={{0,24},{1,25},{2,26},{3,27},{4,28},{5,29},{6,30},{7,31},{8,16},{9,... | collective-permute-start | bytes 786440 | tf_op jit(solution)/shard_map/ppermute | solution.py:33
  5.5 1.9 %copy-start = (bf16[1,1,768,2048]{3,2,1,0:T(8,128)(2,1)S(1)}, bf16[1,1,768,2048]{3,2,1,0:T(8,128)(2,1)}, u32[]{:S(2)}) copy-start(bf16[1,1,768,2048]{3,2,1,0:T(8,128)(2,1)} %param.7) | copy-start | bytes 9437188
  7.4 0.7 copy-start.2
  8.1 0.7 copy-start.3
  8.8 12.5 %copy-start.1 = (bf16[1,1,768,2048]{3,2,1,0:T(8,128)(2,1)S(1)}, bf16[1,1,768,2048]{3,2,1,0:T(8,128)(2,1)}, u32[]{:S(2)}) copy-start(bf16[1,1,768,2048]{3,2,1,0:T(8,128)(2,1)} %param.7) | copy-start | bytes 9437188
  8.9 9.9 %collective-permute-start.1 = (bf16[64,128]{1,0:T(8,128)(2,1)S(1)}, bf16[64,128]{1,0:T(8,128)(2,1)S(1)}, u32[]{:S(2)}, u32[]{:S(2)}) collective-permute-start(bf16[64,128]{1,0:T(8,128)(2,1)S(1)} %shard_map.46.columns), channel_id=1, source_target_pairs={{0,8},{1,9},{2,10},{3,11},{4,12},{5,13},{6,14},{7,15},{8,0},{9,1},... | collective-permute-start | bytes 49160 | tf_op jit(solution)/shard_map/ppermute | solution.py:23
  11.3 15.9 %collective-permute-start.5 = (bf16[64,2176]{1,0:T(8,128)(2,1)S(1)}, bf16[64,2176]{1,0:T(8,128)(2,1)S(1)}, u32[]{:S(2)}, u32[]{:S(2)}) collective-permute-start(bf16[64,2176]{1,0:T(8,128)(2,1)S(1)} %shard_map.47.refs_0_), channel_id=1, source_target_pairs={{0,2},{1,3},{2,0},{3,1},{4,6},{5,7},{6,4},{7,5},{8,10},{9,11},{10,... | collective-permute-start | bytes 835592 | tf_op jit(solution)/shard_map/ppermute | solution.py:23
  19.6 9.9 %collective-permute-start.4 = (bf16[64,2176]{1,0:T(8,128)(2,1)S(1)}, bf16[64,2176]{1,0:T(8,128)(2,1)S(1)}, u32[]{:S(2)}, u32[]{:S(2)}) collective-permute-start(bf16[64,2176]{1,0:T(8,128)(2,1)S(1)} %shard_map.48.refs_0_), channel_id=1, source_target_pairs={{0,4},{1,5},{2,6},{3,7},{4,0},{5,1},{6,2},{7,3},{8,12},{9,13},{10,... | collective-permute-start | bytes 835592 | tf_op jit(solution)/shard_map/ppermute | solution.py:23
  19.7 13.0 %collective-permute-start.9 = (bf16[64,2176]{1,0:T(8,128)(2,1)S(1)}, bf16[64,2176]{1,0:T(8,128)(2,1)S(1)}, u32[]{:S(2)}, u32[]{:S(2)}) collective-permute-start(bf16[64,2176]{1,0:T(8,128)(2,1)S(1)} %shard_map.48.refs_0_), channel_id=1, source_target_pairs={{0,2},{1,3},{2,0},{3,1},{4,6},{5,7},{6,4},{7,5},{8,10},{9,11},{10,... | collective-permute-start | bytes 835592 | tf_op jit(solution)/shard_map/ppermute | solution.py:23
  23.2 14.2 %collective-permute-start.7 = (bf16[2,64,768]{2,1,0:T(8,128)(2,1)S(1)}, bf16[2,64,768]{2,1,0:T(8,128)(2,1)S(1)}, u32[]{:S(2)}, u32[]{:S(2)}) collective-permute-start(bf16[2,64,768]{2,1,0:T(8,128)(2,1)S(1)} %shard_map.49), channel_id=1, source_target_pairs={{0,8},{1,9},{2,10},{3,11},{4,12},{5,13},{6,14},{7,15},{8,0},{9,1},... | collective-permute-start | bytes 589832 | tf_op jit(solution)/shard_map/ppermute | solution.py:23
  29.4 22.5 %collective-permute-start.10 = (bf16[128,2176]{1,0:T(8,128)(2,1)S(1)}, bf16[128,2176]{1,0:T(8,128)(2,1)S(1)}, u32[]{:S(2)}, u32[]{:S(2)}) collective-permute-start(bf16[128,2176]{1,0:T(8,128)(2,1)S(1)} %get-tuple-element.42), channel_id=1, source_target_pairs={{0,4},{1,5},{2,6},{3,7},{4,0},{5,1},{6,2},{7,3},{8,12},{9,13},{10,... | collective-permute-start | bytes 1671176 | tf_op jit(solution)/shard_map/ppermute | solution.py:23
  29.5 16.1 %collective-permute-start.6 = (bf16[64,2176]{1,0:T(8,128)(2,1)S(1)}, bf16[64,2176]{1,0:T(8,128)(2,1)S(1)}, u32[]{:S(2)}, u32[]{:S(2)}) collective-permute-start(bf16[64,2176]{1,0:T(8,128)(2,1)S(1)} %collective-permute-done.4.refs_0_), channel_id=1, source_target_pairs={{0,2},{1,3},{2,0},{3,1},{4,6},{5,7},{6,4},{7,5},{8,10},{9,11},{10,... | collective-permute-start | bytes 835592 | tf_op jit(solution)/shard_map/ppermute | solution.py:23
  32.7 13.0 %collective-permute-start.8 = (bf16[2,64,768]{2,1,0:T(8,128)(2,1)S(1)}, bf16[2,64,768]{2,1,0:T(8,128)(2,1)S(1)}, u32[]{:S(2)}, u32[]{:S(2)}) collective-permute-start(bf16[2,64,768]{2,1,0:T(8,128)(2,1)S(1)} %get-tuple-element.38), channel_id=1, source_target_pairs={{0,2},{1,3},{2,0},{3,1},{4,6},{5,7},{6,4},{7,5},{8,10},{9,11},{10,... | collective-permute-start | bytes 589832 | tf_op jit(solution)/shard_map/ppermute | solution.py:23
  34.9 21.2 %collective-permute-start.13 = (bf16[2,64,768]{2,1,0:T(8,128)(2,1)S(1)}, bf16[2,64,768]{2,1,0:T(8,128)(2,1)S(1)}, u32[]{:S(2)}, u32[]{:S(2)}) collective-permute-start(bf16[2,64,768]{2,1,0:T(8,128)(2,1)S(1)} %get-tuple-element.48), channel_id=1, source_target_pairs={{0,10},{1,11},{2,8},{3,9},{4,14},{5,15},{6,12},{7,13},{8,2},{9,3},... | collective-permute-start | bytes 589832 | tf_op jit(solution)/shard_map/ppermute | solution.py:23
  37.4 18.7 %collective-permute-start.14 = (bf16[2,64,768]{2,1,0:T(8,128)(2,1)S(1)}, bf16[2,64,768]{2,1,0:T(8,128)(2,1)S(1)}, u32[]{:S(2)}, u32[]{:S(2)}) collective-permute-start(bf16[2,64,768]{2,1,0:T(8,128)(2,1)S(1)} %get-tuple-element.40), channel_id=1, source_target_pairs={{0,12},{1,13},{2,14},{3,15},{4,8},{5,9},{6,10},{7,11},{8,4},{9,5},... | collective-permute-start | bytes 589832 | tf_op jit(solution)/shard_map/ppermute | solution.py:23
  47.7 12.1 %collective-permute-start.15 = (bf16[2,64,768]{2,1,0:T(8,128)(2,1)S(1)}, bf16[2,64,768]{2,1,0:T(8,128)(2,1)S(1)}, u32[]{:S(2)}, u32[]{:S(2)}) collective-permute-start(bf16[2,64,768]{2,1,0:T(8,128)(2,1)S(1)} %shard_map.52), channel_id=1, source_target_pairs={{0,14},{1,15},{2,12},{3,13},{4,10},{5,11},{6,8},{7,9},{8,6},{9,7},... | collective-permute-start | bytes 589832 | tf_op jit(solution)/shard_map/ppermute | solution.py:23
  54.0 9.0 %collective-permute-start.11 = (bf16[2,64,768]{2,1,0:T(8,128)(2,1)S(1)}, bf16[2,64,768]{2,1,0:T(8,128)(2,1)S(1)}, u32[]{:S(2)}, u32[]{:S(2)}) collective-permute-start(bf16[2,64,768]{2,1,0:T(8,128)(2,1)S(1)} %get-tuple-element.45), channel_id=1, source_target_pairs={{0,4},{1,5},{2,6},{3,7},{4,0},{5,1},{6,2},{7,3},{8,12},{9,13},{10,... | collective-permute-start | bytes 589832 | tf_op jit(solution)/shard_map/ppermute | solution.py:23
  54.1 14.0 %collective-permute-start.12 = (bf16[2,64,768]{2,1,0:T(8,128)(2,1)S(1)}, bf16[2,64,768]{2,1,0:T(8,128)(2,1)S(1)}, u32[]{:S(2)}, u32[]{:S(2)}) collective-permute-start(bf16[2,64,768]{2,1,0:T(8,128)(2,1)S(1)} %get-tuple-element.46), channel_id=1, source_target_pairs={{0,6},{1,7},{2,4},{3,5},{4,2},{5,3},{6,0},{7,1},{8,14},{9,15},{10,... | collective-permute-start | bytes 589832 | tf_op jit(solution)/shard_map/ppermute | solution.py:23

commit v16 on v15

--- a/solution.py
+++ b/solution.py
@@ -159,29 +159,30 @@
     rows, columns = tie((rows, columns))
     rows = widened(rows, columns)
     side = send(rows, owners, X)
-    far, far_columns, rows, other_mat = tie((far, far_columns, rows, other_mat))
+    (out_own,) = work(rows)
+    far, far_columns, _ = tie((far, far_columns, out_own))
     far = widened(far, far_columns)
     cross = send(far, owners, Z_NEAR)
     far_side = send(far, owners, X)
     (out_far,) = work(far)
     back_far = send(out_far, owners, Z_FAR)
-    side, rows, _ = tie((side, rows, out_far))
-    pair, out_own, out_side = work(rows, side, stack=True)
-    pair = send(pair, owners, Z_NEAR)
-    cross, out_side, _ = tie((cross, out_side, out_own))
-    back_side = send(out_side, owners, X)
+    rows, side, _ = tie((rows, side, out_far))
+    near = send(rows, owners, Z_NEAR)
     cross_side = send(cross, owners, X)
     far_side, _ = tie((far_side, cross))
     out_cross, out_far_side = work(cross, far_side)
     back_cross = send(out_cross, owners, Z_NEAR ^ Z_FAR)
+    near, out_far_side, _ = tie((near, out_far_side, out_cross))
+    near_side = send(near, owners, X)
     back_far_side = send(out_far_side, owners, X ^ Z_FAR)
-    cross_side, back_far, back_side, _ = tie((cross_side, back_far, back_side, out_cross))
+    cross_side, back_far, _ = tie((cross_side, back_far, near))
     (out_cross_side,) = work(cross_side)
     back_cross_side = send(out_cross_side, owners, X ^ Z_NEAR ^ Z_FAR)
-    pair, _ = tie((pair, out_cross_side))
-    out_near, out_near_side = work(pair)
+    near_side, _ = tie((near_side, out_cross_side))
+    out_side, out_near, out_near_side = work(side, near, near_side)
+    back_near_side = send(out_near_side, owners, X ^ Z_NEAR)
+    back_side = send(out_side, owners, X)
     back_near = send(out_near, owners, Z_NEAR)
-    back_near_side = send(out_near_side, owners, X ^ Z_NEAR)
     far_parts = {
         0: out_own,
         Z_FAR: back_far,

time: 69.6 us -> 70.1 us (level)
  the two profiles are of different devices: /device:TPU:0 before, /device:TPU:4 now
where the time goes in v16:
time: 70.1 us; the launch traced here: 69.9 us
  waiting for transfers between devices  27.3 us (39%)
  starting transfers between devices  26.9 us (38%)
  Pallas kernels  12.3 us (18%)
  local copies, waits for them, and re-layouts  3.26 us (5%)
    ppermute x15, waiting for transfers between devices, send(): return lax.ppermute(block, 'expert', route)  25.1 us
    ppermute x15, starting transfers between devices, send(): return lax.ppermute(block, 'expert', route)  22.9 us
    pallas_call x5, Pallas kernels, products(): pl.pallas_call(functools.partial(products_kernel, len(pieces), int(stack)...  10.4 us
    ppermute x2, starting transfers between devices, send_across(): return lax.ppermute(block, ('pipe', 'expert'), route)  4.05 us
    unnamed x8, local copies, waits for them, and re-layouts  3.26 us
    ppermute x2, waiting for transfers between devices, send_across(): return lax.ppermute(block, ('pipe', 'expert'), route)  2.25 us
    pallas_call x2, Pallas kernels, pick_routes(): pl.pallas_call(functools.partial(pick_kernel, flips), out_shape=jax.Shape...  1.74 us
  transfers between devices with their start and end apart: 17, of which 7 were waited for; matrix products, arithmetic and copies ran while one was open for 0% of the time, Pallas kernels for 16%

profile of v16, /device:TPU:4, one launch (start us, length us, event | category | flops | bytes accessed | tf_op | source)
XLA Modules:
  0.0 69.9 jit_solution(3216300688791970375)
XLA Ops:
  0.0 0.0 collective-permute-start
  0.0 0.0 collective-permute-start.1
  0.0 4.0 %collective-permute-start.3 = (bf16[64,2048]{1,0:T(8,128)(2,1)}, bf16[64,2048]{1,0:T(8,128)(2,1)S(1)}, u32[]{:S(2)}, u32[]{:S(2)}) collective-permute-start(bf16[64,2048]{1,0:T(8,128)(2,1)} %bitcast.21), channel_id=1, source_target_pairs={{0,24},{1,25},{2,26},{3,27},{4,28},{5,29},{6,30},{7,31},{8,16},{9,... | collective-permute-start | bytes 786440 | tf_op jit(solution)/shard_map/ppermute | solution.py:33
  4.1 0.0 copy-start
  4.1 1.9 %copy-done = bf16[1,1,768,2048]{3,2,1,0:T(8,128)(2,1)S(1)} copy-done((bf16[1,1,768,2048]{3,2,1,0:T(8,128)(2,1)S(1)}, bf16[1,1,768,2048]{3,2,1,0:T(8,128)(2,1)}, u32[]{:S(2)}) %copy-start) | copy-done | bytes 3145752
  5.9 0.0 copy-start.2
  5.9 0.7 copy-done.2
  6.6 0.0 copy-start.3
  6.6 0.7 copy-done.3
  7.3 0.0 copy-start.1
  7.3 0.1 shard_map.46.columns
  7.4 0.4 collective-permute-start.4
  7.8 2.2 %collective-permute-done.1.rows = bf16[64,2048]{1,0:T(8,128)(2,1)S(1)} collective-permute-done((bf16[64,2048]{1,0:T(8,128)(2,1)}, bf16[64,2048]{1,0:T(8,128)(2,1)S(1)}, u32[]{:S(2)}, u32[]{:S(2)}) %collective-permute-start.1) | collective-permute-done | bytes 262176 | tf_op jit(solution)/shard_map/ppermute | solution.py:33
  10.1 1.6 %collective-permute-start.2 = (bf16[64,2176]{1,0:T(8,128)(2,1)S(1)}, bf16[64,2176]{1,0:T(8,128)(2,1)S(1)}, u32[]{:S(2)}, u32[]{:S(2)}) collective-permute-start(bf16[64,2176]{1,0:T(8,128)(2,1)S(1)} %shard_map.47.refs_0_), channel_id=1, source_target_pairs={{0,2},{1,3},{2,0},{3,1},{4,6},{5,7},{6,4},{7,5},{8,10},{9,11},{10,... | collective-permute-start | bytes 835592 | tf_op jit(solution)/shard_map/ppermute | solution.py:23
  11.6 0.0 collective-permute-done.other
  11.6 0.0 copy-done.1
  11.6 2.0 %shard_map.48.refs_0_ = bf16[2,64,768]{2,1,0:T(8,128)(2,1)S(1)} custom-call(bf16[768,2048]{1,0:T(8,128)(2,1)S(1)} %bitcast.11, bf16[768,2048]{1,0:T(8,128)(2,1)S(1)} %collective-permute-done.other, bf16[64,2176]{1,0:T(8,128)(2,1)S(1)} %shard_map.47.refs_0_), custom_call_target="tpu_custom_call" | custom-call | flops 4026531840 | bytes 6750208 | tf_op jit(solution)/shard_map/pallas_call | solution.py:98
  13.6 3.7 %collective-permute-done.4.columns = bf16[64,128]{1,0:T(8,128)(2,1)S(1)} collective-permute-done((bf16[64,128]{1,0:T(8,128)(2,1)S(1)}, bf16[64,128]{1,0:T(8,128)(2,1)S(1)}, u32[]{:S(2)}, u32[]{:S(2)}) %collective-permute-start.4) | collective-permute-done | bytes 16416 | tf_op jit(solution)/shard_map/ppermute | solution.py:23
  17.3 0.0 collective-permute-done.3.rows
  17.4 1.6 %collective-permute-start.7 = (bf16[64,2176]{1,0:T(8,128)(2,1)S(1)}, bf16[64,2176]{1,0:T(8,128)(2,1)S(1)}, u32[]{:S(2)}, u32[]{:S(2)}) collective-permute-start(bf16[64,2176]{1,0:T(8,128)(2,1)S(1)} %shard_map.49.refs_0_), channel_id=1, source_target_pairs={{0,2},{1,3},{2,0},{3,1},{4,6},{5,7},{6,4},{7,5},{8,10},{9,11},{10,... | collective-permute-start | bytes 835592 | tf_op jit(solution)/shard_map/ppermute | solution.py:23
  18.9 1.5 %collective-permute-start.6 = (bf16[64,2176]{1,0:T(8,128)(2,1)S(1)}, bf16[64,2176]{1,0:T(8,128)(2,1)S(1)}, u32[]{:S(2)}, u32[]{:S(2)}) collective-permute-start(bf16[64,2176]{1,0:T(8,128)(2,1)S(1)} %shard_map.49.refs_0_), channel_id=1, source_target_pairs={{0,4},{1,5},{2,6},{3,7},{4,0},{5,1},{6,2},{7,3},{8,12},{9,13},{10,... | collective-permute-start | bytes 835592 | tf_op jit(solution)/shard_map/ppermute | solution.py:23
  20.4 2.0 %shard_map.50 = bf16[2,64,768]{2,1,0:T(8,128)(2,1)S(1)} custom-call(bf16[768,2048]{1,0:T(8,128)(2,1)S(1)} %bitcast.12, bf16[768,2048]{1,0:T(8,128)(2,1)S(1)} %collective-permute-done.other, bf16[64,2176]{1,0:T(8,128)(2,1)S(1)} %shard_map.49.refs_0_), custom_call_target="tpu_custom_call" | custom-call | flops 4026531840 | bytes 6750208 | tf_op jit(solution)/shard_map/pallas_call | solution.py:98
  22.4 2.7 %collective-permute-start.10 = (bf16[2,64,768]{2,1,0:T(8,128)(2,1)S(1)}, bf16[2,64,768]{2,1,0:T(8,128)(2,1)S(1)}, u32[]{:S(2)}, u32[]{:S(2)}) collective-permute-start(bf16[2,64,768]{2,1,0:T(8,128)(2,1)S(1)} %shard_map.50), channel_id=1, source_target_pairs={{0,8},{1,9},{2,10},{3,11},{4,12},{5,13},{6,14},{7,15},{8,0},{9,1},... | collective-permute-start | bytes 589832 | tf_op jit(solution)/shard_map/ppermute | solution.py:23
  25.1 0.0 collective-permute-done.2.refs_0_
  25.1 0.7 %collective-permute-start.5 = (bf16[64,2176]{1,0:T(8,128)(2,1)S(1)}, bf16[64,2176]{1,0:T(8,128)(2,1)S(1)}, u32[]{:S(2)}, u32[]{:S(2)}) collective-permute-start(bf16[64,2176]{1,0:T(8,128)(2,1)S(1)} %shard_map.47.refs_0_), channel_id=1, source_target_pairs={{0,4},{1,5},{2,6},{3,7},{4,0},{5,1},{6,2},{7,3},{8,12},{9,13},{10,... | collective-permute-start | bytes 835592 | tf_op jit(solution)/shard_map/ppermute | solution.py:23
  25.8 0.0 collective-permute-done.7.refs_1_
  25.8 5.5 %collective-permute-done.6.refs_0_ = bf16[64,2176]{1,0:T(8,128)(2,1)S(1)} collective-permute-done((bf16[64,2176]{1,0:T(8,128)(2,1)S(1)}, bf16[64,2176]{1,0:T(8,128)(2,1)S(1)}, u32[]{:S(2)}, u32[]{:S(2)}) %collective-permute-start.6) | collective-permute-done | bytes 278560 | tf_op jit(solution)/shard_map/ppermute | solution.py:23
  31.3 2.1 %collective-permute-start.9 = (bf16[64,2176]{1,0:T(8,128)(2,1)S(1)}, bf16[64,2176]{1,0:T(8,128)(2,1)S(1)}, u32[]{:S(2)}, u32[]{:S(2)}) collective-permute-start(bf16[64,2176]{1,0:T(8,128)(2,1)S(1)} %collective-permute-done.6.refs_0_), channel_id=1, source_target_pairs={{0,2},{1,3},{2,0},{3,1},{4,6},{5,7},{6,4},{7,5},{8,10},{9,11},{10,... | collective-permute-start | bytes 835592 | tf_op jit(solution)/shard_map/ppermute | solution.py:23
  33.4 2.2 %shard_map.51 = (bf16[2,64,768]{2,1,0:T(8,128)(2,1)S(1)}, bf16[2,64,768]{2,1,0:T(8,128)(2,1)S(1)}) custom-call(bf16[768,2048]{1,0:T(8,128)(2,1)S(1)} %bitcast.13, bf16[768,2048]{1,0:T(8,128)(2,1)S(1)} %collective-permute-done.other, bf16[64,2176]{1,0:T(8,128)(2,1)S(1)} %collective-permute-done.6.refs_0_, bf16[64,2176]{1,0:T(8,128)(2,1)S(1)} %collective-permute-done.7.refs_1_), custom_call_target="tpu_custom_call" | custom-call | flops 8053063680 | bytes 7208960 | tf_op jit(solution)/shard_map/pallas_call | solution.py:98
  35.6 3.1 %collective-permute-start.15 = (bf16[2,64,768]{2,1,0:T(8,128)(2,1)S(1)}, bf16[2,64,768]{2,1,0:T(8,128)(2,1)S(1)}, u32[]{:S(2)}, u32[]{:S(2)}) collective-permute-start(bf16[2,64,768]{2,1,0:T(8,128)(2,1)S(1)} %get-tuple-element.30), channel_id=1, source_target_pairs={{0,12},{1,13},{2,14},{3,15},{4,8},{5,9},{6,10},{7,11},{8,4},{9,5},... | collective-permute-start | bytes 589832 | tf_op jit(solution)/shard_map/ppermute | solution.py:23
  38.7 0.0 collective-permute-done.5.refs_1_
  38.7 3.4 %collective-permute-start.14 = (bf16[2,64,768]{2,1,0:T(8,128)(2,1)S(1)}, bf16[2,64,768]{2,1,0:T(8,128)(2,1)S(1)}, u32[]{:S(2)}, u32[]{:S(2)}) collective-permute-start(bf16[2,64,768]{2,1,0:T(8,128)(2,1)S(1)} %get-tuple-element.38), channel_id=1, source_target_pairs={{0,10},{1,11},{2,8},{3,9},{4,14},{5,15},{6,12},{7,13},{8,2},{9,3},... | collective-permute-start | bytes 589832 | tf_op jit(solution)/shard_map/ppermute | solution.py:23
  42.1 0.6 collective-permute-start.8
  42.7 0.0 collective-permute-done.10.refs_1_
  42.7 0.0 collective-permute-done.9.refs_0_
  42.7 2.0 %shard_map.52 = bf16[2,64,768]{2,1,0:T(8,128)(2,1)S(1)} custom-call(bf16[768,2048]{1,0:T(8,128)(2,1)S(1)} %bitcast.14, bf16[768,2048]{1,0:T(8,128)(2,1)S(1)} %collective-permute-done.other, bf16[64,2176]{1,0:T(8,128)(2,1)S(1)} %collective-permute-done.9.refs_0_), custom_call_target="tpu_custom_call" | custom-call | flops 4026531840 | bytes 6750208 | tf_op jit(solution)/shard_map/pallas_call | solution.py:98
  44.7 1.9 %collective-permute-start.16 = (bf16[2,64,768]{2,1,0:T(8,128)(2,1)S(1)}, bf16[2,64,768]{2,1,0:T(8,128)(2,1)S(1)}, u32[]{:S(2)}, u32[]{:S(2)}) collective-permute-start(bf16[2,64,768]{2,1,0:T(8,128)(2,1)S(1)} %shard_map.52), channel_id=1, source_target_pairs={{0,14},{1,15},{2,12},{3,13},{4,10},{5,11},{6,8},{7,9},{8,6},{9,7},... | collective-permute-start | bytes 589832 | tf_op jit(solution)/shard_map/ppermute | solution.py:23
  46.6 10.5 %collective-permute-done.8.refs_2_ = bf16[64,2176]{1,0:T(8,128)(2,1)S(1)} collective-permute-done((bf16[64,2176]{1,0:T(8,128)(2,1)S(1)}, bf16[64,2176]{1,0:T(8,128)(2,1)S(1)}, u32[]{:S(2)}, u32[]{:S(2)}) %collective-permute-start.8) | collective-permute-done | bytes 278560 | tf_op jit(solution)/shard_map/ppermute | solution.py:23
  57.1 2.2 %shard_map.53 = (bf16[2,64,768]{2,1,0:T(8,128)(2,1)S(1)}, bf16[2,64,768]{2,1,0:T(8,128)(2,1)S(1)}, bf16[2,64,768]{2,1,0:T(8,128)(2,1)S(1)}) custom-call(bf16[768,2048]{1,0:T(8,128)(2,1)S(1)} %bitcast.15, bf16[768,2048]{1,0:T(8,128)(2,1)S(1)} %collective-permute-done.other, bf16[64,2176]{1,0:T(8,128)(2,1)S(1)} %collective-permute-done.2.refs_0_, ...), custom_call_target="tpu_custom_call" | custom-call | flops 12079595520 | bytes 7667712 | tf_op jit(solution)/shard_map/pallas_call | solution.py:98
  59.3 0.1 collective-permute-start.11
  59.4 0.1 collective-permute-start.12
  59.5 0.0 collective-permute-done.14.refs_2_
  59.5 3.4 %collective-permute-start.13 = (bf16[2,64,768]{2,1,0:T(8,128)(2,1)S(1)}, bf16[2,64,768]{2,1,0:T(8,128)(2,1)S(1)}, u32[]{:S(2)}, u32[]{:S(2)}) collective-permute-start(bf16[2,64,768]{2,1,0:T(8,128)(2,1)S(1)} %get-tuple-element.36), channel_id=1, source_target_pairs={{0,6},{1,7},{2,4},{3,5},{4,2},{5,3},{6,0},{7,1},{8,14},{9,15},{10,... | collective-permute-start | bytes 589832 | tf_op jit(solution)/shard_map/ppermute | solution.py:23
  62.9 0.0 collective-permute-done.15.refs_3_
  62.9 0.0 collective-permute-done.16.refs_4_
  62.9 0.4 shard_map.54.refs_3_
  63.3 1.7 %collective-permute-done.11.refs_0_ = bf16[2,64,768]{2,1,0:T(8,128)(2,1)S(1)} collective-permute-done((bf16[2,64,768]{2,1,0:T(8,128)(2,1)S(1)}, bf16[2,64,768]{2,1,0:T(8,128)(2,1)S(1)}, u32[]{:S(2)}, u32[]{:S(2)}) %collective-permute-start.11) | collective-permute-done | bytes 196640 | tf_op jit(solution)/shard_map/ppermute | solution.py:23
  65.0 0.1 collective-permute-done.12.refs_1_
  65.1 3.5 %collective-permute-done.13.refs_2_ = bf16[2,64,768]{2,1,0:T(8,128)(2,1)S(1)} collective-permute-done((bf16[2,64,768]{2,1,0:T(8,128)(2,1)S(1)}, bf16[2,64,768]{2,1,0:T(8,128)(2,1)S(1)}, u32[]{:S(2)}, u32[]{:S(2)}) %collective-permute-start.13) | collective-permute-done | bytes 196640 | tf_op jit(solution)/shard_map/ppermute | solution.py:23
  68.6 1.3 %shard_map.55 = bf16[512,768]{1,0:T(8,128)(2,1)} custom-call(s32[8,64]{1,0:T(8,128)S(1)} %bitcast.18, bf16[2,64,768]{2,1,0:T(8,128)(2,1)S(1)} %collective-permute-done.11.refs_0_, bf16[2,64,768]{2,1,0:T(8,128)(2,1)S(1)} %collective-permute-done.12.refs_1_, bf16[2,64,768]{2,1,0:T(8,128)(2,1)S(1)} %collective-permute-done.13.refs_2_, ...), custom_call_target="tpu_custom_call" | custom-call | tf_op jit(solution)/shard_map/pallas_call | solution.py:139
  (2 shorter events, 0.0 us)
Async XLA Ops:
  0.0 11.6 %collective-permute-start = (bf16[768,2048]{1,0:T(8,128)(2,1)}, bf16[768,2048]{1,0:T(8,128)(2,1)S(1)}, u32[]{:S(2)}, u32[]{:S(2)}) collective-permute-start(bf16[768,2048]{1,0:T(8,128)(2,1)} %bitcast.9), channel_id=1, source_target_pairs={{0,1},{1,0},{2,3},{3,2},{4,5},{5,4},{6,7},{7,6},{8,9},{9,8},{10,11... | collective-permute-start | bytes 9437192 | tf_op jit(solution)/shard_map/ppermute | solution.py:23
  0.0 10.0 %collective-permute-start.1 = (bf16[64,2048]{1,0:T(8,128)(2,1)}, bf16[64,2048]{1,0:T(8,128)(2,1)S(1)}, u32[]{:S(2)}, u32[]{:S(2)}) collective-permute-start(bf16[64,2048]{1,0:T(8,128)(2,1)} %bitcast.20), channel_id=1, source_target_pairs={{0,16},{1,17},{2,18},{3,19},{4,20},{5,21},{6,22},{7,23},{8,24},{9,... | collective-permute-start | bytes 786440 | tf_op jit(solution)/shard_map/ppermute | solution.py:33
  0.0 17.3 %collective-permute-start.3 = (bf16[64,2048]{1,0:T(8,128)(2,1)}, bf16[64,2048]{1,0:T(8,128)(2,1)S(1)}, u32[]{:S(2)}, u32[]{:S(2)}) collective-permute-start(bf16[64,2048]{1,0:T(8,128)(2,1)} %bitcast.21), channel_id=1, source_target_pairs={{0,24},{1,25},{2,26},{3,27},{4,28},{5,29},{6,30},{7,31},{8,16},{9,... | collective-permute-start | bytes 786440 | tf_op jit(solution)/shard_map/ppermute | solution.py:33
  4.1 1.9 %copy-start = (bf16[1,1,768,2048]{3,2,1,0:T(8,128)(2,1)S(1)}, bf16[1,1,768,2048]{3,2,1,0:T(8,128)(2,1)}, u32[]{:S(2)}) copy-start(bf16[1,1,768,2048]{3,2,1,0:T(8,128)(2,1)} %param.7) | copy-start | bytes 9437188
  5.9 0.7 copy-start.2
  6.6 0.7 copy-start.3
  7.3 4.3 %copy-start.1 = (bf16[1,1,768,2048]{3,2,1,0:T(8,128)(2,1)S(1)}, bf16[1,1,768,2048]{3,2,1,0:T(8,128)(2,1)}, u32[]{:S(2)}) copy-start(bf16[1,1,768,2048]{3,2,1,0:T(8,128)(2,1)} %param.7) | copy-start | bytes 9437188
  7.4 9.9 %collective-permute-start.4 = (bf16[64,128]{1,0:T(8,128)(2,1)S(1)}, bf16[64,128]{1,0:T(8,128)(2,1)S(1)}, u32[]{:S(2)}, u32[]{:S(2)}) collective-permute-start(bf16[64,128]{1,0:T(8,128)(2,1)S(1)} %shard_map.46.columns), channel_id=1, source_target_pairs={{0,8},{1,9},{2,10},{3,11},{4,12},{5,13},{6,14},{7,15},{8,0},{9,1},... | collective-permute-start | bytes 49160 | tf_op jit(solution)/shard_map/ppermute | solution.py:23
  10.1 15.0 %collective-permute-start.2 = (bf16[64,2176]{1,0:T(8,128)(2,1)S(1)}, bf16[64,2176]{1,0:T(8,128)(2,1)S(1)}, u32[]{:S(2)}, u32[]{:S(2)}) collective-permute-start(bf16[64,2176]{1,0:T(8,128)(2,1)S(1)} %shard_map.47.refs_0_), channel_id=1, source_target_pairs={{0,2},{1,3},{2,0},{3,1},{4,6},{5,7},{6,4},{7,5},{8,10},{9,11},{10,... | collective-permute-start | bytes 835592 | tf_op jit(solution)/shard_map/ppermute | solution.py:23
  17.4 8.4 %collective-permute-start.7 = (bf16[64,2176]{1,0:T(8,128)(2,1)S(1)}, bf16[64,2176]{1,0:T(8,128)(2,1)S(1)}, u32[]{:S(2)}, u32[]{:S(2)}) collective-permute-start(bf16[64,2176]{1,0:T(8,128)(2,1)S(1)} %shard_map.49.refs_0_), channel_id=1, source_target_pairs={{0,2},{1,3},{2,0},{3,1},{4,6},{5,7},{6,4},{7,5},{8,10},{9,11},{10,... | collective-permute-start | bytes 835592 | tf_op jit(solution)/shard_map/ppermute | solution.py:23
  18.9 12.4 %collective-permute-start.6 = (bf16[64,2176]{1,0:T(8,128)(2,1)S(1)}, bf16[64,2176]{1,0:T(8,128)(2,1)S(1)}, u32[]{:S(2)}, u32[]{:S(2)}) collective-permute-start(bf16[64,2176]{1,0:T(8,128)(2,1)S(1)} %shard_map.49.refs_0_), channel_id=1, source_target_pairs={{0,4},{1,5},{2,6},{3,7},{4,0},{5,1},{6,2},{7,3},{8,12},{9,13},{10,... | collective-permute-start | bytes 835592 | tf_op jit(solution)/shard_map/ppermute | solution.py:23
  22.4 20.3 %collective-permute-start.10 = (bf16[2,64,768]{2,1,0:T(8,128)(2,1)S(1)}, bf16[2,64,768]{2,1,0:T(8,128)(2,1)S(1)}, u32[]{:S(2)}, u32[]{:S(2)}) collective-permute-start(bf16[2,64,768]{2,1,0:T(8,128)(2,1)S(1)} %shard_map.50), channel_id=1, source_target_pairs={{0,8},{1,9},{2,10},{3,11},{4,12},{5,13},{6,14},{7,15},{8,0},{9,1},... | collective-permute-start | bytes 589832 | tf_op jit(solution)/shard_map/ppermute | solution.py:23
  25.1 13.6 %collective-permute-start.5 = (bf16[64,2176]{1,0:T(8,128)(2,1)S(1)}, bf16[64,2176]{1,0:T(8,128)(2,1)S(1)}, u32[]{:S(2)}, u32[]{:S(2)}) collective-permute-start(bf16[64,2176]{1,0:T(8,128)(2,1)S(1)} %shard_map.47.refs_0_), channel_id=1, source_target_pairs={{0,4},{1,5},{2,6},{3,7},{4,0},{5,1},{6,2},{7,3},{8,12},{9,13},{10,... | collective-permute-start | bytes 835592 | tf_op jit(solution)/shard_map/ppermute | solution.py:23
  31.3 11.3 %collective-permute-start.9 = (bf16[64,2176]{1,0:T(8,128)(2,1)S(1)}, bf16[64,2176]{1,0:T(8,128)(2,1)S(1)}, u32[]{:S(2)}, u32[]{:S(2)}) collective-permute-start(bf16[64,2176]{1,0:T(8,128)(2,1)S(1)} %collective-permute-done.6.refs_0_), channel_id=1, source_target_pairs={{0,2},{1,3},{2,0},{3,1},{4,6},{5,7},{6,4},{7,5},{8,10},{9,11},{10,... | collective-permute-start | bytes 835592 | tf_op jit(solution)/shard_map/ppermute | solution.py:23
  35.6 27.3 %collective-permute-start.15 = (bf16[2,64,768]{2,1,0:T(8,128)(2,1)S(1)}, bf16[2,64,768]{2,1,0:T(8,128)(2,1)S(1)}, u32[]{:S(2)}, u32[]{:S(2)}) collective-permute-start(bf16[2,64,768]{2,1,0:T(8,128)(2,1)S(1)} %get-tuple-element.30), channel_id=1, source_target_pairs={{0,12},{1,13},{2,14},{3,15},{4,8},{5,9},{6,10},{7,11},{8,4},{9,5},... | collective-permute-start | bytes 589832 | tf_op jit(solution)/shard_map/ppermute | solution.py:23
  38.7 20.8 %collective-permute-start.14 = (bf16[2,64,768]{2,1,0:T(8,128)(2,1)S(1)}, bf16[2,64,768]{2,1,0:T(8,128)(2,1)S(1)}, u32[]{:S(2)}, u32[]{:S(2)}) collective-permute-start(bf16[2,64,768]{2,1,0:T(8,128)(2,1)S(1)} %get-tuple-element.38), channel_id=1, source_target_pairs={{0,10},{1,11},{2,8},{3,9},{4,14},{5,15},{6,12},{7,13},{8,2},{9,3},... | collective-permute-start | bytes 589832 | tf_op jit(solution)/shard_map/ppermute | solution.py:23
  42.1 15.0 %collective-permute-start.8 = (bf16[64,2176]{1,0:T(8,128)(2,1)S(1)}, bf16[64,2176]{1,0:T(8,128)(2,1)S(1)}, u32[]{:S(2)}, u32[]{:S(2)}) collective-permute-start(bf16[64,2176]{1,0:T(8,128)(2,1)S(1)} %collective-permute-done.5.refs_1_), channel_id=1, source_target_pairs={{0,2},{1,3},{2,0},{3,1},{4,6},{5,7},{6,4},{7,5},{8,10},{9,11},{10,... | collective-permute-start | bytes 835592 | tf_op jit(solution)/shard_map/ppermute | solution.py:23
  44.7 18.2 %collective-permute-start.16 = (bf16[2,64,768]{2,1,0:T(8,128)(2,1)S(1)}, bf16[2,64,768]{2,1,0:T(8,128)(2,1)S(1)}, u32[]{:S(2)}, u32[]{:S(2)}) collective-permute-start(bf16[2,64,768]{2,1,0:T(8,128)(2,1)S(1)} %shard_map.52), channel_id=1, source_target_pairs={{0,14},{1,15},{2,12},{3,13},{4,10},{5,11},{6,8},{7,9},{8,6},{9,7},... | collective-permute-start | bytes 589832 | tf_op jit(solution)/shard_map/ppermute | solution.py:23
  59.3 5.7 %collective-permute-start.11 = (bf16[2,64,768]{2,1,0:T(8,128)(2,1)S(1)}, bf16[2,64,768]{2,1,0:T(8,128)(2,1)S(1)}, u32[]{:S(2)}, u32[]{:S(2)}) collective-permute-start(bf16[2,64,768]{2,1,0:T(8,128)(2,1)S(1)} %get-tuple-element.34), channel_id=1, source_target_pairs={{0,2},{1,3},{2,0},{3,1},{4,6},{5,7},{6,4},{7,5},{8,10},{9,11},{10,... | collective-permute-start | bytes 589832 | tf_op jit(solution)/shard_map/ppermute | solution.py:23
  59.4 5.7 %collective-permute-start.12 = (bf16[2,64,768]{2,1,0:T(8,128)(2,1)S(1)}, bf16[2,64,768]{2,1,0:T(8,128)(2,1)S(1)}, u32[]{:S(2)}, u32[]{:S(2)}) collective-permute-start(bf16[2,64,768]{2,1,0:T(8,128)(2,1)S(1)} %get-tuple-element.35), channel_id=1, source_target_pairs={{0,4},{1,5},{2,6},{3,7},{4,0},{5,1},{6,2},{7,3},{8,12},{9,13},{10,... | collective-permute-start | bytes 589832 | tf_op jit(solution)/shard_map/ppermute | solution.py:23
  59.5 9.1 %collective-permute-start.13 = (bf16[2,64,768]{2,1,0:T(8,128)(2,1)S(1)}, bf16[2,64,768]{2,1,0:T(8,128)(2,1)S(1)}, u32[]{:S(2)}, u32[]{:S(2)}) collective-permute-start(bf16[2,64,768]{2,1,0:T(8,128)(2,1)S(1)} %get-tuple-element.36), channel_id=1, source_target_pairs={{0,6},{1,7},{2,4},{3,5},{4,2},{5,3},{6,0},{7,1},{8,14},{9,15},{10,... | collective-permute-start | bytes 589832 | tf_op jit(solution)/shard_map/ppermute | solution.py:23

commit v17 on v13

--- a/solution.py
+++ b/solution.py
@@ -33,7 +33,7 @@
     return lax.ppermute(block, ("pipe", "expert"), route)
 
 
-def gates_kernel(ids, gates, weight, out):
+def gates_kernel(ids, gates, out):
     top, tokens = ids.shape
     expert = lax.broadcasted_iota(jnp.int32, (LANES, tokens), 0)
     total = jnp.zeros((LANES, tokens), jnp.float32)
@@ -43,12 +43,12 @@
     out[...] = total.T.astype(jnp.bfloat16)
 
 
-def gate_columns(ids, gates, weight):
+def gate_columns(ids, gates):
     return pl.pallas_call(
         gates_kernel,
         out_shape=jax.ShapeDtypeStruct((ids.shape[1], LANES), jnp.bfloat16),
         compiler_params=pltpu.CompilerParams(vmem_limit_bytes=16 << 20),
-    )(ids, gates, weight)
+    )(ids, gates)
 
 
 def widen_kernel(rows, columns, out):
@@ -66,46 +66,56 @@
     )(rows, columns)
 
 
-def products_kernel(paired, weight, other, *refs):
+def turn_kernel(weight, other, out):
+    hidden = weight.shape[0]
+    out[:, :hidden] = weight[...].T
+    out[:, hidden:] = other[...].T
+
+
+def turned(weight, other):
     hidden, depth = weight.shape
-    rows, gates, at = [], [], 0
-    for pair in paired:
-        rows.append(refs[at][:, :depth])
-        gates.append(refs[at + 1][...] if pair else refs[at][:, depth:])
-        at += 1 + pair
-    outs = refs[at:]
+    return pl.pallas_call(
+        turn_kernel,
+        out_shape=jax.ShapeDtypeStruct((depth, CORES * hidden), weight.dtype),
+        compiler_params=pltpu.CompilerParams(vmem_limit_bytes=24 << 20),
+        cost_estimate=pl.CostEstimate(
+            flops=4 * CORES * 1024 * hidden * depth, bytes_accessed=0, transcendentals=0
+        ),
+    )(weight, other)
+
+
+def products_kernel(count, weights, *refs):
+    pieces, outs = refs[:count], refs[count:]
+    depth, width = weights.shape
+    hidden = width // CORES
     tokens = outs[0].shape[1]
     me = lax.axis_index("expert")
     core = lax.rem(me, CORES)
-    stacked = jnp.concatenate(rows, axis=0)
-    gates = jnp.concatenate(gates, axis=0).astype(jnp.float32)
+    stacked = jnp.concatenate([p[...] for p in pieces], axis=0)
+    gates = stacked[:, depth:].astype(jnp.float32)
     column = lax.broadcasted_iota(jnp.int32, gates.shape, 1)
-    for mat, to in ((weight, core), (other, 1 - core)):
+    product = jnp.dot(stacked[:, :depth], weights[...], preferred_element_type=jnp.float32)
+    for half, to in enumerate((core, 1 - core)):
         scale = jnp.sum(jnp.where(column == me - core + to, gates, 0.0), axis=1, keepdims=True)
-        product = lax.dot_general(
-            stacked, mat[...], (((1,), (1,)), ((), ())), preferred_element_type=jnp.float32
-        )
-        scaled = (product * scale).astype(jnp.bfloat16)
+        scaled = (product[:, half * hidden : (half + 1) * hidden] * scale).astype(jnp.bfloat16)
         for j, out in enumerate(outs):
             out[to] = scaled[j * tokens : (j + 1) * tokens]
 
 
-def products(pieces, weight, other):
-    hidden, depth = weight.shape
-    paired = [isinstance(p, tuple) for p in pieces]
-    operands = [x for p in pieces for x in (p if isinstance(p, tuple) else (p,))]
-    tokens = operands[0].shape[0]
-    total = len(pieces) * tokens
-    return pl.pallas_call(
-        functools.partial(products_kernel, paired),
-        out_shape=[jax.ShapeDtypeStruct((CORES, tokens, hidden), jnp.bfloat16)] * len(pieces),
+def products(pieces, tokens, weights):
+    depth, width = weights.shape
+    total = sum(p.shape[0] for p in pieces)
+    one = jax.ShapeDtypeStruct((CORES, tokens, width // CORES), jnp.bfloat16)
+    return pl.pallas_call(
+        functools.partial(products_kernel, len(pieces)),
+        out_shape=[one] * (total // tokens),
         compiler_params=pltpu.CompilerParams(vmem_limit_bytes=16 << 20),
         cost_estimate=pl.CostEstimate(
-            flops=20 * CORES * total * hidden * depth,
-            bytes_accessed=2 * (total * (2 * hidden + depth) + 2 * hidden * depth),
+            flops=20 * total * width * depth,
+            bytes_accessed=2 * (total * (width + depth) + width * depth),
             transcendentals=0,
         ),
-    )(weight, other, *operands)
+    )(weights, *pieces)
 
 
 def pick_kernel(ids, *refs):
@@ -144,14 +154,15 @@
     tie = lax.optimization_barrier
 
     def work(*pieces):
-        return products(list(pieces), weight_mat, other_mat)
+        return products(list(pieces), tokens, weights)
 
     far = send_across(upstream, owners, Z_FAR)
     rows = send_across(upstream, owners, 0)
     other_mat = send(weight_mat, owners, 0, 1)
-    columns = gate_columns(route_ids.T, route_gates.T, weight_mat)
+    columns = gate_columns(route_ids.T, route_gates.T)
     far_columns = send(columns, owners, Z_FAR)
-    far, far_columns, other_mat = tie((far, far_columns, other_mat))
+    weights = turned(weight_mat, other_mat)
+    far, far_columns, weights = tie((far, far_columns, weights))
     far = widened(far, far_columns)
     cross = send(far, owners, Z_NEAR)
     far_side = send(far, owners, X)
@@ -165,20 +176,18 @@
     cross_side = send(cross, owners, X)
     (out_cross,) = work(cross)
     back_cross = send(out_cross, owners, Z_NEAR ^ Z_FAR)
-    far_side, back_far, _ = tie((far_side, back_far, out_cross))
+    far_side, back_far, near, _ = tie((far_side, back_far, near, out_cross))
+    near_side = send(near, owners, X)
     (out_far_side,) = work(far_side)
     back_far_side = send(out_far_side, owners, X ^ Z_FAR)
-    near, cross_side, _ = tie((near, cross_side, out_far_side))
-    near_side = send(near, owners, X)
+    cross_side, _ = tie((cross_side, out_far_side))
     (out_cross_side,) = work(cross_side)
     back_cross_side = send(out_cross_side, owners, X ^ Z_NEAR ^ Z_FAR)
-    side, near, _ = tie((side, near, out_cross_side))
-    out_side, out_near = work(side, near)
+    side, near_side, _ = tie((side, near_side, out_cross_side))
+    out_side, out_near, out_near_side = work(side, near, near_side)
+    back_near_side = send(out_near_side, owners, X ^ Z_NEAR)
     back_side = send(out_side, owners, X)
     back_near = send(out_near, owners, Z_NEAR)
-    near_side, _ = tie((near_side, out_near))
-    (out_near_side,) = work(near_side)
-    back_near_side = send(out_near_side, owners, X ^ Z_NEAR)
     rows, _ = tie((rows, out_near_side))
     (out_own,) = work(rows)
     received = {

time: 67.2 us -> 71.1 us (1.058)
  the two profiles are of different devices: /device:TPU:0 before, /device:TPU:26 now
where the time goes in v17:
time: 71.1 us; the launch traced here: 70.9 us
  waiting for transfers between devices  40.6 us (57%)
  starting transfers between devices  16.4 us (23%)
  Pallas kernels  10.5 us (15%)
  local copies, waits for them, and re-layouts  3.26 us (5%)
    ppermute x15, waiting for transfers between devices, send(): return lax.ppermute(block, 'expert', route)  40.6 us
    ppermute x15, starting transfers between devices, send(): return lax.ppermute(block, 'expert', route)  14.6 us
    pallas_call x6, Pallas kernels, products(): pl.pallas_call(functools.partial(products_kernel, len(pieces)), out_shape...  7.34 us
    unnamed x8, local copies, waits for them, and re-layouts  3.26 us
    ppermute x2, starting transfers between devices, send_across(): return lax.ppermute(block, ('pipe', 'expert'), route)  1.8 us
    pallas_call x1, Pallas kernels, turned(): pl.pallas_call(turn_kernel, out_shape=jax.ShapeDtypeStruct((depth, CORES...  1.67 us
  transfers between devices with their start and end apart: 17, of which 6 were waited for; matrix products, arithmetic and copies ran while one was open for 0% of the time, Pallas kernels for 13%

profile of v17, /device:TPU:26, one launch (start us, length us, event | category | flops | bytes accessed | tf_op | source)
XLA Modules:
  0.0 70.9 jit_solution(3173630253444268901)
XLA Ops:
  0.0 0.0 collective-permute-start.2
  0.0 1.3 %collective-permute-start = (bf16[64,2048]{1,0:T(8,128)(2,1)}, bf16[64,2048]{1,0:T(8,128)(2,1)S(1)}, u32[]{:S(2)}, u32[]{:S(2)}) collective-permute-start(bf16[64,2048]{1,0:T(8,128)(2,1)} %bitcast.14), channel_id=1, source_target_pairs={{0,24},{1,25},{2,26},{3,27},{4,28},{5,29},{6,30},{7,31},{8,16},{9,... | collective-permute-start | bytes 786440 | tf_op jit(solution)/shard_map/ppermute | solution.py:33
  1.3 0.5 collective-permute-start.4
  1.8 0.0 copy-start
  1.8 0.7 copy-done
  2.5 0.0 copy-start.2
  2.5 0.7 copy-done.2
  3.2 0.1 shard_map.46.columns
  3.3 2.6 %collective-permute-start.1 = (bf16[64,128]{1,0:T(8,128)(2,1)S(1)}, bf16[64,128]{1,0:T(8,128)(2,1)S(1)}, u32[]{:S(2)}, u32[]{:S(2)}) collective-permute-start(bf16[64,128]{1,0:T(8,128)(2,1)S(1)} %shard_map.46.columns), channel_id=1, source_target_pairs={{0,8},{1,9},{2,10},{3,11},{4,12},{5,13},{6,14},{7,15},{8,0},{9,1},... | collective-permute-start | bytes 49160 | tf_op jit(solution)/shard_map/ppermute | solution.py:23
  5.9 0.0 collective-permute-done.2.other
  5.9 0.0 copy-start.3
  5.9 1.9 %copy-done.3 = bf16[1,1,768,2048]{3,2,1,0:T(8,128)(2,1)S(1)} copy-done((bf16[1,1,768,2048]{3,2,1,0:T(8,128)(2,1)S(1)}, bf16[1,1,768,2048]{3,2,1,0:T(8,128)(2,1)}, u32[]{:S(2)}) %copy-start.3) | copy-done | bytes 3145752
  7.8 1.7 %shard_map.47.weights = bf16[2048,1536]{1,0:T(8,128)(2,1)S(1)} custom-call(bf16[768,2048]{1,0:T(8,128)(2,1)S(1)} %bitcast.13, bf16[768,2048]{1,0:T(8,128)(2,1)S(1)} %collective-permute-done.2.other), custom_call_target="tpu_custom_call" | custom-call | flops 12884901888 | tf_op jit(solution)/shard_map/pallas_call | solution.py:77
  9.5 7.5 %collective-permute-done.1.columns = bf16[64,128]{1,0:T(8,128)(2,1)S(1)} collective-permute-done((bf16[64,128]{1,0:T(8,128)(2,1)S(1)}, bf16[64,128]{1,0:T(8,128)(2,1)S(1)}, u32[]{:S(2)}, u32[]{:S(2)}) %collective-permute-start.1) | collective-permute-done | bytes 16416 | tf_op jit(solution)/shard_map/ppermute | solution.py:23
  17.0 0.0 collective-permute-done.rows
  17.0 0.1 collective-permute-start.3
  17.1 0.6 collective-permute-start.6
  17.7 1.2 %shard_map.49 = bf16[2,64,768]{2,1,0:T(8,128)(2,1)S(1)} custom-call(bf16[2048,1536]{1,0:T(8,128)(2,1)S(1)} %shard_map.47.weights, bf16[64,2176]{1,0:T(8,128)(2,1)S(1)} %shard_map.48.refs_0_), custom_call_target="tpu_custom_call" | custom-call | flops 4026531840 | bytes 6750208 | tf_op jit(solution)/shard_map/pallas_call | solution.py:109
  18.9 0.9 %collective-permute-start.7 = (bf16[2,64,768]{2,1,0:T(8,128)(2,1)S(1)}, bf16[2,64,768]{2,1,0:T(8,128)(2,1)S(1)}, u32[]{:S(2)}, u32[]{:S(2)}) collective-permute-start(bf16[2,64,768]{2,1,0:T(8,128)(2,1)S(1)} %shard_map.49), channel_id=1, source_target_pairs={{0,8},{1,9},{2,10},{3,11},{4,12},{5,13},{6,14},{7,15},{8,0},{9,1},... | collective-permute-start | bytes 589832 | tf_op jit(solution)/shard_map/ppermute | solution.py:23
  19.8 0.0 collective-permute-done.4.rows
  19.8 1.2 %collective-permute-start.8 = (bf16[64,2176]{1,0:T(8,128)(2,1)S(1)}, bf16[64,2176]{1,0:T(8,128)(2,1)S(1)}, u32[]{:S(2)}, u32[]{:S(2)}) collective-permute-start(bf16[64,2176]{1,0:T(8,128)(2,1)S(1)} %shard_map.50.refs_0_), channel_id=1, source_target_pairs={{0,4},{1,5},{2,6},{3,7},{4,0},{5,1},{6,2},{7,3},{8,12},{9,13},{10,... | collective-permute-start | bytes 835592 | tf_op jit(solution)/shard_map/ppermute | solution.py:23
  21.0 1.5 %collective-permute-start.5 = (bf16[64,2176]{1,0:T(8,128)(2,1)S(1)}, bf16[64,2176]{1,0:T(8,128)(2,1)S(1)}, u32[]{:S(2)}, u32[]{:S(2)}) collective-permute-start(bf16[64,2176]{1,0:T(8,128)(2,1)S(1)} %shard_map.50.refs_0_), channel_id=1, source_target_pairs={{0,2},{1,3},{2,0},{3,1},{4,6},{5,7},{6,4},{7,5},{8,10},{9,11},{10,... | collective-permute-start | bytes 835592 | tf_op jit(solution)/shard_map/ppermute | solution.py:23
  22.5 7.4 %collective-permute-done.3.refs_0_ = bf16[64,2176]{1,0:T(8,128)(2,1)S(1)} collective-permute-done((bf16[64,2176]{1,0:T(8,128)(2,1)S(1)}, bf16[64,2176]{1,0:T(8,128)(2,1)S(1)}, u32[]{:S(2)}, u32[]{:S(2)}) %collective-permute-start.3) | collective-permute-done | bytes 278560 | tf_op jit(solution)/shard_map/ppermute | solution.py:23
  30.0 0.0 collective-permute-start.10
  30.0 1.2 %shard_map.51 = bf16[2,64,768]{2,1,0:T(8,128)(2,1)S(1)} custom-call(bf16[2048,1536]{1,0:T(8,128)(2,1)S(1)} %shard_map.47.weights, bf16[64,2176]{1,0:T(8,128)(2,1)S(1)} %collective-permute-done.3.refs_0_), custom_call_target="tpu_custom_call" | custom-call | flops 4026531840 | bytes 6750208 | tf_op jit(solution)/shard_map/pallas_call | solution.py:109
  31.2 0.0 collective-permute-done.7.refs_4_
  31.2 1.3 %collective-permute-start.15 = (bf16[2,64,768]{2,1,0:T(8,128)(2,1)S(1)}, bf16[2,64,768]{2,1,0:T(8,128)(2,1)S(1)}, u32[]{:S(2)}, u32[]{:S(2)}) collective-permute-start(bf16[2,64,768]{2,1,0:T(8,128)(2,1)S(1)} %shard_map.51), channel_id=1, source_target_pairs={{0,12},{1,13},{2,14},{3,15},{4,8},{5,9},{6,10},{7,11},{8,4},{9,5},... | collective-permute-start | bytes 589832 | tf_op jit(solution)/shard_map/ppermute | solution.py:23
  32.5 7.6 %collective-permute-done.8.refs_1_ = bf16[64,2176]{1,0:T(8,128)(2,1)S(1)} collective-permute-done((bf16[64,2176]{1,0:T(8,128)(2,1)S(1)}, bf16[64,2176]{1,0:T(8,128)(2,1)S(1)}, u32[]{:S(2)}, u32[]{:S(2)}) %collective-permute-start.8) | collective-permute-done | bytes 278560 | tf_op jit(solution)/shard_map/ppermute | solution.py:23
  40.1 0.0 collective-permute-done.6.refs_0_
  40.1 0.0 collective-permute-start.9
  40.1 1.2 %shard_map.52 = bf16[2,64,768]{2,1,0:T(8,128)(2,1)S(1)} custom-call(bf16[2048,1536]{1,0:T(8,128)(2,1)S(1)} %shard_map.47.weights, bf16[64,2176]{1,0:T(8,128)(2,1)S(1)} %collective-permute-done.6.refs_0_), custom_call_target="tpu_custom_call" | custom-call | flops 4026531840 | bytes 6750208 | tf_op jit(solution)/shard_map/pallas_call | solution.py:109
  41.3 0.1 collective-permute-start.14
  41.4 0.0 collective-permute-done.10.refs_0_
  41.4 1.2 %shard_map.53 = bf16[2,64,768]{2,1,0:T(8,128)(2,1)S(1)} custom-call(bf16[2048,1536]{1,0:T(8,128)(2,1)S(1)} %shard_map.47.weights, bf16[64,2176]{1,0:T(8,128)(2,1)S(1)} %collective-permute-done.10.refs_0_), custom_call_target="tpu_custom_call" | custom-call | flops 4026531840 | bytes 6750208 | tf_op jit(solution)/shard_map/pallas_call | solution.py:109
  42.6 2.9 %collective-permute-start.16 = (bf16[2,64,768]{2,1,0:T(8,128)(2,1)S(1)}, bf16[2,64,768]{2,1,0:T(8,128)(2,1)S(1)}, u32[]{:S(2)}, u32[]{:S(2)}) collective-permute-start(bf16[2,64,768]{2,1,0:T(8,128)(2,1)S(1)} %shard_map.53), channel_id=1, source_target_pairs={{0,14},{1,15},{2,12},{3,13},{4,10},{5,11},{6,8},{7,9},{8,6},{9,7},... | collective-permute-start | bytes 589832 | tf_op jit(solution)/shard_map/ppermute | solution.py:23
  45.5 0.0 collective-permute-done.5.refs_0_
  45.5 13.4 %collective-permute-done.9.refs_2_ = bf16[64,2176]{1,0:T(8,128)(2,1)S(1)} collective-permute-done((bf16[64,2176]{1,0:T(8,128)(2,1)S(1)}, bf16[64,2176]{1,0:T(8,128)(2,1)S(1)}, u32[]{:S(2)}, u32[]{:S(2)}) %collective-permute-start.9) | collective-permute-done | bytes 278560 | tf_op jit(solution)/shard_map/ppermute | solution.py:23
  58.9 1.4 %shard_map.54 = (bf16[2,64,768]{2,1,0:T(8,128)(2,1)S(1)}, bf16[2,64,768]{2,1,0:T(8,128)(2,1)S(1)}, bf16[2,64,768]{2,1,0:T(8,128)(2,1)S(1)}) custom-call(bf16[2048,1536]{1,0:T(8,128)(2,1)S(1)} %shard_map.47.weights, bf16[64,2176]{1,0:T(8,128)(2,1)S(1)} %collective-permute-done.5.refs_0_, bf16[64,2176]{1,0:T(8,128)(2,1)S(1)} %collective-permute-done.8.refs_1_, ...), custom_call_target="tpu_custom_call" | custom-call | flops 12079595520 | bytes 7667712 | tf_op jit(solution)/shard_map/pallas_call | solution.py:109
  60.3 0.1 collective-permute-start.11
  60.4 0.0 collective-permute-start.13
  60.4 0.0 collective-permute-done.14.refs_5_
  60.4 0.0 copy-start.1
  60.5 3.4 %collective-permute-start.12 = (bf16[2,64,768]{2,1,0:T(8,128)(2,1)S(1)}, bf16[2,64,768]{2,1,0:T(8,128)(2,1)S(1)}, u32[]{:S(2)}, u32[]{:S(2)}) collective-permute-start(bf16[2,64,768]{2,1,0:T(8,128)(2,1)S(1)} %get-tuple-element.37), channel_id=1, source_target_pairs={{0,4},{1,5},{2,6},{3,7},{4,0},{5,1},{6,2},{7,3},{8,12},{9,13},{10,... | collective-permute-start | bytes 589832 | tf_op jit(solution)/shard_map/ppermute | solution.py:23
  63.8 1.2 %shard_map.55.refs_0_ = bf16[2,64,768]{2,1,0:T(8,128)(2,1)S(1)} custom-call(bf16[2048,1536]{1,0:T(8,128)(2,1)S(1)} %shard_map.47.weights, bf16[64,2176]{1,0:T(8,128)(2,1)S(1)} %shard_map.50.refs_0_), custom_call_target="tpu_custom_call" | custom-call | flops 4026531840 | bytes 6750208 | tf_op jit(solution)/shard_map/pallas_call | solution.py:109
  65.0 0.0 collective-permute-done.15.refs_6_
  65.1 3.1 %collective-permute-done.11.refs_1_ = bf16[2,64,768]{2,1,0:T(8,128)(2,1)S(1)} collective-permute-done((bf16[2,64,768]{2,1,0:T(8,128)(2,1)S(1)}, bf16[2,64,768]{2,1,0:T(8,128)(2,1)S(1)}, u32[]{:S(2)}, u32[]{:S(2)}) %collective-permute-start.11) | collective-permute-done | bytes 196640 | tf_op jit(solution)/shard_map/ppermute | solution.py:23
  68.1 1.5 %collective-permute-done.12.refs_2_ = bf16[2,64,768]{2,1,0:T(8,128)(2,1)S(1)} collective-permute-done((bf16[2,64,768]{2,1,0:T(8,128)(2,1)S(1)}, bf16[2,64,768]{2,1,0:T(8,128)(2,1)S(1)}, u32[]{:S(2)}, u32[]{:S(2)}) %collective-permute-start.12) | collective-permute-done | bytes 196640 | tf_op jit(solution)/shard_map/ppermute | solution.py:23
  69.6 0.0 collective-permute-done.13.refs_3_
  69.6 0.0 collective-permute-done.16.refs_7_
  69.6 0.0 copy-done.1
  69.6 1.3 %shard_map.56 = bf16[512,768]{1,0:T(8,128)(2,1)} custom-call(s32[8,64]{1,0:T(8,128)S(1)} %bitcast.10, bf16[2,64,768]{2,1,0:T(8,128)(2,1)S(1)} %shard_map.55.refs_0_, bf16[2,64,768]{2,1,0:T(8,128)(2,1)S(1)} %collective-permute-done.11.refs_1_, bf16[2,64,768]{2,1,0:T(8,128)(2,1)S(1)} %collective-permute-done.12.refs_2_, ...), custom_call_target="tpu_custom_call" | custom-call | tf_op jit(solution)/shard_map/pallas_call | solution.py:144
  (2 shorter events, 0.0 us)
Async XLA Ops:
  0.0 5.9 %collective-permute-start.2 = (bf16[768,2048]{1,0:T(8,128)(2,1)}, bf16[768,2048]{1,0:T(8,128)(2,1)S(1)}, u32[]{:S(2)}, u32[]{:S(2)}) collective-permute-start(bf16[768,2048]{1,0:T(8,128)(2,1)} %bitcast.12), channel_id=1, source_target_pairs={{0,1},{1,0},{2,3},{3,2},{4,5},{5,4},{6,7},{7,6},{8,9},{9,8},{10,11... | collective-permute-start | bytes 9437192 | tf_op jit(solution)/shard_map/ppermute | solution.py:23
  0.0 17.0 %collective-permute-start = (bf16[64,2048]{1,0:T(8,128)(2,1)}, bf16[64,2048]{1,0:T(8,128)(2,1)S(1)}, u32[]{:S(2)}, u32[]{:S(2)}) collective-permute-start(bf16[64,2048]{1,0:T(8,128)(2,1)} %bitcast.14), channel_id=1, source_target_pairs={{0,24},{1,25},{2,26},{3,27},{4,28},{5,29},{6,30},{7,31},{8,16},{9,... | collective-permute-start | bytes 786440 | tf_op jit(solution)/shard_map/ppermute | solution.py:33
  1.3 18.5 %collective-permute-start.4 = (bf16[64,2048]{1,0:T(8,128)(2,1)}, bf16[64,2048]{1,0:T(8,128)(2,1)S(1)}, u32[]{:S(2)}, u32[]{:S(2)}) collective-permute-start(bf16[64,2048]{1,0:T(8,128)(2,1)} %bitcast.15), channel_id=1, source_target_pairs={{0,16},{1,17},{2,18},{3,19},{4,20},{5,21},{6,22},{7,23},{8,24},{9,... | collective-permute-start | bytes 786440 | tf_op jit(solution)/shard_map/ppermute | solution.py:33
  1.8 0.7 copy-start
  2.5 0.7 copy-start.2
  3.3 13.7 %collective-permute-start.1 = (bf16[64,128]{1,0:T(8,128)(2,1)S(1)}, bf16[64,128]{1,0:T(8,128)(2,1)S(1)}, u32[]{:S(2)}, u32[]{:S(2)}) collective-permute-start(bf16[64,128]{1,0:T(8,128)(2,1)S(1)} %shard_map.46.columns), channel_id=1, source_target_pairs={{0,8},{1,9},{2,10},{3,11},{4,12},{5,13},{6,14},{7,15},{8,0},{9,1},... | collective-permute-start | bytes 49160 | tf_op jit(solution)/shard_map/ppermute | solution.py:23
  5.9 1.9 %copy-start.3 = (bf16[1,1,768,2048]{3,2,1,0:T(8,128)(2,1)S(1)}, bf16[1,1,768,2048]{3,2,1,0:T(8,128)(2,1)}, u32[]{:S(2)}) copy-start(bf16[1,1,768,2048]{3,2,1,0:T(8,128)(2,1)} %param.7) | copy-start | bytes 9437188
  17.0 13.0 %collective-permute-start.3 = (bf16[64,2176]{1,0:T(8,128)(2,1)S(1)}, bf16[64,2176]{1,0:T(8,128)(2,1)S(1)}, u32[]{:S(2)}, u32[]{:S(2)}) collective-permute-start(bf16[64,2176]{1,0:T(8,128)(2,1)S(1)} %shard_map.48.refs_0_), channel_id=1, source_target_pairs={{0,4},{1,5},{2,6},{3,7},{4,0},{5,1},{6,2},{7,3},{8,12},{9,13},{10,... | collective-permute-start | bytes 835592 | tf_op jit(solution)/shard_map/ppermute | solution.py:23
  17.1 23.0 %collective-permute-start.6 = (bf16[64,2176]{1,0:T(8,128)(2,1)S(1)}, bf16[64,2176]{1,0:T(8,128)(2,1)S(1)}, u32[]{:S(2)}, u32[]{:S(2)}) collective-permute-start(bf16[64,2176]{1,0:T(8,128)(2,1)S(1)} %shard_map.48.refs_0_), channel_id=1, source_target_pairs={{0,2},{1,3},{2,0},{3,1},{4,6},{5,7},{6,4},{7,5},{8,10},{9,11},{10,... | collective-permute-start | bytes 835592 | tf_op jit(solution)/shard_map/ppermute | solution.py:23
  18.9 12.3 %collective-permute-start.7 = (bf16[2,64,768]{2,1,0:T(8,128)(2,1)S(1)}, bf16[2,64,768]{2,1,0:T(8,128)(2,1)S(1)}, u32[]{:S(2)}, u32[]{:S(2)}) collective-permute-start(bf16[2,64,768]{2,1,0:T(8,128)(2,1)S(1)} %shard_map.49), channel_id=1, source_target_pairs={{0,8},{1,9},{2,10},{3,11},{4,12},{5,13},{6,14},{7,15},{8,0},{9,1},... | collective-permute-start | bytes 589832 | tf_op jit(solution)/shard_map/ppermute | solution.py:23
  19.8 20.3 %collective-permute-start.8 = (bf16[64,2176]{1,0:T(8,128)(2,1)S(1)}, bf16[64,2176]{1,0:T(8,128)(2,1)S(1)}, u32[]{:S(2)}, u32[]{:S(2)}) collective-permute-start(bf16[64,2176]{1,0:T(8,128)(2,1)S(1)} %shard_map.50.refs_0_), channel_id=1, source_target_pairs={{0,4},{1,5},{2,6},{3,7},{4,0},{5,1},{6,2},{7,3},{8,12},{9,13},{10,... | collective-permute-start | bytes 835592 | tf_op jit(solution)/shard_map/ppermute | solution.py:23
  21.0 24.4 %collective-permute-start.5 = (bf16[64,2176]{1,0:T(8,128)(2,1)S(1)}, bf16[64,2176]{1,0:T(8,128)(2,1)S(1)}, u32[]{:S(2)}, u32[]{:S(2)}) collective-permute-start(bf16[64,2176]{1,0:T(8,128)(2,1)S(1)} %shard_map.50.refs_0_), channel_id=1, source_target_pairs={{0,2},{1,3},{2,0},{3,1},{4,6},{5,7},{6,4},{7,5},{8,10},{9,11},{10,... | collective-permute-start | bytes 835592 | tf_op jit(solution)/shard_map/ppermute | solution.py:23
  30.0 11.4 %collective-permute-start.10 = (bf16[64,2176]{1,0:T(8,128)(2,1)S(1)}, bf16[64,2176]{1,0:T(8,128)(2,1)S(1)}, u32[]{:S(2)}, u32[]{:S(2)}) collective-permute-start(bf16[64,2176]{1,0:T(8,128)(2,1)S(1)} %collective-permute-done.3.refs_0_), channel_id=1, source_target_pairs={{0,2},{1,3},{2,0},{3,1},{4,6},{5,7},{6,4},{7,5},{8,10},{9,11},{10,... | collective-permute-start | bytes 835592 | tf_op jit(solution)/shard_map/ppermute | solution.py:23
  31.2 33.9 %collective-permute-start.15 = (bf16[2,64,768]{2,1,0:T(8,128)(2,1)S(1)}, bf16[2,64,768]{2,1,0:T(8,128)(2,1)S(1)}, u32[]{:S(2)}, u32[]{:S(2)}) collective-permute-start(bf16[2,64,768]{2,1,0:T(8,128)(2,1)S(1)} %shard_map.51), channel_id=1, source_target_pairs={{0,12},{1,13},{2,14},{3,15},{4,8},{5,9},{6,10},{7,11},{8,4},{9,5},... | collective-permute-start | bytes 589832 | tf_op jit(solution)/shard_map/ppermute | solution.py:23
  40.1 18.8 %collective-permute-start.9 = (bf16[64,2176]{1,0:T(8,128)(2,1)S(1)}, bf16[64,2176]{1,0:T(8,128)(2,1)S(1)}, u32[]{:S(2)}, u32[]{:S(2)}) collective-permute-start(bf16[64,2176]{1,0:T(8,128)(2,1)S(1)} %collective-permute-done.8.refs_1_), channel_id=1, source_target_pairs={{0,2},{1,3},{2,0},{3,1},{4,6},{5,7},{6,4},{7,5},{8,10},{9,11},{10,... | collective-permute-start | bytes 835592 | tf_op jit(solution)/shard_map/ppermute | solution.py:23
  41.3 19.1 %collective-permute-start.14 = (bf16[2,64,768]{2,1,0:T(8,128)(2,1)S(1)}, bf16[2,64,768]{2,1,0:T(8,128)(2,1)S(1)}, u32[]{:S(2)}, u32[]{:S(2)}) collective-permute-start(bf16[2,64,768]{2,1,0:T(8,128)(2,1)S(1)} %shard_map.52), channel_id=1, source_target_pairs={{0,10},{1,11},{2,8},{3,9},{4,14},{5,15},{6,12},{7,13},{8,2},{9,3},... | collective-permute-start | bytes 589832 | tf_op jit(solution)/shard_map/ppermute | solution.py:23
  42.6 27.0 %collective-permute-start.16 = (bf16[2,64,768]{2,1,0:T(8,128)(2,1)S(1)}, bf16[2,64,768]{2,1,0:T(8,128)(2,1)S(1)}, u32[]{:S(2)}, u32[]{:S(2)}) collective-permute-start(bf16[2,64,768]{2,1,0:T(8,128)(2,1)S(1)} %shard_map.53), channel_id=1, source_target_pairs={{0,14},{1,15},{2,12},{3,13},{4,10},{5,11},{6,8},{7,9},{8,6},{9,7},... | collective-permute-start | bytes 589832 | tf_op jit(solution)/shard_map/ppermute | solution.py:23
  60.3 7.8 %collective-permute-start.11 = (bf16[2,64,768]{2,1,0:T(8,128)(2,1)S(1)}, bf16[2,64,768]{2,1,0:T(8,128)(2,1)S(1)}, u32[]{:S(2)}, u32[]{:S(2)}) collective-permute-start(bf16[2,64,768]{2,1,0:T(8,128)(2,1)S(1)} %get-tuple-element.36), channel_id=1, source_target_pairs={{0,2},{1,3},{2,0},{3,1},{4,6},{5,7},{6,4},{7,5},{8,10},{9,11},{10,... | collective-permute-start | bytes 589832 | tf_op jit(solution)/shard_map/ppermute | solution.py:23
  60.4 9.2 %collective-permute-start.13 = (bf16[2,64,768]{2,1,0:T(8,128)(2,1)S(1)}, bf16[2,64,768]{2,1,0:T(8,128)(2,1)S(1)}, u32[]{:S(2)}, u32[]{:S(2)}) collective-permute-start(bf16[2,64,768]{2,1,0:T(8,128)(2,1)S(1)} %get-tuple-element.34), channel_id=1, source_target_pairs={{0,6},{1,7},{2,4},{3,5},{4,2},{5,3},{6,0},{7,1},{8,14},{9,15},{10,... | collective-permute-start | bytes 589832 | tf_op jit(solution)/shard_map/ppermute | solution.py:23
  60.4 9.1 %copy-start.1 = (s32[1,64,8]{1,2,0:T(8,128)S(1)}, s32[1,64,8]{1,2,0:T(8,128)}, u32[]{:S(2)}) copy-start(s32[1,64,8]{1,2,0:T(8,128)} %param.5) | copy-start | bytes 6148
  60.5 9.1 %collective-permute-start.12 = (bf16[2,64,768]{2,1,0:T(8,128)(2,1)S(1)}, bf16[2,64,768]{2,1,0:T(8,128)(2,1)S(1)}, u32[]{:S(2)}, u32[]{:S(2)}) collective-permute-start(bf16[2,64,768]{2,1,0:T(8,128)(2,1)S(1)} %get-tuple-element.37), channel_id=1, source_target_pairs={{0,4},{1,5},{2,6},{3,7},{4,0},{5,1},{6,2},{7,3},{8,12},{9,13},{10,... | collective-permute-start | bytes 589832 | tf_op jit(solution)/shard_map/ppermute | solution.py:23

commit v18 on v17

--- a/solution.py
+++ b/solution.py
@@ -162,28 +162,30 @@
     columns = gate_columns(route_ids.T, route_gates.T)
     far_columns = send(columns, owners, Z_FAR)
     weights = turned(weight_mat, other_mat)
-    far, far_columns, weights = tie((far, far_columns, weights))
+    rows, columns, weights = tie((rows, columns, weights))
+    rows = widened(rows, columns)
+    side = send(rows, owners, X)
+    near = send(rows, owners, Z_NEAR)
+    far, far_columns, rows = tie((far, far_columns, rows))
     far = widened(far, far_columns)
     cross = send(far, owners, Z_NEAR)
     far_side = send(far, owners, X)
     (out_far,) = work(far)
     back_far = send(out_far, owners, Z_FAR)
-    rows, columns, _ = tie((rows, columns, out_far))
-    rows = widened(rows, columns)
-    near = send(rows, owners, Z_NEAR)
-    side = send(rows, owners, X)
-    cross, rows = tie((cross, rows))
+    side, _ = tie((side, out_far))
+    near, side = tie((near, side))
+    near_side = send(near, owners, X)
+    cross, _ = tie((cross, near))
     cross_side = send(cross, owners, X)
     (out_cross,) = work(cross)
     back_cross = send(out_cross, owners, Z_NEAR ^ Z_FAR)
-    far_side, back_far, near, _ = tie((far_side, back_far, near, out_cross))
-    near_side = send(near, owners, X)
+    far_side, back_far, _ = tie((far_side, back_far, out_cross))
     (out_far_side,) = work(far_side)
     back_far_side = send(out_far_side, owners, X ^ Z_FAR)
     cross_side, _ = tie((cross_side, out_far_side))
     (out_cross_side,) = work(cross_side)
     back_cross_side = send(out_cross_side, owners, X ^ Z_NEAR ^ Z_FAR)
-    side, near_side, _ = tie((side, near_side, out_cross_side))
+    near_side, _ = tie((near_side, out_cross_side))
     out_side, out_near, out_near_side = work(side, near, near_side)
     back_near_side = send(out_near_side, owners, X ^ Z_NEAR)
     back_side = send(out_side, owners, X)

time: 71.1 us -> 69.2 us (0.973)
  the two profiles are of different devices: /device:TPU:26 before, /device:TPU:0 now
where the time goes in v18:
time: 69.2 us; the launch traced here: 69 us
  starting transfers between devices  29.5 us (43%)
  waiting for transfers between devices  25.7 us (37%)
  Pallas kernels  10.5 us (15%)
  local copies, waits for them, and re-layouts  3.26 us (5%)
    ppermute x15, waiting for transfers between devices, send(): return lax.ppermute(block, 'expert', route)  24.6 us
    ppermute x15, starting transfers between devices, send(): return lax.ppermute(block, 'expert', route)  24.5 us
    pallas_call x6, Pallas kernels, products(): pl.pallas_call(functools.partial(products_kernel, len(pieces)), out_shape...  7.34 us
    ppermute x2, starting transfers between devices, send_across(): return lax.ppermute(block, ('pipe', 'expert'), route)  5.05 us
    unnamed x8, local copies, waits for them, and re-layouts  3.26 us
    pallas_call x1, Pallas kernels, turned(): pl.pallas_call(turn_kernel, out_shape=jax.ShapeDtypeStruct((depth, CORES...  1.67 us
  transfers between devices with their start and end apart: 17, of which 8 were waited for; matrix products, arithmetic and copies ran while one was open for 0% of the time, Pallas kernels for 13%

profile of v18, /device:TPU:0, one launch (start us, length us, event | category | flops | bytes accessed | tf_op | source)
XLA Modules:
  0.0 69.0 jit_solution(8932128885541620111)
XLA Ops:
  0.0 0.5 collective-permute-start.1
  0.5 2.5 %collective-permute-start = (bf16[64,2048]{1,0:T(8,128)(2,1)}, bf16[64,2048]{1,0:T(8,128)(2,1)S(1)}, u32[]{:S(2)}, u32[]{:S(2)}) collective-permute-start(bf16[64,2048]{1,0:T(8,128)(2,1)} %bitcast.14), channel_id=1, source_target_pairs={{0,16},{1,17},{2,18},{3,19},{4,20},{5,21},{6,22},{7,23},{8,24},{9,... | collective-permute-start | bytes 786440 | tf_op jit(solution)/shard_map/ppermute | solution.py:33
  3.0 2.5 %collective-permute-start.2 = (bf16[64,2048]{1,0:T(8,128)(2,1)}, bf16[64,2048]{1,0:T(8,128)(2,1)S(1)}, u32[]{:S(2)}, u32[]{:S(2)}) collective-permute-start(bf16[64,2048]{1,0:T(8,128)(2,1)} %bitcast.15), channel_id=1, source_target_pairs={{0,24},{1,25},{2,26},{3,27},{4,28},{5,29},{6,30},{7,31},{8,16},{9,... | collective-permute-start | bytes 786440 | tf_op jit(solution)/shard_map/ppermute | solution.py:33
  5.5 0.0 copy-start
  5.5 0.7 copy-done
  6.2 0.0 copy-start.2
  6.2 0.7 copy-done.2
  6.9 0.1 shard_map.46.columns
  7.0 0.1 collective-permute-start.3
  7.1 0.0 collective-permute-done.1.other
  7.1 0.0 copy-start.3
  7.1 1.9 %copy-done.3 = bf16[1,1,768,2048]{3,2,1,0:T(8,128)(2,1)S(1)} copy-done((bf16[1,1,768,2048]{3,2,1,0:T(8,128)(2,1)S(1)}, bf16[1,1,768,2048]{3,2,1,0:T(8,128)(2,1)}, u32[]{:S(2)}) %copy-start.3) | copy-done | bytes 3145752
  9.0 1.7 %shard_map.47.weights = bf16[2048,1536]{1,0:T(8,128)(2,1)S(1)} custom-call(bf16[768,2048]{1,0:T(8,128)(2,1)S(1)} %bitcast.13, bf16[768,2048]{1,0:T(8,128)(2,1)S(1)} %collective-permute-done.1.other), custom_call_target="tpu_custom_call" | custom-call | flops 12884901888 | tf_op jit(solution)/shard_map/pallas_call | solution.py:77
  10.7 0.6 collective-permute-done.rows
  11.3 1.8 %collective-permute-start.5 = (bf16[64,2176]{1,0:T(8,128)(2,1)S(1)}, bf16[64,2176]{1,0:T(8,128)(2,1)S(1)}, u32[]{:S(2)}, u32[]{:S(2)}) collective-permute-start(bf16[64,2176]{1,0:T(8,128)(2,1)S(1)} %shard_map.48.refs_0_), channel_id=1, source_target_pairs={{0,2},{1,3},{2,0},{3,1},{4,6},{5,7},{6,4},{7,5},{8,10},{9,11},{10,... | collective-permute-start | bytes 835592 | tf_op jit(solution)/shard_map/ppermute | solution.py:23
  13.1 6.1 %collective-permute-start.4 = (bf16[64,2176]{1,0:T(8,128)(2,1)S(1)}, bf16[64,2176]{1,0:T(8,128)(2,1)S(1)}, u32[]{:S(2)}, u32[]{:S(2)}) collective-permute-start(bf16[64,2176]{1,0:T(8,128)(2,1)S(1)} %shard_map.48.refs_0_), channel_id=1, source_target_pairs={{0,4},{1,5},{2,6},{3,7},{4,0},{5,1},{6,2},{7,3},{8,12},{9,13},{10,... | collective-permute-start | bytes 835592 | tf_op jit(solution)/shard_map/ppermute | solution.py:23
  19.2 0.0 collective-permute-done.3.columns
  19.2 0.4 collective-permute-done.2.rows
  19.6 0.1 collective-permute-start.7
  19.7 1.6 %collective-permute-start.9 = (bf16[64,2176]{1,0:T(8,128)(2,1)S(1)}, bf16[64,2176]{1,0:T(8,128)(2,1)S(1)}, u32[]{:S(2)}, u32[]{:S(2)}) collective-permute-start(bf16[64,2176]{1,0:T(8,128)(2,1)S(1)} %shard_map.49.refs_0_), channel_id=1, source_target_pairs={{0,2},{1,3},{2,0},{3,1},{4,6},{5,7},{6,4},{7,5},{8,10},{9,11},{10,... | collective-permute-start | bytes 835592 | tf_op jit(solution)/shard_map/ppermute | solution.py:23
  21.2 1.2 %shard_map.50 = bf16[2,64,768]{2,1,0:T(8,128)(2,1)S(1)} custom-call(bf16[2048,1536]{1,0:T(8,128)(2,1)S(1)} %shard_map.47.weights, bf16[64,2176]{1,0:T(8,128)(2,1)S(1)} %shard_map.49.refs_0_), custom_call_target="tpu_custom_call" | custom-call | flops 4026531840 | bytes 6750208 | tf_op jit(solution)/shard_map/pallas_call | solution.py:109
  22.4 4.0 %collective-permute-start.10 = (bf16[2,64,768]{2,1,0:T(8,128)(2,1)S(1)}, bf16[2,64,768]{2,1,0:T(8,128)(2,1)S(1)}, u32[]{:S(2)}, u32[]{:S(2)}) collective-permute-start(bf16[2,64,768]{2,1,0:T(8,128)(2,1)S(1)} %shard_map.50), channel_id=1, source_target_pairs={{0,8},{1,9},{2,10},{3,11},{4,12},{5,13},{6,14},{7,15},{8,0},{9,1},... | collective-permute-start | bytes 589832 | tf_op jit(solution)/shard_map/ppermute | solution.py:23
  26.4 0.0 collective-permute-done.5.refs_0_
  26.5 0.3 collective-permute-done.4.refs_1_
  26.7 0.5 collective-permute-start.6
  27.2 8.4 %collective-permute-done.7.refs_0_ = bf16[64,2176]{1,0:T(8,128)(2,1)S(1)} collective-permute-done((bf16[64,2176]{1,0:T(8,128)(2,1)S(1)}, bf16[64,2176]{1,0:T(8,128)(2,1)S(1)}, u32[]{:S(2)}, u32[]{:S(2)}) %collective-permute-start.7) | collective-permute-done | bytes 278560 | tf_op jit(solution)/shard_map/ppermute | solution.py:23
  35.6 0.9 %collective-permute-start.8 = (bf16[64,2176]{1,0:T(8,128)(2,1)S(1)}, bf16[64,2176]{1,0:T(8,128)(2,1)S(1)}, u32[]{:S(2)}, u32[]{:S(2)}) collective-permute-start(bf16[64,2176]{1,0:T(8,128)(2,1)S(1)} %collective-permute-done.7.refs_0_), channel_id=1, source_target_pairs={{0,2},{1,3},{2,0},{3,1},{4,6},{5,7},{6,4},{7,5},{8,10},{9,11},{10,... | collective-permute-start | bytes 835592 | tf_op jit(solution)/shard_map/ppermute | solution.py:23
  36.5 1.2 %shard_map.51 = bf16[2,64,768]{2,1,0:T(8,128)(2,1)S(1)} custom-call(bf16[2048,1536]{1,0:T(8,128)(2,1)S(1)} %shard_map.47.weights, bf16[64,2176]{1,0:T(8,128)(2,1)S(1)} %collective-permute-done.7.refs_0_), custom_call_target="tpu_custom_call" | custom-call | flops 4026531840 | bytes 6750208 | tf_op jit(solution)/shard_map/pallas_call | solution.py:109
  37.7 3.5 %collective-permute-start.15 = (bf16[2,64,768]{2,1,0:T(8,128)(2,1)S(1)}, bf16[2,64,768]{2,1,0:T(8,128)(2,1)S(1)}, u32[]{:S(2)}, u32[]{:S(2)}) collective-permute-start(bf16[2,64,768]{2,1,0:T(8,128)(2,1)S(1)} %shard_map.51), channel_id=1, source_target_pairs={{0,12},{1,13},{2,14},{3,15},{4,8},{5,9},{6,10},{7,11},{8,4},{9,5},... | collective-permute-start | bytes 589832 | tf_op jit(solution)/shard_map/ppermute | solution.py:23
  41.2 0.0 collective-permute-done.10.refs_4_
  41.2 0.0 collective-permute-done.9.refs_0_
  41.2 1.2 %shard_map.52 = bf16[2,64,768]{2,1,0:T(8,128)(2,1)S(1)} custom-call(bf16[2048,1536]{1,0:T(8,128)(2,1)S(1)} %shard_map.47.weights, bf16[64,2176]{1,0:T(8,128)(2,1)S(1)} %collective-permute-done.9.refs_0_), custom_call_target="tpu_custom_call" | custom-call | flops 4026531840 | bytes 6750208 | tf_op jit(solution)/shard_map/pallas_call | solution.py:109
  42.4 0.1 collective-permute-start.14
  42.5 0.5 collective-permute-done.8.refs_0_
  43.0 1.2 %shard_map.53 = bf16[2,64,768]{2,1,0:T(8,128)(2,1)S(1)} custom-call(bf16[2048,1536]{1,0:T(8,128)(2,1)S(1)} %shard_map.47.weights, bf16[64,2176]{1,0:T(8,128)(2,1)S(1)} %collective-permute-done.8.refs_0_), custom_call_target="tpu_custom_call" | custom-call | flops 4026531840 | bytes 6750208 | tf_op jit(solution)/shard_map/pallas_call | solution.py:109
  44.2 5.0 %collective-permute-start.16 = (bf16[2,64,768]{2,1,0:T(8,128)(2,1)S(1)}, bf16[2,64,768]{2,1,0:T(8,128)(2,1)S(1)}, u32[]{:S(2)}, u32[]{:S(2)}) collective-permute-start(bf16[2,64,768]{2,1,0:T(8,128)(2,1)S(1)} %shard_map.53), channel_id=1, source_target_pairs={{0,14},{1,15},{2,12},{3,13},{4,10},{5,11},{6,8},{7,9},{8,6},{9,7},... | collective-permute-start | bytes 589832 | tf_op jit(solution)/shard_map/ppermute | solution.py:23
  49.2 0.0 collective-permute-done.6.refs_2_
  49.2 1.4 %shard_map.54 = (bf16[2,64,768]{2,1,0:T(8,128)(2,1)S(1)}, bf16[2,64,768]{2,1,0:T(8,128)(2,1)S(1)}, bf16[2,64,768]{2,1,0:T(8,128)(2,1)S(1)}) custom-call(bf16[2048,1536]{1,0:T(8,128)(2,1)S(1)} %shard_map.47.weights, bf16[64,2176]{1,0:T(8,128)(2,1)S(1)} %collective-permute-done.5.refs_0_, bf16[64,2176]{1,0:T(8,128)(2,1)S(1)} %collective-permute-done.4.refs_1_, ...), custom_call_target="tpu_custom_call" | custom-call | flops 12079595520 | bytes 7667712 | tf_op jit(solution)/shard_map/pallas_call | solution.py:109
  50.6 0.4 collective-permute-start.11
  50.9 0.1 collective-permute-start.13
  51.0 11.0 %collective-permute-done.14.refs_5_ = bf16[2,64,768]{2,1,0:T(8,128)(2,1)S(1)} collective-permute-done((bf16[2,64,768]{2,1,0:T(8,128)(2,1)S(1)}, bf16[2,64,768]{2,1,0:T(8,128)(2,1)S(1)}, u32[]{:S(2)}, u32[]{:S(2)}) %collective-permute-start.14) | collective-permute-done | bytes 196640 | tf_op jit(solution)/shard_map/ppermute | solution.py:23
  62.0 0.0 copy-start.1
  62.0 0.0 collective-permute-start.12
  62.0 1.2 %shard_map.55.refs_0_ = bf16[2,64,768]{2,1,0:T(8,128)(2,1)S(1)} custom-call(bf16[2048,1536]{1,0:T(8,128)(2,1)S(1)} %shard_map.47.weights, bf16[64,2176]{1,0:T(8,128)(2,1)S(1)} %shard_map.48.refs_0_), custom_call_target="tpu_custom_call" | custom-call | flops 4026531840 | bytes 6750208 | tf_op jit(solution)/shard_map/pallas_call | solution.py:109
  63.2 0.0 collective-permute-done.15.refs_6_
  63.3 3.7 %collective-permute-done.11.refs_1_ = bf16[2,64,768]{2,1,0:T(8,128)(2,1)S(1)} collective-permute-done((bf16[2,64,768]{2,1,0:T(8,128)(2,1)S(1)}, bf16[2,64,768]{2,1,0:T(8,128)(2,1)S(1)}, u32[]{:S(2)}, u32[]{:S(2)}) %collective-permute-start.11) | collective-permute-done | bytes 196640 | tf_op jit(solution)/shard_map/ppermute | solution.py:23
  66.9 0.8 %collective-permute-done.12.refs_2_ = bf16[2,64,768]{2,1,0:T(8,128)(2,1)S(1)} collective-permute-done((bf16[2,64,768]{2,1,0:T(8,128)(2,1)S(1)}, bf16[2,64,768]{2,1,0:T(8,128)(2,1)S(1)}, u32[]{:S(2)}, u32[]{:S(2)}) %collective-permute-start.12) | collective-permute-done | bytes 196640 | tf_op jit(solution)/shard_map/ppermute | solution.py:23
  67.7 0.0 collective-permute-done.13.refs_3_
  67.7 0.0 collective-permute-done.16.refs_7_
  67.7 0.0 copy-done.1
  67.7 1.3 %shard_map.56 = bf16[512,768]{1,0:T(8,128)(2,1)} custom-call(s32[8,64]{1,0:T(8,128)S(1)} %bitcast.10, bf16[2,64,768]{2,1,0:T(8,128)(2,1)S(1)} %shard_map.55.refs_0_, bf16[2,64,768]{2,1,0:T(8,128)(2,1)S(1)} %collective-permute-done.11.refs_1_, bf16[2,64,768]{2,1,0:T(8,128)(2,1)S(1)} %collective-permute-done.12.refs_2_, ...), custom_call_target="tpu_custom_call" | custom-call | tf_op jit(solution)/shard_map/pallas_call | solution.py:144
  (2 shorter events, 0.0 us)
Async XLA Ops:
  0.0 7.1 %collective-permute-start.1 = (bf16[768,2048]{1,0:T(8,128)(2,1)}, bf16[768,2048]{1,0:T(8,128)(2,1)S(1)}, u32[]{:S(2)}, u32[]{:S(2)}) collective-permute-start(bf16[768,2048]{1,0:T(8,128)(2,1)} %bitcast.12), channel_id=1, source_target_pairs={{0,1},{1,0},{2,3},{3,2},{4,5},{5,4},{6,7},{7,6},{8,9},{9,8},{10,11... | collective-permute-start | bytes 9437192 | tf_op jit(solution)/shard_map/ppermute | solution.py:23
  0.5 10.8 %collective-permute-start = (bf16[64,2048]{1,0:T(8,128)(2,1)}, bf16[64,2048]{1,0:T(8,128)(2,1)S(1)}, u32[]{:S(2)}, u32[]{:S(2)}) collective-permute-start(bf16[64,2048]{1,0:T(8,128)(2,1)} %bitcast.14), channel_id=1, source_target_pairs={{0,16},{1,17},{2,18},{3,19},{4,20},{5,21},{6,22},{7,23},{8,24},{9,... | collective-permute-start | bytes 786440 | tf_op jit(solution)/shard_map/ppermute | solution.py:33
  3.0 16.6 %collective-permute-start.2 = (bf16[64,2048]{1,0:T(8,128)(2,1)}, bf16[64,2048]{1,0:T(8,128)(2,1)S(1)}, u32[]{:S(2)}, u32[]{:S(2)}) collective-permute-start(bf16[64,2048]{1,0:T(8,128)(2,1)} %bitcast.15), channel_id=1, source_target_pairs={{0,24},{1,25},{2,26},{3,27},{4,28},{5,29},{6,30},{7,31},{8,16},{9,... | collective-permute-start | bytes 786440 | tf_op jit(solution)/shard_map/ppermute | solution.py:33
  5.5 0.7 copy-start
  6.2 0.7 copy-start.2
  7.0 12.2 %collective-permute-start.3 = (bf16[64,128]{1,0:T(8,128)(2,1)S(1)}, bf16[64,128]{1,0:T(8,128)(2,1)S(1)}, u32[]{:S(2)}, u32[]{:S(2)}) collective-permute-start(bf16[64,128]{1,0:T(8,128)(2,1)S(1)} %shard_map.46.columns), channel_id=1, source_target_pairs={{0,8},{1,9},{2,10},{3,11},{4,12},{5,13},{6,14},{7,15},{8,0},{9,1},... | collective-permute-start | bytes 49160 | tf_op jit(solution)/shard_map/ppermute | solution.py:23
  7.1 1.9 %copy-start.3 = (bf16[1,1,768,2048]{3,2,1,0:T(8,128)(2,1)S(1)}, bf16[1,1,768,2048]{3,2,1,0:T(8,128)(2,1)}, u32[]{:S(2)}) copy-start(bf16[1,1,768,2048]{3,2,1,0:T(8,128)(2,1)} %param.7) | copy-start | bytes 9437188
  11.3 15.2 %collective-permute-start.5 = (bf16[64,2176]{1,0:T(8,128)(2,1)S(1)}, bf16[64,2176]{1,0:T(8,128)(2,1)S(1)}, u32[]{:S(2)}, u32[]{:S(2)}) collective-permute-start(bf16[64,2176]{1,0:T(8,128)(2,1)S(1)} %shard_map.48.refs_0_), channel_id=1, source_target_pairs={{0,2},{1,3},{2,0},{3,1},{4,6},{5,7},{6,4},{7,5},{8,10},{9,11},{10,... | collective-permute-start | bytes 835592 | tf_op jit(solution)/shard_map/ppermute | solution.py:23
  13.1 13.6 %collective-permute-start.4 = (bf16[64,2176]{1,0:T(8,128)(2,1)S(1)}, bf16[64,2176]{1,0:T(8,128)(2,1)S(1)}, u32[]{:S(2)}, u32[]{:S(2)}) collective-permute-start(bf16[64,2176]{1,0:T(8,128)(2,1)S(1)} %shard_map.48.refs_0_), channel_id=1, source_target_pairs={{0,4},{1,5},{2,6},{3,7},{4,0},{5,1},{6,2},{7,3},{8,12},{9,13},{10,... | collective-permute-start | bytes 835592 | tf_op jit(solution)/shard_map/ppermute | solution.py:23
  19.6 16.0 %collective-permute-start.7 = (bf16[64,2176]{1,0:T(8,128)(2,1)S(1)}, bf16[64,2176]{1,0:T(8,128)(2,1)S(1)}, u32[]{:S(2)}, u32[]{:S(2)}) collective-permute-start(bf16[64,2176]{1,0:T(8,128)(2,1)S(1)} %shard_map.49.refs_0_), channel_id=1, source_target_pairs={{0,4},{1,5},{2,6},{3,7},{4,0},{5,1},{6,2},{7,3},{8,12},{9,13},{10,... | collective-permute-start | bytes 835592 | tf_op jit(solution)/shard_map/ppermute | solution.py:23
  19.7 21.5 %collective-permute-start.9 = (bf16[64,2176]{1,0:T(8,128)(2,1)S(1)}, bf16[64,2176]{1,0:T(8,128)(2,1)S(1)}, u32[]{:S(2)}, u32[]{:S(2)}) collective-permute-start(bf16[64,2176]{1,0:T(8,128)(2,1)S(1)} %shard_map.49.refs_0_), channel_id=1, source_target_pairs={{0,2},{1,3},{2,0},{3,1},{4,6},{5,7},{6,4},{7,5},{8,10},{9,11},{10,... | collective-permute-start | bytes 835592 | tf_op jit(solution)/shard_map/ppermute | solution.py:23
  22.4 18.7 %collective-permute-start.10 = (bf16[2,64,768]{2,1,0:T(8,128)(2,1)S(1)}, bf16[2,64,768]{2,1,0:T(8,128)(2,1)S(1)}, u32[]{:S(2)}, u32[]{:S(2)}) collective-permute-start(bf16[2,64,768]{2,1,0:T(8,128)(2,1)S(1)} %shard_map.50), channel_id=1, source_target_pairs={{0,8},{1,9},{2,10},{3,11},{4,12},{5,13},{6,14},{7,15},{8,0},{9,1},... | collective-permute-start | bytes 589832 | tf_op jit(solution)/shard_map/ppermute | solution.py:23
  26.7 22.5 %collective-permute-start.6 = (bf16[64,2176]{1,0:T(8,128)(2,1)S(1)}, bf16[64,2176]{1,0:T(8,128)(2,1)S(1)}, u32[]{:S(2)}, u32[]{:S(2)}) collective-permute-start(bf16[64,2176]{1,0:T(8,128)(2,1)S(1)} %collective-permute-done.4.refs_1_), channel_id=1, source_target_pairs={{0,2},{1,3},{2,0},{3,1},{4,6},{5,7},{6,4},{7,5},{8,10},{9,11},{10,... | collective-permute-start | bytes 835592 | tf_op jit(solution)/shard_map/ppermute | solution.py:23
  35.6 7.4 %collective-permute-start.8 = (bf16[64,2176]{1,0:T(8,128)(2,1)S(1)}, bf16[64,2176]{1,0:T(8,128)(2,1)S(1)}, u32[]{:S(2)}, u32[]{:S(2)}) collective-permute-start(bf16[64,2176]{1,0:T(8,128)(2,1)S(1)} %collective-permute-done.7.refs_0_), channel_id=1, source_target_pairs={{0,2},{1,3},{2,0},{3,1},{4,6},{5,7},{6,4},{7,5},{8,10},{9,11},{10,... | collective-permute-start | bytes 835592 | tf_op jit(solution)/shard_map/ppermute | solution.py:23
  37.7 25.6 %collective-permute-start.15 = (bf16[2,64,768]{2,1,0:T(8,128)(2,1)S(1)}, bf16[2,64,768]{2,1,0:T(8,128)(2,1)S(1)}, u32[]{:S(2)}, u32[]{:S(2)}) collective-permute-start(bf16[2,64,768]{2,1,0:T(8,128)(2,1)S(1)} %shard_map.51), channel_id=1, source_target_pairs={{0,12},{1,13},{2,14},{3,15},{4,8},{5,9},{6,10},{7,11},{8,4},{9,5},... | collective-permute-start | bytes 589832 | tf_op jit(solution)/shard_map/ppermute | solution.py:23
  42.4 19.7 %collective-permute-start.14 = (bf16[2,64,768]{2,1,0:T(8,128)(2,1)S(1)}, bf16[2,64,768]{2,1,0:T(8,128)(2,1)S(1)}, u32[]{:S(2)}, u32[]{:S(2)}) collective-permute-start(bf16[2,64,768]{2,1,0:T(8,128)(2,1)S(1)} %shard_map.52), channel_id=1, source_target_pairs={{0,10},{1,11},{2,8},{3,9},{4,14},{5,15},{6,12},{7,13},{8,2},{9,3},... | collective-permute-start | bytes 589832 | tf_op jit(solution)/shard_map/ppermute | solution.py:23
  44.2 23.5 %collective-permute-start.16 = (bf16[2,64,768]{2,1,0:T(8,128)(2,1)S(1)}, bf16[2,64,768]{2,1,0:T(8,128)(2,1)S(1)}, u32[]{:S(2)}, u32[]{:S(2)}) collective-permute-start(bf16[2,64,768]{2,1,0:T(8,128)(2,1)S(1)} %shard_map.53), channel_id=1, source_target_pairs={{0,14},{1,15},{2,12},{3,13},{4,10},{5,11},{6,8},{7,9},{8,6},{9,7},... | collective-permute-start | bytes 589832 | tf_op jit(solution)/shard_map/ppermute | solution.py:23
  50.6 16.3 %collective-permute-start.11 = (bf16[2,64,768]{2,1,0:T(8,128)(2,1)S(1)}, bf16[2,64,768]{2,1,0:T(8,128)(2,1)S(1)}, u32[]{:S(2)}, u32[]{:S(2)}) collective-permute-start(bf16[2,64,768]{2,1,0:T(8,128)(2,1)S(1)} %get-tuple-element.38), channel_id=1, source_target_pairs={{0,2},{1,3},{2,0},{3,1},{4,6},{5,7},{6,4},{7,5},{8,10},{9,11},{10,... | collective-permute-start | bytes 589832 | tf_op jit(solution)/shard_map/ppermute | solution.py:23
  50.9 16.8 %collective-permute-start.13 = (bf16[2,64,768]{2,1,0:T(8,128)(2,1)S(1)}, bf16[2,64,768]{2,1,0:T(8,128)(2,1)S(1)}, u32[]{:S(2)}, u32[]{:S(2)}) collective-permute-start(bf16[2,64,768]{2,1,0:T(8,128)(2,1)S(1)} %get-tuple-element.36), channel_id=1, source_target_pairs={{0,6},{1,7},{2,4},{3,5},{4,2},{5,3},{6,0},{7,1},{8,14},{9,15},{10,... | collective-permute-start | bytes 589832 | tf_op jit(solution)/shard_map/ppermute | solution.py:23
  62.0 5.7 %copy-start.1 = (s32[1,64,8]{1,2,0:T(8,128)S(1)}, s32[1,64,8]{1,2,0:T(8,128)}, u32[]{:S(2)}) copy-start(s32[1,64,8]{1,2,0:T(8,128)} %param.5) | copy-start | bytes 6148
  62.0 5.7 %collective-permute-start.12 = (bf16[2,64,768]{2,1,0:T(8,128)(2,1)S(1)}, bf16[2,64,768]{2,1,0:T(8,128)(2,1)S(1)}, u32[]{:S(2)}, u32[]{:S(2)}) collective-permute-start(bf16[2,64,768]{2,1,0:T(8,128)(2,1)S(1)} %get-tuple-element.39), channel_id=1, source_target_pairs={{0,4},{1,5},{2,6},{3,7},{4,0},{5,1},{6,2},{7,3},{8,12},{9,13},{10,... | collective-permute-start | bytes 589832 | tf_op jit(solution)/shard_map/ppermute | solution.py:23

commit v19 on v18

--- a/solution.py
+++ b/solution.py
@@ -118,34 +118,40 @@
     )(weights, *pieces)
 
 
-def pick_kernel(ids, *refs):
-    blocks, out = refs[:-1], refs[-1]
+def pick_kernel(flips, ids, *refs):
+    blocks, kept, out = refs[: len(flips)], refs[len(flips) : -1], refs[-1]
     experts, tokens, _ = blocks[0].shape
     top = ids.shape[0]
     span = 16
     chip = lax.div(lax.axis_index("expert"), CORES)
-    label = (lax.div(ids[...], CORES) ^ chip) * CORES + lax.rem(ids[...], CORES)
+    flip = lax.div(ids[...], CORES) ^ chip
+    place = jnp.full(flip.shape, -1, jnp.int32)
+    for j, known in enumerate(flips):
+        place = jnp.where(flip == known, j * CORES + lax.rem(ids[...], CORES), place)
     column = lax.broadcasted_iota(jnp.int32, (top, len(blocks) * experts * span), 1)
     for g in range(tokens // span):
         stacked = jnp.concatenate(
             [b[c, g * span : (g + 1) * span, :] for b in blocks for c in range(experts)], axis=0
         )
         picks = [
-            jnp.where(column == label[:, g * span + t : g * span + t + 1] * span + t, 1.0, 0.0)
+            jnp.where(column == place[:, g * span + t : g * span + t + 1] * span + t, 1.0, 0.0)
             for t in range(span)
         ]
         pick = jnp.concatenate(picks, axis=0).astype(jnp.bfloat16)
-        rows = jnp.dot(pick, stacked, preferred_element_type=jnp.float32)
-        out[g * span * top : (g + 1) * span * top, :] = rows.astype(jnp.bfloat16)
-
-
-def pick_routes(ids, blocks):
+        rows = jnp.dot(pick, stacked, preferred_element_type=jnp.float32).astype(jnp.bfloat16)
+        part = slice(g * span * top, (g + 1) * span * top)
+        out[part, :] = rows + kept[0][part, :] if kept else rows
+
+
+def pick_routes(ids, received, *kept):
     top, tokens = ids.shape
-    return pl.pallas_call(
-        pick_kernel,
+    flips = sorted(received)
+    blocks = [received[flip] for flip in flips]
+    return pl.pallas_call(
+        functools.partial(pick_kernel, flips),
         out_shape=jax.ShapeDtypeStruct((top * tokens, blocks[0].shape[2]), jnp.bfloat16),
         compiler_params=pltpu.CompilerParams(vmem_limit_bytes=16 << 20),
-    )(ids, *blocks)
+    )(ids, *blocks, *kept)
 
 
 def dense_device(upstream, route_ids, route_gates, weight_mat):
@@ -165,44 +171,38 @@
     rows, columns, weights = tie((rows, columns, weights))
     rows = widened(rows, columns)
     side = send(rows, owners, X)
-    near = send(rows, owners, Z_NEAR)
     far, far_columns, rows = tie((far, far_columns, rows))
     far = widened(far, far_columns)
     cross = send(far, owners, Z_NEAR)
     far_side = send(far, owners, X)
     (out_far,) = work(far)
     back_far = send(out_far, owners, Z_FAR)
-    side, _ = tie((side, out_far))
-    near, side = tie((near, side))
-    near_side = send(near, owners, X)
-    cross, _ = tie((cross, near))
+    side, rows, _ = tie((side, rows, out_far))
+    near = send(rows, owners, Z_NEAR)
+    out_side, out_own = work(side, rows)
+    back_side = send(out_side, owners, X)
+    cross, _ = tie((cross, out_own))
     cross_side = send(cross, owners, X)
     (out_cross,) = work(cross)
     back_cross = send(out_cross, owners, Z_NEAR ^ Z_FAR)
-    far_side, back_far, _ = tie((far_side, back_far, out_cross))
+    far_side, back_far, near, _ = tie((far_side, back_far, near, out_cross))
+    near_side = send(near, owners, X)
     (out_far_side,) = work(far_side)
     back_far_side = send(out_far_side, owners, X ^ Z_FAR)
-    cross_side, _ = tie((cross_side, out_far_side))
-    (out_cross_side,) = work(cross_side)
+    cross_side, near_side, back_side, _ = tie((cross_side, near_side, back_side, out_far_side))
+    out_cross_side, out_near, out_near_side = work(cross_side, near, near_side)
     back_cross_side = send(out_cross_side, owners, X ^ Z_NEAR ^ Z_FAR)
-    near_side, _ = tie((near_side, out_cross_side))
-    out_side, out_near, out_near_side = work(side, near, near_side)
     back_near_side = send(out_near_side, owners, X ^ Z_NEAR)
-    back_side = send(out_side, owners, X)
     back_near = send(out_near, owners, Z_NEAR)
-    rows, _ = tie((rows, out_near_side))
-    (out_own,) = work(rows)
-    received = {
+    far_parts = {
         0: out_own,
-        X: back_side,
-        Z_NEAR: back_near,
-        X ^ Z_NEAR: back_near_side,
         Z_FAR: back_far,
         X ^ Z_FAR: back_far_side,
         Z_NEAR ^ Z_FAR: back_cross,
         X ^ Z_NEAR ^ Z_FAR: back_cross_side,
     }
-    out = pick_routes(route_ids.T, [received[flip] for flip in sorted(received)])
+    near_parts = {X: back_side, Z_NEAR: back_near, X ^ Z_NEAR: back_near_side}
+    out = pick_routes(route_ids.T, near_parts, pick_routes(route_ids.T, far_parts))
     return out.reshape(1, tokens, top, weight_mat.shape[0])
 
 

time: 69.2 us -> 68.9 us (level)
  starting transfers between devices: 29.5 us -> 31.6 us
  waiting for transfers between devices: 25.7 us -> 24.3 us
  Pallas kernels: 10.5 us -> 9.5 us
    ppermute x15, starting transfers between devices: 24.5 us -> 26.5 us  [send(): return lax.ppermute(block, 'expert', route)]
    ppermute x15, waiting for transfers between devices: 24.6 us -> 23 us  [send(): return lax.ppermute(block, 'expert', route)]
    pallas_call x6 -> x5, Pallas kernels: 7.34 us -> 5.95 us  [products(): pl.pallas_call(functools.partial(products_kernel, len(pieces)), out_shape...]
    pallas_call x1 -> x2, Pallas kernels: 1.32 us -> 1.74 us  [pick_routes(): pl.pallas_call(functools.partial(pick_kernel, flips), out_shape=jax.Shape...]
  transfers between devices with their start and end apart: 17 -> 17, of which waited for: 8 -> 9; matrix products, arithmetic and copies ran while one was open for 0% -> 0% of each run, Pallas kernels for 13% -> 12%
where the time goes in v19:
time: 68.9 us; the launch traced here: 68.7 us
  starting transfers between devices  31.6 us (46%)
  waiting for transfers between devices  24.3 us (35%)
  Pallas kernels  9.5 us (14%)
  local copies, waits for them, and re-layouts  3.26 us (5%)
    ppermute x15, starting transfers between devices, send(): return lax.ppermute(block, 'expert', route)  26.5 us
    ppermute x15, waiting for transfers between devices, send(): return lax.ppermute(block, 'expert', route)  23 us
    pallas_call x5, Pallas kernels, products(): pl.pallas_call(functools.partial(products_kernel, len(pieces)), out_shape...  5.95 us
    ppermute x2, starting transfers between devices, send_across(): return lax.ppermute(block, ('pipe', 'expert'), route)  5.05 us
    unnamed x8, local copies, waits for them, and re-layouts  3.26 us
    pallas_call x2, Pallas kernels, pick_routes(): pl.pallas_call(functools.partial(pick_kernel, flips), out_shape=jax.Shape...  1.74 us
    pallas_call x1, Pallas kernels, turned(): pl.pallas_call(turn_kernel, out_shape=jax.ShapeDtypeStruct((depth, CORES...  1.67 us
  transfers between devices with their start and end apart: 17, of which 9 were waited for; matrix products, arithmetic and copies ran while one was open for 0% of the time, Pallas kernels for 12%

profile of v19, /device:TPU:0, one launch (start us, length us, event | category | flops | bytes accessed | tf_op | source)
XLA Modules:
  0.0 68.7 jit_solution(1965005737234526017)
XLA Ops:
  0.0 0.5 collective-permute-start.3
  0.5 2.5 %collective-permute-start.2 = (bf16[64,2048]{1,0:T(8,128)(2,1)}, bf16[64,2048]{1,0:T(8,128)(2,1)S(1)}, u32[]{:S(2)}, u32[]{:S(2)}) collective-permute-start(bf16[64,2048]{1,0:T(8,128)(2,1)} %bitcast.15), channel_id=1, source_target_pairs={{0,16},{1,17},{2,18},{3,19},{4,20},{5,21},{6,22},{7,23},{8,24},{9,... | collective-permute-start | bytes 786440 | tf_op jit(solution)/shard_map/ppermute | solution.py:33
  3.0 2.5 %collective-permute-start = (bf16[64,2048]{1,0:T(8,128)(2,1)}, bf16[64,2048]{1,0:T(8,128)(2,1)S(1)}, u32[]{:S(2)}, u32[]{:S(2)}) collective-permute-start(bf16[64,2048]{1,0:T(8,128)(2,1)} %bitcast.16), channel_id=1, source_target_pairs={{0,24},{1,25},{2,26},{3,27},{4,28},{5,29},{6,30},{7,31},{8,16},{9,... | collective-permute-start | bytes 786440 | tf_op jit(solution)/shard_map/ppermute | solution.py:33
  5.5 0.0 copy-start
  5.5 0.7 copy-done
  6.2 0.0 copy-start.2
  6.2 0.7 copy-done.2
  6.9 0.1 shard_map.46.columns
  7.0 0.1 collective-permute-start.1
  7.1 0.0 collective-permute-done.3.other
  7.1 0.0 copy-start.3
  7.1 1.9 %copy-done.3 = bf16[1,1,768,2048]{3,2,1,0:T(8,128)(2,1)S(1)} copy-done((bf16[1,1,768,2048]{3,2,1,0:T(8,128)(2,1)S(1)}, bf16[1,1,768,2048]{3,2,1,0:T(8,128)(2,1)}, u32[]{:S(2)}) %copy-start.3) | copy-done | bytes 3145752
  9.0 1.7 %shard_map.47.weights = bf16[2048,1536]{1,0:T(8,128)(2,1)S(1)} custom-call(bf16[768,2048]{1,0:T(8,128)(2,1)S(1)} %bitcast.14, bf16[768,2048]{1,0:T(8,128)(2,1)S(1)} %collective-permute-done.3.other), custom_call_target="tpu_custom_call" | custom-call | flops 12884901888 | tf_op jit(solution)/shard_map/pallas_call | solution.py:77
  10.7 0.6 collective-permute-done.2.rows
  11.3 1.8 %collective-permute-start.5 = (bf16[64,2176]{1,0:T(8,128)(2,1)S(1)}, bf16[64,2176]{1,0:T(8,128)(2,1)S(1)}, u32[]{:S(2)}, u32[]{:S(2)}) collective-permute-start(bf16[64,2176]{1,0:T(8,128)(2,1)S(1)} %shard_map.48.refs_1_), channel_id=1, source_target_pairs={{0,2},{1,3},{2,0},{3,1},{4,6},{5,7},{6,4},{7,5},{8,10},{9,11},{10,... | collective-permute-start | bytes 835592 | tf_op jit(solution)/shard_map/ppermute | solution.py:23
  13.1 5.7 %collective-permute-done.1.columns = bf16[64,128]{1,0:T(8,128)(2,1)S(1)} collective-permute-done((bf16[64,128]{1,0:T(8,128)(2,1)S(1)}, bf16[64,128]{1,0:T(8,128)(2,1)S(1)}, u32[]{:S(2)}, u32[]{:S(2)}) %collective-permute-start.1) | collective-permute-done | bytes 16416 | tf_op jit(solution)/shard_map/ppermute | solution.py:23
  18.8 0.7 %collective-permute-done.rows = bf16[64,2048]{1,0:T(8,128)(2,1)S(1)} collective-permute-done((bf16[64,2048]{1,0:T(8,128)(2,1)}, bf16[64,2048]{1,0:T(8,128)(2,1)S(1)}, u32[]{:S(2)}, u32[]{:S(2)}) %collective-permute-start) | collective-permute-done | bytes 262176 | tf_op jit(solution)/shard_map/ppermute | solution.py:33
  19.6 0.1 collective-permute-start.4
  19.7 1.6 %collective-permute-start.7 = (bf16[64,2176]{1,0:T(8,128)(2,1)S(1)}, bf16[64,2176]{1,0:T(8,128)(2,1)S(1)}, u32[]{:S(2)}, u32[]{:S(2)}) collective-permute-start(bf16[64,2176]{1,0:T(8,128)(2,1)S(1)} %shard_map.49.refs_0_), channel_id=1, source_target_pairs={{0,2},{1,3},{2,0},{3,1},{4,6},{5,7},{6,4},{7,5},{8,10},{9,11},{10,... | collective-permute-start | bytes 835592 | tf_op jit(solution)/shard_map/ppermute | solution.py:23
  21.2 1.2 %shard_map.50 = bf16[2,64,768]{2,1,0:T(8,128)(2,1)S(1)} custom-call(bf16[2048,1536]{1,0:T(8,128)(2,1)S(1)} %shard_map.47.weights, bf16[64,2176]{1,0:T(8,128)(2,1)S(1)} %shard_map.49.refs_0_), custom_call_target="tpu_custom_call" | custom-call | flops 4026531840 | bytes 6750208 | tf_op jit(solution)/shard_map/pallas_call | solution.py:109
  22.4 3.9 %collective-permute-start.8 = (bf16[2,64,768]{2,1,0:T(8,128)(2,1)S(1)}, bf16[2,64,768]{2,1,0:T(8,128)(2,1)S(1)}, u32[]{:S(2)}, u32[]{:S(2)}) collective-permute-start(bf16[2,64,768]{2,1,0:T(8,128)(2,1)S(1)} %shard_map.50), channel_id=1, source_target_pairs={{0,8},{1,9},{2,10},{3,11},{4,12},{5,13},{6,14},{7,15},{8,0},{9,1},... | collective-permute-start | bytes 589832 | tf_op jit(solution)/shard_map/ppermute | solution.py:23
  26.4 0.0 collective-permute-done.5.refs_0_
  26.4 0.9 %collective-permute-start.9 = (bf16[64,2176]{1,0:T(8,128)(2,1)S(1)}, bf16[64,2176]{1,0:T(8,128)(2,1)S(1)}, u32[]{:S(2)}, u32[]{:S(2)}) collective-permute-start(bf16[64,2176]{1,0:T(8,128)(2,1)S(1)} %shard_map.48.refs_1_), channel_id=1, source_target_pairs={{0,4},{1,5},{2,6},{3,7},{4,0},{5,1},{6,2},{7,3},{8,12},{9,13},{10,... | collective-permute-start | bytes 835592 | tf_op jit(solution)/shard_map/ppermute | solution.py:23
  27.2 1.0 %shard_map.51 = (bf16[2,64,768]{2,1,0:T(8,128)(2,1)S(1)}, bf16[2,64,768]{2,1,0:T(8,128)(2,1)S(1)}) custom-call(bf16[2048,1536]{1,0:T(8,128)(2,1)S(1)} %shard_map.47.weights, bf16[64,2176]{1,0:T(8,128)(2,1)S(1)} %collective-permute-done.5.refs_0_, bf16[64,2176]{1,0:T(8,128)(2,1)S(1)} %shard_map.48.refs_1_), custom_call_target="tpu_custom_call" | custom-call | flops 8053063680 | bytes 7208960 | tf_op jit(solution)/shard_map/pallas_call | solution.py:109
  28.2 3.1 %collective-permute-done.4.refs_0_ = bf16[64,2176]{1,0:T(8,128)(2,1)S(1)} collective-permute-done((bf16[64,2176]{1,0:T(8,128)(2,1)S(1)}, bf16[64,2176]{1,0:T(8,128)(2,1)S(1)}, u32[]{:S(2)}, u32[]{:S(2)}) %collective-permute-start.4) | collective-permute-done | bytes 278560 | tf_op jit(solution)/shard_map/ppermute | solution.py:23
  31.4 3.4 %collective-permute-start.6 = (bf16[64,2176]{1,0:T(8,128)(2,1)S(1)}, bf16[64,2176]{1,0:T(8,128)(2,1)S(1)}, u32[]{:S(2)}, u32[]{:S(2)}) collective-permute-start(bf16[64,2176]{1,0:T(8,128)(2,1)S(1)} %collective-permute-done.4.refs_0_), channel_id=1, source_target_pairs={{0,2},{1,3},{2,0},{3,1},{4,6},{5,7},{6,4},{7,5},{8,10},{9,11},{10,... | collective-permute-start | bytes 835592 | tf_op jit(solution)/shard_map/ppermute | solution.py:23
  34.8 0.0 collective-permute-start.11
  34.8 1.2 %shard_map.52 = bf16[2,64,768]{2,1,0:T(8,128)(2,1)S(1)} custom-call(bf16[2048,1536]{1,0:T(8,128)(2,1)S(1)} %shard_map.47.weights, bf16[64,2176]{1,0:T(8,128)(2,1)S(1)} %collective-permute-done.4.refs_0_), custom_call_target="tpu_custom_call" | custom-call | flops 4026531840 | bytes 6750208 | tf_op jit(solution)/shard_map/pallas_call | solution.py:109
  36.0 0.0 collective-permute-done.8.refs_1_
  36.0 3.6 %collective-permute-start.15 = (bf16[2,64,768]{2,1,0:T(8,128)(2,1)S(1)}, bf16[2,64,768]{2,1,0:T(8,128)(2,1)S(1)}, u32[]{:S(2)}, u32[]{:S(2)}) collective-permute-start(bf16[2,64,768]{2,1,0:T(8,128)(2,1)S(1)} %shard_map.52), channel_id=1, source_target_pairs={{0,12},{1,13},{2,14},{3,15},{4,8},{5,9},{6,10},{7,11},{8,4},{9,5},... | collective-permute-start | bytes 589832 | tf_op jit(solution)/shard_map/ppermute | solution.py:23
  39.6 0.0 collective-permute-done.7.refs_0_
  39.6 0.0 collective-permute-done.9.refs_1_
  39.6 2.0 %collective-permute-start.10 = (bf16[64,2176]{1,0:T(8,128)(2,1)S(1)}, bf16[64,2176]{1,0:T(8,128)(2,1)S(1)}, u32[]{:S(2)}, u32[]{:S(2)}) collective-permute-start(bf16[64,2176]{1,0:T(8,128)(2,1)S(1)} %collective-permute-done.9.refs_1_), channel_id=1, source_target_pairs={{0,2},{1,3},{2,0},{3,1},{4,6},{5,7},{6,4},{7,5},{8,10},{9,11},{10,... | collective-permute-start | bytes 835592 | tf_op jit(solution)/shard_map/ppermute | solution.py:23
  41.6 1.2 %shard_map.53 = bf16[2,64,768]{2,1,0:T(8,128)(2,1)S(1)} custom-call(bf16[2048,1536]{1,0:T(8,128)(2,1)S(1)} %shard_map.47.weights, bf16[64,2176]{1,0:T(8,128)(2,1)S(1)} %collective-permute-done.7.refs_0_), custom_call_target="tpu_custom_call" | custom-call | flops 4026531840 | bytes 6750208 | tf_op jit(solution)/shard_map/pallas_call | solution.py:109
  42.8 0.0 copy-start.1
  42.8 1.9 %collective-permute-start.14 = (bf16[2,64,768]{2,1,0:T(8,128)(2,1)S(1)}, bf16[2,64,768]{2,1,0:T(8,128)(2,1)S(1)}, u32[]{:S(2)}, u32[]{:S(2)}) collective-permute-start(bf16[2,64,768]{2,1,0:T(8,128)(2,1)S(1)} %shard_map.53), channel_id=1, source_target_pairs={{0,10},{1,11},{2,8},{3,9},{4,14},{5,15},{6,12},{7,13},{8,2},{9,3},... | collective-permute-start | bytes 589832 | tf_op jit(solution)/shard_map/ppermute | solution.py:23
  44.7 0.0 collective-permute-done.11.refs_0_
  44.7 0.0 collective-permute-done.6.refs_0_
  44.7 3.7 %collective-permute-done.10.refs_2_ = bf16[64,2176]{1,0:T(8,128)(2,1)S(1)} collective-permute-done((bf16[64,2176]{1,0:T(8,128)(2,1)S(1)}, bf16[64,2176]{1,0:T(8,128)(2,1)S(1)}, u32[]{:S(2)}, u32[]{:S(2)}) %collective-permute-start.10) | collective-permute-done | bytes 278560 | tf_op jit(solution)/shard_map/ppermute | solution.py:23
  48.4 1.4 %shard_map.54 = (bf16[2,64,768]{2,1,0:T(8,128)(2,1)S(1)}, bf16[2,64,768]{2,1,0:T(8,128)(2,1)S(1)}, bf16[2,64,768]{2,1,0:T(8,128)(2,1)S(1)}) custom-call(bf16[2048,1536]{1,0:T(8,128)(2,1)S(1)} %shard_map.47.weights, bf16[64,2176]{1,0:T(8,128)(2,1)S(1)} %collective-permute-done.6.refs_0_, bf16[64,2176]{1,0:T(8,128)(2,1)S(1)} %collective-permute-done.9.refs_1_, ...), custom_call_target="tpu_custom_call" | custom-call | flops 12079595520 | bytes 7667712 | tf_op jit(solution)/shard_map/pallas_call | solution.py:109
  49.8 4.5 %collective-permute-start.16 = (bf16[2,64,768]{2,1,0:T(8,128)(2,1)S(1)}, bf16[2,64,768]{2,1,0:T(8,128)(2,1)S(1)}, u32[]{:S(2)}, u32[]{:S(2)}) collective-permute-start(bf16[2,64,768]{2,1,0:T(8,128)(2,1)S(1)} %get-tuple-element.44), channel_id=1, source_target_pairs={{0,14},{1,15},{2,12},{3,13},{4,10},{5,11},{6,8},{7,9},{8,6},{9,7},... | collective-permute-start | bytes 589832 | tf_op jit(solution)/shard_map/ppermute | solution.py:23
  54.3 2.4 %collective-permute-start.12 = (bf16[2,64,768]{2,1,0:T(8,128)(2,1)S(1)}, bf16[2,64,768]{2,1,0:T(8,128)(2,1)S(1)}, u32[]{:S(2)}, u32[]{:S(2)}) collective-permute-start(bf16[2,64,768]{2,1,0:T(8,128)(2,1)S(1)} %get-tuple-element.41), channel_id=1, source_target_pairs={{0,4},{1,5},{2,6},{3,7},{4,0},{5,1},{6,2},{7,3},{8,12},{9,13},{10,... | collective-permute-start | bytes 589832 | tf_op jit(solution)/shard_map/ppermute | solution.py:23
  56.7 0.0 collective-permute-start.13
  56.7 0.0 collective-permute-done.15.refs_3_
  56.7 3.2 %collective-permute-done.14.refs_2_ = bf16[2,64,768]{2,1,0:T(8,128)(2,1)S(1)} collective-permute-done((bf16[2,64,768]{2,1,0:T(8,128)(2,1)S(1)}, bf16[2,64,768]{2,1,0:T(8,128)(2,1)S(1)}, u32[]{:S(2)}, u32[]{:S(2)}) %collective-permute-start.14) | collective-permute-done | bytes 196640 | tf_op jit(solution)/shard_map/ppermute | solution.py:23
  59.9 0.3 collective-permute-done.16.refs_4_
  60.2 0.0 copy-done.1
  60.2 0.4 shard_map.55.refs_3_
  60.6 3.4 %collective-permute-done.12.refs_1_ = bf16[2,64,768]{2,1,0:T(8,128)(2,1)S(1)} collective-permute-done((bf16[2,64,768]{2,1,0:T(8,128)(2,1)S(1)}, bf16[2,64,768]{2,1,0:T(8,128)(2,1)S(1)}, u32[]{:S(2)}, u32[]{:S(2)}) %collective-permute-start.12) | collective-permute-done | bytes 196640 | tf_op jit(solution)/shard_map/ppermute | solution.py:23
  64.0 3.4 %collective-permute-done.13.refs_2_ = bf16[2,64,768]{2,1,0:T(8,128)(2,1)S(1)} collective-permute-done((bf16[2,64,768]{2,1,0:T(8,128)(2,1)S(1)}, bf16[2,64,768]{2,1,0:T(8,128)(2,1)S(1)}, u32[]{:S(2)}, u32[]{:S(2)}) %collective-permute-start.13) | collective-permute-done | bytes 196640 | tf_op jit(solution)/shard_map/ppermute | solution.py:23
  67.4 1.3 %shard_map.56 = bf16[512,768]{1,0:T(8,128)(2,1)} custom-call(s32[8,64]{1,0:T(8,128)S(1)} %bitcast.11, bf16[2,64,768]{2,1,0:T(8,128)(2,1)S(1)} %collective-permute-done.11.refs_0_, bf16[2,64,768]{2,1,0:T(8,128)(2,1)S(1)} %collective-permute-done.12.refs_1_, bf16[2,64,768]{2,1,0:T(8,128)(2,1)S(1)} %collective-permute-done.13.refs_2_, ...), custom_call_target="tpu_custom_call" | custom-call | tf_op jit(solution)/shard_map/pallas_call | solution.py:150
  (2 shorter events, 0.0 us)
Async XLA Ops:
  0.0 7.1 %collective-permute-start.3 = (bf16[768,2048]{1,0:T(8,128)(2,1)}, bf16[768,2048]{1,0:T(8,128)(2,1)S(1)}, u32[]{:S(2)}, u32[]{:S(2)}) collective-permute-start(bf16[768,2048]{1,0:T(8,128)(2,1)} %bitcast.13), channel_id=1, source_target_pairs={{0,1},{1,0},{2,3},{3,2},{4,5},{5,4},{6,7},{7,6},{8,9},{9,8},{10,11... | collective-permute-start | bytes 9437192 | tf_op jit(solution)/shard_map/ppermute | solution.py:23
  0.5 10.8 %collective-permute-start.2 = (bf16[64,2048]{1,0:T(8,128)(2,1)}, bf16[64,2048]{1,0:T(8,128)(2,1)S(1)}, u32[]{:S(2)}, u32[]{:S(2)}) collective-permute-start(bf16[64,2048]{1,0:T(8,128)(2,1)} %bitcast.15), channel_id=1, source_target_pairs={{0,16},{1,17},{2,18},{3,19},{4,20},{5,21},{6,22},{7,23},{8,24},{9,... | collective-permute-start | bytes 786440 | tf_op jit(solution)/shard_map/ppermute | solution.py:33
  3.0 16.6 %collective-permute-start = (bf16[64,2048]{1,0:T(8,128)(2,1)}, bf16[64,2048]{1,0:T(8,128)(2,1)S(1)}, u32[]{:S(2)}, u32[]{:S(2)}) collective-permute-start(bf16[64,2048]{1,0:T(8,128)(2,1)} %bitcast.16), channel_id=1, source_target_pairs={{0,24},{1,25},{2,26},{3,27},{4,28},{5,29},{6,30},{7,31},{8,16},{9,... | collective-permute-start | bytes 786440 | tf_op jit(solution)/shard_map/ppermute | solution.py:33
  5.5 0.7 copy-start
  6.2 0.7 copy-start.2
  7.0 11.8 %collective-permute-start.1 = (bf16[64,128]{1,0:T(8,128)(2,1)S(1)}, bf16[64,128]{1,0:T(8,128)(2,1)S(1)}, u32[]{:S(2)}, u32[]{:S(2)}) collective-permute-start(bf16[64,128]{1,0:T(8,128)(2,1)S(1)} %shard_map.46.columns), channel_id=1, source_target_pairs={{0,8},{1,9},{2,10},{3,11},{4,12},{5,13},{6,14},{7,15},{8,0},{9,1},... | collective-permute-start | bytes 49160 | tf_op jit(solution)/shard_map/ppermute | solution.py:23
  7.1 1.9 %copy-start.3 = (bf16[1,1,768,2048]{3,2,1,0:T(8,128)(2,1)S(1)}, bf16[1,1,768,2048]{3,2,1,0:T(8,128)(2,1)}, u32[]{:S(2)}) copy-start(bf16[1,1,768,2048]{3,2,1,0:T(8,128)(2,1)} %param.7) | copy-start | bytes 9437188
  11.3 15.1 %collective-permute-start.5 = (bf16[64,2176]{1,0:T(8,128)(2,1)S(1)}, bf16[64,2176]{1,0:T(8,128)(2,1)S(1)}, u32[]{:S(2)}, u32[]{:S(2)}) collective-permute-start(bf16[64,2176]{1,0:T(8,128)(2,1)S(1)} %shard_map.48.refs_1_), channel_id=1, source_target_pairs={{0,2},{1,3},{2,0},{3,1},{4,6},{5,7},{6,4},{7,5},{8,10},{9,11},{10,... | collective-permute-start | bytes 835592 | tf_op jit(solution)/shard_map/ppermute | solution.py:23
  19.6 11.8 %collective-permute-start.4 = (bf16[64,2176]{1,0:T(8,128)(2,1)S(1)}, bf16[64,2176]{1,0:T(8,128)(2,1)S(1)}, u32[]{:S(2)}, u32[]{:S(2)}) collective-permute-start(bf16[64,2176]{1,0:T(8,128)(2,1)S(1)} %shard_map.49.refs_0_), channel_id=1, source_target_pairs={{0,4},{1,5},{2,6},{3,7},{4,0},{5,1},{6,2},{7,3},{8,12},{9,13},{10,... | collective-permute-start | bytes 835592 | tf_op jit(solution)/shard_map/ppermute | solution.py:23
  19.7 19.9 %collective-permute-start.7 = (bf16[64,2176]{1,0:T(8,128)(2,1)S(1)}, bf16[64,2176]{1,0:T(8,128)(2,1)S(1)}, u32[]{:S(2)}, u32[]{:S(2)}) collective-permute-start(bf16[64,2176]{1,0:T(8,128)(2,1)S(1)} %shard_map.49.refs_0_), channel_id=1, source_target_pairs={{0,2},{1,3},{2,0},{3,1},{4,6},{5,7},{6,4},{7,5},{8,10},{9,11},{10,... | collective-permute-start | bytes 835592 | tf_op jit(solution)/shard_map/ppermute | solution.py:23
  22.4 13.6 %collective-permute-start.8 = (bf16[2,64,768]{2,1,0:T(8,128)(2,1)S(1)}, bf16[2,64,768]{2,1,0:T(8,128)(2,1)S(1)}, u32[]{:S(2)}, u32[]{:S(2)}) collective-permute-start(bf16[2,64,768]{2,1,0:T(8,128)(2,1)S(1)} %shard_map.50), channel_id=1, source_target_pairs={{0,8},{1,9},{2,10},{3,11},{4,12},{5,13},{6,14},{7,15},{8,0},{9,1},... | collective-permute-start | bytes 589832 | tf_op jit(solution)/shard_map/ppermute | solution.py:23
  26.4 13.2 %collective-permute-start.9 = (bf16[64,2176]{1,0:T(8,128)(2,1)S(1)}, bf16[64,2176]{1,0:T(8,128)(2,1)S(1)}, u32[]{:S(2)}, u32[]{:S(2)}) collective-permute-start(bf16[64,2176]{1,0:T(8,128)(2,1)S(1)} %shard_map.48.refs_1_), channel_id=1, source_target_pairs={{0,4},{1,5},{2,6},{3,7},{4,0},{5,1},{6,2},{7,3},{8,12},{9,13},{10,... | collective-permute-start | bytes 835592 | tf_op jit(solution)/shard_map/ppermute | solution.py:23
  31.4 13.3 %collective-permute-start.6 = (bf16[64,2176]{1,0:T(8,128)(2,1)S(1)}, bf16[64,2176]{1,0:T(8,128)(2,1)S(1)}, u32[]{:S(2)}, u32[]{:S(2)}) collective-permute-start(bf16[64,2176]{1,0:T(8,128)(2,1)S(1)} %collective-permute-done.4.refs_0_), channel_id=1, source_target_pairs={{0,2},{1,3},{2,0},{3,1},{4,6},{5,7},{6,4},{7,5},{8,10},{9,11},{10,... | collective-permute-start | bytes 835592 | tf_op jit(solution)/shard_map/ppermute | solution.py:23
  34.8 9.9 %collective-permute-start.11 = (bf16[2,64,768]{2,1,0:T(8,128)(2,1)S(1)}, bf16[2,64,768]{2,1,0:T(8,128)(2,1)S(1)}, u32[]{:S(2)}, u32[]{:S(2)}) collective-permute-start(bf16[2,64,768]{2,1,0:T(8,128)(2,1)S(1)} %get-tuple-element.36), channel_id=1, source_target_pairs={{0,2},{1,3},{2,0},{3,1},{4,6},{5,7},{6,4},{7,5},{8,10},{9,11},{10,... | collective-permute-start | bytes 589832 | tf_op jit(solution)/shard_map/ppermute | solution.py:23
  36.0 20.7 %collective-permute-start.15 = (bf16[2,64,768]{2,1,0:T(8,128)(2,1)S(1)}, bf16[2,64,768]{2,1,0:T(8,128)(2,1)S(1)}, u32[]{:S(2)}, u32[]{:S(2)}) collective-permute-start(bf16[2,64,768]{2,1,0:T(8,128)(2,1)S(1)} %shard_map.52), channel_id=1, source_target_pairs={{0,12},{1,13},{2,14},{3,15},{4,8},{5,9},{6,10},{7,11},{8,4},{9,5},... | collective-permute-start | bytes 589832 | tf_op jit(solution)/shard_map/ppermute | solution.py:23
  39.6 8.8 %collective-permute-start.10 = (bf16[64,2176]{1,0:T(8,128)(2,1)S(1)}, bf16[64,2176]{1,0:T(8,128)(2,1)S(1)}, u32[]{:S(2)}, u32[]{:S(2)}) collective-permute-start(bf16[64,2176]{1,0:T(8,128)(2,1)S(1)} %collective-permute-done.9.refs_1_), channel_id=1, source_target_pairs={{0,2},{1,3},{2,0},{3,1},{4,6},{5,7},{6,4},{7,5},{8,10},{9,11},{10,... | collective-permute-start | bytes 835592 | tf_op jit(solution)/shard_map/ppermute | solution.py:23
  42.8 17.4 %copy-start.1 = (s32[1,64,8]{1,2,0:T(8,128)S(1)}, s32[1,64,8]{1,2,0:T(8,128)}, u32[]{:S(2)}) copy-start(s32[1,64,8]{1,2,0:T(8,128)} %param.5) | copy-start | bytes 6148
  42.8 17.1 %collective-permute-start.14 = (bf16[2,64,768]{2,1,0:T(8,128)(2,1)S(1)}, bf16[2,64,768]{2,1,0:T(8,128)(2,1)S(1)}, u32[]{:S(2)}, u32[]{:S(2)}) collective-permute-start(bf16[2,64,768]{2,1,0:T(8,128)(2,1)S(1)} %shard_map.53), channel_id=1, source_target_pairs={{0,10},{1,11},{2,8},{3,9},{4,14},{5,15},{6,12},{7,13},{8,2},{9,3},... | collective-permute-start | bytes 589832 | tf_op jit(solution)/shard_map/ppermute | solution.py:23
  49.8 10.4 %collective-permute-start.16 = (bf16[2,64,768]{2,1,0:T(8,128)(2,1)S(1)}, bf16[2,64,768]{2,1,0:T(8,128)(2,1)S(1)}, u32[]{:S(2)}, u32[]{:S(2)}) collective-permute-start(bf16[2,64,768]{2,1,0:T(8,128)(2,1)S(1)} %get-tuple-element.44), channel_id=1, source_target_pairs={{0,14},{1,15},{2,12},{3,13},{4,10},{5,11},{6,8},{7,9},{8,6},{9,7},... | collective-permute-start | bytes 589832 | tf_op jit(solution)/shard_map/ppermute | solution.py:23
  54.3 9.7 %collective-permute-start.12 = (bf16[2,64,768]{2,1,0:T(8,128)(2,1)S(1)}, bf16[2,64,768]{2,1,0:T(8,128)(2,1)S(1)}, u32[]{:S(2)}, u32[]{:S(2)}) collective-permute-start(bf16[2,64,768]{2,1,0:T(8,128)(2,1)S(1)} %get-tuple-element.41), channel_id=1, source_target_pairs={{0,4},{1,5},{2,6},{3,7},{4,0},{5,1},{6,2},{7,3},{8,12},{9,13},{10,... | collective-permute-start | bytes 589832 | tf_op jit(solution)/shard_map/ppermute | solution.py:23
  56.7 10.8 %collective-permute-start.13 = (bf16[2,64,768]{2,1,0:T(8,128)(2,1)S(1)}, bf16[2,64,768]{2,1,0:T(8,128)(2,1)S(1)}, u32[]{:S(2)}, u32[]{:S(2)}) collective-permute-start(bf16[2,64,768]{2,1,0:T(8,128)(2,1)S(1)} %get-tuple-element.42), channel_id=1, source_target_pairs={{0,6},{1,7},{2,4},{3,5},{4,2},{5,3},{6,0},{7,1},{8,14},{9,15},{10,... | collective-permute-start | bytes 589832 | tf_op jit(solution)/shard_map/ppermute | solution.py:23

commit v20 on v17

--- a/solution.py
+++ b/solution.py
@@ -176,18 +176,20 @@
     cross_side = send(cross, owners, X)
     (out_cross,) = work(cross)
     back_cross = send(out_cross, owners, Z_NEAR ^ Z_FAR)
-    far_side, back_far, near, _ = tie((far_side, back_far, near, out_cross))
-    near_side = send(near, owners, X)
+    far_side, back_far, _ = tie((far_side, back_far, out_cross))
     (out_far_side,) = work(far_side)
     back_far_side = send(out_far_side, owners, X ^ Z_FAR)
-    cross_side, _ = tie((cross_side, out_far_side))
+    near, cross_side, _ = tie((near, cross_side, out_far_side))
+    near_side = send(near, owners, X)
     (out_cross_side,) = work(cross_side)
     back_cross_side = send(out_cross_side, owners, X ^ Z_NEAR ^ Z_FAR)
-    side, near_side, _ = tie((side, near_side, out_cross_side))
-    out_side, out_near, out_near_side = work(side, near, near_side)
-    back_near_side = send(out_near_side, owners, X ^ Z_NEAR)
+    side, near, _ = tie((side, near, out_cross_side))
+    out_side, out_near = work(side, near)
     back_side = send(out_side, owners, X)
     back_near = send(out_near, owners, Z_NEAR)
+    near_side, _ = tie((near_side, out_near))
+    (out_near_side,) = work(near_side)
+    back_near_side = send(out_near_side, owners, X ^ Z_NEAR)
     rows, _ = tie((rows, out_near_side))
     (out_own,) = work(rows)
     received = {

time: 71.1 us -> 68.9 us (0.969)
  the two profiles are of different devices: /device:TPU:26 before, /device:TPU:22 now
where the time goes in v20:
time: 68.9 us; the launch traced here: 68.7 us
  starting transfers between devices  32.6 us (47%)
  waiting for transfers between devices  21.4 us (31%)
  Pallas kernels  11.3 us (16%)
  local copies, waits for them, and re-layouts  3.26 us (5%)
    ppermute x15, starting transfers between devices, send(): return lax.ppermute(block, 'expert', route)  30.8 us
    ppermute x15, waiting for transfers between devices, send(): return lax.ppermute(block, 'expert', route)  21.4 us
    pallas_call x7, Pallas kernels, products(): pl.pallas_call(functools.partial(products_kernel, len(pieces)), out_shape...  8.14 us
    unnamed x8, local copies, waits for them, and re-layouts  3.26 us
    ppermute x2, starting transfers between devices, send_across(): return lax.ppermute(block, ('pipe', 'expert'), route)  1.8 us
    pallas_call x1, Pallas kernels, turned(): pl.pallas_call(turn_kernel, out_shape=jax.ShapeDtypeStruct((depth, CORES...  1.67 us
  transfers between devices with their start and end apart: 17, of which 6 were waited for; matrix products, arithmetic and copies ran while one was open for 0% of the time, Pallas kernels for 14%

profile of v20, /device:TPU:22, one launch (start us, length us, event | category | flops | bytes accessed | tf_op | source)
XLA Modules:
  0.0 68.7 jit_solution(7588644877002836800)
XLA Ops:
  0.0 0.0 collective-permute-start.2
  0.0 0.3 collective-permute-start
  0.3 1.5 %collective-permute-start.4 = (bf16[64,2048]{1,0:T(8,128)(2,1)}, bf16[64,2048]{1,0:T(8,128)(2,1)S(1)}, u32[]{:S(2)}, u32[]{:S(2)}) collective-permute-start(bf16[64,2048]{1,0:T(8,128)(2,1)} %bitcast.15), channel_id=1, source_target_pairs={{0,16},{1,17},{2,18},{3,19},{4,20},{5,21},{6,22},{7,23},{8,24},{9,... | collective-permute-start | bytes 786440 | tf_op jit(solution)/shard_map/ppermute | solution.py:33
  1.8 0.0 copy-start
  1.8 0.7 copy-done
  2.5 0.0 copy-start.2
  2.5 0.7 copy-done.2
  3.2 0.1 shard_map.46.columns
  3.3 2.6 %collective-permute-start.1 = (bf16[64,128]{1,0:T(8,128)(2,1)S(1)}, bf16[64,128]{1,0:T(8,128)(2,1)S(1)}, u32[]{:S(2)}, u32[]{:S(2)}) collective-permute-start(bf16[64,128]{1,0:T(8,128)(2,1)S(1)} %shard_map.46.columns), channel_id=1, source_target_pairs={{0,8},{1,9},{2,10},{3,11},{4,12},{5,13},{6,14},{7,15},{8,0},{9,1},... | collective-permute-start | bytes 49160 | tf_op jit(solution)/shard_map/ppermute | solution.py:23
  5.9 0.0 collective-permute-done.2.other
  5.9 0.0 copy-start.3
  5.9 1.9 %copy-done.3 = bf16[1,1,768,2048]{3,2,1,0:T(8,128)(2,1)S(1)} copy-done((bf16[1,1,768,2048]{3,2,1,0:T(8,128)(2,1)S(1)}, bf16[1,1,768,2048]{3,2,1,0:T(8,128)(2,1)}, u32[]{:S(2)}) %copy-start.3) | copy-done | bytes 3145752
  7.8 1.7 %shard_map.47.weights = bf16[2048,1536]{1,0:T(8,128)(2,1)S(1)} custom-call(bf16[768,2048]{1,0:T(8,128)(2,1)S(1)} %bitcast.13, bf16[768,2048]{1,0:T(8,128)(2,1)S(1)} %collective-permute-done.2.other), custom_call_target="tpu_custom_call" | custom-call | flops 12884901888 | tf_op jit(solution)/shard_map/pallas_call | solution.py:77
  9.5 3.6 %collective-permute-done.1.columns = bf16[64,128]{1,0:T(8,128)(2,1)S(1)} collective-permute-done((bf16[64,128]{1,0:T(8,128)(2,1)S(1)}, bf16[64,128]{1,0:T(8,128)(2,1)S(1)}, u32[]{:S(2)}, u32[]{:S(2)}) %collective-permute-start.1) | collective-permute-done | bytes 16416 | tf_op jit(solution)/shard_map/ppermute | solution.py:23
  13.1 0.0 collective-permute-done.rows
  13.1 5.2 %collective-permute-start.3 = (bf16[64,2176]{1,0:T(8,128)(2,1)S(1)}, bf16[64,2176]{1,0:T(8,128)(2,1)S(1)}, u32[]{:S(2)}, u32[]{:S(2)}) collective-permute-start(bf16[64,2176]{1,0:T(8,128)(2,1)S(1)} %shard_map.48.refs_0_), channel_id=1, source_target_pairs={{0,4},{1,5},{2,6},{3,7},{4,0},{5,1},{6,2},{7,3},{8,12},{9,13},{10,... | collective-permute-start | bytes 835592 | tf_op jit(solution)/shard_map/ppermute | solution.py:23
  18.3 0.5 collective-permute-start.7
  18.8 1.2 %shard_map.49 = bf16[2,64,768]{2,1,0:T(8,128)(2,1)S(1)} custom-call(bf16[2048,1536]{1,0:T(8,128)(2,1)S(1)} %shard_map.47.weights, bf16[64,2176]{1,0:T(8,128)(2,1)S(1)} %shard_map.48.refs_0_), custom_call_target="tpu_custom_call" | custom-call | flops 4026531840 | bytes 6750208 | tf_op jit(solution)/shard_map/pallas_call | solution.py:109
  20.0 0.1 collective-permute-start.8
  20.1 0.0 collective-permute-done.4.rows
  20.1 1.1 %collective-permute-start.5 = (bf16[64,2176]{1,0:T(8,128)(2,1)S(1)}, bf16[64,2176]{1,0:T(8,128)(2,1)S(1)}, u32[]{:S(2)}, u32[]{:S(2)}) collective-permute-start(bf16[64,2176]{1,0:T(8,128)(2,1)S(1)} %shard_map.50.refs_0_), channel_id=1, source_target_pairs={{0,4},{1,5},{2,6},{3,7},{4,0},{5,1},{6,2},{7,3},{8,12},{9,13},{10,... | collective-permute-start | bytes 835592 | tf_op jit(solution)/shard_map/ppermute | solution.py:23
  21.2 1.5 %collective-permute-start.10 = (bf16[64,2176]{1,0:T(8,128)(2,1)S(1)}, bf16[64,2176]{1,0:T(8,128)(2,1)S(1)}, u32[]{:S(2)}, u32[]{:S(2)}) collective-permute-start(bf16[64,2176]{1,0:T(8,128)(2,1)S(1)} %shard_map.50.refs_0_), channel_id=1, source_target_pairs={{0,2},{1,3},{2,0},{3,1},{4,6},{5,7},{6,4},{7,5},{8,10},{9,11},{10,... | collective-permute-start | bytes 835592 | tf_op jit(solution)/shard_map/ppermute | solution.py:23
  22.7 4.9 %collective-permute-done.3.refs_0_ = bf16[64,2176]{1,0:T(8,128)(2,1)S(1)} collective-permute-done((bf16[64,2176]{1,0:T(8,128)(2,1)S(1)}, bf16[64,2176]{1,0:T(8,128)(2,1)S(1)}, u32[]{:S(2)}, u32[]{:S(2)}) %collective-permute-start.3) | collective-permute-done | bytes 278560 | tf_op jit(solution)/shard_map/ppermute | solution.py:23
  27.6 0.0 collective-permute-start.6
  27.6 1.2 %shard_map.51 = bf16[2,64,768]{2,1,0:T(8,128)(2,1)S(1)} custom-call(bf16[2048,1536]{1,0:T(8,128)(2,1)S(1)} %shard_map.47.weights, bf16[64,2176]{1,0:T(8,128)(2,1)S(1)} %collective-permute-done.3.refs_0_), custom_call_target="tpu_custom_call" | custom-call | flops 4026531840 | bytes 6750208 | tf_op jit(solution)/shard_map/pallas_call | solution.py:109
  28.8 0.0 collective-permute-done.8.refs_4_
  28.9 2.6 %collective-permute-start.15 = (bf16[2,64,768]{2,1,0:T(8,128)(2,1)S(1)}, bf16[2,64,768]{2,1,0:T(8,128)(2,1)S(1)}, u32[]{:S(2)}, u32[]{:S(2)}) collective-permute-start(bf16[2,64,768]{2,1,0:T(8,128)(2,1)S(1)} %shard_map.51), channel_id=1, source_target_pairs={{0,12},{1,13},{2,14},{3,15},{4,8},{5,9},{6,10},{7,11},{8,4},{9,5},... | collective-permute-start | bytes 589832 | tf_op jit(solution)/shard_map/ppermute | solution.py:23
  31.5 0.0 collective-permute-done.7.refs_0_
  31.5 1.2 %shard_map.52 = bf16[2,64,768]{2,1,0:T(8,128)(2,1)S(1)} custom-call(bf16[2048,1536]{1,0:T(8,128)(2,1)S(1)} %shard_map.47.weights, bf16[64,2176]{1,0:T(8,128)(2,1)S(1)} %collective-permute-done.7.refs_0_), custom_call_target="tpu_custom_call" | custom-call | flops 4026531840 | bytes 6750208 | tf_op jit(solution)/shard_map/pallas_call | solution.py:109
  32.7 5.7 %collective-permute-start.14 = (bf16[2,64,768]{2,1,0:T(8,128)(2,1)S(1)}, bf16[2,64,768]{2,1,0:T(8,128)(2,1)S(1)}, u32[]{:S(2)}, u32[]{:S(2)}) collective-permute-start(bf16[2,64,768]{2,1,0:T(8,128)(2,1)S(1)} %shard_map.52), channel_id=1, source_target_pairs={{0,10},{1,11},{2,8},{3,9},{4,14},{5,15},{6,12},{7,13},{8,2},{9,3},... | collective-permute-start | bytes 589832 | tf_op jit(solution)/shard_map/ppermute | solution.py:23
  38.4 0.0 collective-permute-done.5.refs_1_
  38.4 2.3 %collective-permute-done.6.refs_0_ = bf16[64,2176]{1,0:T(8,128)(2,1)S(1)} collective-permute-done((bf16[64,2176]{1,0:T(8,128)(2,1)S(1)}, bf16[64,2176]{1,0:T(8,128)(2,1)S(1)}, u32[]{:S(2)}, u32[]{:S(2)}) %collective-permute-start.6) | collective-permute-done | bytes 278560 | tf_op jit(solution)/shard_map/ppermute | solution.py:23
  40.7 0.5 collective-permute-start.9
  41.2 1.2 %shard_map.53 = bf16[2,64,768]{2,1,0:T(8,128)(2,1)S(1)} custom-call(bf16[2048,1536]{1,0:T(8,128)(2,1)S(1)} %shard_map.47.weights, bf16[64,2176]{1,0:T(8,128)(2,1)S(1)} %collective-permute-done.6.refs_0_), custom_call_target="tpu_custom_call" | custom-call | flops 4026531840 | bytes 6750208 | tf_op jit(solution)/shard_map/pallas_call | solution.py:109
  42.4 0.1 collective-permute-start.16
  42.5 0.0 collective-permute-done.10.refs_0_
  42.5 1.0 %shard_map.54 = (bf16[2,64,768]{2,1,0:T(8,128)(2,1)S(1)}, bf16[2,64,768]{2,1,0:T(8,128)(2,1)S(1)}) custom-call(bf16[2048,1536]{1,0:T(8,128)(2,1)S(1)} %shard_map.47.weights, bf16[64,2176]{1,0:T(8,128)(2,1)S(1)} %collective-permute-done.10.refs_0_, bf16[64,2176]{1,0:T(8,128)(2,1)S(1)} %collective-permute-done.5.refs_1_), custom_call_target="tpu_custom_call" | custom-call | flops 8053063680 | bytes 7208960 | tf_op jit(solution)/shard_map/pallas_call | solution.py:109
  43.5 1.5 %collective-permute-start.11 = (bf16[2,64,768]{2,1,0:T(8,128)(2,1)S(1)}, bf16[2,64,768]{2,1,0:T(8,128)(2,1)S(1)}, u32[]{:S(2)}, u32[]{:S(2)}) collective-permute-start(bf16[2,64,768]{2,1,0:T(8,128)(2,1)S(1)} %get-tuple-element.37), channel_id=1, source_target_pairs={{0,2},{1,3},{2,0},{3,1},{4,6},{5,7},{6,4},{7,5},{8,10},{9,11},{10,... | collective-permute-start | bytes 589832 | tf_op jit(solution)/shard_map/ppermute | solution.py:23
  45.0 5.2 %collective-permute-done.9.refs_0_ = bf16[64,2176]{1,0:T(8,128)(2,1)S(1)} collective-permute-done((bf16[64,2176]{1,0:T(8,128)(2,1)S(1)}, bf16[64,2176]{1,0:T(8,128)(2,1)S(1)}, u32[]{:S(2)}, u32[]{:S(2)}) %collective-permute-start.9) | collective-permute-done | bytes 278560 | tf_op jit(solution)/shard_map/ppermute | solution.py:23
  50.2 9.3 %collective-permute-start.12 = (bf16[2,64,768]{2,1,0:T(8,128)(2,1)S(1)}, bf16[2,64,768]{2,1,0:T(8,128)(2,1)S(1)}, u32[]{:S(2)}, u32[]{:S(2)}) collective-permute-start(bf16[2,64,768]{2,1,0:T(8,128)(2,1)S(1)} %get-tuple-element.34), channel_id=1, source_target_pairs={{0,4},{1,5},{2,6},{3,7},{4,0},{5,1},{6,2},{7,3},{8,12},{9,13},{10,... | collective-permute-start | bytes 589832 | tf_op jit(solution)/shard_map/ppermute | solution.py:23
  59.5 1.2 %shard_map.55 = bf16[2,64,768]{2,1,0:T(8,128)(2,1)S(1)} custom-call(bf16[2048,1536]{1,0:T(8,128)(2,1)S(1)} %shard_map.47.weights, bf16[64,2176]{1,0:T(8,128)(2,1)S(1)} %collective-permute-done.9.refs_0_), custom_call_target="tpu_custom_call" | custom-call | flops 4026531840 | bytes 6750208 | tf_op jit(solution)/shard_map/pallas_call | solution.py:109
  60.7 0.0 copy-start.1
  60.8 0.0 collective-permute-done.14.refs_5_
  60.8 0.1 collective-permute-start.13
  60.8 1.2 %shard_map.56.refs_0_ = bf16[2,64,768]{2,1,0:T(8,128)(2,1)S(1)} custom-call(bf16[2048,1536]{1,0:T(8,128)(2,1)S(1)} %shard_map.47.weights, bf16[64,2176]{1,0:T(8,128)(2,1)S(1)} %shard_map.50.refs_0_), custom_call_target="tpu_custom_call" | custom-call | flops 4026531840 | bytes 6750208 | tf_op jit(solution)/shard_map/pallas_call | solution.py:109
  62.0 0.0 collective-permute-done.15.refs_6_
  62.1 0.0 collective-permute-done.11.refs_1_
  62.1 1.1 %collective-permute-done.12.refs_2_ = bf16[2,64,768]{2,1,0:T(8,128)(2,1)S(1)} collective-permute-done((bf16[2,64,768]{2,1,0:T(8,128)(2,1)S(1)}, bf16[2,64,768]{2,1,0:T(8,128)(2,1)S(1)}, u32[]{:S(2)}, u32[]{:S(2)}) %collective-permute-start.12) | collective-permute-done | bytes 196640 | tf_op jit(solution)/shard_map/ppermute | solution.py:23
  63.2 0.0 collective-permute-done.16.refs_7_
  63.2 4.2 %collective-permute-done.13.refs_3_ = bf16[2,64,768]{2,1,0:T(8,128)(2,1)S(1)} collective-permute-done((bf16[2,64,768]{2,1,0:T(8,128)(2,1)S(1)}, bf16[2,64,768]{2,1,0:T(8,128)(2,1)S(1)}, u32[]{:S(2)}, u32[]{:S(2)}) %collective-permute-start.13) | collective-permute-done | bytes 196640 | tf_op jit(solution)/shard_map/ppermute | solution.py:23
  67.4 0.0 copy-done.1
  67.4 1.3 %shard_map.57 = bf16[512,768]{1,0:T(8,128)(2,1)} custom-call(s32[8,64]{1,0:T(8,128)S(1)} %bitcast.10, bf16[2,64,768]{2,1,0:T(8,128)(2,1)S(1)} %shard_map.56.refs_0_, bf16[2,64,768]{2,1,0:T(8,128)(2,1)S(1)} %collective-permute-done.11.refs_1_, bf16[2,64,768]{2,1,0:T(8,128)(2,1)S(1)} %collective-permute-done.12.refs_2_, ...), custom_call_target="tpu_custom_call" | custom-call | tf_op jit(solution)/shard_map/pallas_call | solution.py:144
  (2 shorter events, 0.0 us)
Async XLA Ops:
  0.0 5.9 %collective-permute-start.2 = (bf16[768,2048]{1,0:T(8,128)(2,1)}, bf16[768,2048]{1,0:T(8,128)(2,1)S(1)}, u32[]{:S(2)}, u32[]{:S(2)}) collective-permute-start(bf16[768,2048]{1,0:T(8,128)(2,1)} %bitcast.12), channel_id=1, source_target_pairs={{0,1},{1,0},{2,3},{3,2},{4,5},{5,4},{6,7},{7,6},{8,9},{9,8},{10,11... | collective-permute-start | bytes 9437192 | tf_op jit(solution)/shard_map/ppermute | solution.py:23
  0.0 13.1 %collective-permute-start = (bf16[64,2048]{1,0:T(8,128)(2,1)}, bf16[64,2048]{1,0:T(8,128)(2,1)S(1)}, u32[]{:S(2)}, u32[]{:S(2)}) collective-permute-start(bf16[64,2048]{1,0:T(8,128)(2,1)} %bitcast.14), channel_id=1, source_target_pairs={{0,24},{1,25},{2,26},{3,27},{4,28},{5,29},{6,30},{7,31},{8,16},{9,... | collective-permute-start | bytes 786440 | tf_op jit(solution)/shard_map/ppermute | solution.py:33
  0.3 19.8 %collective-permute-start.4 = (bf16[64,2048]{1,0:T(8,128)(2,1)}, bf16[64,2048]{1,0:T(8,128)(2,1)S(1)}, u32[]{:S(2)}, u32[]{:S(2)}) collective-permute-start(bf16[64,2048]{1,0:T(8,128)(2,1)} %bitcast.15), channel_id=1, source_target_pairs={{0,16},{1,17},{2,18},{3,19},{4,20},{5,21},{6,22},{7,23},{8,24},{9,... | collective-permute-start | bytes 786440 | tf_op jit(solution)/shard_map/ppermute | solution.py:33
  1.8 0.7 copy-start
  2.5 0.7 copy-start.2
  3.3 9.8 %collective-permute-start.1 = (bf16[64,128]{1,0:T(8,128)(2,1)S(1)}, bf16[64,128]{1,0:T(8,128)(2,1)S(1)}, u32[]{:S(2)}, u32[]{:S(2)}) collective-permute-start(bf16[64,128]{1,0:T(8,128)(2,1)S(1)} %shard_map.46.columns), channel_id=1, source_target_pairs={{0,8},{1,9},{2,10},{3,11},{4,12},{5,13},{6,14},{7,15},{8,0},{9,1},... | collective-permute-start | bytes 49160 | tf_op jit(solution)/shard_map/ppermute | solution.py:23
  5.9 1.9 %copy-start.3 = (bf16[1,1,768,2048]{3,2,1,0:T(8,128)(2,1)S(1)}, bf16[1,1,768,2048]{3,2,1,0:T(8,128)(2,1)}, u32[]{:S(2)}) copy-start(bf16[1,1,768,2048]{3,2,1,0:T(8,128)(2,1)} %param.7) | copy-start | bytes 9437188
  13.1 14.5 %collective-permute-start.3 = (bf16[64,2176]{1,0:T(8,128)(2,1)S(1)}, bf16[64,2176]{1,0:T(8,128)(2,1)S(1)}, u32[]{:S(2)}, u32[]{:S(2)}) collective-permute-start(bf16[64,2176]{1,0:T(8,128)(2,1)S(1)} %shard_map.48.refs_0_), channel_id=1, source_target_pairs={{0,4},{1,5},{2,6},{3,7},{4,0},{5,1},{6,2},{7,3},{8,12},{9,13},{10,... | collective-permute-start | bytes 835592 | tf_op jit(solution)/shard_map/ppermute | solution.py:23
  18.3 13.2 %collective-permute-start.7 = (bf16[64,2176]{1,0:T(8,128)(2,1)S(1)}, bf16[64,2176]{1,0:T(8,128)(2,1)S(1)}, u32[]{:S(2)}, u32[]{:S(2)}) collective-permute-start(bf16[64,2176]{1,0:T(8,128)(2,1)S(1)} %shard_map.48.refs_0_), channel_id=1, source_target_pairs={{0,2},{1,3},{2,0},{3,1},{4,6},{5,7},{6,4},{7,5},{8,10},{9,11},{10,... | collective-permute-start | bytes 835592 | tf_op jit(solution)/shard_map/ppermute | solution.py:23
  20.0 8.9 %collective-permute-start.8 = (bf16[2,64,768]{2,1,0:T(8,128)(2,1)S(1)}, bf16[2,64,768]{2,1,0:T(8,128)(2,1)S(1)}, u32[]{:S(2)}, u32[]{:S(2)}) collective-permute-start(bf16[2,64,768]{2,1,0:T(8,128)(2,1)S(1)} %shard_map.49), channel_id=1, source_target_pairs={{0,8},{1,9},{2,10},{3,11},{4,12},{5,13},{6,14},{7,15},{8,0},{9,1},... | collective-permute-start | bytes 589832 | tf_op jit(solution)/shard_map/ppermute | solution.py:23
  20.1 18.2 %collective-permute-start.5 = (bf16[64,2176]{1,0:T(8,128)(2,1)S(1)}, bf16[64,2176]{1,0:T(8,128)(2,1)S(1)}, u32[]{:S(2)}, u32[]{:S(2)}) collective-permute-start(bf16[64,2176]{1,0:T(8,128)(2,1)S(1)} %shard_map.50.refs_0_), channel_id=1, source_target_pairs={{0,4},{1,5},{2,6},{3,7},{4,0},{5,1},{6,2},{7,3},{8,12},{9,13},{10,... | collective-permute-start | bytes 835592 | tf_op jit(solution)/shard_map/ppermute | solution.py:23
  21.2 21.2 %collective-permute-start.10 = (bf16[64,2176]{1,0:T(8,128)(2,1)S(1)}, bf16[64,2176]{1,0:T(8,128)(2,1)S(1)}, u32[]{:S(2)}, u32[]{:S(2)}) collective-permute-start(bf16[64,2176]{1,0:T(8,128)(2,1)S(1)} %shard_map.50.refs_0_), channel_id=1, source_target_pairs={{0,2},{1,3},{2,0},{3,1},{4,6},{5,7},{6,4},{7,5},{8,10},{9,11},{10,... | collective-permute-start | bytes 835592 | tf_op jit(solution)/shard_map/ppermute | solution.py:23
  27.6 13.0 %collective-permute-start.6 = (bf16[64,2176]{1,0:T(8,128)(2,1)S(1)}, bf16[64,2176]{1,0:T(8,128)(2,1)S(1)}, u32[]{:S(2)}, u32[]{:S(2)}) collective-permute-start(bf16[64,2176]{1,0:T(8,128)(2,1)S(1)} %collective-permute-done.3.refs_0_), channel_id=1, source_target_pairs={{0,2},{1,3},{2,0},{3,1},{4,6},{5,7},{6,4},{7,5},{8,10},{9,11},{10,... | collective-permute-start | bytes 835592 | tf_op jit(solution)/shard_map/ppermute | solution.py:23
  28.9 33.2 %collective-permute-start.15 = (bf16[2,64,768]{2,1,0:T(8,128)(2,1)S(1)}, bf16[2,64,768]{2,1,0:T(8,128)(2,1)S(1)}, u32[]{:S(2)}, u32[]{:S(2)}) collective-permute-start(bf16[2,64,768]{2,1,0:T(8,128)(2,1)S(1)} %shard_map.51), channel_id=1, source_target_pairs={{0,12},{1,13},{2,14},{3,15},{4,8},{5,9},{6,10},{7,11},{8,4},{9,5},... | collective-permute-start | bytes 589832 | tf_op jit(solution)/shard_map/ppermute | solution.py:23
  32.7 28.1 %collective-permute-start.14 = (bf16[2,64,768]{2,1,0:T(8,128)(2,1)S(1)}, bf16[2,64,768]{2,1,0:T(8,128)(2,1)S(1)}, u32[]{:S(2)}, u32[]{:S(2)}) collective-permute-start(bf16[2,64,768]{2,1,0:T(8,128)(2,1)S(1)} %shard_map.52), channel_id=1, source_target_pairs={{0,10},{1,11},{2,8},{3,9},{4,14},{5,15},{6,12},{7,13},{8,2},{9,3},... | collective-permute-start | bytes 589832 | tf_op jit(solution)/shard_map/ppermute | solution.py:23
  40.7 9.6 %collective-permute-start.9 = (bf16[64,2176]{1,0:T(8,128)(2,1)S(1)}, bf16[64,2176]{1,0:T(8,128)(2,1)S(1)}, u32[]{:S(2)}, u32[]{:S(2)}) collective-permute-start(bf16[64,2176]{1,0:T(8,128)(2,1)S(1)} %collective-permute-done.5.refs_1_), channel_id=1, source_target_pairs={{0,2},{1,3},{2,0},{3,1},{4,6},{5,7},{6,4},{7,5},{8,10},{9,11},{10,... | collective-permute-start | bytes 835592 | tf_op jit(solution)/shard_map/ppermute | solution.py:23
  42.4 20.8 %collective-permute-start.16 = (bf16[2,64,768]{2,1,0:T(8,128)(2,1)S(1)}, bf16[2,64,768]{2,1,0:T(8,128)(2,1)S(1)}, u32[]{:S(2)}, u32[]{:S(2)}) collective-permute-start(bf16[2,64,768]{2,1,0:T(8,128)(2,1)S(1)} %shard_map.53), channel_id=1, source_target_pairs={{0,14},{1,15},{2,12},{3,13},{4,10},{5,11},{6,8},{7,9},{8,6},{9,7},... | collective-permute-start | bytes 589832 | tf_op jit(solution)/shard_map/ppermute | solution.py:23
  43.5 18.6 %collective-permute-start.11 = (bf16[2,64,768]{2,1,0:T(8,128)(2,1)S(1)}, bf16[2,64,768]{2,1,0:T(8,128)(2,1)S(1)}, u32[]{:S(2)}, u32[]{:S(2)}) collective-permute-start(bf16[2,64,768]{2,1,0:T(8,128)(2,1)S(1)} %get-tuple-element.37), channel_id=1, source_target_pairs={{0,2},{1,3},{2,0},{3,1},{4,6},{5,7},{6,4},{7,5},{8,10},{9,11},{10,... | collective-permute-start | bytes 589832 | tf_op jit(solution)/shard_map/ppermute | solution.py:23
  50.2 12.9 %collective-permute-start.12 = (bf16[2,64,768]{2,1,0:T(8,128)(2,1)S(1)}, bf16[2,64,768]{2,1,0:T(8,128)(2,1)S(1)}, u32[]{:S(2)}, u32[]{:S(2)}) collective-permute-start(bf16[2,64,768]{2,1,0:T(8,128)(2,1)S(1)} %get-tuple-element.34), channel_id=1, source_target_pairs={{0,4},{1,5},{2,6},{3,7},{4,0},{5,1},{6,2},{7,3},{8,12},{9,13},{10,... | collective-permute-start | bytes 589832 | tf_op jit(solution)/shard_map/ppermute | solution.py:23
  60.7 6.7 %copy-start.1 = (s32[1,64,8]{1,2,0:T(8,128)S(1)}, s32[1,64,8]{1,2,0:T(8,128)}, u32[]{:S(2)}) copy-start(s32[1,64,8]{1,2,0:T(8,128)} %param.5) | copy-start | bytes 6148
  60.8 6.6 %collective-permute-start.13 = (bf16[2,64,768]{2,1,0:T(8,128)(2,1)S(1)}, bf16[2,64,768]{2,1,0:T(8,128)(2,1)S(1)}, u32[]{:S(2)}, u32[]{:S(2)}) collective-permute-start(bf16[2,64,768]{2,1,0:T(8,128)(2,1)S(1)} %shard_map.55), channel_id=1, source_target_pairs={{0,6},{1,7},{2,4},{3,5},{4,2},{5,3},{6,0},{7,1},{8,14},{9,15},{10,... | collective-permute-start | bytes 589832 | tf_op jit(solution)/shard_map/ppermute | solution.py:23

commit v21 on v19

--- a/solution.py
+++ b/solution.py
@@ -171,27 +171,30 @@
     rows, columns, weights = tie((rows, columns, weights))
     rows = widened(rows, columns)
     side = send(rows, owners, X)
+    near = send(rows, owners, Z_NEAR)
     far, far_columns, rows = tie((far, far_columns, rows))
     far = widened(far, far_columns)
     cross = send(far, owners, Z_NEAR)
     far_side = send(far, owners, X)
     (out_far,) = work(far)
     back_far = send(out_far, owners, Z_FAR)
-    side, rows, _ = tie((side, rows, out_far))
-    near = send(rows, owners, Z_NEAR)
+    side, _ = tie((side, out_far))
     out_side, out_own = work(side, rows)
     back_side = send(out_side, owners, X)
-    cross, _ = tie((cross, out_own))
+    near, _ = tie((near, out_side))
+    near_side = send(near, owners, X)
+    cross, _ = tie((cross, near))
     cross_side = send(cross, owners, X)
     (out_cross,) = work(cross)
     back_cross = send(out_cross, owners, Z_NEAR ^ Z_FAR)
-    far_side, back_far, near, _ = tie((far_side, back_far, near, out_cross))
-    near_side = send(near, owners, X)
+    far_side, back_far, back_side, _ = tie((far_side, back_far, back_side, out_cross))
     (out_far_side,) = work(far_side)
     back_far_side = send(out_far_side, owners, X ^ Z_FAR)
-    cross_side, near_side, back_side, _ = tie((cross_side, near_side, back_side, out_far_side))
-    out_cross_side, out_near, out_near_side = work(cross_side, near, near_side)
+    cross_side, _ = tie((cross_side, out_far_side))
+    (out_cross_side,) = work(cross_side)
     back_cross_side = send(out_cross_side, owners, X ^ Z_NEAR ^ Z_FAR)
+    near_side, _ = tie((near_side, out_cross_side))
+    out_near, out_near_side = work(near, near_side)
     back_near_side = send(out_near_side, owners, X ^ Z_NEAR)
     back_near = send(out_near, owners, Z_NEAR)
     far_parts = {

time: 68.9 us -> 68.9 us (level)
  waiting for transfers between devices: 24.3 us -> 19.7 us
  starting transfers between devices: 31.6 us -> 35.3 us
  Pallas kernels: 9.5 us -> 10.3 us
    ppermute x15, waiting for transfers between devices: 23 us -> 18.7 us  [send(): return lax.ppermute(block, 'expert', route)]
    ppermute x15, starting transfers between devices: 26.5 us -> 30.3 us  [send(): return lax.ppermute(block, 'expert', route)]
    pallas_call x5 -> x6, Pallas kernels: 5.95 us -> 6.73 us  [products(): pl.pallas_call(functools.partial(products_kernel, len(pieces)), out_shape...]
  transfers between devices with their start and end apart: 17 -> 17, of which waited for: 9 -> 7; matrix products, arithmetic and copies ran while one was open for 0% -> 0% of each run, Pallas kernels for 12% -> 13%
where the time goes in v21:
time: 68.9 us; the launch traced here: 68.7 us
  starting transfers between devices  35.3 us (51%)
  waiting for transfers between devices  19.7 us (29%)
  Pallas kernels  10.3 us (15%)
  local copies, waits for them, and re-layouts  3.26 us (5%)
    ppermute x15, starting transfers between devices, send(): return lax.ppermute(block, 'expert', route)  30.3 us
    ppermute x15, waiting for transfers between devices, send(): return lax.ppermute(block, 'expert', route)  18.7 us
    pallas_call x6, Pallas kernels, products(): pl.pallas_call(functools.partial(products_kernel, len(pieces)), out_shape...  6.73 us
    ppermute x2, starting transfers between devices, send_across(): return lax.ppermute(block, ('pipe', 'expert'), route)  5.05 us
    unnamed x8, local copies, waits for them, and re-layouts  3.26 us
    pallas_call x2, Pallas kernels, pick_routes(): pl.pallas_call(functools.partial(pick_kernel, flips), out_shape=jax.Shape...  1.75 us
    pallas_call x1, Pallas kernels, turned(): pl.pallas_call(turn_kernel, out_shape=jax.ShapeDtypeStruct((depth, CORES...  1.67 us
  transfers between devices with their start and end apart: 17, of which 7 were waited for; matrix products, arithmetic and copies ran while one was open for 0% of the time, Pallas kernels for 13%

profile of v21, /device:TPU:0, one launch (start us, length us, event | category | flops | bytes accessed | tf_op | source)
XLA Modules:
  0.0 68.7 jit_solution(3665684166644547714)
XLA Ops:
  0.0 0.5 collective-permute-start.3
  0.5 2.5 %collective-permute-start.2 = (bf16[64,2048]{1,0:T(8,128)(2,1)}, bf16[64,2048]{1,0:T(8,128)(2,1)S(1)}, u32[]{:S(2)}, u32[]{:S(2)}) collective-permute-start(bf16[64,2048]{1,0:T(8,128)(2,1)} %bitcast.15), channel_id=1, source_target_pairs={{0,16},{1,17},{2,18},{3,19},{4,20},{5,21},{6,22},{7,23},{8,24},{9,... | collective-permute-start | bytes 786440 | tf_op jit(solution)/shard_map/ppermute | solution.py:33
  3.0 2.5 %collective-permute-start = (bf16[64,2048]{1,0:T(8,128)(2,1)}, bf16[64,2048]{1,0:T(8,128)(2,1)S(1)}, u32[]{:S(2)}, u32[]{:S(2)}) collective-permute-start(bf16[64,2048]{1,0:T(8,128)(2,1)} %bitcast.16), channel_id=1, source_target_pairs={{0,24},{1,25},{2,26},{3,27},{4,28},{5,29},{6,30},{7,31},{8,16},{9,... | collective-permute-start | bytes 786440 | tf_op jit(solution)/shard_map/ppermute | solution.py:33
  5.5 0.0 copy-start
  5.5 0.7 copy-done
  6.2 0.0 copy-start.2
  6.2 0.7 copy-done.2
  6.9 0.1 shard_map.46.columns
  7.0 0.1 collective-permute-start.1
  7.1 0.0 collective-permute-done.3.other
  7.1 0.0 copy-start.3
  7.1 1.9 %copy-done.3 = bf16[1,1,768,2048]{3,2,1,0:T(8,128)(2,1)S(1)} copy-done((bf16[1,1,768,2048]{3,2,1,0:T(8,128)(2,1)S(1)}, bf16[1,1,768,2048]{3,2,1,0:T(8,128)(2,1)}, u32[]{:S(2)}) %copy-start.3) | copy-done | bytes 3145752
  9.0 1.7 %shard_map.47.weights = bf16[2048,1536]{1,0:T(8,128)(2,1)S(1)} custom-call(bf16[768,2048]{1,0:T(8,128)(2,1)S(1)} %bitcast.14, bf16[768,2048]{1,0:T(8,128)(2,1)S(1)} %collective-permute-done.3.other), custom_call_target="tpu_custom_call" | custom-call | flops 12884901888 | tf_op jit(solution)/shard_map/pallas_call | solution.py:77
  10.7 0.6 collective-permute-done.2.rows
  11.3 1.8 %collective-permute-start.6 = (bf16[64,2176]{1,0:T(8,128)(2,1)S(1)}, bf16[64,2176]{1,0:T(8,128)(2,1)S(1)}, u32[]{:S(2)}, u32[]{:S(2)}) collective-permute-start(bf16[64,2176]{1,0:T(8,128)(2,1)S(1)} %shard_map.48.refs_1_), channel_id=1, source_target_pairs={{0,2},{1,3},{2,0},{3,1},{4,6},{5,7},{6,4},{7,5},{8,10},{9,11},{10,... | collective-permute-start | bytes 835592 | tf_op jit(solution)/shard_map/ppermute | solution.py:23
  13.1 6.1 %collective-permute-start.9 = (bf16[64,2176]{1,0:T(8,128)(2,1)S(1)}, bf16[64,2176]{1,0:T(8,128)(2,1)S(1)}, u32[]{:S(2)}, u32[]{:S(2)}) collective-permute-start(bf16[64,2176]{1,0:T(8,128)(2,1)S(1)} %shard_map.48.refs_1_), channel_id=1, source_target_pairs={{0,4},{1,5},{2,6},{3,7},{4,0},{5,1},{6,2},{7,3},{8,12},{9,13},{10,... | collective-permute-start | bytes 835592 | tf_op jit(solution)/shard_map/ppermute | solution.py:23
  19.2 0.0 collective-permute-done.1.columns
  19.2 0.4 collective-permute-done.rows
  19.6 0.1 collective-permute-start.8
  19.7 1.6 %collective-permute-start.4 = (bf16[64,2176]{1,0:T(8,128)(2,1)S(1)}, bf16[64,2176]{1,0:T(8,128)(2,1)S(1)}, u32[]{:S(2)}, u32[]{:S(2)}) collective-permute-start(bf16[64,2176]{1,0:T(8,128)(2,1)S(1)} %shard_map.49.refs_0_), channel_id=1, source_target_pairs={{0,2},{1,3},{2,0},{3,1},{4,6},{5,7},{6,4},{7,5},{8,10},{9,11},{10,... | collective-permute-start | bytes 835592 | tf_op jit(solution)/shard_map/ppermute | solution.py:23
  21.2 1.2 %shard_map.50 = bf16[2,64,768]{2,1,0:T(8,128)(2,1)S(1)} custom-call(bf16[2048,1536]{1,0:T(8,128)(2,1)S(1)} %shard_map.47.weights, bf16[64,2176]{1,0:T(8,128)(2,1)S(1)} %shard_map.49.refs_0_), custom_call_target="tpu_custom_call" | custom-call | flops 4026531840 | bytes 6750208 | tf_op jit(solution)/shard_map/pallas_call | solution.py:109
  22.4 4.0 %collective-permute-start.5 = (bf16[2,64,768]{2,1,0:T(8,128)(2,1)S(1)}, bf16[2,64,768]{2,1,0:T(8,128)(2,1)S(1)}, u32[]{:S(2)}, u32[]{:S(2)}) collective-permute-start(bf16[2,64,768]{2,1,0:T(8,128)(2,1)S(1)} %shard_map.50), channel_id=1, source_target_pairs={{0,8},{1,9},{2,10},{3,11},{4,12},{5,13},{6,14},{7,15},{8,0},{9,1},... | collective-permute-start | bytes 589832 | tf_op jit(solution)/shard_map/ppermute | solution.py:23
  26.4 0.0 collective-permute-done.6.refs_0_
  26.5 1.0 %shard_map.51 = (bf16[2,64,768]{2,1,0:T(8,128)(2,1)S(1)}, bf16[2,64,768]{2,1,0:T(8,128)(2,1)S(1)}) custom-call(bf16[2048,1536]{1,0:T(8,128)(2,1)S(1)} %shard_map.47.weights, bf16[64,2176]{1,0:T(8,128)(2,1)S(1)} %collective-permute-done.6.refs_0_, bf16[64,2176]{1,0:T(8,128)(2,1)S(1)} %shard_map.48.refs_1_), custom_call_target="tpu_custom_call" | custom-call | flops 8053063680 | bytes 7208960 | tf_op jit(solution)/shard_map/pallas_call | solution.py:109
  27.4 0.5 collective-permute-start.7
  27.9 0.0 collective-permute-done.9.refs_0_
  28.0 1.6 %collective-permute-start.10 = (bf16[64,2176]{1,0:T(8,128)(2,1)S(1)}, bf16[64,2176]{1,0:T(8,128)(2,1)S(1)}, u32[]{:S(2)}, u32[]{:S(2)}) collective-permute-start(bf16[64,2176]{1,0:T(8,128)(2,1)S(1)} %collective-permute-done.9.refs_0_), channel_id=1, source_target_pairs={{0,2},{1,3},{2,0},{3,1},{4,6},{5,7},{6,4},{7,5},{8,10},{9,11},{10,... | collective-permute-start | bytes 835592 | tf_op jit(solution)/shard_map/ppermute | solution.py:23
  29.5 6.1 %collective-permute-done.8.refs_0_ = bf16[64,2176]{1,0:T(8,128)(2,1)S(1)} collective-permute-done((bf16[64,2176]{1,0:T(8,128)(2,1)S(1)}, bf16[64,2176]{1,0:T(8,128)(2,1)S(1)}, u32[]{:S(2)}, u32[]{:S(2)}) %collective-permute-start.8) | collective-permute-done | bytes 278560 | tf_op jit(solution)/shard_map/ppermute | solution.py:23
  35.6 0.9 %collective-permute-start.11 = (bf16[64,2176]{1,0:T(8,128)(2,1)S(1)}, bf16[64,2176]{1,0:T(8,128)(2,1)S(1)}, u32[]{:S(2)}, u32[]{:S(2)}) collective-permute-start(bf16[64,2176]{1,0:T(8,128)(2,1)S(1)} %collective-permute-done.8.refs_0_), channel_id=1, source_target_pairs={{0,2},{1,3},{2,0},{3,1},{4,6},{5,7},{6,4},{7,5},{8,10},{9,11},{10,... | collective-permute-start | bytes 835592 | tf_op jit(solution)/shard_map/ppermute | solution.py:23
  36.5 1.2 %shard_map.52 = bf16[2,64,768]{2,1,0:T(8,128)(2,1)S(1)} custom-call(bf16[2048,1536]{1,0:T(8,128)(2,1)S(1)} %shard_map.47.weights, bf16[64,2176]{1,0:T(8,128)(2,1)S(1)} %collective-permute-done.8.refs_0_), custom_call_target="tpu_custom_call" | custom-call | flops 4026531840 | bytes 6750208 | tf_op jit(solution)/shard_map/pallas_call | solution.py:109
  37.7 0.0 collective-permute-done.5.refs_1_
  37.7 3.5 %collective-permute-start.15 = (bf16[2,64,768]{2,1,0:T(8,128)(2,1)S(1)}, bf16[2,64,768]{2,1,0:T(8,128)(2,1)S(1)}, u32[]{:S(2)}, u32[]{:S(2)}) collective-permute-start(bf16[2,64,768]{2,1,0:T(8,128)(2,1)S(1)} %shard_map.52), channel_id=1, source_target_pairs={{0,12},{1,13},{2,14},{3,15},{4,8},{5,9},{6,10},{7,11},{8,4},{9,5},... | collective-permute-start | bytes 589832 | tf_op jit(solution)/shard_map/ppermute | solution.py:23
  41.2 0.0 collective-permute-done.4.refs_0_
  41.2 0.0 collective-permute-done.7.refs_0_
  41.2 1.2 %shard_map.53 = bf16[2,64,768]{2,1,0:T(8,128)(2,1)S(1)} custom-call(bf16[2048,1536]{1,0:T(8,128)(2,1)S(1)} %shard_map.47.weights, bf16[64,2176]{1,0:T(8,128)(2,1)S(1)} %collective-permute-done.4.refs_0_), custom_call_target="tpu_custom_call" | custom-call | flops 4026531840 | bytes 6750208 | tf_op jit(solution)/shard_map/pallas_call | solution.py:109
  42.4 0.1 collective-permute-start.14
  42.5 2.8 %collective-permute-done.11.refs_0_ = bf16[64,2176]{1,0:T(8,128)(2,1)S(1)} collective-permute-done((bf16[64,2176]{1,0:T(8,128)(2,1)S(1)}, bf16[64,2176]{1,0:T(8,128)(2,1)S(1)}, u32[]{:S(2)}, u32[]{:S(2)}) %collective-permute-start.11) | collective-permute-done | bytes 278560 | tf_op jit(solution)/shard_map/ppermute | solution.py:23
  45.3 1.2 %shard_map.54 = bf16[2,64,768]{2,1,0:T(8,128)(2,1)S(1)} custom-call(bf16[2048,1536]{1,0:T(8,128)(2,1)S(1)} %shard_map.47.weights, bf16[64,2176]{1,0:T(8,128)(2,1)S(1)} %collective-permute-done.11.refs_0_), custom_call_target="tpu_custom_call" | custom-call | flops 4026531840 | bytes 6750208 | tf_op jit(solution)/shard_map/pallas_call | solution.py:109
  46.5 0.0 copy-start.1
  46.5 3.5 %collective-permute-start.16 = (bf16[2,64,768]{2,1,0:T(8,128)(2,1)S(1)}, bf16[2,64,768]{2,1,0:T(8,128)(2,1)S(1)}, u32[]{:S(2)}, u32[]{:S(2)}) collective-permute-start(bf16[2,64,768]{2,1,0:T(8,128)(2,1)S(1)} %shard_map.54), channel_id=1, source_target_pairs={{0,14},{1,15},{2,12},{3,13},{4,10},{5,11},{6,8},{7,9},{8,6},{9,7},... | collective-permute-start | bytes 589832 | tf_op jit(solution)/shard_map/ppermute | solution.py:23
  50.0 0.0 collective-permute-done.10.refs_1_
  50.0 1.0 %shard_map.55 = (bf16[2,64,768]{2,1,0:T(8,128)(2,1)S(1)}, bf16[2,64,768]{2,1,0:T(8,128)(2,1)S(1)}) custom-call(bf16[2048,1536]{1,0:T(8,128)(2,1)S(1)} %shard_map.47.weights, bf16[64,2176]{1,0:T(8,128)(2,1)S(1)} %collective-permute-done.9.refs_0_, bf16[64,2176]{1,0:T(8,128)(2,1)S(1)} %collective-permute-done.10.refs_1_), custom_call_target="tpu_custom_call" | custom-call | flops 8053063680 | bytes 7208960 | tf_op jit(solution)/shard_map/pallas_call | solution.py:109
  51.0 6.1 %collective-permute-start.12 = (bf16[2,64,768]{2,1,0:T(8,128)(2,1)S(1)}, bf16[2,64,768]{2,1,0:T(8,128)(2,1)S(1)}, u32[]{:S(2)}, u32[]{:S(2)}) collective-permute-start(bf16[2,64,768]{2,1,0:T(8,128)(2,1)S(1)} %get-tuple-element.37), channel_id=1, source_target_pairs={{0,4},{1,5},{2,6},{3,7},{4,0},{5,1},{6,2},{7,3},{8,12},{9,13},{10,... | collective-permute-start | bytes 589832 | tf_op jit(solution)/shard_map/ppermute | solution.py:23
  57.1 0.0 collective-permute-start.13
  57.2 0.0 collective-permute-done.15.refs_3_
  57.2 5.3 %collective-permute-done.14.refs_2_ = bf16[2,64,768]{2,1,0:T(8,128)(2,1)S(1)} collective-permute-done((bf16[2,64,768]{2,1,0:T(8,128)(2,1)S(1)}, bf16[2,64,768]{2,1,0:T(8,128)(2,1)S(1)}, u32[]{:S(2)}, u32[]{:S(2)}) %collective-permute-start.14) | collective-permute-done | bytes 196640 | tf_op jit(solution)/shard_map/ppermute | solution.py:23
  62.5 0.0 collective-permute-done.16.refs_4_
  62.5 0.0 copy-done.1
  62.5 0.4 shard_map.56.refs_3_
  62.9 2.2 %collective-permute-done.12.refs_1_ = bf16[2,64,768]{2,1,0:T(8,128)(2,1)S(1)} collective-permute-done((bf16[2,64,768]{2,1,0:T(8,128)(2,1)S(1)}, bf16[2,64,768]{2,1,0:T(8,128)(2,1)S(1)}, u32[]{:S(2)}, u32[]{:S(2)}) %collective-permute-start.12) | collective-permute-done | bytes 196640 | tf_op jit(solution)/shard_map/ppermute | solution.py:23
  65.1 2.3 %collective-permute-done.13.refs_2_ = bf16[2,64,768]{2,1,0:T(8,128)(2,1)S(1)} collective-permute-done((bf16[2,64,768]{2,1,0:T(8,128)(2,1)S(1)}, bf16[2,64,768]{2,1,0:T(8,128)(2,1)S(1)}, u32[]{:S(2)}, u32[]{:S(2)}) %collective-permute-start.13) | collective-permute-done | bytes 196640 | tf_op jit(solution)/shard_map/ppermute | solution.py:23
  67.4 1.3 %shard_map.57 = bf16[512,768]{1,0:T(8,128)(2,1)} custom-call(s32[8,64]{1,0:T(8,128)S(1)} %bitcast.11, bf16[2,64,768]{2,1,0:T(8,128)(2,1)S(1)} %collective-permute-done.7.refs_0_, bf16[2,64,768]{2,1,0:T(8,128)(2,1)S(1)} %collective-permute-done.12.refs_1_, bf16[2,64,768]{2,1,0:T(8,128)(2,1)S(1)} %collective-permute-done.13.refs_2_, ...), custom_call_target="tpu_custom_call" | custom-call | tf_op jit(solution)/shard_map/pallas_call | solution.py:150
  (2 shorter events, 0.0 us)
Async XLA Ops:
  0.0 7.1 %collective-permute-start.3 = (bf16[768,2048]{1,0:T(8,128)(2,1)}, bf16[768,2048]{1,0:T(8,128)(2,1)S(1)}, u32[]{:S(2)}, u32[]{:S(2)}) collective-permute-start(bf16[768,2048]{1,0:T(8,128)(2,1)} %bitcast.13), channel_id=1, source_target_pairs={{0,1},{1,0},{2,3},{3,2},{4,5},{5,4},{6,7},{7,6},{8,9},{9,8},{10,11... | collective-permute-start | bytes 9437192 | tf_op jit(solution)/shard_map/ppermute | solution.py:23
  0.5 10.8 %collective-permute-start.2 = (bf16[64,2048]{1,0:T(8,128)(2,1)}, bf16[64,2048]{1,0:T(8,128)(2,1)S(1)}, u32[]{:S(2)}, u32[]{:S(2)}) collective-permute-start(bf16[64,2048]{1,0:T(8,128)(2,1)} %bitcast.15), channel_id=1, source_target_pairs={{0,16},{1,17},{2,18},{3,19},{4,20},{5,21},{6,22},{7,23},{8,24},{9,... | collective-permute-start | bytes 786440 | tf_op jit(solution)/shard_map/ppermute | solution.py:33
  3.0 16.6 %collective-permute-start = (bf16[64,2048]{1,0:T(8,128)(2,1)}, bf16[64,2048]{1,0:T(8,128)(2,1)S(1)}, u32[]{:S(2)}, u32[]{:S(2)}) collective-permute-start(bf16[64,2048]{1,0:T(8,128)(2,1)} %bitcast.16), channel_id=1, source_target_pairs={{0,24},{1,25},{2,26},{3,27},{4,28},{5,29},{6,30},{7,31},{8,16},{9,... | collective-permute-start | bytes 786440 | tf_op jit(solution)/shard_map/ppermute | solution.py:33
  5.5 0.7 copy-start
  6.2 0.7 copy-start.2
  7.0 12.2 %collective-permute-start.1 = (bf16[64,128]{1,0:T(8,128)(2,1)S(1)}, bf16[64,128]{1,0:T(8,128)(2,1)S(1)}, u32[]{:S(2)}, u32[]{:S(2)}) collective-permute-start(bf16[64,128]{1,0:T(8,128)(2,1)S(1)} %shard_map.46.columns), channel_id=1, source_target_pairs={{0,8},{1,9},{2,10},{3,11},{4,12},{5,13},{6,14},{7,15},{8,0},{9,1},... | collective-permute-start | bytes 49160 | tf_op jit(solution)/shard_map/ppermute | solution.py:23
  7.1 1.9 %copy-start.3 = (bf16[1,1,768,2048]{3,2,1,0:T(8,128)(2,1)S(1)}, bf16[1,1,768,2048]{3,2,1,0:T(8,128)(2,1)}, u32[]{:S(2)}) copy-start(bf16[1,1,768,2048]{3,2,1,0:T(8,128)(2,1)} %param.7) | copy-start | bytes 9437188
  11.3 15.2 %collective-permute-start.6 = (bf16[64,2176]{1,0:T(8,128)(2,1)S(1)}, bf16[64,2176]{1,0:T(8,128)(2,1)S(1)}, u32[]{:S(2)}, u32[]{:S(2)}) collective-permute-start(bf16[64,2176]{1,0:T(8,128)(2,1)S(1)} %shard_map.48.refs_1_), channel_id=1, source_target_pairs={{0,2},{1,3},{2,0},{3,1},{4,6},{5,7},{6,4},{7,5},{8,10},{9,11},{10,... | collective-permute-start | bytes 835592 | tf_op jit(solution)/shard_map/ppermute | solution.py:23
  13.1 14.9 %collective-permute-start.9 = (bf16[64,2176]{1,0:T(8,128)(2,1)S(1)}, bf16[64,2176]{1,0:T(8,128)(2,1)S(1)}, u32[]{:S(2)}, u32[]{:S(2)}) collective-permute-start(bf16[64,2176]{1,0:T(8,128)(2,1)S(1)} %shard_map.48.refs_1_), channel_id=1, source_target_pairs={{0,4},{1,5},{2,6},{3,7},{4,0},{5,1},{6,2},{7,3},{8,12},{9,13},{10,... | collective-permute-start | bytes 835592 | tf_op jit(solution)/shard_map/ppermute | solution.py:23
  19.6 16.0 %collective-permute-start.8 = (bf16[64,2176]{1,0:T(8,128)(2,1)S(1)}, bf16[64,2176]{1,0:T(8,128)(2,1)S(1)}, u32[]{:S(2)}, u32[]{:S(2)}) collective-permute-start(bf16[64,2176]{1,0:T(8,128)(2,1)S(1)} %shard_map.49.refs_0_), channel_id=1, source_target_pairs={{0,4},{1,5},{2,6},{3,7},{4,0},{5,1},{6,2},{7,3},{8,12},{9,13},{10,... | collective-permute-start | bytes 835592 | tf_op jit(solution)/shard_map/ppermute | solution.py:23
  19.7 21.5 %collective-permute-start.4 = (bf16[64,2176]{1,0:T(8,128)(2,1)S(1)}, bf16[64,2176]{1,0:T(8,128)(2,1)S(1)}, u32[]{:S(2)}, u32[]{:S(2)}) collective-permute-start(bf16[64,2176]{1,0:T(8,128)(2,1)S(1)} %shard_map.49.refs_0_), channel_id=1, source_target_pairs={{0,2},{1,3},{2,0},{3,1},{4,6},{5,7},{6,4},{7,5},{8,10},{9,11},{10,... | collective-permute-start | bytes 835592 | tf_op jit(solution)/shard_map/ppermute | solution.py:23
  22.4 15.2 %collective-permute-start.5 = (bf16[2,64,768]{2,1,0:T(8,128)(2,1)S(1)}, bf16[2,64,768]{2,1,0:T(8,128)(2,1)S(1)}, u32[]{:S(2)}, u32[]{:S(2)}) collective-permute-start(bf16[2,64,768]{2,1,0:T(8,128)(2,1)S(1)} %shard_map.50), channel_id=1, source_target_pairs={{0,8},{1,9},{2,10},{3,11},{4,12},{5,13},{6,14},{7,15},{8,0},{9,1},... | collective-permute-start | bytes 589832 | tf_op jit(solution)/shard_map/ppermute | solution.py:23
  27.4 13.7 %collective-permute-start.7 = (bf16[2,64,768]{2,1,0:T(8,128)(2,1)S(1)}, bf16[2,64,768]{2,1,0:T(8,128)(2,1)S(1)}, u32[]{:S(2)}, u32[]{:S(2)}) collective-permute-start(bf16[2,64,768]{2,1,0:T(8,128)(2,1)S(1)} %get-tuple-element.30), channel_id=1, source_target_pairs={{0,2},{1,3},{2,0},{3,1},{4,6},{5,7},{6,4},{7,5},{8,10},{9,11},{10,... | collective-permute-start | bytes 589832 | tf_op jit(solution)/shard_map/ppermute | solution.py:23
  28.0 22.1 %collective-permute-start.10 = (bf16[64,2176]{1,0:T(8,128)(2,1)S(1)}, bf16[64,2176]{1,0:T(8,128)(2,1)S(1)}, u32[]{:S(2)}, u32[]{:S(2)}) collective-permute-start(bf16[64,2176]{1,0:T(8,128)(2,1)S(1)} %collective-permute-done.9.refs_0_), channel_id=1, source_target_pairs={{0,2},{1,3},{2,0},{3,1},{4,6},{5,7},{6,4},{7,5},{8,10},{9,11},{10,... | collective-permute-start | bytes 835592 | tf_op jit(solution)/shard_map/ppermute | solution.py:23
  35.6 9.7 %collective-permute-start.11 = (bf16[64,2176]{1,0:T(8,128)(2,1)S(1)}, bf16[64,2176]{1,0:T(8,128)(2,1)S(1)}, u32[]{:S(2)}, u32[]{:S(2)}) collective-permute-start(bf16[64,2176]{1,0:T(8,128)(2,1)S(1)} %collective-permute-done.8.refs_0_), channel_id=1, source_target_pairs={{0,2},{1,3},{2,0},{3,1},{4,6},{5,7},{6,4},{7,5},{8,10},{9,11},{10,... | collective-permute-start | bytes 835592 | tf_op jit(solution)/shard_map/ppermute | solution.py:23
  37.7 19.5 %collective-permute-start.15 = (bf16[2,64,768]{2,1,0:T(8,128)(2,1)S(1)}, bf16[2,64,768]{2,1,0:T(8,128)(2,1)S(1)}, u32[]{:S(2)}, u32[]{:S(2)}) collective-permute-start(bf16[2,64,768]{2,1,0:T(8,128)(2,1)S(1)} %shard_map.52), channel_id=1, source_target_pairs={{0,12},{1,13},{2,14},{3,15},{4,8},{5,9},{6,10},{7,11},{8,4},{9,5},... | collective-permute-start | bytes 589832 | tf_op jit(solution)/shard_map/ppermute | solution.py:23
  42.4 20.1 %collective-permute-start.14 = (bf16[2,64,768]{2,1,0:T(8,128)(2,1)S(1)}, bf16[2,64,768]{2,1,0:T(8,128)(2,1)S(1)}, u32[]{:S(2)}, u32[]{:S(2)}) collective-permute-start(bf16[2,64,768]{2,1,0:T(8,128)(2,1)S(1)} %shard_map.53), channel_id=1, source_target_pairs={{0,10},{1,11},{2,8},{3,9},{4,14},{5,15},{6,12},{7,13},{8,2},{9,3},... | collective-permute-start | bytes 589832 | tf_op jit(solution)/shard_map/ppermute | solution.py:23
  46.5 16.0 %copy-start.1 = (s32[1,64,8]{1,2,0:T(8,128)S(1)}, s32[1,64,8]{1,2,0:T(8,128)}, u32[]{:S(2)}) copy-start(s32[1,64,8]{1,2,0:T(8,128)} %param.5) | copy-start | bytes 6148
  46.5 16.0 %collective-permute-start.16 = (bf16[2,64,768]{2,1,0:T(8,128)(2,1)S(1)}, bf16[2,64,768]{2,1,0:T(8,128)(2,1)S(1)}, u32[]{:S(2)}, u32[]{:S(2)}) collective-permute-start(bf16[2,64,768]{2,1,0:T(8,128)(2,1)S(1)} %shard_map.54), channel_id=1, source_target_pairs={{0,14},{1,15},{2,12},{3,13},{4,10},{5,11},{6,8},{7,9},{8,6},{9,7},... | collective-permute-start | bytes 589832 | tf_op jit(solution)/shard_map/ppermute | solution.py:23
  51.0 14.1 %collective-permute-start.12 = (bf16[2,64,768]{2,1,0:T(8,128)(2,1)S(1)}, bf16[2,64,768]{2,1,0:T(8,128)(2,1)S(1)}, u32[]{:S(2)}, u32[]{:S(2)}) collective-permute-start(bf16[2,64,768]{2,1,0:T(8,128)(2,1)S(1)} %get-tuple-element.37), channel_id=1, source_target_pairs={{0,4},{1,5},{2,6},{3,7},{4,0},{5,1},{6,2},{7,3},{8,12},{9,13},{10,... | collective-permute-start | bytes 589832 | tf_op jit(solution)/shard_map/ppermute | solution.py:23
  57.1 10.3 %collective-permute-start.13 = (bf16[2,64,768]{2,1,0:T(8,128)(2,1)S(1)}, bf16[2,64,768]{2,1,0:T(8,128)(2,1)S(1)}, u32[]{:S(2)}, u32[]{:S(2)}) collective-permute-start(bf16[2,64,768]{2,1,0:T(8,128)(2,1)S(1)} %get-tuple-element.38), channel_id=1, source_target_pairs={{0,6},{1,7},{2,4},{3,5},{4,2},{5,3},{6,0},{7,1},{8,14},{9,15},{10,... | collective-permute-start | bytes 589832 | tf_op jit(solution)/shard_map/ppermute | solution.py:23

commit v22 on v21

--- a/solution.py
+++ b/solution.py
@@ -164,6 +164,7 @@
 
     far = send_across(upstream, owners, Z_FAR)
     rows = send_across(upstream, owners, 0)
+    far = send_across(upstream, owners, Z_FAR)
     other_mat = send(weight_mat, owners, 0, 1)
     columns = gate_columns(route_ids.T, route_gates.T)
     far_columns = send(columns, owners, Z_FAR)
@@ -179,24 +180,22 @@
     (out_far,) = work(far)
     back_far = send(out_far, owners, Z_FAR)
     side, _ = tie((side, out_far))
-    out_side, out_own = work(side, rows)
+    near, far_side, side = tie((near, far_side, side))
+    near_side = send(near, owners, X)
+    out_far_side, out_side = work(far_side, side)
+    back_far_side = send(out_far_side, owners, X ^ Z_FAR)
     back_side = send(out_side, owners, X)
-    near, _ = tie((near, out_side))
-    near_side = send(near, owners, X)
-    cross, _ = tie((cross, near))
+    cross, _ = tie((cross, out_far_side))
     cross_side = send(cross, owners, X)
     (out_cross,) = work(cross)
     back_cross = send(out_cross, owners, Z_NEAR ^ Z_FAR)
-    far_side, back_far, back_side, _ = tie((far_side, back_far, back_side, out_cross))
-    (out_far_side,) = work(far_side)
-    back_far_side = send(out_far_side, owners, X ^ Z_FAR)
-    cross_side, _ = tie((cross_side, out_far_side))
+    near_side, back_far, back_side, _ = tie((near_side, back_far, back_side, out_cross))
+    out_near, out_near_side, out_own = work(near, near_side, rows)
+    back_near_side = send(out_near_side, owners, X ^ Z_NEAR)
+    back_near = send(out_near, owners, Z_NEAR)
+    cross_side, _ = tie((cross_side, out_near_side))
     (out_cross_side,) = work(cross_side)
     back_cross_side = send(out_cross_side, owners, X ^ Z_NEAR ^ Z_FAR)
-    near_side, _ = tie((near_side, out_cross_side))
-    out_near, out_near_side = work(near, near_side)
-    back_near_side = send(out_near_side, owners, X ^ Z_NEAR)
-    back_near = send(out_near, owners, Z_NEAR)
     far_parts = {
         0: out_own,
         Z_FAR: back_far,

time: 68.9 us -> 78.1 us (1.13)
  waiting for transfers between devices: 19.7 us -> 27.1 us
  starting transfers between devices: 35.3 us -> 37.9 us
  Pallas kernels: 10.3 us -> 9.5 us
    ppermute x15, waiting for transfers between devices: 18.7 us -> 26.1 us  [send(): return lax.ppermute(block, 'expert', route)]
    ppermute x15, starting transfers between devices: 30.3 us -> 32.8 us  [send(): return lax.ppermute(block, 'expert', route)]
    pallas_call x6 -> x5, Pallas kernels: 6.73 us -> 5.94 us  [products(): pl.pallas_call(functools.partial(products_kernel, len(pieces)), out_shape...]
  transfers between devices with their start and end apart: 17 -> 17, of which waited for: 7 -> 10; matrix products, arithmetic and copies ran while one was open for 0% -> 0% of each run, Pallas kernels for 13% -> 11%
where the time goes in v22:
time: 78.1 us; the launch traced here: 77.9 us
  starting transfers between devices  37.9 us (49%)
  waiting for transfers between devices  27.1 us (35%)
  Pallas kernels  9.5 us (12%)
  local copies, waits for them, and re-layouts  3.26 us (4%)
    ppermute x15, starting transfers between devices, send(): return lax.ppermute(block, 'expert', route)  32.8 us
    ppermute x15, waiting for transfers between devices, send(): return lax.ppermute(block, 'expert', route)  26.1 us
    pallas_call x5, Pallas kernels, products(): pl.pallas_call(functools.partial(products_kernel, len(pieces)), out_shape...  5.94 us
    ppermute x2, starting transfers between devices, send_across(): return lax.ppermute(block, ('pipe', 'expert'), route)  5.05 us
    unnamed x8, local copies, waits for them, and re-layouts  3.26 us
    pallas_call x2, Pallas kernels, pick_routes(): pl.pallas_call(functools.partial(pick_kernel, flips), out_shape=jax.Shape...  1.74 us
    pallas_call x1, Pallas kernels, turned(): pl.pallas_call(turn_kernel, out_shape=jax.ShapeDtypeStruct((depth, CORES...  1.67 us
  transfers between devices with their start and end apart: 17, of which 10 were waited for; matrix products, arithmetic and copies ran while one was open for 0% of the time, Pallas kernels for 11%

profile of v22, /device:TPU:0, one launch (start us, length us, event | category | flops | bytes accessed | tf_op | source)
XLA Modules:
  0.0 77.9 jit_solution(10640690831894206677)
XLA Ops:
  0.0 0.5 collective-permute-start.1
  0.5 2.5 %collective-permute-start = (bf16[64,2048]{1,0:T(8,128)(2,1)}, bf16[64,2048]{1,0:T(8,128)(2,1)S(1)}, u32[]{:S(2)}, u32[]{:S(2)}) collective-permute-start(bf16[64,2048]{1,0:T(8,128)(2,1)} %bitcast.15), channel_id=1, source_target_pairs={{0,16},{1,17},{2,18},{3,19},{4,20},{5,21},{6,22},{7,23},{8,24},{9,... | collective-permute-start | bytes 786440 | tf_op jit(solution)/shard_map/ppermute | solution.py:33
  3.0 2.5 %collective-permute-start.3 = (bf16[64,2048]{1,0:T(8,128)(2,1)}, bf16[64,2048]{1,0:T(8,128)(2,1)S(1)}, u32[]{:S(2)}, u32[]{:S(2)}) collective-permute-start(bf16[64,2048]{1,0:T(8,128)(2,1)} %bitcast.16), channel_id=1, source_target_pairs={{0,24},{1,25},{2,26},{3,27},{4,28},{5,29},{6,30},{7,31},{8,16},{9,... | collective-permute-start | bytes 786440 | tf_op jit(solution)/shard_map/ppermute | solution.py:33
  5.5 0.0 copy-start
  5.5 0.7 copy-done
  6.2 0.0 copy-start.2
  6.2 0.7 copy-done.2
  6.9 0.1 shard_map.46.columns
  7.0 0.1 collective-permute-start.4
  7.1 0.0 collective-permute-done.1.other
  7.1 0.0 copy-start.3
  7.1 1.9 %copy-done.3 = bf16[1,1,768,2048]{3,2,1,0:T(8,128)(2,1)S(1)} copy-done((bf16[1,1,768,2048]{3,2,1,0:T(8,128)(2,1)S(1)}, bf16[1,1,768,2048]{3,2,1,0:T(8,128)(2,1)}, u32[]{:S(2)}) %copy-start.3) | copy-done | bytes 3145752
  9.0 1.7 %shard_map.47.weights = bf16[2048,1536]{1,0:T(8,128)(2,1)S(1)} custom-call(bf16[768,2048]{1,0:T(8,128)(2,1)S(1)} %bitcast.14, bf16[768,2048]{1,0:T(8,128)(2,1)S(1)} %collective-permute-done.1.other), custom_call_target="tpu_custom_call" | custom-call | flops 12884901888 | tf_op jit(solution)/shard_map/pallas_call | solution.py:77
  10.7 0.6 collective-permute-done.rows
  11.3 1.8 %collective-permute-start.6 = (bf16[64,2176]{1,0:T(8,128)(2,1)S(1)}, bf16[64,2176]{1,0:T(8,128)(2,1)S(1)}, u32[]{:S(2)}, u32[]{:S(2)}) collective-permute-start(bf16[64,2176]{1,0:T(8,128)(2,1)S(1)} %shard_map.48.refs_2_), channel_id=1, source_target_pairs={{0,2},{1,3},{2,0},{3,1},{4,6},{5,7},{6,4},{7,5},{8,10},{9,11},{10,... | collective-permute-start | bytes 835592 | tf_op jit(solution)/shard_map/ppermute | solution.py:23
  13.1 6.1 %collective-permute-start.2 = (bf16[64,2176]{1,0:T(8,128)(2,1)S(1)}, bf16[64,2176]{1,0:T(8,128)(2,1)S(1)}, u32[]{:S(2)}, u32[]{:S(2)}) collective-permute-start(bf16[64,2176]{1,0:T(8,128)(2,1)S(1)} %shard_map.48.refs_2_), channel_id=1, source_target_pairs={{0,4},{1,5},{2,6},{3,7},{4,0},{5,1},{6,2},{7,3},{8,12},{9,13},{10,... | collective-permute-start | bytes 835592 | tf_op jit(solution)/shard_map/ppermute | solution.py:23
  19.2 0.0 collective-permute-done.4.columns
  19.2 0.4 collective-permute-done.3.rows
  19.6 1.6 %collective-permute-start.5 = (bf16[64,2176]{1,0:T(8,128)(2,1)S(1)}, bf16[64,2176]{1,0:T(8,128)(2,1)S(1)}, u32[]{:S(2)}, u32[]{:S(2)}) collective-permute-start(bf16[64,2176]{1,0:T(8,128)(2,1)S(1)} %shard_map.49.refs_0_), channel_id=1, source_target_pairs={{0,2},{1,3},{2,0},{3,1},{4,6},{5,7},{6,4},{7,5},{8,10},{9,11},{10,... | collective-permute-start | bytes 835592 | tf_op jit(solution)/shard_map/ppermute | solution.py:23
  21.2 0.0 collective-permute-start.10
  21.2 1.2 %shard_map.50 = bf16[2,64,768]{2,1,0:T(8,128)(2,1)S(1)} custom-call(bf16[2048,1536]{1,0:T(8,128)(2,1)S(1)} %shard_map.47.weights, bf16[64,2176]{1,0:T(8,128)(2,1)S(1)} %shard_map.49.refs_0_), custom_call_target="tpu_custom_call" | custom-call | flops 4026531840 | bytes 6750208 | tf_op jit(solution)/shard_map/pallas_call | solution.py:109
  22.4 4.1 %collective-permute-start.8 = (bf16[2,64,768]{2,1,0:T(8,128)(2,1)S(1)}, bf16[2,64,768]{2,1,0:T(8,128)(2,1)S(1)}, u32[]{:S(2)}, u32[]{:S(2)}) collective-permute-start(bf16[2,64,768]{2,1,0:T(8,128)(2,1)S(1)} %shard_map.50), channel_id=1, source_target_pairs={{0,8},{1,9},{2,10},{3,11},{4,12},{5,13},{6,14},{7,15},{8,0},{9,1},... | collective-permute-start | bytes 589832 | tf_op jit(solution)/shard_map/ppermute | solution.py:23
  26.4 0.0 collective-permute-done.6.refs_1_
  26.5 1.0 %collective-permute-done.5.refs_0_ = bf16[64,2176]{1,0:T(8,128)(2,1)S(1)} collective-permute-done((bf16[64,2176]{1,0:T(8,128)(2,1)S(1)}, bf16[64,2176]{1,0:T(8,128)(2,1)S(1)}, u32[]{:S(2)}, u32[]{:S(2)}) %collective-permute-start.5) | collective-permute-done | bytes 278560 | tf_op jit(solution)/shard_map/ppermute | solution.py:23
  27.4 0.0 collective-permute-done.2.refs_0_
  27.4 1.0 %shard_map.51 = (bf16[2,64,768]{2,1,0:T(8,128)(2,1)S(1)}, bf16[2,64,768]{2,1,0:T(8,128)(2,1)S(1)}) custom-call(bf16[2048,1536]{1,0:T(8,128)(2,1)S(1)} %shard_map.47.weights, bf16[64,2176]{1,0:T(8,128)(2,1)S(1)} %collective-permute-done.5.refs_0_, bf16[64,2176]{1,0:T(8,128)(2,1)S(1)} %collective-permute-done.6.refs_1_), custom_call_target="tpu_custom_call" | custom-call | flops 8053063680 | bytes 7208960 | tf_op jit(solution)/shard_map/pallas_call | solution.py:109
  28.4 6.5 %collective-permute-start.13 = (bf16[2,64,768]{2,1,0:T(8,128)(2,1)S(1)}, bf16[2,64,768]{2,1,0:T(8,128)(2,1)S(1)}, u32[]{:S(2)}, u32[]{:S(2)}) collective-permute-start(bf16[2,64,768]{2,1,0:T(8,128)(2,1)S(1)} %get-tuple-element.35), channel_id=1, source_target_pairs={{0,10},{1,11},{2,8},{3,9},{4,14},{5,15},{6,12},{7,13},{8,2},{9,3},... | collective-permute-start | bytes 589832 | tf_op jit(solution)/shard_map/ppermute | solution.py:23
  34.9 1.5 %collective-permute-done.10.refs_0_ = bf16[64,2176]{1,0:T(8,128)(2,1)S(1)} collective-permute-done((bf16[64,2176]{1,0:T(8,128)(2,1)S(1)}, bf16[64,2176]{1,0:T(8,128)(2,1)S(1)}, u32[]{:S(2)}, u32[]{:S(2)}) %collective-permute-start.10) | collective-permute-done | bytes 278560 | tf_op jit(solution)/shard_map/ppermute | solution.py:23
  36.4 0.4 collective-permute-start.9
  36.8 1.7 %collective-permute-start.7 = (bf16[64,2176]{1,0:T(8,128)(2,1)S(1)}, bf16[64,2176]{1,0:T(8,128)(2,1)S(1)}, u32[]{:S(2)}, u32[]{:S(2)}) collective-permute-start(bf16[64,2176]{1,0:T(8,128)(2,1)S(1)} %collective-permute-done.2.refs_0_), channel_id=1, source_target_pairs={{0,2},{1,3},{2,0},{3,1},{4,6},{5,7},{6,4},{7,5},{8,10},{9,11},{10,... | collective-permute-start | bytes 835592 | tf_op jit(solution)/shard_map/ppermute | solution.py:23
  38.5 0.4 collective-permute-start.15
  38.9 1.2 %shard_map.52 = bf16[2,64,768]{2,1,0:T(8,128)(2,1)S(1)} custom-call(bf16[2048,1536]{1,0:T(8,128)(2,1)S(1)} %shard_map.47.weights, bf16[64,2176]{1,0:T(8,128)(2,1)S(1)} %collective-permute-done.10.refs_0_), custom_call_target="tpu_custom_call" | custom-call | flops 4026531840 | bytes 6750208 | tf_op jit(solution)/shard_map/pallas_call | solution.py:109
  40.0 0.0 collective-permute-done.8.refs_1_
  40.1 3.4 %collective-permute-start.14 = (bf16[2,64,768]{2,1,0:T(8,128)(2,1)S(1)}, bf16[2,64,768]{2,1,0:T(8,128)(2,1)S(1)}, u32[]{:S(2)}, u32[]{:S(2)}) collective-permute-start(bf16[2,64,768]{2,1,0:T(8,128)(2,1)S(1)} %shard_map.52), channel_id=1, source_target_pairs={{0,12},{1,13},{2,14},{3,15},{4,8},{5,9},{6,10},{7,11},{8,4},{9,5},... | collective-permute-start | bytes 589832 | tf_op jit(solution)/shard_map/ppermute | solution.py:23
  43.5 2.2 %collective-permute-done.9.refs_0_ = bf16[2,64,768]{2,1,0:T(8,128)(2,1)S(1)} collective-permute-done((bf16[2,64,768]{2,1,0:T(8,128)(2,1)S(1)}, bf16[2,64,768]{2,1,0:T(8,128)(2,1)S(1)}, u32[]{:S(2)}, u32[]{:S(2)}) %collective-permute-start.9) | collective-permute-done | bytes 196640 | tf_op jit(solution)/shard_map/ppermute | solution.py:23
  45.7 8.4 %collective-permute-done.7.refs_1_ = bf16[64,2176]{1,0:T(8,128)(2,1)S(1)} collective-permute-done((bf16[64,2176]{1,0:T(8,128)(2,1)S(1)}, bf16[64,2176]{1,0:T(8,128)(2,1)S(1)}, u32[]{:S(2)}, u32[]{:S(2)}) %collective-permute-start.7) | collective-permute-done | bytes 278560 | tf_op jit(solution)/shard_map/ppermute | solution.py:23
  54.1 1.4 %shard_map.53 = (bf16[2,64,768]{2,1,0:T(8,128)(2,1)S(1)}, bf16[2,64,768]{2,1,0:T(8,128)(2,1)S(1)}, bf16[2,64,768]{2,1,0:T(8,128)(2,1)S(1)}) custom-call(bf16[2048,1536]{1,0:T(8,128)(2,1)S(1)} %shard_map.47.weights, bf16[64,2176]{1,0:T(8,128)(2,1)S(1)} %collective-permute-done.2.refs_0_, bf16[64,2176]{1,0:T(8,128)(2,1)S(1)} %collective-permute-done.7.refs_1_, ...), custom_call_target="tpu_custom_call" | custom-call | flops 12079595520 | bytes 7667712 | tf_op jit(solution)/shard_map/pallas_call | solution.py:109
  55.5 2.2 %collective-permute-done.15.refs_0_ = bf16[64,2176]{1,0:T(8,128)(2,1)S(1)} collective-permute-done((bf16[64,2176]{1,0:T(8,128)(2,1)S(1)}, bf16[64,2176]{1,0:T(8,128)(2,1)S(1)}, u32[]{:S(2)}, u32[]{:S(2)}) %collective-permute-start.15) | collective-permute-done | bytes 278560 | tf_op jit(solution)/shard_map/ppermute | solution.py:23
  57.7 0.0 copy-start.1
  57.7 1.2 %shard_map.54 = bf16[2,64,768]{2,1,0:T(8,128)(2,1)S(1)} custom-call(bf16[2048,1536]{1,0:T(8,128)(2,1)S(1)} %shard_map.47.weights, bf16[64,2176]{1,0:T(8,128)(2,1)S(1)} %collective-permute-done.15.refs_0_), custom_call_target="tpu_custom_call" | custom-call | flops 4026531840 | bytes 6750208 | tf_op jit(solution)/shard_map/pallas_call | solution.py:109
  58.9 4.9 %collective-permute-start.16 = (bf16[2,64,768]{2,1,0:T(8,128)(2,1)S(1)}, bf16[2,64,768]{2,1,0:T(8,128)(2,1)S(1)}, u32[]{:S(2)}, u32[]{:S(2)}) collective-permute-start(bf16[2,64,768]{2,1,0:T(8,128)(2,1)S(1)} %shard_map.54), channel_id=1, source_target_pairs={{0,14},{1,15},{2,12},{3,13},{4,10},{5,11},{6,8},{7,9},{8,6},{9,7},... | collective-permute-start | bytes 589832 | tf_op jit(solution)/shard_map/ppermute | solution.py:23
  63.8 0.0 collective-permute-start.11
  63.8 1.6 %collective-permute-start.12 = (bf16[2,64,768]{2,1,0:T(8,128)(2,1)S(1)}, bf16[2,64,768]{2,1,0:T(8,128)(2,1)S(1)}, u32[]{:S(2)}, u32[]{:S(2)}) collective-permute-start(bf16[2,64,768]{2,1,0:T(8,128)(2,1)S(1)} %get-tuple-element.41), channel_id=1, source_target_pairs={{0,6},{1,7},{2,4},{3,5},{4,2},{5,3},{6,0},{7,1},{8,14},{9,15},{10,... | collective-permute-start | bytes 589832 | tf_op jit(solution)/shard_map/ppermute | solution.py:23
  65.3 0.0 collective-permute-done.14.refs_3_
  65.3 0.0 collective-permute-done.13.refs_2_
  65.3 4.2 %collective-permute-done.16.refs_4_ = bf16[2,64,768]{2,1,0:T(8,128)(2,1)S(1)} collective-permute-done((bf16[2,64,768]{2,1,0:T(8,128)(2,1)S(1)}, bf16[2,64,768]{2,1,0:T(8,128)(2,1)S(1)}, u32[]{:S(2)}, u32[]{:S(2)}) %collective-permute-start.16) | collective-permute-done | bytes 196640 | tf_op jit(solution)/shard_map/ppermute | solution.py:23
  69.6 0.0 copy-done.1
  69.6 0.4 shard_map.55.refs_3_
  70.0 3.3 %collective-permute-done.11.refs_1_ = bf16[2,64,768]{2,1,0:T(8,128)(2,1)S(1)} collective-permute-done((bf16[2,64,768]{2,1,0:T(8,128)(2,1)S(1)}, bf16[2,64,768]{2,1,0:T(8,128)(2,1)S(1)}, u32[]{:S(2)}, u32[]{:S(2)}) %collective-permute-start.11) | collective-permute-done | bytes 196640 | tf_op jit(solution)/shard_map/ppermute | solution.py:23
  73.3 3.2 %collective-permute-done.12.refs_2_ = bf16[2,64,768]{2,1,0:T(8,128)(2,1)S(1)} collective-permute-done((bf16[2,64,768]{2,1,0:T(8,128)(2,1)S(1)}, bf16[2,64,768]{2,1,0:T(8,128)(2,1)S(1)}, u32[]{:S(2)}, u32[]{:S(2)}) %collective-permute-start.12) | collective-permute-done | bytes 196640 | tf_op jit(solution)/shard_map/ppermute | solution.py:23
  76.6 1.3 %shard_map.56 = bf16[512,768]{1,0:T(8,128)(2,1)} custom-call(s32[8,64]{1,0:T(8,128)S(1)} %bitcast.11, bf16[2,64,768]{2,1,0:T(8,128)(2,1)S(1)} %collective-permute-done.9.refs_0_, bf16[2,64,768]{2,1,0:T(8,128)(2,1)S(1)} %collective-permute-done.11.refs_1_, bf16[2,64,768]{2,1,0:T(8,128)(2,1)S(1)} %collective-permute-done.12.refs_2_, ...), custom_call_target="tpu_custom_call" | custom-call | tf_op jit(solution)/shard_map/pallas_call | solution.py:150
  (2 shorter events, 0.0 us)
Async XLA Ops:
  0.0 7.1 %collective-permute-start.1 = (bf16[768,2048]{1,0:T(8,128)(2,1)}, bf16[768,2048]{1,0:T(8,128)(2,1)S(1)}, u32[]{:S(2)}, u32[]{:S(2)}) collective-permute-start(bf16[768,2048]{1,0:T(8,128)(2,1)} %bitcast.13), channel_id=1, source_target_pairs={{0,1},{1,0},{2,3},{3,2},{4,5},{5,4},{6,7},{7,6},{8,9},{9,8},{10,11... | collective-permute-start | bytes 9437192 | tf_op jit(solution)/shard_map/ppermute | solution.py:23
  0.5 10.8 %collective-permute-start = (bf16[64,2048]{1,0:T(8,128)(2,1)}, bf16[64,2048]{1,0:T(8,128)(2,1)S(1)}, u32[]{:S(2)}, u32[]{:S(2)}) collective-permute-start(bf16[64,2048]{1,0:T(8,128)(2,1)} %bitcast.15), channel_id=1, source_target_pairs={{0,16},{1,17},{2,18},{3,19},{4,20},{5,21},{6,22},{7,23},{8,24},{9,... | collective-permute-start | bytes 786440 | tf_op jit(solution)/shard_map/ppermute | solution.py:33
  3.0 16.6 %collective-permute-start.3 = (bf16[64,2048]{1,0:T(8,128)(2,1)}, bf16[64,2048]{1,0:T(8,128)(2,1)S(1)}, u32[]{:S(2)}, u32[]{:S(2)}) collective-permute-start(bf16[64,2048]{1,0:T(8,128)(2,1)} %bitcast.16), channel_id=1, source_target_pairs={{0,24},{1,25},{2,26},{3,27},{4,28},{5,29},{6,30},{7,31},{8,16},{9,... | collective-permute-start | bytes 786440 | tf_op jit(solution)/shard_map/ppermute | solution.py:33
  5.5 0.7 copy-start
  6.2 0.7 copy-start.2
  7.0 12.2 %collective-permute-start.4 = (bf16[64,128]{1,0:T(8,128)(2,1)S(1)}, bf16[64,128]{1,0:T(8,128)(2,1)S(1)}, u32[]{:S(2)}, u32[]{:S(2)}) collective-permute-start(bf16[64,128]{1,0:T(8,128)(2,1)S(1)} %shard_map.46.columns), channel_id=1, source_target_pairs={{0,8},{1,9},{2,10},{3,11},{4,12},{5,13},{6,14},{7,15},{8,0},{9,1},... | collective-permute-start | bytes 49160 | tf_op jit(solution)/shard_map/ppermute | solution.py:23
  7.1 1.9 %copy-start.3 = (bf16[1,1,768,2048]{3,2,1,0:T(8,128)(2,1)S(1)}, bf16[1,1,768,2048]{3,2,1,0:T(8,128)(2,1)}, u32[]{:S(2)}) copy-start(bf16[1,1,768,2048]{3,2,1,0:T(8,128)(2,1)} %param.7) | copy-start | bytes 9437188
  11.3 15.2 %collective-permute-start.6 = (bf16[64,2176]{1,0:T(8,128)(2,1)S(1)}, bf16[64,2176]{1,0:T(8,128)(2,1)S(1)}, u32[]{:S(2)}, u32[]{:S(2)}) collective-permute-start(bf16[64,2176]{1,0:T(8,128)(2,1)S(1)} %shard_map.48.refs_2_), channel_id=1, source_target_pairs={{0,2},{1,3},{2,0},{3,1},{4,6},{5,7},{6,4},{7,5},{8,10},{9,11},{10,... | collective-permute-start | bytes 835592 | tf_op jit(solution)/shard_map/ppermute | solution.py:23
  13.1 14.4 %collective-permute-start.2 = (bf16[64,2176]{1,0:T(8,128)(2,1)S(1)}, bf16[64,2176]{1,0:T(8,128)(2,1)S(1)}, u32[]{:S(2)}, u32[]{:S(2)}) collective-permute-start(bf16[64,2176]{1,0:T(8,128)(2,1)S(1)} %shard_map.48.refs_2_), channel_id=1, source_target_pairs={{0,4},{1,5},{2,6},{3,7},{4,0},{5,1},{6,2},{7,3},{8,12},{9,13},{10,... | collective-permute-start | bytes 835592 | tf_op jit(solution)/shard_map/ppermute | solution.py:23
  19.6 7.9 %collective-permute-start.5 = (bf16[64,2176]{1,0:T(8,128)(2,1)S(1)}, bf16[64,2176]{1,0:T(8,128)(2,1)S(1)}, u32[]{:S(2)}, u32[]{:S(2)}) collective-permute-start(bf16[64,2176]{1,0:T(8,128)(2,1)S(1)} %shard_map.49.refs_0_), channel_id=1, source_target_pairs={{0,2},{1,3},{2,0},{3,1},{4,6},{5,7},{6,4},{7,5},{8,10},{9,11},{10,... | collective-permute-start | bytes 835592 | tf_op jit(solution)/shard_map/ppermute | solution.py:23
  21.2 15.3 %collective-permute-start.10 = (bf16[64,2176]{1,0:T(8,128)(2,1)S(1)}, bf16[64,2176]{1,0:T(8,128)(2,1)S(1)}, u32[]{:S(2)}, u32[]{:S(2)}) collective-permute-start(bf16[64,2176]{1,0:T(8,128)(2,1)S(1)} %shard_map.49.refs_0_), channel_id=1, source_target_pairs={{0,4},{1,5},{2,6},{3,7},{4,0},{5,1},{6,2},{7,3},{8,12},{9,13},{10,... | collective-permute-start | bytes 835592 | tf_op jit(solution)/shard_map/ppermute | solution.py:23
  22.4 17.7 %collective-permute-start.8 = (bf16[2,64,768]{2,1,0:T(8,128)(2,1)S(1)}, bf16[2,64,768]{2,1,0:T(8,128)(2,1)S(1)}, u32[]{:S(2)}, u32[]{:S(2)}) collective-permute-start(bf16[2,64,768]{2,1,0:T(8,128)(2,1)S(1)} %shard_map.50), channel_id=1, source_target_pairs={{0,8},{1,9},{2,10},{3,11},{4,12},{5,13},{6,14},{7,15},{8,0},{9,1},... | collective-permute-start | bytes 589832 | tf_op jit(solution)/shard_map/ppermute | solution.py:23
  28.4 36.9 %collective-permute-start.13 = (bf16[2,64,768]{2,1,0:T(8,128)(2,1)S(1)}, bf16[2,64,768]{2,1,0:T(8,128)(2,1)S(1)}, u32[]{:S(2)}, u32[]{:S(2)}) collective-permute-start(bf16[2,64,768]{2,1,0:T(8,128)(2,1)S(1)} %get-tuple-element.35), channel_id=1, source_target_pairs={{0,10},{1,11},{2,8},{3,9},{4,14},{5,15},{6,12},{7,13},{8,2},{9,3},... | collective-permute-start | bytes 589832 | tf_op jit(solution)/shard_map/ppermute | solution.py:23
  36.4 9.3 %collective-permute-start.9 = (bf16[2,64,768]{2,1,0:T(8,128)(2,1)S(1)}, bf16[2,64,768]{2,1,0:T(8,128)(2,1)S(1)}, u32[]{:S(2)}, u32[]{:S(2)}) collective-permute-start(bf16[2,64,768]{2,1,0:T(8,128)(2,1)S(1)} %get-tuple-element.34), channel_id=1, source_target_pairs={{0,2},{1,3},{2,0},{3,1},{4,6},{5,7},{6,4},{7,5},{8,10},{9,11},{10,... | collective-permute-start | bytes 589832 | tf_op jit(solution)/shard_map/ppermute | solution.py:23
  36.8 17.3 %collective-permute-start.7 = (bf16[64,2176]{1,0:T(8,128)(2,1)S(1)}, bf16[64,2176]{1,0:T(8,128)(2,1)S(1)}, u32[]{:S(2)}, u32[]{:S(2)}) collective-permute-start(bf16[64,2176]{1,0:T(8,128)(2,1)S(1)} %collective-permute-done.2.refs_0_), channel_id=1, source_target_pairs={{0,2},{1,3},{2,0},{3,1},{4,6},{5,7},{6,4},{7,5},{8,10},{9,11},{10,... | collective-permute-start | bytes 835592 | tf_op jit(solution)/shard_map/ppermute | solution.py:23
  38.5 19.2 %collective-permute-start.15 = (bf16[64,2176]{1,0:T(8,128)(2,1)S(1)}, bf16[64,2176]{1,0:T(8,128)(2,1)S(1)}, u32[]{:S(2)}, u32[]{:S(2)}) collective-permute-start(bf16[64,2176]{1,0:T(8,128)(2,1)S(1)} %collective-permute-done.10.refs_0_), channel_id=1, source_target_pairs={{0,2},{1,3},{2,0},{3,1},{4,6},{5,7},{6,4},{7,5},{8,10},{9,11},{10,... | collective-permute-start | bytes 835592 | tf_op jit(solution)/shard_map/ppermute | solution.py:23
  40.1 25.3 %collective-permute-start.14 = (bf16[2,64,768]{2,1,0:T(8,128)(2,1)S(1)}, bf16[2,64,768]{2,1,0:T(8,128)(2,1)S(1)}, u32[]{:S(2)}, u32[]{:S(2)}) collective-permute-start(bf16[2,64,768]{2,1,0:T(8,128)(2,1)S(1)} %shard_map.52), channel_id=1, source_target_pairs={{0,12},{1,13},{2,14},{3,15},{4,8},{5,9},{6,10},{7,11},{8,4},{9,5},... | collective-permute-start | bytes 589832 | tf_op jit(solution)/shard_map/ppermute | solution.py:23
  57.7 11.9 %copy-start.1 = (s32[1,64,8]{1,2,0:T(8,128)S(1)}, s32[1,64,8]{1,2,0:T(8,128)}, u32[]{:S(2)}) copy-start(s32[1,64,8]{1,2,0:T(8,128)} %param.5) | copy-start | bytes 6148
  58.9 10.7 %collective-permute-start.16 = (bf16[2,64,768]{2,1,0:T(8,128)(2,1)S(1)}, bf16[2,64,768]{2,1,0:T(8,128)(2,1)S(1)}, u32[]{:S(2)}, u32[]{:S(2)}) collective-permute-start(bf16[2,64,768]{2,1,0:T(8,128)(2,1)S(1)} %shard_map.54), channel_id=1, source_target_pairs={{0,14},{1,15},{2,12},{3,13},{4,10},{5,11},{6,8},{7,9},{8,6},{9,7},... | collective-permute-start | bytes 589832 | tf_op jit(solution)/shard_map/ppermute | solution.py:23
  63.8 9.6 %collective-permute-start.11 = (bf16[2,64,768]{2,1,0:T(8,128)(2,1)S(1)}, bf16[2,64,768]{2,1,0:T(8,128)(2,1)S(1)}, u32[]{:S(2)}, u32[]{:S(2)}) collective-permute-start(bf16[2,64,768]{2,1,0:T(8,128)(2,1)S(1)} %get-tuple-element.40), channel_id=1, source_target_pairs={{0,4},{1,5},{2,6},{3,7},{4,0},{5,1},{6,2},{7,3},{8,12},{9,13},{10,... | collective-permute-start | bytes 589832 | tf_op jit(solution)/shard_map/ppermute | solution.py:23
  63.8 12.8 %collective-permute-start.12 = (bf16[2,64,768]{2,1,0:T(8,128)(2,1)S(1)}, bf16[2,64,768]{2,1,0:T(8,128)(2,1)S(1)}, u32[]{:S(2)}, u32[]{:S(2)}) collective-permute-start(bf16[2,64,768]{2,1,0:T(8,128)(2,1)S(1)} %get-tuple-element.41), channel_id=1, source_target_pairs={{0,6},{1,7},{2,4},{3,5},{4,2},{5,3},{6,0},{7,1},{8,14},{9,15},{10,... | collective-permute-start | bytes 589832 | tf_op jit(solution)/shard_map/ppermute | solution.py:23

commit v23 on v18

--- a/solution.py
+++ b/solution.py
@@ -189,6 +189,7 @@
     out_side, out_near, out_near_side = work(side, near, near_side)
     back_near_side = send(out_near_side, owners, X ^ Z_NEAR)
     back_side = send(out_side, owners, X)
+    out_near, back_cross = tie((out_near, back_cross))
     back_near = send(out_near, owners, Z_NEAR)
     rows, _ = tie((rows, out_near_side))
     (out_own,) = work(rows)

time: 69.2 us -> 70.7 us (1.022)
  starting transfers between devices: 29.5 us -> 38.2 us
  waiting for transfers between devices: 25.7 us -> 18.5 us
    ppermute x15, starting transfers between devices: 24.5 us -> 33.1 us  [send(): return lax.ppermute(block, 'expert', route)]
    ppermute x15, waiting for transfers between devices: 24.6 us -> 17.5 us  [send(): return lax.ppermute(block, 'expert', route)]
where the time goes in v23:
time: 70.7 us; the launch traced here: 70.5 us
  starting transfers between devices  38.2 us (54%)
  waiting for transfers between devices  18.5 us (26%)
  Pallas kernels  10.5 us (15%)
  local copies, waits for them, and re-layouts  3.26 us (5%)
    ppermute x15, starting transfers between devices, send(): return lax.ppermute(block, 'expert', route)  33.1 us
    ppermute x15, waiting for transfers between devices, send(): return lax.ppermute(block, 'expert', route)  17.5 us
    pallas_call x6, Pallas kernels, products(): pl.pallas_call(functools.partial(products_kernel, len(pieces)), out_shape...  7.34 us
    ppermute x2, starting transfers between devices, send_across(): return lax.ppermute(block, ('pipe', 'expert'), route)  5.05 us
    unnamed x8, local copies, waits for them, and re-layouts  3.26 us
    pallas_call x1, Pallas kernels, turned(): pl.pallas_call(turn_kernel, out_shape=jax.ShapeDtypeStruct((depth, CORES...  1.67 us
  transfers between devices with their start and end apart: 17, of which 8 were waited for; matrix products, arithmetic and copies ran while one was open for 0% of the time, Pallas kernels for 13%

profile of v23, /device:TPU:0, one launch (start us, length us, event | category | flops | bytes accessed | tf_op | source)
XLA Modules:
  0.0 70.5 jit_solution(10364695055142531734)
XLA Ops:
  0.0 0.5 collective-permute-start.1
  0.5 2.5 %collective-permute-start = (bf16[64,2048]{1,0:T(8,128)(2,1)}, bf16[64,2048]{1,0:T(8,128)(2,1)S(1)}, u32[]{:S(2)}, u32[]{:S(2)}) collective-permute-start(bf16[64,2048]{1,0:T(8,128)(2,1)} %bitcast.14), channel_id=1, source_target_pairs={{0,16},{1,17},{2,18},{3,19},{4,20},{5,21},{6,22},{7,23},{8,24},{9,... | collective-permute-start | bytes 786440 | tf_op jit(solution)/shard_map/ppermute | solution.py:33
  3.0 2.5 %collective-permute-start.2 = (bf16[64,2048]{1,0:T(8,128)(2,1)}, bf16[64,2048]{1,0:T(8,128)(2,1)S(1)}, u32[]{:S(2)}, u32[]{:S(2)}) collective-permute-start(bf16[64,2048]{1,0:T(8,128)(2,1)} %bitcast.15), channel_id=1, source_target_pairs={{0,24},{1,25},{2,26},{3,27},{4,28},{5,29},{6,30},{7,31},{8,16},{9,... | collective-permute-start | bytes 786440 | tf_op jit(solution)/shard_map/ppermute | solution.py:33
  5.5 0.0 copy-start
  5.5 0.7 copy-done
  6.2 0.0 copy-start.2
  6.2 0.7 copy-done.2
  6.9 0.1 shard_map.46.columns
  7.0 0.1 collective-permute-start.3
  7.1 0.0 collective-permute-done.1.other
  7.1 0.0 copy-start.3
  7.1 1.9 %copy-done.3 = bf16[1,1,768,2048]{3,2,1,0:T(8,128)(2,1)S(1)} copy-done((bf16[1,1,768,2048]{3,2,1,0:T(8,128)(2,1)S(1)}, bf16[1,1,768,2048]{3,2,1,0:T(8,128)(2,1)}, u32[]{:S(2)}) %copy-start.3) | copy-done | bytes 3145752
  9.0 1.7 %shard_map.47.weights = bf16[2048,1536]{1,0:T(8,128)(2,1)S(1)} custom-call(bf16[768,2048]{1,0:T(8,128)(2,1)S(1)} %bitcast.13, bf16[768,2048]{1,0:T(8,128)(2,1)S(1)} %collective-permute-done.1.other), custom_call_target="tpu_custom_call" | custom-call | flops 12884901888 | tf_op jit(solution)/shard_map/pallas_call | solution.py:77
  10.7 0.6 collective-permute-done.rows
  11.3 1.8 %collective-permute-start.5 = (bf16[64,2176]{1,0:T(8,128)(2,1)S(1)}, bf16[64,2176]{1,0:T(8,128)(2,1)S(1)}, u32[]{:S(2)}, u32[]{:S(2)}) collective-permute-start(bf16[64,2176]{1,0:T(8,128)(2,1)S(1)} %shard_map.48.refs_0_), channel_id=1, source_target_pairs={{0,2},{1,3},{2,0},{3,1},{4,6},{5,7},{6,4},{7,5},{8,10},{9,11},{10,... | collective-permute-start | bytes 835592 | tf_op jit(solution)/shard_map/ppermute | solution.py:23
  13.1 6.1 %collective-permute-start.4 = (bf16[64,2176]{1,0:T(8,128)(2,1)S(1)}, bf16[64,2176]{1,0:T(8,128)(2,1)S(1)}, u32[]{:S(2)}, u32[]{:S(2)}) collective-permute-start(bf16[64,2176]{1,0:T(8,128)(2,1)S(1)} %shard_map.48.refs_0_), channel_id=1, source_target_pairs={{0,4},{1,5},{2,6},{3,7},{4,0},{5,1},{6,2},{7,3},{8,12},{9,13},{10,... | collective-permute-start | bytes 835592 | tf_op jit(solution)/shard_map/ppermute | solution.py:23
  19.2 0.0 collective-permute-done.3.columns
  19.2 0.4 collective-permute-done.2.rows
  19.6 0.1 collective-permute-start.7
  19.7 1.6 %collective-permute-start.9 = (bf16[64,2176]{1,0:T(8,128)(2,1)S(1)}, bf16[64,2176]{1,0:T(8,128)(2,1)S(1)}, u32[]{:S(2)}, u32[]{:S(2)}) collective-permute-start(bf16[64,2176]{1,0:T(8,128)(2,1)S(1)} %shard_map.49.refs_0_), channel_id=1, source_target_pairs={{0,2},{1,3},{2,0},{3,1},{4,6},{5,7},{6,4},{7,5},{8,10},{9,11},{10,... | collective-permute-start | bytes 835592 | tf_op jit(solution)/shard_map/ppermute | solution.py:23
  21.2 1.2 %shard_map.50 = bf16[2,64,768]{2,1,0:T(8,128)(2,1)S(1)} custom-call(bf16[2048,1536]{1,0:T(8,128)(2,1)S(1)} %shard_map.47.weights, bf16[64,2176]{1,0:T(8,128)(2,1)S(1)} %shard_map.49.refs_0_), custom_call_target="tpu_custom_call" | custom-call | flops 4026531840 | bytes 6750208 | tf_op jit(solution)/shard_map/pallas_call | solution.py:109
  22.4 4.0 %collective-permute-start.10 = (bf16[2,64,768]{2,1,0:T(8,128)(2,1)S(1)}, bf16[2,64,768]{2,1,0:T(8,128)(2,1)S(1)}, u32[]{:S(2)}, u32[]{:S(2)}) collective-permute-start(bf16[2,64,768]{2,1,0:T(8,128)(2,1)S(1)} %shard_map.50), channel_id=1, source_target_pairs={{0,8},{1,9},{2,10},{3,11},{4,12},{5,13},{6,14},{7,15},{8,0},{9,1},... | collective-permute-start | bytes 589832 | tf_op jit(solution)/shard_map/ppermute | solution.py:23
  26.4 0.0 collective-permute-done.5.refs_0_
  26.5 0.3 collective-permute-done.4.refs_1_
  26.7 0.5 collective-permute-start.6
  27.2 8.4 %collective-permute-done.7.refs_0_ = bf16[64,2176]{1,0:T(8,128)(2,1)S(1)} collective-permute-done((bf16[64,2176]{1,0:T(8,128)(2,1)S(1)}, bf16[64,2176]{1,0:T(8,128)(2,1)S(1)}, u32[]{:S(2)}, u32[]{:S(2)}) %collective-permute-start.7) | collective-permute-done | bytes 278560 | tf_op jit(solution)/shard_map/ppermute | solution.py:23
  35.6 0.9 %collective-permute-start.8 = (bf16[64,2176]{1,0:T(8,128)(2,1)S(1)}, bf16[64,2176]{1,0:T(8,128)(2,1)S(1)}, u32[]{:S(2)}, u32[]{:S(2)}) collective-permute-start(bf16[64,2176]{1,0:T(8,128)(2,1)S(1)} %collective-permute-done.7.refs_0_), channel_id=1, source_target_pairs={{0,2},{1,3},{2,0},{3,1},{4,6},{5,7},{6,4},{7,5},{8,10},{9,11},{10,... | collective-permute-start | bytes 835592 | tf_op jit(solution)/shard_map/ppermute | solution.py:23
  36.5 1.2 %shard_map.51 = bf16[2,64,768]{2,1,0:T(8,128)(2,1)S(1)} custom-call(bf16[2048,1536]{1,0:T(8,128)(2,1)S(1)} %shard_map.47.weights, bf16[64,2176]{1,0:T(8,128)(2,1)S(1)} %collective-permute-done.7.refs_0_), custom_call_target="tpu_custom_call" | custom-call | flops 4026531840 | bytes 6750208 | tf_op jit(solution)/shard_map/pallas_call | solution.py:109
  37.7 3.5 %collective-permute-start.12 = (bf16[2,64,768]{2,1,0:T(8,128)(2,1)S(1)}, bf16[2,64,768]{2,1,0:T(8,128)(2,1)S(1)}, u32[]{:S(2)}, u32[]{:S(2)}) collective-permute-start(bf16[2,64,768]{2,1,0:T(8,128)(2,1)S(1)} %shard_map.51), channel_id=1, source_target_pairs={{0,12},{1,13},{2,14},{3,15},{4,8},{5,9},{6,10},{7,11},{8,4},{9,5},... | collective-permute-start | bytes 589832 | tf_op jit(solution)/shard_map/ppermute | solution.py:23
  41.2 0.0 collective-permute-done.10.refs_4_
  41.2 0.0 collective-permute-done.9.refs_0_
  41.2 1.2 %shard_map.52 = bf16[2,64,768]{2,1,0:T(8,128)(2,1)S(1)} custom-call(bf16[2048,1536]{1,0:T(8,128)(2,1)S(1)} %shard_map.47.weights, bf16[64,2176]{1,0:T(8,128)(2,1)S(1)} %collective-permute-done.9.refs_0_), custom_call_target="tpu_custom_call" | custom-call | flops 4026531840 | bytes 6750208 | tf_op jit(solution)/shard_map/pallas_call | solution.py:109
  42.4 0.1 collective-permute-start.15
  42.5 0.5 collective-permute-done.8.refs_0_
  43.0 1.2 %shard_map.53 = bf16[2,64,768]{2,1,0:T(8,128)(2,1)S(1)} custom-call(bf16[2048,1536]{1,0:T(8,128)(2,1)S(1)} %shard_map.47.weights, bf16[64,2176]{1,0:T(8,128)(2,1)S(1)} %collective-permute-done.8.refs_0_), custom_call_target="tpu_custom_call" | custom-call | flops 4026531840 | bytes 6750208 | tf_op jit(solution)/shard_map/pallas_call | solution.py:109
  44.2 5.0 %collective-permute-start.16 = (bf16[2,64,768]{2,1,0:T(8,128)(2,1)S(1)}, bf16[2,64,768]{2,1,0:T(8,128)(2,1)S(1)}, u32[]{:S(2)}, u32[]{:S(2)}) collective-permute-start(bf16[2,64,768]{2,1,0:T(8,128)(2,1)S(1)} %shard_map.53), channel_id=1, source_target_pairs={{0,14},{1,15},{2,12},{3,13},{4,10},{5,11},{6,8},{7,9},{8,6},{9,7},... | collective-permute-start | bytes 589832 | tf_op jit(solution)/shard_map/ppermute | solution.py:23
  49.2 0.0 collective-permute-done.6.refs_2_
  49.2 1.4 %shard_map.54 = (bf16[2,64,768]{2,1,0:T(8,128)(2,1)S(1)}, bf16[2,64,768]{2,1,0:T(8,128)(2,1)S(1)}, bf16[2,64,768]{2,1,0:T(8,128)(2,1)S(1)}) custom-call(bf16[2048,1536]{1,0:T(8,128)(2,1)S(1)} %shard_map.47.weights, bf16[64,2176]{1,0:T(8,128)(2,1)S(1)} %collective-permute-done.5.refs_0_, bf16[64,2176]{1,0:T(8,128)(2,1)S(1)} %collective-permute-done.4.refs_1_, ...), custom_call_target="tpu_custom_call" | custom-call | flops 12079595520 | bytes 7667712 | tf_op jit(solution)/shard_map/pallas_call | solution.py:109
  50.6 0.0 collective-permute-done.12.refs_6_
  50.6 7.6 %collective-permute-start.13 = (bf16[2,64,768]{2,1,0:T(8,128)(2,1)S(1)}, bf16[2,64,768]{2,1,0:T(8,128)(2,1)S(1)}, u32[]{:S(2)}, u32[]{:S(2)}) collective-permute-start(bf16[2,64,768]{2,1,0:T(8,128)(2,1)S(1)} %get-tuple-element.42), channel_id=1, source_target_pairs={{0,4},{1,5},{2,6},{3,7},{4,0},{5,1},{6,2},{7,3},{8,12},{9,13},{10,... | collective-permute-start | bytes 589832 | tf_op jit(solution)/shard_map/ppermute | solution.py:23
  58.2 0.7 collective-permute-start.11
  58.9 0.0 copy-start.1
  58.9 0.8 %collective-permute-start.14 = (bf16[2,64,768]{2,1,0:T(8,128)(2,1)S(1)}, bf16[2,64,768]{2,1,0:T(8,128)(2,1)S(1)}, u32[]{:S(2)}, u32[]{:S(2)}) collective-permute-start(bf16[2,64,768]{2,1,0:T(8,128)(2,1)S(1)} %get-tuple-element.38), channel_id=1, source_target_pairs={{0,6},{1,7},{2,4},{3,5},{4,2},{5,3},{6,0},{7,1},{8,14},{9,15},{10,... | collective-permute-start | bytes 589832 | tf_op jit(solution)/shard_map/ppermute | solution.py:23
  59.7 1.2 %shard_map.55.refs_0_ = bf16[2,64,768]{2,1,0:T(8,128)(2,1)S(1)} custom-call(bf16[2048,1536]{1,0:T(8,128)(2,1)S(1)} %shard_map.47.weights, bf16[64,2176]{1,0:T(8,128)(2,1)S(1)} %shard_map.48.refs_0_), custom_call_target="tpu_custom_call" | custom-call | flops 4026531840 | bytes 6750208 | tf_op jit(solution)/shard_map/pallas_call | solution.py:109
  60.9 1.1 %collective-permute-done.15.refs_5_ = bf16[2,64,768]{2,1,0:T(8,128)(2,1)S(1)} collective-permute-done((bf16[2,64,768]{2,1,0:T(8,128)(2,1)S(1)}, bf16[2,64,768]{2,1,0:T(8,128)(2,1)S(1)}, u32[]{:S(2)}, u32[]{:S(2)}) %collective-permute-start.15) | collective-permute-done | bytes 196640 | tf_op jit(solution)/shard_map/ppermute | solution.py:23
  62.0 3.2 %collective-permute-done.13.refs_2_ = bf16[2,64,768]{2,1,0:T(8,128)(2,1)S(1)} collective-permute-done((bf16[2,64,768]{2,1,0:T(8,128)(2,1)S(1)}, bf16[2,64,768]{2,1,0:T(8,128)(2,1)S(1)}, u32[]{:S(2)}, u32[]{:S(2)}) %collective-permute-start.13) | collective-permute-done | bytes 196640 | tf_op jit(solution)/shard_map/ppermute | solution.py:23
  65.2 3.9 %collective-permute-done.11.refs_1_ = bf16[2,64,768]{2,1,0:T(8,128)(2,1)S(1)} collective-permute-done((bf16[2,64,768]{2,1,0:T(8,128)(2,1)S(1)}, bf16[2,64,768]{2,1,0:T(8,128)(2,1)S(1)}, u32[]{:S(2)}, u32[]{:S(2)}) %collective-permute-start.11) | collective-permute-done | bytes 196640 | tf_op jit(solution)/shard_map/ppermute | solution.py:23
  69.2 0.0 collective-permute-done.14.refs_3_
  69.2 0.0 collective-permute-done.16.refs_7_
  69.2 0.0 copy-done.1
  69.2 1.3 %shard_map.56 = bf16[512,768]{1,0:T(8,128)(2,1)} custom-call(s32[8,64]{1,0:T(8,128)S(1)} %bitcast.10, bf16[2,64,768]{2,1,0:T(8,128)(2,1)S(1)} %shard_map.55.refs_0_, bf16[2,64,768]{2,1,0:T(8,128)(2,1)S(1)} %collective-permute-done.11.refs_1_, bf16[2,64,768]{2,1,0:T(8,128)(2,1)S(1)} %collective-permute-done.13.refs_2_, ...), custom_call_target="tpu_custom_call" | custom-call | tf_op jit(solution)/shard_map/pallas_call | solution.py:144
  (2 shorter events, 0.0 us)
Async XLA Ops:
  0.0 7.1 %collective-permute-start.1 = (bf16[768,2048]{1,0:T(8,128)(2,1)}, bf16[768,2048]{1,0:T(8,128)(2,1)S(1)}, u32[]{:S(2)}, u32[]{:S(2)}) collective-permute-start(bf16[768,2048]{1,0:T(8,128)(2,1)} %bitcast.12), channel_id=1, source_target_pairs={{0,1},{1,0},{2,3},{3,2},{4,5},{5,4},{6,7},{7,6},{8,9},{9,8},{10,11... | collective-permute-start | bytes 9437192 | tf_op jit(solution)/shard_map/ppermute | solution.py:23
  0.5 10.8 %collective-permute-start = (bf16[64,2048]{1,0:T(8,128)(2,1)}, bf16[64,2048]{1,0:T(8,128)(2,1)S(1)}, u32[]{:S(2)}, u32[]{:S(2)}) collective-permute-start(bf16[64,2048]{1,0:T(8,128)(2,1)} %bitcast.14), channel_id=1, source_target_pairs={{0,16},{1,17},{2,18},{3,19},{4,20},{5,21},{6,22},{7,23},{8,24},{9,... | collective-permute-start | bytes 786440 | tf_op jit(solution)/shard_map/ppermute | solution.py:33
  3.0 16.6 %collective-permute-start.2 = (bf16[64,2048]{1,0:T(8,128)(2,1)}, bf16[64,2048]{1,0:T(8,128)(2,1)S(1)}, u32[]{:S(2)}, u32[]{:S(2)}) collective-permute-start(bf16[64,2048]{1,0:T(8,128)(2,1)} %bitcast.15), channel_id=1, source_target_pairs={{0,24},{1,25},{2,26},{3,27},{4,28},{5,29},{6,30},{7,31},{8,16},{9,... | collective-permute-start | bytes 786440 | tf_op jit(solution)/shard_map/ppermute | solution.py:33
  5.5 0.7 copy-start
  6.2 0.7 copy-start.2
  7.0 12.2 %collective-permute-start.3 = (bf16[64,128]{1,0:T(8,128)(2,1)S(1)}, bf16[64,128]{1,0:T(8,128)(2,1)S(1)}, u32[]{:S(2)}, u32[]{:S(2)}) collective-permute-start(bf16[64,128]{1,0:T(8,128)(2,1)S(1)} %shard_map.46.columns), channel_id=1, source_target_pairs={{0,8},{1,9},{2,10},{3,11},{4,12},{5,13},{6,14},{7,15},{8,0},{9,1},... | collective-permute-start | bytes 49160 | tf_op jit(solution)/shard_map/ppermute | solution.py:23
  7.1 1.9 %copy-start.3 = (bf16[1,1,768,2048]{3,2,1,0:T(8,128)(2,1)S(1)}, bf16[1,1,768,2048]{3,2,1,0:T(8,128)(2,1)}, u32[]{:S(2)}) copy-start(bf16[1,1,768,2048]{3,2,1,0:T(8,128)(2,1)} %param.7) | copy-start | bytes 9437188
  11.3 15.2 %collective-permute-start.5 = (bf16[64,2176]{1,0:T(8,128)(2,1)S(1)}, bf16[64,2176]{1,0:T(8,128)(2,1)S(1)}, u32[]{:S(2)}, u32[]{:S(2)}) collective-permute-start(bf16[64,2176]{1,0:T(8,128)(2,1)S(1)} %shard_map.48.refs_0_), channel_id=1, source_target_pairs={{0,2},{1,3},{2,0},{3,1},{4,6},{5,7},{6,4},{7,5},{8,10},{9,11},{10,... | collective-permute-start | bytes 835592 | tf_op jit(solution)/shard_map/ppermute | solution.py:23
  13.1 13.6 %collective-permute-start.4 = (bf16[64,2176]{1,0:T(8,128)(2,1)S(1)}, bf16[64,2176]{1,0:T(8,128)(2,1)S(1)}, u32[]{:S(2)}, u32[]{:S(2)}) collective-permute-start(bf16[64,2176]{1,0:T(8,128)(2,1)S(1)} %shard_map.48.refs_0_), channel_id=1, source_target_pairs={{0,4},{1,5},{2,6},{3,7},{4,0},{5,1},{6,2},{7,3},{8,12},{9,13},{10,... | collective-permute-start | bytes 835592 | tf_op jit(solution)/shard_map/ppermute | solution.py:23
  19.6 16.0 %collective-permute-start.7 = (bf16[64,2176]{1,0:T(8,128)(2,1)S(1)}, bf16[64,2176]{1,0:T(8,128)(2,1)S(1)}, u32[]{:S(2)}, u32[]{:S(2)}) collective-permute-start(bf16[64,2176]{1,0:T(8,128)(2,1)S(1)} %shard_map.49.refs_0_), channel_id=1, source_target_pairs={{0,4},{1,5},{2,6},{3,7},{4,0},{5,1},{6,2},{7,3},{8,12},{9,13},{10,... | collective-permute-start | bytes 835592 | tf_op jit(solution)/shard_map/ppermute | solution.py:23
  19.7 21.5 %collective-permute-start.9 = (bf16[64,2176]{1,0:T(8,128)(2,1)S(1)}, bf16[64,2176]{1,0:T(8,128)(2,1)S(1)}, u32[]{:S(2)}, u32[]{:S(2)}) collective-permute-start(bf16[64,2176]{1,0:T(8,128)(2,1)S(1)} %shard_map.49.refs_0_), channel_id=1, source_target_pairs={{0,2},{1,3},{2,0},{3,1},{4,6},{5,7},{6,4},{7,5},{8,10},{9,11},{10,... | collective-permute-start | bytes 835592 | tf_op jit(solution)/shard_map/ppermute | solution.py:23
  22.4 18.7 %collective-permute-start.10 = (bf16[2,64,768]{2,1,0:T(8,128)(2,1)S(1)}, bf16[2,64,768]{2,1,0:T(8,128)(2,1)S(1)}, u32[]{:S(2)}, u32[]{:S(2)}) collective-permute-start(bf16[2,64,768]{2,1,0:T(8,128)(2,1)S(1)} %shard_map.50), channel_id=1, source_target_pairs={{0,8},{1,9},{2,10},{3,11},{4,12},{5,13},{6,14},{7,15},{8,0},{9,1},... | collective-permute-start | bytes 589832 | tf_op jit(solution)/shard_map/ppermute | solution.py:23
  26.7 22.5 %collective-permute-start.6 = (bf16[64,2176]{1,0:T(8,128)(2,1)S(1)}, bf16[64,2176]{1,0:T(8,128)(2,1)S(1)}, u32[]{:S(2)}, u32[]{:S(2)}) collective-permute-start(bf16[64,2176]{1,0:T(8,128)(2,1)S(1)} %collective-permute-done.4.refs_1_), channel_id=1, source_target_pairs={{0,2},{1,3},{2,0},{3,1},{4,6},{5,7},{6,4},{7,5},{8,10},{9,11},{10,... | collective-permute-start | bytes 835592 | tf_op jit(solution)/shard_map/ppermute | solution.py:23
  35.6 7.4 %collective-permute-start.8 = (bf16[64,2176]{1,0:T(8,128)(2,1)S(1)}, bf16[64,2176]{1,0:T(8,128)(2,1)S(1)}, u32[]{:S(2)}, u32[]{:S(2)}) collective-permute-start(bf16[64,2176]{1,0:T(8,128)(2,1)S(1)} %collective-permute-done.7.refs_0_), channel_id=1, source_target_pairs={{0,2},{1,3},{2,0},{3,1},{4,6},{5,7},{6,4},{7,5},{8,10},{9,11},{10,... | collective-permute-start | bytes 835592 | tf_op jit(solution)/shard_map/ppermute | solution.py:23
  37.7 12.9 %collective-permute-start.12 = (bf16[2,64,768]{2,1,0:T(8,128)(2,1)S(1)}, bf16[2,64,768]{2,1,0:T(8,128)(2,1)S(1)}, u32[]{:S(2)}, u32[]{:S(2)}) collective-permute-start(bf16[2,64,768]{2,1,0:T(8,128)(2,1)S(1)} %shard_map.51), channel_id=1, source_target_pairs={{0,12},{1,13},{2,14},{3,15},{4,8},{5,9},{6,10},{7,11},{8,4},{9,5},... | collective-permute-start | bytes 589832 | tf_op jit(solution)/shard_map/ppermute | solution.py:23
  42.4 19.6 %collective-permute-start.15 = (bf16[2,64,768]{2,1,0:T(8,128)(2,1)S(1)}, bf16[2,64,768]{2,1,0:T(8,128)(2,1)S(1)}, u32[]{:S(2)}, u32[]{:S(2)}) collective-permute-start(bf16[2,64,768]{2,1,0:T(8,128)(2,1)S(1)} %shard_map.52), channel_id=1, source_target_pairs={{0,10},{1,11},{2,8},{3,9},{4,14},{5,15},{6,12},{7,13},{8,2},{9,3},... | collective-permute-start | bytes 589832 | tf_op jit(solution)/shard_map/ppermute | solution.py:23
  44.2 25.0 %collective-permute-start.16 = (bf16[2,64,768]{2,1,0:T(8,128)(2,1)S(1)}, bf16[2,64,768]{2,1,0:T(8,128)(2,1)S(1)}, u32[]{:S(2)}, u32[]{:S(2)}) collective-permute-start(bf16[2,64,768]{2,1,0:T(8,128)(2,1)S(1)} %shard_map.53), channel_id=1, source_target_pairs={{0,14},{1,15},{2,12},{3,13},{4,10},{5,11},{6,8},{7,9},{8,6},{9,7},... | collective-permute-start | bytes 589832 | tf_op jit(solution)/shard_map/ppermute | solution.py:23
  50.6 14.6 %collective-permute-start.13 = (bf16[2,64,768]{2,1,0:T(8,128)(2,1)S(1)}, bf16[2,64,768]{2,1,0:T(8,128)(2,1)S(1)}, u32[]{:S(2)}, u32[]{:S(2)}) collective-permute-start(bf16[2,64,768]{2,1,0:T(8,128)(2,1)S(1)} %get-tuple-element.42), channel_id=1, source_target_pairs={{0,4},{1,5},{2,6},{3,7},{4,0},{5,1},{6,2},{7,3},{8,12},{9,13},{10,... | collective-permute-start | bytes 589832 | tf_op jit(solution)/shard_map/ppermute | solution.py:23
  58.2 11.0 %collective-permute-start.11 = (bf16[2,64,768]{2,1,0:T(8,128)(2,1)S(1)}, bf16[2,64,768]{2,1,0:T(8,128)(2,1)S(1)}, u32[]{:S(2)}, u32[]{:S(2)}) collective-permute-start(bf16[2,64,768]{2,1,0:T(8,128)(2,1)S(1)} %get-tuple-element.40), channel_id=1, source_target_pairs={{0,2},{1,3},{2,0},{3,1},{4,6},{5,7},{6,4},{7,5},{8,10},{9,11},{10,... | collective-permute-start | bytes 589832 | tf_op jit(solution)/shard_map/ppermute | solution.py:23
  58.9 10.3 %copy-start.1 = (s32[1,64,8]{1,2,0:T(8,128)S(1)}, s32[1,64,8]{1,2,0:T(8,128)}, u32[]{:S(2)}) copy-start(s32[1,64,8]{1,2,0:T(8,128)} %param.5) | copy-start | bytes 6148
  58.9 10.3 %collective-permute-start.14 = (bf16[2,64,768]{2,1,0:T(8,128)(2,1)S(1)}, bf16[2,64,768]{2,1,0:T(8,128)(2,1)S(1)}, u32[]{:S(2)}, u32[]{:S(2)}) collective-permute-start(bf16[2,64,768]{2,1,0:T(8,128)(2,1)S(1)} %get-tuple-element.38), channel_id=1, source_target_pairs={{0,6},{1,7},{2,4},{3,5},{4,2},{5,3},{6,0},{7,1},{8,14},{9,15},{10,... | collective-permute-start | bytes 589832 | tf_op jit(solution)/shard_map/ppermute | solution.py:23

commit v24 on v18

--- a/solution.py
+++ b/solution.py
@@ -180,18 +180,18 @@
     (out_cross,) = work(cross)
     back_cross = send(out_cross, owners, Z_NEAR ^ Z_FAR)
     far_side, back_far, _ = tie((far_side, back_far, out_cross))
-    (out_far_side,) = work(far_side)
+    out_far_side, out_side, out_own = work(far_side, side, rows)
     back_far_side = send(out_far_side, owners, X ^ Z_FAR)
     cross_side, _ = tie((cross_side, out_far_side))
     (out_cross_side,) = work(cross_side)
     back_cross_side = send(out_cross_side, owners, X ^ Z_NEAR ^ Z_FAR)
+    out_side, _ = tie((out_side, out_cross_side))
+    back_side = send(out_side, owners, X)
     near_side, _ = tie((near_side, out_cross_side))
-    out_side, out_near, out_near_side = work(side, near, near_side)
+    out_near, out_near_side = work(near, near_side)
     back_near_side = send(out_near_side, owners, X ^ Z_NEAR)
-    back_side = send(out_side, owners, X)
+    out_near, back_side = tie((out_near, back_side))
     back_near = send(out_near, owners, Z_NEAR)
-    rows, _ = tie((rows, out_near_side))
-    (out_own,) = work(rows)
     received = {
         0: out_own,
         X: back_side,

time: 69.2 us -> 75.1 us (1.085)
  waiting for transfers between devices: 25.7 us -> 32.8 us
  Pallas kernels: 10.5 us -> 9.07 us
    ppermute x15, waiting for transfers between devices: 24.6 us -> 31.8 us  [send(): return lax.ppermute(block, 'expert', route)]
    pallas_call x6 -> x5, Pallas kernels: 7.34 us -> 5.94 us  [products(): pl.pallas_call(functools.partial(products_kernel, len(pieces)), out_shape...]
  transfers between devices with their start and end apart: 17 -> 17, of which waited for: 8 -> 7; matrix products, arithmetic and copies ran while one was open for 0% -> 0% of each run, Pallas kernels for 13% -> 10%
where the time goes in v24:
time: 75.1 us; the launch traced here: 75 us
  waiting for transfers between devices  32.8 us (44%)
  starting transfers between devices  29.7 us (40%)
  Pallas kernels  9.07 us (12%)
  local copies, waits for them, and re-layouts  3.26 us (4%)
    ppermute x15, waiting for transfers between devices, send(): return lax.ppermute(block, 'expert', route)  31.8 us
    ppermute x15, starting transfers between devices, send(): return lax.ppermute(block, 'expert', route)  24.7 us
    pallas_call x5, Pallas kernels, products(): pl.pallas_call(functools.partial(products_kernel, len(pieces)), out_shape...  5.94 us
    ppermute x2, starting transfers between devices, send_across(): return lax.ppermute(block, ('pipe', 'expert'), route)  5.05 us
    unnamed x8, local copies, waits for them, and re-layouts  3.26 us
    pallas_call x1, Pallas kernels, turned(): pl.pallas_call(turn_kernel, out_shape=jax.ShapeDtypeStruct((depth, CORES...  1.67 us
  transfers between devices with their start and end apart: 17, of which 7 were waited for; matrix products, arithmetic and copies ran while one was open for 0% of the time, Pallas kernels for 10%

profile of v24, /device:TPU:0, one launch (start us, length us, event | category | flops | bytes accessed | tf_op | source)
XLA Modules:
  0.0 75.0 jit_solution(9314160415851270548)
XLA Ops:
  0.0 0.5 collective-permute-start.1
  0.5 2.5 %collective-permute-start = (bf16[64,2048]{1,0:T(8,128)(2,1)}, bf16[64,2048]{1,0:T(8,128)(2,1)S(1)}, u32[]{:S(2)}, u32[]{:S(2)}) collective-permute-start(bf16[64,2048]{1,0:T(8,128)(2,1)} %bitcast.14), channel_id=1, source_target_pairs={{0,16},{1,17},{2,18},{3,19},{4,20},{5,21},{6,22},{7,23},{8,24},{9,... | collective-permute-start | bytes 786440 | tf_op jit(solution)/shard_map/ppermute | solution.py:33
  3.0 2.5 %collective-permute-start.2 = (bf16[64,2048]{1,0:T(8,128)(2,1)}, bf16[64,2048]{1,0:T(8,128)(2,1)S(1)}, u32[]{:S(2)}, u32[]{:S(2)}) collective-permute-start(bf16[64,2048]{1,0:T(8,128)(2,1)} %bitcast.15), channel_id=1, source_target_pairs={{0,24},{1,25},{2,26},{3,27},{4,28},{5,29},{6,30},{7,31},{8,16},{9,... | collective-permute-start | bytes 786440 | tf_op jit(solution)/shard_map/ppermute | solution.py:33
  5.5 0.0 copy-start
  5.5 0.7 copy-done
  6.2 0.0 copy-start.2
  6.2 0.7 copy-done.2
  6.9 0.1 shard_map.46.columns
  7.0 0.1 collective-permute-start.3
  7.1 0.0 collective-permute-done.1.other
  7.1 0.0 copy-start.3
  7.1 1.9 %copy-done.3 = bf16[1,1,768,2048]{3,2,1,0:T(8,128)(2,1)S(1)} copy-done((bf16[1,1,768,2048]{3,2,1,0:T(8,128)(2,1)S(1)}, bf16[1,1,768,2048]{3,2,1,0:T(8,128)(2,1)}, u32[]{:S(2)}) %copy-start.3) | copy-done | bytes 3145752
  9.0 1.7 %shard_map.47.weights = bf16[2048,1536]{1,0:T(8,128)(2,1)S(1)} custom-call(bf16[768,2048]{1,0:T(8,128)(2,1)S(1)} %bitcast.13, bf16[768,2048]{1,0:T(8,128)(2,1)S(1)} %collective-permute-done.1.other), custom_call_target="tpu_custom_call" | custom-call | flops 12884901888 | tf_op jit(solution)/shard_map/pallas_call | solution.py:77
  10.7 0.6 collective-permute-done.rows
  11.3 1.8 %collective-permute-start.8 = (bf16[64,2176]{1,0:T(8,128)(2,1)S(1)}, bf16[64,2176]{1,0:T(8,128)(2,1)S(1)}, u32[]{:S(2)}, u32[]{:S(2)}) collective-permute-start(bf16[64,2176]{1,0:T(8,128)(2,1)S(1)} %shard_map.48.refs_2_), channel_id=1, source_target_pairs={{0,2},{1,3},{2,0},{3,1},{4,6},{5,7},{6,4},{7,5},{8,10},{9,11},{10,... | collective-permute-start | bytes 835592 | tf_op jit(solution)/shard_map/ppermute | solution.py:23
  13.1 6.1 %collective-permute-start.7 = (bf16[64,2176]{1,0:T(8,128)(2,1)S(1)}, bf16[64,2176]{1,0:T(8,128)(2,1)S(1)}, u32[]{:S(2)}, u32[]{:S(2)}) collective-permute-start(bf16[64,2176]{1,0:T(8,128)(2,1)S(1)} %shard_map.48.refs_2_), channel_id=1, source_target_pairs={{0,4},{1,5},{2,6},{3,7},{4,0},{5,1},{6,2},{7,3},{8,12},{9,13},{10,... | collective-permute-start | bytes 835592 | tf_op jit(solution)/shard_map/ppermute | solution.py:23
  19.2 0.0 collective-permute-done.3.columns
  19.2 0.4 collective-permute-done.2.rows
  19.6 0.1 collective-permute-start.6
  19.7 1.6 %collective-permute-start.4 = (bf16[64,2176]{1,0:T(8,128)(2,1)S(1)}, bf16[64,2176]{1,0:T(8,128)(2,1)S(1)}, u32[]{:S(2)}, u32[]{:S(2)}) collective-permute-start(bf16[64,2176]{1,0:T(8,128)(2,1)S(1)} %shard_map.49.refs_0_), channel_id=1, source_target_pairs={{0,2},{1,3},{2,0},{3,1},{4,6},{5,7},{6,4},{7,5},{8,10},{9,11},{10,... | collective-permute-start | bytes 835592 | tf_op jit(solution)/shard_map/ppermute | solution.py:23
  21.2 1.2 %shard_map.50 = bf16[2,64,768]{2,1,0:T(8,128)(2,1)S(1)} custom-call(bf16[2048,1536]{1,0:T(8,128)(2,1)S(1)} %shard_map.47.weights, bf16[64,2176]{1,0:T(8,128)(2,1)S(1)} %shard_map.49.refs_0_), custom_call_target="tpu_custom_call" | custom-call | flops 4026531840 | bytes 6750208 | tf_op jit(solution)/shard_map/pallas_call | solution.py:109
  22.4 4.0 %collective-permute-start.5 = (bf16[2,64,768]{2,1,0:T(8,128)(2,1)S(1)}, bf16[2,64,768]{2,1,0:T(8,128)(2,1)S(1)}, u32[]{:S(2)}, u32[]{:S(2)}) collective-permute-start(bf16[2,64,768]{2,1,0:T(8,128)(2,1)S(1)} %shard_map.50), channel_id=1, source_target_pairs={{0,8},{1,9},{2,10},{3,11},{4,12},{5,13},{6,14},{7,15},{8,0},{9,1},... | collective-permute-start | bytes 589832 | tf_op jit(solution)/shard_map/ppermute | solution.py:23
  26.4 0.0 collective-permute-done.8.refs_1_
  26.5 0.3 collective-permute-done.7.refs_0_
  26.7 0.5 collective-permute-start.9
  27.2 8.4 %collective-permute-done.6.refs_0_ = bf16[64,2176]{1,0:T(8,128)(2,1)S(1)} collective-permute-done((bf16[64,2176]{1,0:T(8,128)(2,1)S(1)}, bf16[64,2176]{1,0:T(8,128)(2,1)S(1)}, u32[]{:S(2)}, u32[]{:S(2)}) %collective-permute-start.6) | collective-permute-done | bytes 278560 | tf_op jit(solution)/shard_map/ppermute | solution.py:23
  35.6 0.9 %collective-permute-start.10 = (bf16[64,2176]{1,0:T(8,128)(2,1)S(1)}, bf16[64,2176]{1,0:T(8,128)(2,1)S(1)}, u32[]{:S(2)}, u32[]{:S(2)}) collective-permute-start(bf16[64,2176]{1,0:T(8,128)(2,1)S(1)} %collective-permute-done.6.refs_0_), channel_id=1, source_target_pairs={{0,2},{1,3},{2,0},{3,1},{4,6},{5,7},{6,4},{7,5},{8,10},{9,11},{10,... | collective-permute-start | bytes 835592 | tf_op jit(solution)/shard_map/ppermute | solution.py:23
  36.5 1.2 %shard_map.51 = bf16[2,64,768]{2,1,0:T(8,128)(2,1)S(1)} custom-call(bf16[2048,1536]{1,0:T(8,128)(2,1)S(1)} %shard_map.47.weights, bf16[64,2176]{1,0:T(8,128)(2,1)S(1)} %collective-permute-done.6.refs_0_), custom_call_target="tpu_custom_call" | custom-call | flops 4026531840 | bytes 6750208 | tf_op jit(solution)/shard_map/pallas_call | solution.py:109
  37.7 3.5 %collective-permute-start.15 = (bf16[2,64,768]{2,1,0:T(8,128)(2,1)S(1)}, bf16[2,64,768]{2,1,0:T(8,128)(2,1)S(1)}, u32[]{:S(2)}, u32[]{:S(2)}) collective-permute-start(bf16[2,64,768]{2,1,0:T(8,128)(2,1)S(1)} %shard_map.51), channel_id=1, source_target_pairs={{0,12},{1,13},{2,14},{3,15},{4,8},{5,9},{6,10},{7,11},{8,4},{9,5},... | collective-permute-start | bytes 589832 | tf_op jit(solution)/shard_map/ppermute | solution.py:23
  41.2 0.0 collective-permute-done.5.refs_4_
  41.2 0.0 collective-permute-done.4.refs_0_
  41.2 1.4 %shard_map.52 = (bf16[2,64,768]{2,1,0:T(8,128)(2,1)S(1)}, bf16[2,64,768]{2,1,0:T(8,128)(2,1)S(1)}, bf16[2,64,768]{2,1,0:T(8,128)(2,1)S(1)}) custom-call(bf16[2048,1536]{1,0:T(8,128)(2,1)S(1)} %shard_map.47.weights, bf16[64,2176]{1,0:T(8,128)(2,1)S(1)} %collective-permute-done.4.refs_0_, bf16[64,2176]{1,0:T(8,128)(2,1)S(1)} %collective-permute-done.8.refs_1_, ...), custom_call_target="tpu_custom_call" | custom-call | flops 12079595520 | bytes 7667712 | tf_op jit(solution)/shard_map/pallas_call | solution.py:109
  42.6 0.1 collective-permute-start.14
  42.7 0.3 collective-permute-done.10.refs_0_
  43.0 1.2 %shard_map.53 = bf16[2,64,768]{2,1,0:T(8,128)(2,1)S(1)} custom-call(bf16[2048,1536]{1,0:T(8,128)(2,1)S(1)} %shard_map.47.weights, bf16[64,2176]{1,0:T(8,128)(2,1)S(1)} %collective-permute-done.10.refs_0_), custom_call_target="tpu_custom_call" | custom-call | flops 4026531840 | bytes 6750208 | tf_op jit(solution)/shard_map/pallas_call | solution.py:109
  44.2 5.0 %collective-permute-start.16 = (bf16[2,64,768]{2,1,0:T(8,128)(2,1)S(1)}, bf16[2,64,768]{2,1,0:T(8,128)(2,1)S(1)}, u32[]{:S(2)}, u32[]{:S(2)}) collective-permute-start(bf16[2,64,768]{2,1,0:T(8,128)(2,1)S(1)} %shard_map.53), channel_id=1, source_target_pairs={{0,14},{1,15},{2,12},{3,13},{4,10},{5,11},{6,8},{7,9},{8,6},{9,7},... | collective-permute-start | bytes 589832 | tf_op jit(solution)/shard_map/ppermute | solution.py:23
  49.2 0.0 copy-start.1
  49.2 0.3 collective-permute-start.11
  49.5 0.0 collective-permute-done.9.refs_1_
  49.5 1.0 %shard_map.54 = (bf16[2,64,768]{2,1,0:T(8,128)(2,1)S(1)}, bf16[2,64,768]{2,1,0:T(8,128)(2,1)S(1)}) custom-call(bf16[2048,1536]{1,0:T(8,128)(2,1)S(1)} %shard_map.47.weights, bf16[64,2176]{1,0:T(8,128)(2,1)S(1)} %collective-permute-done.7.refs_0_, bf16[64,2176]{1,0:T(8,128)(2,1)S(1)} %collective-permute-done.9.refs_1_), custom_call_target="tpu_custom_call" | custom-call | flops 8053063680 | bytes 7208960 | tf_op jit(solution)/shard_map/pallas_call | solution.py:109
  50.5 0.3 collective-permute-start.13
  50.8 16.0 %collective-permute-done.11.refs_1_ = bf16[2,64,768]{2,1,0:T(8,128)(2,1)S(1)} collective-permute-done((bf16[2,64,768]{2,1,0:T(8,128)(2,1)S(1)}, bf16[2,64,768]{2,1,0:T(8,128)(2,1)S(1)}, u32[]{:S(2)}, u32[]{:S(2)}) %collective-permute-start.11) | collective-permute-done | bytes 196640 | tf_op jit(solution)/shard_map/ppermute | solution.py:23
  66.9 0.0 collective-permute-start.12
  66.9 0.0 collective-permute-done.14.refs_5_
  66.9 0.0 collective-permute-done.15.refs_6_
  66.9 0.0 collective-permute-done.13.refs_3_
  66.9 0.0 collective-permute-done.16.refs_7_
  66.9 6.7 %collective-permute-done.12.refs_2_ = bf16[2,64,768]{2,1,0:T(8,128)(2,1)S(1)} collective-permute-done((bf16[2,64,768]{2,1,0:T(8,128)(2,1)S(1)}, bf16[2,64,768]{2,1,0:T(8,128)(2,1)S(1)}, u32[]{:S(2)}, u32[]{:S(2)}) %collective-permute-start.12) | collective-permute-done | bytes 196640 | tf_op jit(solution)/shard_map/ppermute | solution.py:23
  73.6 0.0 copy-done.1
  73.6 1.3 %shard_map.55 = bf16[512,768]{1,0:T(8,128)(2,1)} custom-call(s32[8,64]{1,0:T(8,128)S(1)} %bitcast.10, bf16[2,64,768]{2,1,0:T(8,128)(2,1)S(1)} %get-tuple-element.38.refs_0_, bf16[2,64,768]{2,1,0:T(8,128)(2,1)S(1)} %collective-permute-done.11.refs_1_, bf16[2,64,768]{2,1,0:T(8,128)(2,1)S(1)} %collective-permute-done.12.refs_2_, ...), custom_call_target="tpu_custom_call" | custom-call | tf_op jit(solution)/shard_map/pallas_call | solution.py:144
  (2 shorter events, 0.0 us)
Async XLA Ops:
  0.0 7.1 %collective-permute-start.1 = (bf16[768,2048]{1,0:T(8,128)(2,1)}, bf16[768,2048]{1,0:T(8,128)(2,1)S(1)}, u32[]{:S(2)}, u32[]{:S(2)}) collective-permute-start(bf16[768,2048]{1,0:T(8,128)(2,1)} %bitcast.12), channel_id=1, source_target_pairs={{0,1},{1,0},{2,3},{3,2},{4,5},{5,4},{6,7},{7,6},{8,9},{9,8},{10,11... | collective-permute-start | bytes 9437192 | tf_op jit(solution)/shard_map/ppermute | solution.py:23
  0.5 10.8 %collective-permute-start = (bf16[64,2048]{1,0:T(8,128)(2,1)}, bf16[64,2048]{1,0:T(8,128)(2,1)S(1)}, u32[]{:S(2)}, u32[]{:S(2)}) collective-permute-start(bf16[64,2048]{1,0:T(8,128)(2,1)} %bitcast.14), channel_id=1, source_target_pairs={{0,16},{1,17},{2,18},{3,19},{4,20},{5,21},{6,22},{7,23},{8,24},{9,... | collective-permute-start | bytes 786440 | tf_op jit(solution)/shard_map/ppermute | solution.py:33
  3.0 16.6 %collective-permute-start.2 = (bf16[64,2048]{1,0:T(8,128)(2,1)}, bf16[64,2048]{1,0:T(8,128)(2,1)S(1)}, u32[]{:S(2)}, u32[]{:S(2)}) collective-permute-start(bf16[64,2048]{1,0:T(8,128)(2,1)} %bitcast.15), channel_id=1, source_target_pairs={{0,24},{1,25},{2,26},{3,27},{4,28},{5,29},{6,30},{7,31},{8,16},{9,... | collective-permute-start | bytes 786440 | tf_op jit(solution)/shard_map/ppermute | solution.py:33
  5.5 0.7 copy-start
  6.2 0.7 copy-start.2
  7.0 12.2 %collective-permute-start.3 = (bf16[64,128]{1,0:T(8,128)(2,1)S(1)}, bf16[64,128]{1,0:T(8,128)(2,1)S(1)}, u32[]{:S(2)}, u32[]{:S(2)}) collective-permute-start(bf16[64,128]{1,0:T(8,128)(2,1)S(1)} %shard_map.46.columns), channel_id=1, source_target_pairs={{0,8},{1,9},{2,10},{3,11},{4,12},{5,13},{6,14},{7,15},{8,0},{9,1},... | collective-permute-start | bytes 49160 | tf_op jit(solution)/shard_map/ppermute | solution.py:23
  7.1 1.9 %copy-start.3 = (bf16[1,1,768,2048]{3,2,1,0:T(8,128)(2,1)S(1)}, bf16[1,1,768,2048]{3,2,1,0:T(8,128)(2,1)}, u32[]{:S(2)}) copy-start(bf16[1,1,768,2048]{3,2,1,0:T(8,128)(2,1)} %param.7) | copy-start | bytes 9437188
  11.3 15.2 %collective-permute-start.8 = (bf16[64,2176]{1,0:T(8,128)(2,1)S(1)}, bf16[64,2176]{1,0:T(8,128)(2,1)S(1)}, u32[]{:S(2)}, u32[]{:S(2)}) collective-permute-start(bf16[64,2176]{1,0:T(8,128)(2,1)S(1)} %shard_map.48.refs_2_), channel_id=1, source_target_pairs={{0,2},{1,3},{2,0},{3,1},{4,6},{5,7},{6,4},{7,5},{8,10},{9,11},{10,... | collective-permute-start | bytes 835592 | tf_op jit(solution)/shard_map/ppermute | solution.py:23
  13.1 13.6 %collective-permute-start.7 = (bf16[64,2176]{1,0:T(8,128)(2,1)S(1)}, bf16[64,2176]{1,0:T(8,128)(2,1)S(1)}, u32[]{:S(2)}, u32[]{:S(2)}) collective-permute-start(bf16[64,2176]{1,0:T(8,128)(2,1)S(1)} %shard_map.48.refs_2_), channel_id=1, source_target_pairs={{0,4},{1,5},{2,6},{3,7},{4,0},{5,1},{6,2},{7,3},{8,12},{9,13},{10,... | collective-permute-start | bytes 835592 | tf_op jit(solution)/shard_map/ppermute | solution.py:23
  19.6 16.0 %collective-permute-start.6 = (bf16[64,2176]{1,0:T(8,128)(2,1)S(1)}, bf16[64,2176]{1,0:T(8,128)(2,1)S(1)}, u32[]{:S(2)}, u32[]{:S(2)}) collective-permute-start(bf16[64,2176]{1,0:T(8,128)(2,1)S(1)} %shard_map.49.refs_0_), channel_id=1, source_target_pairs={{0,4},{1,5},{2,6},{3,7},{4,0},{5,1},{6,2},{7,3},{8,12},{9,13},{10,... | collective-permute-start | bytes 835592 | tf_op jit(solution)/shard_map/ppermute | solution.py:23
  19.7 21.5 %collective-permute-start.4 = (bf16[64,2176]{1,0:T(8,128)(2,1)S(1)}, bf16[64,2176]{1,0:T(8,128)(2,1)S(1)}, u32[]{:S(2)}, u32[]{:S(2)}) collective-permute-start(bf16[64,2176]{1,0:T(8,128)(2,1)S(1)} %shard_map.49.refs_0_), channel_id=1, source_target_pairs={{0,2},{1,3},{2,0},{3,1},{4,6},{5,7},{6,4},{7,5},{8,10},{9,11},{10,... | collective-permute-start | bytes 835592 | tf_op jit(solution)/shard_map/ppermute | solution.py:23
  22.4 18.7 %collective-permute-start.5 = (bf16[2,64,768]{2,1,0:T(8,128)(2,1)S(1)}, bf16[2,64,768]{2,1,0:T(8,128)(2,1)S(1)}, u32[]{:S(2)}, u32[]{:S(2)}) collective-permute-start(bf16[2,64,768]{2,1,0:T(8,128)(2,1)S(1)} %shard_map.50), channel_id=1, source_target_pairs={{0,8},{1,9},{2,10},{3,11},{4,12},{5,13},{6,14},{7,15},{8,0},{9,1},... | collective-permute-start | bytes 589832 | tf_op jit(solution)/shard_map/ppermute | solution.py:23
  26.7 22.8 %collective-permute-start.9 = (bf16[64,2176]{1,0:T(8,128)(2,1)S(1)}, bf16[64,2176]{1,0:T(8,128)(2,1)S(1)}, u32[]{:S(2)}, u32[]{:S(2)}) collective-permute-start(bf16[64,2176]{1,0:T(8,128)(2,1)S(1)} %collective-permute-done.7.refs_0_), channel_id=1, source_target_pairs={{0,2},{1,3},{2,0},{3,1},{4,6},{5,7},{6,4},{7,5},{8,10},{9,11},{10,... | collective-permute-start | bytes 835592 | tf_op jit(solution)/shard_map/ppermute | solution.py:23
  35.6 7.4 %collective-permute-start.10 = (bf16[64,2176]{1,0:T(8,128)(2,1)S(1)}, bf16[64,2176]{1,0:T(8,128)(2,1)S(1)}, u32[]{:S(2)}, u32[]{:S(2)}) collective-permute-start(bf16[64,2176]{1,0:T(8,128)(2,1)S(1)} %collective-permute-done.6.refs_0_), channel_id=1, source_target_pairs={{0,2},{1,3},{2,0},{3,1},{4,6},{5,7},{6,4},{7,5},{8,10},{9,11},{10,... | collective-permute-start | bytes 835592 | tf_op jit(solution)/shard_map/ppermute | solution.py:23
  37.7 29.2 %collective-permute-start.15 = (bf16[2,64,768]{2,1,0:T(8,128)(2,1)S(1)}, bf16[2,64,768]{2,1,0:T(8,128)(2,1)S(1)}, u32[]{:S(2)}, u32[]{:S(2)}) collective-permute-start(bf16[2,64,768]{2,1,0:T(8,128)(2,1)S(1)} %shard_map.51), channel_id=1, source_target_pairs={{0,12},{1,13},{2,14},{3,15},{4,8},{5,9},{6,10},{7,11},{8,4},{9,5},... | collective-permute-start | bytes 589832 | tf_op jit(solution)/shard_map/ppermute | solution.py:23
  42.6 24.3 %collective-permute-start.14 = (bf16[2,64,768]{2,1,0:T(8,128)(2,1)S(1)}, bf16[2,64,768]{2,1,0:T(8,128)(2,1)S(1)}, u32[]{:S(2)}, u32[]{:S(2)}) collective-permute-start(bf16[2,64,768]{2,1,0:T(8,128)(2,1)S(1)} %get-tuple-element.39), channel_id=1, source_target_pairs={{0,10},{1,11},{2,8},{3,9},{4,14},{5,15},{6,12},{7,13},{8,2},{9,3},... | collective-permute-start | bytes 589832 | tf_op jit(solution)/shard_map/ppermute | solution.py:23
  44.2 22.7 %collective-permute-start.16 = (bf16[2,64,768]{2,1,0:T(8,128)(2,1)S(1)}, bf16[2,64,768]{2,1,0:T(8,128)(2,1)S(1)}, u32[]{:S(2)}, u32[]{:S(2)}) collective-permute-start(bf16[2,64,768]{2,1,0:T(8,128)(2,1)S(1)} %shard_map.53), channel_id=1, source_target_pairs={{0,14},{1,15},{2,12},{3,13},{4,10},{5,11},{6,8},{7,9},{8,6},{9,7},... | collective-permute-start | bytes 589832 | tf_op jit(solution)/shard_map/ppermute | solution.py:23
  49.2 24.4 %copy-start.1 = (s32[1,64,8]{1,2,0:T(8,128)S(1)}, s32[1,64,8]{1,2,0:T(8,128)}, u32[]{:S(2)}) copy-start(s32[1,64,8]{1,2,0:T(8,128)} %param.5) | copy-start | bytes 6148
  49.2 17.7 %collective-permute-start.11 = (bf16[2,64,768]{2,1,0:T(8,128)(2,1)S(1)}, bf16[2,64,768]{2,1,0:T(8,128)(2,1)S(1)}, u32[]{:S(2)}, u32[]{:S(2)}) collective-permute-start(bf16[2,64,768]{2,1,0:T(8,128)(2,1)S(1)} %get-tuple-element.44), channel_id=1, source_target_pairs={{0,2},{1,3},{2,0},{3,1},{4,6},{5,7},{6,4},{7,5},{8,10},{9,11},{10,... | collective-permute-start | bytes 589832 | tf_op jit(solution)/shard_map/ppermute | solution.py:23
  50.5 16.4 %collective-permute-start.13 = (bf16[2,64,768]{2,1,0:T(8,128)(2,1)S(1)}, bf16[2,64,768]{2,1,0:T(8,128)(2,1)S(1)}, u32[]{:S(2)}, u32[]{:S(2)}) collective-permute-start(bf16[2,64,768]{2,1,0:T(8,128)(2,1)S(1)} %get-tuple-element.47), channel_id=1, source_target_pairs={{0,6},{1,7},{2,4},{3,5},{4,2},{5,3},{6,0},{7,1},{8,14},{9,15},{10,... | collective-permute-start | bytes 589832 | tf_op jit(solution)/shard_map/ppermute | solution.py:23
  66.9 6.8 %collective-permute-start.12 = (bf16[2,64,768]{2,1,0:T(8,128)(2,1)S(1)}, bf16[2,64,768]{2,1,0:T(8,128)(2,1)S(1)}, u32[]{:S(2)}, u32[]{:S(2)}) collective-permute-start(bf16[2,64,768]{2,1,0:T(8,128)(2,1)S(1)} %get-tuple-element.46), channel_id=1, source_target_pairs={{0,4},{1,5},{2,6},{3,7},{4,0},{5,1},{6,2},{7,3},{8,12},{9,13},{10,... | collective-permute-start | bytes 589832 | tf_op jit(solution)/shard_map/ppermute | solution.py:23

commit v25 on v21

--- a/solution.py
+++ b/solution.py
@@ -118,40 +118,81 @@
     )(weights, *pieces)
 
 
+def group_kernel(flips, weights, *refs):
+    pieces, out = refs[: len(flips)], refs[len(flips)]
+    depth, width = weights.shape
+    hidden = width // CORES
+    tokens = out.shape[2]
+    me = lax.axis_index("expert")
+    core, chip = lax.rem(me, CORES), lax.div(me, CORES)
+    stacked = jnp.concatenate([p[...] for p in pieces], axis=0)
+    gates = stacked[:, depth:].astype(jnp.float32)
+    column = lax.broadcasted_iota(jnp.int32, gates.shape, 1)
+    product = jnp.dot(stacked[:, :depth], weights[...], preferred_element_type=jnp.float32)
+    for half, to in enumerate((core, 1 - core)):
+        scale = jnp.sum(jnp.where(column == me - core + to, gates, 0.0), axis=1, keepdims=True)
+        scaled = (product[:, half * hidden : (half + 1) * hidden] * scale).astype(jnp.bfloat16)
+        for j, flip in enumerate(flips):
+            slot = lax.rem(chip, len(flips)) ^ flip
+            out[slot, to] = scaled[j * tokens : (j + 1) * tokens]
+
+
+def group_results(pieces, tokens, weights):
+    flips = sorted(pieces)
+    depth, width = weights.shape
+    shape = (len(flips), CORES, tokens, width // CORES)
+    return pl.pallas_call(
+        functools.partial(group_kernel, flips),
+        out_shape=jax.ShapeDtypeStruct(shape, jnp.bfloat16),
+        compiler_params=pltpu.CompilerParams(vmem_limit_bytes=16 << 20),
+        cost_estimate=pl.CostEstimate(
+            flops=20 * len(flips) * tokens * width * depth,
+            bytes_accessed=2 * (len(flips) * tokens * (width + depth) + width * depth),
+            transcendentals=0,
+        ),
+    )(weights, *[pieces[flip] for flip in flips])
+
+
 def pick_kernel(flips, ids, *refs):
-    blocks, kept, out = refs[: len(flips)], refs[len(flips) : -1], refs[-1]
-    experts, tokens, _ = blocks[0].shape
-    top = ids.shape[0]
+    count = len(flips) or 1
+    blocks, kept, out = refs[:count], refs[count:-1], refs[-1]
+    top, tokens = ids.shape
     span = 16
     chip = lax.div(lax.axis_index("expert"), CORES)
-    flip = lax.div(ids[...], CORES) ^ chip
-    place = jnp.full(flip.shape, -1, jnp.int32)
-    for j, known in enumerate(flips):
-        place = jnp.where(flip == known, j * CORES + lax.rem(ids[...], CORES), place)
-    column = lax.broadcasted_iota(jnp.int32, (top, len(blocks) * experts * span), 1)
+    owner, core = lax.div(ids[...], CORES), lax.rem(ids[...], CORES)
+    if flips:
+        parts = [(b, (c,)) for b in blocks for c in range(CORES)]
+        place = jnp.full(owner.shape, -1, jnp.int32)
+        for j, flip in enumerate(flips):
+            place = jnp.where((owner ^ chip) == flip, j * CORES + core, place)
+    else:
+        size = blocks[0].shape[0]
+        parts = [(blocks[0], (j, c)) for j in range(size) for c in range(CORES)]
+        mine = lax.div(owner, size) == lax.div(chip, size)
+        place = jnp.where(mine, lax.rem(owner, size) * CORES + core, -1)
+    column = lax.broadcasted_iota(jnp.int32, (top, len(parts) * span), 1)
     for g in range(tokens // span):
-        stacked = jnp.concatenate(
-            [b[c, g * span : (g + 1) * span, :] for b in blocks for c in range(experts)], axis=0
-        )
+        rows = slice(g * span, (g + 1) * span)
+        stacked = jnp.concatenate([b[(*at, rows)] for b, at in parts], axis=0)
         picks = [
             jnp.where(column == place[:, g * span + t : g * span + t + 1] * span + t, 1.0, 0.0)
             for t in range(span)
         ]
         pick = jnp.concatenate(picks, axis=0).astype(jnp.bfloat16)
-        rows = jnp.dot(pick, stacked, preferred_element_type=jnp.float32).astype(jnp.bfloat16)
-        part = slice(g * span * top, (g + 1) * span * top)
-        out[part, :] = rows + kept[0][part, :] if kept else rows
-
-
-def pick_routes(ids, received, *kept):
+        found = jnp.dot(pick, stacked, preferred_element_type=jnp.float32).astype(jnp.bfloat16)
+        routes = slice(g * span * top, (g + 1) * span * top)
+        out[routes, :] = found + kept[0][routes, :] if kept else found
+
+
+def pick_routes(ids, blocks, *kept):
     top, tokens = ids.shape
-    flips = sorted(received)
-    blocks = [received[flip] for flip in flips]
+    flips = sorted(blocks) if isinstance(blocks, dict) else []
+    arrays = [blocks[flip] for flip in flips] if flips else [blocks]
     return pl.pallas_call(
         functools.partial(pick_kernel, flips),
-        out_shape=jax.ShapeDtypeStruct((top * tokens, blocks[0].shape[2]), jnp.bfloat16),
-        compiler_params=pltpu.CompilerParams(vmem_limit_bytes=16 << 20),
-    )(ids, *blocks, *kept)
+        out_shape=jax.ShapeDtypeStruct((top * tokens, arrays[0].shape[-1]), jnp.bfloat16),
+        compiler_params=pltpu.CompilerParams(vmem_limit_bytes=16 << 20),
+    )(ids, *arrays, *kept)
 
 
 def dense_device(upstream, route_ids, route_gates, weight_mat):
@@ -179,33 +220,42 @@
     (out_far,) = work(far)
     back_far = send(out_far, owners, Z_FAR)
     side, _ = tie((side, out_far))
-    out_side, out_own = work(side, rows)
-    back_side = send(out_side, owners, X)
-    near, _ = tie((near, out_side))
+    near, side = tie((near, side))
     near_side = send(near, owners, X)
     cross, _ = tie((cross, near))
     cross_side = send(cross, owners, X)
     (out_cross,) = work(cross)
     back_cross = send(out_cross, owners, Z_NEAR ^ Z_FAR)
-    far_side, back_far, back_side, _ = tie((far_side, back_far, back_side, out_cross))
+    far_side, back_far, _ = tie((far_side, back_far, out_cross))
     (out_far_side,) = work(far_side)
     back_far_side = send(out_far_side, owners, X ^ Z_FAR)
     cross_side, _ = tie((cross_side, out_far_side))
     (out_cross_side,) = work(cross_side)
     back_cross_side = send(out_cross_side, owners, X ^ Z_NEAR ^ Z_FAR)
-    near_side, _ = tie((near_side, out_cross_side))
-    out_near, out_near_side = work(near, near_side)
-    back_near_side = send(out_near_side, owners, X ^ Z_NEAR)
-    back_near = send(out_near, owners, Z_NEAR)
+    near_side, rows, _ = tie((near_side, rows, out_cross_side))
+    family = {0: rows, X: side, Z_NEAR: near, X ^ Z_NEAR: near_side}
+    found = group_results(family, tokens, weights)
+    span = Z_FAR * CORES
+    groups = [
+        [first + core + CORES * j for j in range(Z_FAR)]
+        for first in range(0, owners, span)
+        for core in range(CORES)
+    ]
+    back_near = lax.all_to_all(
+        found.reshape(Z_FAR, CORES * tokens, found.shape[3]),
+        "expert",
+        split_axis=0,
+        concat_axis=0,
+        tiled=True,
+        axis_index_groups=groups,
+    ).reshape(found.shape)
     far_parts = {
-        0: out_own,
         Z_FAR: back_far,
         X ^ Z_FAR: back_far_side,
         Z_NEAR ^ Z_FAR: back_cross,
         X ^ Z_NEAR ^ Z_FAR: back_cross_side,
     }
-    near_parts = {X: back_side, Z_NEAR: back_near, X ^ Z_NEAR: back_near_side}
-    out = pick_routes(route_ids.T, near_parts, pick_routes(route_ids.T, far_parts))
+    out = pick_routes(route_ids.T, far_parts, pick_routes(route_ids.T, back_near))
     return out.reshape(1, tokens, top, weight_mat.shape[0])
 
 

time: 68.9 us -> 80.1 us (1.16)
  the two profiles are of different devices: /device:TPU:0 before, /device:TPU:16 now
where the time goes in v25:
time: 80.1 us; the launch traced here: 79.8 us
  waiting for transfers between devices  43.1 us (54%)
  starting transfers between devices  22.3 us (28%)
  Pallas kernels  11 us (14%)
  local copies, waits for them, and re-layouts  3.26 us (4%)
    ppermute x12, waiting for transfers between devices, send(): return lax.ppermute(block, 'expert', route)  22.5 us
    ppermute x12, starting transfers between devices, send(): return lax.ppermute(block, 'expert', route)  15.9 us
    all_to_all x1, waiting for transfers between devices, dense_device(): lax.all_to_all(found.reshape(Z_FAR, CORES * tokens, found.shape[3]), 'exp...  15.6 us
    ppermute x2, waiting for transfers between devices, send_across(): return lax.ppermute(block, ('pipe', 'expert'), route)  5.08 us
    all_to_all x1, starting transfers between devices, dense_device(): lax.all_to_all(found.reshape(Z_FAR, CORES * tokens, found.shape[3]), 'exp...  4.89 us
    pallas_call x4, Pallas kernels, products(): pl.pallas_call(functools.partial(products_kernel, len(pieces)), out_shape...  4.77 us
    unnamed x8, local copies, waits for them, and re-layouts  3.26 us
    pallas_call x1, Pallas kernels, group_results(): pl.pallas_call(functools.partial(group_kernel, flips), out_shape=jax.Shap...  2.68 us
  transfers between devices with their start and end apart: 15, of which 8 were waited for; matrix products, arithmetic and copies ran while one was open for 0% of the time, Pallas kernels for 9%

profile of v25, /device:TPU:16, one launch (start us, length us, event | category | flops | bytes accessed | tf_op | source)
XLA Modules:
  0.0 79.8 jit_solution(12826108934260853872)
XLA Ops:
  0.0 0.0 collective-permute-start.3
  0.0 1.5 %collective-permute-start.2 = (bf16[64,2048]{1,0:T(8,128)(2,1)}, bf16[64,2048]{1,0:T(8,128)(2,1)S(1)}, u32[]{:S(2)}, u32[]{:S(2)}) collective-permute-start(bf16[64,2048]{1,0:T(8,128)(2,1)} %bitcast.18), channel_id=1, source_target_pairs={{0,16},{1,17},{2,18},{3,19},{4,20},{5,21},{6,22},{7,23},{8,24},{9,... | collective-permute-start | bytes 786440 | tf_op jit(solution)/shard_map/ppermute | solution.py:33
  1.5 0.0 collective-permute-start
  1.5 0.0 copy-start
  1.5 0.7 copy-done
  2.2 0.0 copy-start.2
  2.2 0.7 copy-done.2
  2.9 0.1 shard_map.46.columns
  3.0 2.9 %collective-permute-start.1 = (bf16[64,128]{1,0:T(8,128)(2,1)S(1)}, bf16[64,128]{1,0:T(8,128)(2,1)S(1)}, u32[]{:S(2)}, u32[]{:S(2)}) collective-permute-start(bf16[64,128]{1,0:T(8,128)(2,1)S(1)} %shard_map.46.columns), channel_id=1, source_target_pairs={{0,8},{1,9},{2,10},{3,11},{4,12},{5,13},{6,14},{7,15},{8,0},{9,1},... | collective-permute-start | bytes 49160 | tf_op jit(solution)/shard_map/ppermute | solution.py:23
  5.9 0.0 collective-permute-done.3.other
  5.9 0.0 copy-start.3
  5.9 1.9 %copy-done.3 = bf16[1,1,768,2048]{3,2,1,0:T(8,128)(2,1)S(1)} copy-done((bf16[1,1,768,2048]{3,2,1,0:T(8,128)(2,1)S(1)}, bf16[1,1,768,2048]{3,2,1,0:T(8,128)(2,1)}, u32[]{:S(2)}) %copy-start.3) | copy-done | bytes 3145752
  7.8 1.7 %shard_map.47.weights = bf16[2048,1536]{1,0:T(8,128)(2,1)S(1)} custom-call(bf16[768,2048]{1,0:T(8,128)(2,1)S(1)} %bitcast.17, bf16[768,2048]{1,0:T(8,128)(2,1)S(1)} %collective-permute-done.3.other), custom_call_target="tpu_custom_call" | custom-call | flops 12884901888 | tf_op jit(solution)/shard_map/pallas_call | solution.py:77
  9.5 5.1 %collective-permute-done.2.rows = bf16[64,2048]{1,0:T(8,128)(2,1)S(1)} collective-permute-done((bf16[64,2048]{1,0:T(8,128)(2,1)}, bf16[64,2048]{1,0:T(8,128)(2,1)S(1)}, u32[]{:S(2)}, u32[]{:S(2)}) %collective-permute-start.2) | collective-permute-done | bytes 262176 | tf_op jit(solution)/shard_map/ppermute | solution.py:33
  14.6 1.6 %collective-permute-start.8 = (bf16[64,2176]{1,0:T(8,128)(2,1)S(1)}, bf16[64,2176]{1,0:T(8,128)(2,1)S(1)}, u32[]{:S(2)}, u32[]{:S(2)}) collective-permute-start(bf16[64,2176]{1,0:T(8,128)(2,1)S(1)} %shard_map.48.refs_0_), channel_id=1, source_target_pairs={{0,2},{1,3},{2,0},{3,1},{4,6},{5,7},{6,4},{7,5},{8,10},{9,11},{10,... | collective-permute-start | bytes 835592 | tf_op jit(solution)/shard_map/ppermute | solution.py:23
  16.1 0.0 collective-permute-start.7
  16.1 0.0 collective-permute-done.1.columns
  16.1 0.0 collective-permute-done.rows
  16.2 3.4 %collective-permute-start.6 = (bf16[64,2176]{1,0:T(8,128)(2,1)S(1)}, bf16[64,2176]{1,0:T(8,128)(2,1)S(1)}, u32[]{:S(2)}, u32[]{:S(2)}) collective-permute-start(bf16[64,2176]{1,0:T(8,128)(2,1)S(1)} %shard_map.49.refs_0_), channel_id=1, source_target_pairs={{0,4},{1,5},{2,6},{3,7},{4,0},{5,1},{6,2},{7,3},{8,12},{9,13},{10,... | collective-permute-start | bytes 835592 | tf_op jit(solution)/shard_map/ppermute | solution.py:23
  19.6 1.6 %collective-permute-start.4 = (bf16[64,2176]{1,0:T(8,128)(2,1)S(1)}, bf16[64,2176]{1,0:T(8,128)(2,1)S(1)}, u32[]{:S(2)}, u32[]{:S(2)}) collective-permute-start(bf16[64,2176]{1,0:T(8,128)(2,1)S(1)} %shard_map.49.refs_0_), channel_id=1, source_target_pairs={{0,2},{1,3},{2,0},{3,1},{4,6},{5,7},{6,4},{7,5},{8,10},{9,11},{10,... | collective-permute-start | bytes 835592 | tf_op jit(solution)/shard_map/ppermute | solution.py:23
  21.1 1.2 %shard_map.50 = bf16[2,64,768]{2,1,0:T(8,128)(2,1)S(1)} custom-call(bf16[2048,1536]{1,0:T(8,128)(2,1)S(1)} %shard_map.47.weights, bf16[64,2176]{1,0:T(8,128)(2,1)S(1)} %shard_map.49.refs_0_), custom_call_target="tpu_custom_call" | custom-call | flops 4026531840 | bytes 6750208 | tf_op jit(solution)/shard_map/pallas_call | solution.py:109
  22.3 0.1 collective-permute-start.5
  22.4 1.5 %collective-permute-done.8.refs_1_ = bf16[64,2176]{1,0:T(8,128)(2,1)S(1)} collective-permute-done((bf16[64,2176]{1,0:T(8,128)(2,1)S(1)}, bf16[64,2176]{1,0:T(8,128)(2,1)S(1)}, u32[]{:S(2)}, u32[]{:S(2)}) %collective-permute-start.8) | collective-permute-done | bytes 278560 | tf_op jit(solution)/shard_map/ppermute | solution.py:23
  23.9 1.8 %collective-permute-done.7.refs_2_ = bf16[64,2176]{1,0:T(8,128)(2,1)S(1)} collective-permute-done((bf16[64,2176]{1,0:T(8,128)(2,1)S(1)}, bf16[64,2176]{1,0:T(8,128)(2,1)S(1)}, u32[]{:S(2)}, u32[]{:S(2)}) %collective-permute-start.7) | collective-permute-done | bytes 278560 | tf_op jit(solution)/shard_map/ppermute | solution.py:23
  25.7 0.5 collective-permute-start.13
  26.3 6.2 %collective-permute-done.6.refs_0_ = bf16[64,2176]{1,0:T(8,128)(2,1)S(1)} collective-permute-done((bf16[64,2176]{1,0:T(8,128)(2,1)S(1)}, bf16[64,2176]{1,0:T(8,128)(2,1)S(1)}, u32[]{:S(2)}, u32[]{:S(2)}) %collective-permute-start.6) | collective-permute-done | bytes 278560 | tf_op jit(solution)/shard_map/ppermute | solution.py:23
  32.5 1.5 %collective-permute-start.11 = (bf16[64,2176]{1,0:T(8,128)(2,1)S(1)}, bf16[64,2176]{1,0:T(8,128)(2,1)S(1)}, u32[]{:S(2)}, u32[]{:S(2)}) collective-permute-start(bf16[64,2176]{1,0:T(8,128)(2,1)S(1)} %collective-permute-done.6.refs_0_), channel_id=1, source_target_pairs={{0,2},{1,3},{2,0},{3,1},{4,6},{5,7},{6,4},{7,5},{8,10},{9,11},{10,... | collective-permute-start | bytes 835592 | tf_op jit(solution)/shard_map/ppermute | solution.py:23
  34.0 1.2 %shard_map.51 = bf16[2,64,768]{2,1,0:T(8,128)(2,1)S(1)} custom-call(bf16[2048,1536]{1,0:T(8,128)(2,1)S(1)} %shard_map.47.weights, bf16[64,2176]{1,0:T(8,128)(2,1)S(1)} %collective-permute-done.6.refs_0_), custom_call_target="tpu_custom_call" | custom-call | flops 4026531840 | bytes 6750208 | tf_op jit(solution)/shard_map/pallas_call | solution.py:109
  35.2 0.0 collective-permute-done.5.refs_0_
  35.2 0.0 collective-permute-done.4.refs_0_
  35.2 1.2 %shard_map.52 = bf16[2,64,768]{2,1,0:T(8,128)(2,1)S(1)} custom-call(bf16[2048,1536]{1,0:T(8,128)(2,1)S(1)} %shard_map.47.weights, bf16[64,2176]{1,0:T(8,128)(2,1)S(1)} %collective-permute-done.4.refs_0_), custom_call_target="tpu_custom_call" | custom-call | flops 4026531840 | bytes 6750208 | tf_op jit(solution)/shard_map/pallas_call | solution.py:109
  36.4 4.5 %collective-permute-done.11.refs_0_ = bf16[64,2176]{1,0:T(8,128)(2,1)S(1)} collective-permute-done((bf16[64,2176]{1,0:T(8,128)(2,1)S(1)}, bf16[64,2176]{1,0:T(8,128)(2,1)S(1)}, u32[]{:S(2)}, u32[]{:S(2)}) %collective-permute-start.11) | collective-permute-done | bytes 278560 | tf_op jit(solution)/shard_map/ppermute | solution.py:23
  40.8 1.2 %shard_map.53 = bf16[2,64,768]{2,1,0:T(8,128)(2,1)S(1)} custom-call(bf16[2048,1536]{1,0:T(8,128)(2,1)S(1)} %shard_map.47.weights, bf16[64,2176]{1,0:T(8,128)(2,1)S(1)} %collective-permute-done.11.refs_0_), custom_call_target="tpu_custom_call" | custom-call | flops 4026531840 | bytes 6750208 | tf_op jit(solution)/shard_map/pallas_call | solution.py:109
  42.0 0.0 copy-start.1
  42.0 0.0 collective-permute-done.13.refs_3_
  42.1 2.7 %shard_map.54 = bf16[4,2,64,768]{3,2,1,0:T(8,128)(2,1)} custom-call(bf16[2048,1536]{1,0:T(8,128)(2,1)S(1)} %shard_map.47.weights, bf16[64,2176]{1,0:T(8,128)(2,1)S(1)} %shard_map.48.refs_0_, bf16[64,2176]{1,0:T(8,128)(2,1)S(1)} %collective-permute-done.8.refs_1_, bf16[64,2176]{1,0:T(8,128)(2,1)S(1)} %collective-permute-done.7.refs_2_, ...), custom_call_target="tpu_custom_call" | custom-call | flops 16106127360 | bytes 8126464 | tf_op jit(solution)/shard_map/pallas_call | solution.py:144
  44.7 4.9 %all-to-all-start = ((bf16[4,128,768]{2,1,0:T(8,128)(2,1)}), bf16[4,128,768]{2,1,0:T(8,128)(2,1)S(1)}, u32[]{:S(2)}, u32[]{:S(2)}) async-start(bf16[4,128,768]{2,1,0:T(8,128)(2,1)} %bitcast.7), calls=%async_computation | async-start | bytes 1572864 | tf_op jit(solution)/shard_map/all_to_all | solution.py:244
  49.6 1.1 %collective-permute-start.9 = (bf16[2,64,768]{2,1,0:T(8,128)(2,1)S(1)}, bf16[2,64,768]{2,1,0:T(8,128)(2,1)S(1)}, u32[]{:S(2)}, u32[]{:S(2)}) collective-permute-start(bf16[2,64,768]{2,1,0:T(8,128)(2,1)S(1)} %shard_map.52), channel_id=1, source_target_pairs={{0,10},{1,11},{2,8},{3,9},{4,14},{5,15},{6,12},{7,13},{8,2},{9,3},... | collective-permute-start | bytes 589832 | tf_op jit(solution)/shard_map/ppermute | solution.py:23
  50.7 3.3 %collective-permute-start.10 = (bf16[2,64,768]{2,1,0:T(8,128)(2,1)S(1)}, bf16[2,64,768]{2,1,0:T(8,128)(2,1)S(1)}, u32[]{:S(2)}, u32[]{:S(2)}) collective-permute-start(bf16[2,64,768]{2,1,0:T(8,128)(2,1)S(1)} %shard_map.51), channel_id=1, source_target_pairs={{0,12},{1,13},{2,14},{3,15},{4,8},{5,9},{6,10},{7,11},{8,4},{9,5},... | collective-permute-start | bytes 589832 | tf_op jit(solution)/shard_map/ppermute | solution.py:23
  54.0 0.0 collective-permute-start.12
  54.0 15.6 %all-to-all-done = bf16[4,128,768]{2,1,0:T(8,128)(2,1)S(1)} async-done(((bf16[4,128,768]{2,1,0:T(8,128)(2,1)}), bf16[4,128,768]{2,1,0:T(8,128)(2,1)S(1)}, u32[]{:S(2)}, u32[]{:S(2)}) %all-to-all-start) | async-done | bytes 786464 | tf_op jit(solution)/shard_map/all_to_all | solution.py:244
  69.6 0.0 copy-done.1
  69.6 0.4 shard_map.55.refs_4_
  70.0 0.0 collective-permute-done.9.refs_1_
  70.0 6.1 %collective-permute-done.10.refs_2_ = bf16[2,64,768]{2,1,0:T(8,128)(2,1)S(1)} collective-permute-done((bf16[2,64,768]{2,1,0:T(8,128)(2,1)S(1)}, bf16[2,64,768]{2,1,0:T(8,128)(2,1)S(1)}, u32[]{:S(2)}, u32[]{:S(2)}) %collective-permute-start.10) | collective-permute-done | bytes 196640 | tf_op jit(solution)/shard_map/ppermute | solution.py:23
  76.1 2.5 %collective-permute-done.12.refs_3_ = bf16[2,64,768]{2,1,0:T(8,128)(2,1)S(1)} collective-permute-done((bf16[2,64,768]{2,1,0:T(8,128)(2,1)S(1)}, bf16[2,64,768]{2,1,0:T(8,128)(2,1)S(1)}, u32[]{:S(2)}, u32[]{:S(2)}) %collective-permute-start.12) | collective-permute-done | bytes 196640 | tf_op jit(solution)/shard_map/ppermute | solution.py:23
  78.5 1.3 %shard_map.56 = bf16[512,768]{1,0:T(8,128)(2,1)} custom-call(s32[8,64]{1,0:T(8,128)S(1)} %bitcast.14, bf16[2,64,768]{2,1,0:T(8,128)(2,1)S(1)} %collective-permute-done.5.refs_0_, bf16[2,64,768]{2,1,0:T(8,128)(2,1)S(1)} %collective-permute-done.9.refs_1_, bf16[2,64,768]{2,1,0:T(8,128)(2,1)S(1)} %collective-permute-done.10.refs_2_, ...), custom_call_target="tpu_custom_call" | custom-call | tf_op jit(solution)/shard_map/pallas_call | solution.py:191
  (2 shorter events, 0.0 us)
Async XLA Ops:
  0.0 5.9 %collective-permute-start.3 = (bf16[768,2048]{1,0:T(8,128)(2,1)}, bf16[768,2048]{1,0:T(8,128)(2,1)S(1)}, u32[]{:S(2)}, u32[]{:S(2)}) collective-permute-start(bf16[768,2048]{1,0:T(8,128)(2,1)} %bitcast.16), channel_id=1, source_target_pairs={{0,1},{1,0},{2,3},{3,2},{4,5},{5,4},{6,7},{7,6},{8,9},{9,8},{10,11... | collective-permute-start | bytes 9437192 | tf_op jit(solution)/shard_map/ppermute | solution.py:23
  0.0 14.5 %collective-permute-start.2 = (bf16[64,2048]{1,0:T(8,128)(2,1)}, bf16[64,2048]{1,0:T(8,128)(2,1)S(1)}, u32[]{:S(2)}, u32[]{:S(2)}) collective-permute-start(bf16[64,2048]{1,0:T(8,128)(2,1)} %bitcast.18), channel_id=1, source_target_pairs={{0,16},{1,17},{2,18},{3,19},{4,20},{5,21},{6,22},{7,23},{8,24},{9,... | collective-permute-start | bytes 786440 | tf_op jit(solution)/shard_map/ppermute | solution.py:33
  1.5 14.6 %collective-permute-start = (bf16[64,2048]{1,0:T(8,128)(2,1)}, bf16[64,2048]{1,0:T(8,128)(2,1)S(1)}, u32[]{:S(2)}, u32[]{:S(2)}) collective-permute-start(bf16[64,2048]{1,0:T(8,128)(2,1)} %bitcast.19), channel_id=1, source_target_pairs={{0,24},{1,25},{2,26},{3,27},{4,28},{5,29},{6,30},{7,31},{8,16},{9,... | collective-permute-start | bytes 786440 | tf_op jit(solution)/shard_map/ppermute | solution.py:33
  1.5 0.7 copy-start
  2.2 0.7 copy-start.2
  3.0 13.1 %collective-permute-start.1 = (bf16[64,128]{1,0:T(8,128)(2,1)S(1)}, bf16[64,128]{1,0:T(8,128)(2,1)S(1)}, u32[]{:S(2)}, u32[]{:S(2)}) collective-permute-start(bf16[64,128]{1,0:T(8,128)(2,1)S(1)} %shard_map.46.columns), channel_id=1, source_target_pairs={{0,8},{1,9},{2,10},{3,11},{4,12},{5,13},{6,14},{7,15},{8,0},{9,1},... | collective-permute-start | bytes 49160 | tf_op jit(solution)/shard_map/ppermute | solution.py:23
  5.9 1.9 %copy-start.3 = (bf16[1,1,768,2048]{3,2,1,0:T(8,128)(2,1)S(1)}, bf16[1,1,768,2048]{3,2,1,0:T(8,128)(2,1)}, u32[]{:S(2)}) copy-start(bf16[1,1,768,2048]{3,2,1,0:T(8,128)(2,1)} %param.7) | copy-start | bytes 9437188
  14.6 9.4 %collective-permute-start.8 = (bf16[64,2176]{1,0:T(8,128)(2,1)S(1)}, bf16[64,2176]{1,0:T(8,128)(2,1)S(1)}, u32[]{:S(2)}, u32[]{:S(2)}) collective-permute-start(bf16[64,2176]{1,0:T(8,128)(2,1)S(1)} %shard_map.48.refs_0_), channel_id=1, source_target_pairs={{0,2},{1,3},{2,0},{3,1},{4,6},{5,7},{6,4},{7,5},{8,10},{9,11},{10,... | collective-permute-start | bytes 835592 | tf_op jit(solution)/shard_map/ppermute | solution.py:23
  16.1 9.6 %collective-permute-start.7 = (bf16[64,2176]{1,0:T(8,128)(2,1)S(1)}, bf16[64,2176]{1,0:T(8,128)(2,1)S(1)}, u32[]{:S(2)}, u32[]{:S(2)}) collective-permute-start(bf16[64,2176]{1,0:T(8,128)(2,1)S(1)} %shard_map.48.refs_0_), channel_id=1, source_target_pairs={{0,4},{1,5},{2,6},{3,7},{4,0},{5,1},{6,2},{7,3},{8,12},{9,13},{10,... | collective-permute-start | bytes 835592 | tf_op jit(solution)/shard_map/ppermute | solution.py:23
  16.2 16.3 %collective-permute-start.6 = (bf16[64,2176]{1,0:T(8,128)(2,1)S(1)}, bf16[64,2176]{1,0:T(8,128)(2,1)S(1)}, u32[]{:S(2)}, u32[]{:S(2)}) collective-permute-start(bf16[64,2176]{1,0:T(8,128)(2,1)S(1)} %shard_map.49.refs_0_), channel_id=1, source_target_pairs={{0,4},{1,5},{2,6},{3,7},{4,0},{5,1},{6,2},{7,3},{8,12},{9,13},{10,... | collective-permute-start | bytes 835592 | tf_op jit(solution)/shard_map/ppermute | solution.py:23
  19.6 15.6 %collective-permute-start.4 = (bf16[64,2176]{1,0:T(8,128)(2,1)S(1)}, bf16[64,2176]{1,0:T(8,128)(2,1)S(1)}, u32[]{:S(2)}, u32[]{:S(2)}) collective-permute-start(bf16[64,2176]{1,0:T(8,128)(2,1)S(1)} %shard_map.49.refs_0_), channel_id=1, source_target_pairs={{0,2},{1,3},{2,0},{3,1},{4,6},{5,7},{6,4},{7,5},{8,10},{9,11},{10,... | collective-permute-start | bytes 835592 | tf_op jit(solution)/shard_map/ppermute | solution.py:23
  22.3 12.8 %collective-permute-start.5 = (bf16[2,64,768]{2,1,0:T(8,128)(2,1)S(1)}, bf16[2,64,768]{2,1,0:T(8,128)(2,1)S(1)}, u32[]{:S(2)}, u32[]{:S(2)}) collective-permute-start(bf16[2,64,768]{2,1,0:T(8,128)(2,1)S(1)} %shard_map.50), channel_id=1, source_target_pairs={{0,8},{1,9},{2,10},{3,11},{4,12},{5,13},{6,14},{7,15},{8,0},{9,1},... | collective-permute-start | bytes 589832 | tf_op jit(solution)/shard_map/ppermute | solution.py:23
  25.7 16.3 %collective-permute-start.13 = (bf16[64,2176]{1,0:T(8,128)(2,1)S(1)}, bf16[64,2176]{1,0:T(8,128)(2,1)S(1)}, u32[]{:S(2)}, u32[]{:S(2)}) collective-permute-start(bf16[64,2176]{1,0:T(8,128)(2,1)S(1)} %collective-permute-done.7.refs_2_), channel_id=1, source_target_pairs={{0,2},{1,3},{2,0},{3,1},{4,6},{5,7},{6,4},{7,5},{8,10},{9,11},{10,... | collective-permute-start | bytes 835592 | tf_op jit(solution)/shard_map/ppermute | solution.py:23
  32.5 8.4 %collective-permute-start.11 = (bf16[64,2176]{1,0:T(8,128)(2,1)S(1)}, bf16[64,2176]{1,0:T(8,128)(2,1)S(1)}, u32[]{:S(2)}, u32[]{:S(2)}) collective-permute-start(bf16[64,2176]{1,0:T(8,128)(2,1)S(1)} %collective-permute-done.6.refs_0_), channel_id=1, source_target_pairs={{0,2},{1,3},{2,0},{3,1},{4,6},{5,7},{6,4},{7,5},{8,10},{9,11},{10,... | collective-permute-start | bytes 835592 | tf_op jit(solution)/shard_map/ppermute | solution.py:23
  42.0 27.5 %copy-start.1 = (s32[1,64,8]{1,2,0:T(8,128)S(1)}, s32[1,64,8]{1,2,0:T(8,128)}, u32[]{:S(2)}) copy-start(s32[1,64,8]{1,2,0:T(8,128)} %param.5) | copy-start | bytes 6148
  44.7 24.8 %all-to-all-start = ((bf16[4,128,768]{2,1,0:T(8,128)(2,1)}), bf16[4,128,768]{2,1,0:T(8,128)(2,1)S(1)}, u32[]{:S(2)}, u32[]{:S(2)}) async-start(bf16[4,128,768]{2,1,0:T(8,128)(2,1)} %bitcast.7), calls=%async_computation | async-start | bytes 1572864 | tf_op jit(solution)/shard_map/all_to_all | solution.py:244
  49.6 20.4 %collective-permute-start.9 = (bf16[2,64,768]{2,1,0:T(8,128)(2,1)S(1)}, bf16[2,64,768]{2,1,0:T(8,128)(2,1)S(1)}, u32[]{:S(2)}, u32[]{:S(2)}) collective-permute-start(bf16[2,64,768]{2,1,0:T(8,128)(2,1)S(1)} %shard_map.52), channel_id=1, source_target_pairs={{0,10},{1,11},{2,8},{3,9},{4,14},{5,15},{6,12},{7,13},{8,2},{9,3},... | collective-permute-start | bytes 589832 | tf_op jit(solution)/shard_map/ppermute | solution.py:23
  50.7 25.4 %collective-permute-start.10 = (bf16[2,64,768]{2,1,0:T(8,128)(2,1)S(1)}, bf16[2,64,768]{2,1,0:T(8,128)(2,1)S(1)}, u32[]{:S(2)}, u32[]{:S(2)}) collective-permute-start(bf16[2,64,768]{2,1,0:T(8,128)(2,1)S(1)} %shard_map.51), channel_id=1, source_target_pairs={{0,12},{1,13},{2,14},{3,15},{4,8},{5,9},{6,10},{7,11},{8,4},{9,5},... | collective-permute-start | bytes 589832 | tf_op jit(solution)/shard_map/ppermute | solution.py:23
  54.0 24.5 %collective-permute-start.12 = (bf16[2,64,768]{2,1,0:T(8,128)(2,1)S(1)}, bf16[2,64,768]{2,1,0:T(8,128)(2,1)S(1)}, u32[]{:S(2)}, u32[]{:S(2)}) collective-permute-start(bf16[2,64,768]{2,1,0:T(8,128)(2,1)S(1)} %shard_map.53), channel_id=1, source_target_pairs={{0,14},{1,15},{2,12},{3,13},{4,10},{5,11},{6,8},{7,9},{8,6},{9,7},... | collective-permute-start | bytes 589832 | tf_op jit(solution)/shard_map/ppermute | solution.py:23

commit v26 on v25

--- a/solution.py
+++ b/solution.py
@@ -255,7 +255,7 @@
         Z_NEAR ^ Z_FAR: back_cross,
         X ^ Z_NEAR ^ Z_FAR: back_cross_side,
     }
-    out = pick_routes(route_ids.T, far_parts, pick_routes(route_ids.T, back_near))
+    out = pick_routes(route_ids.T, back_near, pick_routes(route_ids.T, far_parts))
     return out.reshape(1, tokens, top, weight_mat.shape[0])
 
 

time: 80.1 us -> 80.5 us (level)
    ppermute x12, waiting for transfers between devices: 22.5 us -> 38.5 us  [send(): return lax.ppermute(block, 'expert', route)]
    all_to_all x1, waiting for transfers between devices: 15.6 us -> 0.01 us  [dense_device(): lax.all_to_all(found.reshape(Z_FAR, CORES * tokens, found.shape[3]), 'exp...]
where the time goes in v26:
time: 80.5 us; the launch traced here: 80.3 us
  waiting for transfers between devices  43.6 us (54%)
  starting transfers between devices  22.3 us (28%)
  Pallas kernels  11 us (14%)
  local copies, waits for them, and re-layouts  3.26 us (4%)
    ppermute x12, waiting for transfers between devices, send(): return lax.ppermute(block, 'expert', route)  38.5 us
    ppermute x12, starting transfers between devices, send(): return lax.ppermute(block, 'expert', route)  15.9 us
    ppermute x2, waiting for transfers between devices, send_across(): return lax.ppermute(block, ('pipe', 'expert'), route)  5.08 us
    all_to_all x1, starting transfers between devices, dense_device(): lax.all_to_all(found.reshape(Z_FAR, CORES * tokens, found.shape[3]), 'exp...  4.89 us
    pallas_call x4, Pallas kernels, products(): pl.pallas_call(functools.partial(products_kernel, len(pieces)), out_shape...  4.77 us
    unnamed x8, local copies, waits for them, and re-layouts  3.26 us
    pallas_call x1, Pallas kernels, group_results(): pl.pallas_call(functools.partial(group_kernel, flips), out_shape=jax.Shap...  2.68 us
    pallas_call x2, Pallas kernels, pick_routes(): pl.pallas_call(functools.partial(pick_kernel, flips), out_shape=jax.Shape...  1.73 us
  transfers between devices with their start and end apart: 15, of which 8 were waited for; matrix products, arithmetic and copies ran while one was open for 0% of the time, Pallas kernels for 9%

profile of v26, /device:TPU:16, one launch (start us, length us, event | category | flops | bytes accessed | tf_op | source)
XLA Modules:
  0.0 80.3 jit_solution(15226689484107832323)
XLA Ops:
  0.0 0.0 collective-permute-start.1
  0.0 1.5 %collective-permute-start = (bf16[64,2048]{1,0:T(8,128)(2,1)}, bf16[64,2048]{1,0:T(8,128)(2,1)S(1)}, u32[]{:S(2)}, u32[]{:S(2)}) collective-permute-start(bf16[64,2048]{1,0:T(8,128)(2,1)} %bitcast.18), channel_id=1, source_target_pairs={{0,16},{1,17},{2,18},{3,19},{4,20},{5,21},{6,22},{7,23},{8,24},{9,... | collective-permute-start | bytes 786440 | tf_op jit(solution)/shard_map/ppermute | solution.py:33
  1.5 0.0 collective-permute-start.4
  1.5 0.0 copy-start
  1.5 0.7 copy-done
  2.2 0.0 copy-start.2
  2.2 0.7 copy-done.2
  2.9 0.1 shard_map.46.columns
  3.0 2.9 %collective-permute-start.5 = (bf16[64,128]{1,0:T(8,128)(2,1)S(1)}, bf16[64,128]{1,0:T(8,128)(2,1)S(1)}, u32[]{:S(2)}, u32[]{:S(2)}) collective-permute-start(bf16[64,128]{1,0:T(8,128)(2,1)S(1)} %shard_map.46.columns), channel_id=1, source_target_pairs={{0,8},{1,9},{2,10},{3,11},{4,12},{5,13},{6,14},{7,15},{8,0},{9,1},... | collective-permute-start | bytes 49160 | tf_op jit(solution)/shard_map/ppermute | solution.py:23
  5.9 0.0 collective-permute-done.1.other
  5.9 0.0 copy-start.3
  5.9 1.9 %copy-done.3 = bf16[1,1,768,2048]{3,2,1,0:T(8,128)(2,1)S(1)} copy-done((bf16[1,1,768,2048]{3,2,1,0:T(8,128)(2,1)S(1)}, bf16[1,1,768,2048]{3,2,1,0:T(8,128)(2,1)}, u32[]{:S(2)}) %copy-start.3) | copy-done | bytes 3145752
  7.8 1.7 %shard_map.47.weights = bf16[2048,1536]{1,0:T(8,128)(2,1)S(1)} custom-call(bf16[768,2048]{1,0:T(8,128)(2,1)S(1)} %bitcast.17, bf16[768,2048]{1,0:T(8,128)(2,1)S(1)} %collective-permute-done.1.other), custom_call_target="tpu_custom_call" | custom-call | flops 12884901888 | tf_op jit(solution)/shard_map/pallas_call | solution.py:77
  9.5 5.1 %collective-permute-done.rows = bf16[64,2048]{1,0:T(8,128)(2,1)S(1)} collective-permute-done((bf16[64,2048]{1,0:T(8,128)(2,1)}, bf16[64,2048]{1,0:T(8,128)(2,1)S(1)}, u32[]{:S(2)}, u32[]{:S(2)}) %collective-permute-start) | collective-permute-done | bytes 262176 | tf_op jit(solution)/shard_map/ppermute | solution.py:33
  14.6 1.6 %collective-permute-start.3 = (bf16[64,2176]{1,0:T(8,128)(2,1)S(1)}, bf16[64,2176]{1,0:T(8,128)(2,1)S(1)}, u32[]{:S(2)}, u32[]{:S(2)}) collective-permute-start(bf16[64,2176]{1,0:T(8,128)(2,1)S(1)} %shard_map.48.refs_0_), channel_id=1, source_target_pairs={{0,2},{1,3},{2,0},{3,1},{4,6},{5,7},{6,4},{7,5},{8,10},{9,11},{10,... | collective-permute-start | bytes 835592 | tf_op jit(solution)/shard_map/ppermute | solution.py:23
  16.1 0.0 collective-permute-start.2
  16.1 0.0 collective-permute-done.5.columns
  16.1 0.0 collective-permute-done.4.rows
  16.2 3.4 %collective-permute-start.7 = (bf16[64,2176]{1,0:T(8,128)(2,1)S(1)}, bf16[64,2176]{1,0:T(8,128)(2,1)S(1)}, u32[]{:S(2)}, u32[]{:S(2)}) collective-permute-start(bf16[64,2176]{1,0:T(8,128)(2,1)S(1)} %shard_map.49.refs_0_), channel_id=1, source_target_pairs={{0,4},{1,5},{2,6},{3,7},{4,0},{5,1},{6,2},{7,3},{8,12},{9,13},{10,... | collective-permute-start | bytes 835592 | tf_op jit(solution)/shard_map/ppermute | solution.py:23
  19.6 1.6 %collective-permute-start.9 = (bf16[64,2176]{1,0:T(8,128)(2,1)S(1)}, bf16[64,2176]{1,0:T(8,128)(2,1)S(1)}, u32[]{:S(2)}, u32[]{:S(2)}) collective-permute-start(bf16[64,2176]{1,0:T(8,128)(2,1)S(1)} %shard_map.49.refs_0_), channel_id=1, source_target_pairs={{0,2},{1,3},{2,0},{3,1},{4,6},{5,7},{6,4},{7,5},{8,10},{9,11},{10,... | collective-permute-start | bytes 835592 | tf_op jit(solution)/shard_map/ppermute | solution.py:23
  21.1 1.2 %shard_map.50 = bf16[2,64,768]{2,1,0:T(8,128)(2,1)S(1)} custom-call(bf16[2048,1536]{1,0:T(8,128)(2,1)S(1)} %shard_map.47.weights, bf16[64,2176]{1,0:T(8,128)(2,1)S(1)} %shard_map.49.refs_0_), custom_call_target="tpu_custom_call" | custom-call | flops 4026531840 | bytes 6750208 | tf_op jit(solution)/shard_map/pallas_call | solution.py:109
  22.3 0.1 collective-permute-start.10
  22.4 1.5 %collective-permute-done.3.refs_1_ = bf16[64,2176]{1,0:T(8,128)(2,1)S(1)} collective-permute-done((bf16[64,2176]{1,0:T(8,128)(2,1)S(1)}, bf16[64,2176]{1,0:T(8,128)(2,1)S(1)}, u32[]{:S(2)}, u32[]{:S(2)}) %collective-permute-start.3) | collective-permute-done | bytes 278560 | tf_op jit(solution)/shard_map/ppermute | solution.py:23
  23.9 1.8 %collective-permute-done.2.refs_2_ = bf16[64,2176]{1,0:T(8,128)(2,1)S(1)} collective-permute-done((bf16[64,2176]{1,0:T(8,128)(2,1)S(1)}, bf16[64,2176]{1,0:T(8,128)(2,1)S(1)}, u32[]{:S(2)}, u32[]{:S(2)}) %collective-permute-start.2) | collective-permute-done | bytes 278560 | tf_op jit(solution)/shard_map/ppermute | solution.py:23
  25.7 0.5 collective-permute-start.6
  26.3 6.2 %collective-permute-done.7.refs_0_ = bf16[64,2176]{1,0:T(8,128)(2,1)S(1)} collective-permute-done((bf16[64,2176]{1,0:T(8,128)(2,1)S(1)}, bf16[64,2176]{1,0:T(8,128)(2,1)S(1)}, u32[]{:S(2)}, u32[]{:S(2)}) %collective-permute-start.7) | collective-permute-done | bytes 278560 | tf_op jit(solution)/shard_map/ppermute | solution.py:23
  32.5 1.5 %collective-permute-start.8 = (bf16[64,2176]{1,0:T(8,128)(2,1)S(1)}, bf16[64,2176]{1,0:T(8,128)(2,1)S(1)}, u32[]{:S(2)}, u32[]{:S(2)}) collective-permute-start(bf16[64,2176]{1,0:T(8,128)(2,1)S(1)} %collective-permute-done.7.refs_0_), channel_id=1, source_target_pairs={{0,2},{1,3},{2,0},{3,1},{4,6},{5,7},{6,4},{7,5},{8,10},{9,11},{10,... | collective-permute-start | bytes 835592 | tf_op jit(solution)/shard_map/ppermute | solution.py:23
  34.0 1.2 %shard_map.51 = bf16[2,64,768]{2,1,0:T(8,128)(2,1)S(1)} custom-call(bf16[2048,1536]{1,0:T(8,128)(2,1)S(1)} %shard_map.47.weights, bf16[64,2176]{1,0:T(8,128)(2,1)S(1)} %collective-permute-done.7.refs_0_), custom_call_target="tpu_custom_call" | custom-call | flops 4026531840 | bytes 6750208 | tf_op jit(solution)/shard_map/pallas_call | solution.py:109
  35.2 0.0 collective-permute-done.10.refs_0_
  35.2 0.0 collective-permute-done.9.refs_0_
  35.2 1.2 %shard_map.52 = bf16[2,64,768]{2,1,0:T(8,128)(2,1)S(1)} custom-call(bf16[2048,1536]{1,0:T(8,128)(2,1)S(1)} %shard_map.47.weights, bf16[64,2176]{1,0:T(8,128)(2,1)S(1)} %collective-permute-done.9.refs_0_), custom_call_target="tpu_custom_call" | custom-call | flops 4026531840 | bytes 6750208 | tf_op jit(solution)/shard_map/pallas_call | solution.py:109
  36.4 4.5 %collective-permute-done.8.refs_0_ = bf16[64,2176]{1,0:T(8,128)(2,1)S(1)} collective-permute-done((bf16[64,2176]{1,0:T(8,128)(2,1)S(1)}, bf16[64,2176]{1,0:T(8,128)(2,1)S(1)}, u32[]{:S(2)}, u32[]{:S(2)}) %collective-permute-start.8) | collective-permute-done | bytes 278560 | tf_op jit(solution)/shard_map/ppermute | solution.py:23
  40.8 1.2 %shard_map.53 = bf16[2,64,768]{2,1,0:T(8,128)(2,1)S(1)} custom-call(bf16[2048,1536]{1,0:T(8,128)(2,1)S(1)} %shard_map.47.weights, bf16[64,2176]{1,0:T(8,128)(2,1)S(1)} %collective-permute-done.8.refs_0_), custom_call_target="tpu_custom_call" | custom-call | flops 4026531840 | bytes 6750208 | tf_op jit(solution)/shard_map/pallas_call | solution.py:109
  42.0 0.0 copy-start.1
  42.0 0.0 collective-permute-done.6.refs_3_
  42.1 2.7 %shard_map.54 = bf16[4,2,64,768]{3,2,1,0:T(8,128)(2,1)} custom-call(bf16[2048,1536]{1,0:T(8,128)(2,1)S(1)} %shard_map.47.weights, bf16[64,2176]{1,0:T(8,128)(2,1)S(1)} %shard_map.48.refs_0_, bf16[64,2176]{1,0:T(8,128)(2,1)S(1)} %collective-permute-done.3.refs_1_, bf16[64,2176]{1,0:T(8,128)(2,1)S(1)} %collective-permute-done.2.refs_2_, ...), custom_call_target="tpu_custom_call" | custom-call | flops 16106127360 | bytes 8126464 | tf_op jit(solution)/shard_map/pallas_call | solution.py:144
  44.7 4.9 %all-to-all-start = ((bf16[4,128,768]{2,1,0:T(8,128)(2,1)}), bf16[4,128,768]{2,1,0:T(8,128)(2,1)S(1)}, u32[]{:S(2)}, u32[]{:S(2)}) async-start(bf16[4,128,768]{2,1,0:T(8,128)(2,1)} %bitcast.7), calls=%async_computation | async-start | bytes 1572864 | tf_op jit(solution)/shard_map/all_to_all | solution.py:244
  49.6 1.1 %collective-permute-start.11 = (bf16[2,64,768]{2,1,0:T(8,128)(2,1)S(1)}, bf16[2,64,768]{2,1,0:T(8,128)(2,1)S(1)}, u32[]{:S(2)}, u32[]{:S(2)}) collective-permute-start(bf16[2,64,768]{2,1,0:T(8,128)(2,1)S(1)} %shard_map.52), channel_id=1, source_target_pairs={{0,10},{1,11},{2,8},{3,9},{4,14},{5,15},{6,12},{7,13},{8,2},{9,3},... | collective-permute-start | bytes 589832 | tf_op jit(solution)/shard_map/ppermute | solution.py:23
  50.7 3.3 %collective-permute-start.12 = (bf16[2,64,768]{2,1,0:T(8,128)(2,1)S(1)}, bf16[2,64,768]{2,1,0:T(8,128)(2,1)S(1)}, u32[]{:S(2)}, u32[]{:S(2)}) collective-permute-start(bf16[2,64,768]{2,1,0:T(8,128)(2,1)S(1)} %shard_map.51), channel_id=1, source_target_pairs={{0,12},{1,13},{2,14},{3,15},{4,8},{5,9},{6,10},{7,11},{8,4},{9,5},... | collective-permute-start | bytes 589832 | tf_op jit(solution)/shard_map/ppermute | solution.py:23
  54.0 0.0 collective-permute-start.13
  54.0 11.3 %collective-permute-done.11.refs_1_ = bf16[2,64,768]{2,1,0:T(8,128)(2,1)S(1)} collective-permute-done((bf16[2,64,768]{2,1,0:T(8,128)(2,1)S(1)}, bf16[2,64,768]{2,1,0:T(8,128)(2,1)S(1)}, u32[]{:S(2)}, u32[]{:S(2)}) %collective-permute-start.11) | collective-permute-done | bytes 196640 | tf_op jit(solution)/shard_map/ppermute | solution.py:23
  65.3 10.8 %collective-permute-done.12.refs_2_ = bf16[2,64,768]{2,1,0:T(8,128)(2,1)S(1)} collective-permute-done((bf16[2,64,768]{2,1,0:T(8,128)(2,1)S(1)}, bf16[2,64,768]{2,1,0:T(8,128)(2,1)S(1)}, u32[]{:S(2)}, u32[]{:S(2)}) %collective-permute-start.12) | collective-permute-done | bytes 196640 | tf_op jit(solution)/shard_map/ppermute | solution.py:23
  76.1 2.5 %collective-permute-done.13.refs_3_ = bf16[2,64,768]{2,1,0:T(8,128)(2,1)S(1)} collective-permute-done((bf16[2,64,768]{2,1,0:T(8,128)(2,1)S(1)}, bf16[2,64,768]{2,1,0:T(8,128)(2,1)S(1)}, u32[]{:S(2)}, u32[]{:S(2)}) %collective-permute-start.13) | collective-permute-done | bytes 196640 | tf_op jit(solution)/shard_map/ppermute | solution.py:23
  78.5 0.0 copy-done.1
  78.5 0.4 shard_map.55.refs_1_
  79.0 0.0 all-to-all-done
  79.0 1.3 %shard_map.56 = bf16[512,768]{1,0:T(8,128)(2,1)} custom-call(s32[8,64]{1,0:T(8,128)S(1)} %bitcast.14, bf16[4,2,64,768]{3,2,1,0:T(8,128)(2,1)S(1)} %bitcast.11, bf16[512,768]{1,0:T(8,128)(2,1)S(1)} %shard_map.55.refs_1_), custom_call_target="tpu_custom_call" | custom-call | tf_op jit(solution)/shard_map/pallas_call | solution.py:191
  (2 shorter events, 0.0 us)
Async XLA Ops:
  0.0 5.9 %collective-permute-start.1 = (bf16[768,2048]{1,0:T(8,128)(2,1)}, bf16[768,2048]{1,0:T(8,128)(2,1)S(1)}, u32[]{:S(2)}, u32[]{:S(2)}) collective-permute-start(bf16[768,2048]{1,0:T(8,128)(2,1)} %bitcast.16), channel_id=1, source_target_pairs={{0,1},{1,0},{2,3},{3,2},{4,5},{5,4},{6,7},{7,6},{8,9},{9,8},{10,11... | collective-permute-start | bytes 9437192 | tf_op jit(solution)/shard_map/ppermute | solution.py:23
  0.0 14.5 %collective-permute-start = (bf16[64,2048]{1,0:T(8,128)(2,1)}, bf16[64,2048]{1,0:T(8,128)(2,1)S(1)}, u32[]{:S(2)}, u32[]{:S(2)}) collective-permute-start(bf16[64,2048]{1,0:T(8,128)(2,1)} %bitcast.18), channel_id=1, source_target_pairs={{0,16},{1,17},{2,18},{3,19},{4,20},{5,21},{6,22},{7,23},{8,24},{9,... | collective-permute-start | bytes 786440 | tf_op jit(solution)/shard_map/ppermute | solution.py:33
  1.5 14.6 %collective-permute-start.4 = (bf16[64,2048]{1,0:T(8,128)(2,1)}, bf16[64,2048]{1,0:T(8,128)(2,1)S(1)}, u32[]{:S(2)}, u32[]{:S(2)}) collective-permute-start(bf16[64,2048]{1,0:T(8,128)(2,1)} %bitcast.19), channel_id=1, source_target_pairs={{0,24},{1,25},{2,26},{3,27},{4,28},{5,29},{6,30},{7,31},{8,16},{9,... | collective-permute-start | bytes 786440 | tf_op jit(solution)/shard_map/ppermute | solution.py:33
  1.5 0.7 copy-start
  2.2 0.7 copy-start.2
  3.0 13.1 %collective-permute-start.5 = (bf16[64,128]{1,0:T(8,128)(2,1)S(1)}, bf16[64,128]{1,0:T(8,128)(2,1)S(1)}, u32[]{:S(2)}, u32[]{:S(2)}) collective-permute-start(bf16[64,128]{1,0:T(8,128)(2,1)S(1)} %shard_map.46.columns), channel_id=1, source_target_pairs={{0,8},{1,9},{2,10},{3,11},{4,12},{5,13},{6,14},{7,15},{8,0},{9,1},... | collective-permute-start | bytes 49160 | tf_op jit(solution)/shard_map/ppermute | solution.py:23
  5.9 1.9 %copy-start.3 = (bf16[1,1,768,2048]{3,2,1,0:T(8,128)(2,1)S(1)}, bf16[1,1,768,2048]{3,2,1,0:T(8,128)(2,1)}, u32[]{:S(2)}) copy-start(bf16[1,1,768,2048]{3,2,1,0:T(8,128)(2,1)} %param.7) | copy-start | bytes 9437188
  14.6 9.4 %collective-permute-start.3 = (bf16[64,2176]{1,0:T(8,128)(2,1)S(1)}, bf16[64,2176]{1,0:T(8,128)(2,1)S(1)}, u32[]{:S(2)}, u32[]{:S(2)}) collective-permute-start(bf16[64,2176]{1,0:T(8,128)(2,1)S(1)} %shard_map.48.refs_0_), channel_id=1, source_target_pairs={{0,2},{1,3},{2,0},{3,1},{4,6},{5,7},{6,4},{7,5},{8,10},{9,11},{10,... | collective-permute-start | bytes 835592 | tf_op jit(solution)/shard_map/ppermute | solution.py:23
  16.1 9.6 %collective-permute-start.2 = (bf16[64,2176]{1,0:T(8,128)(2,1)S(1)}, bf16[64,2176]{1,0:T(8,128)(2,1)S(1)}, u32[]{:S(2)}, u32[]{:S(2)}) collective-permute-start(bf16[64,2176]{1,0:T(8,128)(2,1)S(1)} %shard_map.48.refs_0_), channel_id=1, source_target_pairs={{0,4},{1,5},{2,6},{3,7},{4,0},{5,1},{6,2},{7,3},{8,12},{9,13},{10,... | collective-permute-start | bytes 835592 | tf_op jit(solution)/shard_map/ppermute | solution.py:23
  16.2 16.3 %collective-permute-start.7 = (bf16[64,2176]{1,0:T(8,128)(2,1)S(1)}, bf16[64,2176]{1,0:T(8,128)(2,1)S(1)}, u32[]{:S(2)}, u32[]{:S(2)}) collective-permute-start(bf16[64,2176]{1,0:T(8,128)(2,1)S(1)} %shard_map.49.refs_0_), channel_id=1, source_target_pairs={{0,4},{1,5},{2,6},{3,7},{4,0},{5,1},{6,2},{7,3},{8,12},{9,13},{10,... | collective-permute-start | bytes 835592 | tf_op jit(solution)/shard_map/ppermute | solution.py:23
  19.6 15.6 %collective-permute-start.9 = (bf16[64,2176]{1,0:T(8,128)(2,1)S(1)}, bf16[64,2176]{1,0:T(8,128)(2,1)S(1)}, u32[]{:S(2)}, u32[]{:S(2)}) collective-permute-start(bf16[64,2176]{1,0:T(8,128)(2,1)S(1)} %shard_map.49.refs_0_), channel_id=1, source_target_pairs={{0,2},{1,3},{2,0},{3,1},{4,6},{5,7},{6,4},{7,5},{8,10},{9,11},{10,... | collective-permute-start | bytes 835592 | tf_op jit(solution)/shard_map/ppermute | solution.py:23
  22.3 12.8 %collective-permute-start.10 = (bf16[2,64,768]{2,1,0:T(8,128)(2,1)S(1)}, bf16[2,64,768]{2,1,0:T(8,128)(2,1)S(1)}, u32[]{:S(2)}, u32[]{:S(2)}) collective-permute-start(bf16[2,64,768]{2,1,0:T(8,128)(2,1)S(1)} %shard_map.50), channel_id=1, source_target_pairs={{0,8},{1,9},{2,10},{3,11},{4,12},{5,13},{6,14},{7,15},{8,0},{9,1},... | collective-permute-start | bytes 589832 | tf_op jit(solution)/shard_map/ppermute | solution.py:23
  25.7 16.3 %collective-permute-start.6 = (bf16[64,2176]{1,0:T(8,128)(2,1)S(1)}, bf16[64,2176]{1,0:T(8,128)(2,1)S(1)}, u32[]{:S(2)}, u32[]{:S(2)}) collective-permute-start(bf16[64,2176]{1,0:T(8,128)(2,1)S(1)} %collective-permute-done.2.refs_2_), channel_id=1, source_target_pairs={{0,2},{1,3},{2,0},{3,1},{4,6},{5,7},{6,4},{7,5},{8,10},{9,11},{10,... | collective-permute-start | bytes 835592 | tf_op jit(solution)/shard_map/ppermute | solution.py:23
  32.5 8.4 %collective-permute-start.8 = (bf16[64,2176]{1,0:T(8,128)(2,1)S(1)}, bf16[64,2176]{1,0:T(8,128)(2,1)S(1)}, u32[]{:S(2)}, u32[]{:S(2)}) collective-permute-start(bf16[64,2176]{1,0:T(8,128)(2,1)S(1)} %collective-permute-done.7.refs_0_), channel_id=1, source_target_pairs={{0,2},{1,3},{2,0},{3,1},{4,6},{5,7},{6,4},{7,5},{8,10},{9,11},{10,... | collective-permute-start | bytes 835592 | tf_op jit(solution)/shard_map/ppermute | solution.py:23
  42.0 36.5 %copy-start.1 = (s32[1,64,8]{1,2,0:T(8,128)S(1)}, s32[1,64,8]{1,2,0:T(8,128)}, u32[]{:S(2)}) copy-start(s32[1,64,8]{1,2,0:T(8,128)} %param.5) | copy-start | bytes 6148
  44.7 34.2 %all-to-all-start = ((bf16[4,128,768]{2,1,0:T(8,128)(2,1)}), bf16[4,128,768]{2,1,0:T(8,128)(2,1)S(1)}, u32[]{:S(2)}, u32[]{:S(2)}) async-start(bf16[4,128,768]{2,1,0:T(8,128)(2,1)} %bitcast.7), calls=%async_computation | async-start | bytes 1572864 | tf_op jit(solution)/shard_map/all_to_all | solution.py:244
  49.6 15.6 %collective-permute-start.11 = (bf16[2,64,768]{2,1,0:T(8,128)(2,1)S(1)}, bf16[2,64,768]{2,1,0:T(8,128)(2,1)S(1)}, u32[]{:S(2)}, u32[]{:S(2)}) collective-permute-start(bf16[2,64,768]{2,1,0:T(8,128)(2,1)S(1)} %shard_map.52), channel_id=1, source_target_pairs={{0,10},{1,11},{2,8},{3,9},{4,14},{5,15},{6,12},{7,13},{8,2},{9,3},... | collective-permute-start | bytes 589832 | tf_op jit(solution)/shard_map/ppermute | solution.py:23
  50.7 25.4 %collective-permute-start.12 = (bf16[2,64,768]{2,1,0:T(8,128)(2,1)S(1)}, bf16[2,64,768]{2,1,0:T(8,128)(2,1)S(1)}, u32[]{:S(2)}, u32[]{:S(2)}) collective-permute-start(bf16[2,64,768]{2,1,0:T(8,128)(2,1)S(1)} %shard_map.51), channel_id=1, source_target_pairs={{0,12},{1,13},{2,14},{3,15},{4,8},{5,9},{6,10},{7,11},{8,4},{9,5},... | collective-permute-start | bytes 589832 | tf_op jit(solution)/shard_map/ppermute | solution.py:23
  54.0 24.5 %collective-permute-start.13 = (bf16[2,64,768]{2,1,0:T(8,128)(2,1)S(1)}, bf16[2,64,768]{2,1,0:T(8,128)(2,1)S(1)}, u32[]{:S(2)}, u32[]{:S(2)}) collective-permute-start(bf16[2,64,768]{2,1,0:T(8,128)(2,1)S(1)} %shard_map.53), channel_id=1, source_target_pairs={{0,14},{1,15},{2,12},{3,13},{4,10},{5,11},{6,8},{7,9},{8,6},{9,7},... | collective-permute-start | bytes 589832 | tf_op jit(solution)/shard_map/ppermute | solution.py:23

commit v27 on v21

--- a/solution.py
+++ b/solution.py
@@ -167,11 +167,13 @@
     other_mat = send(weight_mat, owners, 0, 1)
     columns = gate_columns(route_ids.T, route_gates.T)
     far_columns = send(columns, owners, Z_FAR)
+    upstream, columns = tie((upstream, columns))
+    near = send_across(upstream, owners, Z_NEAR)
+    near_columns = send(columns, owners, Z_NEAR)
     weights = turned(weight_mat, other_mat)
-    rows, columns, weights = tie((rows, columns, weights))
+    rows, columns, weights, near_columns = tie((rows, columns, weights, near_columns))
     rows = widened(rows, columns)
     side = send(rows, owners, X)
-    near = send(rows, owners, Z_NEAR)
     far, far_columns, rows = tie((far, far_columns, rows))
     far = widened(far, far_columns)
     cross = send(far, owners, Z_NEAR)
@@ -179,21 +181,21 @@
     (out_far,) = work(far)
     back_far = send(out_far, owners, Z_FAR)
     side, _ = tie((side, out_far))
-    out_side, out_own = work(side, rows)
-    back_side = send(out_side, owners, X)
-    near, _ = tie((near, out_side))
+    near, side = tie((near, side))
+    near = widened(near, near_columns)
     near_side = send(near, owners, X)
-    cross, _ = tie((cross, near))
+    cross, near = tie((cross, near))
     cross_side = send(cross, owners, X)
     (out_cross,) = work(cross)
     back_cross = send(out_cross, owners, Z_NEAR ^ Z_FAR)
-    far_side, back_far, back_side, _ = tie((far_side, back_far, back_side, out_cross))
-    (out_far_side,) = work(far_side)
+    far_side, side, back_far, _ = tie((far_side, side, back_far, out_cross))
+    out_far_side, out_side, out_own = work(far_side, side, rows)
     back_far_side = send(out_far_side, owners, X ^ Z_FAR)
     cross_side, _ = tie((cross_side, out_far_side))
     (out_cross_side,) = work(cross_side)
     back_cross_side = send(out_cross_side, owners, X ^ Z_NEAR ^ Z_FAR)
-    near_side, _ = tie((near_side, out_cross_side))
+    back_side = send(out_side, owners, X)
+    near_side, back_side, _ = tie((near_side, back_side, out_cross_side))
     out_near, out_near_side = work(near, near_side)
     back_near_side = send(out_near_side, owners, X ^ Z_NEAR)
     back_near = send(out_near, owners, Z_NEAR)

time: 68.9 us -> 70.2 us (1.019)
  waiting for transfers between devices: 19.7 us -> 22.1 us
  Pallas kernels: 10.3 us -> 9.52 us
    ppermute x15, waiting for transfers between devices: 18.7 us -> 21.4 us  [send(): return lax.ppermute(block, 'expert', route)]
    ppermute x15, starting transfers between devices: 30.3 us -> 28.5 us  [send(): return lax.ppermute(block, 'expert', route)]
    ppermute x2 -> x3, starting transfers between devices: 5.05 us -> 6.45 us  [send_across(): return lax.ppermute(block, ('pipe', 'expert'), route)]
    pallas_call x6 -> x5, Pallas kernels: 6.73 us -> 5.94 us  [products(): pl.pallas_call(functools.partial(products_kernel, len(pieces)), out_shape...]
  transfers between devices with their start and end apart: 17 -> 18, of which waited for: 7 -> 7; matrix products, arithmetic and copies ran while one was open for 0% -> 0% of each run, Pallas kernels for 13% -> 12%
where the time goes in v27:
time: 70.2 us; the launch traced here: 70 us
  starting transfers between devices  35 us (50%)
  waiting for transfers between devices  22.1 us (31%)
  Pallas kernels  9.52 us (14%)
  local copies, waits for them, and re-layouts  3.26 us (5%)
    ppermute x15, starting transfers between devices, send(): return lax.ppermute(block, 'expert', route)  28.5 us
    ppermute x15, waiting for transfers between devices, send(): return lax.ppermute(block, 'expert', route)  21.4 us
    ppermute x3, starting transfers between devices, send_across(): return lax.ppermute(block, ('pipe', 'expert'), route)  6.45 us
    pallas_call x5, Pallas kernels, products(): pl.pallas_call(functools.partial(products_kernel, len(pieces)), out_shape...  5.94 us
    unnamed x8, local copies, waits for them, and re-layouts  3.26 us
    pallas_call x2, Pallas kernels, pick_routes(): pl.pallas_call(functools.partial(pick_kernel, flips), out_shape=jax.Shape...  1.74 us
    pallas_call x1, Pallas kernels, turned(): pl.pallas_call(turn_kernel, out_shape=jax.ShapeDtypeStruct((depth, CORES...  1.67 us
  transfers between devices with their start and end apart: 18, of which 7 were waited for; matrix products, arithmetic and copies ran while one was open for 0% of the time, Pallas kernels for 12%

profile of v27, /device:TPU:0, one launch (start us, length us, event | category | flops | bytes accessed | tf_op | source)
XLA Modules:
  0.0 70.0 jit_solution(8395001557966684575)
XLA Ops:
  0.0 0.5 collective-permute-start.2
  0.5 2.5 %collective-permute-start.1 = (bf16[64,2048]{1,0:T(8,128)(2,1)}, bf16[64,2048]{1,0:T(8,128)(2,1)S(1)}, u32[]{:S(2)}, u32[]{:S(2)}) collective-permute-start(bf16[64,2048]{1,0:T(8,128)(2,1)} %bitcast.15), channel_id=1, source_target_pairs={{0,16},{1,17},{2,18},{3,19},{4,20},{5,21},{6,22},{7,23},{8,24},{9,... | collective-permute-start | bytes 786440 | tf_op jit(solution)/shard_map/ppermute | solution.py:33
  3.0 2.5 %collective-permute-start.5 = (bf16[64,2048]{1,0:T(8,128)(2,1)}, bf16[64,2048]{1,0:T(8,128)(2,1)S(1)}, u32[]{:S(2)}, u32[]{:S(2)}) collective-permute-start(bf16[64,2048]{1,0:T(8,128)(2,1)} %bitcast.16), channel_id=1, source_target_pairs={{0,24},{1,25},{2,26},{3,27},{4,28},{5,29},{6,30},{7,31},{8,16},{9,... | collective-permute-start | bytes 786440 | tf_op jit(solution)/shard_map/ppermute | solution.py:33
  5.5 0.0 copy-start
  5.5 0.7 copy-done
  6.2 0.0 copy-start.2
  6.2 0.7 copy-done.2
  6.9 0.1 shard_map.46.columns
  7.0 0.1 collective-permute-start.6
  7.1 1.9 %collective-permute-start.3 = (bf16[64,128]{1,0:T(8,128)(2,1)S(1)}, bf16[64,128]{1,0:T(8,128)(2,1)S(1)}, u32[]{:S(2)}, u32[]{:S(2)}) collective-permute-start(bf16[64,128]{1,0:T(8,128)(2,1)S(1)} %shard_map.46.columns), channel_id=1, source_target_pairs={{0,4},{1,5},{2,6},{3,7},{4,0},{5,1},{6,2},{7,3},{8,12},{9,13},{10,... | collective-permute-start | bytes 49160 | tf_op jit(solution)/shard_map/ppermute | solution.py:23
  8.9 0.0 collective-permute-done.2.other
  8.9 1.4 %collective-permute-start = (bf16[64,2048]{1,0:T(8,128)(2,1)}, bf16[64,2048]{1,0:T(8,128)(2,1)S(1)}, u32[]{:S(2)}, u32[]{:S(2)}) collective-permute-start(bf16[64,2048]{1,0:T(8,128)(2,1)} %bitcast.17), channel_id=1, source_target_pairs={{0,20},{1,21},{2,22},{3,23},{4,16},{5,17},{6,18},{7,19},{8,28},{9,... | collective-permute-start | bytes 786440 | tf_op jit(solution)/shard_map/ppermute | solution.py:33
  10.3 0.0 copy-start.3
  10.3 1.9 %copy-done.3 = bf16[1,1,768,2048]{3,2,1,0:T(8,128)(2,1)S(1)} copy-done((bf16[1,1,768,2048]{3,2,1,0:T(8,128)(2,1)S(1)}, bf16[1,1,768,2048]{3,2,1,0:T(8,128)(2,1)}, u32[]{:S(2)}) %copy-start.3) | copy-done | bytes 3145752
  12.2 1.7 %shard_map.47.weights = bf16[2048,1536]{1,0:T(8,128)(2,1)S(1)} custom-call(bf16[768,2048]{1,0:T(8,128)(2,1)S(1)} %bitcast.14, bf16[768,2048]{1,0:T(8,128)(2,1)S(1)} %collective-permute-done.2.other), custom_call_target="tpu_custom_call" | custom-call | flops 12884901888 | tf_op jit(solution)/shard_map/pallas_call | solution.py:77
  13.9 0.0 collective-permute-done.3.columns
  13.9 0.0 collective-permute-done.1.rows
  14.0 1.6 %collective-permute-start.4 = (bf16[64,2176]{1,0:T(8,128)(2,1)S(1)}, bf16[64,2176]{1,0:T(8,128)(2,1)S(1)}, u32[]{:S(2)}, u32[]{:S(2)}) collective-permute-start(bf16[64,2176]{1,0:T(8,128)(2,1)S(1)} %shard_map.48.refs_2_), channel_id=1, source_target_pairs={{0,2},{1,3},{2,0},{3,1},{4,6},{5,7},{6,4},{7,5},{8,10},{9,11},{10,... | collective-permute-start | bytes 835592 | tf_op jit(solution)/shard_map/ppermute | solution.py:23
  15.5 3.4 %collective-permute-done.6.columns = bf16[64,128]{1,0:T(8,128)(2,1)S(1)} collective-permute-done((bf16[64,128]{1,0:T(8,128)(2,1)S(1)}, bf16[64,128]{1,0:T(8,128)(2,1)S(1)}, u32[]{:S(2)}, u32[]{:S(2)}) %collective-permute-start.6) | collective-permute-done | bytes 16416 | tf_op jit(solution)/shard_map/ppermute | solution.py:23
  18.9 0.7 %collective-permute-done.5.rows = bf16[64,2048]{1,0:T(8,128)(2,1)S(1)} collective-permute-done((bf16[64,2048]{1,0:T(8,128)(2,1)}, bf16[64,2048]{1,0:T(8,128)(2,1)S(1)}, u32[]{:S(2)}, u32[]{:S(2)}) %collective-permute-start.5) | collective-permute-done | bytes 262176 | tf_op jit(solution)/shard_map/ppermute | solution.py:33
  19.7 5.2 %collective-permute-start.10 = (bf16[64,2176]{1,0:T(8,128)(2,1)S(1)}, bf16[64,2176]{1,0:T(8,128)(2,1)S(1)}, u32[]{:S(2)}, u32[]{:S(2)}) collective-permute-start(bf16[64,2176]{1,0:T(8,128)(2,1)S(1)} %shard_map.49.refs_0_), channel_id=1, source_target_pairs={{0,4},{1,5},{2,6},{3,7},{4,0},{5,1},{6,2},{7,3},{8,12},{9,13},{10,... | collective-permute-start | bytes 835592 | tf_op jit(solution)/shard_map/ppermute | solution.py:23
  24.9 0.5 collective-permute-start.8
  25.4 1.2 %shard_map.50 = bf16[2,64,768]{2,1,0:T(8,128)(2,1)S(1)} custom-call(bf16[2048,1536]{1,0:T(8,128)(2,1)S(1)} %shard_map.47.weights, bf16[64,2176]{1,0:T(8,128)(2,1)S(1)} %shard_map.49.refs_0_), custom_call_target="tpu_custom_call" | custom-call | flops 4026531840 | bytes 6750208 | tf_op jit(solution)/shard_map/pallas_call | solution.py:109
  26.6 1.2 %collective-permute-start.9 = (bf16[2,64,768]{2,1,0:T(8,128)(2,1)S(1)}, bf16[2,64,768]{2,1,0:T(8,128)(2,1)S(1)}, u32[]{:S(2)}, u32[]{:S(2)}) collective-permute-start(bf16[2,64,768]{2,1,0:T(8,128)(2,1)S(1)} %shard_map.50), channel_id=1, source_target_pairs={{0,8},{1,9},{2,10},{3,11},{4,12},{5,13},{6,14},{7,15},{8,0},{9,1},... | collective-permute-start | bytes 589832 | tf_op jit(solution)/shard_map/ppermute | solution.py:23
  27.8 0.0 collective-permute-done.4.refs_1_
  27.8 0.0 collective-permute-done.rows
  27.8 1.6 %collective-permute-start.7 = (bf16[64,2176]{1,0:T(8,128)(2,1)S(1)}, bf16[64,2176]{1,0:T(8,128)(2,1)S(1)}, u32[]{:S(2)}, u32[]{:S(2)}) collective-permute-start(bf16[64,2176]{1,0:T(8,128)(2,1)S(1)} %shard_map.51.refs_0_), channel_id=1, source_target_pairs={{0,2},{1,3},{2,0},{3,1},{4,6},{5,7},{6,4},{7,5},{8,10},{9,11},{10,... | collective-permute-start | bytes 835592 | tf_op jit(solution)/shard_map/ppermute | solution.py:23
  29.4 6.0 %collective-permute-done.10.refs_0_ = bf16[64,2176]{1,0:T(8,128)(2,1)S(1)} collective-permute-done((bf16[64,2176]{1,0:T(8,128)(2,1)S(1)}, bf16[64,2176]{1,0:T(8,128)(2,1)S(1)}, u32[]{:S(2)}, u32[]{:S(2)}) %collective-permute-start.10) | collective-permute-done | bytes 278560 | tf_op jit(solution)/shard_map/ppermute | solution.py:23
  35.4 0.0 collective-permute-start.12
  35.4 1.2 %shard_map.52 = bf16[2,64,768]{2,1,0:T(8,128)(2,1)S(1)} custom-call(bf16[2048,1536]{1,0:T(8,128)(2,1)S(1)} %shard_map.47.weights, bf16[64,2176]{1,0:T(8,128)(2,1)S(1)} %collective-permute-done.10.refs_0_), custom_call_target="tpu_custom_call" | custom-call | flops 4026531840 | bytes 6750208 | tf_op jit(solution)/shard_map/pallas_call | solution.py:109
  36.6 1.5 %collective-permute-start.16 = (bf16[2,64,768]{2,1,0:T(8,128)(2,1)S(1)}, bf16[2,64,768]{2,1,0:T(8,128)(2,1)S(1)}, u32[]{:S(2)}, u32[]{:S(2)}) collective-permute-start(bf16[2,64,768]{2,1,0:T(8,128)(2,1)S(1)} %shard_map.52), channel_id=1, source_target_pairs={{0,12},{1,13},{2,14},{3,15},{4,8},{5,9},{6,10},{7,11},{8,4},{9,5},... | collective-permute-start | bytes 589832 | tf_op jit(solution)/shard_map/ppermute | solution.py:23
  38.1 0.0 collective-permute-done.9.refs_1_
  38.1 0.0 collective-permute-done.8.refs_0_
  38.1 1.4 %shard_map.53 = (bf16[2,64,768]{2,1,0:T(8,128)(2,1)S(1)}, bf16[2,64,768]{2,1,0:T(8,128)(2,1)S(1)}, bf16[2,64,768]{2,1,0:T(8,128)(2,1)S(1)}) custom-call(bf16[2048,1536]{1,0:T(8,128)(2,1)S(1)} %shard_map.47.weights, bf16[64,2176]{1,0:T(8,128)(2,1)S(1)} %collective-permute-done.8.refs_0_, bf16[64,2176]{1,0:T(8,128)(2,1)S(1)} %collective-permute-done.4.refs_1_, ...), custom_call_target="tpu_custom_call" | custom-call | flops 12079595520 | bytes 7667712 | tf_op jit(solution)/shard_map/pallas_call | solution.py:109
  39.5 2.7 %collective-permute-start.15 = (bf16[2,64,768]{2,1,0:T(8,128)(2,1)S(1)}, bf16[2,64,768]{2,1,0:T(8,128)(2,1)S(1)}, u32[]{:S(2)}, u32[]{:S(2)}) collective-permute-start(bf16[2,64,768]{2,1,0:T(8,128)(2,1)S(1)} %get-tuple-element.46), channel_id=1, source_target_pairs={{0,10},{1,11},{2,8},{3,9},{4,14},{5,15},{6,12},{7,13},{8,2},{9,3},... | collective-permute-start | bytes 589832 | tf_op jit(solution)/shard_map/ppermute | solution.py:23
  42.2 0.5 collective-permute-start.11
  42.7 3.7 %collective-permute-done.12.refs_0_ = bf16[64,2176]{1,0:T(8,128)(2,1)S(1)} collective-permute-done((bf16[64,2176]{1,0:T(8,128)(2,1)S(1)}, bf16[64,2176]{1,0:T(8,128)(2,1)S(1)}, u32[]{:S(2)}, u32[]{:S(2)}) %collective-permute-start.12) | collective-permute-done | bytes 278560 | tf_op jit(solution)/shard_map/ppermute | solution.py:23
  46.4 1.2 %shard_map.54 = bf16[2,64,768]{2,1,0:T(8,128)(2,1)S(1)} custom-call(bf16[2048,1536]{1,0:T(8,128)(2,1)S(1)} %shard_map.47.weights, bf16[64,2176]{1,0:T(8,128)(2,1)S(1)} %collective-permute-done.12.refs_0_), custom_call_target="tpu_custom_call" | custom-call | flops 4026531840 | bytes 6750208 | tf_op jit(solution)/shard_map/pallas_call | solution.py:109
  47.6 0.0 copy-start.1
  47.6 5.9 %collective-permute-start.17 = (bf16[2,64,768]{2,1,0:T(8,128)(2,1)S(1)}, bf16[2,64,768]{2,1,0:T(8,128)(2,1)S(1)}, u32[]{:S(2)}, u32[]{:S(2)}) collective-permute-start(bf16[2,64,768]{2,1,0:T(8,128)(2,1)S(1)} %shard_map.54), channel_id=1, source_target_pairs={{0,14},{1,15},{2,12},{3,13},{4,10},{5,11},{6,8},{7,9},{8,6},{9,7},... | collective-permute-start | bytes 589832 | tf_op jit(solution)/shard_map/ppermute | solution.py:23
  53.6 0.0 collective-permute-done.11.refs_0_
  53.6 0.0 collective-permute-done.7.refs_1_
  53.6 1.0 %shard_map.55 = (bf16[2,64,768]{2,1,0:T(8,128)(2,1)S(1)}, bf16[2,64,768]{2,1,0:T(8,128)(2,1)S(1)}) custom-call(bf16[2048,1536]{1,0:T(8,128)(2,1)S(1)} %shard_map.47.weights, bf16[64,2176]{1,0:T(8,128)(2,1)S(1)} %shard_map.51.refs_0_, bf16[64,2176]{1,0:T(8,128)(2,1)S(1)} %collective-permute-done.7.refs_1_), custom_call_target="tpu_custom_call" | custom-call | flops 8053063680 | bytes 7208960 | tf_op jit(solution)/shard_map/pallas_call | solution.py:109
  54.6 5.3 %collective-permute-start.13 = (bf16[2,64,768]{2,1,0:T(8,128)(2,1)S(1)}, bf16[2,64,768]{2,1,0:T(8,128)(2,1)S(1)}, u32[]{:S(2)}, u32[]{:S(2)}) collective-permute-start(bf16[2,64,768]{2,1,0:T(8,128)(2,1)S(1)} %get-tuple-element.51), channel_id=1, source_target_pairs={{0,4},{1,5},{2,6},{3,7},{4,0},{5,1},{6,2},{7,3},{8,12},{9,13},{10,... | collective-permute-start | bytes 589832 | tf_op jit(solution)/shard_map/ppermute | solution.py:23
  59.8 0.2 collective-permute-start.14
  60.0 1.0 %collective-permute-done.15.refs_2_ = bf16[2,64,768]{2,1,0:T(8,128)(2,1)S(1)} collective-permute-done((bf16[2,64,768]{2,1,0:T(8,128)(2,1)S(1)}, bf16[2,64,768]{2,1,0:T(8,128)(2,1)S(1)}, u32[]{:S(2)}, u32[]{:S(2)}) %collective-permute-start.15) | collective-permute-done | bytes 196640 | tf_op jit(solution)/shard_map/ppermute | solution.py:23
  60.9 0.0 collective-permute-done.16.refs_3_
  60.9 0.0 collective-permute-done.17.refs_4_
  60.9 0.0 copy-done.1
  60.9 0.4 shard_map.56.refs_3_
  61.4 3.9 %collective-permute-done.13.refs_1_ = bf16[2,64,768]{2,1,0:T(8,128)(2,1)S(1)} collective-permute-done((bf16[2,64,768]{2,1,0:T(8,128)(2,1)S(1)}, bf16[2,64,768]{2,1,0:T(8,128)(2,1)S(1)}, u32[]{:S(2)}, u32[]{:S(2)}) %collective-permute-start.13) | collective-permute-done | bytes 196640 | tf_op jit(solution)/shard_map/ppermute | solution.py:23
  65.3 3.4 %collective-permute-done.14.refs_2_ = bf16[2,64,768]{2,1,0:T(8,128)(2,1)S(1)} collective-permute-done((bf16[2,64,768]{2,1,0:T(8,128)(2,1)S(1)}, bf16[2,64,768]{2,1,0:T(8,128)(2,1)S(1)}, u32[]{:S(2)}, u32[]{:S(2)}) %collective-permute-start.14) | collective-permute-done | bytes 196640 | tf_op jit(solution)/shard_map/ppermute | solution.py:23
  68.7 1.3 %shard_map.57 = bf16[512,768]{1,0:T(8,128)(2,1)} custom-call(s32[8,64]{1,0:T(8,128)S(1)} %bitcast.11, bf16[2,64,768]{2,1,0:T(8,128)(2,1)S(1)} %collective-permute-done.11.refs_0_, bf16[2,64,768]{2,1,0:T(8,128)(2,1)S(1)} %collective-permute-done.13.refs_1_, bf16[2,64,768]{2,1,0:T(8,128)(2,1)S(1)} %collective-permute-done.14.refs_2_, ...), custom_call_target="tpu_custom_call" | custom-call | tf_op jit(solution)/shard_map/pallas_call | solution.py:150
  (3 shorter events, 0.1 us)
Async XLA Ops:
  0.0 8.9 %collective-permute-start.2 = (bf16[768,2048]{1,0:T(8,128)(2,1)}, bf16[768,2048]{1,0:T(8,128)(2,1)S(1)}, u32[]{:S(2)}, u32[]{:S(2)}) collective-permute-start(bf16[768,2048]{1,0:T(8,128)(2,1)} %bitcast.13), channel_id=1, source_target_pairs={{0,1},{1,0},{2,3},{3,2},{4,5},{5,4},{6,7},{7,6},{8,9},{9,8},{10,11... | collective-permute-start | bytes 9437192 | tf_op jit(solution)/shard_map/ppermute | solution.py:23
  0.5 13.5 %collective-permute-start.1 = (bf16[64,2048]{1,0:T(8,128)(2,1)}, bf16[64,2048]{1,0:T(8,128)(2,1)S(1)}, u32[]{:S(2)}, u32[]{:S(2)}) collective-permute-start(bf16[64,2048]{1,0:T(8,128)(2,1)} %bitcast.15), channel_id=1, source_target_pairs={{0,16},{1,17},{2,18},{3,19},{4,20},{5,21},{6,22},{7,23},{8,24},{9,... | collective-permute-start | bytes 786440 | tf_op jit(solution)/shard_map/ppermute | solution.py:33
  3.0 16.7 %collective-permute-start.5 = (bf16[64,2048]{1,0:T(8,128)(2,1)}, bf16[64,2048]{1,0:T(8,128)(2,1)S(1)}, u32[]{:S(2)}, u32[]{:S(2)}) collective-permute-start(bf16[64,2048]{1,0:T(8,128)(2,1)} %bitcast.16), channel_id=1, source_target_pairs={{0,24},{1,25},{2,26},{3,27},{4,28},{5,29},{6,30},{7,31},{8,16},{9,... | collective-permute-start | bytes 786440 | tf_op jit(solution)/shard_map/ppermute | solution.py:33
  5.5 0.7 copy-start
  6.2 0.7 copy-start.2
  7.0 11.9 %collective-permute-start.6 = (bf16[64,128]{1,0:T(8,128)(2,1)S(1)}, bf16[64,128]{1,0:T(8,128)(2,1)S(1)}, u32[]{:S(2)}, u32[]{:S(2)}) collective-permute-start(bf16[64,128]{1,0:T(8,128)(2,1)S(1)} %shard_map.46.columns), channel_id=1, source_target_pairs={{0,8},{1,9},{2,10},{3,11},{4,12},{5,13},{6,14},{7,15},{8,0},{9,1},... | collective-permute-start | bytes 49160 | tf_op jit(solution)/shard_map/ppermute | solution.py:23
  7.1 6.8 %collective-permute-start.3 = (bf16[64,128]{1,0:T(8,128)(2,1)S(1)}, bf16[64,128]{1,0:T(8,128)(2,1)S(1)}, u32[]{:S(2)}, u32[]{:S(2)}) collective-permute-start(bf16[64,128]{1,0:T(8,128)(2,1)S(1)} %shard_map.46.columns), channel_id=1, source_target_pairs={{0,4},{1,5},{2,6},{3,7},{4,0},{5,1},{6,2},{7,3},{8,12},{9,13},{10,... | collective-permute-start | bytes 49160 | tf_op jit(solution)/shard_map/ppermute | solution.py:23
  8.9 18.8 %collective-permute-start = (bf16[64,2048]{1,0:T(8,128)(2,1)}, bf16[64,2048]{1,0:T(8,128)(2,1)S(1)}, u32[]{:S(2)}, u32[]{:S(2)}) collective-permute-start(bf16[64,2048]{1,0:T(8,128)(2,1)} %bitcast.17), channel_id=1, source_target_pairs={{0,20},{1,21},{2,22},{3,23},{4,16},{5,17},{6,18},{7,19},{8,28},{9,... | collective-permute-start | bytes 786440 | tf_op jit(solution)/shard_map/ppermute | solution.py:33
  10.3 1.9 %copy-start.3 = (bf16[1,1,768,2048]{3,2,1,0:T(8,128)(2,1)S(1)}, bf16[1,1,768,2048]{3,2,1,0:T(8,128)(2,1)}, u32[]{:S(2)}) copy-start(bf16[1,1,768,2048]{3,2,1,0:T(8,128)(2,1)} %param.7) | copy-start | bytes 9437188
  14.0 13.8 %collective-permute-start.4 = (bf16[64,2176]{1,0:T(8,128)(2,1)S(1)}, bf16[64,2176]{1,0:T(8,128)(2,1)S(1)}, u32[]{:S(2)}, u32[]{:S(2)}) collective-permute-start(bf16[64,2176]{1,0:T(8,128)(2,1)S(1)} %shard_map.48.refs_2_), channel_id=1, source_target_pairs={{0,2},{1,3},{2,0},{3,1},{4,6},{5,7},{6,4},{7,5},{8,10},{9,11},{10,... | collective-permute-start | bytes 835592 | tf_op jit(solution)/shard_map/ppermute | solution.py:23
  19.7 15.7 %collective-permute-start.10 = (bf16[64,2176]{1,0:T(8,128)(2,1)S(1)}, bf16[64,2176]{1,0:T(8,128)(2,1)S(1)}, u32[]{:S(2)}, u32[]{:S(2)}) collective-permute-start(bf16[64,2176]{1,0:T(8,128)(2,1)S(1)} %shard_map.49.refs_0_), channel_id=1, source_target_pairs={{0,4},{1,5},{2,6},{3,7},{4,0},{5,1},{6,2},{7,3},{8,12},{9,13},{10,... | collective-permute-start | bytes 835592 | tf_op jit(solution)/shard_map/ppermute | solution.py:23
  24.9 13.2 %collective-permute-start.8 = (bf16[64,2176]{1,0:T(8,128)(2,1)S(1)}, bf16[64,2176]{1,0:T(8,128)(2,1)S(1)}, u32[]{:S(2)}, u32[]{:S(2)}) collective-permute-start(bf16[64,2176]{1,0:T(8,128)(2,1)S(1)} %shard_map.49.refs_0_), channel_id=1, source_target_pairs={{0,2},{1,3},{2,0},{3,1},{4,6},{5,7},{6,4},{7,5},{8,10},{9,11},{10,... | collective-permute-start | bytes 835592 | tf_op jit(solution)/shard_map/ppermute | solution.py:23
  26.6 11.5 %collective-permute-start.9 = (bf16[2,64,768]{2,1,0:T(8,128)(2,1)S(1)}, bf16[2,64,768]{2,1,0:T(8,128)(2,1)S(1)}, u32[]{:S(2)}, u32[]{:S(2)}) collective-permute-start(bf16[2,64,768]{2,1,0:T(8,128)(2,1)S(1)} %shard_map.50), channel_id=1, source_target_pairs={{0,8},{1,9},{2,10},{3,11},{4,12},{5,13},{6,14},{7,15},{8,0},{9,1},... | collective-permute-start | bytes 589832 | tf_op jit(solution)/shard_map/ppermute | solution.py:23
  27.8 25.8 %collective-permute-start.7 = (bf16[64,2176]{1,0:T(8,128)(2,1)S(1)}, bf16[64,2176]{1,0:T(8,128)(2,1)S(1)}, u32[]{:S(2)}, u32[]{:S(2)}) collective-permute-start(bf16[64,2176]{1,0:T(8,128)(2,1)S(1)} %shard_map.51.refs_0_), channel_id=1, source_target_pairs={{0,2},{1,3},{2,0},{3,1},{4,6},{5,7},{6,4},{7,5},{8,10},{9,11},{10,... | collective-permute-start | bytes 835592 | tf_op jit(solution)/shard_map/ppermute | solution.py:23
  35.4 11.1 %collective-permute-start.12 = (bf16[64,2176]{1,0:T(8,128)(2,1)S(1)}, bf16[64,2176]{1,0:T(8,128)(2,1)S(1)}, u32[]{:S(2)}, u32[]{:S(2)}) collective-permute-start(bf16[64,2176]{1,0:T(8,128)(2,1)S(1)} %collective-permute-done.10.refs_0_), channel_id=1, source_target_pairs={{0,2},{1,3},{2,0},{3,1},{4,6},{5,7},{6,4},{7,5},{8,10},{9,11},{10,... | collective-permute-start | bytes 835592 | tf_op jit(solution)/shard_map/ppermute | solution.py:23
  36.6 24.4 %collective-permute-start.16 = (bf16[2,64,768]{2,1,0:T(8,128)(2,1)S(1)}, bf16[2,64,768]{2,1,0:T(8,128)(2,1)S(1)}, u32[]{:S(2)}, u32[]{:S(2)}) collective-permute-start(bf16[2,64,768]{2,1,0:T(8,128)(2,1)S(1)} %shard_map.52), channel_id=1, source_target_pairs={{0,12},{1,13},{2,14},{3,15},{4,8},{5,9},{6,10},{7,11},{8,4},{9,5},... | collective-permute-start | bytes 589832 | tf_op jit(solution)/shard_map/ppermute | solution.py:23
  39.5 21.4 %collective-permute-start.15 = (bf16[2,64,768]{2,1,0:T(8,128)(2,1)S(1)}, bf16[2,64,768]{2,1,0:T(8,128)(2,1)S(1)}, u32[]{:S(2)}, u32[]{:S(2)}) collective-permute-start(bf16[2,64,768]{2,1,0:T(8,128)(2,1)S(1)} %get-tuple-element.46), channel_id=1, source_target_pairs={{0,10},{1,11},{2,8},{3,9},{4,14},{5,15},{6,12},{7,13},{8,2},{9,3},... | collective-permute-start | bytes 589832 | tf_op jit(solution)/shard_map/ppermute | solution.py:23
  42.2 11.4 %collective-permute-start.11 = (bf16[2,64,768]{2,1,0:T(8,128)(2,1)S(1)}, bf16[2,64,768]{2,1,0:T(8,128)(2,1)S(1)}, u32[]{:S(2)}, u32[]{:S(2)}) collective-permute-start(bf16[2,64,768]{2,1,0:T(8,128)(2,1)S(1)} %get-tuple-element.45), channel_id=1, source_target_pairs={{0,2},{1,3},{2,0},{3,1},{4,6},{5,7},{6,4},{7,5},{8,10},{9,11},{10,... | collective-permute-start | bytes 589832 | tf_op jit(solution)/shard_map/ppermute | solution.py:23
  47.6 13.3 %copy-start.1 = (s32[1,64,8]{1,2,0:T(8,128)S(1)}, s32[1,64,8]{1,2,0:T(8,128)}, u32[]{:S(2)}) copy-start(s32[1,64,8]{1,2,0:T(8,128)} %param.5) | copy-start | bytes 6148
  47.6 13.3 %collective-permute-start.17 = (bf16[2,64,768]{2,1,0:T(8,128)(2,1)S(1)}, bf16[2,64,768]{2,1,0:T(8,128)(2,1)S(1)}, u32[]{:S(2)}, u32[]{:S(2)}) collective-permute-start(bf16[2,64,768]{2,1,0:T(8,128)(2,1)S(1)} %shard_map.54), channel_id=1, source_target_pairs={{0,14},{1,15},{2,12},{3,13},{4,10},{5,11},{6,8},{7,9},{8,6},{9,7},... | collective-permute-start | bytes 589832 | tf_op jit(solution)/shard_map/ppermute | solution.py:23
  54.6 10.7 %collective-permute-start.13 = (bf16[2,64,768]{2,1,0:T(8,128)(2,1)S(1)}, bf16[2,64,768]{2,1,0:T(8,128)(2,1)S(1)}, u32[]{:S(2)}, u32[]{:S(2)}) collective-permute-start(bf16[2,64,768]{2,1,0:T(8,128)(2,1)S(1)} %get-tuple-element.51), channel_id=1, source_target_pairs={{0,4},{1,5},{2,6},{3,7},{4,0},{5,1},{6,2},{7,3},{8,12},{9,13},{10,... | collective-permute-start | bytes 589832 | tf_op jit(solution)/shard_map/ppermute | solution.py:23
  59.8 8.9 %collective-permute-start.14 = (bf16[2,64,768]{2,1,0:T(8,128)(2,1)S(1)}, bf16[2,64,768]{2,1,0:T(8,128)(2,1)S(1)}, u32[]{:S(2)}, u32[]{:S(2)}) collective-permute-start(bf16[2,64,768]{2,1,0:T(8,128)(2,1)S(1)} %get-tuple-element.52), channel_id=1, source_target_pairs={{0,6},{1,7},{2,4},{3,5},{4,2},{5,3},{6,0},{7,1},{8,14},{9,15},{10,... | collective-permute-start | bytes 589832 | tf_op jit(solution)/shard_map/ppermute | solution.py:23

commit v28 on v27

--- a/solution.py
+++ b/solution.py
@@ -171,33 +171,34 @@
     near = send_across(upstream, owners, Z_NEAR)
     near_columns = send(columns, owners, Z_NEAR)
     weights = turned(weight_mat, other_mat)
-    rows, columns, weights, near_columns = tie((rows, columns, weights, near_columns))
-    rows = widened(rows, columns)
-    side = send(rows, owners, X)
-    far, far_columns, rows = tie((far, far_columns, rows))
+    weights, near_columns = tie((weights, near_columns))
+    far, far_columns, weights = tie((far, far_columns, weights))
     far = widened(far, far_columns)
     cross = send(far, owners, Z_NEAR)
     far_side = send(far, owners, X)
     (out_far,) = work(far)
     back_far = send(out_far, owners, Z_FAR)
-    side, _ = tie((side, out_far))
-    near, side = tie((near, side))
+    near, _ = tie((near, out_far))
     near = widened(near, near_columns)
     near_side = send(near, owners, X)
-    cross, near = tie((cross, near))
+    rows, near = tie((rows, near))
+    rows = widened(rows, columns)
+    side = send(rows, owners, X)
+    cross, near, rows = tie((cross, near, rows))
     cross_side = send(cross, owners, X)
     (out_cross,) = work(cross)
     back_cross = send(out_cross, owners, Z_NEAR ^ Z_FAR)
-    far_side, side, back_far, _ = tie((far_side, side, back_far, out_cross))
-    out_far_side, out_side, out_own = work(far_side, side, rows)
+    far_side, back_far, _ = tie((far_side, back_far, out_cross))
+    (out_far_side,) = work(far_side)
     back_far_side = send(out_far_side, owners, X ^ Z_FAR)
     cross_side, _ = tie((cross_side, out_far_side))
     (out_cross_side,) = work(cross_side)
     back_cross_side = send(out_cross_side, owners, X ^ Z_NEAR ^ Z_FAR)
+    near_side, side, _ = tie((near_side, side, out_cross_side))
+    out_own, out_side, out_near, out_near_side = work(rows, side, near, near_side)
+    back_near_side = send(out_near_side, owners, X ^ Z_NEAR)
+    out_side, back_far_side = tie((out_side, back_far_side))
     back_side = send(out_side, owners, X)
-    near_side, back_side, _ = tie((near_side, back_side, out_cross_side))
-    out_near, out_near_side = work(near, near_side)
-    back_near_side = send(out_near_side, owners, X ^ Z_NEAR)
     back_near = send(out_near, owners, Z_NEAR)
     far_parts = {
         0: out_own,

time: 70.2 us -> 70 us (level)
  starting transfers between devices: 35 us -> 30.7 us
  waiting for transfers between devices: 22.1 us -> 25.6 us
    ppermute x15, starting transfers between devices: 28.5 us -> 24.3 us  [send(): return lax.ppermute(block, 'expert', route)]
    ppermute x15, waiting for transfers between devices: 21.4 us -> 25.5 us  [send(): return lax.ppermute(block, 'expert', route)]
    ppermute x3, waiting for transfers between devices: 0.74 us -> 0.01 us  [send_across(): return lax.ppermute(block, ('pipe', 'expert'), route)]
  transfers between devices with their start and end apart: 18 -> 18, of which waited for: 7 -> 7; matrix products, arithmetic and copies ran while one was open for 0% -> 0% of each run, Pallas kernels for 12% -> 13%
where the time goes in v28:
time: 70 us; the launch traced here: 69.8 us
  starting transfers between devices  30.7 us (44%)
  waiting for transfers between devices  25.6 us (37%)
  Pallas kernels  10.1 us (14%)
  local copies, waits for them, and re-layouts  3.26 us (5%)
    ppermute x15, waiting for transfers between devices, send(): return lax.ppermute(block, 'expert', route)  25.5 us
    ppermute x15, starting transfers between devices, send(): return lax.ppermute(block, 'expert', route)  24.3 us
    pallas_call x5, Pallas kernels, products(): pl.pallas_call(functools.partial(products_kernel, len(pieces)), out_shape...  6.55 us
    ppermute x3, starting transfers between devices, send_across(): return lax.ppermute(block, ('pipe', 'expert'), route)  6.45 us
    unnamed x8, local copies, waits for them, and re-layouts  3.26 us
    pallas_call x2, Pallas kernels, pick_routes(): pl.pallas_call(functools.partial(pick_kernel, flips), out_shape=jax.Shape...  1.74 us
    pallas_call x1, Pallas kernels, turned(): pl.pallas_call(turn_kernel, out_shape=jax.ShapeDtypeStruct((depth, CORES...  1.67 us
  transfers between devices with their start and end apart: 18, of which 7 were waited for; matrix products, arithmetic and copies ran while one was open for 0% of the time, Pallas kernels for 13%

profile of v28, /device:TPU:0, one launch (start us, length us, event | category | flops | bytes accessed | tf_op | source)
XLA Modules:
  0.0 69.8 jit_solution(12373972556684557084)
XLA Ops:
  0.0 0.5 collective-permute-start.2
  0.5 4.5 %collective-permute-start = (bf16[64,2048]{1,0:T(8,128)(2,1)}, bf16[64,2048]{1,0:T(8,128)(2,1)S(1)}, u32[]{:S(2)}, u32[]{:S(2)}) collective-permute-start(bf16[64,2048]{1,0:T(8,128)(2,1)} %bitcast.15), channel_id=1, source_target_pairs={{0,24},{1,25},{2,26},{3,27},{4,28},{5,29},{6,30},{7,31},{8,16},{9,... | collective-permute-start | bytes 786440 | tf_op jit(solution)/shard_map/ppermute | solution.py:33
  5.0 0.5 collective-permute-start.5
  5.5 0.0 copy-start
  5.5 0.7 copy-done
  6.2 0.0 copy-start.2
  6.2 0.7 copy-done.2
  6.9 0.1 shard_map.46.columns
  7.0 0.2 collective-permute-start.1
  7.1 1.8 %collective-permute-start.3 = (bf16[64,128]{1,0:T(8,128)(2,1)S(1)}, bf16[64,128]{1,0:T(8,128)(2,1)S(1)}, u32[]{:S(2)}, u32[]{:S(2)}) collective-permute-start(bf16[64,128]{1,0:T(8,128)(2,1)S(1)} %shard_map.46.columns), channel_id=1, source_target_pairs={{0,4},{1,5},{2,6},{3,7},{4,0},{5,1},{6,2},{7,3},{8,12},{9,13},{10,... | collective-permute-start | bytes 49160 | tf_op jit(solution)/shard_map/ppermute | solution.py:23
  8.9 0.0 collective-permute-done.2.other
  8.9 1.4 %collective-permute-start.6 = (bf16[64,2048]{1,0:T(8,128)(2,1)}, bf16[64,2048]{1,0:T(8,128)(2,1)S(1)}, u32[]{:S(2)}, u32[]{:S(2)}) collective-permute-start(bf16[64,2048]{1,0:T(8,128)(2,1)} %bitcast.17), channel_id=1, source_target_pairs={{0,20},{1,21},{2,22},{3,23},{4,16},{5,17},{6,18},{7,19},{8,28},{9,... | collective-permute-start | bytes 786440 | tf_op jit(solution)/shard_map/ppermute | solution.py:33
  10.3 0.0 copy-start.3
  10.3 1.9 %copy-done.3 = bf16[1,1,768,2048]{3,2,1,0:T(8,128)(2,1)S(1)} copy-done((bf16[1,1,768,2048]{3,2,1,0:T(8,128)(2,1)S(1)}, bf16[1,1,768,2048]{3,2,1,0:T(8,128)(2,1)}, u32[]{:S(2)}) %copy-start.3) | copy-done | bytes 3145752
  12.2 1.7 %shard_map.47.weights = bf16[2048,1536]{1,0:T(8,128)(2,1)S(1)} custom-call(bf16[768,2048]{1,0:T(8,128)(2,1)S(1)} %bitcast.14, bf16[768,2048]{1,0:T(8,128)(2,1)S(1)} %collective-permute-done.2.other), custom_call_target="tpu_custom_call" | custom-call | flops 12884901888 | tf_op jit(solution)/shard_map/pallas_call | solution.py:77
  13.9 0.0 collective-permute-done.3.columns
  13.9 4.7 %collective-permute-done.1.columns = bf16[64,128]{1,0:T(8,128)(2,1)S(1)} collective-permute-done((bf16[64,128]{1,0:T(8,128)(2,1)S(1)}, bf16[64,128]{1,0:T(8,128)(2,1)S(1)}, u32[]{:S(2)}, u32[]{:S(2)}) %collective-permute-start.1) | collective-permute-done | bytes 16416 | tf_op jit(solution)/shard_map/ppermute | solution.py:23
  18.7 0.0 collective-permute-done.rows
  18.7 0.7 %collective-permute-start.4 = (bf16[64,2176]{1,0:T(8,128)(2,1)S(1)}, bf16[64,2176]{1,0:T(8,128)(2,1)S(1)}, u32[]{:S(2)}, u32[]{:S(2)}) collective-permute-start(bf16[64,2176]{1,0:T(8,128)(2,1)S(1)} %shard_map.48.refs_0_), channel_id=1, source_target_pairs={{0,4},{1,5},{2,6},{3,7},{4,0},{5,1},{6,2},{7,3},{8,12},{9,13},{10,... | collective-permute-start | bytes 835592 | tf_op jit(solution)/shard_map/ppermute | solution.py:23
  19.4 1.5 %collective-permute-start.10 = (bf16[64,2176]{1,0:T(8,128)(2,1)S(1)}, bf16[64,2176]{1,0:T(8,128)(2,1)S(1)}, u32[]{:S(2)}, u32[]{:S(2)}) collective-permute-start(bf16[64,2176]{1,0:T(8,128)(2,1)S(1)} %shard_map.48.refs_0_), channel_id=1, source_target_pairs={{0,2},{1,3},{2,0},{3,1},{4,6},{5,7},{6,4},{7,5},{8,10},{9,11},{10,... | collective-permute-start | bytes 835592 | tf_op jit(solution)/shard_map/ppermute | solution.py:23
  20.9 1.2 %shard_map.49 = bf16[2,64,768]{2,1,0:T(8,128)(2,1)S(1)} custom-call(bf16[2048,1536]{1,0:T(8,128)(2,1)S(1)} %shard_map.47.weights, bf16[64,2176]{1,0:T(8,128)(2,1)S(1)} %shard_map.48.refs_0_), custom_call_target="tpu_custom_call" | custom-call | flops 4026531840 | bytes 6750208 | tf_op jit(solution)/shard_map/pallas_call | solution.py:109
  22.1 3.5 %collective-permute-start.11 = (bf16[2,64,768]{2,1,0:T(8,128)(2,1)S(1)}, bf16[2,64,768]{2,1,0:T(8,128)(2,1)S(1)}, u32[]{:S(2)}, u32[]{:S(2)}) collective-permute-start(bf16[2,64,768]{2,1,0:T(8,128)(2,1)S(1)} %shard_map.49), channel_id=1, source_target_pairs={{0,8},{1,9},{2,10},{3,11},{4,12},{5,13},{6,14},{7,15},{8,0},{9,1},... | collective-permute-start | bytes 589832 | tf_op jit(solution)/shard_map/ppermute | solution.py:23
  25.6 0.0 collective-permute-done.6.rows
  25.6 0.6 collective-permute-start.7
  26.2 0.0 collective-permute-done.5.rows
  26.2 1.6 %collective-permute-start.8 = (bf16[64,2176]{1,0:T(8,128)(2,1)S(1)}, bf16[64,2176]{1,0:T(8,128)(2,1)S(1)}, u32[]{:S(2)}, u32[]{:S(2)}) collective-permute-start(bf16[64,2176]{1,0:T(8,128)(2,1)S(1)} %shard_map.51.refs_0_), channel_id=1, source_target_pairs={{0,2},{1,3},{2,0},{3,1},{4,6},{5,7},{6,4},{7,5},{8,10},{9,11},{10,... | collective-permute-start | bytes 835592 | tf_op jit(solution)/shard_map/ppermute | solution.py:23
  27.8 4.0 %collective-permute-done.4.refs_0_ = bf16[64,2176]{1,0:T(8,128)(2,1)S(1)} collective-permute-done((bf16[64,2176]{1,0:T(8,128)(2,1)S(1)}, bf16[64,2176]{1,0:T(8,128)(2,1)S(1)}, u32[]{:S(2)}, u32[]{:S(2)}) %collective-permute-start.4) | collective-permute-done | bytes 278560 | tf_op jit(solution)/shard_map/ppermute | solution.py:23
  31.8 2.4 %collective-permute-start.9 = (bf16[64,2176]{1,0:T(8,128)(2,1)S(1)}, bf16[64,2176]{1,0:T(8,128)(2,1)S(1)}, u32[]{:S(2)}, u32[]{:S(2)}) collective-permute-start(bf16[64,2176]{1,0:T(8,128)(2,1)S(1)} %collective-permute-done.4.refs_0_), channel_id=1, source_target_pairs={{0,2},{1,3},{2,0},{3,1},{4,6},{5,7},{6,4},{7,5},{8,10},{9,11},{10,... | collective-permute-start | bytes 835592 | tf_op jit(solution)/shard_map/ppermute | solution.py:23
  34.3 1.2 %shard_map.52 = bf16[2,64,768]{2,1,0:T(8,128)(2,1)S(1)} custom-call(bf16[2048,1536]{1,0:T(8,128)(2,1)S(1)} %shard_map.47.weights, bf16[64,2176]{1,0:T(8,128)(2,1)S(1)} %collective-permute-done.4.refs_0_), custom_call_target="tpu_custom_call" | custom-call | flops 4026531840 | bytes 6750208 | tf_op jit(solution)/shard_map/pallas_call | solution.py:109
  35.5 0.0 collective-permute-done.11.refs_1_
  35.5 3.8 %collective-permute-start.16 = (bf16[2,64,768]{2,1,0:T(8,128)(2,1)S(1)}, bf16[2,64,768]{2,1,0:T(8,128)(2,1)S(1)}, u32[]{:S(2)}, u32[]{:S(2)}) collective-permute-start(bf16[2,64,768]{2,1,0:T(8,128)(2,1)S(1)} %shard_map.52), channel_id=1, source_target_pairs={{0,12},{1,13},{2,14},{3,15},{4,8},{5,9},{6,10},{7,11},{8,4},{9,5},... | collective-permute-start | bytes 589832 | tf_op jit(solution)/shard_map/ppermute | solution.py:23
  39.3 0.0 collective-permute-done.10.refs_0_
  39.3 1.2 %shard_map.53 = bf16[2,64,768]{2,1,0:T(8,128)(2,1)S(1)} custom-call(bf16[2048,1536]{1,0:T(8,128)(2,1)S(1)} %shard_map.47.weights, bf16[64,2176]{1,0:T(8,128)(2,1)S(1)} %collective-permute-done.10.refs_0_), custom_call_target="tpu_custom_call" | custom-call | flops 4026531840 | bytes 6750208 | tf_op jit(solution)/shard_map/pallas_call | solution.py:109
  40.5 0.1 collective-permute-start.12
  40.5 5.1 %collective-permute-done.9.refs_0_ = bf16[64,2176]{1,0:T(8,128)(2,1)S(1)} collective-permute-done((bf16[64,2176]{1,0:T(8,128)(2,1)S(1)}, bf16[64,2176]{1,0:T(8,128)(2,1)S(1)}, u32[]{:S(2)}, u32[]{:S(2)}) %collective-permute-start.9) | collective-permute-done | bytes 278560 | tf_op jit(solution)/shard_map/ppermute | solution.py:23
  45.6 1.2 %shard_map.54 = bf16[2,64,768]{2,1,0:T(8,128)(2,1)S(1)} custom-call(bf16[2048,1536]{1,0:T(8,128)(2,1)S(1)} %shard_map.47.weights, bf16[64,2176]{1,0:T(8,128)(2,1)S(1)} %collective-permute-done.9.refs_0_), custom_call_target="tpu_custom_call" | custom-call | flops 4026531840 | bytes 6750208 | tf_op jit(solution)/shard_map/pallas_call | solution.py:109
  46.8 0.0 copy-start.1
  46.8 4.3 %collective-permute-start.17 = (bf16[2,64,768]{2,1,0:T(8,128)(2,1)S(1)}, bf16[2,64,768]{2,1,0:T(8,128)(2,1)S(1)}, u32[]{:S(2)}, u32[]{:S(2)}) collective-permute-start(bf16[2,64,768]{2,1,0:T(8,128)(2,1)S(1)} %shard_map.54), channel_id=1, source_target_pairs={{0,14},{1,15},{2,12},{3,13},{4,10},{5,11},{6,8},{7,9},{8,6},{9,7},... | collective-permute-start | bytes 589832 | tf_op jit(solution)/shard_map/ppermute | solution.py:23
  51.1 0.0 collective-permute-done.8.refs_1_
  51.1 0.0 collective-permute-done.7.refs_3_
  51.1 1.8 %shard_map.55 = (bf16[2,64,768]{2,1,0:T(8,128)(2,1)S(1)}, bf16[2,64,768]{2,1,0:T(8,128)(2,1)S(1)}, bf16[2,64,768]{2,1,0:T(8,128)(2,1)S(1)}, bf16[2,64,768]{2,1,0:T(8,128)(2,1)S(1)}) custom-call(bf16[2048,1536]{1,0:T(8,128)(2,1)S(1)} %shard_map.47.weights, bf16[64,2176]{1,0:T(8,128)(2,1)S(1)} %shard_map.51.refs_0_, ...), custom_call_target="tpu_custom_call" | custom-call | flops 16106127360 | bytes 8126464 | tf_op jit(solution)/shard_map/pallas_call | solution.py:109
  52.9 6.3 %collective-permute-done.12.refs_2_ = bf16[2,64,768]{2,1,0:T(8,128)(2,1)S(1)} collective-permute-done((bf16[2,64,768]{2,1,0:T(8,128)(2,1)S(1)}, bf16[2,64,768]{2,1,0:T(8,128)(2,1)S(1)}, u32[]{:S(2)}, u32[]{:S(2)}) %collective-permute-start.12) | collective-permute-done | bytes 196640 | tf_op jit(solution)/shard_map/ppermute | solution.py:23
  59.2 1.2 %collective-permute-start.13 = (bf16[2,64,768]{2,1,0:T(8,128)(2,1)S(1)}, bf16[2,64,768]{2,1,0:T(8,128)(2,1)S(1)}, u32[]{:S(2)}, u32[]{:S(2)}) collective-permute-start(bf16[2,64,768]{2,1,0:T(8,128)(2,1)S(1)} %get-tuple-element.47), channel_id=1, source_target_pairs={{0,2},{1,3},{2,0},{3,1},{4,6},{5,7},{6,4},{7,5},{8,10},{9,11},{10,... | collective-permute-start | bytes 589832 | tf_op jit(solution)/shard_map/ppermute | solution.py:23
  60.5 0.0 collective-permute-start.14
  60.5 2.2 %collective-permute-start.15 = (bf16[2,64,768]{2,1,0:T(8,128)(2,1)S(1)}, bf16[2,64,768]{2,1,0:T(8,128)(2,1)S(1)}, u32[]{:S(2)}, u32[]{:S(2)}) collective-permute-start(bf16[2,64,768]{2,1,0:T(8,128)(2,1)S(1)} %get-tuple-element.49), channel_id=1, source_target_pairs={{0,6},{1,7},{2,4},{3,5},{4,2},{5,3},{6,0},{7,1},{8,14},{9,15},{10,... | collective-permute-start | bytes 589832 | tf_op jit(solution)/shard_map/ppermute | solution.py:23
  62.7 0.0 collective-permute-done.16.refs_3_
  62.7 0.0 collective-permute-done.17.refs_4_
  62.7 0.0 copy-done.1
  62.7 0.4 shard_map.56.refs_3_
  63.2 2.6 %collective-permute-done.13.refs_0_ = bf16[2,64,768]{2,1,0:T(8,128)(2,1)S(1)} collective-permute-done((bf16[2,64,768]{2,1,0:T(8,128)(2,1)S(1)}, bf16[2,64,768]{2,1,0:T(8,128)(2,1)S(1)}, u32[]{:S(2)}, u32[]{:S(2)}) %collective-permute-start.13) | collective-permute-done | bytes 196640 | tf_op jit(solution)/shard_map/ppermute | solution.py:23
  65.8 0.4 collective-permute-done.14.refs_1_
  66.2 2.3 %collective-permute-done.15.refs_2_ = bf16[2,64,768]{2,1,0:T(8,128)(2,1)S(1)} collective-permute-done((bf16[2,64,768]{2,1,0:T(8,128)(2,1)S(1)}, bf16[2,64,768]{2,1,0:T(8,128)(2,1)S(1)}, u32[]{:S(2)}, u32[]{:S(2)}) %collective-permute-start.15) | collective-permute-done | bytes 196640 | tf_op jit(solution)/shard_map/ppermute | solution.py:23
  68.5 1.3 %shard_map.57 = bf16[512,768]{1,0:T(8,128)(2,1)} custom-call(s32[8,64]{1,0:T(8,128)S(1)} %bitcast.11, bf16[2,64,768]{2,1,0:T(8,128)(2,1)S(1)} %collective-permute-done.13.refs_0_, bf16[2,64,768]{2,1,0:T(8,128)(2,1)S(1)} %collective-permute-done.14.refs_1_, bf16[2,64,768]{2,1,0:T(8,128)(2,1)S(1)} %collective-permute-done.15.refs_2_, ...), custom_call_target="tpu_custom_call" | custom-call | tf_op jit(solution)/shard_map/pallas_call | solution.py:150
  (3 shorter events, 0.1 us)
Async XLA Ops:
  0.0 8.9 %collective-permute-start.2 = (bf16[768,2048]{1,0:T(8,128)(2,1)}, bf16[768,2048]{1,0:T(8,128)(2,1)S(1)}, u32[]{:S(2)}, u32[]{:S(2)}) collective-permute-start(bf16[768,2048]{1,0:T(8,128)(2,1)} %bitcast.13), channel_id=1, source_target_pairs={{0,1},{1,0},{2,3},{3,2},{4,5},{5,4},{6,7},{7,6},{8,9},{9,8},{10,11... | collective-permute-start | bytes 9437192 | tf_op jit(solution)/shard_map/ppermute | solution.py:23
  0.5 18.2 %collective-permute-start = (bf16[64,2048]{1,0:T(8,128)(2,1)}, bf16[64,2048]{1,0:T(8,128)(2,1)S(1)}, u32[]{:S(2)}, u32[]{:S(2)}) collective-permute-start(bf16[64,2048]{1,0:T(8,128)(2,1)} %bitcast.15), channel_id=1, source_target_pairs={{0,24},{1,25},{2,26},{3,27},{4,28},{5,29},{6,30},{7,31},{8,16},{9,... | collective-permute-start | bytes 786440 | tf_op jit(solution)/shard_map/ppermute | solution.py:33
  5.0 21.2 %collective-permute-start.5 = (bf16[64,2048]{1,0:T(8,128)(2,1)}, bf16[64,2048]{1,0:T(8,128)(2,1)S(1)}, u32[]{:S(2)}, u32[]{:S(2)}) collective-permute-start(bf16[64,2048]{1,0:T(8,128)(2,1)} %bitcast.16), channel_id=1, source_target_pairs={{0,16},{1,17},{2,18},{3,19},{4,20},{5,21},{6,22},{7,23},{8,24},{9,... | collective-permute-start | bytes 786440 | tf_op jit(solution)/shard_map/ppermute | solution.py:33
  5.5 0.7 copy-start
  6.2 0.7 copy-start.2
  7.0 11.7 %collective-permute-start.1 = (bf16[64,128]{1,0:T(8,128)(2,1)S(1)}, bf16[64,128]{1,0:T(8,128)(2,1)S(1)}, u32[]{:S(2)}, u32[]{:S(2)}) collective-permute-start(bf16[64,128]{1,0:T(8,128)(2,1)S(1)} %shard_map.46.columns), channel_id=1, source_target_pairs={{0,8},{1,9},{2,10},{3,11},{4,12},{5,13},{6,14},{7,15},{8,0},{9,1},... | collective-permute-start | bytes 49160 | tf_op jit(solution)/shard_map/ppermute | solution.py:23
  7.1 6.8 %collective-permute-start.3 = (bf16[64,128]{1,0:T(8,128)(2,1)S(1)}, bf16[64,128]{1,0:T(8,128)(2,1)S(1)}, u32[]{:S(2)}, u32[]{:S(2)}) collective-permute-start(bf16[64,128]{1,0:T(8,128)(2,1)S(1)} %shard_map.46.columns), channel_id=1, source_target_pairs={{0,4},{1,5},{2,6},{3,7},{4,0},{5,1},{6,2},{7,3},{8,12},{9,13},{10,... | collective-permute-start | bytes 49160 | tf_op jit(solution)/shard_map/ppermute | solution.py:23
  8.9 16.6 %collective-permute-start.6 = (bf16[64,2048]{1,0:T(8,128)(2,1)}, bf16[64,2048]{1,0:T(8,128)(2,1)S(1)}, u32[]{:S(2)}, u32[]{:S(2)}) collective-permute-start(bf16[64,2048]{1,0:T(8,128)(2,1)} %bitcast.17), channel_id=1, source_target_pairs={{0,20},{1,21},{2,22},{3,23},{4,16},{5,17},{6,18},{7,19},{8,28},{9,... | collective-permute-start | bytes 786440 | tf_op jit(solution)/shard_map/ppermute | solution.py:33
  10.3 1.9 %copy-start.3 = (bf16[1,1,768,2048]{3,2,1,0:T(8,128)(2,1)S(1)}, bf16[1,1,768,2048]{3,2,1,0:T(8,128)(2,1)}, u32[]{:S(2)}) copy-start(bf16[1,1,768,2048]{3,2,1,0:T(8,128)(2,1)} %param.7) | copy-start | bytes 9437188
  18.7 13.1 %collective-permute-start.4 = (bf16[64,2176]{1,0:T(8,128)(2,1)S(1)}, bf16[64,2176]{1,0:T(8,128)(2,1)S(1)}, u32[]{:S(2)}, u32[]{:S(2)}) collective-permute-start(bf16[64,2176]{1,0:T(8,128)(2,1)S(1)} %shard_map.48.refs_0_), channel_id=1, source_target_pairs={{0,4},{1,5},{2,6},{3,7},{4,0},{5,1},{6,2},{7,3},{8,12},{9,13},{10,... | collective-permute-start | bytes 835592 | tf_op jit(solution)/shard_map/ppermute | solution.py:23
  19.4 19.9 %collective-permute-start.10 = (bf16[64,2176]{1,0:T(8,128)(2,1)S(1)}, bf16[64,2176]{1,0:T(8,128)(2,1)S(1)}, u32[]{:S(2)}, u32[]{:S(2)}) collective-permute-start(bf16[64,2176]{1,0:T(8,128)(2,1)S(1)} %shard_map.48.refs_0_), channel_id=1, source_target_pairs={{0,2},{1,3},{2,0},{3,1},{4,6},{5,7},{6,4},{7,5},{8,10},{9,11},{10,... | collective-permute-start | bytes 835592 | tf_op jit(solution)/shard_map/ppermute | solution.py:23
  22.1 13.4 %collective-permute-start.11 = (bf16[2,64,768]{2,1,0:T(8,128)(2,1)S(1)}, bf16[2,64,768]{2,1,0:T(8,128)(2,1)S(1)}, u32[]{:S(2)}, u32[]{:S(2)}) collective-permute-start(bf16[2,64,768]{2,1,0:T(8,128)(2,1)S(1)} %shard_map.49), channel_id=1, source_target_pairs={{0,8},{1,9},{2,10},{3,11},{4,12},{5,13},{6,14},{7,15},{8,0},{9,1},... | collective-permute-start | bytes 589832 | tf_op jit(solution)/shard_map/ppermute | solution.py:23
  25.6 25.5 %collective-permute-start.7 = (bf16[64,2176]{1,0:T(8,128)(2,1)S(1)}, bf16[64,2176]{1,0:T(8,128)(2,1)S(1)}, u32[]{:S(2)}, u32[]{:S(2)}) collective-permute-start(bf16[64,2176]{1,0:T(8,128)(2,1)S(1)} %shard_map.50.refs_2_), channel_id=1, source_target_pairs={{0,2},{1,3},{2,0},{3,1},{4,6},{5,7},{6,4},{7,5},{8,10},{9,11},{10,... | collective-permute-start | bytes 835592 | tf_op jit(solution)/shard_map/ppermute | solution.py:23
  26.2 24.9 %collective-permute-start.8 = (bf16[64,2176]{1,0:T(8,128)(2,1)S(1)}, bf16[64,2176]{1,0:T(8,128)(2,1)S(1)}, u32[]{:S(2)}, u32[]{:S(2)}) collective-permute-start(bf16[64,2176]{1,0:T(8,128)(2,1)S(1)} %shard_map.51.refs_0_), channel_id=1, source_target_pairs={{0,2},{1,3},{2,0},{3,1},{4,6},{5,7},{6,4},{7,5},{8,10},{9,11},{10,... | collective-permute-start | bytes 835592 | tf_op jit(solution)/shard_map/ppermute | solution.py:23
  31.8 13.8 %collective-permute-start.9 = (bf16[64,2176]{1,0:T(8,128)(2,1)S(1)}, bf16[64,2176]{1,0:T(8,128)(2,1)S(1)}, u32[]{:S(2)}, u32[]{:S(2)}) collective-permute-start(bf16[64,2176]{1,0:T(8,128)(2,1)S(1)} %collective-permute-done.4.refs_0_), channel_id=1, source_target_pairs={{0,2},{1,3},{2,0},{3,1},{4,6},{5,7},{6,4},{7,5},{8,10},{9,11},{10,... | collective-permute-start | bytes 835592 | tf_op jit(solution)/shard_map/ppermute | solution.py:23
  35.5 27.3 %collective-permute-start.16 = (bf16[2,64,768]{2,1,0:T(8,128)(2,1)S(1)}, bf16[2,64,768]{2,1,0:T(8,128)(2,1)S(1)}, u32[]{:S(2)}, u32[]{:S(2)}) collective-permute-start(bf16[2,64,768]{2,1,0:T(8,128)(2,1)S(1)} %shard_map.52), channel_id=1, source_target_pairs={{0,12},{1,13},{2,14},{3,15},{4,8},{5,9},{6,10},{7,11},{8,4},{9,5},... | collective-permute-start | bytes 589832 | tf_op jit(solution)/shard_map/ppermute | solution.py:23
  40.5 18.8 %collective-permute-start.12 = (bf16[2,64,768]{2,1,0:T(8,128)(2,1)S(1)}, bf16[2,64,768]{2,1,0:T(8,128)(2,1)S(1)}, u32[]{:S(2)}, u32[]{:S(2)}) collective-permute-start(bf16[2,64,768]{2,1,0:T(8,128)(2,1)S(1)} %shard_map.53), channel_id=1, source_target_pairs={{0,10},{1,11},{2,8},{3,9},{4,14},{5,15},{6,12},{7,13},{8,2},{9,3},... | collective-permute-start | bytes 589832 | tf_op jit(solution)/shard_map/ppermute | solution.py:23
  46.8 15.9 %copy-start.1 = (s32[1,64,8]{1,2,0:T(8,128)S(1)}, s32[1,64,8]{1,2,0:T(8,128)}, u32[]{:S(2)}) copy-start(s32[1,64,8]{1,2,0:T(8,128)} %param.5) | copy-start | bytes 6148
  46.8 15.9 %collective-permute-start.17 = (bf16[2,64,768]{2,1,0:T(8,128)(2,1)S(1)}, bf16[2,64,768]{2,1,0:T(8,128)(2,1)S(1)}, u32[]{:S(2)}, u32[]{:S(2)}) collective-permute-start(bf16[2,64,768]{2,1,0:T(8,128)(2,1)S(1)} %shard_map.54), channel_id=1, source_target_pairs={{0,14},{1,15},{2,12},{3,13},{4,10},{5,11},{6,8},{7,9},{8,6},{9,7},... | collective-permute-start | bytes 589832 | tf_op jit(solution)/shard_map/ppermute | solution.py:23
  59.2 6.5 %collective-permute-start.13 = (bf16[2,64,768]{2,1,0:T(8,128)(2,1)S(1)}, bf16[2,64,768]{2,1,0:T(8,128)(2,1)S(1)}, u32[]{:S(2)}, u32[]{:S(2)}) collective-permute-start(bf16[2,64,768]{2,1,0:T(8,128)(2,1)S(1)} %get-tuple-element.47), channel_id=1, source_target_pairs={{0,2},{1,3},{2,0},{3,1},{4,6},{5,7},{6,4},{7,5},{8,10},{9,11},{10,... | collective-permute-start | bytes 589832 | tf_op jit(solution)/shard_map/ppermute | solution.py:23
  60.5 5.7 %collective-permute-start.14 = (bf16[2,64,768]{2,1,0:T(8,128)(2,1)S(1)}, bf16[2,64,768]{2,1,0:T(8,128)(2,1)S(1)}, u32[]{:S(2)}, u32[]{:S(2)}) collective-permute-start(bf16[2,64,768]{2,1,0:T(8,128)(2,1)S(1)} %get-tuple-element.48), channel_id=1, source_target_pairs={{0,4},{1,5},{2,6},{3,7},{4,0},{5,1},{6,2},{7,3},{8,12},{9,13},{10,... | collective-permute-start | bytes 589832 | tf_op jit(solution)/shard_map/ppermute | solution.py:23
  60.5 8.0 %collective-permute-start.15 = (bf16[2,64,768]{2,1,0:T(8,128)(2,1)S(1)}, bf16[2,64,768]{2,1,0:T(8,128)(2,1)S(1)}, u32[]{:S(2)}, u32[]{:S(2)}) collective-permute-start(bf16[2,64,768]{2,1,0:T(8,128)(2,1)S(1)} %get-tuple-element.49), channel_id=1, source_target_pairs={{0,6},{1,7},{2,4},{3,5},{4,2},{5,3},{6,0},{7,1},{8,14},{9,15},{10,... | collective-permute-start | bytes 589832 | tf_op jit(solution)/shard_map/ppermute | solution.py:23

commit v29 on v19

--- a/solution.py
+++ b/solution.py
@@ -51,19 +51,24 @@
     )(ids, gates)
 
 
-def widen_kernel(rows, columns, out):
-    depth = rows.shape[1]
-    out[:, :depth] = rows[...]
-    out[:, depth:] = columns[...]
+def widen_kernel(*refs):
+    third = len(refs) // 3
+    for rows, columns, out in zip(refs[:third], refs[third : 2 * third], refs[2 * third :]):
+        depth = rows.shape[1]
+        out[:, :depth] = rows[...]
+        out[:, depth:] = columns[...]
 
 
 def widened(rows, columns):
-    width = rows.shape[1] + columns.shape[1]
+    shapes = [
+        jax.ShapeDtypeStruct((r.shape[0], r.shape[1] + c.shape[1]), jnp.bfloat16)
+        for r, c in zip(rows, columns)
+    ]
     return pl.pallas_call(
         widen_kernel,
-        out_shape=jax.ShapeDtypeStruct((rows.shape[0], width), jnp.bfloat16),
-        compiler_params=pltpu.CompilerParams(vmem_limit_bytes=16 << 20),
-    )(rows, columns)
+        out_shape=shapes,
+        compiler_params=pltpu.CompilerParams(vmem_limit_bytes=16 << 20),
+    )(*rows, *columns)
 
 
 def turn_kernel(weight, other, out):
@@ -163,35 +168,39 @@
         return products(list(pieces), tokens, weights)
 
     far = send_across(upstream, owners, Z_FAR)
-    rows = send_across(upstream, owners, 0)
+    side = send_across(upstream, owners, X)
     other_mat = send(weight_mat, owners, 0, 1)
+    route_gates, other_mat = tie((route_gates, other_mat))
     columns = gate_columns(route_ids.T, route_gates.T)
     far_columns = send(columns, owners, Z_FAR)
+    side_columns = send(columns, owners, X)
+    rows = send_across(upstream, owners, 0)
     weights = turned(weight_mat, other_mat)
-    rows, columns, weights = tie((rows, columns, weights))
-    rows = widened(rows, columns)
-    side = send(rows, owners, X)
-    far, far_columns, rows = tie((far, far_columns, rows))
-    far = widened(far, far_columns)
+    far, far_columns, side, side_columns, weights = tie(
+        (far, far_columns, side, side_columns, weights)
+    )
+    far, side = widened([far, side], [far_columns, side_columns])
     cross = send(far, owners, Z_NEAR)
     far_side = send(far, owners, X)
-    (out_far,) = work(far)
+    out_far, out_side = work(far, side)
     back_far = send(out_far, owners, Z_FAR)
-    side, rows, _ = tie((side, rows, out_far))
+    rows, columns, _ = tie((rows, columns, out_far))
+    (rows,) = widened([rows], [columns])
     near = send(rows, owners, Z_NEAR)
-    out_side, out_own = work(side, rows)
-    back_side = send(out_side, owners, X)
-    cross, _ = tie((cross, out_own))
+    back_side = send(tie((out_side, rows))[0], owners, X)
+    cross, rows = tie((cross, rows))
     cross_side = send(cross, owners, X)
     (out_cross,) = work(cross)
     back_cross = send(out_cross, owners, Z_NEAR ^ Z_FAR)
-    far_side, back_far, near, _ = tie((far_side, back_far, near, out_cross))
+    far_side, back_far, near, back_side, _ = tie((far_side, back_far, near, back_side, out_cross))
     near_side = send(near, owners, X)
     (out_far_side,) = work(far_side)
     back_far_side = send(out_far_side, owners, X ^ Z_FAR)
-    cross_side, near_side, back_side, _ = tie((cross_side, near_side, back_side, out_far_side))
-    out_cross_side, out_near, out_near_side = work(cross_side, near, near_side)
+    cross_side, _ = tie((cross_side, out_far_side))
+    (out_cross_side,) = work(cross_side)
     back_cross_side = send(out_cross_side, owners, X ^ Z_NEAR ^ Z_FAR)
+    near_side, _ = tie((near_side, out_cross_side))
+    out_near, out_near_side, out_own = work(near, near_side, rows)
     back_near_side = send(out_near_side, owners, X ^ Z_NEAR)
     back_near = send(out_near, owners, Z_NEAR)
     far_parts = {

time: 68.9 us -> 68.6 us (level)
  the two profiles are of different devices: /device:TPU:0 before, /device:TPU:24 now
where the time goes in v29:
time: 68.6 us; the launch traced here: 68.4 us
  waiting for transfers between devices  29.3 us (43%)
  starting transfers between devices  26.2 us (38%)
  Pallas kernels  9.52 us (14%)
  local copies, waits for them, and re-layouts  3.26 us (5%)
    ppermute x15, waiting for transfers between devices, send(): return lax.ppermute(block, 'expert', route)  24.7 us
    ppermute x15, starting transfers between devices, send(): return lax.ppermute(block, 'expert', route)  22 us
    pallas_call x5, Pallas kernels, products(): pl.pallas_call(functools.partial(products_kernel, len(pieces)), out_shape...  5.94 us
    ppermute x3, waiting for transfers between devices, send_across(): return lax.ppermute(block, ('pipe', 'expert'), route)  4.64 us
    ppermute x3, starting transfers between devices, send_across(): return lax.ppermute(block, ('pipe', 'expert'), route)  4.24 us
    unnamed x8, local copies, waits for them, and re-layouts  3.26 us
    pallas_call x2, Pallas kernels, pick_routes(): pl.pallas_call(functools.partial(pick_kernel, flips), out_shape=jax.Shape...  1.74 us
    pallas_call x1, Pallas kernels, turned(): pl.pallas_call(turn_kernel, out_shape=jax.ShapeDtypeStruct((depth, CORES...  1.67 us
  transfers between devices with their start and end apart: 18, of which 9 were waited for; matrix products, arithmetic and copies ran while one was open for 0% of the time, Pallas kernels for 12%

profile of v29, /device:TPU:24, one launch (start us, length us, event | category | flops | bytes accessed | tf_op | source)
XLA Modules:
  0.0 68.4 jit_solution(2369223968697301339)
XLA Ops:
  0.0 0.0 collective-permute-start.1
  0.0 1.3 %collective-permute-start = (bf16[64,2048]{1,0:T(8,128)(2,1)}, bf16[64,2048]{1,0:T(8,128)(2,1)S(1)}, u32[]{:S(2)}, u32[]{:S(2)}) collective-permute-start(bf16[64,2048]{1,0:T(8,128)(2,1)} %bitcast.14), channel_id=1, source_target_pairs={{0,24},{1,25},{2,26},{3,27},{4,28},{5,29},{6,30},{7,31},{8,16},{9,... | collective-permute-start | bytes 786440 | tf_op jit(solution)/shard_map/ppermute | solution.py:33
  1.3 1.4 %collective-permute-start.3 = (bf16[64,2048]{1,0:T(8,128)(2,1)}, bf16[64,2048]{1,0:T(8,128)(2,1)S(1)}, u32[]{:S(2)}, u32[]{:S(2)}) collective-permute-start(bf16[64,2048]{1,0:T(8,128)(2,1)} %bitcast.15), channel_id=1, source_target_pairs={{0,18},{1,19},{2,16},{3,17},{4,22},{5,23},{6,20},{7,21},{8,26},{9,... | collective-permute-start | bytes 786440 | tf_op jit(solution)/shard_map/ppermute | solution.py:33
  2.7 1.5 %collective-permute-start.7 = (bf16[64,2048]{1,0:T(8,128)(2,1)}, bf16[64,2048]{1,0:T(8,128)(2,1)S(1)}, u32[]{:S(2)}, u32[]{:S(2)}) collective-permute-start(bf16[64,2048]{1,0:T(8,128)(2,1)} %bitcast.16), channel_id=1, source_target_pairs={{0,16},{1,17},{2,18},{3,19},{4,20},{5,21},{6,22},{7,23},{8,24},{9,... | collective-permute-start | bytes 786440 | tf_op jit(solution)/shard_map/ppermute | solution.py:33
  4.2 1.6 %collective-permute-done.1.other = bf16[768,2048]{1,0:T(8,128)(2,1)S(1)} collective-permute-done((bf16[768,2048]{1,0:T(8,128)(2,1)}, bf16[768,2048]{1,0:T(8,128)(2,1)S(1)}, u32[]{:S(2)}, u32[]{:S(2)}) %collective-permute-start.1) | collective-permute-done | bytes 3145760 | tf_op jit(solution)/shard_map/ppermute | solution.py:23
  5.9 0.0 copy-start
  5.9 0.7 %copy-done = s32[1,64,8]{1,2,0:T(8,128)S(1)} copy-done((s32[1,64,8]{1,2,0:T(8,128)S(1)}, s32[1,64,8]{1,2,0:T(8,128)}, u32[]{:S(2)}) %copy-start) | copy-done | bytes 2072
  6.6 0.0 copy-start.2
  6.6 0.7 copy-done.2
  7.2 0.1 shard_map.46.refs_1_
  7.4 1.0 %collective-permute-start.2 = (bf16[64,128]{1,0:T(8,128)(2,1)S(1)}, bf16[64,128]{1,0:T(8,128)(2,1)S(1)}, u32[]{:S(2)}, u32[]{:S(2)}) collective-permute-start(bf16[64,128]{1,0:T(8,128)(2,1)S(1)} %shard_map.46.refs_1_), channel_id=1, source_target_pairs={{0,8},{1,9},{2,10},{3,11},{4,12},{5,13},{6,14},{7,15},{8,0},{9,1},... | collective-permute-start | bytes 49160 | tf_op jit(solution)/shard_map/ppermute | solution.py:23
  8.4 0.9 %collective-permute-start.4 = (bf16[64,128]{1,0:T(8,128)(2,1)S(1)}, bf16[64,128]{1,0:T(8,128)(2,1)S(1)}, u32[]{:S(2)}, u32[]{:S(2)}) collective-permute-start(bf16[64,128]{1,0:T(8,128)(2,1)S(1)} %shard_map.46.refs_1_), channel_id=1, source_target_pairs={{0,2},{1,3},{2,0},{3,1},{4,6},{5,7},{6,4},{7,5},{8,10},{9,11},{10,... | collective-permute-start | bytes 49160 | tf_op jit(solution)/shard_map/ppermute | solution.py:23
  9.2 0.0 copy-start.3
  9.2 1.9 %copy-done.3 = bf16[1,1,768,2048]{3,2,1,0:T(8,128)(2,1)S(1)} copy-done((bf16[1,1,768,2048]{3,2,1,0:T(8,128)(2,1)S(1)}, bf16[1,1,768,2048]{3,2,1,0:T(8,128)(2,1)}, u32[]{:S(2)}) %copy-start.3) | copy-done | bytes 3145752
  11.1 1.7 %shard_map.47.weights = bf16[2048,1536]{1,0:T(8,128)(2,1)S(1)} custom-call(bf16[768,2048]{1,0:T(8,128)(2,1)S(1)} %bitcast.13, bf16[768,2048]{1,0:T(8,128)(2,1)S(1)} %collective-permute-done.1.other), custom_call_target="tpu_custom_call" | custom-call | flops 12884901888 | tf_op jit(solution)/shard_map/pallas_call | solution.py:82
  12.8 3.9 %collective-permute-done.refs_0_ = bf16[64,2048]{1,0:T(8,128)(2,1)S(1)} collective-permute-done((bf16[64,2048]{1,0:T(8,128)(2,1)}, bf16[64,2048]{1,0:T(8,128)(2,1)S(1)}, u32[]{:S(2)}, u32[]{:S(2)}) %collective-permute-start) | collective-permute-done | bytes 262176 | tf_op jit(solution)/shard_map/ppermute | solution.py:33
  16.6 0.0 collective-permute-done.3.refs_1_
  16.6 0.3 collective-permute-done.2.refs_2_
  17.0 0.0 collective-permute-done.4.refs_3_
  17.0 0.1 collective-permute-start.10
  17.1 1.6 %collective-permute-start.5 = (bf16[64,2176]{1,0:T(8,128)(2,1)S(1)}, bf16[64,2176]{1,0:T(8,128)(2,1)S(1)}, u32[]{:S(2)}, u32[]{:S(2)}) collective-permute-start(bf16[64,2176]{1,0:T(8,128)(2,1)S(1)} %get-tuple-element.36.refs_0_), channel_id=1, source_target_pairs={{0,2},{1,3},{2,0},{3,1},{4,6},{5,7},{6,4},{7,5},{8,10},{9,11},{10,... | collective-permute-start | bytes 835592 | tf_op jit(solution)/shard_map/ppermute | solution.py:23
  18.7 1.0 %shard_map.49 = (bf16[2,64,768]{2,1,0:T(8,128)(2,1)S(1)}, bf16[2,64,768]{2,1,0:T(8,128)(2,1)S(1)}) custom-call(bf16[2048,1536]{1,0:T(8,128)(2,1)S(1)} %shard_map.47.weights, bf16[64,2176]{1,0:T(8,128)(2,1)S(1)} %get-tuple-element.36.refs_0_, bf16[64,2176]{1,0:T(8,128)(2,1)S(1)} %get-tuple-element.38.refs_1_), custom_call_target="tpu_custom_call" | custom-call | flops 8053063680 | bytes 7208960 | tf_op jit(solution)/shard_map/pallas_call | solution.py:114
  19.7 1.6 %collective-permute-start.6 = (bf16[2,64,768]{2,1,0:T(8,128)(2,1)S(1)}, bf16[2,64,768]{2,1,0:T(8,128)(2,1)S(1)}, u32[]{:S(2)}, u32[]{:S(2)}) collective-permute-start(bf16[2,64,768]{2,1,0:T(8,128)(2,1)S(1)} %get-tuple-element.39), channel_id=1, source_target_pairs={{0,8},{1,9},{2,10},{3,11},{4,12},{5,13},{6,14},{7,15},{8,0},{9,1},... | collective-permute-start | bytes 589832 | tf_op jit(solution)/shard_map/ppermute | solution.py:23
  21.3 0.8 %collective-permute-done.7.refs_0_ = bf16[64,2048]{1,0:T(8,128)(2,1)S(1)} collective-permute-done((bf16[64,2048]{1,0:T(8,128)(2,1)}, bf16[64,2048]{1,0:T(8,128)(2,1)S(1)}, u32[]{:S(2)}, u32[]{:S(2)}) %collective-permute-start.7) | collective-permute-done | bytes 262176 | tf_op jit(solution)/shard_map/ppermute | solution.py:33
  22.1 0.4 collective-permute-start.8
  22.5 0.9 %collective-permute-start.9 = (bf16[2,64,768]{2,1,0:T(8,128)(2,1)S(1)}, bf16[2,64,768]{2,1,0:T(8,128)(2,1)S(1)}, u32[]{:S(2)}, u32[]{:S(2)}) collective-permute-start(bf16[2,64,768]{2,1,0:T(8,128)(2,1)S(1)} %get-tuple-element.43), channel_id=1, source_target_pairs={{0,2},{1,3},{2,0},{3,1},{4,6},{5,7},{6,4},{7,5},{8,10},{9,11},{10,... | collective-permute-start | bytes 589832 | tf_op jit(solution)/shard_map/ppermute | solution.py:23
  23.4 5.2 %collective-permute-done.10.refs_0_ = bf16[64,2176]{1,0:T(8,128)(2,1)S(1)} collective-permute-done((bf16[64,2176]{1,0:T(8,128)(2,1)S(1)}, bf16[64,2176]{1,0:T(8,128)(2,1)S(1)}, u32[]{:S(2)}, u32[]{:S(2)}) %collective-permute-start.10) | collective-permute-done | bytes 278560 | tf_op jit(solution)/shard_map/ppermute | solution.py:23
  28.6 3.7 %collective-permute-start.12 = (bf16[64,2176]{1,0:T(8,128)(2,1)S(1)}, bf16[64,2176]{1,0:T(8,128)(2,1)S(1)}, u32[]{:S(2)}, u32[]{:S(2)}) collective-permute-start(bf16[64,2176]{1,0:T(8,128)(2,1)S(1)} %collective-permute-done.10.refs_0_), channel_id=1, source_target_pairs={{0,2},{1,3},{2,0},{3,1},{4,6},{5,7},{6,4},{7,5},{8,10},{9,11},{10,... | collective-permute-start | bytes 835592 | tf_op jit(solution)/shard_map/ppermute | solution.py:23
  32.3 1.2 %shard_map.51 = bf16[2,64,768]{2,1,0:T(8,128)(2,1)S(1)} custom-call(bf16[2048,1536]{1,0:T(8,128)(2,1)S(1)} %shard_map.47.weights, bf16[64,2176]{1,0:T(8,128)(2,1)S(1)} %collective-permute-done.10.refs_0_), custom_call_target="tpu_custom_call" | custom-call | flops 4026531840 | bytes 6750208 | tf_op jit(solution)/shard_map/pallas_call | solution.py:114
  33.5 0.0 collective-permute-done.9.refs_0_
  33.5 1.2 %collective-permute-start.16 = (bf16[2,64,768]{2,1,0:T(8,128)(2,1)S(1)}, bf16[2,64,768]{2,1,0:T(8,128)(2,1)S(1)}, u32[]{:S(2)}, u32[]{:S(2)}) collective-permute-start(bf16[2,64,768]{2,1,0:T(8,128)(2,1)S(1)} %shard_map.51), channel_id=1, source_target_pairs={{0,12},{1,13},{2,14},{3,15},{4,8},{5,9},{6,10},{7,11},{8,4},{9,5},... | collective-permute-start | bytes 589832 | tf_op jit(solution)/shard_map/ppermute | solution.py:23
  34.8 0.0 collective-permute-done.6.refs_1_
  34.8 3.3 %collective-permute-done.8.refs_0_ = bf16[64,2176]{1,0:T(8,128)(2,1)S(1)} collective-permute-done((bf16[64,2176]{1,0:T(8,128)(2,1)S(1)}, bf16[64,2176]{1,0:T(8,128)(2,1)S(1)}, u32[]{:S(2)}, u32[]{:S(2)}) %collective-permute-start.8) | collective-permute-done | bytes 278560 | tf_op jit(solution)/shard_map/ppermute | solution.py:23
  38.0 0.0 collective-permute-done.5.refs_0_
  38.0 3.6 %collective-permute-start.11 = (bf16[64,2176]{1,0:T(8,128)(2,1)S(1)}, bf16[64,2176]{1,0:T(8,128)(2,1)S(1)}, u32[]{:S(2)}, u32[]{:S(2)}) collective-permute-start(bf16[64,2176]{1,0:T(8,128)(2,1)S(1)} %collective-permute-done.8.refs_0_), channel_id=1, source_target_pairs={{0,2},{1,3},{2,0},{3,1},{4,6},{5,7},{6,4},{7,5},{8,10},{9,11},{10,... | collective-permute-start | bytes 835592 | tf_op jit(solution)/shard_map/ppermute | solution.py:23
  41.6 1.2 %shard_map.52 = bf16[2,64,768]{2,1,0:T(8,128)(2,1)S(1)} custom-call(bf16[2048,1536]{1,0:T(8,128)(2,1)S(1)} %shard_map.47.weights, bf16[64,2176]{1,0:T(8,128)(2,1)S(1)} %collective-permute-done.5.refs_0_), custom_call_target="tpu_custom_call" | custom-call | flops 4026531840 | bytes 6750208 | tf_op jit(solution)/shard_map/pallas_call | solution.py:114
  42.8 0.1 collective-permute-start.15
  42.9 0.0 collective-permute-done.12.refs_0_
  42.9 1.2 %shard_map.53 = bf16[2,64,768]{2,1,0:T(8,128)(2,1)S(1)} custom-call(bf16[2048,1536]{1,0:T(8,128)(2,1)S(1)} %shard_map.47.weights, bf16[64,2176]{1,0:T(8,128)(2,1)S(1)} %collective-permute-done.12.refs_0_), custom_call_target="tpu_custom_call" | custom-call | flops 4026531840 | bytes 6750208 | tf_op jit(solution)/shard_map/pallas_call | solution.py:114
  44.1 0.0 copy-start.1
  44.1 2.9 %collective-permute-start.17 = (bf16[2,64,768]{2,1,0:T(8,128)(2,1)S(1)}, bf16[2,64,768]{2,1,0:T(8,128)(2,1)S(1)}, u32[]{:S(2)}, u32[]{:S(2)}) collective-permute-start(bf16[2,64,768]{2,1,0:T(8,128)(2,1)S(1)} %shard_map.53), channel_id=1, source_target_pairs={{0,14},{1,15},{2,12},{3,13},{4,10},{5,11},{6,8},{7,9},{8,6},{9,7},... | collective-permute-start | bytes 589832 | tf_op jit(solution)/shard_map/ppermute | solution.py:23
  47.0 9.0 %collective-permute-done.11.refs_1_ = bf16[64,2176]{1,0:T(8,128)(2,1)S(1)} collective-permute-done((bf16[64,2176]{1,0:T(8,128)(2,1)S(1)}, bf16[64,2176]{1,0:T(8,128)(2,1)S(1)}, u32[]{:S(2)}, u32[]{:S(2)}) %collective-permute-start.11) | collective-permute-done | bytes 278560 | tf_op jit(solution)/shard_map/ppermute | solution.py:23
  56.0 1.4 %shard_map.54 = (bf16[2,64,768]{2,1,0:T(8,128)(2,1)S(1)}, bf16[2,64,768]{2,1,0:T(8,128)(2,1)S(1)}, bf16[2,64,768]{2,1,0:T(8,128)(2,1)S(1)}) custom-call(bf16[2048,1536]{1,0:T(8,128)(2,1)S(1)} %shard_map.47.weights, bf16[64,2176]{1,0:T(8,128)(2,1)S(1)} %collective-permute-done.8.refs_0_, bf16[64,2176]{1,0:T(8,128)(2,1)S(1)} %collective-permute-done.11.refs_1_, ...), custom_call_target="tpu_custom_call" | custom-call | flops 12079595520 | bytes 7667712 | tf_op jit(solution)/shard_map/pallas_call | solution.py:114
  57.4 0.1 collective-permute-start.13
  57.4 3.9 %collective-permute-start.14 = (bf16[2,64,768]{2,1,0:T(8,128)(2,1)S(1)}, bf16[2,64,768]{2,1,0:T(8,128)(2,1)S(1)}, u32[]{:S(2)}, u32[]{:S(2)}) collective-permute-start(bf16[2,64,768]{2,1,0:T(8,128)(2,1)S(1)} %get-tuple-element.52), channel_id=1, source_target_pairs={{0,6},{1,7},{2,4},{3,5},{4,2},{5,3},{6,0},{7,1},{8,14},{9,15},{10,... | collective-permute-start | bytes 589832 | tf_op jit(solution)/shard_map/ppermute | solution.py:23
  61.4 0.0 collective-permute-done.15.refs_2_
  61.4 0.0 collective-permute-done.16.refs_3_
  61.4 0.0 collective-permute-done.17.refs_4_
  61.4 0.0 copy-done.1
  61.4 0.4 shard_map.55.refs_3_
  61.8 1.3 %collective-permute-done.13.refs_1_ = bf16[2,64,768]{2,1,0:T(8,128)(2,1)S(1)} collective-permute-done((bf16[2,64,768]{2,1,0:T(8,128)(2,1)S(1)}, bf16[2,64,768]{2,1,0:T(8,128)(2,1)S(1)}, u32[]{:S(2)}, u32[]{:S(2)}) %collective-permute-start.13) | collective-permute-done | bytes 196640 | tf_op jit(solution)/shard_map/ppermute | solution.py:23
  63.1 4.0 %collective-permute-done.14.refs_2_ = bf16[2,64,768]{2,1,0:T(8,128)(2,1)S(1)} collective-permute-done((bf16[2,64,768]{2,1,0:T(8,128)(2,1)S(1)}, bf16[2,64,768]{2,1,0:T(8,128)(2,1)S(1)}, u32[]{:S(2)}, u32[]{:S(2)}) %collective-permute-start.14) | collective-permute-done | bytes 196640 | tf_op jit(solution)/shard_map/ppermute | solution.py:23
  67.1 1.3 %shard_map.56 = bf16[512,768]{1,0:T(8,128)(2,1)} custom-call(s32[8,64]{1,0:T(8,128)S(1)} %bitcast.10, bf16[2,64,768]{2,1,0:T(8,128)(2,1)S(1)} %collective-permute-done.9.refs_0_, bf16[2,64,768]{2,1,0:T(8,128)(2,1)S(1)} %collective-permute-done.13.refs_1_, bf16[2,64,768]{2,1,0:T(8,128)(2,1)S(1)} %collective-permute-done.14.refs_2_, ...), custom_call_target="tpu_custom_call" | custom-call | tf_op jit(solution)/shard_map/pallas_call | solution.py:155
  (2 shorter events, 0.1 us)
Async XLA Ops:
  0.0 5.9 %collective-permute-start.1 = (bf16[768,2048]{1,0:T(8,128)(2,1)}, bf16[768,2048]{1,0:T(8,128)(2,1)S(1)}, u32[]{:S(2)}, u32[]{:S(2)}) collective-permute-start(bf16[768,2048]{1,0:T(8,128)(2,1)} %bitcast.12), channel_id=1, source_target_pairs={{0,1},{1,0},{2,3},{3,2},{4,5},{5,4},{6,7},{7,6},{8,9},{9,8},{10,11... | collective-permute-start | bytes 9437192 | tf_op jit(solution)/shard_map/ppermute | solution.py:23
  0.0 16.6 %collective-permute-start = (bf16[64,2048]{1,0:T(8,128)(2,1)}, bf16[64,2048]{1,0:T(8,128)(2,1)S(1)}, u32[]{:S(2)}, u32[]{:S(2)}) collective-permute-start(bf16[64,2048]{1,0:T(8,128)(2,1)} %bitcast.14), channel_id=1, source_target_pairs={{0,24},{1,25},{2,26},{3,27},{4,28},{5,29},{6,30},{7,31},{8,16},{9,... | collective-permute-start | bytes 786440 | tf_op jit(solution)/shard_map/ppermute | solution.py:33
  1.3 15.4 %collective-permute-start.3 = (bf16[64,2048]{1,0:T(8,128)(2,1)}, bf16[64,2048]{1,0:T(8,128)(2,1)S(1)}, u32[]{:S(2)}, u32[]{:S(2)}) collective-permute-start(bf16[64,2048]{1,0:T(8,128)(2,1)} %bitcast.15), channel_id=1, source_target_pairs={{0,18},{1,19},{2,16},{3,17},{4,22},{5,23},{6,20},{7,21},{8,26},{9,... | collective-permute-start | bytes 786440 | tf_op jit(solution)/shard_map/ppermute | solution.py:33
  2.7 19.3 %collective-permute-start.7 = (bf16[64,2048]{1,0:T(8,128)(2,1)}, bf16[64,2048]{1,0:T(8,128)(2,1)S(1)}, u32[]{:S(2)}, u32[]{:S(2)}) collective-permute-start(bf16[64,2048]{1,0:T(8,128)(2,1)} %bitcast.16), channel_id=1, source_target_pairs={{0,16},{1,17},{2,18},{3,19},{4,20},{5,21},{6,22},{7,23},{8,24},{9,... | collective-permute-start | bytes 786440 | tf_op jit(solution)/shard_map/ppermute | solution.py:33
  5.9 0.7 %copy-start = (s32[1,64,8]{1,2,0:T(8,128)S(1)}, s32[1,64,8]{1,2,0:T(8,128)}, u32[]{:S(2)}) copy-start(s32[1,64,8]{1,2,0:T(8,128)} %param.5) | copy-start | bytes 6148
  6.6 0.7 copy-start.2
  7.4 9.6 %collective-permute-start.2 = (bf16[64,128]{1,0:T(8,128)(2,1)S(1)}, bf16[64,128]{1,0:T(8,128)(2,1)S(1)}, u32[]{:S(2)}, u32[]{:S(2)}) collective-permute-start(bf16[64,128]{1,0:T(8,128)(2,1)S(1)} %shard_map.46.refs_1_), channel_id=1, source_target_pairs={{0,8},{1,9},{2,10},{3,11},{4,12},{5,13},{6,14},{7,15},{8,0},{9,1},... | collective-permute-start | bytes 49160 | tf_op jit(solution)/shard_map/ppermute | solution.py:23
  8.4 8.6 %collective-permute-start.4 = (bf16[64,128]{1,0:T(8,128)(2,1)S(1)}, bf16[64,128]{1,0:T(8,128)(2,1)S(1)}, u32[]{:S(2)}, u32[]{:S(2)}) collective-permute-start(bf16[64,128]{1,0:T(8,128)(2,1)S(1)} %shard_map.46.refs_1_), channel_id=1, source_target_pairs={{0,2},{1,3},{2,0},{3,1},{4,6},{5,7},{6,4},{7,5},{8,10},{9,11},{10,... | collective-permute-start | bytes 49160 | tf_op jit(solution)/shard_map/ppermute | solution.py:23
  9.2 1.9 %copy-start.3 = (bf16[1,1,768,2048]{3,2,1,0:T(8,128)(2,1)S(1)}, bf16[1,1,768,2048]{3,2,1,0:T(8,128)(2,1)}, u32[]{:S(2)}) copy-start(bf16[1,1,768,2048]{3,2,1,0:T(8,128)(2,1)} %param.7) | copy-start | bytes 9437188
  17.0 11.5 %collective-permute-start.10 = (bf16[64,2176]{1,0:T(8,128)(2,1)S(1)}, bf16[64,2176]{1,0:T(8,128)(2,1)S(1)}, u32[]{:S(2)}, u32[]{:S(2)}) collective-permute-start(bf16[64,2176]{1,0:T(8,128)(2,1)S(1)} %get-tuple-element.36.refs_0_), channel_id=1, source_target_pairs={{0,4},{1,5},{2,6},{3,7},{4,0},{5,1},{6,2},{7,3},{8,12},{9,13},{10,... | collective-permute-start | bytes 835592 | tf_op jit(solution)/shard_map/ppermute | solution.py:23
  17.1 20.9 %collective-permute-start.5 = (bf16[64,2176]{1,0:T(8,128)(2,1)S(1)}, bf16[64,2176]{1,0:T(8,128)(2,1)S(1)}, u32[]{:S(2)}, u32[]{:S(2)}) collective-permute-start(bf16[64,2176]{1,0:T(8,128)(2,1)S(1)} %get-tuple-element.36.refs_0_), channel_id=1, source_target_pairs={{0,2},{1,3},{2,0},{3,1},{4,6},{5,7},{6,4},{7,5},{8,10},{9,11},{10,... | collective-permute-start | bytes 835592 | tf_op jit(solution)/shard_map/ppermute | solution.py:23
  19.7 15.1 %collective-permute-start.6 = (bf16[2,64,768]{2,1,0:T(8,128)(2,1)S(1)}, bf16[2,64,768]{2,1,0:T(8,128)(2,1)S(1)}, u32[]{:S(2)}, u32[]{:S(2)}) collective-permute-start(bf16[2,64,768]{2,1,0:T(8,128)(2,1)S(1)} %get-tuple-element.39), channel_id=1, source_target_pairs={{0,8},{1,9},{2,10},{3,11},{4,12},{5,13},{6,14},{7,15},{8,0},{9,1},... | collective-permute-start | bytes 589832 | tf_op jit(solution)/shard_map/ppermute | solution.py:23
  22.1 15.9 %collective-permute-start.8 = (bf16[64,2176]{1,0:T(8,128)(2,1)S(1)}, bf16[64,2176]{1,0:T(8,128)(2,1)S(1)}, u32[]{:S(2)}, u32[]{:S(2)}) collective-permute-start(bf16[64,2176]{1,0:T(8,128)(2,1)S(1)} %shard_map.50.refs_2_), channel_id=1, source_target_pairs={{0,4},{1,5},{2,6},{3,7},{4,0},{5,1},{6,2},{7,3},{8,12},{9,13},{10,... | collective-permute-start | bytes 835592 | tf_op jit(solution)/shard_map/ppermute | solution.py:23
  22.5 11.0 %collective-permute-start.9 = (bf16[2,64,768]{2,1,0:T(8,128)(2,1)S(1)}, bf16[2,64,768]{2,1,0:T(8,128)(2,1)S(1)}, u32[]{:S(2)}, u32[]{:S(2)}) collective-permute-start(bf16[2,64,768]{2,1,0:T(8,128)(2,1)S(1)} %get-tuple-element.43), channel_id=1, source_target_pairs={{0,2},{1,3},{2,0},{3,1},{4,6},{5,7},{6,4},{7,5},{8,10},{9,11},{10,... | collective-permute-start | bytes 589832 | tf_op jit(solution)/shard_map/ppermute | solution.py:23
  28.6 14.3 %collective-permute-start.12 = (bf16[64,2176]{1,0:T(8,128)(2,1)S(1)}, bf16[64,2176]{1,0:T(8,128)(2,1)S(1)}, u32[]{:S(2)}, u32[]{:S(2)}) collective-permute-start(bf16[64,2176]{1,0:T(8,128)(2,1)S(1)} %collective-permute-done.10.refs_0_), channel_id=1, source_target_pairs={{0,2},{1,3},{2,0},{3,1},{4,6},{5,7},{6,4},{7,5},{8,10},{9,11},{10,... | collective-permute-start | bytes 835592 | tf_op jit(solution)/shard_map/ppermute | solution.py:23
  33.5 27.9 %collective-permute-start.16 = (bf16[2,64,768]{2,1,0:T(8,128)(2,1)S(1)}, bf16[2,64,768]{2,1,0:T(8,128)(2,1)S(1)}, u32[]{:S(2)}, u32[]{:S(2)}) collective-permute-start(bf16[2,64,768]{2,1,0:T(8,128)(2,1)S(1)} %shard_map.51), channel_id=1, source_target_pairs={{0,12},{1,13},{2,14},{3,15},{4,8},{5,9},{6,10},{7,11},{8,4},{9,5},... | collective-permute-start | bytes 589832 | tf_op jit(solution)/shard_map/ppermute | solution.py:23
  38.0 17.9 %collective-permute-start.11 = (bf16[64,2176]{1,0:T(8,128)(2,1)S(1)}, bf16[64,2176]{1,0:T(8,128)(2,1)S(1)}, u32[]{:S(2)}, u32[]{:S(2)}) collective-permute-start(bf16[64,2176]{1,0:T(8,128)(2,1)S(1)} %collective-permute-done.8.refs_0_), channel_id=1, source_target_pairs={{0,2},{1,3},{2,0},{3,1},{4,6},{5,7},{6,4},{7,5},{8,10},{9,11},{10,... | collective-permute-start | bytes 835592 | tf_op jit(solution)/shard_map/ppermute | solution.py:23
  42.8 18.5 %collective-permute-start.15 = (bf16[2,64,768]{2,1,0:T(8,128)(2,1)S(1)}, bf16[2,64,768]{2,1,0:T(8,128)(2,1)S(1)}, u32[]{:S(2)}, u32[]{:S(2)}) collective-permute-start(bf16[2,64,768]{2,1,0:T(8,128)(2,1)S(1)} %shard_map.52), channel_id=1, source_target_pairs={{0,10},{1,11},{2,8},{3,9},{4,14},{5,15},{6,12},{7,13},{8,2},{9,3},... | collective-permute-start | bytes 589832 | tf_op jit(solution)/shard_map/ppermute | solution.py:23
  44.1 17.3 %copy-start.1 = (s32[1,64,8]{1,2,0:T(8,128)S(1)}, s32[1,64,8]{1,2,0:T(8,128)}, u32[]{:S(2)}) copy-start(s32[1,64,8]{1,2,0:T(8,128)} %param.5) | copy-start | bytes 6148
  44.1 17.3 %collective-permute-start.17 = (bf16[2,64,768]{2,1,0:T(8,128)(2,1)S(1)}, bf16[2,64,768]{2,1,0:T(8,128)(2,1)S(1)}, u32[]{:S(2)}, u32[]{:S(2)}) collective-permute-start(bf16[2,64,768]{2,1,0:T(8,128)(2,1)S(1)} %shard_map.53), channel_id=1, source_target_pairs={{0,14},{1,15},{2,12},{3,13},{4,10},{5,11},{6,8},{7,9},{8,6},{9,7},... | collective-permute-start | bytes 589832 | tf_op jit(solution)/shard_map/ppermute | solution.py:23
  57.4 5.7 %collective-permute-start.13 = (bf16[2,64,768]{2,1,0:T(8,128)(2,1)S(1)}, bf16[2,64,768]{2,1,0:T(8,128)(2,1)S(1)}, u32[]{:S(2)}, u32[]{:S(2)}) collective-permute-start(bf16[2,64,768]{2,1,0:T(8,128)(2,1)S(1)} %get-tuple-element.51), channel_id=1, source_target_pairs={{0,4},{1,5},{2,6},{3,7},{4,0},{5,1},{6,2},{7,3},{8,12},{9,13},{10,... | collective-permute-start | bytes 589832 | tf_op jit(solution)/shard_map/ppermute | solution.py:23
  57.4 9.7 %collective-permute-start.14 = (bf16[2,64,768]{2,1,0:T(8,128)(2,1)S(1)}, bf16[2,64,768]{2,1,0:T(8,128)(2,1)S(1)}, u32[]{:S(2)}, u32[]{:S(2)}) collective-permute-start(bf16[2,64,768]{2,1,0:T(8,128)(2,1)S(1)} %get-tuple-element.52), channel_id=1, source_target_pairs={{0,6},{1,7},{2,4},{3,5},{4,2},{5,3},{6,0},{7,1},{8,14},{9,15},{10,... | collective-permute-start | bytes 589832 | tf_op jit(solution)/shard_map/ppermute | solution.py:23

commit v30 on v29

--- a/solution.py
+++ b/solution.py
@@ -169,12 +169,13 @@
 
     far = send_across(upstream, owners, Z_FAR)
     side = send_across(upstream, owners, X)
+    near = send_across(upstream, owners, Z_NEAR)
     other_mat = send(weight_mat, owners, 0, 1)
     route_gates, other_mat = tie((route_gates, other_mat))
     columns = gate_columns(route_ids.T, route_gates.T)
     far_columns = send(columns, owners, Z_FAR)
     side_columns = send(columns, owners, X)
-    rows = send_across(upstream, owners, 0)
+    near_columns = send(columns, owners, Z_NEAR)
     weights = turned(weight_mat, other_mat)
     far, far_columns, side, side_columns, weights = tie(
         (far, far_columns, side, side_columns, weights)
@@ -184,22 +185,25 @@
     far_side = send(far, owners, X)
     out_far, out_side = work(far, side)
     back_far = send(out_far, owners, Z_FAR)
-    rows, columns, _ = tie((rows, columns, out_far))
-    (rows,) = widened([rows], [columns])
-    near = send(rows, owners, Z_NEAR)
-    back_side = send(tie((out_side, rows))[0], owners, X)
-    cross, rows = tie((cross, rows))
+    near, near_columns, _ = tie((near, near_columns, out_far))
+    (near,) = widened([near], [near_columns])
+    near_side = send(near, owners, X)
+    back_side = send(tie((out_side, near))[0], owners, X)
+    cross, near = tie((cross, near))
     cross_side = send(cross, owners, X)
     (out_cross,) = work(cross)
     back_cross = send(out_cross, owners, Z_NEAR ^ Z_FAR)
-    far_side, back_far, near, back_side, _ = tie((far_side, back_far, near, back_side, out_cross))
-    near_side = send(near, owners, X)
+    far_side, back_far, back_side, upstream, _ = tie(
+        (far_side, back_far, back_side, upstream, out_cross)
+    )
+    rows = send_across(upstream, owners, 0)
     (out_far_side,) = work(far_side)
     back_far_side = send(out_far_side, owners, X ^ Z_FAR)
     cross_side, _ = tie((cross_side, out_far_side))
     (out_cross_side,) = work(cross_side)
     back_cross_side = send(out_cross_side, owners, X ^ Z_NEAR ^ Z_FAR)
-    near_side, _ = tie((near_side, out_cross_side))
+    rows, near_side, _ = tie((rows, near_side, out_cross_side))
+    (rows,) = widened([rows], [columns])
     out_near, out_near_side, out_own = work(near, near_side, rows)
     back_near_side = send(out_near_side, owners, X ^ Z_NEAR)
     back_near = send(out_near, owners, Z_NEAR)

time: 68.6 us -> 73.8 us (1.076)
  the two profiles are of different devices: /device:TPU:24 before, /device:TPU:0 now
where the time goes in v30:
time: 73.8 us; the launch traced here: 73.6 us
  starting transfers between devices  30.5 us (41%)
  waiting for transfers between devices  30.2 us (41%)
  Pallas kernels  9.54 us (13%)
  local copies, waits for them, and re-layouts  3.27 us (4%)
    ppermute x15, waiting for transfers between devices, send(): return lax.ppermute(block, 'expert', route)  26.4 us
    ppermute x15, starting transfers between devices, send(): return lax.ppermute(block, 'expert', route)  21.4 us
    ppermute x4, starting transfers between devices, send_across(): return lax.ppermute(block, ('pipe', 'expert'), route)  9.08 us
    pallas_call x5, Pallas kernels, products(): pl.pallas_call(functools.partial(products_kernel, len(pieces)), out_shape...  5.94 us
    ppermute x4, waiting for transfers between devices, send_across(): return lax.ppermute(block, ('pipe', 'expert'), route)  3.72 us
    unnamed x10, local copies, waits for them, and re-layouts  3.27 us
    pallas_call x2, Pallas kernels, pick_routes(): pl.pallas_call(functools.partial(pick_kernel, flips), out_shape=jax.Shape...  1.74 us
    pallas_call x1, Pallas kernels, turned(): pl.pallas_call(turn_kernel, out_shape=jax.ShapeDtypeStruct((depth, CORES...  1.67 us
  transfers between devices with their start and end apart: 19, of which 6 were waited for; matrix products, arithmetic and copies ran while one was open for 0% of the time, Pallas kernels for 11%

profile of v30, /device:TPU:0, one launch (start us, length us, event | category | flops | bytes accessed | tf_op | source)
XLA Modules:
  0.0 73.6 jit_solution(955808099168732526)
XLA Ops:
  0.0 0.5 collective-permute-start.1
  0.5 4.5 %collective-permute-start = (bf16[64,2048]{1,0:T(8,128)(2,1)}, bf16[64,2048]{1,0:T(8,128)(2,1)S(1)}, u32[]{:S(2)}, u32[]{:S(2)}) collective-permute-start(bf16[64,2048]{1,0:T(8,128)(2,1)} %bitcast.14), channel_id=1, source_target_pairs={{0,24},{1,25},{2,26},{3,27},{4,28},{5,29},{6,30},{7,31},{8,16},{9,... | collective-permute-start | bytes 786440 | tf_op jit(solution)/shard_map/ppermute | solution.py:33
  5.0 1.4 %collective-permute-start.3 = (bf16[64,2048]{1,0:T(8,128)(2,1)}, bf16[64,2048]{1,0:T(8,128)(2,1)S(1)}, u32[]{:S(2)}, u32[]{:S(2)}) collective-permute-start(bf16[64,2048]{1,0:T(8,128)(2,1)} %bitcast.15), channel_id=1, source_target_pairs={{0,18},{1,19},{2,16},{3,17},{4,22},{5,23},{6,20},{7,21},{8,26},{9,... | collective-permute-start | bytes 786440 | tf_op jit(solution)/shard_map/ppermute | solution.py:33
  6.4 2.5 %collective-permute-start.7 = (bf16[64,2048]{1,0:T(8,128)(2,1)}, bf16[64,2048]{1,0:T(8,128)(2,1)S(1)}, u32[]{:S(2)}, u32[]{:S(2)}) collective-permute-start(bf16[64,2048]{1,0:T(8,128)(2,1)} %bitcast.16), channel_id=1, source_target_pairs={{0,20},{1,21},{2,22},{3,23},{4,16},{5,17},{6,18},{7,19},{8,28},{9,... | collective-permute-start | bytes 786440 | tf_op jit(solution)/shard_map/ppermute | solution.py:33
  9.0 0.0 collective-permute-done.1.other
  9.0 0.0 copy-start
  9.0 0.7 copy-done
  9.7 0.0 copy-start.2
  9.7 0.7 copy-done.2
  10.3 0.1 shard_map.46.refs_1_
  10.4 1.0 %collective-permute-start.2 = (bf16[64,128]{1,0:T(8,128)(2,1)S(1)}, bf16[64,128]{1,0:T(8,128)(2,1)S(1)}, u32[]{:S(2)}, u32[]{:S(2)}) collective-permute-start(bf16[64,128]{1,0:T(8,128)(2,1)S(1)} %shard_map.46.refs_1_), channel_id=1, source_target_pairs={{0,8},{1,9},{2,10},{3,11},{4,12},{5,13},{6,14},{7,15},{8,0},{9,1},... | collective-permute-start | bytes 49160 | tf_op jit(solution)/shard_map/ppermute | solution.py:23
  11.4 1.5 %collective-permute-start.4 = (bf16[64,128]{1,0:T(8,128)(2,1)S(1)}, bf16[64,128]{1,0:T(8,128)(2,1)S(1)}, u32[]{:S(2)}, u32[]{:S(2)}) collective-permute-start(bf16[64,128]{1,0:T(8,128)(2,1)S(1)} %shard_map.46.refs_1_), channel_id=1, source_target_pairs={{0,2},{1,3},{2,0},{3,1},{4,6},{5,7},{6,4},{7,5},{8,10},{9,11},{10,... | collective-permute-start | bytes 49160 | tf_op jit(solution)/shard_map/ppermute | solution.py:23
  12.9 0.0 copy-start.3
  12.9 1.9 %copy-done.3 = bf16[1,1,768,2048]{3,2,1,0:T(8,128)(2,1)S(1)} copy-done((bf16[1,1,768,2048]{3,2,1,0:T(8,128)(2,1)S(1)}, bf16[1,1,768,2048]{3,2,1,0:T(8,128)(2,1)}, u32[]{:S(2)}) %copy-start.3) | copy-done | bytes 3145752
  14.8 1.7 %shard_map.47.weights = bf16[2048,1536]{1,0:T(8,128)(2,1)S(1)} custom-call(bf16[768,2048]{1,0:T(8,128)(2,1)S(1)} %bitcast.13, bf16[768,2048]{1,0:T(8,128)(2,1)S(1)} %collective-permute-done.1.other), custom_call_target="tpu_custom_call" | custom-call | flops 12884901888 | tf_op jit(solution)/shard_map/pallas_call | solution.py:82
  16.5 3.7 %collective-permute-done.refs_0_ = bf16[64,2048]{1,0:T(8,128)(2,1)S(1)} collective-permute-done((bf16[64,2048]{1,0:T(8,128)(2,1)}, bf16[64,2048]{1,0:T(8,128)(2,1)S(1)}, u32[]{:S(2)}, u32[]{:S(2)}) %collective-permute-start) | collective-permute-done | bytes 262176 | tf_op jit(solution)/shard_map/ppermute | solution.py:33
  20.2 0.0 collective-permute-start.8
  20.2 0.0 collective-permute-done.3.refs_1_
  20.2 2.9 %collective-permute-done.2.refs_2_ = bf16[64,128]{1,0:T(8,128)(2,1)S(1)} collective-permute-done((bf16[64,128]{1,0:T(8,128)(2,1)S(1)}, bf16[64,128]{1,0:T(8,128)(2,1)S(1)}, u32[]{:S(2)}, u32[]{:S(2)}) %collective-permute-start.2) | collective-permute-done | bytes 16416 | tf_op jit(solution)/shard_map/ppermute | solution.py:23
  23.1 0.0 collective-permute-done.4.refs_3_
  23.2 2.6 %collective-permute-start.10 = (bf16[64,2176]{1,0:T(8,128)(2,1)S(1)}, bf16[64,2176]{1,0:T(8,128)(2,1)S(1)}, u32[]{:S(2)}, u32[]{:S(2)}) collective-permute-start(bf16[64,2176]{1,0:T(8,128)(2,1)S(1)} %get-tuple-element.37.refs_0_), channel_id=1, source_target_pairs={{0,4},{1,5},{2,6},{3,7},{4,0},{5,1},{6,2},{7,3},{8,12},{9,13},{10,... | collective-permute-start | bytes 835592 | tf_op jit(solution)/shard_map/ppermute | solution.py:23
  25.7 1.5 %collective-permute-start.5 = (bf16[64,2176]{1,0:T(8,128)(2,1)S(1)}, bf16[64,2176]{1,0:T(8,128)(2,1)S(1)}, u32[]{:S(2)}, u32[]{:S(2)}) collective-permute-start(bf16[64,2176]{1,0:T(8,128)(2,1)S(1)} %get-tuple-element.37.refs_0_), channel_id=1, source_target_pairs={{0,2},{1,3},{2,0},{3,1},{4,6},{5,7},{6,4},{7,5},{8,10},{9,11},{10,... | collective-permute-start | bytes 835592 | tf_op jit(solution)/shard_map/ppermute | solution.py:23
  27.2 1.0 %shard_map.49 = (bf16[2,64,768]{2,1,0:T(8,128)(2,1)S(1)}, bf16[2,64,768]{2,1,0:T(8,128)(2,1)S(1)}) custom-call(bf16[2048,1536]{1,0:T(8,128)(2,1)S(1)} %shard_map.47.weights, bf16[64,2176]{1,0:T(8,128)(2,1)S(1)} %get-tuple-element.37.refs_0_, bf16[64,2176]{1,0:T(8,128)(2,1)S(1)} %get-tuple-element.39.refs_1_), custom_call_target="tpu_custom_call" | custom-call | flops 8053063680 | bytes 7208960 | tf_op jit(solution)/shard_map/pallas_call | solution.py:114
  28.2 1.0 %collective-permute-start.6 = (bf16[2,64,768]{2,1,0:T(8,128)(2,1)S(1)}, bf16[2,64,768]{2,1,0:T(8,128)(2,1)S(1)}, u32[]{:S(2)}, u32[]{:S(2)}) collective-permute-start(bf16[2,64,768]{2,1,0:T(8,128)(2,1)S(1)} %get-tuple-element.40), channel_id=1, source_target_pairs={{0,8},{1,9},{2,10},{3,11},{4,12},{5,13},{6,14},{7,15},{8,0},{9,1},... | collective-permute-start | bytes 589832 | tf_op jit(solution)/shard_map/ppermute | solution.py:23
  29.3 0.0 collective-permute-done.7.refs_0_
  29.3 0.0 collective-permute-done.8.refs_1_
  29.3 0.6 collective-permute-start.12
  29.9 0.0 copy-start.4
  29.9 1.5 %collective-permute-start.9 = (bf16[2,64,768]{2,1,0:T(8,128)(2,1)S(1)}, bf16[2,64,768]{2,1,0:T(8,128)(2,1)S(1)}, u32[]{:S(2)}, u32[]{:S(2)}) collective-permute-start(bf16[2,64,768]{2,1,0:T(8,128)(2,1)S(1)} %get-tuple-element.44), channel_id=1, source_target_pairs={{0,2},{1,3},{2,0},{3,1},{4,6},{5,7},{6,4},{7,5},{8,10},{9,11},{10,... | collective-permute-start | bytes 589832 | tf_op jit(solution)/shard_map/ppermute | solution.py:23
  31.4 3.9 %collective-permute-done.10.refs_0_ = bf16[64,2176]{1,0:T(8,128)(2,1)S(1)} collective-permute-done((bf16[64,2176]{1,0:T(8,128)(2,1)S(1)}, bf16[64,2176]{1,0:T(8,128)(2,1)S(1)}, u32[]{:S(2)}, u32[]{:S(2)}) %collective-permute-start.10) | collective-permute-done | bytes 278560 | tf_op jit(solution)/shard_map/ppermute | solution.py:23
  35.3 2.5 %collective-permute-start.13 = (bf16[64,2176]{1,0:T(8,128)(2,1)S(1)}, bf16[64,2176]{1,0:T(8,128)(2,1)S(1)}, u32[]{:S(2)}, u32[]{:S(2)}) collective-permute-start(bf16[64,2176]{1,0:T(8,128)(2,1)S(1)} %collective-permute-done.10.refs_0_), channel_id=1, source_target_pairs={{0,2},{1,3},{2,0},{3,1},{4,6},{5,7},{6,4},{7,5},{8,10},{9,11},{10,... | collective-permute-start | bytes 835592 | tf_op jit(solution)/shard_map/ppermute | solution.py:23
  37.8 1.2 %shard_map.51 = bf16[2,64,768]{2,1,0:T(8,128)(2,1)S(1)} custom-call(bf16[2048,1536]{1,0:T(8,128)(2,1)S(1)} %shard_map.47.weights, bf16[64,2176]{1,0:T(8,128)(2,1)S(1)} %collective-permute-done.10.refs_0_), custom_call_target="tpu_custom_call" | custom-call | flops 4026531840 | bytes 6750208 | tf_op jit(solution)/shard_map/pallas_call | solution.py:114
  39.0 6.5 %collective-permute-done.9.refs_0_ = bf16[2,64,768]{2,1,0:T(8,128)(2,1)S(1)} collective-permute-done((bf16[2,64,768]{2,1,0:T(8,128)(2,1)S(1)}, bf16[2,64,768]{2,1,0:T(8,128)(2,1)S(1)}, u32[]{:S(2)}, u32[]{:S(2)}) %collective-permute-start.9) | collective-permute-done | bytes 196640 | tf_op jit(solution)/shard_map/ppermute | solution.py:23
  45.5 2.3 %collective-permute-start.17 = (bf16[2,64,768]{2,1,0:T(8,128)(2,1)S(1)}, bf16[2,64,768]{2,1,0:T(8,128)(2,1)S(1)}, u32[]{:S(2)}, u32[]{:S(2)}) collective-permute-start(bf16[2,64,768]{2,1,0:T(8,128)(2,1)S(1)} %shard_map.51), channel_id=1, source_target_pairs={{0,12},{1,13},{2,14},{3,15},{4,8},{5,9},{6,10},{7,11},{8,4},{9,5},... | collective-permute-start | bytes 589832 | tf_op jit(solution)/shard_map/ppermute | solution.py:23
  47.9 0.0 collective-permute-done.6.refs_1_
  47.9 0.0 collective-permute-done.5.refs_0_
  47.9 0.0 copy-done.4
  47.9 0.6 collective-permute-start.11
  48.5 1.2 %shard_map.52 = bf16[2,64,768]{2,1,0:T(8,128)(2,1)S(1)} custom-call(bf16[2048,1536]{1,0:T(8,128)(2,1)S(1)} %shard_map.47.weights, bf16[64,2176]{1,0:T(8,128)(2,1)S(1)} %collective-permute-done.5.refs_0_), custom_call_target="tpu_custom_call" | custom-call | flops 4026531840 | bytes 6750208 | tf_op jit(solution)/shard_map/pallas_call | solution.py:114
  49.7 1.1 %collective-permute-start.16 = (bf16[2,64,768]{2,1,0:T(8,128)(2,1)S(1)}, bf16[2,64,768]{2,1,0:T(8,128)(2,1)S(1)}, u32[]{:S(2)}, u32[]{:S(2)}) collective-permute-start(bf16[2,64,768]{2,1,0:T(8,128)(2,1)S(1)} %shard_map.52), channel_id=1, source_target_pairs={{0,10},{1,11},{2,8},{3,9},{4,14},{5,15},{6,12},{7,13},{8,2},{9,3},... | collective-permute-start | bytes 589832 | tf_op jit(solution)/shard_map/ppermute | solution.py:23
  50.7 0.0 collective-permute-done.13.refs_0_
  50.7 1.2 %shard_map.53 = bf16[2,64,768]{2,1,0:T(8,128)(2,1)S(1)} custom-call(bf16[2048,1536]{1,0:T(8,128)(2,1)S(1)} %shard_map.47.weights, bf16[64,2176]{1,0:T(8,128)(2,1)S(1)} %collective-permute-done.13.refs_0_), custom_call_target="tpu_custom_call" | custom-call | flops 4026531840 | bytes 6750208 | tf_op jit(solution)/shard_map/pallas_call | solution.py:114
  51.9 2.4 %collective-permute-start.18 = (bf16[2,64,768]{2,1,0:T(8,128)(2,1)S(1)}, bf16[2,64,768]{2,1,0:T(8,128)(2,1)S(1)}, u32[]{:S(2)}, u32[]{:S(2)}) collective-permute-start(bf16[2,64,768]{2,1,0:T(8,128)(2,1)S(1)} %shard_map.53), channel_id=1, source_target_pairs={{0,14},{1,15},{2,12},{3,13},{4,10},{5,11},{6,8},{7,9},{8,6},{9,7},... | collective-permute-start | bytes 589832 | tf_op jit(solution)/shard_map/ppermute | solution.py:23
  54.3 0.0 collective-permute-done.12.refs_1_
  54.3 0.0 collective-permute-done.11.refs_0_
  54.3 0.0 copy-start.1
  54.4 1.4 %shard_map.55 = (bf16[2,64,768]{2,1,0:T(8,128)(2,1)S(1)}, bf16[2,64,768]{2,1,0:T(8,128)(2,1)S(1)}, bf16[2,64,768]{2,1,0:T(8,128)(2,1)S(1)}) custom-call(bf16[2048,1536]{1,0:T(8,128)(2,1)S(1)} %shard_map.47.weights, bf16[64,2176]{1,0:T(8,128)(2,1)S(1)} %shard_map.50.refs_0_, bf16[64,2176]{1,0:T(8,128)(2,1)S(1)} %collective-permute-done.12.refs_1_, ...), custom_call_target="tpu_custom_call" | custom-call | flops 12079595520 | bytes 7667712 | tf_op jit(solution)/shard_map/pallas_call | solution.py:114
  55.8 1.1 %collective-permute-start.14 = (bf16[2,64,768]{2,1,0:T(8,128)(2,1)S(1)}, bf16[2,64,768]{2,1,0:T(8,128)(2,1)S(1)}, u32[]{:S(2)}, u32[]{:S(2)}) collective-permute-start(bf16[2,64,768]{2,1,0:T(8,128)(2,1)S(1)} %get-tuple-element.53), channel_id=1, source_target_pairs={{0,4},{1,5},{2,6},{3,7},{4,0},{5,1},{6,2},{7,3},{8,12},{9,13},{10,... | collective-permute-start | bytes 589832 | tf_op jit(solution)/shard_map/ppermute | solution.py:23
  56.9 1.9 %collective-permute-start.15 = (bf16[2,64,768]{2,1,0:T(8,128)(2,1)S(1)}, bf16[2,64,768]{2,1,0:T(8,128)(2,1)S(1)}, u32[]{:S(2)}, u32[]{:S(2)}) collective-permute-start(bf16[2,64,768]{2,1,0:T(8,128)(2,1)S(1)} %get-tuple-element.54), channel_id=1, source_target_pairs={{0,6},{1,7},{2,4},{3,5},{4,2},{5,3},{6,0},{7,1},{8,14},{9,15},{10,... | collective-permute-start | bytes 589832 | tf_op jit(solution)/shard_map/ppermute | solution.py:23
  58.8 9.9 %collective-permute-done.16.refs_2_ = bf16[2,64,768]{2,1,0:T(8,128)(2,1)S(1)} collective-permute-done((bf16[2,64,768]{2,1,0:T(8,128)(2,1)S(1)}, bf16[2,64,768]{2,1,0:T(8,128)(2,1)S(1)}, u32[]{:S(2)}, u32[]{:S(2)}) %collective-permute-start.16) | collective-permute-done | bytes 196640 | tf_op jit(solution)/shard_map/ppermute | solution.py:23
  68.7 0.0 collective-permute-done.17.refs_3_
  68.7 0.0 collective-permute-done.18.refs_4_
  68.7 0.0 copy-done.1
  68.7 0.4 shard_map.56.refs_3_
  69.1 0.0 collective-permute-done.14.refs_1_
  69.1 3.2 %collective-permute-done.15.refs_2_ = bf16[2,64,768]{2,1,0:T(8,128)(2,1)S(1)} collective-permute-done((bf16[2,64,768]{2,1,0:T(8,128)(2,1)S(1)}, bf16[2,64,768]{2,1,0:T(8,128)(2,1)S(1)}, u32[]{:S(2)}, u32[]{:S(2)}) %collective-permute-start.15) | collective-permute-done | bytes 196640 | tf_op jit(solution)/shard_map/ppermute | solution.py:23
  72.3 1.3 %shard_map.57 = bf16[512,768]{1,0:T(8,128)(2,1)} custom-call(s32[8,64]{1,0:T(8,128)S(1)} %bitcast.10, bf16[2,64,768]{2,1,0:T(8,128)(2,1)S(1)} %collective-permute-done.9.refs_0_, bf16[2,64,768]{2,1,0:T(8,128)(2,1)S(1)} %collective-permute-done.14.refs_1_, bf16[2,64,768]{2,1,0:T(8,128)(2,1)S(1)} %collective-permute-done.15.refs_2_, ...), custom_call_target="tpu_custom_call" | custom-call | tf_op jit(solution)/shard_map/pallas_call | solution.py:155
  (3 shorter events, 0.1 us)
Async XLA Ops:
  0.0 9.0 %collective-permute-start.1 = (bf16[768,2048]{1,0:T(8,128)(2,1)}, bf16[768,2048]{1,0:T(8,128)(2,1)S(1)}, u32[]{:S(2)}, u32[]{:S(2)}) collective-permute-start(bf16[768,2048]{1,0:T(8,128)(2,1)} %bitcast.12), channel_id=1, source_target_pairs={{0,1},{1,0},{2,3},{3,2},{4,5},{5,4},{6,7},{7,6},{8,9},{9,8},{10,11... | collective-permute-start | bytes 9437192 | tf_op jit(solution)/shard_map/ppermute | solution.py:23
  0.5 19.7 %collective-permute-start = (bf16[64,2048]{1,0:T(8,128)(2,1)}, bf16[64,2048]{1,0:T(8,128)(2,1)S(1)}, u32[]{:S(2)}, u32[]{:S(2)}) collective-permute-start(bf16[64,2048]{1,0:T(8,128)(2,1)} %bitcast.14), channel_id=1, source_target_pairs={{0,24},{1,25},{2,26},{3,27},{4,28},{5,29},{6,30},{7,31},{8,16},{9,... | collective-permute-start | bytes 786440 | tf_op jit(solution)/shard_map/ppermute | solution.py:33
  5.0 15.2 %collective-permute-start.3 = (bf16[64,2048]{1,0:T(8,128)(2,1)}, bf16[64,2048]{1,0:T(8,128)(2,1)S(1)}, u32[]{:S(2)}, u32[]{:S(2)}) collective-permute-start(bf16[64,2048]{1,0:T(8,128)(2,1)} %bitcast.15), channel_id=1, source_target_pairs={{0,18},{1,19},{2,16},{3,17},{4,22},{5,23},{6,20},{7,21},{8,26},{9,... | collective-permute-start | bytes 786440 | tf_op jit(solution)/shard_map/ppermute | solution.py:33
  6.4 22.8 %collective-permute-start.7 = (bf16[64,2048]{1,0:T(8,128)(2,1)}, bf16[64,2048]{1,0:T(8,128)(2,1)S(1)}, u32[]{:S(2)}, u32[]{:S(2)}) collective-permute-start(bf16[64,2048]{1,0:T(8,128)(2,1)} %bitcast.16), channel_id=1, source_target_pairs={{0,20},{1,21},{2,22},{3,23},{4,16},{5,17},{6,18},{7,19},{8,28},{9,... | collective-permute-start | bytes 786440 | tf_op jit(solution)/shard_map/ppermute | solution.py:33
  9.0 0.7 copy-start
  9.7 0.7 copy-start.2
  10.4 12.7 %collective-permute-start.2 = (bf16[64,128]{1,0:T(8,128)(2,1)S(1)}, bf16[64,128]{1,0:T(8,128)(2,1)S(1)}, u32[]{:S(2)}, u32[]{:S(2)}) collective-permute-start(bf16[64,128]{1,0:T(8,128)(2,1)S(1)} %shard_map.46.refs_1_), channel_id=1, source_target_pairs={{0,8},{1,9},{2,10},{3,11},{4,12},{5,13},{6,14},{7,15},{8,0},{9,1},... | collective-permute-start | bytes 49160 | tf_op jit(solution)/shard_map/ppermute | solution.py:23
  11.4 11.7 %collective-permute-start.4 = (bf16[64,128]{1,0:T(8,128)(2,1)S(1)}, bf16[64,128]{1,0:T(8,128)(2,1)S(1)}, u32[]{:S(2)}, u32[]{:S(2)}) collective-permute-start(bf16[64,128]{1,0:T(8,128)(2,1)S(1)} %shard_map.46.refs_1_), channel_id=1, source_target_pairs={{0,2},{1,3},{2,0},{3,1},{4,6},{5,7},{6,4},{7,5},{8,10},{9,11},{10,... | collective-permute-start | bytes 49160 | tf_op jit(solution)/shard_map/ppermute | solution.py:23
  12.9 1.9 %copy-start.3 = (bf16[1,1,768,2048]{3,2,1,0:T(8,128)(2,1)S(1)}, bf16[1,1,768,2048]{3,2,1,0:T(8,128)(2,1)}, u32[]{:S(2)}) copy-start(bf16[1,1,768,2048]{3,2,1,0:T(8,128)(2,1)} %param.7) | copy-start | bytes 9437188
  20.2 9.1 %collective-permute-start.8 = (bf16[64,128]{1,0:T(8,128)(2,1)S(1)}, bf16[64,128]{1,0:T(8,128)(2,1)S(1)}, u32[]{:S(2)}, u32[]{:S(2)}) collective-permute-start(bf16[64,128]{1,0:T(8,128)(2,1)S(1)} %shard_map.46.refs_1_), channel_id=1, source_target_pairs={{0,4},{1,5},{2,6},{3,7},{4,0},{5,1},{6,2},{7,3},{8,12},{9,13},{10,... | collective-permute-start | bytes 49160 | tf_op jit(solution)/shard_map/ppermute | solution.py:23
  23.2 12.1 %collective-permute-start.10 = (bf16[64,2176]{1,0:T(8,128)(2,1)S(1)}, bf16[64,2176]{1,0:T(8,128)(2,1)S(1)}, u32[]{:S(2)}, u32[]{:S(2)}) collective-permute-start(bf16[64,2176]{1,0:T(8,128)(2,1)S(1)} %get-tuple-element.37.refs_0_), channel_id=1, source_target_pairs={{0,4},{1,5},{2,6},{3,7},{4,0},{5,1},{6,2},{7,3},{8,12},{9,13},{10,... | collective-permute-start | bytes 835592 | tf_op jit(solution)/shard_map/ppermute | solution.py:23
  25.7 22.1 %collective-permute-start.5 = (bf16[64,2176]{1,0:T(8,128)(2,1)S(1)}, bf16[64,2176]{1,0:T(8,128)(2,1)S(1)}, u32[]{:S(2)}, u32[]{:S(2)}) collective-permute-start(bf16[64,2176]{1,0:T(8,128)(2,1)S(1)} %get-tuple-element.37.refs_0_), channel_id=1, source_target_pairs={{0,2},{1,3},{2,0},{3,1},{4,6},{5,7},{6,4},{7,5},{8,10},{9,11},{10,... | collective-permute-start | bytes 835592 | tf_op jit(solution)/shard_map/ppermute | solution.py:23
  28.2 19.6 %collective-permute-start.6 = (bf16[2,64,768]{2,1,0:T(8,128)(2,1)S(1)}, bf16[2,64,768]{2,1,0:T(8,128)(2,1)S(1)}, u32[]{:S(2)}, u32[]{:S(2)}) collective-permute-start(bf16[2,64,768]{2,1,0:T(8,128)(2,1)S(1)} %get-tuple-element.40), channel_id=1, source_target_pairs={{0,8},{1,9},{2,10},{3,11},{4,12},{5,13},{6,14},{7,15},{8,0},{9,1},... | collective-permute-start | bytes 589832 | tf_op jit(solution)/shard_map/ppermute | solution.py:23
  29.3 25.0 %collective-permute-start.12 = (bf16[64,2176]{1,0:T(8,128)(2,1)S(1)}, bf16[64,2176]{1,0:T(8,128)(2,1)S(1)}, u32[]{:S(2)}, u32[]{:S(2)}) collective-permute-start(bf16[64,2176]{1,0:T(8,128)(2,1)S(1)} %shard_map.50.refs_0_), channel_id=1, source_target_pairs={{0,2},{1,3},{2,0},{3,1},{4,6},{5,7},{6,4},{7,5},{8,10},{9,11},{10,... | collective-permute-start | bytes 835592 | tf_op jit(solution)/shard_map/ppermute | solution.py:23
  29.9 18.0 %copy-start.4 = (bf16[1,64,2048]{2,1,0:T(8,128)(2,1)S(1)}, bf16[1,64,2048]{2,1,0:T(8,128)(2,1)}, u32[]{:S(2)}) copy-start(bf16[1,64,2048]{2,1,0:T(8,128)(2,1)} %param.4) | copy-start | bytes 786436
  29.9 15.6 %collective-permute-start.9 = (bf16[2,64,768]{2,1,0:T(8,128)(2,1)S(1)}, bf16[2,64,768]{2,1,0:T(8,128)(2,1)S(1)}, u32[]{:S(2)}, u32[]{:S(2)}) collective-permute-start(bf16[2,64,768]{2,1,0:T(8,128)(2,1)S(1)} %get-tuple-element.44), channel_id=1, source_target_pairs={{0,2},{1,3},{2,0},{3,1},{4,6},{5,7},{6,4},{7,5},{8,10},{9,11},{10,... | collective-permute-start | bytes 589832 | tf_op jit(solution)/shard_map/ppermute | solution.py:23
  35.3 15.4 %collective-permute-start.13 = (bf16[64,2176]{1,0:T(8,128)(2,1)S(1)}, bf16[64,2176]{1,0:T(8,128)(2,1)S(1)}, u32[]{:S(2)}, u32[]{:S(2)}) collective-permute-start(bf16[64,2176]{1,0:T(8,128)(2,1)S(1)} %collective-permute-done.10.refs_0_), channel_id=1, source_target_pairs={{0,2},{1,3},{2,0},{3,1},{4,6},{5,7},{6,4},{7,5},{8,10},{9,11},{10,... | collective-permute-start | bytes 835592 | tf_op jit(solution)/shard_map/ppermute | solution.py:23
  45.5 23.1 %collective-permute-start.17 = (bf16[2,64,768]{2,1,0:T(8,128)(2,1)S(1)}, bf16[2,64,768]{2,1,0:T(8,128)(2,1)S(1)}, u32[]{:S(2)}, u32[]{:S(2)}) collective-permute-start(bf16[2,64,768]{2,1,0:T(8,128)(2,1)S(1)} %shard_map.51), channel_id=1, source_target_pairs={{0,12},{1,13},{2,14},{3,15},{4,8},{5,9},{6,10},{7,11},{8,4},{9,5},... | collective-permute-start | bytes 589832 | tf_op jit(solution)/shard_map/ppermute | solution.py:23
  47.9 6.4 %collective-permute-start.11 = (bf16[64,2048]{1,0:T(8,128)(2,1)S(1)}, bf16[64,2048]{1,0:T(8,128)(2,1)S(1)}, u32[]{:S(2)}, u32[]{:S(2)}) collective-permute-start(bf16[64,2048]{1,0:T(8,128)(2,1)S(1)} %bitcast.17), channel_id=1, source_target_pairs={{0,16},{1,17},{2,18},{3,19},{4,20},{5,21},{6,22},{7,23},{8,24},{9,... | collective-permute-start | bytes 786440 | tf_op jit(solution)/shard_map/ppermute | solution.py:33
  49.7 19.0 %collective-permute-start.16 = (bf16[2,64,768]{2,1,0:T(8,128)(2,1)S(1)}, bf16[2,64,768]{2,1,0:T(8,128)(2,1)S(1)}, u32[]{:S(2)}, u32[]{:S(2)}) collective-permute-start(bf16[2,64,768]{2,1,0:T(8,128)(2,1)S(1)} %shard_map.52), channel_id=1, source_target_pairs={{0,10},{1,11},{2,8},{3,9},{4,14},{5,15},{6,12},{7,13},{8,2},{9,3},... | collective-permute-start | bytes 589832 | tf_op jit(solution)/shard_map/ppermute | solution.py:23
  51.9 16.7 %collective-permute-start.18 = (bf16[2,64,768]{2,1,0:T(8,128)(2,1)S(1)}, bf16[2,64,768]{2,1,0:T(8,128)(2,1)S(1)}, u32[]{:S(2)}, u32[]{:S(2)}) collective-permute-start(bf16[2,64,768]{2,1,0:T(8,128)(2,1)S(1)} %shard_map.53), channel_id=1, source_target_pairs={{0,14},{1,15},{2,12},{3,13},{4,10},{5,11},{6,8},{7,9},{8,6},{9,7},... | collective-permute-start | bytes 589832 | tf_op jit(solution)/shard_map/ppermute | solution.py:23
  54.3 14.3 %copy-start.1 = (s32[1,64,8]{1,2,0:T(8,128)S(1)}, s32[1,64,8]{1,2,0:T(8,128)}, u32[]{:S(2)}) copy-start(s32[1,64,8]{1,2,0:T(8,128)} %param.5) | copy-start | bytes 6148
  55.8 13.4 %collective-permute-start.14 = (bf16[2,64,768]{2,1,0:T(8,128)(2,1)S(1)}, bf16[2,64,768]{2,1,0:T(8,128)(2,1)S(1)}, u32[]{:S(2)}, u32[]{:S(2)}) collective-permute-start(bf16[2,64,768]{2,1,0:T(8,128)(2,1)S(1)} %get-tuple-element.53), channel_id=1, source_target_pairs={{0,4},{1,5},{2,6},{3,7},{4,0},{5,1},{6,2},{7,3},{8,12},{9,13},{10,... | collective-permute-start | bytes 589832 | tf_op jit(solution)/shard_map/ppermute | solution.py:23
  56.9 15.4 %collective-permute-start.15 = (bf16[2,64,768]{2,1,0:T(8,128)(2,1)S(1)}, bf16[2,64,768]{2,1,0:T(8,128)(2,1)S(1)}, u32[]{:S(2)}, u32[]{:S(2)}) collective-permute-start(bf16[2,64,768]{2,1,0:T(8,128)(2,1)S(1)} %get-tuple-element.54), channel_id=1, source_target_pairs={{0,6},{1,7},{2,4},{3,5},{4,2},{5,3},{6,0},{7,1},{8,14},{9,15},{10,... | collective-permute-start | bytes 589832 | tf_op jit(solution)/shard_map/ppermute | solution.py:23

commit v31 on v30

--- a/solution.py
+++ b/solution.py
@@ -188,23 +188,22 @@
     near, near_columns, _ = tie((near, near_columns, out_far))
     (near,) = widened([near], [near_columns])
     near_side = send(near, owners, X)
-    back_side = send(tie((out_side, near))[0], owners, X)
+    upstream, near = tie((upstream, near))
+    rows = send_across(upstream, owners, 0)
     cross, near = tie((cross, near))
     cross_side = send(cross, owners, X)
     (out_cross,) = work(cross)
     back_cross = send(out_cross, owners, Z_NEAR ^ Z_FAR)
-    far_side, back_far, back_side, upstream, _ = tie(
-        (far_side, back_far, back_side, upstream, out_cross)
-    )
-    rows = send_across(upstream, owners, 0)
-    (out_far_side,) = work(far_side)
+    far_side, back_far, rows, _ = tie((far_side, back_far, rows, out_cross))
+    (rows,) = widened([rows], [columns])
+    out_far_side, out_own = work(far_side, rows)
     back_far_side = send(out_far_side, owners, X ^ Z_FAR)
     cross_side, _ = tie((cross_side, out_far_side))
     (out_cross_side,) = work(cross_side)
     back_cross_side = send(out_cross_side, owners, X ^ Z_NEAR ^ Z_FAR)
-    rows, near_side, _ = tie((rows, near_side, out_cross_side))
-    (rows,) = widened([rows], [columns])
-    out_near, out_near_side, out_own = work(near, near_side, rows)
+    near_side, out_side, _ = tie((near_side, out_side, out_cross_side))
+    out_near, out_near_side = work(near, near_side)
+    back_side = send(out_side, owners, X)
     back_near_side = send(out_near_side, owners, X ^ Z_NEAR)
     back_near = send(out_near, owners, Z_NEAR)
     far_parts = {

time: 73.8 us -> 72.1 us (0.977)
  waiting for transfers between devices: 30.2 us -> 28.1 us
  starting transfers between devices: 30.5 us -> 31.6 us
    ppermute x15, waiting for transfers between devices: 26.4 us -> 24.3 us  [send(): return lax.ppermute(block, 'expert', route)]
    ppermute x15, starting transfers between devices: 21.4 us -> 22.5 us  [send(): return lax.ppermute(block, 'expert', route)]
  transfers between devices with their start and end apart: 19 -> 19, of which waited for: 6 -> 8; matrix products, arithmetic and copies ran while one was open for 0% -> 0% of each run, Pallas kernels for 11% -> 11%
where the time goes in v31:
time: 72.1 us; the launch traced here: 71.9 us
  starting transfers between devices  31.6 us (44%)
  waiting for transfers between devices  28.1 us (39%)
  Pallas kernels  8.93 us (12%)
  local copies, waits for them, and re-layouts  3.26 us (5%)
    ppermute x15, waiting for transfers between devices, send(): return lax.ppermute(block, 'expert', route)  24.3 us
    ppermute x15, starting transfers between devices, send(): return lax.ppermute(block, 'expert', route)  22.5 us
    ppermute x4, starting transfers between devices, send_across(): return lax.ppermute(block, ('pipe', 'expert'), route)  9.02 us
    pallas_call x5, Pallas kernels, products(): pl.pallas_call(functools.partial(products_kernel, len(pieces)), out_shape...  5.33 us
    ppermute x4, waiting for transfers between devices, send_across(): return lax.ppermute(block, ('pipe', 'expert'), route)  3.71 us
    unnamed x10, local copies, waits for them, and re-layouts  3.26 us
    pallas_call x2, Pallas kernels, pick_routes(): pl.pallas_call(functools.partial(pick_kernel, flips), out_shape=jax.Shape...  1.74 us
    pallas_call x1, Pallas kernels, turned(): pl.pallas_call(turn_kernel, out_shape=jax.ShapeDtypeStruct((depth, CORES...  1.67 us
  transfers between devices with their start and end apart: 19, of which 8 were waited for; matrix products, arithmetic and copies ran while one was open for 0% of the time, Pallas kernels for 11%

profile of v31, /device:TPU:0, one launch (start us, length us, event | category | flops | bytes accessed | tf_op | source)
XLA Modules:
  0.0 71.9 jit_solution(18222795599744231183)
XLA Ops:
  0.0 0.5 collective-permute-start.1
  0.5 4.5 %collective-permute-start.3 = (bf16[64,2048]{1,0:T(8,128)(2,1)}, bf16[64,2048]{1,0:T(8,128)(2,1)S(1)}, u32[]{:S(2)}, u32[]{:S(2)}) collective-permute-start(bf16[64,2048]{1,0:T(8,128)(2,1)} %bitcast.14), channel_id=1, source_target_pairs={{0,24},{1,25},{2,26},{3,27},{4,28},{5,29},{6,30},{7,31},{8,16},{9,... | collective-permute-start | bytes 786440 | tf_op jit(solution)/shard_map/ppermute | solution.py:33
  5.0 1.4 %collective-permute-start.5 = (bf16[64,2048]{1,0:T(8,128)(2,1)}, bf16[64,2048]{1,0:T(8,128)(2,1)S(1)}, u32[]{:S(2)}, u32[]{:S(2)}) collective-permute-start(bf16[64,2048]{1,0:T(8,128)(2,1)} %bitcast.15), channel_id=1, source_target_pairs={{0,18},{1,19},{2,16},{3,17},{4,22},{5,23},{6,20},{7,21},{8,26},{9,... | collective-permute-start | bytes 786440 | tf_op jit(solution)/shard_map/ppermute | solution.py:33
  6.4 2.5 %collective-permute-start = (bf16[64,2048]{1,0:T(8,128)(2,1)}, bf16[64,2048]{1,0:T(8,128)(2,1)S(1)}, u32[]{:S(2)}, u32[]{:S(2)}) collective-permute-start(bf16[64,2048]{1,0:T(8,128)(2,1)} %bitcast.16), channel_id=1, source_target_pairs={{0,20},{1,21},{2,22},{3,23},{4,16},{5,17},{6,18},{7,19},{8,28},{9,... | collective-permute-start | bytes 786440 | tf_op jit(solution)/shard_map/ppermute | solution.py:33
  9.0 0.0 collective-permute-done.1.other
  9.0 0.0 copy-start
  9.0 0.7 copy-done
  9.7 0.0 copy-start.2
  9.7 0.7 copy-done.2
  10.3 0.1 shard_map.46.refs_1_
  10.4 1.0 %collective-permute-start.4 = (bf16[64,128]{1,0:T(8,128)(2,1)S(1)}, bf16[64,128]{1,0:T(8,128)(2,1)S(1)}, u32[]{:S(2)}, u32[]{:S(2)}) collective-permute-start(bf16[64,128]{1,0:T(8,128)(2,1)S(1)} %shard_map.46.refs_1_), channel_id=1, source_target_pairs={{0,8},{1,9},{2,10},{3,11},{4,12},{5,13},{6,14},{7,15},{8,0},{9,1},... | collective-permute-start | bytes 49160 | tf_op jit(solution)/shard_map/ppermute | solution.py:23
  11.4 1.5 %collective-permute-start.6 = (bf16[64,128]{1,0:T(8,128)(2,1)S(1)}, bf16[64,128]{1,0:T(8,128)(2,1)S(1)}, u32[]{:S(2)}, u32[]{:S(2)}) collective-permute-start(bf16[64,128]{1,0:T(8,128)(2,1)S(1)} %shard_map.46.refs_1_), channel_id=1, source_target_pairs={{0,2},{1,3},{2,0},{3,1},{4,6},{5,7},{6,4},{7,5},{8,10},{9,11},{10,... | collective-permute-start | bytes 49160 | tf_op jit(solution)/shard_map/ppermute | solution.py:23
  12.9 0.0 copy-start.3
  12.9 1.9 %copy-done.3 = bf16[1,1,768,2048]{3,2,1,0:T(8,128)(2,1)S(1)} copy-done((bf16[1,1,768,2048]{3,2,1,0:T(8,128)(2,1)S(1)}, bf16[1,1,768,2048]{3,2,1,0:T(8,128)(2,1)}, u32[]{:S(2)}) %copy-start.3) | copy-done | bytes 3145752
  14.8 1.7 %shard_map.47.weights = bf16[2048,1536]{1,0:T(8,128)(2,1)S(1)} custom-call(bf16[768,2048]{1,0:T(8,128)(2,1)S(1)} %bitcast.13, bf16[768,2048]{1,0:T(8,128)(2,1)S(1)} %collective-permute-done.1.other), custom_call_target="tpu_custom_call" | custom-call | flops 12884901888 | tf_op jit(solution)/shard_map/pallas_call | solution.py:82
  16.5 3.7 %collective-permute-done.3.refs_0_ = bf16[64,2048]{1,0:T(8,128)(2,1)S(1)} collective-permute-done((bf16[64,2048]{1,0:T(8,128)(2,1)}, bf16[64,2048]{1,0:T(8,128)(2,1)S(1)}, u32[]{:S(2)}, u32[]{:S(2)}) %collective-permute-start.3) | collective-permute-done | bytes 262176 | tf_op jit(solution)/shard_map/ppermute | solution.py:33
  20.2 0.0 collective-permute-start.2
  20.2 0.0 collective-permute-done.5.refs_1_
  20.2 2.9 %collective-permute-done.4.refs_2_ = bf16[64,128]{1,0:T(8,128)(2,1)S(1)} collective-permute-done((bf16[64,128]{1,0:T(8,128)(2,1)S(1)}, bf16[64,128]{1,0:T(8,128)(2,1)S(1)}, u32[]{:S(2)}, u32[]{:S(2)}) %collective-permute-start.4) | collective-permute-done | bytes 16416 | tf_op jit(solution)/shard_map/ppermute | solution.py:23
  23.1 0.0 collective-permute-done.6.refs_3_
  23.2 2.6 %collective-permute-start.8 = (bf16[64,2176]{1,0:T(8,128)(2,1)S(1)}, bf16[64,2176]{1,0:T(8,128)(2,1)S(1)}, u32[]{:S(2)}, u32[]{:S(2)}) collective-permute-start(bf16[64,2176]{1,0:T(8,128)(2,1)S(1)} %get-tuple-element.39.refs_0_), channel_id=1, source_target_pairs={{0,4},{1,5},{2,6},{3,7},{4,0},{5,1},{6,2},{7,3},{8,12},{9,13},{10,... | collective-permute-start | bytes 835592 | tf_op jit(solution)/shard_map/ppermute | solution.py:23
  25.7 1.5 %collective-permute-start.10 = (bf16[64,2176]{1,0:T(8,128)(2,1)S(1)}, bf16[64,2176]{1,0:T(8,128)(2,1)S(1)}, u32[]{:S(2)}, u32[]{:S(2)}) collective-permute-start(bf16[64,2176]{1,0:T(8,128)(2,1)S(1)} %get-tuple-element.39.refs_0_), channel_id=1, source_target_pairs={{0,2},{1,3},{2,0},{3,1},{4,6},{5,7},{6,4},{7,5},{8,10},{9,11},{10,... | collective-permute-start | bytes 835592 | tf_op jit(solution)/shard_map/ppermute | solution.py:23
  27.2 0.0 copy-start.4
  27.2 1.0 %shard_map.49 = (bf16[2,64,768]{2,1,0:T(8,128)(2,1)S(1)}, bf16[2,64,768]{2,1,0:T(8,128)(2,1)S(1)}) custom-call(bf16[2048,1536]{1,0:T(8,128)(2,1)S(1)} %shard_map.47.weights, bf16[64,2176]{1,0:T(8,128)(2,1)S(1)} %get-tuple-element.39.refs_0_, bf16[64,2176]{1,0:T(8,128)(2,1)S(1)} %get-tuple-element.40.refs_1_), custom_call_target="tpu_custom_call" | custom-call | flops 8053063680 | bytes 7208960 | tf_op jit(solution)/shard_map/pallas_call | solution.py:114
  28.2 1.0 %collective-permute-start.11 = (bf16[2,64,768]{2,1,0:T(8,128)(2,1)S(1)}, bf16[2,64,768]{2,1,0:T(8,128)(2,1)S(1)}, u32[]{:S(2)}, u32[]{:S(2)}) collective-permute-start(bf16[2,64,768]{2,1,0:T(8,128)(2,1)S(1)} %get-tuple-element.41), channel_id=1, source_target_pairs={{0,8},{1,9},{2,10},{3,11},{4,12},{5,13},{6,14},{7,15},{8,0},{9,1},... | collective-permute-start | bytes 589832 | tf_op jit(solution)/shard_map/ppermute | solution.py:23
  29.3 0.0 collective-permute-done.refs_0_
  29.3 0.0 collective-permute-done.2.refs_1_
  29.3 0.6 collective-permute-start.7
  29.9 0.0 copy-done.4
  29.9 0.5 collective-permute-start.12
  30.4 4.9 %collective-permute-done.8.refs_0_ = bf16[64,2176]{1,0:T(8,128)(2,1)S(1)} collective-permute-done((bf16[64,2176]{1,0:T(8,128)(2,1)S(1)}, bf16[64,2176]{1,0:T(8,128)(2,1)S(1)}, u32[]{:S(2)}, u32[]{:S(2)}) %collective-permute-start.8) | collective-permute-done | bytes 278560 | tf_op jit(solution)/shard_map/ppermute | solution.py:23
  35.3 2.5 %collective-permute-start.9 = (bf16[64,2176]{1,0:T(8,128)(2,1)S(1)}, bf16[64,2176]{1,0:T(8,128)(2,1)S(1)}, u32[]{:S(2)}, u32[]{:S(2)}) collective-permute-start(bf16[64,2176]{1,0:T(8,128)(2,1)S(1)} %collective-permute-done.8.refs_0_), channel_id=1, source_target_pairs={{0,2},{1,3},{2,0},{3,1},{4,6},{5,7},{6,4},{7,5},{8,10},{9,11},{10,... | collective-permute-start | bytes 835592 | tf_op jit(solution)/shard_map/ppermute | solution.py:23
  37.8 1.2 %shard_map.51 = bf16[2,64,768]{2,1,0:T(8,128)(2,1)S(1)} custom-call(bf16[2048,1536]{1,0:T(8,128)(2,1)S(1)} %shard_map.47.weights, bf16[64,2176]{1,0:T(8,128)(2,1)S(1)} %collective-permute-done.8.refs_0_), custom_call_target="tpu_custom_call" | custom-call | flops 4026531840 | bytes 6750208 | tf_op jit(solution)/shard_map/pallas_call | solution.py:114
  39.0 0.2 collective-permute-done.11.refs_1_
  39.2 2.7 %collective-permute-start.17 = (bf16[2,64,768]{2,1,0:T(8,128)(2,1)S(1)}, bf16[2,64,768]{2,1,0:T(8,128)(2,1)S(1)}, u32[]{:S(2)}, u32[]{:S(2)}) collective-permute-start(bf16[2,64,768]{2,1,0:T(8,128)(2,1)S(1)} %shard_map.51), channel_id=1, source_target_pairs={{0,12},{1,13},{2,14},{3,15},{4,8},{5,9},{6,10},{7,11},{8,4},{9,5},... | collective-permute-start | bytes 589832 | tf_op jit(solution)/shard_map/ppermute | solution.py:23
  42.0 0.0 collective-permute-done.12.refs_0_
  42.0 0.0 collective-permute-done.10.refs_0_
  42.0 1.0 %shard_map.53 = (bf16[2,64,768]{2,1,0:T(8,128)(2,1)S(1)}, bf16[2,64,768]{2,1,0:T(8,128)(2,1)S(1)}) custom-call(bf16[2048,1536]{1,0:T(8,128)(2,1)S(1)} %shard_map.47.weights, bf16[64,2176]{1,0:T(8,128)(2,1)S(1)} %collective-permute-done.10.refs_0_, bf16[64,2176]{1,0:T(8,128)(2,1)S(1)} %shard_map.52.refs_1_), custom_call_target="tpu_custom_call" | custom-call | flops 8053063680 | bytes 7208960 | tf_op jit(solution)/shard_map/pallas_call | solution.py:114
  43.0 0.1 collective-permute-start.16
  43.1 2.4 %collective-permute-done.9.refs_0_ = bf16[64,2176]{1,0:T(8,128)(2,1)S(1)} collective-permute-done((bf16[64,2176]{1,0:T(8,128)(2,1)S(1)}, bf16[64,2176]{1,0:T(8,128)(2,1)S(1)}, u32[]{:S(2)}, u32[]{:S(2)}) %collective-permute-start.9) | collective-permute-done | bytes 278560 | tf_op jit(solution)/shard_map/ppermute | solution.py:23
  45.5 1.2 %shard_map.54 = bf16[2,64,768]{2,1,0:T(8,128)(2,1)S(1)} custom-call(bf16[2048,1536]{1,0:T(8,128)(2,1)S(1)} %shard_map.47.weights, bf16[64,2176]{1,0:T(8,128)(2,1)S(1)} %collective-permute-done.9.refs_0_), custom_call_target="tpu_custom_call" | custom-call | flops 4026531840 | bytes 6750208 | tf_op jit(solution)/shard_map/pallas_call | solution.py:114
  46.7 3.3 %collective-permute-start.18 = (bf16[2,64,768]{2,1,0:T(8,128)(2,1)S(1)}, bf16[2,64,768]{2,1,0:T(8,128)(2,1)S(1)}, u32[]{:S(2)}, u32[]{:S(2)}) collective-permute-start(bf16[2,64,768]{2,1,0:T(8,128)(2,1)S(1)} %shard_map.54), channel_id=1, source_target_pairs={{0,14},{1,15},{2,12},{3,13},{4,10},{5,11},{6,8},{7,9},{8,6},{9,7},... | collective-permute-start | bytes 589832 | tf_op jit(solution)/shard_map/ppermute | solution.py:23
  50.1 0.0 collective-permute-done.7.refs_1_
  50.1 0.0 copy-start.1
  50.1 1.0 %shard_map.55 = (bf16[2,64,768]{2,1,0:T(8,128)(2,1)S(1)}, bf16[2,64,768]{2,1,0:T(8,128)(2,1)S(1)}) custom-call(bf16[2048,1536]{1,0:T(8,128)(2,1)S(1)} %shard_map.47.weights, bf16[64,2176]{1,0:T(8,128)(2,1)S(1)} %shard_map.50.refs_0_, bf16[64,2176]{1,0:T(8,128)(2,1)S(1)} %collective-permute-done.7.refs_1_), custom_call_target="tpu_custom_call" | custom-call | flops 8053063680 | bytes 7208960 | tf_op jit(solution)/shard_map/pallas_call | solution.py:114
  51.1 1.1 %collective-permute-start.14 = (bf16[2,64,768]{2,1,0:T(8,128)(2,1)S(1)}, bf16[2,64,768]{2,1,0:T(8,128)(2,1)S(1)}, u32[]{:S(2)}, u32[]{:S(2)}) collective-permute-start(bf16[2,64,768]{2,1,0:T(8,128)(2,1)S(1)} %get-tuple-element.55), channel_id=1, source_target_pairs={{0,4},{1,5},{2,6},{3,7},{4,0},{5,1},{6,2},{7,3},{8,12},{9,13},{10,... | collective-permute-start | bytes 589832 | tf_op jit(solution)/shard_map/ppermute | solution.py:23
  52.2 2.7 %collective-permute-start.15 = (bf16[2,64,768]{2,1,0:T(8,128)(2,1)S(1)}, bf16[2,64,768]{2,1,0:T(8,128)(2,1)S(1)}, u32[]{:S(2)}, u32[]{:S(2)}) collective-permute-start(bf16[2,64,768]{2,1,0:T(8,128)(2,1)S(1)} %get-tuple-element.56), channel_id=1, source_target_pairs={{0,6},{1,7},{2,4},{3,5},{4,2},{5,3},{6,0},{7,1},{8,14},{9,15},{10,... | collective-permute-start | bytes 589832 | tf_op jit(solution)/shard_map/ppermute | solution.py:23
  54.8 8.0 %collective-permute-done.16.refs_2_ = bf16[2,64,768]{2,1,0:T(8,128)(2,1)S(1)} collective-permute-done((bf16[2,64,768]{2,1,0:T(8,128)(2,1)S(1)}, bf16[2,64,768]{2,1,0:T(8,128)(2,1)S(1)}, u32[]{:S(2)}, u32[]{:S(2)}) %collective-permute-start.16) | collective-permute-done | bytes 196640 | tf_op jit(solution)/shard_map/ppermute | solution.py:23
  62.8 1.5 %collective-permute-start.13 = (bf16[2,64,768]{2,1,0:T(8,128)(2,1)S(1)}, bf16[2,64,768]{2,1,0:T(8,128)(2,1)S(1)}, u32[]{:S(2)}, u32[]{:S(2)}) collective-permute-start(bf16[2,64,768]{2,1,0:T(8,128)(2,1)S(1)} %get-tuple-element.52), channel_id=1, source_target_pairs={{0,2},{1,3},{2,0},{3,1},{4,6},{5,7},{6,4},{7,5},{8,10},{9,11},{10,... | collective-permute-start | bytes 589832 | tf_op jit(solution)/shard_map/ppermute | solution.py:23
  64.3 0.0 collective-permute-done.17.refs_3_
  64.3 0.0 collective-permute-done.18.refs_4_
  64.3 0.0 copy-done.1
  64.3 0.4 shard_map.56.refs_3_
  64.8 0.0 collective-permute-done.14.refs_1_
  64.8 2.6 %collective-permute-done.15.refs_2_ = bf16[2,64,768]{2,1,0:T(8,128)(2,1)S(1)} collective-permute-done((bf16[2,64,768]{2,1,0:T(8,128)(2,1)S(1)}, bf16[2,64,768]{2,1,0:T(8,128)(2,1)S(1)}, u32[]{:S(2)}, u32[]{:S(2)}) %collective-permute-start.15) | collective-permute-done | bytes 196640 | tf_op jit(solution)/shard_map/ppermute | solution.py:23
  67.4 3.2 %collective-permute-done.13.refs_0_ = bf16[2,64,768]{2,1,0:T(8,128)(2,1)S(1)} collective-permute-done((bf16[2,64,768]{2,1,0:T(8,128)(2,1)S(1)}, bf16[2,64,768]{2,1,0:T(8,128)(2,1)S(1)}, u32[]{:S(2)}, u32[]{:S(2)}) %collective-permute-start.13) | collective-permute-done | bytes 196640 | tf_op jit(solution)/shard_map/ppermute | solution.py:23
  70.6 1.3 %shard_map.57 = bf16[512,768]{1,0:T(8,128)(2,1)} custom-call(s32[8,64]{1,0:T(8,128)S(1)} %bitcast.10, bf16[2,64,768]{2,1,0:T(8,128)(2,1)S(1)} %collective-permute-done.13.refs_0_, bf16[2,64,768]{2,1,0:T(8,128)(2,1)S(1)} %collective-permute-done.14.refs_1_, bf16[2,64,768]{2,1,0:T(8,128)(2,1)S(1)} %collective-permute-done.15.refs_2_, ...), custom_call_target="tpu_custom_call" | custom-call | tf_op jit(solution)/shard_map/pallas_call | solution.py:155
  (3 shorter events, 0.1 us)
Async XLA Ops:
  0.0 9.0 %collective-permute-start.1 = (bf16[768,2048]{1,0:T(8,128)(2,1)}, bf16[768,2048]{1,0:T(8,128)(2,1)S(1)}, u32[]{:S(2)}, u32[]{:S(2)}) collective-permute-start(bf16[768,2048]{1,0:T(8,128)(2,1)} %bitcast.12), channel_id=1, source_target_pairs={{0,1},{1,0},{2,3},{3,2},{4,5},{5,4},{6,7},{7,6},{8,9},{9,8},{10,11... | collective-permute-start | bytes 9437192 | tf_op jit(solution)/shard_map/ppermute | solution.py:23
  0.5 19.7 %collective-permute-start.3 = (bf16[64,2048]{1,0:T(8,128)(2,1)}, bf16[64,2048]{1,0:T(8,128)(2,1)S(1)}, u32[]{:S(2)}, u32[]{:S(2)}) collective-permute-start(bf16[64,2048]{1,0:T(8,128)(2,1)} %bitcast.14), channel_id=1, source_target_pairs={{0,24},{1,25},{2,26},{3,27},{4,28},{5,29},{6,30},{7,31},{8,16},{9,... | collective-permute-start | bytes 786440 | tf_op jit(solution)/shard_map/ppermute | solution.py:33
  5.0 15.2 %collective-permute-start.5 = (bf16[64,2048]{1,0:T(8,128)(2,1)}, bf16[64,2048]{1,0:T(8,128)(2,1)S(1)}, u32[]{:S(2)}, u32[]{:S(2)}) collective-permute-start(bf16[64,2048]{1,0:T(8,128)(2,1)} %bitcast.15), channel_id=1, source_target_pairs={{0,18},{1,19},{2,16},{3,17},{4,22},{5,23},{6,20},{7,21},{8,26},{9,... | collective-permute-start | bytes 786440 | tf_op jit(solution)/shard_map/ppermute | solution.py:33
  6.4 22.8 %collective-permute-start = (bf16[64,2048]{1,0:T(8,128)(2,1)}, bf16[64,2048]{1,0:T(8,128)(2,1)S(1)}, u32[]{:S(2)}, u32[]{:S(2)}) collective-permute-start(bf16[64,2048]{1,0:T(8,128)(2,1)} %bitcast.16), channel_id=1, source_target_pairs={{0,20},{1,21},{2,22},{3,23},{4,16},{5,17},{6,18},{7,19},{8,28},{9,... | collective-permute-start | bytes 786440 | tf_op jit(solution)/shard_map/ppermute | solution.py:33
  9.0 0.7 copy-start
  9.7 0.7 copy-start.2
  10.4 12.7 %collective-permute-start.4 = (bf16[64,128]{1,0:T(8,128)(2,1)S(1)}, bf16[64,128]{1,0:T(8,128)(2,1)S(1)}, u32[]{:S(2)}, u32[]{:S(2)}) collective-permute-start(bf16[64,128]{1,0:T(8,128)(2,1)S(1)} %shard_map.46.refs_1_), channel_id=1, source_target_pairs={{0,8},{1,9},{2,10},{3,11},{4,12},{5,13},{6,14},{7,15},{8,0},{9,1},... | collective-permute-start | bytes 49160 | tf_op jit(solution)/shard_map/ppermute | solution.py:23
  11.4 11.7 %collective-permute-start.6 = (bf16[64,128]{1,0:T(8,128)(2,1)S(1)}, bf16[64,128]{1,0:T(8,128)(2,1)S(1)}, u32[]{:S(2)}, u32[]{:S(2)}) collective-permute-start(bf16[64,128]{1,0:T(8,128)(2,1)S(1)} %shard_map.46.refs_1_), channel_id=1, source_target_pairs={{0,2},{1,3},{2,0},{3,1},{4,6},{5,7},{6,4},{7,5},{8,10},{9,11},{10,... | collective-permute-start | bytes 49160 | tf_op jit(solution)/shard_map/ppermute | solution.py:23
  12.9 1.9 %copy-start.3 = (bf16[1,1,768,2048]{3,2,1,0:T(8,128)(2,1)S(1)}, bf16[1,1,768,2048]{3,2,1,0:T(8,128)(2,1)}, u32[]{:S(2)}) copy-start(bf16[1,1,768,2048]{3,2,1,0:T(8,128)(2,1)} %param.7) | copy-start | bytes 9437188
  20.2 9.1 %collective-permute-start.2 = (bf16[64,128]{1,0:T(8,128)(2,1)S(1)}, bf16[64,128]{1,0:T(8,128)(2,1)S(1)}, u32[]{:S(2)}, u32[]{:S(2)}) collective-permute-start(bf16[64,128]{1,0:T(8,128)(2,1)S(1)} %shard_map.46.refs_1_), channel_id=1, source_target_pairs={{0,4},{1,5},{2,6},{3,7},{4,0},{5,1},{6,2},{7,3},{8,12},{9,13},{10,... | collective-permute-start | bytes 49160 | tf_op jit(solution)/shard_map/ppermute | solution.py:23
  23.2 12.1 %collective-permute-start.8 = (bf16[64,2176]{1,0:T(8,128)(2,1)S(1)}, bf16[64,2176]{1,0:T(8,128)(2,1)S(1)}, u32[]{:S(2)}, u32[]{:S(2)}) collective-permute-start(bf16[64,2176]{1,0:T(8,128)(2,1)S(1)} %get-tuple-element.39.refs_0_), channel_id=1, source_target_pairs={{0,4},{1,5},{2,6},{3,7},{4,0},{5,1},{6,2},{7,3},{8,12},{9,13},{10,... | collective-permute-start | bytes 835592 | tf_op jit(solution)/shard_map/ppermute | solution.py:23
  25.7 16.2 %collective-permute-start.10 = (bf16[64,2176]{1,0:T(8,128)(2,1)S(1)}, bf16[64,2176]{1,0:T(8,128)(2,1)S(1)}, u32[]{:S(2)}, u32[]{:S(2)}) collective-permute-start(bf16[64,2176]{1,0:T(8,128)(2,1)S(1)} %get-tuple-element.39.refs_0_), channel_id=1, source_target_pairs={{0,2},{1,3},{2,0},{3,1},{4,6},{5,7},{6,4},{7,5},{8,10},{9,11},{10,... | collective-permute-start | bytes 835592 | tf_op jit(solution)/shard_map/ppermute | solution.py:23
  27.2 2.6 %copy-start.4 = (bf16[1,64,2048]{2,1,0:T(8,128)(2,1)S(1)}, bf16[1,64,2048]{2,1,0:T(8,128)(2,1)}, u32[]{:S(2)}) copy-start(bf16[1,64,2048]{2,1,0:T(8,128)(2,1)} %param.4) | copy-start | bytes 786436
  28.2 11.0 %collective-permute-start.11 = (bf16[2,64,768]{2,1,0:T(8,128)(2,1)S(1)}, bf16[2,64,768]{2,1,0:T(8,128)(2,1)S(1)}, u32[]{:S(2)}, u32[]{:S(2)}) collective-permute-start(bf16[2,64,768]{2,1,0:T(8,128)(2,1)S(1)} %get-tuple-element.41), channel_id=1, source_target_pairs={{0,8},{1,9},{2,10},{3,11},{4,12},{5,13},{6,14},{7,15},{8,0},{9,1},... | collective-permute-start | bytes 589832 | tf_op jit(solution)/shard_map/ppermute | solution.py:23
  29.3 20.8 %collective-permute-start.7 = (bf16[64,2176]{1,0:T(8,128)(2,1)S(1)}, bf16[64,2176]{1,0:T(8,128)(2,1)S(1)}, u32[]{:S(2)}, u32[]{:S(2)}) collective-permute-start(bf16[64,2176]{1,0:T(8,128)(2,1)S(1)} %shard_map.50.refs_0_), channel_id=1, source_target_pairs={{0,2},{1,3},{2,0},{3,1},{4,6},{5,7},{6,4},{7,5},{8,10},{9,11},{10,... | collective-permute-start | bytes 835592 | tf_op jit(solution)/shard_map/ppermute | solution.py:23
  29.9 12.1 %collective-permute-start.12 = (bf16[64,2048]{1,0:T(8,128)(2,1)S(1)}, bf16[64,2048]{1,0:T(8,128)(2,1)S(1)}, u32[]{:S(2)}, u32[]{:S(2)}) collective-permute-start(bf16[64,2048]{1,0:T(8,128)(2,1)S(1)} %bitcast.17), channel_id=1, source_target_pairs={{0,16},{1,17},{2,18},{3,19},{4,20},{5,21},{6,22},{7,23},{8,24},{9,... | collective-permute-start | bytes 786440 | tf_op jit(solution)/shard_map/ppermute | solution.py:33
  35.3 10.2 %collective-permute-start.9 = (bf16[64,2176]{1,0:T(8,128)(2,1)S(1)}, bf16[64,2176]{1,0:T(8,128)(2,1)S(1)}, u32[]{:S(2)}, u32[]{:S(2)}) collective-permute-start(bf16[64,2176]{1,0:T(8,128)(2,1)S(1)} %collective-permute-done.8.refs_0_), channel_id=1, source_target_pairs={{0,2},{1,3},{2,0},{3,1},{4,6},{5,7},{6,4},{7,5},{8,10},{9,11},{10,... | collective-permute-start | bytes 835592 | tf_op jit(solution)/shard_map/ppermute | solution.py:23
  39.2 25.1 %collective-permute-start.17 = (bf16[2,64,768]{2,1,0:T(8,128)(2,1)S(1)}, bf16[2,64,768]{2,1,0:T(8,128)(2,1)S(1)}, u32[]{:S(2)}, u32[]{:S(2)}) collective-permute-start(bf16[2,64,768]{2,1,0:T(8,128)(2,1)S(1)} %shard_map.51), channel_id=1, source_target_pairs={{0,12},{1,13},{2,14},{3,15},{4,8},{5,9},{6,10},{7,11},{8,4},{9,5},... | collective-permute-start | bytes 589832 | tf_op jit(solution)/shard_map/ppermute | solution.py:23
  43.0 19.8 %collective-permute-start.16 = (bf16[2,64,768]{2,1,0:T(8,128)(2,1)S(1)}, bf16[2,64,768]{2,1,0:T(8,128)(2,1)S(1)}, u32[]{:S(2)}, u32[]{:S(2)}) collective-permute-start(bf16[2,64,768]{2,1,0:T(8,128)(2,1)S(1)} %get-tuple-element.50), channel_id=1, source_target_pairs={{0,10},{1,11},{2,8},{3,9},{4,14},{5,15},{6,12},{7,13},{8,2},{9,3},... | collective-permute-start | bytes 589832 | tf_op jit(solution)/shard_map/ppermute | solution.py:23
  46.7 17.6 %collective-permute-start.18 = (bf16[2,64,768]{2,1,0:T(8,128)(2,1)S(1)}, bf16[2,64,768]{2,1,0:T(8,128)(2,1)S(1)}, u32[]{:S(2)}, u32[]{:S(2)}) collective-permute-start(bf16[2,64,768]{2,1,0:T(8,128)(2,1)S(1)} %shard_map.54), channel_id=1, source_target_pairs={{0,14},{1,15},{2,12},{3,13},{4,10},{5,11},{6,8},{7,9},{8,6},{9,7},... | collective-permute-start | bytes 589832 | tf_op jit(solution)/shard_map/ppermute | solution.py:23
  50.1 14.3 %copy-start.1 = (s32[1,64,8]{1,2,0:T(8,128)S(1)}, s32[1,64,8]{1,2,0:T(8,128)}, u32[]{:S(2)}) copy-start(s32[1,64,8]{1,2,0:T(8,128)} %param.5) | copy-start | bytes 6148
  51.1 13.7 %collective-permute-start.14 = (bf16[2,64,768]{2,1,0:T(8,128)(2,1)S(1)}, bf16[2,64,768]{2,1,0:T(8,128)(2,1)S(1)}, u32[]{:S(2)}, u32[]{:S(2)}) collective-permute-start(bf16[2,64,768]{2,1,0:T(8,128)(2,1)S(1)} %get-tuple-element.55), channel_id=1, source_target_pairs={{0,4},{1,5},{2,6},{3,7},{4,0},{5,1},{6,2},{7,3},{8,12},{9,13},{10,... | collective-permute-start | bytes 589832 | tf_op jit(solution)/shard_map/ppermute | solution.py:23
  52.2 15.3 %collective-permute-start.15 = (bf16[2,64,768]{2,1,0:T(8,128)(2,1)S(1)}, bf16[2,64,768]{2,1,0:T(8,128)(2,1)S(1)}, u32[]{:S(2)}, u32[]{:S(2)}) collective-permute-start(bf16[2,64,768]{2,1,0:T(8,128)(2,1)S(1)} %get-tuple-element.56), channel_id=1, source_target_pairs={{0,6},{1,7},{2,4},{3,5},{4,2},{5,3},{6,0},{7,1},{8,14},{9,15},{10,... | collective-permute-start | bytes 589832 | tf_op jit(solution)/shard_map/ppermute | solution.py:23
  62.8 7.8 %collective-permute-start.13 = (bf16[2,64,768]{2,1,0:T(8,128)(2,1)S(1)}, bf16[2,64,768]{2,1,0:T(8,128)(2,1)S(1)}, u32[]{:S(2)}, u32[]{:S(2)}) collective-permute-start(bf16[2,64,768]{2,1,0:T(8,128)(2,1)S(1)} %get-tuple-element.52), channel_id=1, source_target_pairs={{0,2},{1,3},{2,0},{3,1},{4,6},{5,7},{6,4},{7,5},{8,10},{9,11},{10,... | collective-permute-start | bytes 589832 | tf_op jit(solution)/shard_map/ppermute | solution.py:23

commit v32 on v28

--- a/solution.py
+++ b/solution.py
@@ -181,25 +181,25 @@
     near, _ = tie((near, out_far))
     near = widened(near, near_columns)
     near_side = send(near, owners, X)
-    rows, near = tie((rows, near))
-    rows = widened(rows, columns)
-    side = send(rows, owners, X)
-    cross, near, rows = tie((cross, near, rows))
+    cross, near = tie((cross, near))
     cross_side = send(cross, owners, X)
     (out_cross,) = work(cross)
     back_cross = send(out_cross, owners, Z_NEAR ^ Z_FAR)
-    far_side, back_far, _ = tie((far_side, back_far, out_cross))
+    far_side, back_far, rows, _ = tie((far_side, back_far, rows, out_cross))
+    rows = widened(rows, columns)
+    side = send(rows, owners, X)
     (out_far_side,) = work(far_side)
     back_far_side = send(out_far_side, owners, X ^ Z_FAR)
     cross_side, _ = tie((cross_side, out_far_side))
     (out_cross_side,) = work(cross_side)
     back_cross_side = send(out_cross_side, owners, X ^ Z_NEAR ^ Z_FAR)
-    near_side, side, _ = tie((near_side, side, out_cross_side))
-    out_own, out_side, out_near, out_near_side = work(rows, side, near, near_side)
+    near_side, _ = tie((near_side, out_cross_side))
+    out_near, out_near_side = work(near, near_side)
     back_near_side = send(out_near_side, owners, X ^ Z_NEAR)
-    out_side, back_far_side = tie((out_side, back_far_side))
+    back_near = send(out_near, owners, Z_NEAR)
+    side, rows, _ = tie((side, rows, out_near_side))
+    out_side, out_own = work(side, rows)
     back_side = send(out_side, owners, X)
-    back_near = send(out_near, owners, Z_NEAR)
     far_parts = {
         0: out_own,
         Z_FAR: back_far,

time: 70 us -> 66.9 us (0.956)
  waiting for transfers between devices: 25.6 us -> 22.6 us
    ppermute x15, waiting for transfers between devices: 25.5 us -> 22.6 us  [send(): return lax.ppermute(block, 'expert', route)]
    pallas_call x5 -> x6, Pallas kernels: 6.55 us -> 6.72 us  [products(): pl.pallas_call(functools.partial(products_kernel, len(pieces)), out_shape...]
  transfers between devices with their start and end apart: 18 -> 18, of which waited for: 7 -> 6; matrix products, arithmetic and copies ran while one was open for 0% -> 0% of each run, Pallas kernels for 13% -> 13%
where the time goes in v32:
time: 66.9 us; the launch traced here: 66.7 us
  starting transfers between devices  30.3 us (45%)
  waiting for transfers between devices  22.6 us (34%)
  Pallas kernels  10.3 us (15%)
  local copies, waits for them, and re-layouts  3.26 us (5%)
    ppermute x15, starting transfers between devices, send(): return lax.ppermute(block, 'expert', route)  23.9 us
    ppermute x15, waiting for transfers between devices, send(): return lax.ppermute(block, 'expert', route)  22.6 us
    pallas_call x6, Pallas kernels, products(): pl.pallas_call(functools.partial(products_kernel, len(pieces)), out_shape...  6.72 us
    ppermute x3, starting transfers between devices, send_across(): return lax.ppermute(block, ('pipe', 'expert'), route)  6.45 us
    unnamed x8, local copies, waits for them, and re-layouts  3.26 us
    pallas_call x2, Pallas kernels, pick_routes(): pl.pallas_call(functools.partial(pick_kernel, flips), out_shape=jax.Shape...  1.74 us
    pallas_call x1, Pallas kernels, turned(): pl.pallas_call(turn_kernel, out_shape=jax.ShapeDtypeStruct((depth, CORES...  1.67 us
  transfers between devices with their start and end apart: 18, of which 6 were waited for; matrix products, arithmetic and copies ran while one was open for 0% of the time, Pallas kernels for 13%

profile of v32, /device:TPU:0, one launch (start us, length us, event | category | flops | bytes accessed | tf_op | source)
XLA Modules:
  0.0 66.7 jit_solution(9840877784287980210)
XLA Ops:
  0.0 0.5 collective-permute-start.2
  0.5 4.5 %collective-permute-start = (bf16[64,2048]{1,0:T(8,128)(2,1)}, bf16[64,2048]{1,0:T(8,128)(2,1)S(1)}, u32[]{:S(2)}, u32[]{:S(2)}) collective-permute-start(bf16[64,2048]{1,0:T(8,128)(2,1)} %bitcast.15), channel_id=1, source_target_pairs={{0,24},{1,25},{2,26},{3,27},{4,28},{5,29},{6,30},{7,31},{8,16},{9,... | collective-permute-start | bytes 786440 | tf_op jit(solution)/shard_map/ppermute | solution.py:33
  5.0 0.5 collective-permute-start.6
  5.5 0.0 copy-start
  5.5 0.7 %copy-done = s32[1,64,8]{1,2,0:T(8,128)S(1)} copy-done((s32[1,64,8]{1,2,0:T(8,128)S(1)}, s32[1,64,8]{1,2,0:T(8,128)}, u32[]{:S(2)}) %copy-start) | copy-done | bytes 2072
  6.2 0.0 copy-start.2
  6.2 0.7 %copy-done.2 = bf16[1,64,8]{1,2,0:T(8,128)(2,1)S(1)} copy-done((bf16[1,64,8]{1,2,0:T(8,128)(2,1)S(1)}, bf16[1,64,8]{1,2,0:T(8,128)(2,1)}, u32[]{:S(2)}) %copy-start.2) | copy-done | bytes 1048
  6.9 0.1 shard_map.46.columns
  7.0 0.2 collective-permute-start.1
  7.1 1.8 %collective-permute-start.3 = (bf16[64,128]{1,0:T(8,128)(2,1)S(1)}, bf16[64,128]{1,0:T(8,128)(2,1)S(1)}, u32[]{:S(2)}, u32[]{:S(2)}) collective-permute-start(bf16[64,128]{1,0:T(8,128)(2,1)S(1)} %shard_map.46.columns), channel_id=1, source_target_pairs={{0,4},{1,5},{2,6},{3,7},{4,0},{5,1},{6,2},{7,3},{8,12},{9,13},{10,... | collective-permute-start | bytes 49160 | tf_op jit(solution)/shard_map/ppermute | solution.py:23
  8.9 0.0 collective-permute-done.2.other
  8.9 1.4 %collective-permute-start.8 = (bf16[64,2048]{1,0:T(8,128)(2,1)}, bf16[64,2048]{1,0:T(8,128)(2,1)S(1)}, u32[]{:S(2)}, u32[]{:S(2)}) collective-permute-start(bf16[64,2048]{1,0:T(8,128)(2,1)} %bitcast.17), channel_id=1, source_target_pairs={{0,20},{1,21},{2,22},{3,23},{4,16},{5,17},{6,18},{7,19},{8,28},{9,... | collective-permute-start | bytes 786440 | tf_op jit(solution)/shard_map/ppermute | solution.py:33
  10.3 0.0 copy-start.3
  10.3 1.9 %copy-done.3 = bf16[1,1,768,2048]{3,2,1,0:T(8,128)(2,1)S(1)} copy-done((bf16[1,1,768,2048]{3,2,1,0:T(8,128)(2,1)S(1)}, bf16[1,1,768,2048]{3,2,1,0:T(8,128)(2,1)}, u32[]{:S(2)}) %copy-start.3) | copy-done | bytes 3145752
  12.2 1.7 %shard_map.47.weights = bf16[2048,1536]{1,0:T(8,128)(2,1)S(1)} custom-call(bf16[768,2048]{1,0:T(8,128)(2,1)S(1)} %bitcast.14, bf16[768,2048]{1,0:T(8,128)(2,1)S(1)} %collective-permute-done.2.other), custom_call_target="tpu_custom_call" | custom-call | flops 12884901888 | tf_op jit(solution)/shard_map/pallas_call | solution.py:77
  13.9 0.0 collective-permute-done.3.columns
  13.9 4.7 %collective-permute-done.1.columns = bf16[64,128]{1,0:T(8,128)(2,1)S(1)} collective-permute-done((bf16[64,128]{1,0:T(8,128)(2,1)S(1)}, bf16[64,128]{1,0:T(8,128)(2,1)S(1)}, u32[]{:S(2)}, u32[]{:S(2)}) %collective-permute-start.1) | collective-permute-done | bytes 16416 | tf_op jit(solution)/shard_map/ppermute | solution.py:23
  18.7 0.0 collective-permute-done.rows
  18.7 0.7 %collective-permute-start.7 = (bf16[64,2176]{1,0:T(8,128)(2,1)S(1)}, bf16[64,2176]{1,0:T(8,128)(2,1)S(1)}, u32[]{:S(2)}, u32[]{:S(2)}) collective-permute-start(bf16[64,2176]{1,0:T(8,128)(2,1)S(1)} %shard_map.48.refs_0_), channel_id=1, source_target_pairs={{0,4},{1,5},{2,6},{3,7},{4,0},{5,1},{6,2},{7,3},{8,12},{9,13},{10,... | collective-permute-start | bytes 835592 | tf_op jit(solution)/shard_map/ppermute | solution.py:23
  19.4 1.5 %collective-permute-start.4 = (bf16[64,2176]{1,0:T(8,128)(2,1)S(1)}, bf16[64,2176]{1,0:T(8,128)(2,1)S(1)}, u32[]{:S(2)}, u32[]{:S(2)}) collective-permute-start(bf16[64,2176]{1,0:T(8,128)(2,1)S(1)} %shard_map.48.refs_0_), channel_id=1, source_target_pairs={{0,2},{1,3},{2,0},{3,1},{4,6},{5,7},{6,4},{7,5},{8,10},{9,11},{10,... | collective-permute-start | bytes 835592 | tf_op jit(solution)/shard_map/ppermute | solution.py:23
  20.9 1.2 %shard_map.49 = bf16[2,64,768]{2,1,0:T(8,128)(2,1)S(1)} custom-call(bf16[2048,1536]{1,0:T(8,128)(2,1)S(1)} %shard_map.47.weights, bf16[64,2176]{1,0:T(8,128)(2,1)S(1)} %shard_map.48.refs_0_), custom_call_target="tpu_custom_call" | custom-call | flops 4026531840 | bytes 6750208 | tf_op jit(solution)/shard_map/pallas_call | solution.py:109
  22.1 3.5 %collective-permute-start.5 = (bf16[2,64,768]{2,1,0:T(8,128)(2,1)S(1)}, bf16[2,64,768]{2,1,0:T(8,128)(2,1)S(1)}, u32[]{:S(2)}, u32[]{:S(2)}) collective-permute-start(bf16[2,64,768]{2,1,0:T(8,128)(2,1)S(1)} %shard_map.49), channel_id=1, source_target_pairs={{0,8},{1,9},{2,10},{3,11},{4,12},{5,13},{6,14},{7,15},{8,0},{9,1},... | collective-permute-start | bytes 589832 | tf_op jit(solution)/shard_map/ppermute | solution.py:23
  25.6 0.0 collective-permute-done.8.rows
  25.6 0.6 collective-permute-start.10
  26.2 5.6 %collective-permute-done.7.refs_0_ = bf16[64,2176]{1,0:T(8,128)(2,1)S(1)} collective-permute-done((bf16[64,2176]{1,0:T(8,128)(2,1)S(1)}, bf16[64,2176]{1,0:T(8,128)(2,1)S(1)}, u32[]{:S(2)}, u32[]{:S(2)}) %collective-permute-start.7) | collective-permute-done | bytes 278560 | tf_op jit(solution)/shard_map/ppermute | solution.py:23
  31.8 2.4 %collective-permute-start.11 = (bf16[64,2176]{1,0:T(8,128)(2,1)S(1)}, bf16[64,2176]{1,0:T(8,128)(2,1)S(1)}, u32[]{:S(2)}, u32[]{:S(2)}) collective-permute-start(bf16[64,2176]{1,0:T(8,128)(2,1)S(1)} %collective-permute-done.7.refs_0_), channel_id=1, source_target_pairs={{0,2},{1,3},{2,0},{3,1},{4,6},{5,7},{6,4},{7,5},{8,10},{9,11},{10,... | collective-permute-start | bytes 835592 | tf_op jit(solution)/shard_map/ppermute | solution.py:23
  34.3 1.2 %shard_map.51 = bf16[2,64,768]{2,1,0:T(8,128)(2,1)S(1)} custom-call(bf16[2048,1536]{1,0:T(8,128)(2,1)S(1)} %shard_map.47.weights, bf16[64,2176]{1,0:T(8,128)(2,1)S(1)} %collective-permute-done.7.refs_0_), custom_call_target="tpu_custom_call" | custom-call | flops 4026531840 | bytes 6750208 | tf_op jit(solution)/shard_map/pallas_call | solution.py:109
  35.5 0.0 collective-permute-done.6.rows
  35.5 3.8 %collective-permute-start.16 = (bf16[2,64,768]{2,1,0:T(8,128)(2,1)S(1)}, bf16[2,64,768]{2,1,0:T(8,128)(2,1)S(1)}, u32[]{:S(2)}, u32[]{:S(2)}) collective-permute-start(bf16[2,64,768]{2,1,0:T(8,128)(2,1)S(1)} %shard_map.51), channel_id=1, source_target_pairs={{0,12},{1,13},{2,14},{3,15},{4,8},{5,9},{6,10},{7,11},{8,4},{9,5},... | collective-permute-start | bytes 589832 | tf_op jit(solution)/shard_map/ppermute | solution.py:23
  39.3 0.0 collective-permute-done.5.refs_1_
  39.3 0.0 collective-permute-done.4.refs_0_
  39.3 0.1 collective-permute-start.9
  39.4 1.2 %shard_map.53 = bf16[2,64,768]{2,1,0:T(8,128)(2,1)S(1)} custom-call(bf16[2048,1536]{1,0:T(8,128)(2,1)S(1)} %shard_map.47.weights, bf16[64,2176]{1,0:T(8,128)(2,1)S(1)} %collective-permute-done.4.refs_0_), custom_call_target="tpu_custom_call" | custom-call | flops 4026531840 | bytes 6750208 | tf_op jit(solution)/shard_map/pallas_call | solution.py:109
  40.6 0.1 collective-permute-start.15
  40.6 0.7 %collective-permute-done.11.refs_0_ = bf16[64,2176]{1,0:T(8,128)(2,1)S(1)} collective-permute-done((bf16[64,2176]{1,0:T(8,128)(2,1)S(1)}, bf16[64,2176]{1,0:T(8,128)(2,1)S(1)}, u32[]{:S(2)}, u32[]{:S(2)}) %collective-permute-start.11) | collective-permute-done | bytes 278560 | tf_op jit(solution)/shard_map/ppermute | solution.py:23
  41.4 1.2 %shard_map.54 = bf16[2,64,768]{2,1,0:T(8,128)(2,1)S(1)} custom-call(bf16[2048,1536]{1,0:T(8,128)(2,1)S(1)} %shard_map.47.weights, bf16[64,2176]{1,0:T(8,128)(2,1)S(1)} %collective-permute-done.11.refs_0_), custom_call_target="tpu_custom_call" | custom-call | flops 4026531840 | bytes 6750208 | tf_op jit(solution)/shard_map/pallas_call | solution.py:109
  42.6 5.5 %collective-permute-start.17 = (bf16[2,64,768]{2,1,0:T(8,128)(2,1)S(1)}, bf16[2,64,768]{2,1,0:T(8,128)(2,1)S(1)}, u32[]{:S(2)}, u32[]{:S(2)}) collective-permute-start(bf16[2,64,768]{2,1,0:T(8,128)(2,1)S(1)} %shard_map.54), channel_id=1, source_target_pairs={{0,14},{1,15},{2,12},{3,13},{4,10},{5,11},{6,8},{7,9},{8,6},{9,7},... | collective-permute-start | bytes 589832 | tf_op jit(solution)/shard_map/ppermute | solution.py:23
  48.0 0.0 collective-permute-done.10.refs_1_
  48.0 1.0 %shard_map.55 = (bf16[2,64,768]{2,1,0:T(8,128)(2,1)S(1)}, bf16[2,64,768]{2,1,0:T(8,128)(2,1)S(1)}) custom-call(bf16[2048,1536]{1,0:T(8,128)(2,1)S(1)} %shard_map.47.weights, bf16[64,2176]{1,0:T(8,128)(2,1)S(1)} %shard_map.50.refs_0_, bf16[64,2176]{1,0:T(8,128)(2,1)S(1)} %collective-permute-done.10.refs_1_), custom_call_target="tpu_custom_call" | custom-call | flops 8053063680 | bytes 7208960 | tf_op jit(solution)/shard_map/pallas_call | solution.py:109
  49.0 0.0 collective-permute-done.9.refs_0_
  49.0 0.0 copy-start.1
  49.0 1.0 %shard_map.56 = (bf16[2,64,768]{2,1,0:T(8,128)(2,1)S(1)}, bf16[2,64,768]{2,1,0:T(8,128)(2,1)S(1)}) custom-call(bf16[2048,1536]{1,0:T(8,128)(2,1)S(1)} %shard_map.47.weights, bf16[64,2176]{1,0:T(8,128)(2,1)S(1)} %collective-permute-done.9.refs_0_, bf16[64,2176]{1,0:T(8,128)(2,1)S(1)} %shard_map.52.refs_1_), custom_call_target="tpu_custom_call" | custom-call | flops 8053063680 | bytes 7208960 | tf_op jit(solution)/shard_map/pallas_call | solution.py:109
  50.0 0.3 collective-permute-start.12
  50.3 3.1 %collective-permute-start.13 = (bf16[2,64,768]{2,1,0:T(8,128)(2,1)S(1)}, bf16[2,64,768]{2,1,0:T(8,128)(2,1)S(1)}, u32[]{:S(2)}, u32[]{:S(2)}) collective-permute-start(bf16[2,64,768]{2,1,0:T(8,128)(2,1)S(1)} %get-tuple-element.44), channel_id=1, source_target_pairs={{0,4},{1,5},{2,6},{3,7},{4,0},{5,1},{6,2},{7,3},{8,12},{9,13},{10,... | collective-permute-start | bytes 589832 | tf_op jit(solution)/shard_map/ppermute | solution.py:23
  53.4 5.4 %collective-permute-done.15.refs_2_ = bf16[2,64,768]{2,1,0:T(8,128)(2,1)S(1)} collective-permute-done((bf16[2,64,768]{2,1,0:T(8,128)(2,1)S(1)}, bf16[2,64,768]{2,1,0:T(8,128)(2,1)S(1)}, u32[]{:S(2)}, u32[]{:S(2)}) %collective-permute-start.15) | collective-permute-done | bytes 196640 | tf_op jit(solution)/shard_map/ppermute | solution.py:23
  58.8 0.0 collective-permute-start.14
  58.8 0.0 collective-permute-done.16.refs_3_
  58.8 0.0 collective-permute-done.17.refs_4_
  58.8 0.0 copy-done.1
  58.8 0.4 shard_map.57.refs_3_
  59.3 0.0 collective-permute-done.12.refs_0_
  59.3 2.2 %collective-permute-done.13.refs_1_ = bf16[2,64,768]{2,1,0:T(8,128)(2,1)S(1)} collective-permute-done((bf16[2,64,768]{2,1,0:T(8,128)(2,1)S(1)}, bf16[2,64,768]{2,1,0:T(8,128)(2,1)S(1)}, u32[]{:S(2)}, u32[]{:S(2)}) %collective-permute-start.13) | collective-permute-done | bytes 196640 | tf_op jit(solution)/shard_map/ppermute | solution.py:23
  61.5 3.9 %collective-permute-done.14.refs_2_ = bf16[2,64,768]{2,1,0:T(8,128)(2,1)S(1)} collective-permute-done((bf16[2,64,768]{2,1,0:T(8,128)(2,1)S(1)}, bf16[2,64,768]{2,1,0:T(8,128)(2,1)S(1)}, u32[]{:S(2)}, u32[]{:S(2)}) %collective-permute-start.14) | collective-permute-done | bytes 196640 | tf_op jit(solution)/shard_map/ppermute | solution.py:23
  65.4 1.3 %shard_map.58 = bf16[512,768]{1,0:T(8,128)(2,1)} custom-call(s32[8,64]{1,0:T(8,128)S(1)} %bitcast.11, bf16[2,64,768]{2,1,0:T(8,128)(2,1)S(1)} %collective-permute-done.12.refs_0_, bf16[2,64,768]{2,1,0:T(8,128)(2,1)S(1)} %collective-permute-done.13.refs_1_, bf16[2,64,768]{2,1,0:T(8,128)(2,1)S(1)} %collective-permute-done.14.refs_2_, ...), custom_call_target="tpu_custom_call" | custom-call | tf_op jit(solution)/shard_map/pallas_call | solution.py:150
  (3 shorter events, 0.1 us)
Async XLA Ops:
  0.0 8.9 %collective-permute-start.2 = (bf16[768,2048]{1,0:T(8,128)(2,1)}, bf16[768,2048]{1,0:T(8,128)(2,1)S(1)}, u32[]{:S(2)}, u32[]{:S(2)}) collective-permute-start(bf16[768,2048]{1,0:T(8,128)(2,1)} %bitcast.13), channel_id=1, source_target_pairs={{0,1},{1,0},{2,3},{3,2},{4,5},{5,4},{6,7},{7,6},{8,9},{9,8},{10,11... | collective-permute-start | bytes 9437192 | tf_op jit(solution)/shard_map/ppermute | solution.py:23
  0.5 18.2 %collective-permute-start = (bf16[64,2048]{1,0:T(8,128)(2,1)}, bf16[64,2048]{1,0:T(8,128)(2,1)S(1)}, u32[]{:S(2)}, u32[]{:S(2)}) collective-permute-start(bf16[64,2048]{1,0:T(8,128)(2,1)} %bitcast.15), channel_id=1, source_target_pairs={{0,24},{1,25},{2,26},{3,27},{4,28},{5,29},{6,30},{7,31},{8,16},{9,... | collective-permute-start | bytes 786440 | tf_op jit(solution)/shard_map/ppermute | solution.py:33
  5.0 30.5 %collective-permute-start.6 = (bf16[64,2048]{1,0:T(8,128)(2,1)}, bf16[64,2048]{1,0:T(8,128)(2,1)S(1)}, u32[]{:S(2)}, u32[]{:S(2)}) collective-permute-start(bf16[64,2048]{1,0:T(8,128)(2,1)} %bitcast.16), channel_id=1, source_target_pairs={{0,16},{1,17},{2,18},{3,19},{4,20},{5,21},{6,22},{7,23},{8,24},{9,... | collective-permute-start | bytes 786440 | tf_op jit(solution)/shard_map/ppermute | solution.py:33
  5.5 0.7 %copy-start = (s32[1,64,8]{1,2,0:T(8,128)S(1)}, s32[1,64,8]{1,2,0:T(8,128)}, u32[]{:S(2)}) copy-start(s32[1,64,8]{1,2,0:T(8,128)} %param.5) | copy-start | bytes 6148
  6.2 0.7 %copy-start.2 = (bf16[1,64,8]{1,2,0:T(8,128)(2,1)S(1)}, bf16[1,64,8]{1,2,0:T(8,128)(2,1)}, u32[]{:S(2)}) copy-start(bf16[1,64,8]{1,2,0:T(8,128)(2,1)} %param.6) | copy-start | bytes 3076
  7.0 11.7 %collective-permute-start.1 = (bf16[64,128]{1,0:T(8,128)(2,1)S(1)}, bf16[64,128]{1,0:T(8,128)(2,1)S(1)}, u32[]{:S(2)}, u32[]{:S(2)}) collective-permute-start(bf16[64,128]{1,0:T(8,128)(2,1)S(1)} %shard_map.46.columns), channel_id=1, source_target_pairs={{0,8},{1,9},{2,10},{3,11},{4,12},{5,13},{6,14},{7,15},{8,0},{9,1},... | collective-permute-start | bytes 49160 | tf_op jit(solution)/shard_map/ppermute | solution.py:23
  7.1 6.8 %collective-permute-start.3 = (bf16[64,128]{1,0:T(8,128)(2,1)S(1)}, bf16[64,128]{1,0:T(8,128)(2,1)S(1)}, u32[]{:S(2)}, u32[]{:S(2)}) collective-permute-start(bf16[64,128]{1,0:T(8,128)(2,1)S(1)} %shard_map.46.columns), channel_id=1, source_target_pairs={{0,4},{1,5},{2,6},{3,7},{4,0},{5,1},{6,2},{7,3},{8,12},{9,13},{10,... | collective-permute-start | bytes 49160 | tf_op jit(solution)/shard_map/ppermute | solution.py:23
  8.9 16.6 %collective-permute-start.8 = (bf16[64,2048]{1,0:T(8,128)(2,1)}, bf16[64,2048]{1,0:T(8,128)(2,1)S(1)}, u32[]{:S(2)}, u32[]{:S(2)}) collective-permute-start(bf16[64,2048]{1,0:T(8,128)(2,1)} %bitcast.17), channel_id=1, source_target_pairs={{0,20},{1,21},{2,22},{3,23},{4,16},{5,17},{6,18},{7,19},{8,28},{9,... | collective-permute-start | bytes 786440 | tf_op jit(solution)/shard_map/ppermute | solution.py:33
  10.3 1.9 %copy-start.3 = (bf16[1,1,768,2048]{3,2,1,0:T(8,128)(2,1)S(1)}, bf16[1,1,768,2048]{3,2,1,0:T(8,128)(2,1)}, u32[]{:S(2)}) copy-start(bf16[1,1,768,2048]{3,2,1,0:T(8,128)(2,1)} %param.7) | copy-start | bytes 9437188
  18.7 13.1 %collective-permute-start.7 = (bf16[64,2176]{1,0:T(8,128)(2,1)S(1)}, bf16[64,2176]{1,0:T(8,128)(2,1)S(1)}, u32[]{:S(2)}, u32[]{:S(2)}) collective-permute-start(bf16[64,2176]{1,0:T(8,128)(2,1)S(1)} %shard_map.48.refs_0_), channel_id=1, source_target_pairs={{0,4},{1,5},{2,6},{3,7},{4,0},{5,1},{6,2},{7,3},{8,12},{9,13},{10,... | collective-permute-start | bytes 835592 | tf_op jit(solution)/shard_map/ppermute | solution.py:23
  19.4 19.9 %collective-permute-start.4 = (bf16[64,2176]{1,0:T(8,128)(2,1)S(1)}, bf16[64,2176]{1,0:T(8,128)(2,1)S(1)}, u32[]{:S(2)}, u32[]{:S(2)}) collective-permute-start(bf16[64,2176]{1,0:T(8,128)(2,1)S(1)} %shard_map.48.refs_0_), channel_id=1, source_target_pairs={{0,2},{1,3},{2,0},{3,1},{4,6},{5,7},{6,4},{7,5},{8,10},{9,11},{10,... | collective-permute-start | bytes 835592 | tf_op jit(solution)/shard_map/ppermute | solution.py:23
  22.1 17.2 %collective-permute-start.5 = (bf16[2,64,768]{2,1,0:T(8,128)(2,1)S(1)}, bf16[2,64,768]{2,1,0:T(8,128)(2,1)S(1)}, u32[]{:S(2)}, u32[]{:S(2)}) collective-permute-start(bf16[2,64,768]{2,1,0:T(8,128)(2,1)S(1)} %shard_map.49), channel_id=1, source_target_pairs={{0,8},{1,9},{2,10},{3,11},{4,12},{5,13},{6,14},{7,15},{8,0},{9,1},... | collective-permute-start | bytes 589832 | tf_op jit(solution)/shard_map/ppermute | solution.py:23
  25.6 22.4 %collective-permute-start.10 = (bf16[64,2176]{1,0:T(8,128)(2,1)S(1)}, bf16[64,2176]{1,0:T(8,128)(2,1)S(1)}, u32[]{:S(2)}, u32[]{:S(2)}) collective-permute-start(bf16[64,2176]{1,0:T(8,128)(2,1)S(1)} %shard_map.50.refs_0_), channel_id=1, source_target_pairs={{0,2},{1,3},{2,0},{3,1},{4,6},{5,7},{6,4},{7,5},{8,10},{9,11},{10,... | collective-permute-start | bytes 835592 | tf_op jit(solution)/shard_map/ppermute | solution.py:23
  31.8 9.6 %collective-permute-start.11 = (bf16[64,2176]{1,0:T(8,128)(2,1)S(1)}, bf16[64,2176]{1,0:T(8,128)(2,1)S(1)}, u32[]{:S(2)}, u32[]{:S(2)}) collective-permute-start(bf16[64,2176]{1,0:T(8,128)(2,1)S(1)} %collective-permute-done.7.refs_0_), channel_id=1, source_target_pairs={{0,2},{1,3},{2,0},{3,1},{4,6},{5,7},{6,4},{7,5},{8,10},{9,11},{10,... | collective-permute-start | bytes 835592 | tf_op jit(solution)/shard_map/ppermute | solution.py:23
  35.5 23.4 %collective-permute-start.16 = (bf16[2,64,768]{2,1,0:T(8,128)(2,1)S(1)}, bf16[2,64,768]{2,1,0:T(8,128)(2,1)S(1)}, u32[]{:S(2)}, u32[]{:S(2)}) collective-permute-start(bf16[2,64,768]{2,1,0:T(8,128)(2,1)S(1)} %shard_map.51), channel_id=1, source_target_pairs={{0,12},{1,13},{2,14},{3,15},{4,8},{5,9},{6,10},{7,11},{8,4},{9,5},... | collective-permute-start | bytes 589832 | tf_op jit(solution)/shard_map/ppermute | solution.py:23
  39.3 9.7 %collective-permute-start.9 = (bf16[64,2176]{1,0:T(8,128)(2,1)S(1)}, bf16[64,2176]{1,0:T(8,128)(2,1)S(1)}, u32[]{:S(2)}, u32[]{:S(2)}) collective-permute-start(bf16[64,2176]{1,0:T(8,128)(2,1)S(1)} %shard_map.52.refs_1_), channel_id=1, source_target_pairs={{0,2},{1,3},{2,0},{3,1},{4,6},{5,7},{6,4},{7,5},{8,10},{9,11},{10,... | collective-permute-start | bytes 835592 | tf_op jit(solution)/shard_map/ppermute | solution.py:23
  40.6 18.2 %collective-permute-start.15 = (bf16[2,64,768]{2,1,0:T(8,128)(2,1)S(1)}, bf16[2,64,768]{2,1,0:T(8,128)(2,1)S(1)}, u32[]{:S(2)}, u32[]{:S(2)}) collective-permute-start(bf16[2,64,768]{2,1,0:T(8,128)(2,1)S(1)} %shard_map.53), channel_id=1, source_target_pairs={{0,10},{1,11},{2,8},{3,9},{4,14},{5,15},{6,12},{7,13},{8,2},{9,3},... | collective-permute-start | bytes 589832 | tf_op jit(solution)/shard_map/ppermute | solution.py:23
  42.6 16.3 %collective-permute-start.17 = (bf16[2,64,768]{2,1,0:T(8,128)(2,1)S(1)}, bf16[2,64,768]{2,1,0:T(8,128)(2,1)S(1)}, u32[]{:S(2)}, u32[]{:S(2)}) collective-permute-start(bf16[2,64,768]{2,1,0:T(8,128)(2,1)S(1)} %shard_map.54), channel_id=1, source_target_pairs={{0,14},{1,15},{2,12},{3,13},{4,10},{5,11},{6,8},{7,9},{8,6},{9,7},... | collective-permute-start | bytes 589832 | tf_op jit(solution)/shard_map/ppermute | solution.py:23
  49.0 9.8 %copy-start.1 = (s32[1,64,8]{1,2,0:T(8,128)S(1)}, s32[1,64,8]{1,2,0:T(8,128)}, u32[]{:S(2)}) copy-start(s32[1,64,8]{1,2,0:T(8,128)} %param.5) | copy-start | bytes 6148
  50.0 9.2 %collective-permute-start.12 = (bf16[2,64,768]{2,1,0:T(8,128)(2,1)S(1)}, bf16[2,64,768]{2,1,0:T(8,128)(2,1)S(1)}, u32[]{:S(2)}, u32[]{:S(2)}) collective-permute-start(bf16[2,64,768]{2,1,0:T(8,128)(2,1)S(1)} %get-tuple-element.43), channel_id=1, source_target_pairs={{0,2},{1,3},{2,0},{3,1},{4,6},{5,7},{6,4},{7,5},{8,10},{9,11},{10,... | collective-permute-start | bytes 589832 | tf_op jit(solution)/shard_map/ppermute | solution.py:23
  50.3 11.1 %collective-permute-start.13 = (bf16[2,64,768]{2,1,0:T(8,128)(2,1)S(1)}, bf16[2,64,768]{2,1,0:T(8,128)(2,1)S(1)}, u32[]{:S(2)}, u32[]{:S(2)}) collective-permute-start(bf16[2,64,768]{2,1,0:T(8,128)(2,1)S(1)} %get-tuple-element.44), channel_id=1, source_target_pairs={{0,4},{1,5},{2,6},{3,7},{4,0},{5,1},{6,2},{7,3},{8,12},{9,13},{10,... | collective-permute-start | bytes 589832 | tf_op jit(solution)/shard_map/ppermute | solution.py:23
  58.8 6.6 %collective-permute-start.14 = (bf16[2,64,768]{2,1,0:T(8,128)(2,1)S(1)}, bf16[2,64,768]{2,1,0:T(8,128)(2,1)S(1)}, u32[]{:S(2)}, u32[]{:S(2)}) collective-permute-start(bf16[2,64,768]{2,1,0:T(8,128)(2,1)S(1)} %get-tuple-element.40), channel_id=1, source_target_pairs={{0,6},{1,7},{2,4},{3,5},{4,2},{5,3},{6,0},{7,1},{8,14},{9,15},{10,... | collective-permute-start | bytes 589832 | tf_op jit(solution)/shard_map/ppermute | solution.py:23

commit v33 on v32

--- a/solution.py
+++ b/solution.py
@@ -200,15 +200,16 @@
     side, rows, _ = tie((side, rows, out_near_side))
     out_side, out_own = work(side, rows)
     back_side = send(out_side, owners, X)
-    far_parts = {
-        0: out_own,
+    first_parts = {
+        Z_NEAR: back_near,
+        X ^ Z_NEAR: back_near_side,
         Z_FAR: back_far,
         X ^ Z_FAR: back_far_side,
         Z_NEAR ^ Z_FAR: back_cross,
         X ^ Z_NEAR ^ Z_FAR: back_cross_side,
     }
-    near_parts = {X: back_side, Z_NEAR: back_near, X ^ Z_NEAR: back_near_side}
-    out = pick_routes(route_ids.T, near_parts, pick_routes(route_ids.T, far_parts))
+    last_parts = {0: out_own, X: back_side}
+    out = pick_routes(route_ids.T, last_parts, pick_routes(route_ids.T, first_parts))
     return out.reshape(1, tokens, top, weight_mat.shape[0])
 
 

time: 66.9 us -> 67.8 us (1.013)
  starting transfers between devices: 30.3 us -> 32.2 us
  waiting for transfers between devices: 22.6 us -> 21.7 us
    ppermute x15, starting transfers between devices: 23.9 us -> 25.8 us  [send(): return lax.ppermute(block, 'expert', route)]
    ppermute x15, waiting for transfers between devices: 22.6 us -> 21.7 us  [send(): return lax.ppermute(block, 'expert', route)]
where the time goes in v33:
time: 67.8 us; the launch traced here: 67.6 us
  starting transfers between devices  32.2 us (47%)
  waiting for transfers between devices  21.7 us (32%)
  Pallas kernels  10.3 us (15%)
  local copies, waits for them, and re-layouts  3.26 us (5%)
    ppermute x15, starting transfers between devices, send(): return lax.ppermute(block, 'expert', route)  25.8 us
    ppermute x15, waiting for transfers between devices, send(): return lax.ppermute(block, 'expert', route)  21.7 us
    pallas_call x6, Pallas kernels, products(): pl.pallas_call(functools.partial(products_kernel, len(pieces)), out_shape...  6.72 us
    ppermute x3, starting transfers between devices, send_across(): return lax.ppermute(block, ('pipe', 'expert'), route)  6.45 us
    unnamed x8, local copies, waits for them, and re-layouts  3.26 us
    pallas_call x2, Pallas kernels, pick_routes(): pl.pallas_call(functools.partial(pick_kernel, flips), out_shape=jax.Shape...  1.74 us
    pallas_call x1, Pallas kernels, turned(): pl.pallas_call(turn_kernel, out_shape=jax.ShapeDtypeStruct((depth, CORES...  1.67 us
  transfers between devices with their start and end apart: 18, of which 6 were waited for; matrix products, arithmetic and copies ran while one was open for 0% of the time, Pallas kernels for 13%

profile of v33, /device:TPU:0, one launch (start us, length us, event | category | flops | bytes accessed | tf_op | source)
XLA Modules:
  0.0 67.6 jit_solution(3326039901497430728)
XLA Ops:
  0.0 0.5 collective-permute-start.2
  0.5 4.5 %collective-permute-start = (bf16[64,2048]{1,0:T(8,128)(2,1)}, bf16[64,2048]{1,0:T(8,128)(2,1)S(1)}, u32[]{:S(2)}, u32[]{:S(2)}) collective-permute-start(bf16[64,2048]{1,0:T(8,128)(2,1)} %bitcast.15), channel_id=1, source_target_pairs={{0,24},{1,25},{2,26},{3,27},{4,28},{5,29},{6,30},{7,31},{8,16},{9,... | collective-permute-start | bytes 786440 | tf_op jit(solution)/shard_map/ppermute | solution.py:33
  5.0 0.5 collective-permute-start.6
  5.5 0.0 copy-start
  5.5 0.7 %copy-done = s32[1,64,8]{1,2,0:T(8,128)S(1)} copy-done((s32[1,64,8]{1,2,0:T(8,128)S(1)}, s32[1,64,8]{1,2,0:T(8,128)}, u32[]{:S(2)}) %copy-start) | copy-done | bytes 2072
  6.2 0.0 copy-start.2
  6.2 0.7 %copy-done.2 = bf16[1,64,8]{1,2,0:T(8,128)(2,1)S(1)} copy-done((bf16[1,64,8]{1,2,0:T(8,128)(2,1)S(1)}, bf16[1,64,8]{1,2,0:T(8,128)(2,1)}, u32[]{:S(2)}) %copy-start.2) | copy-done | bytes 1048
  6.9 0.1 shard_map.46.columns
  7.0 0.2 collective-permute-start.1
  7.1 1.8 %collective-permute-start.3 = (bf16[64,128]{1,0:T(8,128)(2,1)S(1)}, bf16[64,128]{1,0:T(8,128)(2,1)S(1)}, u32[]{:S(2)}, u32[]{:S(2)}) collective-permute-start(bf16[64,128]{1,0:T(8,128)(2,1)S(1)} %shard_map.46.columns), channel_id=1, source_target_pairs={{0,4},{1,5},{2,6},{3,7},{4,0},{5,1},{6,2},{7,3},{8,12},{9,13},{10,... | collective-permute-start | bytes 49160 | tf_op jit(solution)/shard_map/ppermute | solution.py:23
  8.9 0.0 collective-permute-done.2.other
  8.9 1.4 %collective-permute-start.8 = (bf16[64,2048]{1,0:T(8,128)(2,1)}, bf16[64,2048]{1,0:T(8,128)(2,1)S(1)}, u32[]{:S(2)}, u32[]{:S(2)}) collective-permute-start(bf16[64,2048]{1,0:T(8,128)(2,1)} %bitcast.17), channel_id=1, source_target_pairs={{0,20},{1,21},{2,22},{3,23},{4,16},{5,17},{6,18},{7,19},{8,28},{9,... | collective-permute-start | bytes 786440 | tf_op jit(solution)/shard_map/ppermute | solution.py:33
  10.3 0.0 copy-start.3
  10.3 1.9 %copy-done.3 = bf16[1,1,768,2048]{3,2,1,0:T(8,128)(2,1)S(1)} copy-done((bf16[1,1,768,2048]{3,2,1,0:T(8,128)(2,1)S(1)}, bf16[1,1,768,2048]{3,2,1,0:T(8,128)(2,1)}, u32[]{:S(2)}) %copy-start.3) | copy-done | bytes 3145752
  12.2 1.7 %shard_map.47.weights = bf16[2048,1536]{1,0:T(8,128)(2,1)S(1)} custom-call(bf16[768,2048]{1,0:T(8,128)(2,1)S(1)} %bitcast.14, bf16[768,2048]{1,0:T(8,128)(2,1)S(1)} %collective-permute-done.2.other), custom_call_target="tpu_custom_call" | custom-call | flops 12884901888 | tf_op jit(solution)/shard_map/pallas_call | solution.py:77
  13.9 0.0 collective-permute-done.3.columns
  13.9 4.7 %collective-permute-done.1.columns = bf16[64,128]{1,0:T(8,128)(2,1)S(1)} collective-permute-done((bf16[64,128]{1,0:T(8,128)(2,1)S(1)}, bf16[64,128]{1,0:T(8,128)(2,1)S(1)}, u32[]{:S(2)}, u32[]{:S(2)}) %collective-permute-start.1) | collective-permute-done | bytes 16416 | tf_op jit(solution)/shard_map/ppermute | solution.py:23
  18.7 0.0 collective-permute-done.rows
  18.7 0.7 %collective-permute-start.7 = (bf16[64,2176]{1,0:T(8,128)(2,1)S(1)}, bf16[64,2176]{1,0:T(8,128)(2,1)S(1)}, u32[]{:S(2)}, u32[]{:S(2)}) collective-permute-start(bf16[64,2176]{1,0:T(8,128)(2,1)S(1)} %shard_map.48.refs_0_), channel_id=1, source_target_pairs={{0,4},{1,5},{2,6},{3,7},{4,0},{5,1},{6,2},{7,3},{8,12},{9,13},{10,... | collective-permute-start | bytes 835592 | tf_op jit(solution)/shard_map/ppermute | solution.py:23
  19.4 1.5 %collective-permute-start.4 = (bf16[64,2176]{1,0:T(8,128)(2,1)S(1)}, bf16[64,2176]{1,0:T(8,128)(2,1)S(1)}, u32[]{:S(2)}, u32[]{:S(2)}) collective-permute-start(bf16[64,2176]{1,0:T(8,128)(2,1)S(1)} %shard_map.48.refs_0_), channel_id=1, source_target_pairs={{0,2},{1,3},{2,0},{3,1},{4,6},{5,7},{6,4},{7,5},{8,10},{9,11},{10,... | collective-permute-start | bytes 835592 | tf_op jit(solution)/shard_map/ppermute | solution.py:23
  20.9 1.2 %shard_map.49 = bf16[2,64,768]{2,1,0:T(8,128)(2,1)S(1)} custom-call(bf16[2048,1536]{1,0:T(8,128)(2,1)S(1)} %shard_map.47.weights, bf16[64,2176]{1,0:T(8,128)(2,1)S(1)} %shard_map.48.refs_0_), custom_call_target="tpu_custom_call" | custom-call | flops 4026531840 | bytes 6750208 | tf_op jit(solution)/shard_map/pallas_call | solution.py:109
  22.1 3.5 %collective-permute-start.5 = (bf16[2,64,768]{2,1,0:T(8,128)(2,1)S(1)}, bf16[2,64,768]{2,1,0:T(8,128)(2,1)S(1)}, u32[]{:S(2)}, u32[]{:S(2)}) collective-permute-start(bf16[2,64,768]{2,1,0:T(8,128)(2,1)S(1)} %shard_map.49), channel_id=1, source_target_pairs={{0,8},{1,9},{2,10},{3,11},{4,12},{5,13},{6,14},{7,15},{8,0},{9,1},... | collective-permute-start | bytes 589832 | tf_op jit(solution)/shard_map/ppermute | solution.py:23
  25.6 0.0 collective-permute-done.8.rows
  25.6 0.6 collective-permute-start.10
  26.2 5.6 %collective-permute-done.7.refs_0_ = bf16[64,2176]{1,0:T(8,128)(2,1)S(1)} collective-permute-done((bf16[64,2176]{1,0:T(8,128)(2,1)S(1)}, bf16[64,2176]{1,0:T(8,128)(2,1)S(1)}, u32[]{:S(2)}, u32[]{:S(2)}) %collective-permute-start.7) | collective-permute-done | bytes 278560 | tf_op jit(solution)/shard_map/ppermute | solution.py:23
  31.8 2.4 %collective-permute-start.11 = (bf16[64,2176]{1,0:T(8,128)(2,1)S(1)}, bf16[64,2176]{1,0:T(8,128)(2,1)S(1)}, u32[]{:S(2)}, u32[]{:S(2)}) collective-permute-start(bf16[64,2176]{1,0:T(8,128)(2,1)S(1)} %collective-permute-done.7.refs_0_), channel_id=1, source_target_pairs={{0,2},{1,3},{2,0},{3,1},{4,6},{5,7},{6,4},{7,5},{8,10},{9,11},{10,... | collective-permute-start | bytes 835592 | tf_op jit(solution)/shard_map/ppermute | solution.py:23
  34.3 1.2 %shard_map.51 = bf16[2,64,768]{2,1,0:T(8,128)(2,1)S(1)} custom-call(bf16[2048,1536]{1,0:T(8,128)(2,1)S(1)} %shard_map.47.weights, bf16[64,2176]{1,0:T(8,128)(2,1)S(1)} %collective-permute-done.7.refs_0_), custom_call_target="tpu_custom_call" | custom-call | flops 4026531840 | bytes 6750208 | tf_op jit(solution)/shard_map/pallas_call | solution.py:109
  35.5 0.0 collective-permute-done.6.rows
  35.5 3.8 %collective-permute-start.16 = (bf16[2,64,768]{2,1,0:T(8,128)(2,1)S(1)}, bf16[2,64,768]{2,1,0:T(8,128)(2,1)S(1)}, u32[]{:S(2)}, u32[]{:S(2)}) collective-permute-start(bf16[2,64,768]{2,1,0:T(8,128)(2,1)S(1)} %shard_map.51), channel_id=1, source_target_pairs={{0,12},{1,13},{2,14},{3,15},{4,8},{5,9},{6,10},{7,11},{8,4},{9,5},... | collective-permute-start | bytes 589832 | tf_op jit(solution)/shard_map/ppermute | solution.py:23
  39.3 0.0 collective-permute-done.5.refs_2_
  39.3 0.0 collective-permute-done.4.refs_0_
  39.3 1.2 %shard_map.53 = bf16[2,64,768]{2,1,0:T(8,128)(2,1)S(1)} custom-call(bf16[2048,1536]{1,0:T(8,128)(2,1)S(1)} %shard_map.47.weights, bf16[64,2176]{1,0:T(8,128)(2,1)S(1)} %collective-permute-done.4.refs_0_), custom_call_target="tpu_custom_call" | custom-call | flops 4026531840 | bytes 6750208 | tf_op jit(solution)/shard_map/pallas_call | solution.py:109
  40.5 0.1 collective-permute-start.15
  40.6 0.1 collective-permute-start.9
  40.6 0.0 collective-permute-done.11.refs_0_
  40.7 1.2 %shard_map.54 = bf16[2,64,768]{2,1,0:T(8,128)(2,1)S(1)} custom-call(bf16[2048,1536]{1,0:T(8,128)(2,1)S(1)} %shard_map.47.weights, bf16[64,2176]{1,0:T(8,128)(2,1)S(1)} %collective-permute-done.11.refs_0_), custom_call_target="tpu_custom_call" | custom-call | flops 4026531840 | bytes 6750208 | tf_op jit(solution)/shard_map/pallas_call | solution.py:109
  41.9 6.0 %collective-permute-start.17 = (bf16[2,64,768]{2,1,0:T(8,128)(2,1)S(1)}, bf16[2,64,768]{2,1,0:T(8,128)(2,1)S(1)}, u32[]{:S(2)}, u32[]{:S(2)}) collective-permute-start(bf16[2,64,768]{2,1,0:T(8,128)(2,1)S(1)} %shard_map.54), channel_id=1, source_target_pairs={{0,14},{1,15},{2,12},{3,13},{4,10},{5,11},{6,8},{7,9},{8,6},{9,7},... | collective-permute-start | bytes 589832 | tf_op jit(solution)/shard_map/ppermute | solution.py:23
  47.9 0.0 collective-permute-done.10.refs_1_
  47.9 1.0 %shard_map.55 = (bf16[2,64,768]{2,1,0:T(8,128)(2,1)S(1)}, bf16[2,64,768]{2,1,0:T(8,128)(2,1)S(1)}) custom-call(bf16[2048,1536]{1,0:T(8,128)(2,1)S(1)} %shard_map.47.weights, bf16[64,2176]{1,0:T(8,128)(2,1)S(1)} %shard_map.50.refs_0_, bf16[64,2176]{1,0:T(8,128)(2,1)S(1)} %collective-permute-done.10.refs_1_), custom_call_target="tpu_custom_call" | custom-call | flops 8053063680 | bytes 7208960 | tf_op jit(solution)/shard_map/pallas_call | solution.py:109
  48.9 1.2 %collective-permute-start.13 = (bf16[2,64,768]{2,1,0:T(8,128)(2,1)S(1)}, bf16[2,64,768]{2,1,0:T(8,128)(2,1)S(1)}, u32[]{:S(2)}, u32[]{:S(2)}) collective-permute-start(bf16[2,64,768]{2,1,0:T(8,128)(2,1)S(1)} %get-tuple-element.45), channel_id=1, source_target_pairs={{0,4},{1,5},{2,6},{3,7},{4,0},{5,1},{6,2},{7,3},{8,12},{9,13},{10,... | collective-permute-start | bytes 589832 | tf_op jit(solution)/shard_map/ppermute | solution.py:23
  50.0 0.4 collective-permute-done.9.refs_0_
  50.4 0.0 copy-start.1
  50.4 1.8 %collective-permute-start.14 = (bf16[2,64,768]{2,1,0:T(8,128)(2,1)S(1)}, bf16[2,64,768]{2,1,0:T(8,128)(2,1)S(1)}, u32[]{:S(2)}, u32[]{:S(2)}) collective-permute-start(bf16[2,64,768]{2,1,0:T(8,128)(2,1)S(1)} %get-tuple-element.40), channel_id=1, source_target_pairs={{0,6},{1,7},{2,4},{3,5},{4,2},{5,3},{6,0},{7,1},{8,14},{9,15},{10,... | collective-permute-start | bytes 589832 | tf_op jit(solution)/shard_map/ppermute | solution.py:23
  52.2 1.0 %shard_map.56 = (bf16[2,64,768]{2,1,0:T(8,128)(2,1)S(1)}, bf16[2,64,768]{2,1,0:T(8,128)(2,1)S(1)}) custom-call(bf16[2048,1536]{1,0:T(8,128)(2,1)S(1)} %shard_map.47.weights, bf16[64,2176]{1,0:T(8,128)(2,1)S(1)} %collective-permute-done.9.refs_0_, bf16[64,2176]{1,0:T(8,128)(2,1)S(1)} %shard_map.52.refs_1_), custom_call_target="tpu_custom_call" | custom-call | flops 8053063680 | bytes 7208960 | tf_op jit(solution)/shard_map/pallas_call | solution.py:109
  53.2 5.8 %collective-permute-done.15.refs_3_ = bf16[2,64,768]{2,1,0:T(8,128)(2,1)S(1)} collective-permute-done((bf16[2,64,768]{2,1,0:T(8,128)(2,1)S(1)}, bf16[2,64,768]{2,1,0:T(8,128)(2,1)S(1)}, u32[]{:S(2)}, u32[]{:S(2)}) %collective-permute-start.15) | collective-permute-done | bytes 196640 | tf_op jit(solution)/shard_map/ppermute | solution.py:23
  59.0 1.7 %collective-permute-start.12 = (bf16[2,64,768]{2,1,0:T(8,128)(2,1)S(1)}, bf16[2,64,768]{2,1,0:T(8,128)(2,1)S(1)}, u32[]{:S(2)}, u32[]{:S(2)}) collective-permute-start(bf16[2,64,768]{2,1,0:T(8,128)(2,1)S(1)} %get-tuple-element.44), channel_id=1, source_target_pairs={{0,2},{1,3},{2,0},{3,1},{4,6},{5,7},{6,4},{7,5},{8,10},{9,11},{10,... | collective-permute-start | bytes 589832 | tf_op jit(solution)/shard_map/ppermute | solution.py:23
  60.7 0.0 collective-permute-done.16.refs_4_
  60.7 0.0 collective-permute-done.13.refs_0_
  60.7 2.4 %collective-permute-done.14.refs_1_ = bf16[2,64,768]{2,1,0:T(8,128)(2,1)S(1)} collective-permute-done((bf16[2,64,768]{2,1,0:T(8,128)(2,1)S(1)}, bf16[2,64,768]{2,1,0:T(8,128)(2,1)S(1)}, u32[]{:S(2)}, u32[]{:S(2)}) %collective-permute-start.14) | collective-permute-done | bytes 196640 | tf_op jit(solution)/shard_map/ppermute | solution.py:23
  63.2 0.0 collective-permute-done.17.refs_5_
  63.2 0.0 copy-done.1
  63.2 0.4 shard_map.57.refs_2_
  63.6 2.7 %collective-permute-done.12.refs_1_ = bf16[2,64,768]{2,1,0:T(8,128)(2,1)S(1)} collective-permute-done((bf16[2,64,768]{2,1,0:T(8,128)(2,1)S(1)}, bf16[2,64,768]{2,1,0:T(8,128)(2,1)S(1)}, u32[]{:S(2)}, u32[]{:S(2)}) %collective-permute-start.12) | collective-permute-done | bytes 196640 | tf_op jit(solution)/shard_map/ppermute | solution.py:23
  66.3 1.3 %shard_map.58 = bf16[512,768]{1,0:T(8,128)(2,1)} custom-call(s32[8,64]{1,0:T(8,128)S(1)} %bitcast.11, bf16[2,64,768]{2,1,0:T(8,128)(2,1)S(1)} %get-tuple-element.43.refs_0_, bf16[2,64,768]{2,1,0:T(8,128)(2,1)S(1)} %collective-permute-done.12.refs_1_, bf16[512,768]{1,0:T(8,128)(2,1)S(1)} %shard_map.57.refs_2_), custom_call_target="tpu_custom_call" | custom-call | tf_op jit(solution)/shard_map/pallas_call | solution.py:150
  (3 shorter events, 0.1 us)
Async XLA Ops:
  0.0 8.9 %collective-permute-start.2 = (bf16[768,2048]{1,0:T(8,128)(2,1)}, bf16[768,2048]{1,0:T(8,128)(2,1)S(1)}, u32[]{:S(2)}, u32[]{:S(2)}) collective-permute-start(bf16[768,2048]{1,0:T(8,128)(2,1)} %bitcast.13), channel_id=1, source_target_pairs={{0,1},{1,0},{2,3},{3,2},{4,5},{5,4},{6,7},{7,6},{8,9},{9,8},{10,11... | collective-permute-start | bytes 9437192 | tf_op jit(solution)/shard_map/ppermute | solution.py:23
  0.5 18.2 %collective-permute-start = (bf16[64,2048]{1,0:T(8,128)(2,1)}, bf16[64,2048]{1,0:T(8,128)(2,1)S(1)}, u32[]{:S(2)}, u32[]{:S(2)}) collective-permute-start(bf16[64,2048]{1,0:T(8,128)(2,1)} %bitcast.15), channel_id=1, source_target_pairs={{0,24},{1,25},{2,26},{3,27},{4,28},{5,29},{6,30},{7,31},{8,16},{9,... | collective-permute-start | bytes 786440 | tf_op jit(solution)/shard_map/ppermute | solution.py:33
  5.0 30.5 %collective-permute-start.6 = (bf16[64,2048]{1,0:T(8,128)(2,1)}, bf16[64,2048]{1,0:T(8,128)(2,1)S(1)}, u32[]{:S(2)}, u32[]{:S(2)}) collective-permute-start(bf16[64,2048]{1,0:T(8,128)(2,1)} %bitcast.16), channel_id=1, source_target_pairs={{0,16},{1,17},{2,18},{3,19},{4,20},{5,21},{6,22},{7,23},{8,24},{9,... | collective-permute-start | bytes 786440 | tf_op jit(solution)/shard_map/ppermute | solution.py:33
  5.5 0.7 %copy-start = (s32[1,64,8]{1,2,0:T(8,128)S(1)}, s32[1,64,8]{1,2,0:T(8,128)}, u32[]{:S(2)}) copy-start(s32[1,64,8]{1,2,0:T(8,128)} %param.5) | copy-start | bytes 6148
  6.2 0.7 %copy-start.2 = (bf16[1,64,8]{1,2,0:T(8,128)(2,1)S(1)}, bf16[1,64,8]{1,2,0:T(8,128)(2,1)}, u32[]{:S(2)}) copy-start(bf16[1,64,8]{1,2,0:T(8,128)(2,1)} %param.6) | copy-start | bytes 3076
  7.0 11.7 %collective-permute-start.1 = (bf16[64,128]{1,0:T(8,128)(2,1)S(1)}, bf16[64,128]{1,0:T(8,128)(2,1)S(1)}, u32[]{:S(2)}, u32[]{:S(2)}) collective-permute-start(bf16[64,128]{1,0:T(8,128)(2,1)S(1)} %shard_map.46.columns), channel_id=1, source_target_pairs={{0,8},{1,9},{2,10},{3,11},{4,12},{5,13},{6,14},{7,15},{8,0},{9,1},... | collective-permute-start | bytes 49160 | tf_op jit(solution)/shard_map/ppermute | solution.py:23
  7.1 6.8 %collective-permute-start.3 = (bf16[64,128]{1,0:T(8,128)(2,1)S(1)}, bf16[64,128]{1,0:T(8,128)(2,1)S(1)}, u32[]{:S(2)}, u32[]{:S(2)}) collective-permute-start(bf16[64,128]{1,0:T(8,128)(2,1)S(1)} %shard_map.46.columns), channel_id=1, source_target_pairs={{0,4},{1,5},{2,6},{3,7},{4,0},{5,1},{6,2},{7,3},{8,12},{9,13},{10,... | collective-permute-start | bytes 49160 | tf_op jit(solution)/shard_map/ppermute | solution.py:23
  8.9 16.6 %collective-permute-start.8 = (bf16[64,2048]{1,0:T(8,128)(2,1)}, bf16[64,2048]{1,0:T(8,128)(2,1)S(1)}, u32[]{:S(2)}, u32[]{:S(2)}) collective-permute-start(bf16[64,2048]{1,0:T(8,128)(2,1)} %bitcast.17), channel_id=1, source_target_pairs={{0,20},{1,21},{2,22},{3,23},{4,16},{5,17},{6,18},{7,19},{8,28},{9,... | collective-permute-start | bytes 786440 | tf_op jit(solution)/shard_map/ppermute | solution.py:33
  10.3 1.9 %copy-start.3 = (bf16[1,1,768,2048]{3,2,1,0:T(8,128)(2,1)S(1)}, bf16[1,1,768,2048]{3,2,1,0:T(8,128)(2,1)}, u32[]{:S(2)}) copy-start(bf16[1,1,768,2048]{3,2,1,0:T(8,128)(2,1)} %param.7) | copy-start | bytes 9437188
  18.7 13.1 %collective-permute-start.7 = (bf16[64,2176]{1,0:T(8,128)(2,1)S(1)}, bf16[64,2176]{1,0:T(8,128)(2,1)S(1)}, u32[]{:S(2)}, u32[]{:S(2)}) collective-permute-start(bf16[64,2176]{1,0:T(8,128)(2,1)S(1)} %shard_map.48.refs_0_), channel_id=1, source_target_pairs={{0,4},{1,5},{2,6},{3,7},{4,0},{5,1},{6,2},{7,3},{8,12},{9,13},{10,... | collective-permute-start | bytes 835592 | tf_op jit(solution)/shard_map/ppermute | solution.py:23
  19.4 19.9 %collective-permute-start.4 = (bf16[64,2176]{1,0:T(8,128)(2,1)S(1)}, bf16[64,2176]{1,0:T(8,128)(2,1)S(1)}, u32[]{:S(2)}, u32[]{:S(2)}) collective-permute-start(bf16[64,2176]{1,0:T(8,128)(2,1)S(1)} %shard_map.48.refs_0_), channel_id=1, source_target_pairs={{0,2},{1,3},{2,0},{3,1},{4,6},{5,7},{6,4},{7,5},{8,10},{9,11},{10,... | collective-permute-start | bytes 835592 | tf_op jit(solution)/shard_map/ppermute | solution.py:23
  22.1 17.2 %collective-permute-start.5 = (bf16[2,64,768]{2,1,0:T(8,128)(2,1)S(1)}, bf16[2,64,768]{2,1,0:T(8,128)(2,1)S(1)}, u32[]{:S(2)}, u32[]{:S(2)}) collective-permute-start(bf16[2,64,768]{2,1,0:T(8,128)(2,1)S(1)} %shard_map.49), channel_id=1, source_target_pairs={{0,8},{1,9},{2,10},{3,11},{4,12},{5,13},{6,14},{7,15},{8,0},{9,1},... | collective-permute-start | bytes 589832 | tf_op jit(solution)/shard_map/ppermute | solution.py:23
  25.6 22.3 %collective-permute-start.10 = (bf16[64,2176]{1,0:T(8,128)(2,1)S(1)}, bf16[64,2176]{1,0:T(8,128)(2,1)S(1)}, u32[]{:S(2)}, u32[]{:S(2)}) collective-permute-start(bf16[64,2176]{1,0:T(8,128)(2,1)S(1)} %shard_map.50.refs_0_), channel_id=1, source_target_pairs={{0,2},{1,3},{2,0},{3,1},{4,6},{5,7},{6,4},{7,5},{8,10},{9,11},{10,... | collective-permute-start | bytes 835592 | tf_op jit(solution)/shard_map/ppermute | solution.py:23
  31.8 8.8 %collective-permute-start.11 = (bf16[64,2176]{1,0:T(8,128)(2,1)S(1)}, bf16[64,2176]{1,0:T(8,128)(2,1)S(1)}, u32[]{:S(2)}, u32[]{:S(2)}) collective-permute-start(bf16[64,2176]{1,0:T(8,128)(2,1)S(1)} %collective-permute-done.7.refs_0_), channel_id=1, source_target_pairs={{0,2},{1,3},{2,0},{3,1},{4,6},{5,7},{6,4},{7,5},{8,10},{9,11},{10,... | collective-permute-start | bytes 835592 | tf_op jit(solution)/shard_map/ppermute | solution.py:23
  35.5 25.3 %collective-permute-start.16 = (bf16[2,64,768]{2,1,0:T(8,128)(2,1)S(1)}, bf16[2,64,768]{2,1,0:T(8,128)(2,1)S(1)}, u32[]{:S(2)}, u32[]{:S(2)}) collective-permute-start(bf16[2,64,768]{2,1,0:T(8,128)(2,1)S(1)} %shard_map.51), channel_id=1, source_target_pairs={{0,12},{1,13},{2,14},{3,15},{4,8},{5,9},{6,10},{7,11},{8,4},{9,5},... | collective-permute-start | bytes 589832 | tf_op jit(solution)/shard_map/ppermute | solution.py:23
  40.5 18.5 %collective-permute-start.15 = (bf16[2,64,768]{2,1,0:T(8,128)(2,1)S(1)}, bf16[2,64,768]{2,1,0:T(8,128)(2,1)S(1)}, u32[]{:S(2)}, u32[]{:S(2)}) collective-permute-start(bf16[2,64,768]{2,1,0:T(8,128)(2,1)S(1)} %shard_map.53), channel_id=1, source_target_pairs={{0,10},{1,11},{2,8},{3,9},{4,14},{5,15},{6,12},{7,13},{8,2},{9,3},... | collective-permute-start | bytes 589832 | tf_op jit(solution)/shard_map/ppermute | solution.py:23
  40.6 9.8 %collective-permute-start.9 = (bf16[64,2176]{1,0:T(8,128)(2,1)S(1)}, bf16[64,2176]{1,0:T(8,128)(2,1)S(1)}, u32[]{:S(2)}, u32[]{:S(2)}) collective-permute-start(bf16[64,2176]{1,0:T(8,128)(2,1)S(1)} %shard_map.52.refs_1_), channel_id=1, source_target_pairs={{0,2},{1,3},{2,0},{3,1},{4,6},{5,7},{6,4},{7,5},{8,10},{9,11},{10,... | collective-permute-start | bytes 835592 | tf_op jit(solution)/shard_map/ppermute | solution.py:23
  41.9 21.3 %collective-permute-start.17 = (bf16[2,64,768]{2,1,0:T(8,128)(2,1)S(1)}, bf16[2,64,768]{2,1,0:T(8,128)(2,1)S(1)}, u32[]{:S(2)}, u32[]{:S(2)}) collective-permute-start(bf16[2,64,768]{2,1,0:T(8,128)(2,1)S(1)} %shard_map.54), channel_id=1, source_target_pairs={{0,14},{1,15},{2,12},{3,13},{4,10},{5,11},{6,8},{7,9},{8,6},{9,7},... | collective-permute-start | bytes 589832 | tf_op jit(solution)/shard_map/ppermute | solution.py:23
  48.9 11.9 %collective-permute-start.13 = (bf16[2,64,768]{2,1,0:T(8,128)(2,1)S(1)}, bf16[2,64,768]{2,1,0:T(8,128)(2,1)S(1)}, u32[]{:S(2)}, u32[]{:S(2)}) collective-permute-start(bf16[2,64,768]{2,1,0:T(8,128)(2,1)S(1)} %get-tuple-element.45), channel_id=1, source_target_pairs={{0,4},{1,5},{2,6},{3,7},{4,0},{5,1},{6,2},{7,3},{8,12},{9,13},{10,... | collective-permute-start | bytes 589832 | tf_op jit(solution)/shard_map/ppermute | solution.py:23
  50.4 12.8 %copy-start.1 = (s32[1,64,8]{1,2,0:T(8,128)S(1)}, s32[1,64,8]{1,2,0:T(8,128)}, u32[]{:S(2)}) copy-start(s32[1,64,8]{1,2,0:T(8,128)} %param.5) | copy-start | bytes 6148
  50.4 12.8 %collective-permute-start.14 = (bf16[2,64,768]{2,1,0:T(8,128)(2,1)S(1)}, bf16[2,64,768]{2,1,0:T(8,128)(2,1)S(1)}, u32[]{:S(2)}, u32[]{:S(2)}) collective-permute-start(bf16[2,64,768]{2,1,0:T(8,128)(2,1)S(1)} %get-tuple-element.40), channel_id=1, source_target_pairs={{0,6},{1,7},{2,4},{3,5},{4,2},{5,3},{6,0},{7,1},{8,14},{9,15},{10,... | collective-permute-start | bytes 589832 | tf_op jit(solution)/shard_map/ppermute | solution.py:23
  59.0 7.3 %collective-permute-start.12 = (bf16[2,64,768]{2,1,0:T(8,128)(2,1)S(1)}, bf16[2,64,768]{2,1,0:T(8,128)(2,1)S(1)}, u32[]{:S(2)}, u32[]{:S(2)}) collective-permute-start(bf16[2,64,768]{2,1,0:T(8,128)(2,1)S(1)} %get-tuple-element.44), channel_id=1, source_target_pairs={{0,2},{1,3},{2,0},{3,1},{4,6},{5,7},{6,4},{7,5},{8,10},{9,11},{10,... | collective-permute-start | bytes 589832 | tf_op jit(solution)/shard_map/ppermute | solution.py:23

commit v34 on v32

--- a/solution.py
+++ b/solution.py
@@ -37,9 +37,9 @@
     top, tokens = ids.shape
     expert = lax.broadcasted_iota(jnp.int32, (LANES, tokens), 0)
     total = jnp.zeros((LANES, tokens), jnp.float32)
+    wide = gates[...].astype(jnp.float32)
     for k in range(top):
-        gate = gates[k : k + 1, :].astype(jnp.float32)
-        total += jnp.where(expert == ids[k : k + 1, :], gate, 0.0)
+        total += jnp.where(expert == ids[k : k + 1, :], wide[k : k + 1, :], 0.0)
     out[...] = total.T.astype(jnp.bfloat16)
 
 

time: 66.9 us -> 66.9 us (level)
  no operation moved by 1% of the time
where the time goes in v34:
time: 66.9 us; the launch traced here: 66.7 us
  starting transfers between devices  30.3 us (45%)
  waiting for transfers between devices  22.6 us (34%)
  Pallas kernels  10.3 us (15%)
  local copies, waits for them, and re-layouts  3.26 us (5%)
    ppermute x15, starting transfers between devices, send(): return lax.ppermute(block, 'expert', route)  23.9 us
    ppermute x15, waiting for transfers between devices, send(): return lax.ppermute(block, 'expert', route)  22.6 us
    pallas_call x6, Pallas kernels, products(): pl.pallas_call(functools.partial(products_kernel, len(pieces)), out_shape...  6.72 us
    ppermute x3, starting transfers between devices, send_across(): return lax.ppermute(block, ('pipe', 'expert'), route)  6.45 us
    unnamed x8, local copies, waits for them, and re-layouts  3.26 us
    pallas_call x2, Pallas kernels, pick_routes(): pl.pallas_call(functools.partial(pick_kernel, flips), out_shape=jax.Shape...  1.74 us
    pallas_call x1, Pallas kernels, turned(): pl.pallas_call(turn_kernel, out_shape=jax.ShapeDtypeStruct((depth, CORES...  1.67 us
  transfers between devices with their start and end apart: 18, of which 6 were waited for; matrix products, arithmetic and copies ran while one was open for 0% of the time, Pallas kernels for 13%

profile of v34, /device:TPU:0, one launch (start us, length us, event | category | flops | bytes accessed | tf_op | source)
XLA Modules:
  0.0 66.7 jit_solution(5613083135032972889)
XLA Ops:
  0.0 0.5 collective-permute-start.2
  0.5 4.5 %collective-permute-start = (bf16[64,2048]{1,0:T(8,128)(2,1)}, bf16[64,2048]{1,0:T(8,128)(2,1)S(1)}, u32[]{:S(2)}, u32[]{:S(2)}) collective-permute-start(bf16[64,2048]{1,0:T(8,128)(2,1)} %bitcast.15), channel_id=1, source_target_pairs={{0,24},{1,25},{2,26},{3,27},{4,28},{5,29},{6,30},{7,31},{8,16},{9,... | collective-permute-start | bytes 786440 | tf_op jit(solution)/shard_map/ppermute | solution.py:33
  5.0 0.5 collective-permute-start.6
  5.5 0.0 copy-start
  5.5 0.7 %copy-done = s32[1,64,8]{1,2,0:T(8,128)S(1)} copy-done((s32[1,64,8]{1,2,0:T(8,128)S(1)}, s32[1,64,8]{1,2,0:T(8,128)}, u32[]{:S(2)}) %copy-start) | copy-done | bytes 2072
  6.2 0.0 copy-start.2
  6.2 0.7 %copy-done.2 = bf16[1,64,8]{1,2,0:T(8,128)(2,1)S(1)} copy-done((bf16[1,64,8]{1,2,0:T(8,128)(2,1)S(1)}, bf16[1,64,8]{1,2,0:T(8,128)(2,1)}, u32[]{:S(2)}) %copy-start.2) | copy-done | bytes 1048
  6.9 0.1 shard_map.46.columns
  7.0 0.2 collective-permute-start.1
  7.2 1.8 %collective-permute-start.3 = (bf16[64,128]{1,0:T(8,128)(2,1)S(1)}, bf16[64,128]{1,0:T(8,128)(2,1)S(1)}, u32[]{:S(2)}, u32[]{:S(2)}) collective-permute-start(bf16[64,128]{1,0:T(8,128)(2,1)S(1)} %shard_map.46.columns), channel_id=1, source_target_pairs={{0,4},{1,5},{2,6},{3,7},{4,0},{5,1},{6,2},{7,3},{8,12},{9,13},{10,... | collective-permute-start | bytes 49160 | tf_op jit(solution)/shard_map/ppermute | solution.py:23
  8.9 0.0 collective-permute-done.2.other
  8.9 1.4 %collective-permute-start.8 = (bf16[64,2048]{1,0:T(8,128)(2,1)}, bf16[64,2048]{1,0:T(8,128)(2,1)S(1)}, u32[]{:S(2)}, u32[]{:S(2)}) collective-permute-start(bf16[64,2048]{1,0:T(8,128)(2,1)} %bitcast.17), channel_id=1, source_target_pairs={{0,20},{1,21},{2,22},{3,23},{4,16},{5,17},{6,18},{7,19},{8,28},{9,... | collective-permute-start | bytes 786440 | tf_op jit(solution)/shard_map/ppermute | solution.py:33
  10.3 0.0 copy-start.3
  10.3 1.9 %copy-done.3 = bf16[1,1,768,2048]{3,2,1,0:T(8,128)(2,1)S(1)} copy-done((bf16[1,1,768,2048]{3,2,1,0:T(8,128)(2,1)S(1)}, bf16[1,1,768,2048]{3,2,1,0:T(8,128)(2,1)}, u32[]{:S(2)}) %copy-start.3) | copy-done | bytes 3145752
  12.2 1.7 %shard_map.47.weights = bf16[2048,1536]{1,0:T(8,128)(2,1)S(1)} custom-call(bf16[768,2048]{1,0:T(8,128)(2,1)S(1)} %bitcast.14, bf16[768,2048]{1,0:T(8,128)(2,1)S(1)} %collective-permute-done.2.other), custom_call_target="tpu_custom_call" | custom-call | flops 12884901888 | tf_op jit(solution)/shard_map/pallas_call | solution.py:77
  13.9 0.0 collective-permute-done.3.columns
  13.9 4.7 %collective-permute-done.1.columns = bf16[64,128]{1,0:T(8,128)(2,1)S(1)} collective-permute-done((bf16[64,128]{1,0:T(8,128)(2,1)S(1)}, bf16[64,128]{1,0:T(8,128)(2,1)S(1)}, u32[]{:S(2)}, u32[]{:S(2)}) %collective-permute-start.1) | collective-permute-done | bytes 16416 | tf_op jit(solution)/shard_map/ppermute | solution.py:23
  18.7 0.0 collective-permute-done.rows
  18.7 0.7 %collective-permute-start.7 = (bf16[64,2176]{1,0:T(8,128)(2,1)S(1)}, bf16[64,2176]{1,0:T(8,128)(2,1)S(1)}, u32[]{:S(2)}, u32[]{:S(2)}) collective-permute-start(bf16[64,2176]{1,0:T(8,128)(2,1)S(1)} %shard_map.48.refs_0_), channel_id=1, source_target_pairs={{0,4},{1,5},{2,6},{3,7},{4,0},{5,1},{6,2},{7,3},{8,12},{9,13},{10,... | collective-permute-start | bytes 835592 | tf_op jit(solution)/shard_map/ppermute | solution.py:23
  19.4 1.5 %collective-permute-start.4 = (bf16[64,2176]{1,0:T(8,128)(2,1)S(1)}, bf16[64,2176]{1,0:T(8,128)(2,1)S(1)}, u32[]{:S(2)}, u32[]{:S(2)}) collective-permute-start(bf16[64,2176]{1,0:T(8,128)(2,1)S(1)} %shard_map.48.refs_0_), channel_id=1, source_target_pairs={{0,2},{1,3},{2,0},{3,1},{4,6},{5,7},{6,4},{7,5},{8,10},{9,11},{10,... | collective-permute-start | bytes 835592 | tf_op jit(solution)/shard_map/ppermute | solution.py:23
  20.9 1.2 %shard_map.49 = bf16[2,64,768]{2,1,0:T(8,128)(2,1)S(1)} custom-call(bf16[2048,1536]{1,0:T(8,128)(2,1)S(1)} %shard_map.47.weights, bf16[64,2176]{1,0:T(8,128)(2,1)S(1)} %shard_map.48.refs_0_), custom_call_target="tpu_custom_call" | custom-call | flops 4026531840 | bytes 6750208 | tf_op jit(solution)/shard_map/pallas_call | solution.py:109
  22.1 3.5 %collective-permute-start.5 = (bf16[2,64,768]{2,1,0:T(8,128)(2,1)S(1)}, bf16[2,64,768]{2,1,0:T(8,128)(2,1)S(1)}, u32[]{:S(2)}, u32[]{:S(2)}) collective-permute-start(bf16[2,64,768]{2,1,0:T(8,128)(2,1)S(1)} %shard_map.49), channel_id=1, source_target_pairs={{0,8},{1,9},{2,10},{3,11},{4,12},{5,13},{6,14},{7,15},{8,0},{9,1},... | collective-permute-start | bytes 589832 | tf_op jit(solution)/shard_map/ppermute | solution.py:23
  25.6 0.0 collective-permute-done.8.rows
  25.6 0.6 collective-permute-start.10
  26.2 5.6 %collective-permute-done.7.refs_0_ = bf16[64,2176]{1,0:T(8,128)(2,1)S(1)} collective-permute-done((bf16[64,2176]{1,0:T(8,128)(2,1)S(1)}, bf16[64,2176]{1,0:T(8,128)(2,1)S(1)}, u32[]{:S(2)}, u32[]{:S(2)}) %collective-permute-start.7) | collective-permute-done | bytes 278560 | tf_op jit(solution)/shard_map/ppermute | solution.py:23
  31.8 2.4 %collective-permute-start.11 = (bf16[64,2176]{1,0:T(8,128)(2,1)S(1)}, bf16[64,2176]{1,0:T(8,128)(2,1)S(1)}, u32[]{:S(2)}, u32[]{:S(2)}) collective-permute-start(bf16[64,2176]{1,0:T(8,128)(2,1)S(1)} %collective-permute-done.7.refs_0_), channel_id=1, source_target_pairs={{0,2},{1,3},{2,0},{3,1},{4,6},{5,7},{6,4},{7,5},{8,10},{9,11},{10,... | collective-permute-start | bytes 835592 | tf_op jit(solution)/shard_map/ppermute | solution.py:23
  34.3 1.2 %shard_map.51 = bf16[2,64,768]{2,1,0:T(8,128)(2,1)S(1)} custom-call(bf16[2048,1536]{1,0:T(8,128)(2,1)S(1)} %shard_map.47.weights, bf16[64,2176]{1,0:T(8,128)(2,1)S(1)} %collective-permute-done.7.refs_0_), custom_call_target="tpu_custom_call" | custom-call | flops 4026531840 | bytes 6750208 | tf_op jit(solution)/shard_map/pallas_call | solution.py:109
  35.5 0.0 collective-permute-done.6.rows
  35.5 3.8 %collective-permute-start.16 = (bf16[2,64,768]{2,1,0:T(8,128)(2,1)S(1)}, bf16[2,64,768]{2,1,0:T(8,128)(2,1)S(1)}, u32[]{:S(2)}, u32[]{:S(2)}) collective-permute-start(bf16[2,64,768]{2,1,0:T(8,128)(2,1)S(1)} %shard_map.51), channel_id=1, source_target_pairs={{0,12},{1,13},{2,14},{3,15},{4,8},{5,9},{6,10},{7,11},{8,4},{9,5},... | collective-permute-start | bytes 589832 | tf_op jit(solution)/shard_map/ppermute | solution.py:23
  39.3 0.0 collective-permute-done.5.refs_1_
  39.3 0.0 collective-permute-done.4.refs_0_
  39.3 0.1 collective-permute-start.9
  39.4 1.2 %shard_map.53 = bf16[2,64,768]{2,1,0:T(8,128)(2,1)S(1)} custom-call(bf16[2048,1536]{1,0:T(8,128)(2,1)S(1)} %shard_map.47.weights, bf16[64,2176]{1,0:T(8,128)(2,1)S(1)} %collective-permute-done.4.refs_0_), custom_call_target="tpu_custom_call" | custom-call | flops 4026531840 | bytes 6750208 | tf_op jit(solution)/shard_map/pallas_call | solution.py:109
  40.6 0.1 collective-permute-start.15
  40.6 0.7 %collective-permute-done.11.refs_0_ = bf16[64,2176]{1,0:T(8,128)(2,1)S(1)} collective-permute-done((bf16[64,2176]{1,0:T(8,128)(2,1)S(1)}, bf16[64,2176]{1,0:T(8,128)(2,1)S(1)}, u32[]{:S(2)}, u32[]{:S(2)}) %collective-permute-start.11) | collective-permute-done | bytes 278560 | tf_op jit(solution)/shard_map/ppermute | solution.py:23
  41.4 1.2 %shard_map.54 = bf16[2,64,768]{2,1,0:T(8,128)(2,1)S(1)} custom-call(bf16[2048,1536]{1,0:T(8,128)(2,1)S(1)} %shard_map.47.weights, bf16[64,2176]{1,0:T(8,128)(2,1)S(1)} %collective-permute-done.11.refs_0_), custom_call_target="tpu_custom_call" | custom-call | flops 4026531840 | bytes 6750208 | tf_op jit(solution)/shard_map/pallas_call | solution.py:109
  42.6 5.5 %collective-permute-start.17 = (bf16[2,64,768]{2,1,0:T(8,128)(2,1)S(1)}, bf16[2,64,768]{2,1,0:T(8,128)(2,1)S(1)}, u32[]{:S(2)}, u32[]{:S(2)}) collective-permute-start(bf16[2,64,768]{2,1,0:T(8,128)(2,1)S(1)} %shard_map.54), channel_id=1, source_target_pairs={{0,14},{1,15},{2,12},{3,13},{4,10},{5,11},{6,8},{7,9},{8,6},{9,7},... | collective-permute-start | bytes 589832 | tf_op jit(solution)/shard_map/ppermute | solution.py:23
  48.0 0.0 collective-permute-done.10.refs_1_
  48.0 1.0 %shard_map.55 = (bf16[2,64,768]{2,1,0:T(8,128)(2,1)S(1)}, bf16[2,64,768]{2,1,0:T(8,128)(2,1)S(1)}) custom-call(bf16[2048,1536]{1,0:T(8,128)(2,1)S(1)} %shard_map.47.weights, bf16[64,2176]{1,0:T(8,128)(2,1)S(1)} %shard_map.50.refs_0_, bf16[64,2176]{1,0:T(8,128)(2,1)S(1)} %collective-permute-done.10.refs_1_), custom_call_target="tpu_custom_call" | custom-call | flops 8053063680 | bytes 7208960 | tf_op jit(solution)/shard_map/pallas_call | solution.py:109
  49.0 0.0 collective-permute-done.9.refs_0_
  49.0 0.0 copy-start.1
  49.0 1.0 %shard_map.56 = (bf16[2,64,768]{2,1,0:T(8,128)(2,1)S(1)}, bf16[2,64,768]{2,1,0:T(8,128)(2,1)S(1)}) custom-call(bf16[2048,1536]{1,0:T(8,128)(2,1)S(1)} %shard_map.47.weights, bf16[64,2176]{1,0:T(8,128)(2,1)S(1)} %collective-permute-done.9.refs_0_, bf16[64,2176]{1,0:T(8,128)(2,1)S(1)} %shard_map.52.refs_1_), custom_call_target="tpu_custom_call" | custom-call | flops 8053063680 | bytes 7208960 | tf_op jit(solution)/shard_map/pallas_call | solution.py:109
  50.0 0.3 collective-permute-start.12
  50.3 3.1 %collective-permute-start.13 = (bf16[2,64,768]{2,1,0:T(8,128)(2,1)S(1)}, bf16[2,64,768]{2,1,0:T(8,128)(2,1)S(1)}, u32[]{:S(2)}, u32[]{:S(2)}) collective-permute-start(bf16[2,64,768]{2,1,0:T(8,128)(2,1)S(1)} %get-tuple-element.44), channel_id=1, source_target_pairs={{0,4},{1,5},{2,6},{3,7},{4,0},{5,1},{6,2},{7,3},{8,12},{9,13},{10,... | collective-permute-start | bytes 589832 | tf_op jit(solution)/shard_map/ppermute | solution.py:23
  53.4 5.4 %collective-permute-done.15.refs_2_ = bf16[2,64,768]{2,1,0:T(8,128)(2,1)S(1)} collective-permute-done((bf16[2,64,768]{2,1,0:T(8,128)(2,1)S(1)}, bf16[2,64,768]{2,1,0:T(8,128)(2,1)S(1)}, u32[]{:S(2)}, u32[]{:S(2)}) %collective-permute-start.15) | collective-permute-done | bytes 196640 | tf_op jit(solution)/shard_map/ppermute | solution.py:23
  58.8 0.0 collective-permute-start.14
  58.8 0.0 collective-permute-done.16.refs_3_
  58.8 0.0 collective-permute-done.17.refs_4_
  58.8 0.0 copy-done.1
  58.8 0.4 shard_map.57.refs_3_
  59.3 0.0 collective-permute-done.12.refs_0_
  59.3 2.2 %collective-permute-done.13.refs_1_ = bf16[2,64,768]{2,1,0:T(8,128)(2,1)S(1)} collective-permute-done((bf16[2,64,768]{2,1,0:T(8,128)(2,1)S(1)}, bf16[2,64,768]{2,1,0:T(8,128)(2,1)S(1)}, u32[]{:S(2)}, u32[]{:S(2)}) %collective-permute-start.13) | collective-permute-done | bytes 196640 | tf_op jit(solution)/shard_map/ppermute | solution.py:23
  61.5 3.9 %collective-permute-done.14.refs_2_ = bf16[2,64,768]{2,1,0:T(8,128)(2,1)S(1)} collective-permute-done((bf16[2,64,768]{2,1,0:T(8,128)(2,1)S(1)}, bf16[2,64,768]{2,1,0:T(8,128)(2,1)S(1)}, u32[]{:S(2)}, u32[]{:S(2)}) %collective-permute-start.14) | collective-permute-done | bytes 196640 | tf_op jit(solution)/shard_map/ppermute | solution.py:23
  65.4 1.3 %shard_map.58 = bf16[512,768]{1,0:T(8,128)(2,1)} custom-call(s32[8,64]{1,0:T(8,128)S(1)} %bitcast.11, bf16[2,64,768]{2,1,0:T(8,128)(2,1)S(1)} %collective-permute-done.12.refs_0_, bf16[2,64,768]{2,1,0:T(8,128)(2,1)S(1)} %collective-permute-done.13.refs_1_, bf16[2,64,768]{2,1,0:T(8,128)(2,1)S(1)} %collective-permute-done.14.refs_2_, ...), custom_call_target="tpu_custom_call" | custom-call | tf_op jit(solution)/shard_map/pallas_call | solution.py:150
  (3 shorter events, 0.1 us)
Async XLA Ops:
  0.0 8.9 %collective-permute-start.2 = (bf16[768,2048]{1,0:T(8,128)(2,1)}, bf16[768,2048]{1,0:T(8,128)(2,1)S(1)}, u32[]{:S(2)}, u32[]{:S(2)}) collective-permute-start(bf16[768,2048]{1,0:T(8,128)(2,1)} %bitcast.13), channel_id=1, source_target_pairs={{0,1},{1,0},{2,3},{3,2},{4,5},{5,4},{6,7},{7,6},{8,9},{9,8},{10,11... | collective-permute-start | bytes 9437192 | tf_op jit(solution)/shard_map/ppermute | solution.py:23
  0.5 18.2 %collective-permute-start = (bf16[64,2048]{1,0:T(8,128)(2,1)}, bf16[64,2048]{1,0:T(8,128)(2,1)S(1)}, u32[]{:S(2)}, u32[]{:S(2)}) collective-permute-start(bf16[64,2048]{1,0:T(8,128)(2,1)} %bitcast.15), channel_id=1, source_target_pairs={{0,24},{1,25},{2,26},{3,27},{4,28},{5,29},{6,30},{7,31},{8,16},{9,... | collective-permute-start | bytes 786440 | tf_op jit(solution)/shard_map/ppermute | solution.py:33
  5.0 30.5 %collective-permute-start.6 = (bf16[64,2048]{1,0:T(8,128)(2,1)}, bf16[64,2048]{1,0:T(8,128)(2,1)S(1)}, u32[]{:S(2)}, u32[]{:S(2)}) collective-permute-start(bf16[64,2048]{1,0:T(8,128)(2,1)} %bitcast.16), channel_id=1, source_target_pairs={{0,16},{1,17},{2,18},{3,19},{4,20},{5,21},{6,22},{7,23},{8,24},{9,... | collective-permute-start | bytes 786440 | tf_op jit(solution)/shard_map/ppermute | solution.py:33
  5.5 0.7 %copy-start = (s32[1,64,8]{1,2,0:T(8,128)S(1)}, s32[1,64,8]{1,2,0:T(8,128)}, u32[]{:S(2)}) copy-start(s32[1,64,8]{1,2,0:T(8,128)} %param.5) | copy-start | bytes 6148
  6.2 0.7 %copy-start.2 = (bf16[1,64,8]{1,2,0:T(8,128)(2,1)S(1)}, bf16[1,64,8]{1,2,0:T(8,128)(2,1)}, u32[]{:S(2)}) copy-start(bf16[1,64,8]{1,2,0:T(8,128)(2,1)} %param.6) | copy-start | bytes 3076
  7.0 11.7 %collective-permute-start.1 = (bf16[64,128]{1,0:T(8,128)(2,1)S(1)}, bf16[64,128]{1,0:T(8,128)(2,1)S(1)}, u32[]{:S(2)}, u32[]{:S(2)}) collective-permute-start(bf16[64,128]{1,0:T(8,128)(2,1)S(1)} %shard_map.46.columns), channel_id=1, source_target_pairs={{0,8},{1,9},{2,10},{3,11},{4,12},{5,13},{6,14},{7,15},{8,0},{9,1},... | collective-permute-start | bytes 49160 | tf_op jit(solution)/shard_map/ppermute | solution.py:23
  7.2 6.8 %collective-permute-start.3 = (bf16[64,128]{1,0:T(8,128)(2,1)S(1)}, bf16[64,128]{1,0:T(8,128)(2,1)S(1)}, u32[]{:S(2)}, u32[]{:S(2)}) collective-permute-start(bf16[64,128]{1,0:T(8,128)(2,1)S(1)} %shard_map.46.columns), channel_id=1, source_target_pairs={{0,4},{1,5},{2,6},{3,7},{4,0},{5,1},{6,2},{7,3},{8,12},{9,13},{10,... | collective-permute-start | bytes 49160 | tf_op jit(solution)/shard_map/ppermute | solution.py:23
  8.9 16.6 %collective-permute-start.8 = (bf16[64,2048]{1,0:T(8,128)(2,1)}, bf16[64,2048]{1,0:T(8,128)(2,1)S(1)}, u32[]{:S(2)}, u32[]{:S(2)}) collective-permute-start(bf16[64,2048]{1,0:T(8,128)(2,1)} %bitcast.17), channel_id=1, source_target_pairs={{0,20},{1,21},{2,22},{3,23},{4,16},{5,17},{6,18},{7,19},{8,28},{9,... | collective-permute-start | bytes 786440 | tf_op jit(solution)/shard_map/ppermute | solution.py:33
  10.3 1.9 %copy-start.3 = (bf16[1,1,768,2048]{3,2,1,0:T(8,128)(2,1)S(1)}, bf16[1,1,768,2048]{3,2,1,0:T(8,128)(2,1)}, u32[]{:S(2)}) copy-start(bf16[1,1,768,2048]{3,2,1,0:T(8,128)(2,1)} %param.7) | copy-start | bytes 9437188
  18.7 13.1 %collective-permute-start.7 = (bf16[64,2176]{1,0:T(8,128)(2,1)S(1)}, bf16[64,2176]{1,0:T(8,128)(2,1)S(1)}, u32[]{:S(2)}, u32[]{:S(2)}) collective-permute-start(bf16[64,2176]{1,0:T(8,128)(2,1)S(1)} %shard_map.48.refs_0_), channel_id=1, source_target_pairs={{0,4},{1,5},{2,6},{3,7},{4,0},{5,1},{6,2},{7,3},{8,12},{9,13},{10,... | collective-permute-start | bytes 835592 | tf_op jit(solution)/shard_map/ppermute | solution.py:23
  19.4 19.9 %collective-permute-start.4 = (bf16[64,2176]{1,0:T(8,128)(2,1)S(1)}, bf16[64,2176]{1,0:T(8,128)(2,1)S(1)}, u32[]{:S(2)}, u32[]{:S(2)}) collective-permute-start(bf16[64,2176]{1,0:T(8,128)(2,1)S(1)} %shard_map.48.refs_0_), channel_id=1, source_target_pairs={{0,2},{1,3},{2,0},{3,1},{4,6},{5,7},{6,4},{7,5},{8,10},{9,11},{10,... | collective-permute-start | bytes 835592 | tf_op jit(solution)/shard_map/ppermute | solution.py:23
  22.1 17.2 %collective-permute-start.5 = (bf16[2,64,768]{2,1,0:T(8,128)(2,1)S(1)}, bf16[2,64,768]{2,1,0:T(8,128)(2,1)S(1)}, u32[]{:S(2)}, u32[]{:S(2)}) collective-permute-start(bf16[2,64,768]{2,1,0:T(8,128)(2,1)S(1)} %shard_map.49), channel_id=1, source_target_pairs={{0,8},{1,9},{2,10},{3,11},{4,12},{5,13},{6,14},{7,15},{8,0},{9,1},... | collective-permute-start | bytes 589832 | tf_op jit(solution)/shard_map/ppermute | solution.py:23
  25.6 22.4 %collective-permute-start.10 = (bf16[64,2176]{1,0:T(8,128)(2,1)S(1)}, bf16[64,2176]{1,0:T(8,128)(2,1)S(1)}, u32[]{:S(2)}, u32[]{:S(2)}) collective-permute-start(bf16[64,2176]{1,0:T(8,128)(2,1)S(1)} %shard_map.50.refs_0_), channel_id=1, source_target_pairs={{0,2},{1,3},{2,0},{3,1},{4,6},{5,7},{6,4},{7,5},{8,10},{9,11},{10,... | collective-permute-start | bytes 835592 | tf_op jit(solution)/shard_map/ppermute | solution.py:23
  31.8 9.6 %collective-permute-start.11 = (bf16[64,2176]{1,0:T(8,128)(2,1)S(1)}, bf16[64,2176]{1,0:T(8,128)(2,1)S(1)}, u32[]{:S(2)}, u32[]{:S(2)}) collective-permute-start(bf16[64,2176]{1,0:T(8,128)(2,1)S(1)} %collective-permute-done.7.refs_0_), channel_id=1, source_target_pairs={{0,2},{1,3},{2,0},{3,1},{4,6},{5,7},{6,4},{7,5},{8,10},{9,11},{10,... | collective-permute-start | bytes 835592 | tf_op jit(solution)/shard_map/ppermute | solution.py:23
  35.5 23.4 %collective-permute-start.16 = (bf16[2,64,768]{2,1,0:T(8,128)(2,1)S(1)}, bf16[2,64,768]{2,1,0:T(8,128)(2,1)S(1)}, u32[]{:S(2)}, u32[]{:S(2)}) collective-permute-start(bf16[2,64,768]{2,1,0:T(8,128)(2,1)S(1)} %shard_map.51), channel_id=1, source_target_pairs={{0,12},{1,13},{2,14},{3,15},{4,8},{5,9},{6,10},{7,11},{8,4},{9,5},... | collective-permute-start | bytes 589832 | tf_op jit(solution)/shard_map/ppermute | solution.py:23
  39.3 9.7 %collective-permute-start.9 = (bf16[64,2176]{1,0:T(8,128)(2,1)S(1)}, bf16[64,2176]{1,0:T(8,128)(2,1)S(1)}, u32[]{:S(2)}, u32[]{:S(2)}) collective-permute-start(bf16[64,2176]{1,0:T(8,128)(2,1)S(1)} %shard_map.52.refs_1_), channel_id=1, source_target_pairs={{0,2},{1,3},{2,0},{3,1},{4,6},{5,7},{6,4},{7,5},{8,10},{9,11},{10,... | collective-permute-start | bytes 835592 | tf_op jit(solution)/shard_map/ppermute | solution.py:23
  40.6 18.2 %collective-permute-start.15 = (bf16[2,64,768]{2,1,0:T(8,128)(2,1)S(1)}, bf16[2,64,768]{2,1,0:T(8,128)(2,1)S(1)}, u32[]{:S(2)}, u32[]{:S(2)}) collective-permute-start(bf16[2,64,768]{2,1,0:T(8,128)(2,1)S(1)} %shard_map.53), channel_id=1, source_target_pairs={{0,10},{1,11},{2,8},{3,9},{4,14},{5,15},{6,12},{7,13},{8,2},{9,3},... | collective-permute-start | bytes 589832 | tf_op jit(solution)/shard_map/ppermute | solution.py:23
  42.6 16.3 %collective-permute-start.17 = (bf16[2,64,768]{2,1,0:T(8,128)(2,1)S(1)}, bf16[2,64,768]{2,1,0:T(8,128)(2,1)S(1)}, u32[]{:S(2)}, u32[]{:S(2)}) collective-permute-start(bf16[2,64,768]{2,1,0:T(8,128)(2,1)S(1)} %shard_map.54), channel_id=1, source_target_pairs={{0,14},{1,15},{2,12},{3,13},{4,10},{5,11},{6,8},{7,9},{8,6},{9,7},... | collective-permute-start | bytes 589832 | tf_op jit(solution)/shard_map/ppermute | solution.py:23
  49.0 9.8 %copy-start.1 = (s32[1,64,8]{1,2,0:T(8,128)S(1)}, s32[1,64,8]{1,2,0:T(8,128)}, u32[]{:S(2)}) copy-start(s32[1,64,8]{1,2,0:T(8,128)} %param.5) | copy-start | bytes 6148
  50.0 9.2 %collective-permute-start.12 = (bf16[2,64,768]{2,1,0:T(8,128)(2,1)S(1)}, bf16[2,64,768]{2,1,0:T(8,128)(2,1)S(1)}, u32[]{:S(2)}, u32[]{:S(2)}) collective-permute-start(bf16[2,64,768]{2,1,0:T(8,128)(2,1)S(1)} %get-tuple-element.43), channel_id=1, source_target_pairs={{0,2},{1,3},{2,0},{3,1},{4,6},{5,7},{6,4},{7,5},{8,10},{9,11},{10,... | collective-permute-start | bytes 589832 | tf_op jit(solution)/shard_map/ppermute | solution.py:23
  50.3 11.1 %collective-permute-start.13 = (bf16[2,64,768]{2,1,0:T(8,128)(2,1)S(1)}, bf16[2,64,768]{2,1,0:T(8,128)(2,1)S(1)}, u32[]{:S(2)}, u32[]{:S(2)}) collective-permute-start(bf16[2,64,768]{2,1,0:T(8,128)(2,1)S(1)} %get-tuple-element.44), channel_id=1, source_target_pairs={{0,4},{1,5},{2,6},{3,7},{4,0},{5,1},{6,2},{7,3},{8,12},{9,13},{10,... | collective-permute-start | bytes 589832 | tf_op jit(solution)/shard_map/ppermute | solution.py:23
  58.8 6.6 %collective-permute-start.14 = (bf16[2,64,768]{2,1,0:T(8,128)(2,1)S(1)}, bf16[2,64,768]{2,1,0:T(8,128)(2,1)S(1)}, u32[]{:S(2)}, u32[]{:S(2)}) collective-permute-start(bf16[2,64,768]{2,1,0:T(8,128)(2,1)S(1)} %get-tuple-element.40), channel_id=1, source_target_pairs={{0,6},{1,7},{2,4},{3,5},{4,2},{5,3},{6,0},{7,1},{8,14},{9,15},{10,... | collective-permute-start | bytes 589832 | tf_op jit(solution)/shard_map/ppermute | solution.py:23

commit v35 on v34

--- a/solution.py
+++ b/solution.py
@@ -193,12 +193,10 @@
     cross_side, _ = tie((cross_side, out_far_side))
     (out_cross_side,) = work(cross_side)
     back_cross_side = send(out_cross_side, owners, X ^ Z_NEAR ^ Z_FAR)
-    near_side, _ = tie((near_side, out_cross_side))
-    out_near, out_near_side = work(near, near_side)
+    near_side, side, rows, _ = tie((near_side, side, rows, out_cross_side))
+    out_near, out_near_side, out_side, out_own = work(near, near_side, side, rows)
     back_near_side = send(out_near_side, owners, X ^ Z_NEAR)
     back_near = send(out_near, owners, Z_NEAR)
-    side, rows, _ = tie((side, rows, out_near_side))
-    out_side, out_own = work(side, rows)
     back_side = send(out_side, owners, X)
     far_parts = {
         0: out_own,

time: 66.9 us -> 66.9 us (level)
  starting transfers between devices: 30.3 us -> 31.3 us
  waiting for transfers between devices: 22.6 us -> 21.8 us
    ppermute x15, starting transfers between devices: 23.9 us -> 24.9 us  [send(): return lax.ppermute(block, 'expert', route)]
    ppermute x15, waiting for transfers between devices: 22.6 us -> 21.8 us  [send(): return lax.ppermute(block, 'expert', route)]
    pallas_call x6 -> x5, Pallas kernels: 6.72 us -> 6.55 us  [products(): pl.pallas_call(functools.partial(products_kernel, len(pieces)), out_shape...]
where the time goes in v35:
time: 66.9 us; the launch traced here: 66.7 us
  starting transfers between devices  31.3 us (47%)
  waiting for transfers between devices  21.8 us (33%)
  Pallas kernels  10.1 us (15%)
  local copies, waits for them, and re-layouts  3.26 us (5%)
    ppermute x15, starting transfers between devices, send(): return lax.ppermute(block, 'expert', route)  24.9 us
    ppermute x15, waiting for transfers between devices, send(): return lax.ppermute(block, 'expert', route)  21.8 us
    pallas_call x5, Pallas kernels, products(): pl.pallas_call(functools.partial(products_kernel, len(pieces)), out_shape...  6.55 us
    ppermute x3, starting transfers between devices, send_across(): return lax.ppermute(block, ('pipe', 'expert'), route)  6.45 us
    unnamed x8, local copies, waits for them, and re-layouts  3.26 us
    pallas_call x2, Pallas kernels, pick_routes(): pl.pallas_call(functools.partial(pick_kernel, flips), out_shape=jax.Shape...  1.74 us
    pallas_call x1, Pallas kernels, turned(): pl.pallas_call(turn_kernel, out_shape=jax.ShapeDtypeStruct((depth, CORES...  1.67 us
  transfers between devices with their start and end apart: 18, of which 6 were waited for; matrix products, arithmetic and copies ran while one was open for 0% of the time, Pallas kernels for 13%

profile of v35, /device:TPU:0, one launch (start us, length us, event | category | flops | bytes accessed | tf_op | source)
XLA Modules:
  0.0 66.7 jit_solution(6687235786532765631)
XLA Ops:
  0.0 0.5 collective-permute-start.2
  0.5 4.5 %collective-permute-start = (bf16[64,2048]{1,0:T(8,128)(2,1)}, bf16[64,2048]{1,0:T(8,128)(2,1)S(1)}, u32[]{:S(2)}, u32[]{:S(2)}) collective-permute-start(bf16[64,2048]{1,0:T(8,128)(2,1)} %bitcast.15), channel_id=1, source_target_pairs={{0,24},{1,25},{2,26},{3,27},{4,28},{5,29},{6,30},{7,31},{8,16},{9,... | collective-permute-start | bytes 786440 | tf_op jit(solution)/shard_map/ppermute | solution.py:33
  5.0 0.5 collective-permute-start.9
  5.5 0.0 copy-start
  5.5 0.7 %copy-done = s32[1,64,8]{1,2,0:T(8,128)S(1)} copy-done((s32[1,64,8]{1,2,0:T(8,128)S(1)}, s32[1,64,8]{1,2,0:T(8,128)}, u32[]{:S(2)}) %copy-start) | copy-done | bytes 2072
  6.2 0.0 copy-start.2
  6.2 0.7 %copy-done.2 = bf16[1,64,8]{1,2,0:T(8,128)(2,1)S(1)} copy-done((bf16[1,64,8]{1,2,0:T(8,128)(2,1)S(1)}, bf16[1,64,8]{1,2,0:T(8,128)(2,1)}, u32[]{:S(2)}) %copy-start.2) | copy-done | bytes 1048
  6.9 0.1 shard_map.46.columns
  7.0 0.2 collective-permute-start.1
  7.2 1.8 %collective-permute-start.3 = (bf16[64,128]{1,0:T(8,128)(2,1)S(1)}, bf16[64,128]{1,0:T(8,128)(2,1)S(1)}, u32[]{:S(2)}, u32[]{:S(2)}) collective-permute-start(bf16[64,128]{1,0:T(8,128)(2,1)S(1)} %shard_map.46.columns), channel_id=1, source_target_pairs={{0,4},{1,5},{2,6},{3,7},{4,0},{5,1},{6,2},{7,3},{8,12},{9,13},{10,... | collective-permute-start | bytes 49160 | tf_op jit(solution)/shard_map/ppermute | solution.py:23
  8.9 0.0 collective-permute-done.2.other
  8.9 1.4 %collective-permute-start.5 = (bf16[64,2048]{1,0:T(8,128)(2,1)}, bf16[64,2048]{1,0:T(8,128)(2,1)S(1)}, u32[]{:S(2)}, u32[]{:S(2)}) collective-permute-start(bf16[64,2048]{1,0:T(8,128)(2,1)} %bitcast.17), channel_id=1, source_target_pairs={{0,20},{1,21},{2,22},{3,23},{4,16},{5,17},{6,18},{7,19},{8,28},{9,... | collective-permute-start | bytes 786440 | tf_op jit(solution)/shard_map/ppermute | solution.py:33
  10.3 0.0 copy-start.3
  10.3 1.9 %copy-done.3 = bf16[1,1,768,2048]{3,2,1,0:T(8,128)(2,1)S(1)} copy-done((bf16[1,1,768,2048]{3,2,1,0:T(8,128)(2,1)S(1)}, bf16[1,1,768,2048]{3,2,1,0:T(8,128)(2,1)}, u32[]{:S(2)}) %copy-start.3) | copy-done | bytes 3145752
  12.2 1.7 %shard_map.47.weights = bf16[2048,1536]{1,0:T(8,128)(2,1)S(1)} custom-call(bf16[768,2048]{1,0:T(8,128)(2,1)S(1)} %bitcast.14, bf16[768,2048]{1,0:T(8,128)(2,1)S(1)} %collective-permute-done.2.other), custom_call_target="tpu_custom_call" | custom-call | flops 12884901888 | tf_op jit(solution)/shard_map/pallas_call | solution.py:77
  13.9 0.0 collective-permute-done.3.columns
  13.9 4.7 %collective-permute-done.1.columns = bf16[64,128]{1,0:T(8,128)(2,1)S(1)} collective-permute-done((bf16[64,128]{1,0:T(8,128)(2,1)S(1)}, bf16[64,128]{1,0:T(8,128)(2,1)S(1)}, u32[]{:S(2)}, u32[]{:S(2)}) %collective-permute-start.1) | collective-permute-done | bytes 16416 | tf_op jit(solution)/shard_map/ppermute | solution.py:23
  18.7 0.0 collective-permute-done.rows
  18.7 0.7 %collective-permute-start.4 = (bf16[64,2176]{1,0:T(8,128)(2,1)S(1)}, bf16[64,2176]{1,0:T(8,128)(2,1)S(1)}, u32[]{:S(2)}, u32[]{:S(2)}) collective-permute-start(bf16[64,2176]{1,0:T(8,128)(2,1)S(1)} %shard_map.48.refs_0_), channel_id=1, source_target_pairs={{0,4},{1,5},{2,6},{3,7},{4,0},{5,1},{6,2},{7,3},{8,12},{9,13},{10,... | collective-permute-start | bytes 835592 | tf_op jit(solution)/shard_map/ppermute | solution.py:23
  19.4 1.5 %collective-permute-start.7 = (bf16[64,2176]{1,0:T(8,128)(2,1)S(1)}, bf16[64,2176]{1,0:T(8,128)(2,1)S(1)}, u32[]{:S(2)}, u32[]{:S(2)}) collective-permute-start(bf16[64,2176]{1,0:T(8,128)(2,1)S(1)} %shard_map.48.refs_0_), channel_id=1, source_target_pairs={{0,2},{1,3},{2,0},{3,1},{4,6},{5,7},{6,4},{7,5},{8,10},{9,11},{10,... | collective-permute-start | bytes 835592 | tf_op jit(solution)/shard_map/ppermute | solution.py:23
  20.9 1.2 %shard_map.49 = bf16[2,64,768]{2,1,0:T(8,128)(2,1)S(1)} custom-call(bf16[2048,1536]{1,0:T(8,128)(2,1)S(1)} %shard_map.47.weights, bf16[64,2176]{1,0:T(8,128)(2,1)S(1)} %shard_map.48.refs_0_), custom_call_target="tpu_custom_call" | custom-call | flops 4026531840 | bytes 6750208 | tf_op jit(solution)/shard_map/pallas_call | solution.py:109
  22.1 3.5 %collective-permute-start.8 = (bf16[2,64,768]{2,1,0:T(8,128)(2,1)S(1)}, bf16[2,64,768]{2,1,0:T(8,128)(2,1)S(1)}, u32[]{:S(2)}, u32[]{:S(2)}) collective-permute-start(bf16[2,64,768]{2,1,0:T(8,128)(2,1)S(1)} %shard_map.49), channel_id=1, source_target_pairs={{0,8},{1,9},{2,10},{3,11},{4,12},{5,13},{6,14},{7,15},{8,0},{9,1},... | collective-permute-start | bytes 589832 | tf_op jit(solution)/shard_map/ppermute | solution.py:23
  25.6 0.0 collective-permute-done.5.rows
  25.6 0.6 collective-permute-start.6
  26.2 5.6 %collective-permute-done.4.refs_0_ = bf16[64,2176]{1,0:T(8,128)(2,1)S(1)} collective-permute-done((bf16[64,2176]{1,0:T(8,128)(2,1)S(1)}, bf16[64,2176]{1,0:T(8,128)(2,1)S(1)}, u32[]{:S(2)}, u32[]{:S(2)}) %collective-permute-start.4) | collective-permute-done | bytes 278560 | tf_op jit(solution)/shard_map/ppermute | solution.py:23
  31.8 2.4 %collective-permute-start.11 = (bf16[64,2176]{1,0:T(8,128)(2,1)S(1)}, bf16[64,2176]{1,0:T(8,128)(2,1)S(1)}, u32[]{:S(2)}, u32[]{:S(2)}) collective-permute-start(bf16[64,2176]{1,0:T(8,128)(2,1)S(1)} %collective-permute-done.4.refs_0_), channel_id=1, source_target_pairs={{0,2},{1,3},{2,0},{3,1},{4,6},{5,7},{6,4},{7,5},{8,10},{9,11},{10,... | collective-permute-start | bytes 835592 | tf_op jit(solution)/shard_map/ppermute | solution.py:23
  34.3 1.2 %shard_map.51 = bf16[2,64,768]{2,1,0:T(8,128)(2,1)S(1)} custom-call(bf16[2048,1536]{1,0:T(8,128)(2,1)S(1)} %shard_map.47.weights, bf16[64,2176]{1,0:T(8,128)(2,1)S(1)} %collective-permute-done.4.refs_0_), custom_call_target="tpu_custom_call" | custom-call | flops 4026531840 | bytes 6750208 | tf_op jit(solution)/shard_map/pallas_call | solution.py:109
  35.5 0.0 collective-permute-done.9.rows
  35.5 3.8 %collective-permute-start.16 = (bf16[2,64,768]{2,1,0:T(8,128)(2,1)S(1)}, bf16[2,64,768]{2,1,0:T(8,128)(2,1)S(1)}, u32[]{:S(2)}, u32[]{:S(2)}) collective-permute-start(bf16[2,64,768]{2,1,0:T(8,128)(2,1)S(1)} %shard_map.51), channel_id=1, source_target_pairs={{0,12},{1,13},{2,14},{3,15},{4,8},{5,9},{6,10},{7,11},{8,4},{9,5},... | collective-permute-start | bytes 589832 | tf_op jit(solution)/shard_map/ppermute | solution.py:23
  39.3 0.0 collective-permute-done.8.refs_1_
  39.3 0.0 collective-permute-done.7.refs_0_
  39.3 0.1 collective-permute-start.10
  39.4 1.2 %shard_map.53 = bf16[2,64,768]{2,1,0:T(8,128)(2,1)S(1)} custom-call(bf16[2048,1536]{1,0:T(8,128)(2,1)S(1)} %shard_map.47.weights, bf16[64,2176]{1,0:T(8,128)(2,1)S(1)} %collective-permute-done.7.refs_0_), custom_call_target="tpu_custom_call" | custom-call | flops 4026531840 | bytes 6750208 | tf_op jit(solution)/shard_map/pallas_call | solution.py:109
  40.6 0.1 collective-permute-start.15
  40.6 0.7 %collective-permute-done.11.refs_0_ = bf16[64,2176]{1,0:T(8,128)(2,1)S(1)} collective-permute-done((bf16[64,2176]{1,0:T(8,128)(2,1)S(1)}, bf16[64,2176]{1,0:T(8,128)(2,1)S(1)}, u32[]{:S(2)}, u32[]{:S(2)}) %collective-permute-start.11) | collective-permute-done | bytes 278560 | tf_op jit(solution)/shard_map/ppermute | solution.py:23
  41.4 1.2 %shard_map.54 = bf16[2,64,768]{2,1,0:T(8,128)(2,1)S(1)} custom-call(bf16[2048,1536]{1,0:T(8,128)(2,1)S(1)} %shard_map.47.weights, bf16[64,2176]{1,0:T(8,128)(2,1)S(1)} %collective-permute-done.11.refs_0_), custom_call_target="tpu_custom_call" | custom-call | flops 4026531840 | bytes 6750208 | tf_op jit(solution)/shard_map/pallas_call | solution.py:109
  42.6 0.0 copy-start.1
  42.6 5.5 %collective-permute-start.17 = (bf16[2,64,768]{2,1,0:T(8,128)(2,1)S(1)}, bf16[2,64,768]{2,1,0:T(8,128)(2,1)S(1)}, u32[]{:S(2)}, u32[]{:S(2)}) collective-permute-start(bf16[2,64,768]{2,1,0:T(8,128)(2,1)S(1)} %shard_map.54), channel_id=1, source_target_pairs={{0,14},{1,15},{2,12},{3,13},{4,10},{5,11},{6,8},{7,9},{8,6},{9,7},... | collective-permute-start | bytes 589832 | tf_op jit(solution)/shard_map/ppermute | solution.py:23
  48.0 0.0 collective-permute-done.6.refs_1_
  48.0 0.0 collective-permute-done.10.refs_2_
  48.1 1.8 %shard_map.55 = (bf16[2,64,768]{2,1,0:T(8,128)(2,1)S(1)}, bf16[2,64,768]{2,1,0:T(8,128)(2,1)S(1)}, bf16[2,64,768]{2,1,0:T(8,128)(2,1)S(1)}, bf16[2,64,768]{2,1,0:T(8,128)(2,1)S(1)}) custom-call(bf16[2048,1536]{1,0:T(8,128)(2,1)S(1)} %shard_map.47.weights, bf16[64,2176]{1,0:T(8,128)(2,1)S(1)} %shard_map.50.refs_0_, ...), custom_call_target="tpu_custom_call" | custom-call | flops 16106127360 | bytes 8126464 | tf_op jit(solution)/shard_map/pallas_call | solution.py:109
  49.8 1.0 %collective-permute-start.12 = (bf16[2,64,768]{2,1,0:T(8,128)(2,1)S(1)}, bf16[2,64,768]{2,1,0:T(8,128)(2,1)S(1)}, u32[]{:S(2)}, u32[]{:S(2)}) collective-permute-start(bf16[2,64,768]{2,1,0:T(8,128)(2,1)S(1)} %get-tuple-element.42), channel_id=1, source_target_pairs={{0,2},{1,3},{2,0},{3,1},{4,6},{5,7},{6,4},{7,5},{8,10},{9,11},{10,... | collective-permute-start | bytes 589832 | tf_op jit(solution)/shard_map/ppermute | solution.py:23
  50.8 3.4 %collective-permute-start.13 = (bf16[2,64,768]{2,1,0:T(8,128)(2,1)S(1)}, bf16[2,64,768]{2,1,0:T(8,128)(2,1)S(1)}, u32[]{:S(2)}, u32[]{:S(2)}) collective-permute-start(bf16[2,64,768]{2,1,0:T(8,128)(2,1)S(1)} %get-tuple-element.43), channel_id=1, source_target_pairs={{0,4},{1,5},{2,6},{3,7},{4,0},{5,1},{6,2},{7,3},{8,12},{9,13},{10,... | collective-permute-start | bytes 589832 | tf_op jit(solution)/shard_map/ppermute | solution.py:23
  54.2 4.6 %collective-permute-done.15.refs_2_ = bf16[2,64,768]{2,1,0:T(8,128)(2,1)S(1)} collective-permute-done((bf16[2,64,768]{2,1,0:T(8,128)(2,1)S(1)}, bf16[2,64,768]{2,1,0:T(8,128)(2,1)S(1)}, u32[]{:S(2)}, u32[]{:S(2)}) %collective-permute-start.15) | collective-permute-done | bytes 196640 | tf_op jit(solution)/shard_map/ppermute | solution.py:23
  58.8 0.0 collective-permute-start.14
  58.8 0.0 collective-permute-done.16.refs_3_
  58.8 0.0 collective-permute-done.17.refs_4_
  58.8 0.0 copy-done.1
  58.8 0.4 shard_map.56.refs_3_
  59.3 0.0 collective-permute-done.12.refs_0_
  59.3 2.5 %collective-permute-done.13.refs_1_ = bf16[2,64,768]{2,1,0:T(8,128)(2,1)S(1)} collective-permute-done((bf16[2,64,768]{2,1,0:T(8,128)(2,1)S(1)}, bf16[2,64,768]{2,1,0:T(8,128)(2,1)S(1)}, u32[]{:S(2)}, u32[]{:S(2)}) %collective-permute-start.13) | collective-permute-done | bytes 196640 | tf_op jit(solution)/shard_map/ppermute | solution.py:23
  61.8 3.6 %collective-permute-done.14.refs_2_ = bf16[2,64,768]{2,1,0:T(8,128)(2,1)S(1)} collective-permute-done((bf16[2,64,768]{2,1,0:T(8,128)(2,1)S(1)}, bf16[2,64,768]{2,1,0:T(8,128)(2,1)S(1)}, u32[]{:S(2)}, u32[]{:S(2)}) %collective-permute-start.14) | collective-permute-done | bytes 196640 | tf_op jit(solution)/shard_map/ppermute | solution.py:23
  65.4 1.3 %shard_map.57 = bf16[512,768]{1,0:T(8,128)(2,1)} custom-call(s32[8,64]{1,0:T(8,128)S(1)} %bitcast.11, bf16[2,64,768]{2,1,0:T(8,128)(2,1)S(1)} %collective-permute-done.12.refs_0_, bf16[2,64,768]{2,1,0:T(8,128)(2,1)S(1)} %collective-permute-done.13.refs_1_, bf16[2,64,768]{2,1,0:T(8,128)(2,1)S(1)} %collective-permute-done.14.refs_2_, ...), custom_call_target="tpu_custom_call" | custom-call | tf_op jit(solution)/shard_map/pallas_call | solution.py:150
  (3 shorter events, 0.1 us)
Async XLA Ops:
  0.0 8.9 %collective-permute-start.2 = (bf16[768,2048]{1,0:T(8,128)(2,1)}, bf16[768,2048]{1,0:T(8,128)(2,1)S(1)}, u32[]{:S(2)}, u32[]{:S(2)}) collective-permute-start(bf16[768,2048]{1,0:T(8,128)(2,1)} %bitcast.13), channel_id=1, source_target_pairs={{0,1},{1,0},{2,3},{3,2},{4,5},{5,4},{6,7},{7,6},{8,9},{9,8},{10,11... | collective-permute-start | bytes 9437192 | tf_op jit(solution)/shard_map/ppermute | solution.py:23
  0.5 18.2 %collective-permute-start = (bf16[64,2048]{1,0:T(8,128)(2,1)}, bf16[64,2048]{1,0:T(8,128)(2,1)S(1)}, u32[]{:S(2)}, u32[]{:S(2)}) collective-permute-start(bf16[64,2048]{1,0:T(8,128)(2,1)} %bitcast.15), channel_id=1, source_target_pairs={{0,24},{1,25},{2,26},{3,27},{4,28},{5,29},{6,30},{7,31},{8,16},{9,... | collective-permute-start | bytes 786440 | tf_op jit(solution)/shard_map/ppermute | solution.py:33
  5.0 30.5 %collective-permute-start.9 = (bf16[64,2048]{1,0:T(8,128)(2,1)}, bf16[64,2048]{1,0:T(8,128)(2,1)S(1)}, u32[]{:S(2)}, u32[]{:S(2)}) collective-permute-start(bf16[64,2048]{1,0:T(8,128)(2,1)} %bitcast.16), channel_id=1, source_target_pairs={{0,16},{1,17},{2,18},{3,19},{4,20},{5,21},{6,22},{7,23},{8,24},{9,... | collective-permute-start | bytes 786440 | tf_op jit(solution)/shard_map/ppermute | solution.py:33
  5.5 0.7 %copy-start = (s32[1,64,8]{1,2,0:T(8,128)S(1)}, s32[1,64,8]{1,2,0:T(8,128)}, u32[]{:S(2)}) copy-start(s32[1,64,8]{1,2,0:T(8,128)} %param.5) | copy-start | bytes 6148
  6.2 0.7 %copy-start.2 = (bf16[1,64,8]{1,2,0:T(8,128)(2,1)S(1)}, bf16[1,64,8]{1,2,0:T(8,128)(2,1)}, u32[]{:S(2)}) copy-start(bf16[1,64,8]{1,2,0:T(8,128)(2,1)} %param.6) | copy-start | bytes 3076
  7.0 11.7 %collective-permute-start.1 = (bf16[64,128]{1,0:T(8,128)(2,1)S(1)}, bf16[64,128]{1,0:T(8,128)(2,1)S(1)}, u32[]{:S(2)}, u32[]{:S(2)}) collective-permute-start(bf16[64,128]{1,0:T(8,128)(2,1)S(1)} %shard_map.46.columns), channel_id=1, source_target_pairs={{0,8},{1,9},{2,10},{3,11},{4,12},{5,13},{6,14},{7,15},{8,0},{9,1},... | collective-permute-start | bytes 49160 | tf_op jit(solution)/shard_map/ppermute | solution.py:23
  7.2 6.8 %collective-permute-start.3 = (bf16[64,128]{1,0:T(8,128)(2,1)S(1)}, bf16[64,128]{1,0:T(8,128)(2,1)S(1)}, u32[]{:S(2)}, u32[]{:S(2)}) collective-permute-start(bf16[64,128]{1,0:T(8,128)(2,1)S(1)} %shard_map.46.columns), channel_id=1, source_target_pairs={{0,4},{1,5},{2,6},{3,7},{4,0},{5,1},{6,2},{7,3},{8,12},{9,13},{10,... | collective-permute-start | bytes 49160 | tf_op jit(solution)/shard_map/ppermute | solution.py:23
  8.9 16.6 %collective-permute-start.5 = (bf16[64,2048]{1,0:T(8,128)(2,1)}, bf16[64,2048]{1,0:T(8,128)(2,1)S(1)}, u32[]{:S(2)}, u32[]{:S(2)}) collective-permute-start(bf16[64,2048]{1,0:T(8,128)(2,1)} %bitcast.17), channel_id=1, source_target_pairs={{0,20},{1,21},{2,22},{3,23},{4,16},{5,17},{6,18},{7,19},{8,28},{9,... | collective-permute-start | bytes 786440 | tf_op jit(solution)/shard_map/ppermute | solution.py:33
  10.3 1.9 %copy-start.3 = (bf16[1,1,768,2048]{3,2,1,0:T(8,128)(2,1)S(1)}, bf16[1,1,768,2048]{3,2,1,0:T(8,128)(2,1)}, u32[]{:S(2)}) copy-start(bf16[1,1,768,2048]{3,2,1,0:T(8,128)(2,1)} %param.7) | copy-start | bytes 9437188
  18.7 13.1 %collective-permute-start.4 = (bf16[64,2176]{1,0:T(8,128)(2,1)S(1)}, bf16[64,2176]{1,0:T(8,128)(2,1)S(1)}, u32[]{:S(2)}, u32[]{:S(2)}) collective-permute-start(bf16[64,2176]{1,0:T(8,128)(2,1)S(1)} %shard_map.48.refs_0_), channel_id=1, source_target_pairs={{0,4},{1,5},{2,6},{3,7},{4,0},{5,1},{6,2},{7,3},{8,12},{9,13},{10,... | collective-permute-start | bytes 835592 | tf_op jit(solution)/shard_map/ppermute | solution.py:23
  19.4 19.9 %collective-permute-start.7 = (bf16[64,2176]{1,0:T(8,128)(2,1)S(1)}, bf16[64,2176]{1,0:T(8,128)(2,1)S(1)}, u32[]{:S(2)}, u32[]{:S(2)}) collective-permute-start(bf16[64,2176]{1,0:T(8,128)(2,1)S(1)} %shard_map.48.refs_0_), channel_id=1, source_target_pairs={{0,2},{1,3},{2,0},{3,1},{4,6},{5,7},{6,4},{7,5},{8,10},{9,11},{10,... | collective-permute-start | bytes 835592 | tf_op jit(solution)/shard_map/ppermute | solution.py:23
  22.1 17.2 %collective-permute-start.8 = (bf16[2,64,768]{2,1,0:T(8,128)(2,1)S(1)}, bf16[2,64,768]{2,1,0:T(8,128)(2,1)S(1)}, u32[]{:S(2)}, u32[]{:S(2)}) collective-permute-start(bf16[2,64,768]{2,1,0:T(8,128)(2,1)S(1)} %shard_map.49), channel_id=1, source_target_pairs={{0,8},{1,9},{2,10},{3,11},{4,12},{5,13},{6,14},{7,15},{8,0},{9,1},... | collective-permute-start | bytes 589832 | tf_op jit(solution)/shard_map/ppermute | solution.py:23
  25.6 22.5 %collective-permute-start.6 = (bf16[64,2176]{1,0:T(8,128)(2,1)S(1)}, bf16[64,2176]{1,0:T(8,128)(2,1)S(1)}, u32[]{:S(2)}, u32[]{:S(2)}) collective-permute-start(bf16[64,2176]{1,0:T(8,128)(2,1)S(1)} %shard_map.50.refs_0_), channel_id=1, source_target_pairs={{0,2},{1,3},{2,0},{3,1},{4,6},{5,7},{6,4},{7,5},{8,10},{9,11},{10,... | collective-permute-start | bytes 835592 | tf_op jit(solution)/shard_map/ppermute | solution.py:23
  31.8 9.6 %collective-permute-start.11 = (bf16[64,2176]{1,0:T(8,128)(2,1)S(1)}, bf16[64,2176]{1,0:T(8,128)(2,1)S(1)}, u32[]{:S(2)}, u32[]{:S(2)}) collective-permute-start(bf16[64,2176]{1,0:T(8,128)(2,1)S(1)} %collective-permute-done.4.refs_0_), channel_id=1, source_target_pairs={{0,2},{1,3},{2,0},{3,1},{4,6},{5,7},{6,4},{7,5},{8,10},{9,11},{10,... | collective-permute-start | bytes 835592 | tf_op jit(solution)/shard_map/ppermute | solution.py:23
  35.5 23.4 %collective-permute-start.16 = (bf16[2,64,768]{2,1,0:T(8,128)(2,1)S(1)}, bf16[2,64,768]{2,1,0:T(8,128)(2,1)S(1)}, u32[]{:S(2)}, u32[]{:S(2)}) collective-permute-start(bf16[2,64,768]{2,1,0:T(8,128)(2,1)S(1)} %shard_map.51), channel_id=1, source_target_pairs={{0,12},{1,13},{2,14},{3,15},{4,8},{5,9},{6,10},{7,11},{8,4},{9,5},... | collective-permute-start | bytes 589832 | tf_op jit(solution)/shard_map/ppermute | solution.py:23
  39.3 8.8 %collective-permute-start.10 = (bf16[64,2176]{1,0:T(8,128)(2,1)S(1)}, bf16[64,2176]{1,0:T(8,128)(2,1)S(1)}, u32[]{:S(2)}, u32[]{:S(2)}) collective-permute-start(bf16[64,2176]{1,0:T(8,128)(2,1)S(1)} %shard_map.52.refs_3_), channel_id=1, source_target_pairs={{0,2},{1,3},{2,0},{3,1},{4,6},{5,7},{6,4},{7,5},{8,10},{9,11},{10,... | collective-permute-start | bytes 835592 | tf_op jit(solution)/shard_map/ppermute | solution.py:23
  40.6 18.3 %collective-permute-start.15 = (bf16[2,64,768]{2,1,0:T(8,128)(2,1)S(1)}, bf16[2,64,768]{2,1,0:T(8,128)(2,1)S(1)}, u32[]{:S(2)}, u32[]{:S(2)}) collective-permute-start(bf16[2,64,768]{2,1,0:T(8,128)(2,1)S(1)} %shard_map.53), channel_id=1, source_target_pairs={{0,10},{1,11},{2,8},{3,9},{4,14},{5,15},{6,12},{7,13},{8,2},{9,3},... | collective-permute-start | bytes 589832 | tf_op jit(solution)/shard_map/ppermute | solution.py:23
  42.6 16.3 %copy-start.1 = (s32[1,64,8]{1,2,0:T(8,128)S(1)}, s32[1,64,8]{1,2,0:T(8,128)}, u32[]{:S(2)}) copy-start(s32[1,64,8]{1,2,0:T(8,128)} %param.5) | copy-start | bytes 6148
  42.6 16.2 %collective-permute-start.17 = (bf16[2,64,768]{2,1,0:T(8,128)(2,1)S(1)}, bf16[2,64,768]{2,1,0:T(8,128)(2,1)S(1)}, u32[]{:S(2)}, u32[]{:S(2)}) collective-permute-start(bf16[2,64,768]{2,1,0:T(8,128)(2,1)S(1)} %shard_map.54), channel_id=1, source_target_pairs={{0,14},{1,15},{2,12},{3,13},{4,10},{5,11},{6,8},{7,9},{8,6},{9,7},... | collective-permute-start | bytes 589832 | tf_op jit(solution)/shard_map/ppermute | solution.py:23
  49.8 9.4 %collective-permute-start.12 = (bf16[2,64,768]{2,1,0:T(8,128)(2,1)S(1)}, bf16[2,64,768]{2,1,0:T(8,128)(2,1)S(1)}, u32[]{:S(2)}, u32[]{:S(2)}) collective-permute-start(bf16[2,64,768]{2,1,0:T(8,128)(2,1)S(1)} %get-tuple-element.42), channel_id=1, source_target_pairs={{0,2},{1,3},{2,0},{3,1},{4,6},{5,7},{6,4},{7,5},{8,10},{9,11},{10,... | collective-permute-start | bytes 589832 | tf_op jit(solution)/shard_map/ppermute | solution.py:23
  50.8 10.9 %collective-permute-start.13 = (bf16[2,64,768]{2,1,0:T(8,128)(2,1)S(1)}, bf16[2,64,768]{2,1,0:T(8,128)(2,1)S(1)}, u32[]{:S(2)}, u32[]{:S(2)}) collective-permute-start(bf16[2,64,768]{2,1,0:T(8,128)(2,1)S(1)} %get-tuple-element.43), channel_id=1, source_target_pairs={{0,4},{1,5},{2,6},{3,7},{4,0},{5,1},{6,2},{7,3},{8,12},{9,13},{10,... | collective-permute-start | bytes 589832 | tf_op jit(solution)/shard_map/ppermute | solution.py:23
  58.8 6.6 %collective-permute-start.14 = (bf16[2,64,768]{2,1,0:T(8,128)(2,1)S(1)}, bf16[2,64,768]{2,1,0:T(8,128)(2,1)S(1)}, u32[]{:S(2)}, u32[]{:S(2)}) collective-permute-start(bf16[2,64,768]{2,1,0:T(8,128)(2,1)S(1)} %get-tuple-element.44), channel_id=1, source_target_pairs={{0,6},{1,7},{2,4},{3,5},{4,2},{5,3},{6,0},{7,1},{8,14},{9,15},{10,... | collective-permute-start | bytes 589832 | tf_op jit(solution)/shard_map/ppermute | solution.py:23

commit v36 on v35

--- a/solution.py
+++ b/solution.py
@@ -206,7 +206,7 @@
         X ^ Z_NEAR ^ Z_FAR: back_cross_side,
     }
     near_parts = {X: back_side, Z_NEAR: back_near, X ^ Z_NEAR: back_near_side}
-    out = pick_routes(route_ids.T, near_parts, pick_routes(route_ids.T, far_parts))
+    out = pick_routes(route_ids.T, far_parts, pick_routes(route_ids.T, near_parts))
     return out.reshape(1, tokens, top, weight_mat.shape[0])
 
 

time: 66.9 us -> 78.5 us (1.17)
  the two profiles are of different devices: /device:TPU:0 before, /device:TPU:8 now
where the time goes in v36:
time: 78.5 us; the launch traced here: 78.3 us
  waiting for transfers between devices  37.9 us (48%)
  starting transfers between devices  26.9 us (34%)
  Pallas kernels  10.1 us (13%)
  local copies, waits for them, and re-layouts  3.26 us (4%)
    ppermute x15, waiting for transfers between devices, send(): return lax.ppermute(block, 'expert', route)  37.9 us
    ppermute x15, starting transfers between devices, send(): return lax.ppermute(block, 'expert', route)  20.1 us
    ppermute x3, starting transfers between devices, send_across(): return lax.ppermute(block, ('pipe', 'expert'), route)  6.79 us
    pallas_call x5, Pallas kernels, products(): pl.pallas_call(functools.partial(products_kernel, len(pieces)), out_shape...  6.55 us
    unnamed x8, local copies, waits for them, and re-layouts  3.26 us
    pallas_call x2, Pallas kernels, pick_routes(): pl.pallas_call(functools.partial(pick_kernel, flips), out_shape=jax.Shape...  1.75 us
    pallas_call x1, Pallas kernels, turned(): pl.pallas_call(turn_kernel, out_shape=jax.ShapeDtypeStruct((depth, CORES...  1.67 us
  transfers between devices with their start and end apart: 18, of which 8 were waited for; matrix products, arithmetic and copies ran while one was open for 0% of the time, Pallas kernels for 9%

profile of v36, /device:TPU:8, one launch (start us, length us, event | category | flops | bytes accessed | tf_op | source)
XLA Modules:
  0.0 78.3 jit_solution(3748539590392948463)
XLA Ops:
  0.0 0.0 collective-permute-start.2
  0.0 3.5 %collective-permute-start = (bf16[64,2048]{1,0:T(8,128)(2,1)}, bf16[64,2048]{1,0:T(8,128)(2,1)S(1)}, u32[]{:S(2)}, u32[]{:S(2)}) collective-permute-start(bf16[64,2048]{1,0:T(8,128)(2,1)} %bitcast.15), channel_id=1, source_target_pairs={{0,24},{1,25},{2,26},{3,27},{4,28},{5,29},{6,30},{7,31},{8,16},{9,... | collective-permute-start | bytes 786440 | tf_op jit(solution)/shard_map/ppermute | solution.py:33
  3.5 0.5 collective-permute-start.9
  4.1 0.0 copy-start
  4.1 0.7 copy-done
  4.7 0.0 copy-start.2
  4.7 0.7 copy-done.2
  5.4 0.1 shard_map.46.columns
  5.5 0.4 collective-permute-start.1
  5.9 0.2 collective-permute-start.3
  6.2 0.0 collective-permute-done.2.other
  6.2 2.7 %collective-permute-start.5 = (bf16[64,2048]{1,0:T(8,128)(2,1)}, bf16[64,2048]{1,0:T(8,128)(2,1)S(1)}, u32[]{:S(2)}, u32[]{:S(2)}) collective-permute-start(bf16[64,2048]{1,0:T(8,128)(2,1)} %bitcast.17), channel_id=1, source_target_pairs={{0,20},{1,21},{2,22},{3,23},{4,16},{5,17},{6,18},{7,19},{8,28},{9,... | collective-permute-start | bytes 786440 | tf_op jit(solution)/shard_map/ppermute | solution.py:33
  8.9 0.0 copy-start.3
  8.9 1.9 %copy-done.3 = bf16[1,1,768,2048]{3,2,1,0:T(8,128)(2,1)S(1)} copy-done((bf16[1,1,768,2048]{3,2,1,0:T(8,128)(2,1)S(1)}, bf16[1,1,768,2048]{3,2,1,0:T(8,128)(2,1)}, u32[]{:S(2)}) %copy-start.3) | copy-done | bytes 3145752
  10.8 1.7 %shard_map.47.weights = bf16[2048,1536]{1,0:T(8,128)(2,1)S(1)} custom-call(bf16[768,2048]{1,0:T(8,128)(2,1)S(1)} %bitcast.14, bf16[768,2048]{1,0:T(8,128)(2,1)S(1)} %collective-permute-done.2.other), custom_call_target="tpu_custom_call" | custom-call | flops 12884901888 | tf_op jit(solution)/shard_map/pallas_call | solution.py:77
  12.5 0.0 collective-permute-done.3.columns
  12.5 3.8 %collective-permute-done.1.columns = bf16[64,128]{1,0:T(8,128)(2,1)S(1)} collective-permute-done((bf16[64,128]{1,0:T(8,128)(2,1)S(1)}, bf16[64,128]{1,0:T(8,128)(2,1)S(1)}, u32[]{:S(2)}, u32[]{:S(2)}) %collective-permute-start.1) | collective-permute-done | bytes 16416 | tf_op jit(solution)/shard_map/ppermute | solution.py:23
  16.3 0.0 collective-permute-done.rows
  16.3 1.5 %collective-permute-start.4 = (bf16[64,2176]{1,0:T(8,128)(2,1)S(1)}, bf16[64,2176]{1,0:T(8,128)(2,1)S(1)}, u32[]{:S(2)}, u32[]{:S(2)}) collective-permute-start(bf16[64,2176]{1,0:T(8,128)(2,1)S(1)} %shard_map.48.refs_0_), channel_id=1, source_target_pairs={{0,4},{1,5},{2,6},{3,7},{4,0},{5,1},{6,2},{7,3},{8,12},{9,13},{10,... | collective-permute-start | bytes 835592 | tf_op jit(solution)/shard_map/ppermute | solution.py:23
  17.8 1.5 %collective-permute-start.7 = (bf16[64,2176]{1,0:T(8,128)(2,1)S(1)}, bf16[64,2176]{1,0:T(8,128)(2,1)S(1)}, u32[]{:S(2)}, u32[]{:S(2)}) collective-permute-start(bf16[64,2176]{1,0:T(8,128)(2,1)S(1)} %shard_map.48.refs_0_), channel_id=1, source_target_pairs={{0,2},{1,3},{2,0},{3,1},{4,6},{5,7},{6,4},{7,5},{8,10},{9,11},{10,... | collective-permute-start | bytes 835592 | tf_op jit(solution)/shard_map/ppermute | solution.py:23
  19.2 1.2 %shard_map.49 = bf16[2,64,768]{2,1,0:T(8,128)(2,1)S(1)} custom-call(bf16[2048,1536]{1,0:T(8,128)(2,1)S(1)} %shard_map.47.weights, bf16[64,2176]{1,0:T(8,128)(2,1)S(1)} %shard_map.48.refs_0_), custom_call_target="tpu_custom_call" | custom-call | flops 4026531840 | bytes 6750208 | tf_op jit(solution)/shard_map/pallas_call | solution.py:109
  20.4 2.2 %collective-permute-start.8 = (bf16[2,64,768]{2,1,0:T(8,128)(2,1)S(1)}, bf16[2,64,768]{2,1,0:T(8,128)(2,1)S(1)}, u32[]{:S(2)}, u32[]{:S(2)}) collective-permute-start(bf16[2,64,768]{2,1,0:T(8,128)(2,1)S(1)} %shard_map.49), channel_id=1, source_target_pairs={{0,8},{1,9},{2,10},{3,11},{4,12},{5,13},{6,14},{7,15},{8,0},{9,1},... | collective-permute-start | bytes 589832 | tf_op jit(solution)/shard_map/ppermute | solution.py:23
  22.6 0.0 collective-permute-done.5.rows
  22.6 0.6 collective-permute-start.6
  23.2 5.1 %collective-permute-done.4.refs_0_ = bf16[64,2176]{1,0:T(8,128)(2,1)S(1)} collective-permute-done((bf16[64,2176]{1,0:T(8,128)(2,1)S(1)}, bf16[64,2176]{1,0:T(8,128)(2,1)S(1)}, u32[]{:S(2)}, u32[]{:S(2)}) %collective-permute-start.4) | collective-permute-done | bytes 278560 | tf_op jit(solution)/shard_map/ppermute | solution.py:23
  28.3 2.4 %collective-permute-start.11 = (bf16[64,2176]{1,0:T(8,128)(2,1)S(1)}, bf16[64,2176]{1,0:T(8,128)(2,1)S(1)}, u32[]{:S(2)}, u32[]{:S(2)}) collective-permute-start(bf16[64,2176]{1,0:T(8,128)(2,1)S(1)} %collective-permute-done.4.refs_0_), channel_id=1, source_target_pairs={{0,2},{1,3},{2,0},{3,1},{4,6},{5,7},{6,4},{7,5},{8,10},{9,11},{10,... | collective-permute-start | bytes 835592 | tf_op jit(solution)/shard_map/ppermute | solution.py:23
  30.8 1.2 %shard_map.51 = bf16[2,64,768]{2,1,0:T(8,128)(2,1)S(1)} custom-call(bf16[2048,1536]{1,0:T(8,128)(2,1)S(1)} %shard_map.47.weights, bf16[64,2176]{1,0:T(8,128)(2,1)S(1)} %collective-permute-done.4.refs_0_), custom_call_target="tpu_custom_call" | custom-call | flops 4026531840 | bytes 6750208 | tf_op jit(solution)/shard_map/pallas_call | solution.py:109
  32.0 0.0 collective-permute-done.9.rows
  32.0 0.0 collective-permute-done.8.refs_1_
  32.0 0.0 collective-permute-done.7.refs_0_
  32.0 0.5 collective-permute-start.10
  32.5 1.2 %shard_map.53 = bf16[2,64,768]{2,1,0:T(8,128)(2,1)S(1)} custom-call(bf16[2048,1536]{1,0:T(8,128)(2,1)S(1)} %shard_map.47.weights, bf16[64,2176]{1,0:T(8,128)(2,1)S(1)} %collective-permute-done.7.refs_0_), custom_call_target="tpu_custom_call" | custom-call | flops 4026531840 | bytes 6750208 | tf_op jit(solution)/shard_map/pallas_call | solution.py:109
  33.7 4.8 %collective-permute-done.11.refs_0_ = bf16[64,2176]{1,0:T(8,128)(2,1)S(1)} collective-permute-done((bf16[64,2176]{1,0:T(8,128)(2,1)S(1)}, bf16[64,2176]{1,0:T(8,128)(2,1)S(1)}, u32[]{:S(2)}, u32[]{:S(2)}) %collective-permute-start.11) | collective-permute-done | bytes 278560 | tf_op jit(solution)/shard_map/ppermute | solution.py:23
  38.5 1.2 %shard_map.54 = bf16[2,64,768]{2,1,0:T(8,128)(2,1)S(1)} custom-call(bf16[2048,1536]{1,0:T(8,128)(2,1)S(1)} %shard_map.47.weights, bf16[64,2176]{1,0:T(8,128)(2,1)S(1)} %collective-permute-done.11.refs_0_), custom_call_target="tpu_custom_call" | custom-call | flops 4026531840 | bytes 6750208 | tf_op jit(solution)/shard_map/pallas_call | solution.py:109
  39.7 0.0 copy-start.1
  39.7 0.0 collective-permute-done.6.refs_1_
  39.7 3.9 %collective-permute-done.10.refs_2_ = bf16[64,2176]{1,0:T(8,128)(2,1)S(1)} collective-permute-done((bf16[64,2176]{1,0:T(8,128)(2,1)S(1)}, bf16[64,2176]{1,0:T(8,128)(2,1)S(1)}, u32[]{:S(2)}, u32[]{:S(2)}) %collective-permute-start.10) | collective-permute-done | bytes 278560 | tf_op jit(solution)/shard_map/ppermute | solution.py:23
  43.6 1.8 %shard_map.55 = (bf16[2,64,768]{2,1,0:T(8,128)(2,1)S(1)}, bf16[2,64,768]{2,1,0:T(8,128)(2,1)S(1)}, bf16[2,64,768]{2,1,0:T(8,128)(2,1)S(1)}, bf16[2,64,768]{2,1,0:T(8,128)(2,1)S(1)}) custom-call(bf16[2048,1536]{1,0:T(8,128)(2,1)S(1)} %shard_map.47.weights, bf16[64,2176]{1,0:T(8,128)(2,1)S(1)} %shard_map.50.refs_0_, ...), custom_call_target="tpu_custom_call" | custom-call | flops 16106127360 | bytes 8126464 | tf_op jit(solution)/shard_map/pallas_call | solution.py:109
  45.4 1.6 %collective-permute-start.15 = (bf16[2,64,768]{2,1,0:T(8,128)(2,1)S(1)}, bf16[2,64,768]{2,1,0:T(8,128)(2,1)S(1)}, u32[]{:S(2)}, u32[]{:S(2)}) collective-permute-start(bf16[2,64,768]{2,1,0:T(8,128)(2,1)S(1)} %get-tuple-element.44), channel_id=1, source_target_pairs={{0,2},{1,3},{2,0},{3,1},{4,6},{5,7},{6,4},{7,5},{8,10},{9,11},{10,... | collective-permute-start | bytes 589832 | tf_op jit(solution)/shard_map/ppermute | solution.py:23
  47.0 1.3 %collective-permute-start.16 = (bf16[2,64,768]{2,1,0:T(8,128)(2,1)S(1)}, bf16[2,64,768]{2,1,0:T(8,128)(2,1)S(1)}, u32[]{:S(2)}, u32[]{:S(2)}) collective-permute-start(bf16[2,64,768]{2,1,0:T(8,128)(2,1)S(1)} %get-tuple-element.45), channel_id=1, source_target_pairs={{0,4},{1,5},{2,6},{3,7},{4,0},{5,1},{6,2},{7,3},{8,12},{9,13},{10,... | collective-permute-start | bytes 589832 | tf_op jit(solution)/shard_map/ppermute | solution.py:23
  48.3 0.7 collective-permute-start.17
  49.0 3.7 %collective-permute-start.12 = (bf16[2,64,768]{2,1,0:T(8,128)(2,1)S(1)}, bf16[2,64,768]{2,1,0:T(8,128)(2,1)S(1)}, u32[]{:S(2)}, u32[]{:S(2)}) collective-permute-start(bf16[2,64,768]{2,1,0:T(8,128)(2,1)S(1)} %shard_map.53), channel_id=1, source_target_pairs={{0,10},{1,11},{2,8},{3,9},{4,14},{5,15},{6,12},{7,13},{8,2},{9,3},... | collective-permute-start | bytes 589832 | tf_op jit(solution)/shard_map/ppermute | solution.py:23
  52.6 0.1 collective-permute-start.13
  52.7 0.0 collective-permute-done.15.refs_0_
  52.7 3.6 %collective-permute-start.14 = (bf16[2,64,768]{2,1,0:T(8,128)(2,1)S(1)}, bf16[2,64,768]{2,1,0:T(8,128)(2,1)S(1)}, u32[]{:S(2)}, u32[]{:S(2)}) collective-permute-start(bf16[2,64,768]{2,1,0:T(8,128)(2,1)S(1)} %shard_map.54), channel_id=1, source_target_pairs={{0,14},{1,15},{2,12},{3,13},{4,10},{5,11},{6,8},{7,9},{8,6},{9,7},... | collective-permute-start | bytes 589832 | tf_op jit(solution)/shard_map/ppermute | solution.py:23
  56.3 0.0 collective-permute-done.16.refs_1_
  56.3 2.8 %collective-permute-done.17.refs_2_ = bf16[2,64,768]{2,1,0:T(8,128)(2,1)S(1)} collective-permute-done((bf16[2,64,768]{2,1,0:T(8,128)(2,1)S(1)}, bf16[2,64,768]{2,1,0:T(8,128)(2,1)S(1)}, u32[]{:S(2)}, u32[]{:S(2)}) %collective-permute-start.17) | collective-permute-done | bytes 196640 | tf_op jit(solution)/shard_map/ppermute | solution.py:23
  59.1 0.0 copy-done.1
  59.1 0.4 shard_map.56.refs_5_
  59.5 10.8 %collective-permute-done.12.refs_2_ = bf16[2,64,768]{2,1,0:T(8,128)(2,1)S(1)} collective-permute-done((bf16[2,64,768]{2,1,0:T(8,128)(2,1)S(1)}, bf16[2,64,768]{2,1,0:T(8,128)(2,1)S(1)}, u32[]{:S(2)}, u32[]{:S(2)}) %collective-permute-start.12) | collective-permute-done | bytes 196640 | tf_op jit(solution)/shard_map/ppermute | solution.py:23
  70.3 4.0 %collective-permute-done.13.refs_3_ = bf16[2,64,768]{2,1,0:T(8,128)(2,1)S(1)} collective-permute-done((bf16[2,64,768]{2,1,0:T(8,128)(2,1)S(1)}, bf16[2,64,768]{2,1,0:T(8,128)(2,1)S(1)}, u32[]{:S(2)}, u32[]{:S(2)}) %collective-permute-start.13) | collective-permute-done | bytes 196640 | tf_op jit(solution)/shard_map/ppermute | solution.py:23
  74.4 2.6 %collective-permute-done.14.refs_4_ = bf16[2,64,768]{2,1,0:T(8,128)(2,1)S(1)} collective-permute-done((bf16[2,64,768]{2,1,0:T(8,128)(2,1)S(1)}, bf16[2,64,768]{2,1,0:T(8,128)(2,1)S(1)}, u32[]{:S(2)}, u32[]{:S(2)}) %collective-permute-start.14) | collective-permute-done | bytes 196640 | tf_op jit(solution)/shard_map/ppermute | solution.py:23
  77.0 1.3 %shard_map.57 = bf16[512,768]{1,0:T(8,128)(2,1)} custom-call(s32[8,64]{1,0:T(8,128)S(1)} %bitcast.11, bf16[2,64,768]{2,1,0:T(8,128)(2,1)S(1)} %get-tuple-element.42.refs_0_, bf16[2,64,768]{2,1,0:T(8,128)(2,1)S(1)} %collective-permute-done.8.refs_1_, bf16[2,64,768]{2,1,0:T(8,128)(2,1)S(1)} %collective-permute-done.12.refs_2_, ...), custom_call_target="tpu_custom_call" | custom-call | tf_op jit(solution)/shard_map/pallas_call | solution.py:150
  (3 shorter events, 0.1 us)
Async XLA Ops:
  0.0 6.2 %collective-permute-start.2 = (bf16[768,2048]{1,0:T(8,128)(2,1)}, bf16[768,2048]{1,0:T(8,128)(2,1)S(1)}, u32[]{:S(2)}, u32[]{:S(2)}) collective-permute-start(bf16[768,2048]{1,0:T(8,128)(2,1)} %bitcast.13), channel_id=1, source_target_pairs={{0,1},{1,0},{2,3},{3,2},{4,5},{5,4},{6,7},{7,6},{8,9},{9,8},{10,11... | collective-permute-start | bytes 9437192 | tf_op jit(solution)/shard_map/ppermute | solution.py:23
  0.0 16.3 %collective-permute-start = (bf16[64,2048]{1,0:T(8,128)(2,1)}, bf16[64,2048]{1,0:T(8,128)(2,1)S(1)}, u32[]{:S(2)}, u32[]{:S(2)}) collective-permute-start(bf16[64,2048]{1,0:T(8,128)(2,1)} %bitcast.15), channel_id=1, source_target_pairs={{0,24},{1,25},{2,26},{3,27},{4,28},{5,29},{6,30},{7,31},{8,16},{9,... | collective-permute-start | bytes 786440 | tf_op jit(solution)/shard_map/ppermute | solution.py:33
  3.5 28.4 %collective-permute-start.9 = (bf16[64,2048]{1,0:T(8,128)(2,1)}, bf16[64,2048]{1,0:T(8,128)(2,1)S(1)}, u32[]{:S(2)}, u32[]{:S(2)}) collective-permute-start(bf16[64,2048]{1,0:T(8,128)(2,1)} %bitcast.16), channel_id=1, source_target_pairs={{0,16},{1,17},{2,18},{3,19},{4,20},{5,21},{6,22},{7,23},{8,24},{9,... | collective-permute-start | bytes 786440 | tf_op jit(solution)/shard_map/ppermute | solution.py:33
  4.1 0.7 copy-start
  4.7 0.7 copy-start.2
  5.5 10.7 %collective-permute-start.1 = (bf16[64,128]{1,0:T(8,128)(2,1)S(1)}, bf16[64,128]{1,0:T(8,128)(2,1)S(1)}, u32[]{:S(2)}, u32[]{:S(2)}) collective-permute-start(bf16[64,128]{1,0:T(8,128)(2,1)S(1)} %shard_map.46.columns), channel_id=1, source_target_pairs={{0,8},{1,9},{2,10},{3,11},{4,12},{5,13},{6,14},{7,15},{8,0},{9,1},... | collective-permute-start | bytes 49160 | tf_op jit(solution)/shard_map/ppermute | solution.py:23
  5.9 6.6 %collective-permute-start.3 = (bf16[64,128]{1,0:T(8,128)(2,1)S(1)}, bf16[64,128]{1,0:T(8,128)(2,1)S(1)}, u32[]{:S(2)}, u32[]{:S(2)}) collective-permute-start(bf16[64,128]{1,0:T(8,128)(2,1)S(1)} %shard_map.46.columns), channel_id=1, source_target_pairs={{0,4},{1,5},{2,6},{3,7},{4,0},{5,1},{6,2},{7,3},{8,12},{9,13},{10,... | collective-permute-start | bytes 49160 | tf_op jit(solution)/shard_map/ppermute | solution.py:23
  6.2 16.5 %collective-permute-start.5 = (bf16[64,2048]{1,0:T(8,128)(2,1)}, bf16[64,2048]{1,0:T(8,128)(2,1)S(1)}, u32[]{:S(2)}, u32[]{:S(2)}) collective-permute-start(bf16[64,2048]{1,0:T(8,128)(2,1)} %bitcast.17), channel_id=1, source_target_pairs={{0,20},{1,21},{2,22},{3,23},{4,16},{5,17},{6,18},{7,19},{8,28},{9,... | collective-permute-start | bytes 786440 | tf_op jit(solution)/shard_map/ppermute | solution.py:33
  8.9 1.9 %copy-start.3 = (bf16[1,1,768,2048]{3,2,1,0:T(8,128)(2,1)S(1)}, bf16[1,1,768,2048]{3,2,1,0:T(8,128)(2,1)}, u32[]{:S(2)}) copy-start(bf16[1,1,768,2048]{3,2,1,0:T(8,128)(2,1)} %param.7) | copy-start | bytes 9437188
  16.3 12.0 %collective-permute-start.4 = (bf16[64,2176]{1,0:T(8,128)(2,1)S(1)}, bf16[64,2176]{1,0:T(8,128)(2,1)S(1)}, u32[]{:S(2)}, u32[]{:S(2)}) collective-permute-start(bf16[64,2176]{1,0:T(8,128)(2,1)S(1)} %shard_map.48.refs_0_), channel_id=1, source_target_pairs={{0,4},{1,5},{2,6},{3,7},{4,0},{5,1},{6,2},{7,3},{8,12},{9,13},{10,... | collective-permute-start | bytes 835592 | tf_op jit(solution)/shard_map/ppermute | solution.py:23
  17.8 14.2 %collective-permute-start.7 = (bf16[64,2176]{1,0:T(8,128)(2,1)S(1)}, bf16[64,2176]{1,0:T(8,128)(2,1)S(1)}, u32[]{:S(2)}, u32[]{:S(2)}) collective-permute-start(bf16[64,2176]{1,0:T(8,128)(2,1)S(1)} %shard_map.48.refs_0_), channel_id=1, source_target_pairs={{0,2},{1,3},{2,0},{3,1},{4,6},{5,7},{6,4},{7,5},{8,10},{9,11},{10,... | collective-permute-start | bytes 835592 | tf_op jit(solution)/shard_map/ppermute | solution.py:23
  20.4 11.5 %collective-permute-start.8 = (bf16[2,64,768]{2,1,0:T(8,128)(2,1)S(1)}, bf16[2,64,768]{2,1,0:T(8,128)(2,1)S(1)}, u32[]{:S(2)}, u32[]{:S(2)}) collective-permute-start(bf16[2,64,768]{2,1,0:T(8,128)(2,1)S(1)} %shard_map.49), channel_id=1, source_target_pairs={{0,8},{1,9},{2,10},{3,11},{4,12},{5,13},{6,14},{7,15},{8,0},{9,1},... | collective-permute-start | bytes 589832 | tf_op jit(solution)/shard_map/ppermute | solution.py:23
  22.6 17.1 %collective-permute-start.6 = (bf16[64,2176]{1,0:T(8,128)(2,1)S(1)}, bf16[64,2176]{1,0:T(8,128)(2,1)S(1)}, u32[]{:S(2)}, u32[]{:S(2)}) collective-permute-start(bf16[64,2176]{1,0:T(8,128)(2,1)S(1)} %shard_map.50.refs_0_), channel_id=1, source_target_pairs={{0,2},{1,3},{2,0},{3,1},{4,6},{5,7},{6,4},{7,5},{8,10},{9,11},{10,... | collective-permute-start | bytes 835592 | tf_op jit(solution)/shard_map/ppermute | solution.py:23
  28.3 10.2 %collective-permute-start.11 = (bf16[64,2176]{1,0:T(8,128)(2,1)S(1)}, bf16[64,2176]{1,0:T(8,128)(2,1)S(1)}, u32[]{:S(2)}, u32[]{:S(2)}) collective-permute-start(bf16[64,2176]{1,0:T(8,128)(2,1)S(1)} %collective-permute-done.4.refs_0_), channel_id=1, source_target_pairs={{0,2},{1,3},{2,0},{3,1},{4,6},{5,7},{6,4},{7,5},{8,10},{9,11},{10,... | collective-permute-start | bytes 835592 | tf_op jit(solution)/shard_map/ppermute | solution.py:23
  32.0 11.6 %collective-permute-start.10 = (bf16[64,2176]{1,0:T(8,128)(2,1)S(1)}, bf16[64,2176]{1,0:T(8,128)(2,1)S(1)}, u32[]{:S(2)}, u32[]{:S(2)}) collective-permute-start(bf16[64,2176]{1,0:T(8,128)(2,1)S(1)} %shard_map.52.refs_3_), channel_id=1, source_target_pairs={{0,2},{1,3},{2,0},{3,1},{4,6},{5,7},{6,4},{7,5},{8,10},{9,11},{10,... | collective-permute-start | bytes 835592 | tf_op jit(solution)/shard_map/ppermute | solution.py:23
  39.7 19.4 %copy-start.1 = (s32[1,64,8]{1,2,0:T(8,128)S(1)}, s32[1,64,8]{1,2,0:T(8,128)}, u32[]{:S(2)}) copy-start(s32[1,64,8]{1,2,0:T(8,128)} %param.5) | copy-start | bytes 6148
  45.4 7.3 %collective-permute-start.15 = (bf16[2,64,768]{2,1,0:T(8,128)(2,1)S(1)}, bf16[2,64,768]{2,1,0:T(8,128)(2,1)S(1)}, u32[]{:S(2)}, u32[]{:S(2)}) collective-permute-start(bf16[2,64,768]{2,1,0:T(8,128)(2,1)S(1)} %get-tuple-element.44), channel_id=1, source_target_pairs={{0,2},{1,3},{2,0},{3,1},{4,6},{5,7},{6,4},{7,5},{8,10},{9,11},{10,... | collective-permute-start | bytes 589832 | tf_op jit(solution)/shard_map/ppermute | solution.py:23
  47.0 9.3 %collective-permute-start.16 = (bf16[2,64,768]{2,1,0:T(8,128)(2,1)S(1)}, bf16[2,64,768]{2,1,0:T(8,128)(2,1)S(1)}, u32[]{:S(2)}, u32[]{:S(2)}) collective-permute-start(bf16[2,64,768]{2,1,0:T(8,128)(2,1)S(1)} %get-tuple-element.45), channel_id=1, source_target_pairs={{0,4},{1,5},{2,6},{3,7},{4,0},{5,1},{6,2},{7,3},{8,12},{9,13},{10,... | collective-permute-start | bytes 589832 | tf_op jit(solution)/shard_map/ppermute | solution.py:23
  48.3 10.8 %collective-permute-start.17 = (bf16[2,64,768]{2,1,0:T(8,128)(2,1)S(1)}, bf16[2,64,768]{2,1,0:T(8,128)(2,1)S(1)}, u32[]{:S(2)}, u32[]{:S(2)}) collective-permute-start(bf16[2,64,768]{2,1,0:T(8,128)(2,1)S(1)} %get-tuple-element.46), channel_id=1, source_target_pairs={{0,6},{1,7},{2,4},{3,5},{4,2},{5,3},{6,0},{7,1},{8,14},{9,15},{10,... | collective-permute-start | bytes 589832 | tf_op jit(solution)/shard_map/ppermute | solution.py:23
  49.0 21.4 %collective-permute-start.12 = (bf16[2,64,768]{2,1,0:T(8,128)(2,1)S(1)}, bf16[2,64,768]{2,1,0:T(8,128)(2,1)S(1)}, u32[]{:S(2)}, u32[]{:S(2)}) collective-permute-start(bf16[2,64,768]{2,1,0:T(8,128)(2,1)S(1)} %shard_map.53), channel_id=1, source_target_pairs={{0,10},{1,11},{2,8},{3,9},{4,14},{5,15},{6,12},{7,13},{8,2},{9,3},... | collective-permute-start | bytes 589832 | tf_op jit(solution)/shard_map/ppermute | solution.py:23
  52.6 21.7 %collective-permute-start.13 = (bf16[2,64,768]{2,1,0:T(8,128)(2,1)S(1)}, bf16[2,64,768]{2,1,0:T(8,128)(2,1)S(1)}, u32[]{:S(2)}, u32[]{:S(2)}) collective-permute-start(bf16[2,64,768]{2,1,0:T(8,128)(2,1)S(1)} %shard_map.51), channel_id=1, source_target_pairs={{0,12},{1,13},{2,14},{3,15},{4,8},{5,9},{6,10},{7,11},{8,4},{9,5},... | collective-permute-start | bytes 589832 | tf_op jit(solution)/shard_map/ppermute | solution.py:23
  52.7 24.3 %collective-permute-start.14 = (bf16[2,64,768]{2,1,0:T(8,128)(2,1)S(1)}, bf16[2,64,768]{2,1,0:T(8,128)(2,1)S(1)}, u32[]{:S(2)}, u32[]{:S(2)}) collective-permute-start(bf16[2,64,768]{2,1,0:T(8,128)(2,1)S(1)} %shard_map.54), channel_id=1, source_target_pairs={{0,14},{1,15},{2,12},{3,13},{4,10},{5,11},{6,8},{7,9},{8,6},{9,7},... | collective-permute-start | bytes 589832 | tf_op jit(solution)/shard_map/ppermute | solution.py:23
